TPU v7x, 32 devices: a whole 2x2x4 slice. The times are simulated.
32 devices in a mesh: group: 4 (over y, x), member: 8 (over z, core).
Axes of the slice: x: 2, y: 2, z: 4, core: 2. Of those that a mesh axis runs over, the one named last changes fastest.
Arguments:
- embeddings: bfloat16 [3072, 4096], P(('group', 'member'))
- cluster_ids: int32 [3072], P(('group', 'member')), may hold values from 0 to 7, as said below
- order_index: int32 [3072], P(('group', 'member')), may hold values from 0 to 3071, each once
Outputs:
- best_similarity: float32 [3072], P(('group', 'member'))
Inputs may be any that keep to these rules, and one draw needn't show every extreme that they name: `cluster_ids`: among the documents of one device, at most 48 have a cluster of any one group index g (cluster // 2 == g), and on every device some group index has exactly 48.
All inputs are finite; a program needn't handle non-finite values.
Results may differ from a plain program's by a relative error of at most 0.0004.
Values may be sent and summed in bfloat16 or wider, within the bound.
No kernel may reach another device: no remote copies, remote signals or barrier semaphores. Data moves between devices by JAX's collectives and lax.ppermute only.
A program may use at most 128 MiB of HBM per device.

v0:
```python
import jax
import jax.numpy as jnp
from jax import lax
from jax.sharding import PartitionSpec as P

CL_GROUP = 2


def normalize(embeddings):
    values = embeddings.astype(jnp.float32)
    total = jnp.sum(values * values, axis=1, keepdims=True) + values.shape[1] * 1e-06
    return (values * lax.rsqrt(total)).astype(jnp.bfloat16)


def tile_maxima(rows_left, cluster_left, order_left, rows_right, cluster_right, order_right):
    cosine = lax.dot_general(
        rows_left, rows_right, (((1,), (1,)), ((), ())), preferred_element_type=jnp.float32
    )
    same_cluster = (cluster_left[:, None] == cluster_right[None, :]) & (cluster_left[:, None] >= 0)
    earlier = same_cluster & (order_right[None, :] < order_left[:, None])
    later_pair = same_cluster & (order_left[:, None] < order_right[None, :])
    row_maxima = jnp.max(jnp.where(earlier, cosine, -1.0), axis=1)
    column_max = jnp.max(jnp.where(later_pair, cosine, -1.0), axis=0)
    return (row_maxima, column_max)


def local(embeddings, cluster_ids, order_index):
    groups = lax.axis_size("group")
    row_count = embeddings.shape[0]
    feature_count = embeddings.shape[1]
    capacity = 2 * row_count // groups
    unit_rows = normalize(embeddings)
    target_group = cluster_ids // CL_GROUP
    positions = jnp.arange(row_count, dtype=jnp.int32)
    same_target = target_group[:, None] == target_group[None, :]
    slot_rank = jnp.sum(same_target & (positions[None, :] < positions[:, None]), axis=1)
    slot_index = target_group * capacity + slot_rank
    slot_table = jnp.arange(groups * capacity, dtype=jnp.int32)[:, None] == slot_index[None, :]
    outgoing_rows = jnp.dot(
        slot_table.astype(jnp.bfloat16), unit_rows, preferred_element_type=jnp.float32
    )
    outgoing_rows = outgoing_rows.astype(jnp.bfloat16).reshape(groups, capacity, feature_count)
    outgoing_cluster = (
        jnp.sum(jnp.where(slot_table, cluster_ids[None, :] + 1, 0), axis=1) - 1
    ).reshape(groups, capacity)
    outgoing_order = jnp.sum(jnp.where(slot_table, order_index[None, :], 0), axis=1).reshape(
        groups, capacity
    )
    received, received_cluster, received_order = (
        lax.all_to_all(outgoing_rows, "group", split_axis=0, concat_axis=0, tiled=True),
        lax.all_to_all(outgoing_cluster, "group", split_axis=0, concat_axis=0, tiled=True),
        lax.all_to_all(outgoing_order, "group", split_axis=0, concat_axis=0, tiled=True),
    )
    received = received.reshape(groups * capacity, feature_count)
    received_cluster = received_cluster.reshape(groups * capacity)
    received_order = received_order.reshape(groups * capacity)
    position_count = groups * capacity
    start_value = jnp.full((position_count,), -1.0, dtype=jnp.float32)
    piece_rows = lax.all_gather(received, "member", axis=0, tiled=True)
    piece_cluster = lax.all_gather(received_cluster, "member", axis=0, tiled=True)
    piece_order = lax.all_gather(received_order, "member", axis=0, tiled=True)
    row_maxima, column_max = tile_maxima(
        received, received_cluster, received_order, piece_rows, piece_cluster, piece_order
    )
    best_so_far = jnp.maximum(start_value, row_maxima)
    answered = lax.all_to_all(
        best_so_far.reshape(groups, capacity), "group", split_axis=0, concat_axis=0, tiled=True
    ).reshape(position_count)
    return jnp.sum(jnp.where(slot_table, answered[:, None], 0.0), axis=0)


def solution(mesh):
    placed = (P(("group", "member"), None), P(("group", "member")), P(("group", "member")))
    return jax.shard_map(
        local, mesh=mesh, in_specs=placed, out_specs=P(("group", "member")), check_vma=False
    )
```

profile of v0, /device:TPU:0, one launch (start us, length us, event | category | flops | bytes accessed | tf_op | source)
XLA Modules:
  0.0 178.5 jit_solution(14211602882912240654)
XLA Ops:
  6.5 0.7 broadcast_add_fusion.1
  7.4 1.4 fusion
  8.8 1.8 %convolution_convert_fusion = bf16[192,4096]{1,0:T(8,128)(2,1)S(1)} fusion(bf16[96,4096]{1,0:T(8,128)(2,1)} %param.3, f32[96]{0:T(128)S(1)} %add_rsqrt_fusion, s32[96]{0:T(128)S(1)} %multiply_add_fusion), kind=kOutput, calls=%fused_computation | convolution fusion | flops 152979456 | bytes 2360064 | tf_op jit(solution)/shard_map/dot_general | solution.py:39
  10.6 24.8 %all_to_all.26 = bf16[4,48,4096]{2,1,0:T(8,128)(2,1)} all-to-all(bf16[4,48,4096]{2,1,0:T(8,128)(2,1)S(1)} %bitcast.7), channel_id=1, replica_groups=mesh['group'=4,'member'=8] {'group'}, dimensions={0} | all-to-all | bytes 3145728 | tf_op jit(solution)/shard_map/all_to_all | solution.py:50
  35.4 0.6 copy-done.1
  36.2 0.7 sub.14
  36.9 3.2 %all-to-all-start = ((s32[4,1,48]{2,1,0:T(1,128)}), s32[4,1,48]{2,1,0:T(1,128)S(1)}, u32[]{:S(2)}, u32[]{:S(2)}) async-start(s32[4,1,48]{2,1,0:T(1,128)} %sub.14), calls=%async_computation | async-start | bytes 4096 | tf_op jit(solution)/shard_map/all_to_all | solution.py:51
  40.1 0.7 all_to_all.18
  40.8 3.8 %all-to-all-done = s32[4,1,48]{2,1,0:T(1,128)S(1)} async-done(((s32[4,1,48]{2,1,0:T(1,128)}), s32[4,1,48]{2,1,0:T(1,128)S(1)}, u32[]{:S(2)}, u32[]{:S(2)}) %all-to-all-start) | async-done | bytes 800 | tf_op jit(solution)/shard_map/all_to_all | solution.py:51
  44.6 3.2 %all-to-all-start.1 = ((s32[4,1,48]{2,1,0:T(1,128)}), s32[4,1,48]{2,1,0:T(1,128)S(1)}, u32[]{:S(2)}, u32[]{:S(2)}) async-start(s32[4,1,48]{2,1,0:T(1,128)} %all_to_all.18), calls=%async_computation.1 | async-start | bytes 4096 | tf_op jit(solution)/shard_map/all_to_all | solution.py:52
  47.8 0.6 dynamic-slice
  49.0 0.5 broadcast.67
  49.6 0.7 reduce.10
  50.3 2.1 %all-to-all-done.1 = s32[4,1,48]{2,1,0:T(1,128)S(1)} async-done(((s32[4,1,48]{2,1,0:T(1,128)}), s32[4,1,48]{2,1,0:T(1,128)S(1)}, u32[]{:S(2)}, u32[]{:S(2)}) %all-to-all-start.1) | async-done | bytes 800 | tf_op jit(solution)/shard_map/all_to_all | solution.py:52
  52.4 0.7 reduce.9
  53.2 0.2 dynamic-update-slice
  53.4 0.3 dynamic-update-slice.1
  53.6 32.2 %all-reduce.2 = (s32[1536]{0:T(1024)S(1)}, s32[1536]{0:T(1024)S(1)}) all-reduce(s32[1536]{0:T(1024)S(1)} %dynamic-update-slice.1, s32[1536]{0:T(1024)S(1)} %dynamic-update-slice), channel_id=1, replica_groups=mesh['group'=4,'member'=8] {'member'}, use_global_device_ids=true, to_apply=%add.1 | all-reduce | flops 3072 | bytes 24576
  85.8 66.7 %all-gather.2.cloned.1.call-done = bf16[1536,4096]{1,0:T(8,128)(2,1)} async-done(((bf16[192,4096]{1,0:T(8,128)(2,1)}), bf16[1536,4096]{1,0:T(8,128)(2,1)}) %all-gather.2.cloned.1.call-update) | async-done | bytes 12582928 | tf_op jit(solution)/shard_map/all_gather | solution.py:59
  152.5 9.0 %fusion.2 = f32[192]{0:T(256)S(1)} fusion(bf16[192,4096]{1,0:T(8,128)(2,1)S(1)} %bitcast.6, bf16[1536,4096]{1,0:T(8,128)(2,1)} %all-gather.2.cloned.1.call-done, s32[1536]{0:T(1024)S(1)} %get-tuple-element.7, s32[1536]{0:T(1024)S(1)} %get-tuple-element.8, s32[192]{0:T(256)S(1)} %reshape.82, s32[192]{0:T(256)S(1)} %reshape.79, ...), kind=kOutput, calls=%fused_computation.6 | convolution fusion | flops 2417688320 | bytes 14170560 | tf_op jit(solution)/shard_map/dot_general | solution.py:16
  161.7 8.2 %all_to_all.27 = f32[4,1,48]{2,1,0:T(1,128)S(1)} all-to-all(f32[4,1,48]{2,1,0:T(1,128)S(1)} %max_broadcast_in_dim.15), channel_id=1, replica_groups=mesh['group'=4,'member'=8] {'group'}, dimensions={0} | all-to-all | bytes 1536 | tf_op jit(solution)/shard_map/all_to_all | solution.py:66
  169.8 0.5 broadcast.69
  170.3 0.7 reduce.11
  171.1 0.6 select_reduce_fusion
  (20 shorter events, 0.7 us)
Async XLA Ops:
  6.5 146.0 %all-gather.2.cloned.1.call-start = ((), (), s32[]{:S(2)}) async-start(), calls=%async_computation.4 | async-start | bytes 14155776 | tf_op jit(solution)/shard_map/all_gather | solution.py:59
  35.4 0.7 copy-start.1
  35.4 12.4 %copy-start.2 = (u32[32]{0:T(128)S(1)}, u32[32]{0:T(128)}, u32[]{:S(2)}) copy-start(u32[32]{0:T(128)} %constant.32) | copy-start | bytes 388
  35.4 117.1 %copy-start = (bf16[4,48,4096]{2,1,0:T(8,128)(2,1)S(1)}, bf16[4,48,4096]{2,1,0:T(8,128)(2,1)}, u32[]{:S(2)}) copy-start(bf16[4,48,4096]{2,1,0:T(8,128)(2,1)} %all_to_all.26) | copy-start | bytes 4718596
  36.9 7.7 %all-to-all-start = ((s32[4,1,48]{2,1,0:T(1,128)}), s32[4,1,48]{2,1,0:T(1,128)S(1)}, u32[]{:S(2)}, u32[]{:S(2)}) async-start(s32[4,1,48]{2,1,0:T(1,128)} %sub.14), calls=%async_computation | async-start | bytes 4096 | tf_op jit(solution)/shard_map/all_to_all | solution.py:51
  44.6 7.8 %all-to-all-start.1 = ((s32[4,1,48]{2,1,0:T(1,128)}), s32[4,1,48]{2,1,0:T(1,128)S(1)}, u32[]{:S(2)}, u32[]{:S(2)}) async-start(s32[4,1,48]{2,1,0:T(1,128)} %all_to_all.18), calls=%async_computation.1 | async-start | bytes 4096 | tf_op jit(solution)/shard_map/all_to_all | solution.py:52
Sparse Core Ops, SparseCore 0:
  35.6 116.9 all-gather.1
where the time goes:
time: 179 us
  waiting for transfers between devices  72.6 us (41%)
  blocking collectives  65.2 us (36%)
  between operations  14.1 us (8%)
  matrix products  10.8 us (6%)
  starting transfers between devices  6.42 us (4%)
  other arithmetic  5.02 us (3%)
  local copies, waits for them, and re-layouts  4.39 us (2%)
    all_gather x1, waiting for transfers between devices, local(): piece_rows = lax.all_gather(received, 'member', axis=0, tiled=True)  66.7 us
    unnamed x1, blocking collectives  32.2 us
    all_to_all x1, blocking collectives, local(): lax.all_to_all(outgoing_rows, 'group', split_axis=0, concat_axis=0, tiled...  24.8 us
    dot_general x1, matrix products, tile_maxima(): lax.dot_general(rows_left, rows_right, (((1,), (1,)), ((), ())), preferre...  9.01 us
    all_to_all x1, blocking collectives, local(): lax.all_to_all(best_so_far.reshape(groups, capacity), 'group', split_axis...  8.16 us
    all_to_all x1, waiting for transfers between devices, local(): lax.all_to_all(outgoing_cluster, 'group', split_axis=0, concat_axis=0, ti...  3.79 us
  transfers between devices with their start and end apart: 3, of which 3 were waited for; matrix products, arithmetic and copies ran while one was open for 2% of the time, Pallas kernels for 0%

commit v1 on v0

v1 whole, which is shorter than its diff:
```python
import jax
import jax.numpy as jnp
from jax import lax
from jax.sharding import Mesh, PartitionSpec as P

AXES = ("group", "z", "core")


def ring_pairs(length, shift):
    if 2 * shift < length:
        return [(k, (k + shift) % length) for k in range(length)]
    pairs = []
    for k in range(length // 2):
        low, high = k, k + shift
        pairs.append((low, high) if k % 2 == 0 else (high, low))
    return pairs


def inverse(pairs):
    return [(b, a) for a, b in pairs]


def maxima(rows, row_meta, cols, col_meta):
    dots = lax.dot_general(rows, cols, (((1,), (1,)), ((), ())), preferred_element_type=jnp.float32)
    row_scale, col_scale = row_meta[2][:, None], col_meta[2][None, :]
    live = (row_scale > 0) & (col_scale > 0)
    cosine = jnp.where(live, dots * row_scale * col_scale, 0.0)
    same = (row_meta[0][:, None] == col_meta[0][None, :]) & (row_meta[0][:, None] > 0)
    row_order, col_order = row_meta[1][:, None], col_meta[1][None, :]
    row_best = jnp.max(jnp.where(same & (col_order < row_order), cosine, -1.0), axis=1)
    col_best = jnp.max(jnp.where(same & (row_order < col_order), cosine, -1.0), axis=0)
    return row_best, col_best


def local(embeddings, cluster_ids, order_index):
    row_count, feature_count = embeddings.shape
    length = lax.axis_size("z")
    routes = [ring_pairs(length, shift) for shift in range(1, length // 2 + 1)]
    visitors = [lax.ppermute(embeddings, "z", route) for route in routes]
    plane = lax.all_gather(embeddings, ("group", "core"), axis=0, tiled=True)
    values = embeddings.astype(jnp.float32)
    scale = lax.rsqrt(jnp.sum(values * values, axis=1) + feature_count * 1e-06)
    meta = jnp.stack(
        [(cluster_ids + 1).astype(jnp.float32), order_index.astype(jnp.float32), scale]
    )
    meta = jnp.pad(meta, ((0, 5), (0, -row_count % 128)))
    plane_meta = lax.all_gather(meta, ("group", "core"), axis=0)
    plane_meta = plane_meta[:, :3, :row_count].transpose(1, 0, 2).reshape(3, -1)
    meta_visitors = [lax.ppermute(meta, "z", route)[:3, :row_count] for route in routes]
    own_meta = meta[:3, :row_count]
    best, _ = maxima(embeddings, own_meta, plane, plane_meta)
    rows = jnp.concatenate(visitors)
    row_meta = jnp.concatenate(meta_visitors, axis=1)
    row_best, col_best = maxima(rows, row_meta, plane, plane_meta)
    for index, route in enumerate(routes):
        block = row_best[index * row_count : (index + 1) * row_count]
        home = lax.ppermute(block, "z", inverse(route))
        senders = jnp.array([a for a, b in route])
        sent = jnp.any(senders == lax.axis_index("z"))
        best = jnp.maximum(best, jnp.where(sent, home, -1.0))
    parts = lax.all_to_all(
        col_best.reshape(-1, row_count), ("group", "core"), split_axis=0, concat_axis=0, tiled=True
    )
    return jnp.maximum(best, jnp.max(parts, axis=0))


def solution(mesh):
    groups, members = mesh.devices.shape
    fine = Mesh(mesh.devices.reshape(groups, members // 2, 2), AXES)
    placed = (P(AXES, None), P(AXES), P(AXES))
    return jax.shard_map(local, mesh=fine, in_specs=placed, out_specs=P(AXES), check_vma=False)
```

time: 179 us -> 85.7 us (0.48)
  blocking collectives: 65.2 us -> 9.1 us
  waiting for transfers between devices: 72.6 us -> 27.5 us
  starting transfers between devices: 6.42 us -> 17.8 us
  local copies, waits for them, and re-layouts: 4.39 us -> 1.02 us
    all_gather x1, waiting for transfers between devices: 66.7 us -> 3.11 us  [local(): plane = lax.all_gather(embeddings, ('group', 'core'), axis=0, tiled=True)]
    all_to_all x2 -> x0, blocking collectives: 33 us -> none  [the longest x1 24.8 us: local(): lax.all_to_all(outgoing_rows, 'group', split_axis=0, concat_axis=0, tiled...]
    unnamed x1 -> x0, blocking collectives: 32.2 us -> none
    ppermute x0 -> x6, waiting for transfers between devices: none -> 23.7 us  [the longest x2 23.7 us: local(): visitors = [lax.ppermute(embeddings, 'z', route) for route in routes]]
    ppermute x0 -> x6, starting transfers between devices: none -> 14.5 us  [the longest x2 6 us: local(): lax.ppermute(meta, 'z', route)[:3, :row_count]]
    all_gather x0 -> x1, blocking collectives: none -> 9.1 us  [local(): plane_meta = lax.all_gather(meta, ('group', 'core'), axis=0)]
    all_to_all x2 -> x1, waiting for transfers between devices: 5.89 us -> 0.01 us  [local(): lax.all_to_all(col_best.reshape(-1, row_count), ('group', 'core'), split_...]
    all_to_all x2 -> x1, starting transfers between devices: 6.42 us -> 3.26 us  [local(): lax.all_to_all(col_best.reshape(-1, row_count), ('group', 'core'), split_...]
  transfers between devices with their start and end apart: 3 -> 8, of which waited for: 3 -> 3; matrix products, arithmetic and copies ran while one was open for 2% -> 11% of each run, Pallas kernels for 0% -> 0%
where the time goes in v1:
time: 85.7 us; the launch traced here: 85.4 us
  waiting for transfers between devices  27.5 us (32%)
  starting transfers between devices  17.8 us (21%)
  between operations  13.5 us (16%)
  matrix products  10.4 us (12%)
  blocking collectives  9.1 us (11%)
  other arithmetic  6.02 us (7%)
  local copies, waits for them, and re-layouts  1.02 us (1%)
    ppermute x2, waiting for transfers between devices, local(): visitors = [lax.ppermute(embeddings, 'z', route) for route in routes]  23.7 us
    dot_general x2, matrix products, maxima(): lax.dot_general(rows, cols, (((1,), (1,)), ((), ())), preferred_element_t...  10.4 us
    all_gather x1, blocking collectives, local(): plane_meta = lax.all_gather(meta, ('group', 'core'), axis=0)  9.1 us
    ppermute x2, starting transfers between devices, local(): lax.ppermute(meta, 'z', route)[:3, :row_count]  6 us
    ppermute x2, starting transfers between devices, local(): home = lax.ppermute(block, 'z', inverse(route))  4.61 us
    ppermute x2, starting transfers between devices, local(): visitors = [lax.ppermute(embeddings, 'z', route) for route in routes]  3.9 us
    all_to_all x1, starting transfers between devices, local(): lax.all_to_all(col_best.reshape(-1, row_count), ('group', 'core'), split_...  3.26 us
    all_gather x1, waiting for transfers between devices, local(): plane = lax.all_gather(embeddings, ('group', 'core'), axis=0, tiled=True)  3.11 us
  transfers between devices with their start and end apart: 8, of which 3 were waited for; matrix products, arithmetic and copies ran while one was open for 11% of the time, Pallas kernels for 0%

profile of v1, /device:TPU:0, one launch (start us, length us, event | category | flops | bytes accessed | tf_op | source)
XLA Modules:
  0.0 85.4 jit_solution(9225264698700089764)
XLA Ops:
  6.5 0.7 all-gather.3.cloned.1.call-update
  7.3 1.4 %multiply_reduce_fusion = f32[96]{0:T(128)S(1)} fusion(bf16[96,4096]{1,0:T(8,128)(2,1)} %param.5), kind=kLoop, calls=%fused_computation.4 | loop fusion | flops 1179552 | bytes 786816 | tf_op jit(solution)/shard_map/reduce_sum | solution.py:42
  8.7 0.7 add_convert_fusion
  9.4 5.9 %collective-permute-start.1 = (f32[8,128]{1,0:T(8,128)S(1)}, f32[8,128]{1,0:T(8,128)S(1)}, u32[]{:S(2)}, u32[]{:S(2)}) collective-permute-start(f32[8,128]{1,0:T(8,128)S(1)} %select_maximum_fusion), channel_id=1, source_target_pairs={{0,4},{6,2},{1,5},{7,3},{8,12},{14,10},{9,13},{15,11},{16,20},{22,... | collective-permute-start | bytes 12296 | tf_op jit(solution)/shard_map/ppermute | solution.py:49
  15.4 3.8 %collective-permute-start.3 = (bf16[96,4096]{1,0:T(8,128)(2,1)}, bf16[96,4096]{1,0:T(8,128)(2,1)S(1)}, u32[]{:S(2)}, u32[]{:S(2)}) collective-permute-start(bf16[96,4096]{1,0:T(8,128)(2,1)} %param.5), channel_id=1, source_target_pairs={{0,4},{6,2},{1,5},{7,3},{8,12},{14,10},{9,13},{15,11},{16,20},{22,... | collective-permute-start | bytes 2359304 | tf_op jit(solution)/shard_map/ppermute | solution.py:39
  19.3 9.1 %all-gather = f32[64,128]{1,0:T(8,128)S(1)} all-gather(f32[8,128]{1,0:T(8,128)S(1)} %select_maximum_fusion), channel_id=2, replica_groups=mesh['group'=4,'z'=4,'core'=2] {'group','core'}, dimensions={0}, use_global_device_ids=true | all-gather | bytes 36864 | tf_op jit(solution)/shard_map/all_gather | solution.py:47
  28.4 0.1 slice.51
  28.5 0.7 broadcast_compare_fusion.4
  29.2 0.1 lt.18
  29.3 0.1 eq.43
  29.3 0.7 compare_reduce_fusion.1
  30.0 0.7 compare_reduce_fusion
  30.7 0.1 pad_maximum_fusion.1
  30.8 6.7 %collective-permute-done.3 = bf16[96,4096]{1,0:T(8,128)(2,1)S(1)} collective-permute-done((bf16[96,4096]{1,0:T(8,128)(2,1)}, bf16[96,4096]{1,0:T(8,128)(2,1)S(1)}, u32[]{:S(2)}, u32[]{:S(2)}) %collective-permute-start.3) | collective-permute-done | bytes 786464 | tf_op jit(solution)/shard_map/ppermute | solution.py:39
  37.5 17.0 %collective-permute-done.2 = bf16[96,4096]{1,0:T(8,128)(2,1)S(1)} collective-permute-done((bf16[96,4096]{1,0:T(8,128)(2,1)}, bf16[96,4096]{1,0:T(8,128)(2,1)S(1)}, u32[]{:S(2)}, u32[]{:S(2)}) %collective-permute-start.2) | collective-permute-done | bytes 786464 | tf_op jit(solution)/shard_map/ppermute | solution.py:39
  54.5 3.1 %all-gather.3.cloned.1.call-done = bf16[768,4096]{1,0:T(8,128)(2,1)} async-done(((bf16[96,4096]{1,0:T(8,128)(2,1)}), bf16[768,4096]{1,0:T(8,128)(2,1)}) %all-gather.3.cloned.1.call-update) | async-done | bytes 6291472 | tf_op jit(solution)/shard_map/all_gather | solution.py:40
  57.6 5.5 %select_reduce_fusion.1 = (f32[192]{0:T(256)S(1)}, f32[768]{0:T(1024)S(1)}) fusion(f32[768]{0:T(1024)S(1)} %lt.18, f32[768]{0:T(1024)S(1)} %eq.43, f32[192]{0:T(256)S(1)} %bitcast.20, f32[192]{0:T(256)S(1)} %bitcast.18, pred[192]{0:T(512)(128)(4,1)S(1)} %broadcast_compare_fusion.2, f32[768]{0:T(1024)S(1)} %slice.51, f32[192]{0:T(256)S(1)} %bitcast.22, ...), kind=kOutput, calls=%fused_computation.14 | convolution fusion | flops 1213168640 | bytes 7880832 | tf_op jit(solution)/shard_map/dot_general | solution.py:24
  63.1 0.7 all_to_all.6
  63.8 3.3 %all-to-all-start = ((f32[8,1,96]{2,1,0:T(1,128)}), f32[8,1,96]{2,1,0:T(1,128)S(1)}, u32[]{:S(2)}, u32[]{:S(2)}) async-start(f32[8,1,96]{2,1,0:T(1,128)} %all_to_all.6), calls=%async_computation | async-start | bytes 8192 | tf_op jit(solution)/shard_map/all_to_all | solution.py:61
  67.0 0.1 fusion.23
  67.1 3.3 %collective-permute-start.4 = (f32[96]{0:T(128)S(1)}, f32[96]{0:T(128)S(1)}, u32[]{:S(2)}, u32[]{:S(2)}) collective-permute-start(f32[96]{0:T(128)S(1)} %get-tuple-element.14), channel_id=1, source_target_pairs={{2,0},{4,2},{6,4},{0,6},{3,1},{5,3},{7,5},{1,7},{10,8},{12,10},{14... | collective-permute-start | bytes 1160 | tf_op jit(solution)/shard_map/ppermute | solution.py:57
  70.4 1.3 %collective-permute-start.5 = (f32[96]{0:T(128)S(1)}, f32[96]{0:T(128)S(1)}, u32[]{:S(2)}, u32[]{:S(2)}) collective-permute-start(f32[96]{0:T(128)S(1)} %get-tuple-element.13), channel_id=1, source_target_pairs={{4,0},{2,6},{5,1},{3,7},{12,8},{10,14},{13,9},{11,15},{20,16},{18,... | collective-permute-start | bytes 1160 | tf_op jit(solution)/shard_map/ppermute | solution.py:57
  71.7 5.0 %fusion.16 = f32[96]{0:T(128)S(1)} fusion(bf16[96,4096]{1,0:T(8,128)(2,1)S(1)} %copy-done, bf16[768,4096]{1,0:T(8,128)(2,1)} %all-gather.3.cloned.1.call-done, f32[768]{0:T(1024)S(1)} %slice.51, f32[96]{0:T(128)S(1)} %get-tuple-element.19, f32[768]{0:T(1024)S(1)} %lt.18, f32[768]{0:T(1024)S(1)} %eq.43, f32[96]{0:T(128)S(1)} %get-tuple-element.22, ...), kind=kOutput, calls=%fused_computation.12 | convolution fusion | flops 604716928 | bytes 7089600 | tf_op jit(solution)/shard_map/dot_general | solution.py:24
  76.8 1.8 %fusion.19 = f32[96]{0:T(128)} fusion(f32[96]{0:T(128)S(1)} %reduce_max.39, f32[96]{0:T(128)S(1)} %fusion.16, f32[96]{0:T(128)S(1)} %collective-permute-done.4, pred[]{:T(512)} %compare_reduce_fusion.1, f32[96]{0:T(128)S(1)} %collective-permute-done.5, pred[]{:T(512)} %compare_reduce_fusion), kind=kLoop, calls=%fused_computation.34 | loop fusion | flops 480 | bytes 1922 | tf_op jit(solution)/shard_map/max | solution.py:64
  (21 shorter events, 0.3 us)
Async XLA Ops:
  6.5 51.1 %all-gather.3.cloned.1.call-start = ((), (), s32[]{:S(2)}) async-start(), calls=%async_computation.1 | async-start | bytes 7077888 | tf_op jit(solution)/shard_map/all_gather | solution.py:40
  9.4 21.3 %collective-permute-start.1 = (f32[8,128]{1,0:T(8,128)S(1)}, f32[8,128]{1,0:T(8,128)S(1)}, u32[]{:S(2)}, u32[]{:S(2)}) collective-permute-start(f32[8,128]{1,0:T(8,128)S(1)} %select_maximum_fusion), channel_id=1, source_target_pairs={{0,4},{6,2},{1,5},{7,3},{8,12},{14,10},{9,13},{15,11},{16,20},{22,... | collective-permute-start | bytes 12296 | tf_op jit(solution)/shard_map/ppermute | solution.py:49
  15.3 15.4 %collective-permute-start = (f32[8,128]{1,0:T(8,128)S(1)}, f32[8,128]{1,0:T(8,128)S(1)}, u32[]{:S(2)}, u32[]{:S(2)}) collective-permute-start(f32[8,128]{1,0:T(8,128)S(1)} %select_maximum_fusion), channel_id=1, source_target_pairs={{0,2},{2,4},{4,6},{6,0},{1,3},{3,5},{5,7},{7,1},{8,10},{10,12},{12... | collective-permute-start | bytes 12296 | tf_op jit(solution)/shard_map/ppermute | solution.py:49
  15.4 22.1 %collective-permute-start.3 = (bf16[96,4096]{1,0:T(8,128)(2,1)}, bf16[96,4096]{1,0:T(8,128)(2,1)S(1)}, u32[]{:S(2)}, u32[]{:S(2)}) collective-permute-start(bf16[96,4096]{1,0:T(8,128)(2,1)} %param.5), channel_id=1, source_target_pairs={{0,4},{6,2},{1,5},{7,3},{8,12},{14,10},{9,13},{15,11},{16,20},{22,... | collective-permute-start | bytes 2359304 | tf_op jit(solution)/shard_map/ppermute | solution.py:39
  19.2 35.3 %collective-permute-start.2 = (bf16[96,4096]{1,0:T(8,128)(2,1)}, bf16[96,4096]{1,0:T(8,128)(2,1)S(1)}, u32[]{:S(2)}, u32[]{:S(2)}) collective-permute-start(bf16[96,4096]{1,0:T(8,128)(2,1)} %param.5), channel_id=1, source_target_pairs={{0,2},{2,4},{4,6},{6,0},{1,3},{3,5},{5,7},{7,1},{8,10},{10,12},{12... | collective-permute-start | bytes 2359304 | tf_op jit(solution)/shard_map/ppermute | solution.py:39
  57.6 14.1 %copy-start = (bf16[96,4096]{1,0:T(8,128)(2,1)S(1)}, bf16[96,4096]{1,0:T(8,128)(2,1)}, u32[]{:S(2)}) copy-start(bf16[96,4096]{1,0:T(8,128)(2,1)} %param.5) | copy-start | bytes 2359300
  63.8 12.9 %all-to-all-start = ((f32[8,1,96]{2,1,0:T(1,128)}), f32[8,1,96]{2,1,0:T(1,128)S(1)}, u32[]{:S(2)}, u32[]{:S(2)}) async-start(f32[8,1,96]{2,1,0:T(1,128)} %all_to_all.6), calls=%async_computation | async-start | bytes 8192 | tf_op jit(solution)/shard_map/all_to_all | solution.py:61
  67.1 9.6 %collective-permute-start.4 = (f32[96]{0:T(128)S(1)}, f32[96]{0:T(128)S(1)}, u32[]{:S(2)}, u32[]{:S(2)}) collective-permute-start(f32[96]{0:T(128)S(1)} %get-tuple-element.14), channel_id=1, source_target_pairs={{2,0},{4,2},{6,4},{0,6},{3,1},{5,3},{7,5},{1,7},{10,8},{12,10},{14... | collective-permute-start | bytes 1160 | tf_op jit(solution)/shard_map/ppermute | solution.py:57
  70.4 6.3 %collective-permute-start.5 = (f32[96]{0:T(128)S(1)}, f32[96]{0:T(128)S(1)}, u32[]{:S(2)}, u32[]{:S(2)}) collective-permute-start(f32[96]{0:T(128)S(1)} %get-tuple-element.13), channel_id=1, source_target_pairs={{4,0},{2,6},{5,1},{3,7},{12,8},{10,14},{13,9},{11,15},{20,16},{18,... | collective-permute-start | bytes 1160 | tf_op jit(solution)/shard_map/ppermute | solution.py:57
Sparse Core Ops, SparseCore 0:
  9.2 48.3 all-gather.2

commit v2 on v1

v2 whole, which is shorter than its diff:
```python
import functools

import jax
import jax.numpy as jnp
from jax import lax
from jax.experimental import pallas as pl
from jax.experimental.pallas import tpu as pltpu
from jax.sharding import Mesh, PartitionSpec as P

AXES = ("group", "z", "core")
LANES = 128
CHUNK = 512
PER_CALL = 8


def ring_pairs(length, shift):
    if 2 * shift < length:
        return [(k, (k + shift) % length) for k in range(length)]
    pairs = []
    for k in range(length // 2):
        low, high = k, k + shift
        pairs.append((low, high) if k % 2 == 0 else (high, low))
    return pairs


def inverse(pairs):
    return [(b, a) for a, b in pairs]


def unit_rows(values):
    values = values.astype(jnp.float32)
    total = jnp.sum(values * values, axis=1, keepdims=True) + values.shape[1] * 1e-06
    return (values * lax.rsqrt(total)).astype(jnp.bfloat16)


def normalize_kernel(rows_ref, unit_ref):
    unit_ref[...] = unit_rows(rows_ref[...])


def normalize(rows):
    count, width = rows.shape
    step = 32
    spec = pl.BlockSpec((step, width), lambda i: (i, 0))
    return pl.pallas_call(
        normalize_kernel,
        grid=(count // step,),
        in_specs=[spec],
        out_specs=spec,
        out_shape=jax.ShapeDtypeStruct(rows.shape, jnp.bfloat16),
        cost_estimate=pl.CostEstimate(
            flops=4 * count * width, bytes_accessed=4 * count * width, transcendentals=count
        ),
    )(rows)


def device_index(group, z, core):
    return (group * lax.axis_size("z") + z) * lax.axis_size("core") + core


def source_of(route):
    z = lax.axis_index("z")
    source, valid = jnp.int32(0), jnp.int32(0)
    for a, b in route:
        source = jnp.where(z == b, a, source)
        valid = jnp.where(z == b, 1, valid)
    return source, valid


def maxima_kernel(routes, offsets, own, *refs):
    count = len(offsets)
    visitors = len(routes) + own
    meta_ref, refs = refs[0], refs[1:]
    own_ref, refs = (refs[0], refs[1:]) if own else (None, refs)
    visitor_refs, refs = refs[: len(routes)], refs[len(routes) :]
    block_refs, refs = refs[:count], refs[count:]
    carry_ref, refs = (None, refs) if own else (refs[0], refs[1:])
    row_ref, col_ref, units, dots = refs
    rows, width = block_refs[0].shape

    for v in range(visitors):
        start = v * LANES
        if rows < LANES:
            units[start + rows : start + LANES, :] = jnp.zeros((LANES - rows, width), jnp.bfloat16)
        if own and v == 0:
            units[start : start + rows, :] = own_ref[...]
        else:
            units[start : start + rows, :] = unit_rows(visitor_refs[v - own][...])
    for k in range(0, width, CHUNK):
        left = jnp.concatenate([ref[:, k : k + CHUNK] for ref in block_refs], axis=0)
        part = lax.dot_general(
            left,
            units[:, k : k + CHUNK],
            (((1,), (1,)), ((), ())),
            preferred_element_type=jnp.float32,
        )
        dots[...] = part if k == 0 else dots[...] + part

    group, z, core = (lax.axis_index(name) for name in AXES)
    visitor_meta = []
    if own:
        visitor_meta.append(meta_ref[device_index(group, z, core)])
    for route in routes:
        source, valid = source_of(route)
        visitor_meta.append(meta_ref[device_index(group, source, core)] * valid.astype(jnp.float32))
    row_best = [jnp.full((1, LANES), -1.0, jnp.float32) for _ in range(visitors)]
    lane = lax.broadcasted_iota(jnp.int32, (rows, LANES), 1)
    col_all = jnp.full((rows, LANES), -1.0, jnp.float32)
    for j, (s, c) in enumerate(offsets):
        block_meta = meta_ref[device_index(group ^ s, z, core ^ c)]
        turned = block_meta.T
        block_cluster, block_order = turned[:rows, 0:1], turned[:rows, 1:2]
        col_best = jnp.full((rows, 1), -1.0, jnp.float32)
        for v in range(visitors):
            cosine = dots[j * rows : (j + 1) * rows, v * LANES : (v + 1) * LANES]
            cluster, order = visitor_meta[v][0:1, :], visitor_meta[v][1:2, :]
            same = (block_cluster == cluster) & (cluster > 0)
            seen = jnp.where(same & (block_order < order), cosine, -1.0)
            row_best[v] = jnp.maximum(row_best[v], jnp.max(seen, axis=0, keepdims=True))
            if not (own and v == 0):
                seen = jnp.where(same & (order < block_order), cosine, -1.0)
                col_best = jnp.maximum(col_best, jnp.max(seen, axis=1, keepdims=True))
        col_all = jnp.where(lane == j, col_best, col_all)
    for v in range(visitors):
        row_ref[v] = row_best[v]
    if rows < LANES:
        col_all = jnp.concatenate(
            [col_all, jnp.full((LANES - rows, LANES), -1.0, jnp.float32)], axis=0
        )
    turned = col_all.T
    for j, (s, c) in enumerate(offsets):
        place = ((group ^ s) % (PER_CALL // 2)) * 2 + (core ^ c)
        best = turned[j : j + 1, :]
        col_ref[place] = best if own else jnp.maximum(best, carry_ref[place])


def maxima(routes, offsets, meta, own, visitors, blocks, carry=None):
    count = len(visitors) + (own is not None)
    rows, width = blocks[0].shape
    row_best, col_best = None, []
    for first in range(0, len(blocks), PER_CALL):
        part = blocks[first : first + PER_CALL]
        operands = [meta] + ([own] if own is not None else []) + list(visitors) + part
        if own is None:
            operands.append(carry[first // PER_CALL])
        row, col = pl.pallas_call(
            functools.partial(
                maxima_kernel, routes, offsets[first : first + PER_CALL], int(own is not None)
            ),
            in_specs=[pl.BlockSpec(memory_space=pltpu.VMEM)] * len(operands),
            out_specs=[pl.BlockSpec(memory_space=pltpu.VMEM)] * 2,
            out_shape=[
                jax.ShapeDtypeStruct((count, 1, LANES), jnp.float32),
                jax.ShapeDtypeStruct((len(part), 1, LANES), jnp.float32),
            ],
            scratch_shapes=[
                pltpu.VMEM((count * LANES, width), jnp.bfloat16),
                pltpu.VMEM((len(part) * rows, count * LANES), jnp.float32),
            ],
            compiler_params=pltpu.CompilerParams(vmem_limit_bytes=40 * 2**20),
            cost_estimate=pl.CostEstimate(
                flops=2 * len(part) * rows * count * LANES * width,
                bytes_accessed=2 * (len(part) + count) * rows * width,
                transcendentals=0,
            ),
        )(*operands)
        row_best = row if row_best is None else jnp.maximum(row_best, row)
        col_best.append(col)
    return row_best, col_best


def local(embeddings, cluster_ids, order_index):
    rows, width = embeddings.shape
    groups, length = lax.axis_size("group"), lax.axis_size("z")
    routes = [ring_pairs(length, shift) for shift in range(1, length // 2 + 1)]
    visitors = [lax.ppermute(embeddings, "z", route) for route in routes]
    meta = jnp.stack([(cluster_ids + 1).astype(jnp.float32), order_index.astype(jnp.float32)])
    meta = jnp.pad(meta, ((0, 6), (0, LANES - rows)))
    meta = lax.all_gather(meta, AXES, axis=0)

    unit = normalize(embeddings)
    offsets, blocks = [], []
    for s in range(groups):
        block = unit
        if s:
            block = lax.ppermute(unit, "group", [(k, k ^ s) for k in range(groups)])
        other = lax.ppermute(block, "core", [(0, 1), (1, 0)])
        offsets += [(s, 0), (s, 1)]
        blocks += [block, other]

    row_early, col_early = maxima(routes[:-1], offsets, meta, unit, visitors[:-1], blocks)
    best = row_early[0, 0]
    for index, route in enumerate(routes[:-1]):
        best = jnp.maximum(best, lax.ppermute(row_early[index + 1, 0], "z", inverse(route)))
    row_late, col_late = maxima(
        routes[-1:], offsets, meta, None, visitors[-1:], blocks, col_early
    )
    home = lax.ppermute(row_late[0, 0], "z", inverse(routes[-1]))
    sent = jnp.any(jnp.array([a for a, b in routes[-1]]) == lax.axis_index("z"))
    best = jnp.maximum(best, jnp.where(sent, home, -1.0))
    if len(col_late) > 1:
        turn = (lax.axis_index("group") // (PER_CALL // 2)) ^ jnp.arange(len(col_late))
        col = jnp.stack(col_late)[turn].reshape(-1, 1, LANES)
    else:
        col = col_late[0]
    parts = lax.all_to_all(col, ("group", "core"), split_axis=0, concat_axis=0, tiled=True)
    return jnp.maximum(best, jnp.max(parts, axis=(0, 1)))[:rows]


def solution(mesh):
    groups, members = mesh.devices.shape
    fine = Mesh(mesh.devices.reshape(groups, members // 2, 2), AXES)
    placed = (P(AXES, None), P(AXES), P(AXES))
    return jax.shard_map(local, mesh=fine, in_specs=placed, out_specs=P(AXES), check_vma=False)
```

time: 85.7 us -> 117 us (1.37)
  blocking collectives: 9.1 us -> 52.1 us
  between operations: 13.5 us -> 0.11 us
  matrix products: 10.4 us -> 0 us
  waiting for transfers between devices: 27.5 us -> 36.8 us
  Pallas kernels: 0 us -> 8.25 us
  other arithmetic: 6.02 us -> 1.87 us
  starting transfers between devices: 17.8 us -> 16.2 us
    all_gather x1, blocking collectives: 9.1 us -> 52.1 us  [local(): meta = lax.all_gather(meta, AXES, axis=0)]
    ppermute x4 -> x9, waiting for transfers between devices: 0.03 us -> 34.2 us  [the longest x3 32.5 us: local(): block = lax.ppermute(unit, 'group', [(k, k ^ s) for k in range(groups)])]
    ppermute x2, waiting for transfers between devices: 23.7 us -> 0.01 us  [local(): visitors = [lax.ppermute(embeddings, 'z', route) for route in routes]]
    dot_general x2 -> x0, matrix products: 10.4 us -> none  [maxima(): lax.dot_general(rows, cols, (((1,), (1,)), ((), ())), preferred_element_t...]
    pallas_call x0 -> x3, Pallas kernels: none -> 8.25 us  [the longest x2 5.13 us: maxima(): pl.pallas_call(functools.partial(maxima_kernel, routes, offsets[first:fir...]
    ppermute x4 -> x9, starting transfers between devices: 10.6 us -> 6.34 us  [the longest x3 4.47 us: local(): block = lax.ppermute(unit, 'group', [(k, k ^ s) for k in range(groups)])]
    all_gather x1 -> x0, waiting for transfers between devices: 3.11 us -> none  [local(): plane = lax.all_gather(embeddings, ('group', 'core'), axis=0, tiled=True)]
    ppermute x2, starting transfers between devices: 3.9 us -> 6.57 us  [local(): visitors = [lax.ppermute(embeddings, 'z', route) for route in routes]]
  transfers between devices with their start and end apart: 8 -> 12, of which waited for: 3 -> 4; matrix products, arithmetic and copies ran while one was open for 11% -> 1% of each run, Pallas kernels for 0% -> 2%
where the time goes in v2:
time: 117 us; the launch traced here: 116 us
  blocking collectives  52.1 us (45%)
  waiting for transfers between devices  36.8 us (31%)
  starting transfers between devices  16.2 us (14%)
  Pallas kernels  8.25 us (7%)
  other arithmetic  1.87 us (2%)
    all_gather x1, blocking collectives, local(): meta = lax.all_gather(meta, AXES, axis=0)  52.1 us
    ppermute x3, waiting for transfers between devices, local(): block = lax.ppermute(unit, 'group', [(k, k ^ s) for k in range(groups)])  32.5 us
    ppermute x2, starting transfers between devices, local(): visitors = [lax.ppermute(embeddings, 'z', route) for route in routes]  6.57 us
    pallas_call x2, Pallas kernels, maxima(): pl.pallas_call(functools.partial(maxima_kernel, routes, offsets[first:fir...  5.13 us
    ppermute x3, starting transfers between devices, local(): block = lax.ppermute(unit, 'group', [(k, k ^ s) for k in range(groups)])  4.47 us
    all_to_all x1, starting transfers between devices, local(): lax.all_to_all(col, ('group', 'core'), split_axis=0, concat_axis=0, tiled...  3.29 us
    pallas_call x1, Pallas kernels, normalize(): pl.pallas_call(normalize_kernel, grid=(count // step,), in_specs=[spec],...  3.11 us
    all_to_all x1, waiting for transfers between devices, local(): lax.all_to_all(col, ('group', 'core'), split_axis=0, concat_axis=0, tiled...  2.51 us
  transfers between devices with their start and end apart: 12, of which 4 were waited for; matrix products, arithmetic and copies ran while one was open for 1% of the time, Pallas kernels for 2%

profile of v2, /device:TPU:0, one launch (start us, length us, event | category | flops | bytes accessed | tf_op | source)
XLA Modules:
  0.0 116.4 jit_solution(345033556952420642)
XLA Ops:
  0.0 3.1 %shard_map.46.refs_1_.refs_3_.refs_2_ = bf16[96,4096]{1,0:T(8,128)(2,1)} custom-call(bf16[96,4096]{1,0:T(8,128)(2,1)} %rows_ref.1), custom_call_target="tpu_custom_call" | custom-call | flops 1572864 | bytes 1572864 | tf_op jit(solution)/shard_map/pallas_call | solution.py:44
  3.1 2.9 %collective-permute-start.2 = (bf16[96,4096]{1,0:T(8,128)(2,1)}, bf16[96,4096]{1,0:T(8,128)(2,1)S(1)}, u32[]{:S(2)}, u32[]{:S(2)}) collective-permute-start(bf16[96,4096]{1,0:T(8,128)(2,1)} %shard_map.46.refs_1_.refs_3_.refs_2_), channel_id=1, source_target_pairs={{0,8},{8,0},{16,24},{24,16},{1,9},{9,1},{17,25},{25,17},{2,10},{10... | collective-permute-start | bytes 2359304 | tf_op jit(solution)/shard_map/ppermute | solution.py:185
  6.1 1.5 %collective-permute-start.4 = (bf16[96,4096]{1,0:T(8,128)(2,1)}, bf16[96,4096]{1,0:T(8,128)(2,1)S(1)}, u32[]{:S(2)}, u32[]{:S(2)}) collective-permute-start(bf16[96,4096]{1,0:T(8,128)(2,1)} %shard_map.46.refs_1_.refs_3_.refs_2_), channel_id=1, source_target_pairs={{0,16},{8,24},{16,0},{24,8},{1,17},{9,25},{17,1},{25,9},{2,18},{10... | collective-permute-start | bytes 2359304 | tf_op jit(solution)/shard_map/ppermute | solution.py:185
  7.6 0.0 collective-permute-start.6
  7.6 0.0 collective-permute-start.1
  7.6 2.0 %collective-permute-start = (bf16[96,4096]{1,0:T(8,128)(2,1)S(1)}, bf16[96,4096]{1,0:T(8,128)(2,1)S(1)}, u32[]{:S(2)}, u32[]{:S(2)}) collective-permute-start(bf16[96,4096]{1,0:T(8,128)(2,1)S(1)} %copy-done.1), channel_id=1, source_target_pairs={{0,2},{2,4},{4,6},{6,0},{1,3},{3,5},{5,7},{7,1},{8,10},{10,12},{12... | collective-permute-start | bytes 2359304 | tf_op jit(solution)/shard_map/ppermute | solution.py:175
  9.6 15.0 %collective-permute-done.2.refs_5_.refs_4_ = bf16[96,4096]{1,0:T(8,128)(2,1)S(1)} collective-permute-done((bf16[96,4096]{1,0:T(8,128)(2,1)}, bf16[96,4096]{1,0:T(8,128)(2,1)S(1)}, u32[]{:S(2)}, u32[]{:S(2)}) %collective-permute-start.2) | collective-permute-done | bytes 786464 | tf_op jit(solution)/shard_map/ppermute | solution.py:185
  24.6 0.0 collective-permute-start.3
  24.6 17.5 %collective-permute-done.4.refs_7_.refs_6_ = bf16[96,4096]{1,0:T(8,128)(2,1)S(1)} collective-permute-done((bf16[96,4096]{1,0:T(8,128)(2,1)}, bf16[96,4096]{1,0:T(8,128)(2,1)S(1)}, u32[]{:S(2)}, u32[]{:S(2)}) %collective-permute-start.4) | collective-permute-done | bytes 786464 | tf_op jit(solution)/shard_map/ppermute | solution.py:185
  42.1 0.0 collective-permute-start.5
  42.1 0.0 collective-permute-done.6.refs_9_.refs_8_
  42.1 0.5 collective-permute-start.7
  42.6 4.5 %collective-permute-start.9 = (bf16[96,4096]{1,0:T(8,128)(2,1)S(1)}, bf16[96,4096]{1,0:T(8,128)(2,1)S(1)}, u32[]{:S(2)}, u32[]{:S(2)}) collective-permute-start(bf16[96,4096]{1,0:T(8,128)(2,1)S(1)} %copy-done.1), channel_id=1, source_target_pairs={{0,4},{6,2},{1,5},{7,3},{8,12},{14,10},{9,13},{15,11},{16,20},{22,... | collective-permute-start | bytes 2359304 | tf_op jit(solution)/shard_map/ppermute | solution.py:175
  47.2 52.1 %all-gather = f32[256,128]{1,0:T(8,128)S(1)} all-gather(f32[8,128]{1,0:T(8,128)S(1)} %select_maximum_fusion), channel_id=2, replica_groups=mesh['group'=4,'z'=4,'core'=2] {'group','z','core'}, dimensions={0}, use_global_device_ids=true | all-gather | bytes 135168 | tf_op jit(solution)/shard_map/all_gather | solution.py:178
  99.3 1.1 copy-done
  100.5 2.3 %shard_map.47 = (f32[2,1,128]{2,1,0:T(1,128)S(1)}, f32[8,1,128]{2,1,0:T(1,128)S(1)}) custom-call(f32[32,8,128]{2,1,0:T(8,128)S(1)} %bitcast.13, bf16[96,4096]{1,0:T(8,128)(2,1)S(1)} %copy-done, bf16[96,4096]{1,0:T(8,128)(2,1)S(1)} %collective-permute-done.refs_2_, bf16[96,4096]{1,0:T(8,128)(2,1)S(1)} %copy-done, ...), custom_call_target="tpu_custom_call" | custom-call | flops 1610612736 | bytes 7864320 | tf_op jit(solution)/shard_map/pallas_call | solution.py:145
  102.7 2.8 %shard_map.48 = (f32[1,1,128]{2,1,0:T(1,128)S(1)}, f32[8,1,128]{2,1,0:T(1,128)}) custom-call(f32[32,8,128]{2,1,0:T(8,128)S(1)} %bitcast.14, bf16[96,4096]{1,0:T(8,128)(2,1)S(1)} %collective-permute-done.9.refs_1_, bf16[96,4096]{1,0:T(8,128)(2,1)S(1)} %copy-done, bf16[96,4096]{1,0:T(8,128)(2,1)S(1)} %collective-permute-done.1.refs_4_.refs_3_, ...), custom_call_target="tpu_custom_call" | custom-call | flops 805306368 | bytes 7077888 | tf_op jit(solution)/shard_map/pallas_call | solution.py:145
  105.6 3.3 %all-to-all-start = ((f32[8,1,128]{2,1,0:T(1,128)}), f32[8,1,128]{2,1,0:T(1,128)S(1)}, u32[]{:S(2)}, u32[]{:S(2)}) async-start(f32[8,1,128]{2,1,0:T(1,128)} %get-tuple-element.12), calls=%async_computation | async-start | bytes 8192 | tf_op jit(solution)/shard_map/all_to_all | solution.py:205
  108.9 1.3 %collective-permute-start.10 = (f32[128]{0:T(128)S(1)}, f32[128]{0:T(128)S(1)}, u32[]{:S(2)}, u32[]{:S(2)}) collective-permute-start(f32[128]{0:T(128)S(1)} %bitcast.15), channel_id=1, source_target_pairs={{4,0},{2,6},{5,1},{3,7},{12,8},{10,14},{13,9},{11,15},{20,16},{18,... | collective-permute-start | bytes 1544 | tf_op jit(solution)/shard_map/ppermute | solution.py:197
  110.2 0.1 collective-permute-start.8
  110.3 0.7 compare_reduce_fusion
  111.0 2.5 %all-to-all-done = f32[8,1,128]{2,1,0:T(1,128)S(1)} async-done(((f32[8,1,128]{2,1,0:T(1,128)}), f32[8,1,128]{2,1,0:T(1,128)S(1)}, u32[]{:S(2)}, u32[]{:S(2)}) %all-to-all-start) | async-done | bytes 4128 | tf_op jit(solution)/shard_map/all_to_all | solution.py:205
  113.5 1.8 %collective-permute-done.10 = f32[128]{0:T(128)S(1)} collective-permute-done((f32[128]{0:T(128)S(1)}, f32[128]{0:T(128)S(1)}, u32[]{:S(2)}, u32[]{:S(2)}) %collective-permute-start.10) | collective-permute-done | bytes 544 | tf_op jit(solution)/shard_map/ppermute | solution.py:197
  115.3 1.1 fusion.1
  (18 shorter events, 0.1 us)
Async XLA Ops:
  0.0 7.6 %copy-start.1 = (bf16[96,4096]{1,0:T(8,128)(2,1)S(1)}, bf16[96,4096]{1,0:T(8,128)(2,1)}, u32[]{:S(2)}) copy-start(bf16[96,4096]{1,0:T(8,128)(2,1)} %rows_ref.1) | copy-start | bytes 2359300
  3.1 44.1 %copy-start.2 = (s32[96]{0:T(128)S(1)}, s32[96]{0:T(128)}, u32[]{:S(2)}) copy-start(s32[96]{0:T(128)} %param.6) | copy-start | bytes 1156
  3.1 44.1 %copy-start.3 = (s32[96]{0:T(128)S(1)}, s32[96]{0:T(128)}, u32[]{:S(2)}) copy-start(s32[96]{0:T(128)} %param.5) | copy-start | bytes 1156
  3.1 21.5 %collective-permute-start.2 = (bf16[96,4096]{1,0:T(8,128)(2,1)}, bf16[96,4096]{1,0:T(8,128)(2,1)S(1)}, u32[]{:S(2)}, u32[]{:S(2)}) collective-permute-start(bf16[96,4096]{1,0:T(8,128)(2,1)} %shard_map.46.refs_1_.refs_3_.refs_2_), channel_id=1, source_target_pairs={{0,8},{8,0},{16,24},{24,16},{1,9},{9,1},{17,25},{25,17},{2,10},{10... | collective-permute-start | bytes 2359304 | tf_op jit(solution)/shard_map/ppermute | solution.py:185
  6.1 36.1 %collective-permute-start.4 = (bf16[96,4096]{1,0:T(8,128)(2,1)}, bf16[96,4096]{1,0:T(8,128)(2,1)S(1)}, u32[]{:S(2)}, u32[]{:S(2)}) collective-permute-start(bf16[96,4096]{1,0:T(8,128)(2,1)} %shard_map.46.refs_1_.refs_3_.refs_2_), channel_id=1, source_target_pairs={{0,16},{8,24},{16,0},{24,8},{1,17},{9,25},{17,1},{25,9},{2,18},{10... | collective-permute-start | bytes 2359304 | tf_op jit(solution)/shard_map/ppermute | solution.py:185
  7.6 34.6 %collective-permute-start.6 = (bf16[96,4096]{1,0:T(8,128)(2,1)}, bf16[96,4096]{1,0:T(8,128)(2,1)S(1)}, u32[]{:S(2)}, u32[]{:S(2)}) collective-permute-start(bf16[96,4096]{1,0:T(8,128)(2,1)} %shard_map.46.refs_1_.refs_3_.refs_2_), channel_id=1, source_target_pairs={{0,24},{8,16},{16,8},{24,0},{1,25},{9,17},{17,9},{25,1},{2,26},{10... | collective-permute-start | bytes 2359304 | tf_op jit(solution)/shard_map/ppermute | solution.py:185
  7.6 35.0 %collective-permute-start.1 = (bf16[96,4096]{1,0:T(8,128)(2,1)}, bf16[96,4096]{1,0:T(8,128)(2,1)S(1)}, u32[]{:S(2)}, u32[]{:S(2)}) collective-permute-start(bf16[96,4096]{1,0:T(8,128)(2,1)} %shard_map.46.refs_1_.refs_3_.refs_2_), channel_id=1, source_target_pairs={{0,1},{1,0},{2,3},{3,2},{4,5},{5,4},{6,7},{7,6},{8,9},{9,8},{10,11... | collective-permute-start | bytes 2359304 | tf_op jit(solution)/shard_map/ppermute | solution.py:186
  7.6 91.7 %collective-permute-start = (bf16[96,4096]{1,0:T(8,128)(2,1)S(1)}, bf16[96,4096]{1,0:T(8,128)(2,1)S(1)}, u32[]{:S(2)}, u32[]{:S(2)}) collective-permute-start(bf16[96,4096]{1,0:T(8,128)(2,1)S(1)} %copy-done.1), channel_id=1, source_target_pairs={{0,2},{2,4},{4,6},{6,0},{1,3},{3,5},{5,7},{7,1},{8,10},{10,12},{12... | collective-permute-start | bytes 2359304 | tf_op jit(solution)/shard_map/ppermute | solution.py:175
  24.6 74.7 %collective-permute-start.3 = (bf16[96,4096]{1,0:T(8,128)(2,1)S(1)}, bf16[96,4096]{1,0:T(8,128)(2,1)S(1)}, u32[]{:S(2)}, u32[]{:S(2)}) collective-permute-start(bf16[96,4096]{1,0:T(8,128)(2,1)S(1)} %collective-permute-done.2.refs_5_.refs_4_), channel_id=1, source_target_pairs={{0,1},{1,0},{2,3},{3,2},{4,5},{5,4},{6,7},{7,6},{8,9},{9,8},{10,11... | collective-permute-start | bytes 2359304 | tf_op jit(solution)/shard_map/ppermute | solution.py:186
  42.1 57.2 %collective-permute-start.5 = (bf16[96,4096]{1,0:T(8,128)(2,1)S(1)}, bf16[96,4096]{1,0:T(8,128)(2,1)S(1)}, u32[]{:S(2)}, u32[]{:S(2)}) collective-permute-start(bf16[96,4096]{1,0:T(8,128)(2,1)S(1)} %collective-permute-done.4.refs_7_.refs_6_), channel_id=1, source_target_pairs={{0,1},{1,0},{2,3},{3,2},{4,5},{5,4},{6,7},{7,6},{8,9},{9,8},{10,11... | collective-permute-start | bytes 2359304 | tf_op jit(solution)/shard_map/ppermute | solution.py:186
  42.1 57.2 %collective-permute-start.7 = (bf16[96,4096]{1,0:T(8,128)(2,1)S(1)}, bf16[96,4096]{1,0:T(8,128)(2,1)S(1)}, u32[]{:S(2)}, u32[]{:S(2)}) collective-permute-start(bf16[96,4096]{1,0:T(8,128)(2,1)S(1)} %collective-permute-done.6.refs_9_.refs_8_), channel_id=1, source_target_pairs={{0,1},{1,0},{2,3},{3,2},{4,5},{5,4},{6,7},{7,6},{8,9},{9,8},{10,11... | collective-permute-start | bytes 2359304 | tf_op jit(solution)/shard_map/ppermute | solution.py:186
  42.6 60.1 %collective-permute-start.9 = (bf16[96,4096]{1,0:T(8,128)(2,1)S(1)}, bf16[96,4096]{1,0:T(8,128)(2,1)S(1)}, u32[]{:S(2)}, u32[]{:S(2)}) collective-permute-start(bf16[96,4096]{1,0:T(8,128)(2,1)S(1)} %copy-done.1), channel_id=1, source_target_pairs={{0,4},{6,2},{1,5},{7,3},{8,12},{14,10},{9,13},{15,11},{16,20},{22,... | collective-permute-start | bytes 2359304 | tf_op jit(solution)/shard_map/ppermute | solution.py:175
  99.3 1.1 copy-start
  105.6 7.9 %all-to-all-start = ((f32[8,1,128]{2,1,0:T(1,128)}), f32[8,1,128]{2,1,0:T(1,128)S(1)}, u32[]{:S(2)}, u32[]{:S(2)}) async-start(f32[8,1,128]{2,1,0:T(1,128)} %get-tuple-element.12), calls=%async_computation | async-start | bytes 8192 | tf_op jit(solution)/shard_map/all_to_all | solution.py:205
  108.9 6.4 %collective-permute-start.10 = (f32[128]{0:T(128)S(1)}, f32[128]{0:T(128)S(1)}, u32[]{:S(2)}, u32[]{:S(2)}) collective-permute-start(f32[128]{0:T(128)S(1)} %bitcast.15), channel_id=1, source_target_pairs={{4,0},{2,6},{5,1},{3,7},{12,8},{10,14},{13,9},{11,15},{20,16},{18,... | collective-permute-start | bytes 1544 | tf_op jit(solution)/shard_map/ppermute | solution.py:197
  110.2 5.1 %collective-permute-start.8 = (f32[128]{0:T(128)S(1)}, f32[128]{0:T(128)S(1)}, u32[]{:S(2)}, u32[]{:S(2)}) collective-permute-start(f32[128]{0:T(128)S(1)} %slice_bitcast_fusion), channel_id=1, source_target_pairs={{2,0},{4,2},{6,4},{0,6},{3,1},{5,3},{7,5},{1,7},{10,8},{12,10},{14... | collective-permute-start | bytes 1544 | tf_op jit(solution)/shard_map/ppermute | solution.py:193

commit v3 on v2

v3 whole, which is shorter than its diff:
```python
import functools

import jax
import jax.numpy as jnp
from jax import lax
from jax.experimental import pallas as pl
from jax.experimental.pallas import tpu as pltpu
from jax.sharding import Mesh, PartitionSpec as P

AXES = ("group", "z", "core")
LANES = 128
CHUNK = 512
PER_CALL = 8
VMEM = pl.BlockSpec(memory_space=pltpu.VMEM)


def ring_pairs(length, shift):
    if 2 * shift < length:
        return [(k, (k + shift) % length) for k in range(length)]
    pairs = []
    for k in range(length // 2):
        low, high = k, k + shift
        pairs.append((low, high) if k % 2 == 0 else (high, low))
    return pairs


def inverse(pairs):
    return [(b, a) for a, b in pairs]


def flip(count, bits):
    return [(k, k ^ bits) for k in range(count)]


def unit_rows(values):
    values = values.astype(jnp.float32)
    total = jnp.sum(values * values, axis=1, keepdims=True) + values.shape[1] * 1e-06
    return (values * lax.rsqrt(total)).astype(jnp.bfloat16)


def lane_rows(first, second):
    count = first.shape[1]
    both = jnp.concatenate([first, second, jnp.zeros((6, count), jnp.float32)], axis=0)
    if count < LANES:
        both = jnp.concatenate([both, jnp.zeros((8, LANES - count), jnp.float32)], axis=1)
    return both


def pack_kernel(rows_ref, cluster_ref, order_ref, block_ref, meta_ref):
    rows, width = rows_ref.shape
    block_ref[:, :width] = unit_rows(rows_ref[...])
    meta = lane_rows(cluster_ref[...].astype(jnp.float32) + 1.0, order_ref[...].astype(jnp.float32))
    meta_ref[...] = meta
    turned = meta.T[:rows]
    cluster, order = turned[:, 0:1], turned[:, 1:2]
    high = jnp.floor(order / 256.0)
    lane = lax.broadcasted_iota(jnp.int32, (rows, LANES), 1)
    tail = jnp.where(lane == 0, cluster, jnp.where(lane == 1, high, order - 256.0 * high))
    block_ref[:, width:] = jnp.where(lane < 3, tail, 0.0).astype(jnp.bfloat16)


def pack(rows, cluster_ids, order_index):
    count, width = rows.shape
    return pl.pallas_call(
        pack_kernel,
        in_specs=[VMEM] * 3,
        out_specs=[VMEM] * 2,
        out_shape=[
            jax.ShapeDtypeStruct((count, width + LANES), jnp.bfloat16),
            jax.ShapeDtypeStruct((8, LANES), jnp.float32),
        ],
        cost_estimate=pl.CostEstimate(
            flops=4 * count * width, bytes_accessed=4 * count * width, transcendentals=count
        ),
    )(rows, cluster_ids.reshape(1, count), order_index.reshape(1, count))


def tail_meta(tail):
    tail = tail.astype(jnp.float32)
    return tail[:, 0:1], tail[:, 1:2] * 256.0 + tail[:, 2:3]


def maxima_kernel(packed, raw, pieces, first, carried, *refs):
    take = list(refs)
    packed_refs = [take.pop(0) for _ in range(packed)]
    raw_refs = [(take.pop(0), take.pop(0)) for _ in range(raw)]
    block_refs = [[take.pop(0) for _ in range(n)] for n in pieces]
    carry_ref = take.pop(0) if carried else None
    row_ref, col_ref, units, dots = take
    visitors = packed + raw
    width = units.shape[1]
    rows = sum(ref.shape[0] for ref in block_refs[0])

    visitor_meta = []
    for v in range(visitors):
        start = v * LANES
        if rows < LANES:
            units[start + rows : start + LANES, :] = jnp.zeros((LANES - rows, width), jnp.bfloat16)
        if v < packed:
            units[start : start + rows, :] = packed_refs[v][:, :width]
            tail = packed_refs[v][:, width:].astype(jnp.float32)
            if rows < LANES:
                tail = jnp.concatenate([tail, jnp.zeros((LANES - rows, LANES), jnp.float32)], axis=0)
            turned = tail.T
            visitor_meta.append((turned[0:1], turned[1:2] * 256.0 + turned[2:3]))
        else:
            rows_ref, meta_ref = raw_refs[v - packed]
            units[start : start + rows, :] = unit_rows(rows_ref[...])
            visitor_meta.append((meta_ref[0:1, :], meta_ref[1:2, :]))
    flat = [ref for parts in block_refs for ref in parts]
    for k in range(0, width, CHUNK):
        left = jnp.concatenate([ref[:, k : k + CHUNK] for ref in flat], axis=0)
        part = lax.dot_general(
            left,
            units[:, k : k + CHUNK],
            (((1,), (1,)), ((), ())),
            preferred_element_type=jnp.float32,
        )
        dots[...] = part if k == 0 else dots[...] + part

    row_best = [jnp.full((1, LANES), -1.0, jnp.float32) for _ in range(visitors)]
    lane = lax.broadcasted_iota(jnp.int32, (rows, LANES), 1)
    col_all = jnp.full((rows, LANES), -1.0, jnp.float32)
    for j, parts in enumerate(block_refs):
        tail = jnp.concatenate([ref[:, width:] for ref in parts], axis=0)
        block_cluster, block_order = tail_meta(tail)
        col_best = jnp.full((rows, 1), -1.0, jnp.float32)
        for v in range(visitors):
            cosine = dots[j * rows : (j + 1) * rows, v * LANES : (v + 1) * LANES]
            cluster, order = visitor_meta[v]
            same = (block_cluster == cluster) & (cluster > 0)
            seen = jnp.where(same & (block_order < order), cosine, -1.0)
            row_best[v] = jnp.maximum(row_best[v], jnp.max(seen, axis=0, keepdims=True))
            if carried or v > 0:
                seen = jnp.where(same & (order < block_order), cosine, -1.0)
                col_best = jnp.maximum(col_best, jnp.max(seen, axis=1, keepdims=True))
        col_all = jnp.where(lane == j, col_best, col_all)
    for v in range(visitors):
        row_ref[v] = row_best[v]
    if rows < LANES:
        fill = jnp.full((LANES - rows, LANES), -1.0, jnp.float32)
        col_all = jnp.concatenate([col_all, fill], axis=0)
    turned = col_all.T
    group, core = lax.axis_index("group"), lax.axis_index("core")
    for j in range(len(pieces)):
        s, c = (first + j) // 2, (first + j) % 2
        place = ((group ^ s) & (PER_CALL // 2 - 1)) * 2 + (core ^ c)
        best = turned[j : j + 1, :]
        col_ref[place] = jnp.maximum(best, carry_ref[place]) if carried else best


def maxima(packed, raw, blocks, carry=None):
    count = len(packed) + len(raw)
    rows, width = packed[0].shape[0], packed[0].shape[1] - LANES
    row_best, col_best = None, []
    for first in range(0, len(blocks), PER_CALL):
        part = blocks[first : first + PER_CALL]
        operands = list(packed)
        for pair in raw:
            operands += pair
        operands += [piece for block in part for piece in block]
        if carry is not None:
            operands.append(carry[first // PER_CALL])
        row, col = pl.pallas_call(
            functools.partial(
                maxima_kernel,
                len(packed),
                len(raw),
                [len(block) for block in part],
                first,
                carry is not None,
            ),
            in_specs=[VMEM] * len(operands),
            out_specs=[VMEM] * 2,
            out_shape=[
                jax.ShapeDtypeStruct((count, 1, LANES), jnp.float32),
                jax.ShapeDtypeStruct((len(part), 1, LANES), jnp.float32),
            ],
            scratch_shapes=[
                pltpu.VMEM((count * LANES, width), jnp.bfloat16),
                pltpu.VMEM((len(part) * rows, count * LANES), jnp.float32),
            ],
            compiler_params=pltpu.CompilerParams(vmem_limit_bytes=40 * 2**20),
            cost_estimate=pl.CostEstimate(
                flops=2 * len(part) * rows * count * LANES * width,
                bytes_accessed=2 * (len(part) + count) * rows * width,
                transcendentals=0,
            ),
        )(*operands)
        row_best = row if row_best is None else jnp.maximum(row_best, row)
        col_best.append(col)
    return row_best, col_best


def gather_plane(block, groups):
    half = block.shape[0] // 2
    blocks = {0: [block]}
    for s in range(1, groups):
        low, high = s & -s, 1 << (s.bit_length() - 1)
        if low == high:
            blocks[s] = [lax.ppermute(block, "group", flip(groups, s))]
            continue
        top, bottom = blocks[s ^ high], blocks[s ^ low]
        top = top[0][:half] if len(top) == 1 else top[0]
        bottom = bottom[0][half:] if len(bottom) == 1 else bottom[1]
        blocks[s] = [
            lax.ppermute(top, "group", flip(groups, high)),
            lax.ppermute(bottom, "group", flip(groups, low)),
        ]
    return blocks


def local(embeddings, cluster_ids, order_index):
    rows = embeddings.shape[0]
    groups, length = lax.axis_size("group"), lax.axis_size("z")
    routes = [ring_pairs(length, shift) for shift in range(1, length // 2 + 1)]
    early = [lax.ppermute(embeddings, "z", route) for route in routes[:-1]]
    own, meta = pack(embeddings, cluster_ids, order_index)
    early = [(block, lax.ppermute(meta, "z", route)) for block, route in zip(early, routes)]
    late = lax.ppermute(own, "z", routes[-1])

    blocks = []
    for parts in gather_plane(own, groups).values():
        blocks.append(parts)
        blocks.append([lax.ppermute(part, "core", flip(2, 1)) for part in parts])

    row_early, col_early = maxima([own], early, blocks)
    best = row_early[0, 0]
    for index, route in enumerate(routes[:-1]):
        best = jnp.maximum(best, lax.ppermute(row_early[index + 1, 0], "z", inverse(route)))
    row_late, col_late = maxima([late], [], blocks, col_early)
    home = lax.ppermute(row_late[0, 0], "z", inverse(routes[-1]))
    sent = jnp.any(jnp.array([a for a, b in routes[-1]]) == lax.axis_index("z"))
    best = jnp.maximum(best, jnp.where(sent, home, -1.0))
    if len(col_late) > 1:
        turn = (lax.axis_index("group") // (PER_CALL // 2)) ^ jnp.arange(len(col_late))
        col = jnp.stack(col_late)[turn].reshape(-1, 1, LANES)
    else:
        col = col_late[0]
    parts = lax.all_to_all(col, ("group", "core"), split_axis=0, concat_axis=0, tiled=True)
    return jnp.maximum(best, jnp.max(parts, axis=(0, 1)))[:rows]


def solution(mesh):
    groups, members = mesh.devices.shape
    fine = Mesh(mesh.devices.reshape(groups, members // 2, 2), AXES)
    placed = (P(AXES, None), P(AXES), P(AXES))
    return jax.shard_map(local, mesh=fine, in_specs=placed, out_specs=P(AXES), check_vma=False)
```

time: 117 us -> 63.3 us (0.54)
  blocking collectives: 52.1 us -> 0 us
  starting transfers between devices: 16.2 us -> 21.6 us
  waiting for transfers between devices: 36.8 us -> 32.3 us
    all_gather x1 -> x0, blocking collectives: 52.1 us -> none  [local(): meta = lax.all_gather(meta, AXES, axis=0)]
    ppermute x9 -> x12, starting transfers between devices: 11.6 us -> 15.6 us  [the longest x2 4.46 us: gather_plane(): blocks[s] = [lax.ppermute(block, 'group', flip(groups, s))]]
    ppermute x9 -> x12, waiting for transfers between devices: 32.5 us -> 29.3 us  [the longest x2 13.6 us: gather_plane(): blocks[s] = [lax.ppermute(block, 'group', flip(groups, s))]]
    ppermute x1, starting transfers between devices: 0.06 us -> 1.43 us  [local(): lax.ppermute(row_early[index + 1, 0], 'z', inverse(route))]
    all_to_all x1, waiting for transfers between devices: 2.51 us -> 1.19 us  [local(): lax.all_to_all(col, ('group', 'core'), split_axis=0, concat_axis=0, tiled...]
  transfers between devices with their start and end apart: 12 -> 15, of which waited for: 4 -> 9; matrix products, arithmetic and copies ran while one was open for 1% -> 1% of each run, Pallas kernels for 2% -> 4%
where the time goes in v3:
time: 63.3 us; the launch traced here: 63.1 us
  waiting for transfers between devices  32.3 us (51%)
  starting transfers between devices  21.6 us (34%)
  Pallas kernels  7.19 us (11%)
  other arithmetic  1.83 us (3%)
    ppermute x2, waiting for transfers between devices, gather_plane(): blocks[s] = [lax.ppermute(block, 'group', flip(groups, s))]  13.6 us
    ppermute x1, waiting for transfers between devices, local(): late = lax.ppermute(own, 'z', routes[-1])  10.1 us
    pallas_call x2, Pallas kernels, maxima(): pl.pallas_call(functools.partial(maxima_kernel, len(packed), len(raw), [l...  4.75 us
    ppermute x2, starting transfers between devices, gather_plane(): blocks[s] = [lax.ppermute(block, 'group', flip(groups, s))]  4.46 us
    ppermute x1, starting transfers between devices, local(): late = lax.ppermute(own, 'z', routes[-1])  4.08 us
    all_to_all x1, starting transfers between devices, local(): lax.all_to_all(col, ('group', 'core'), split_axis=0, concat_axis=0, tiled...  3.32 us
    pallas_call x1, Pallas kernels, pack(): pl.pallas_call(pack_kernel, in_specs=[VMEM] * 3, out_specs=[VMEM] * 2, ou...  2.44 us
    ppermute x1, waiting for transfers between devices, gather_plane(): lax.ppermute(bottom, 'group', flip(groups, low))  2.16 us
  transfers between devices with their start and end apart: 15, of which 9 were waited for; matrix products, arithmetic and copies ran while one was open for 1% of the time, Pallas kernels for 4%

profile of v3, /device:TPU:0, one launch (start us, length us, event | category | flops | bytes accessed | tf_op | source)
XLA Modules:
  0.0 63.1 jit_solution(14753950823194991648)
XLA Ops:
  0.0 2.4 %shard_map.46 = (bf16[96,4224]{1,0:T(8,128)(2,1)}, f32[8,128]{1,0:T(8,128)}) custom-call(bf16[96,4096]{1,0:T(8,128)(2,1)} %rows_ref.1, s32[1,96]{1,0:T(1,128)} %bitcast.11, s32[1,96]{1,0:T(1,128)} %bitcast.12), custom_call_target="tpu_custom_call" | custom-call | flops 1572864 | bytes 1572864 | tf_op jit(solution)/shard_map/pallas_call | solution.py:64
  2.4 3.0 %collective-permute-start.5 = (bf16[96,4224]{1,0:T(8,128)(2,1)}, bf16[96,4224]{1,0:T(8,128)(2,1)S(1)}, u32[]{:S(2)}, u32[]{:S(2)}) collective-permute-start(bf16[96,4224]{1,0:T(8,128)(2,1)} %get-tuple-element.11.refs_0_.refs_3_.refs_1_), channel_id=1, source_target_pairs={{0,16},{8,24},{16,0},{24,8},{1,17},{9,25},{17,1},{25,9},{2,18},{10... | collective-permute-start | bytes 2433032 | tf_op jit(solution)/shard_map/ppermute | solution.py:201
  5.4 1.5 %collective-permute-start.3 = (bf16[96,4224]{1,0:T(8,128)(2,1)}, bf16[96,4224]{1,0:T(8,128)(2,1)S(1)}, u32[]{:S(2)}, u32[]{:S(2)}) collective-permute-start(bf16[96,4224]{1,0:T(8,128)(2,1)} %get-tuple-element.11.refs_0_.refs_3_.refs_1_), channel_id=1, source_target_pairs={{0,8},{8,0},{16,24},{24,16},{1,9},{9,1},{17,25},{25,17},{2,10},{10... | collective-permute-start | bytes 2433032 | tf_op jit(solution)/shard_map/ppermute | solution.py:201
  6.9 1.6 %collective-permute-start = (bf16[96,4096]{1,0:T(8,128)(2,1)S(1)}, bf16[96,4096]{1,0:T(8,128)(2,1)S(1)}, u32[]{:S(2)}, u32[]{:S(2)}) collective-permute-start(bf16[96,4096]{1,0:T(8,128)(2,1)S(1)} %copy-done.1), channel_id=1, source_target_pairs={{0,2},{2,4},{4,6},{6,0},{1,3},{3,5},{5,7},{7,1},{8,10},{10,12},{12... | collective-permute-start | bytes 2359304 | tf_op jit(solution)/shard_map/ppermute | solution.py:217
  8.5 1.6 %collective-permute-start.1 = (f32[8,128]{1,0:T(8,128)}, f32[8,128]{1,0:T(8,128)S(1)}, u32[]{:S(2)}, u32[]{:S(2)}) collective-permute-start(f32[8,128]{1,0:T(8,128)} %get-tuple-element.12), channel_id=1, source_target_pairs={{0,2},{2,4},{4,6},{6,0},{1,3},{3,5},{5,7},{7,1},{8,10},{10,12},{12... | collective-permute-start | bytes 12296 | tf_op jit(solution)/shard_map/ppermute | solution.py:219
  10.1 13.6 %collective-permute-done.5.refs_7_.refs_5_ = bf16[96,4224]{1,0:T(8,128)(2,1)S(1)} collective-permute-done((bf16[96,4224]{1,0:T(8,128)(2,1)}, bf16[96,4224]{1,0:T(8,128)(2,1)S(1)}, u32[]{:S(2)}, u32[]{:S(2)}) %collective-permute-start.5) | collective-permute-done | bytes 811040 | tf_op jit(solution)/shard_map/ppermute | solution.py:201
  23.7 1.8 %collective-permute-start.8 = (bf16[48,4224]{1,0:T(8,128)(2,1)S(1)}, bf16[48,4224]{1,0:T(8,128)(2,1)S(1)}, u32[]{:S(2)}, u32[]{:S(2)}) collective-permute-start(bf16[48,4224]{1,0:T(8,128)(2,1)S(1)} %slice.21), channel_id=1, source_target_pairs={{0,8},{8,0},{16,24},{24,16},{1,9},{9,1},{17,25},{25,17},{2,10},{10... | collective-permute-start | bytes 1216520 | tf_op jit(solution)/shard_map/ppermute | solution.py:208
  25.5 1.6 %collective-permute-start.7 = (bf16[48,4224]{1,0:T(8,128)(2,1)S(1)}, bf16[48,4224]{1,0:T(8,128)(2,1)S(1)}, u32[]{:S(2)}, u32[]{:S(2)}) collective-permute-start(bf16[48,4224]{1,0:T(8,128)(2,1)S(1)} %slice.20), channel_id=1, source_target_pairs={{0,16},{8,24},{16,0},{24,8},{1,17},{9,25},{17,1},{25,9},{2,18},{10... | collective-permute-start | bytes 1216520 | tf_op jit(solution)/shard_map/ppermute | solution.py:207
  27.6 0.5 collective-permute-start.6
  28.1 4.1 %collective-permute-start.12 = (bf16[96,4224]{1,0:T(8,128)(2,1)S(1)}, bf16[96,4224]{1,0:T(8,128)(2,1)S(1)}, u32[]{:S(2)}, u32[]{:S(2)}) collective-permute-start(bf16[96,4224]{1,0:T(8,128)(2,1)S(1)} %copy-done), channel_id=1, source_target_pairs={{0,4},{6,2},{1,5},{7,3},{8,12},{14,10},{9,13},{15,11},{16,20},{22,... | collective-permute-start | bytes 2433032 | tf_op jit(solution)/shard_map/ppermute | solution.py:220
  32.2 2.2 %collective-permute-done.8.refs_10_.refs_8_ = bf16[48,4224]{1,0:T(8,128)(2,1)S(1)} collective-permute-done((bf16[48,4224]{1,0:T(8,128)(2,1)S(1)}, bf16[48,4224]{1,0:T(8,128)(2,1)S(1)}, u32[]{:S(2)}, u32[]{:S(2)}) %collective-permute-start.8) | collective-permute-done | bytes 405536 | tf_op jit(solution)/shard_map/ppermute | solution.py:208
  34.4 1.2 %collective-permute-done.7.refs_9_.refs_7_ = bf16[48,4224]{1,0:T(8,128)(2,1)S(1)} collective-permute-done((bf16[48,4224]{1,0:T(8,128)(2,1)S(1)}, bf16[48,4224]{1,0:T(8,128)(2,1)S(1)}, u32[]{:S(2)}, u32[]{:S(2)}) %collective-permute-start.7) | collective-permute-done | bytes 405536 | tf_op jit(solution)/shard_map/ppermute | solution.py:207
  35.6 0.5 collective-permute-done.10.refs_12_.refs_10_
  36.1 1.2 %collective-permute-done.9.refs_11_.refs_9_ = bf16[48,4224]{1,0:T(8,128)(2,1)S(1)} collective-permute-done((bf16[48,4224]{1,0:T(8,128)(2,1)S(1)}, bf16[48,4224]{1,0:T(8,128)(2,1)S(1)}, u32[]{:S(2)}, u32[]{:S(2)}) %collective-permute-start.9) | collective-permute-done | bytes 405536 | tf_op jit(solution)/shard_map/ppermute | solution.py:225
  37.3 2.2 %shard_map.47 = (f32[2,1,128]{2,1,0:T(1,128)S(1)}, f32[8,1,128]{2,1,0:T(1,128)S(1)}) custom-call(bf16[96,4224]{1,0:T(8,128)(2,1)S(1)} %copy-done, bf16[96,4096]{1,0:T(8,128)(2,1)S(1)} %collective-permute-done.refs_1_, f32[8,128]{1,0:T(8,128)S(1)} %collective-permute-done.1.refs_2_, bf16[96,4224]{1,0:T(8,128)(2,1)S(1)} %copy-done, ...), custom_call_target="tpu_custom_call" | custom-call | flops 1610612736 | bytes 7864320 | tf_op jit(solution)/shard_map/pallas_call | solution.py:164
  39.5 10.1 %collective-permute-done.12.refs_0_ = bf16[96,4224]{1,0:T(8,128)(2,1)S(1)} collective-permute-done((bf16[96,4224]{1,0:T(8,128)(2,1)S(1)}, bf16[96,4224]{1,0:T(8,128)(2,1)S(1)}, u32[]{:S(2)}, u32[]{:S(2)}) %collective-permute-start.12) | collective-permute-done | bytes 811040 | tf_op jit(solution)/shard_map/ppermute | solution.py:220
  49.7 2.5 %shard_map.48 = (f32[1,1,128]{2,1,0:T(1,128)S(1)}, f32[8,1,128]{2,1,0:T(1,128)}) custom-call(bf16[96,4224]{1,0:T(8,128)(2,1)S(1)} %collective-permute-done.12.refs_0_, bf16[96,4224]{1,0:T(8,128)(2,1)S(1)} %copy-done, bf16[96,4224]{1,0:T(8,128)(2,1)S(1)} %collective-permute-done.2.refs_4_.refs_2_, ...), custom_call_target="tpu_custom_call" | custom-call | flops 805306368 | bytes 7077888 | tf_op jit(solution)/shard_map/pallas_call | solution.py:164
  52.2 3.3 %all-to-all-start = ((f32[8,1,128]{2,1,0:T(1,128)}), f32[8,1,128]{2,1,0:T(1,128)S(1)}, u32[]{:S(2)}, u32[]{:S(2)}) async-start(f32[8,1,128]{2,1,0:T(1,128)} %get-tuple-element.16), calls=%async_computation | async-start | bytes 8192 | tf_op jit(solution)/shard_map/all_to_all | solution.py:240
  55.5 1.3 %collective-permute-start.13 = (f32[128]{0:T(128)S(1)}, f32[128]{0:T(128)S(1)}, u32[]{:S(2)}, u32[]{:S(2)}) collective-permute-start(f32[128]{0:T(128)S(1)} %bitcast.10), channel_id=1, source_target_pairs={{4,0},{2,6},{5,1},{3,7},{12,8},{10,14},{13,9},{11,15},{20,16},{18,... | collective-permute-start | bytes 1544 | tf_op jit(solution)/shard_map/ppermute | solution.py:232
  56.8 1.4 %collective-permute-start.11 = (f32[128]{0:T(128)S(1)}, f32[128]{0:T(128)S(1)}, u32[]{:S(2)}, u32[]{:S(2)}) collective-permute-start(f32[128]{0:T(128)S(1)} %slice_bitcast_fusion), channel_id=1, source_target_pairs={{2,0},{4,2},{6,4},{0,6},{3,1},{5,3},{7,5},{1,7},{10,8},{12,10},{14... | collective-permute-start | bytes 1544 | tf_op jit(solution)/shard_map/ppermute | solution.py:230
  58.3 0.7 %compare_reduce_fusion = pred[]{:T(512)} fusion(s32[]{:T(128)S(6)} %axis_index.15), kind=kLoop, calls=%fused_computation | loop fusion | flops 5 | bytes 5 | tf_op jit(solution)/shard_map/reduce_or | solution.py:233
  58.9 1.2 %all-to-all-done = f32[8,1,128]{2,1,0:T(1,128)S(1)} async-done(((f32[8,1,128]{2,1,0:T(1,128)}), f32[8,1,128]{2,1,0:T(1,128)S(1)}, u32[]{:S(2)}, u32[]{:S(2)}) %all-to-all-start) | async-done | bytes 4128 | tf_op jit(solution)/shard_map/all_to_all | solution.py:240
  60.1 1.8 %collective-permute-done.13 = f32[128]{0:T(128)S(1)} collective-permute-done((f32[128]{0:T(128)S(1)}, f32[128]{0:T(128)S(1)}, u32[]{:S(2)}, u32[]{:S(2)}) %collective-permute-start.13) | collective-permute-done | bytes 544 | tf_op jit(solution)/shard_map/ppermute | solution.py:232
  61.9 1.2 %fusion.1 = f32[128]{0:T(128)} fusion(f32[128]{0:T(128)S(1)} %reduce_max.9, f32[128]{0:T(128)S(1)} %collective-permute-done.13, pred[]{:T(512)} %compare_reduce_fusion, f32[128]{0:T(128)S(1)} %collective-permute-done.11, f32[2,1,128]{2,1,0:T(1,128)S(1)} %get-tuple-element.13), kind=kLoop, calls=%fused_computation.3 | loop fusion | flops 512 | bytes 2561 | tf_op jit(solution)/shard_map/max | solution.py:241
  (19 shorter events, 0.6 us)
Async XLA Ops:
  0.0 6.9 %copy-start.1 = (bf16[96,4096]{1,0:T(8,128)(2,1)S(1)}, bf16[96,4096]{1,0:T(8,128)(2,1)}, u32[]{:S(2)}) copy-start(bf16[96,4096]{1,0:T(8,128)(2,1)} %rows_ref.1) | copy-start | bytes 2359300
  2.4 21.2 %collective-permute-start.5 = (bf16[96,4224]{1,0:T(8,128)(2,1)}, bf16[96,4224]{1,0:T(8,128)(2,1)S(1)}, u32[]{:S(2)}, u32[]{:S(2)}) collective-permute-start(bf16[96,4224]{1,0:T(8,128)(2,1)} %get-tuple-element.11.refs_0_.refs_3_.refs_1_), channel_id=1, source_target_pairs={{0,16},{8,24},{16,0},{24,8},{1,17},{9,25},{17,1},{25,9},{2,18},{10... | collective-permute-start | bytes 2433032 | tf_op jit(solution)/shard_map/ppermute | solution.py:201
  5.4 20.1 %collective-permute-start.3 = (bf16[96,4224]{1,0:T(8,128)(2,1)}, bf16[96,4224]{1,0:T(8,128)(2,1)S(1)}, u32[]{:S(2)}, u32[]{:S(2)}) collective-permute-start(bf16[96,4224]{1,0:T(8,128)(2,1)} %get-tuple-element.11.refs_0_.refs_3_.refs_1_), channel_id=1, source_target_pairs={{0,8},{8,0},{16,24},{24,16},{1,9},{9,1},{17,25},{25,17},{2,10},{10... | collective-permute-start | bytes 2433032 | tf_op jit(solution)/shard_map/ppermute | solution.py:201
  6.9 20.7 %collective-permute-start = (bf16[96,4096]{1,0:T(8,128)(2,1)S(1)}, bf16[96,4096]{1,0:T(8,128)(2,1)S(1)}, u32[]{:S(2)}, u32[]{:S(2)}) collective-permute-start(bf16[96,4096]{1,0:T(8,128)(2,1)S(1)} %copy-done.1), channel_id=1, source_target_pairs={{0,2},{2,4},{4,6},{6,0},{1,3},{3,5},{5,7},{7,1},{8,10},{10,12},{12... | collective-permute-start | bytes 2359304 | tf_op jit(solution)/shard_map/ppermute | solution.py:217
  8.5 19.6 %collective-permute-start.2 = (bf16[96,4224]{1,0:T(8,128)(2,1)}, bf16[96,4224]{1,0:T(8,128)(2,1)S(1)}, u32[]{:S(2)}, u32[]{:S(2)}) collective-permute-start(bf16[96,4224]{1,0:T(8,128)(2,1)} %get-tuple-element.11.refs_0_.refs_3_.refs_1_), channel_id=1, source_target_pairs={{0,1},{1,0},{2,3},{3,2},{4,5},{5,4},{6,7},{7,6},{8,9},{9,8},{10,11... | collective-permute-start | bytes 2433032 | tf_op jit(solution)/shard_map/ppermute | solution.py:225
  8.5 19.6 %copy-start = (bf16[96,4224]{1,0:T(8,128)(2,1)S(1)}, bf16[96,4224]{1,0:T(8,128)(2,1)}, u32[]{:S(2)}) copy-start(bf16[96,4224]{1,0:T(8,128)(2,1)} %get-tuple-element.11.refs_0_.refs_3_.refs_1_) | copy-start | bytes 2433028
  8.5 19.1 %collective-permute-start.1 = (f32[8,128]{1,0:T(8,128)}, f32[8,128]{1,0:T(8,128)S(1)}, u32[]{:S(2)}, u32[]{:S(2)}) collective-permute-start(f32[8,128]{1,0:T(8,128)} %get-tuple-element.12), channel_id=1, source_target_pairs={{0,2},{2,4},{4,6},{6,0},{1,3},{3,5},{5,7},{7,1},{8,10},{10,12},{12... | collective-permute-start | bytes 12296 | tf_op jit(solution)/shard_map/ppermute | solution.py:219
  23.7 10.6 %collective-permute-start.8 = (bf16[48,4224]{1,0:T(8,128)(2,1)S(1)}, bf16[48,4224]{1,0:T(8,128)(2,1)S(1)}, u32[]{:S(2)}, u32[]{:S(2)}) collective-permute-start(bf16[48,4224]{1,0:T(8,128)(2,1)S(1)} %slice.21), channel_id=1, source_target_pairs={{0,8},{8,0},{16,24},{24,16},{1,9},{9,1},{17,25},{25,17},{2,10},{10... | collective-permute-start | bytes 1216520 | tf_op jit(solution)/shard_map/ppermute | solution.py:208
  25.5 10.0 %collective-permute-start.7 = (bf16[48,4224]{1,0:T(8,128)(2,1)S(1)}, bf16[48,4224]{1,0:T(8,128)(2,1)S(1)}, u32[]{:S(2)}, u32[]{:S(2)}) collective-permute-start(bf16[48,4224]{1,0:T(8,128)(2,1)S(1)} %slice.20), channel_id=1, source_target_pairs={{0,16},{8,24},{16,0},{24,8},{1,17},{9,25},{17,1},{25,9},{2,18},{10... | collective-permute-start | bytes 1216520 | tf_op jit(solution)/shard_map/ppermute | solution.py:207
  27.6 9.7 %collective-permute-start.4 = (bf16[96,4224]{1,0:T(8,128)(2,1)S(1)}, bf16[96,4224]{1,0:T(8,128)(2,1)S(1)}, u32[]{:S(2)}, u32[]{:S(2)}) collective-permute-start(bf16[96,4224]{1,0:T(8,128)(2,1)S(1)} %collective-permute-done.3.refs_5_.refs_3_), channel_id=1, source_target_pairs={{0,1},{1,0},{2,3},{3,2},{4,5},{5,4},{6,7},{7,6},{8,9},{9,8},{10,11... | collective-permute-start | bytes 2433032 | tf_op jit(solution)/shard_map/ppermute | solution.py:225
  27.6 9.7 %collective-permute-start.6 = (bf16[96,4224]{1,0:T(8,128)(2,1)S(1)}, bf16[96,4224]{1,0:T(8,128)(2,1)S(1)}, u32[]{:S(2)}, u32[]{:S(2)}) collective-permute-start(bf16[96,4224]{1,0:T(8,128)(2,1)S(1)} %collective-permute-done.5.refs_7_.refs_5_), channel_id=1, source_target_pairs={{0,1},{1,0},{2,3},{3,2},{4,5},{5,4},{6,7},{7,6},{8,9},{9,8},{10,11... | collective-permute-start | bytes 2433032 | tf_op jit(solution)/shard_map/ppermute | solution.py:225
  28.1 21.6 %collective-permute-start.12 = (bf16[96,4224]{1,0:T(8,128)(2,1)S(1)}, bf16[96,4224]{1,0:T(8,128)(2,1)S(1)}, u32[]{:S(2)}, u32[]{:S(2)}) collective-permute-start(bf16[96,4224]{1,0:T(8,128)(2,1)S(1)} %copy-done), channel_id=1, source_target_pairs={{0,4},{6,2},{1,5},{7,3},{8,12},{14,10},{9,13},{15,11},{16,20},{22,... | collective-permute-start | bytes 2433032 | tf_op jit(solution)/shard_map/ppermute | solution.py:220
  34.4 1.7 %collective-permute-start.10 = (bf16[48,4224]{1,0:T(8,128)(2,1)S(1)}, bf16[48,4224]{1,0:T(8,128)(2,1)S(1)}, u32[]{:S(2)}, u32[]{:S(2)}) collective-permute-start(bf16[48,4224]{1,0:T(8,128)(2,1)S(1)} %collective-permute-done.8.refs_10_.refs_8_), channel_id=1, source_target_pairs={{0,1},{1,0},{2,3},{3,2},{4,5},{5,4},{6,7},{7,6},{8,9},{9,8},{10,11... | collective-permute-start | bytes 1216520 | tf_op jit(solution)/shard_map/ppermute | solution.py:225
  35.6 1.7 %collective-permute-start.9 = (bf16[48,4224]{1,0:T(8,128)(2,1)S(1)}, bf16[48,4224]{1,0:T(8,128)(2,1)S(1)}, u32[]{:S(2)}, u32[]{:S(2)}) collective-permute-start(bf16[48,4224]{1,0:T(8,128)(2,1)S(1)} %collective-permute-done.7.refs_9_.refs_7_), channel_id=1, source_target_pairs={{0,1},{1,0},{2,3},{3,2},{4,5},{5,4},{6,7},{7,6},{8,9},{9,8},{10,11... | collective-permute-start | bytes 1216520 | tf_op jit(solution)/shard_map/ppermute | solution.py:225
  52.2 7.9 %all-to-all-start = ((f32[8,1,128]{2,1,0:T(1,128)}), f32[8,1,128]{2,1,0:T(1,128)S(1)}, u32[]{:S(2)}, u32[]{:S(2)}) async-start(f32[8,1,128]{2,1,0:T(1,128)} %get-tuple-element.16), calls=%async_computation | async-start | bytes 8192 | tf_op jit(solution)/shard_map/all_to_all | solution.py:240
  55.5 6.4 %collective-permute-start.13 = (f32[128]{0:T(128)S(1)}, f32[128]{0:T(128)S(1)}, u32[]{:S(2)}, u32[]{:S(2)}) collective-permute-start(f32[128]{0:T(128)S(1)} %bitcast.10), channel_id=1, source_target_pairs={{4,0},{2,6},{5,1},{3,7},{12,8},{10,14},{13,9},{11,15},{20,16},{18,... | collective-permute-start | bytes 1544 | tf_op jit(solution)/shard_map/ppermute | solution.py:232
  56.8 5.1 %collective-permute-start.11 = (f32[128]{0:T(128)S(1)}, f32[128]{0:T(128)S(1)}, u32[]{:S(2)}, u32[]{:S(2)}) collective-permute-start(f32[128]{0:T(128)S(1)} %slice_bitcast_fusion), channel_id=1, source_target_pairs={{2,0},{4,2},{6,4},{0,6},{3,1},{5,3},{7,5},{1,7},{10,8},{12,10},{14... | collective-permute-start | bytes 1544 | tf_op jit(solution)/shard_map/ppermute | solution.py:230

commit v4 on v3

v4 whole, which is shorter than its diff:
```python
import functools

import jax
import jax.numpy as jnp
from jax import lax
from jax.experimental import pallas as pl
from jax.experimental.pallas import tpu as pltpu
from jax.sharding import Mesh, PartitionSpec as P

AXES = ("group", "z", "core")
LANES = 128
CHUNK = 512
PER_CALL = 4
VMEM = pl.BlockSpec(memory_space=pltpu.VMEM)


def ring_pairs(length, shift):
    if 2 * shift < length:
        return [(k, (k + shift) % length) for k in range(length)]
    pairs = []
    for k in range(length // 2):
        low, high = k, k + shift
        pairs.append((low, high) if k % 2 == 0 else (high, low))
    return pairs


def flip(count, bits):
    return [(k, k ^ bits) for k in range(count)]


def unit_rows(values):
    values = values.astype(jnp.float32)
    total = jnp.sum(values * values, axis=1, keepdims=True) + values.shape[1] * 1e-06
    return (values * lax.rsqrt(total)).astype(jnp.bfloat16)


def lane_rows(first, second):
    count = first.shape[1]
    both = jnp.concatenate([first, second, jnp.zeros((6, count), jnp.float32)], axis=0)
    if count < LANES:
        both = jnp.concatenate([both, jnp.zeros((8, LANES - count), jnp.float32)], axis=1)
    return both


def pack_kernel(rows_ref, cluster_ref, order_ref, block_ref):
    rows, width = rows_ref.shape
    block_ref[:, :width] = unit_rows(rows_ref[...])
    meta = lane_rows(cluster_ref[...].astype(jnp.float32) + 1.0, order_ref[...].astype(jnp.float32))
    turned = meta.T[:rows]
    cluster, order = turned[:, 0:1], turned[:, 1:2]
    high = jnp.floor(order / 256.0)
    lane = lax.broadcasted_iota(jnp.int32, (rows, LANES), 1)
    tail = jnp.where(lane == 0, cluster, jnp.where(lane == 1, high, order - 256.0 * high))
    block_ref[:, width:] = jnp.where(lane < 3, tail, 0.0).astype(jnp.bfloat16)


def pack(rows, cluster_ids, order_index):
    count, width = rows.shape
    return pl.pallas_call(
        pack_kernel,
        in_specs=[VMEM] * 3,
        out_specs=VMEM,
        out_shape=jax.ShapeDtypeStruct((count, width + LANES), jnp.bfloat16),
        cost_estimate=pl.CostEstimate(
            flops=4 * count * width, bytes_accessed=4 * count * width, transcendentals=count
        ),
    )(rows, cluster_ids.reshape(1, count), order_index.reshape(1, count))


def device_index(group, z, core):
    return (group * lax.axis_size("z") + z) * lax.axis_size("core") + core


def source_of(route):
    here = lax.axis_index("z")
    source = here
    for a, b in route:
        source = jnp.where(here == b, a, source)
    return source


def maxima_kernel(homes, pieces, first, carried, *refs):
    take = list(refs)
    visitor_refs = [take.pop(0) for _ in homes]
    block_refs = [[take.pop(0) for _ in range(n)] for n in pieces]
    carry_ref = take.pop(0) if carried else None
    answer_ref, units, dots = take
    width = units.shape[1]
    rows = sum(ref.shape[0] for ref in block_refs[0])

    visitor_meta = []
    for v, ref in enumerate(visitor_refs):
        start = v * LANES
        before = homes[v][2]
        after = LANES - before - ref.shape[0]
        units[start + before : start + LANES - after, :] = ref[:, :width]
        tail = [ref[:, width:].astype(jnp.float32)]
        if before:
            units[start : start + before, :] = jnp.zeros((before, width), jnp.bfloat16)
            tail.insert(0, jnp.zeros((before, LANES), jnp.float32))
        if after:
            units[start + LANES - after : start + LANES, :] = jnp.zeros((after, width), jnp.bfloat16)
            tail.append(jnp.zeros((after, LANES), jnp.float32))
        turned = jnp.concatenate(tail, axis=0).T
        visitor_meta.append((turned[0:1], turned[1:2] * 256.0 + turned[2:3]))
    flat = [ref for parts in block_refs for ref in parts]
    for k in range(0, width, CHUNK):
        left = jnp.concatenate([ref[:, k : k + CHUNK] for ref in flat], axis=0)
        part = lax.dot_general(
            left,
            units[:, k : k + CHUNK],
            (((1,), (1,)), ((), ())),
            preferred_element_type=jnp.float32,
        )
        dots[...] = part if k == 0 else dots[...] + part

    row_best = [jnp.full((1, LANES), -1.0, jnp.float32) for _ in homes]
    lane = lax.broadcasted_iota(jnp.int32, (rows, LANES), 1)
    col_all = jnp.full((rows, LANES), -1.0, jnp.float32)
    for j, parts in enumerate(block_refs):
        tail = jnp.concatenate([ref[:, width:] for ref in parts], axis=0).astype(jnp.float32)
        block_cluster, block_order = tail[:, 0:1], tail[:, 1:2] * 256.0 + tail[:, 2:3]
        col_best = jnp.full((rows, 1), -1.0, jnp.float32)
        for v, (route, _, _) in enumerate(homes):
            cosine = dots[j * rows : (j + 1) * rows, v * LANES : (v + 1) * LANES]
            cluster, order = visitor_meta[v]
            same = (block_cluster == cluster) & (cluster > 0)
            seen = jnp.where(same & (block_order < order), cosine, -1.0)
            row_best[v] = jnp.maximum(row_best[v], jnp.max(seen, axis=0, keepdims=True))
            if route is not None:
                seen = jnp.where(same & (order < block_order), cosine, -1.0)
                col_best = jnp.maximum(col_best, jnp.max(seen, axis=1, keepdims=True))
        col_all = jnp.where(lane == j, col_best, col_all)
    if rows < LANES:
        fill = jnp.full((LANES - rows, LANES), -1.0, jnp.float32)
        col_all = jnp.concatenate([col_all, fill], axis=0)
    turned = col_all.T

    group, z, core = (lax.axis_index(name) for name in AXES)
    answer_ref[...] = carry_ref[...] if carried else jnp.full(answer_ref.shape, -1.0, jnp.float32)
    for v, (route, other, _) in enumerate(homes):
        source = z if route is None else source_of(route)
        home = device_index(group, source, core ^ 1 if other else core)
        answer_ref[home] = jnp.maximum(answer_ref[home], row_best[v])
    for j in range(len(pieces)):
        home = device_index(group ^ (first + j), z, core)
        answer_ref[home] = jnp.maximum(answer_ref[home], turned[j : j + 1, :])


def maxima(homes, visitors, blocks, answer):
    devices = lax.axis_size(AXES)
    rows, width = sum(piece.shape[0] for piece in blocks[0]), visitors[0].shape[1] - LANES
    for first in range(0, len(blocks), PER_CALL):
        part = blocks[first : first + PER_CALL]
        operands = list(visitors) + [piece for block in part for piece in block]
        if answer is not None:
            operands.append(answer)
        answer = pl.pallas_call(
            functools.partial(
                maxima_kernel, homes, [len(block) for block in part], first, answer is not None
            ),
            in_specs=[VMEM] * len(operands),
            out_specs=VMEM,
            out_shape=jax.ShapeDtypeStruct((devices, 1, LANES), jnp.float32),
            scratch_shapes=[
                pltpu.VMEM((len(visitors) * LANES, width), jnp.bfloat16),
                pltpu.VMEM((len(part) * rows, len(visitors) * LANES), jnp.float32),
            ],
            compiler_params=pltpu.CompilerParams(vmem_limit_bytes=40 * 2**20),
            cost_estimate=pl.CostEstimate(
                flops=2 * len(part) * rows * len(visitors) * LANES * width,
                bytes_accessed=2 * (len(part) + len(visitors)) * rows * width,
                transcendentals=0,
            ),
        )(*operands)
    return answer


def after(value, *others):
    anywhere = pl.BlockSpec(memory_space=pl.ANY)
    return pl.pallas_call(
        lambda *refs: None,
        in_specs=[anywhere] * (1 + len(others)),
        out_specs=anywhere,
        out_shape=jax.ShapeDtypeStruct(value.shape, value.dtype),
        input_output_aliases={0: 0},
        cost_estimate=pl.CostEstimate(flops=0, bytes_accessed=0, transcendentals=0),
    )(value, *others)


def gather_plane(block, groups):
    half = block.shape[0] // 2
    blocks = {0: [block]}
    for s in range(1, groups):
        low, high = s & -s, 1 << (s.bit_length() - 1)
        if low == high:
            blocks[s] = [lax.ppermute(block, "group", flip(groups, s))]
            continue
        top, bottom = blocks[s ^ high], blocks[s ^ low]
        top = top[0][:half] if len(top) == 1 else top[0]
        bottom = bottom[0][half:] if len(bottom) == 1 else bottom[1]
        blocks[s] = [
            lax.ppermute(top, "group", flip(groups, high)),
            lax.ppermute(bottom, "group", flip(groups, low)),
        ]
    return blocks


def local(embeddings, cluster_ids, order_index):
    rows = embeddings.shape[0]
    groups, length = lax.axis_size("group"), lax.axis_size("z")
    routes = [ring_pairs(length, shift) for shift in range(1, length // 2 + 1)]
    own = pack(embeddings, cluster_ids, order_index)
    arrived = [lax.ppermute(own, "z", route) for route in routes]
    blocks = list(gather_plane(own, groups).values())

    homes, visitors = [], []
    for block, route in [(own, None)] + list(zip(arrived[:-1], routes)):
        homes += [(route, False, 0), (route, True, 0)]
        visitors += [block, lax.ppermute(block, "core", flip(2, 1))]
    answer = maxima(homes, visitors, blocks, None)
    last = after(arrived[-1], answer)
    other = lax.ppermute(last, "core", flip(2, 1))
    answer = maxima([(routes[-1], False, 0)], [last], blocks, answer)
    answer = maxima([(routes[-1], True, 0)], [other], blocks, answer)
    parts = lax.all_to_all(answer, AXES, split_axis=0, concat_axis=0, tiled=True)
    return jnp.max(parts, axis=(0, 1))[:rows]


def solution(mesh):
    groups, members = mesh.devices.shape
    fine = Mesh(mesh.devices.reshape(groups, members // 2, 2), AXES)
    placed = (P(AXES, None), P(AXES), P(AXES))
    return jax.shard_map(local, mesh=fine, in_specs=placed, out_specs=P(AXES), check_vma=False)
```

time: 63.3 us -> 64.1 us (1.013)
  blocking collectives: 0 us -> 12.6 us
  starting transfers between devices: 21.6 us -> 12.6 us
  waiting for transfers between devices: 32.3 us -> 28.9 us
  local copies, waits for them, and re-layouts: 0.07 us -> 1.38 us
  other arithmetic: 1.83 us -> 0.56 us
    ppermute x2, waiting for transfers between devices: 13.6 us -> 0.01 us  [gather_plane(): blocks[s] = [lax.ppermute(block, 'group', flip(groups, s))]]
    all_to_all x0 -> x1, blocking collectives: none -> 12.6 us  [local(): lax.all_to_all(answer, AXES, split_axis=0, concat_axis=0, tiled=True)]
    ppermute x1, waiting for transfers between devices: 2.16 us -> 8.39 us  [gather_plane(): lax.ppermute(bottom, 'group', flip(groups, low))]
    ppermute x10 -> x5, waiting for transfers between devices: 14.1 us -> 19.2 us  [the longest x2 19.2 us: local(): arrived = [lax.ppermute(own, 'z', route) for route in routes]]
    ppermute x10 -> x5, starting transfers between devices: 10.5 us -> 6.49 us  [the longest x2 6.49 us: local(): arrived = [lax.ppermute(own, 'z', route) for route in routes]]
    all_to_all x1 -> x0, starting transfers between devices: 3.32 us -> none  [local(): lax.all_to_all(col, ('group', 'core'), split_axis=0, concat_axis=0, tiled...]
    ppermute x2, starting transfers between devices: 4.46 us -> 3.01 us  [gather_plane(): blocks[s] = [lax.ppermute(block, 'group', flip(groups, s))]]
    unnamed x4 -> x6, local copies, waits for them, and re-layouts: 0.01 us -> 1.32 us
  transfers between devices with their start and end apart: 15 -> 9, of which waited for: 9 -> 4; matrix products, arithmetic and copies ran while one was open for 1% -> 0% of each run, Pallas kernels for 4% -> 7%
where the time goes in v4:
time: 64.1 us; the launch traced here: 63.9 us
  waiting for transfers between devices  28.9 us (45%)
  starting transfers between devices  12.6 us (20%)
  blocking collectives  12.6 us (20%)
  Pallas kernels  7.78 us (12%)
  local copies, waits for them, and re-layouts  1.38 us (2%)
    ppermute x2, waiting for transfers between devices, local(): arrived = [lax.ppermute(own, 'z', route) for route in routes]  19.2 us
    all_to_all x1, blocking collectives, local(): lax.all_to_all(answer, AXES, split_axis=0, concat_axis=0, tiled=True)  12.6 us
    ppermute x1, waiting for transfers between devices, gather_plane(): lax.ppermute(bottom, 'group', flip(groups, low))  8.39 us
    ppermute x2, starting transfers between devices, local(): arrived = [lax.ppermute(own, 'z', route) for route in routes]  6.49 us
    pallas_call x3, Pallas kernels, maxima(): pl.pallas_call(functools.partial(maxima_kernel, homes, [len(block) for bl...  5.38 us
    ppermute x2, starting transfers between devices, gather_plane(): blocks[s] = [lax.ppermute(block, 'group', flip(groups, s))]  3.01 us
    pallas_call x1, Pallas kernels, pack(): pl.pallas_call(pack_kernel, in_specs=[VMEM] * 3, out_specs=VMEM, out_shap...  2.4 us
    ppermute x1, starting transfers between devices, gather_plane(): lax.ppermute(top, 'group', flip(groups, high))  1.58 us
  transfers between devices with their start and end apart: 9, of which 4 were waited for; matrix products, arithmetic and copies ran while one was open for 0% of the time, Pallas kernels for 7%

profile of v4, /device:TPU:0, one launch (start us, length us, event | category | flops | bytes accessed | tf_op | source)
XLA Modules:
  0.0 63.9 jit_solution(10514915191909707425)
XLA Ops:
  0.0 2.4 %shard_map.37.refs_0_.refs_4_.refs_1_ = bf16[96,4224]{1,0:T(8,128)(2,1)} custom-call(bf16[96,4096]{1,0:T(8,128)(2,1)} %rows_ref.1, s32[1,96]{1,0:T(1,128)} %bitcast.3, s32[1,96]{1,0:T(1,128)} %bitcast.4), custom_call_target="tpu_custom_call" | custom-call | flops 1572864 | bytes 1572864 | tf_op jit(solution)/shard_map/pallas_call | solution.py:59
  2.4 3.0 %collective-permute-start.2 = (bf16[96,4224]{1,0:T(8,128)(2,1)}, bf16[96,4224]{1,0:T(8,128)(2,1)S(1)}, u32[]{:S(2)}, u32[]{:S(2)}) collective-permute-start(bf16[96,4224]{1,0:T(8,128)(2,1)} %shard_map.37.refs_0_.refs_4_.refs_1_), channel_id=1, source_target_pairs={{0,2},{2,4},{4,6},{6,0},{1,3},{3,5},{5,7},{7,1},{8,10},{10,12},{12... | collective-permute-start | bytes 2433032 | tf_op jit(solution)/shard_map/ppermute | solution.py:214
  5.4 1.5 %collective-permute-start.5 = (bf16[96,4224]{1,0:T(8,128)(2,1)}, bf16[96,4224]{1,0:T(8,128)(2,1)S(1)}, u32[]{:S(2)}, u32[]{:S(2)}) collective-permute-start(bf16[96,4224]{1,0:T(8,128)(2,1)} %shard_map.37.refs_0_.refs_4_.refs_1_), channel_id=1, source_target_pairs={{0,16},{8,24},{16,0},{24,8},{1,17},{9,25},{17,1},{25,9},{2,18},{10... | collective-permute-start | bytes 2433032 | tf_op jit(solution)/shard_map/ppermute | solution.py:197
  6.9 1.5 %collective-permute-start.4 = (bf16[96,4224]{1,0:T(8,128)(2,1)}, bf16[96,4224]{1,0:T(8,128)(2,1)S(1)}, u32[]{:S(2)}, u32[]{:S(2)}) collective-permute-start(bf16[96,4224]{1,0:T(8,128)(2,1)} %shard_map.37.refs_0_.refs_4_.refs_1_), channel_id=1, source_target_pairs={{0,8},{8,0},{16,24},{24,16},{1,9},{9,1},{17,25},{25,17},{2,10},{10... | collective-permute-start | bytes 2433032 | tf_op jit(solution)/shard_map/ppermute | solution.py:197
  8.4 0.0 collective-permute-start.1
  8.4 17.4 %collective-permute-done.2.refs_2_ = bf16[96,4224]{1,0:T(8,128)(2,1)S(1)} collective-permute-done((bf16[96,4224]{1,0:T(8,128)(2,1)}, bf16[96,4224]{1,0:T(8,128)(2,1)S(1)}, u32[]{:S(2)}, u32[]{:S(2)}) %collective-permute-start.2) | collective-permute-done | bytes 811040 | tf_op jit(solution)/shard_map/ppermute | solution.py:214
  25.8 3.5 %collective-permute-start = (bf16[96,4224]{1,0:T(8,128)(2,1)}, bf16[96,4224]{1,0:T(8,128)(2,1)}, u32[]{:S(2)}, u32[]{:S(2)}) collective-permute-start(bf16[96,4224]{1,0:T(8,128)(2,1)} %shard_map.37.refs_0_.refs_4_.refs_1_), channel_id=1, source_target_pairs={{0,4},{6,2},{1,5},{7,3},{8,12},{14,10},{9,13},{15,11},{16,20},{22,... | collective-permute-start | bytes 2433032 | tf_op jit(solution)/shard_map/ppermute | solution.py:214
  29.3 1.6 %collective-permute-start.7 = (bf16[48,4224]{1,0:T(8,128)(2,1)S(1)}, bf16[48,4224]{1,0:T(8,128)(2,1)S(1)}, u32[]{:S(2)}, u32[]{:S(2)}) collective-permute-start(bf16[48,4224]{1,0:T(8,128)(2,1)S(1)} %slice.13), channel_id=1, source_target_pairs={{0,8},{8,0},{16,24},{24,16},{1,9},{9,1},{17,25},{25,17},{2,10},{10... | collective-permute-start | bytes 1216520 | tf_op jit(solution)/shard_map/ppermute | solution.py:204
  30.9 0.0 collective-permute-done.4.refs_5_.refs_2_
  30.9 1.6 %collective-permute-start.6 = (bf16[48,4224]{1,0:T(8,128)(2,1)S(1)}, bf16[48,4224]{1,0:T(8,128)(2,1)S(1)}, u32[]{:S(2)}, u32[]{:S(2)}) collective-permute-start(bf16[48,4224]{1,0:T(8,128)(2,1)S(1)} %slice.12), channel_id=1, source_target_pairs={{0,16},{8,24},{16,0},{24,8},{1,17},{9,25},{17,1},{25,9},{2,18},{10... | collective-permute-start | bytes 1216520 | tf_op jit(solution)/shard_map/ppermute | solution.py:203
  32.5 0.0 collective-permute-done.1.refs_1_
  32.5 8.4 %collective-permute-done.7.refs_8_.refs_5_ = bf16[48,4224]{1,0:T(8,128)(2,1)S(1)} collective-permute-done((bf16[48,4224]{1,0:T(8,128)(2,1)S(1)}, bf16[48,4224]{1,0:T(8,128)(2,1)S(1)}, u32[]{:S(2)}, u32[]{:S(2)}) %collective-permute-start.7) | collective-permute-done | bytes 405536 | tf_op jit(solution)/shard_map/ppermute | solution.py:204
  40.9 1.3 %collective-permute-done.6.refs_7_.refs_4_ = bf16[48,4224]{1,0:T(8,128)(2,1)S(1)} collective-permute-done((bf16[48,4224]{1,0:T(8,128)(2,1)S(1)}, bf16[48,4224]{1,0:T(8,128)(2,1)S(1)}, u32[]{:S(2)}, u32[]{:S(2)}) %collective-permute-start.6) | collective-permute-done | bytes 405536 | tf_op jit(solution)/shard_map/ppermute | solution.py:203
  42.2 0.0 collective-permute-done.3.refs_3_
  42.2 2.0 %shard_map.38.refs_1_.refs_6_ = f32[32,1,128]{2,1,0:T(1,128)S(1)} custom-call(bf16[96,4224]{1,0:T(8,128)(2,1)S(1)} %copy-done, bf16[96,4224]{1,0:T(8,128)(2,1)S(1)} %collective-permute-done.1.refs_1_, bf16[96,4224]{1,0:T(8,128)(2,1)S(1)} %collective-permute-done.2.refs_2_, bf16[96,4224]{1,0:T(8,128)(2,1)S(1)} %collective-permute-done.3.refs_3_, ...), custom_call_target="tpu_custom_call" | custom-call | flops 1610612736 | bytes 6291456 | tf_op jit(solution)/shard_map/pallas_call | solution.py:158
  44.3 0.6 copy-done.1
  44.9 1.8 %collective-permute-done.refs_0_ = bf16[96,4224]{1,0:T(8,128)(2,1)} collective-permute-done((bf16[96,4224]{1,0:T(8,128)(2,1)}, bf16[96,4224]{1,0:T(8,128)(2,1)}, u32[]{:S(2)}, u32[]{:S(2)}) %collective-permute-start) | collective-permute-done | bytes 811040 | tf_op jit(solution)/shard_map/ppermute | solution.py:214
  46.7 0.0 collective-permute-start.8
  46.7 0.7 %copy-done.2 = f32[32,1,128]{2,1,0:T(1,128)S(1)} copy-done((f32[32,1,128]{2,1,0:T(1,128)S(1)}, f32[32,1,128]{2,1,0:T(1,128)}, u32[]{:S(2)}) %copy-start.2) | copy-done | bytes 16408
  47.4 2.2 %shard_map.40.refs_6_ = f32[32,1,128]{2,1,0:T(1,128)S(1)} custom-call(bf16[96,4224]{1,0:T(8,128)(2,1)} %shard_map.39.refs_0_, bf16[96,4224]{1,0:T(8,128)(2,1)S(1)} %copy-done, bf16[96,4224]{1,0:T(8,128)(2,1)S(1)} %collective-permute-done.4.refs_5_.refs_2_, bf16[96,4224]{1,0:T(8,128)(2,1)S(1)} %collective-permute-done.5.refs_6_.refs_3_, ...), custom_call_target="tpu_custom_call" | custom-call | flops 402653184 | bytes 3932160 | tf_op jit(solution)/shard_map/pallas_call | solution.py:158
  49.6 0.0 collective-permute-done.8.refs_0_
  49.6 1.1 %shard_map.41 = f32[32,1,128]{2,1,0:T(1,128)S(1)} custom-call(bf16[96,4224]{1,0:T(8,128)(2,1)S(1)} %collective-permute-done.8.refs_0_, bf16[96,4224]{1,0:T(8,128)(2,1)S(1)} %copy-done, bf16[96,4224]{1,0:T(8,128)(2,1)S(1)} %collective-permute-done.4.refs_5_.refs_2_, bf16[96,4224]{1,0:T(8,128)(2,1)S(1)} %collective-permute-done.5.refs_6_.refs_3_, ...), custom_call_target="tpu_custom_call" | custom-call | flops 402653184 | bytes 3932160 | tf_op jit(solution)/shard_map/pallas_call | solution.py:158
  50.7 12.6 %all_to_all.5 = f32[32,1,128]{2,1,0:T(1,128)S(1)} all-to-all(f32[32,1,128]{2,1,0:T(1,128)S(1)} %shard_map.41), channel_id=1, replica_groups=mesh['group'=4,'z'=4,'core'=2] {'group','z','core'}, dimensions={0} | all-to-all | bytes 32768 | tf_op jit(solution)/shard_map/all_to_all | solution.py:226
  63.3 0.6 reduce_max.9
  (9 shorter events, 0.1 us)
Async XLA Ops:
  2.4 39.8 %copy-start = (bf16[96,4224]{1,0:T(8,128)(2,1)S(1)}, bf16[96,4224]{1,0:T(8,128)(2,1)}, u32[]{:S(2)}) copy-start(bf16[96,4224]{1,0:T(8,128)(2,1)} %shard_map.37.refs_0_.refs_4_.refs_1_) | copy-start | bytes 2433028
  2.4 23.4 %collective-permute-start.2 = (bf16[96,4224]{1,0:T(8,128)(2,1)}, bf16[96,4224]{1,0:T(8,128)(2,1)S(1)}, u32[]{:S(2)}, u32[]{:S(2)}) collective-permute-start(bf16[96,4224]{1,0:T(8,128)(2,1)} %shard_map.37.refs_0_.refs_4_.refs_1_), channel_id=1, source_target_pairs={{0,2},{2,4},{4,6},{6,0},{1,3},{3,5},{5,7},{7,1},{8,10},{10,12},{12... | collective-permute-start | bytes 2433032 | tf_op jit(solution)/shard_map/ppermute | solution.py:214
  5.4 23.8 %collective-permute-start.5 = (bf16[96,4224]{1,0:T(8,128)(2,1)}, bf16[96,4224]{1,0:T(8,128)(2,1)S(1)}, u32[]{:S(2)}, u32[]{:S(2)}) collective-permute-start(bf16[96,4224]{1,0:T(8,128)(2,1)} %shard_map.37.refs_0_.refs_4_.refs_1_), channel_id=1, source_target_pairs={{0,16},{8,24},{16,0},{24,8},{1,17},{9,25},{17,1},{25,9},{2,18},{10... | collective-permute-start | bytes 2433032 | tf_op jit(solution)/shard_map/ppermute | solution.py:197
  6.9 23.9 %collective-permute-start.4 = (bf16[96,4224]{1,0:T(8,128)(2,1)}, bf16[96,4224]{1,0:T(8,128)(2,1)S(1)}, u32[]{:S(2)}, u32[]{:S(2)}) collective-permute-start(bf16[96,4224]{1,0:T(8,128)(2,1)} %shard_map.37.refs_0_.refs_4_.refs_1_), channel_id=1, source_target_pairs={{0,8},{8,0},{16,24},{24,16},{1,9},{9,1},{17,25},{25,17},{2,10},{10... | collective-permute-start | bytes 2433032 | tf_op jit(solution)/shard_map/ppermute | solution.py:197
  8.4 24.0 %collective-permute-start.1 = (bf16[96,4224]{1,0:T(8,128)(2,1)}, bf16[96,4224]{1,0:T(8,128)(2,1)S(1)}, u32[]{:S(2)}, u32[]{:S(2)}) collective-permute-start(bf16[96,4224]{1,0:T(8,128)(2,1)} %shard_map.37.refs_0_.refs_4_.refs_1_), channel_id=1, source_target_pairs={{0,1},{1,0},{2,3},{3,2},{4,5},{5,4},{6,7},{7,6},{8,9},{9,8},{10,11... | collective-permute-start | bytes 2433032 | tf_op jit(solution)/shard_map/ppermute | solution.py:220
  25.8 16.4 %collective-permute-start.3 = (bf16[96,4224]{1,0:T(8,128)(2,1)S(1)}, bf16[96,4224]{1,0:T(8,128)(2,1)S(1)}, u32[]{:S(2)}, u32[]{:S(2)}) collective-permute-start(bf16[96,4224]{1,0:T(8,128)(2,1)S(1)} %collective-permute-done.2.refs_2_), channel_id=1, source_target_pairs={{0,1},{1,0},{2,3},{3,2},{4,5},{5,4},{6,7},{7,6},{8,9},{9,8},{10,11... | collective-permute-start | bytes 2433032 | tf_op jit(solution)/shard_map/ppermute | solution.py:220
  25.8 20.9 %collective-permute-start = (bf16[96,4224]{1,0:T(8,128)(2,1)}, bf16[96,4224]{1,0:T(8,128)(2,1)}, u32[]{:S(2)}, u32[]{:S(2)}) collective-permute-start(bf16[96,4224]{1,0:T(8,128)(2,1)} %shard_map.37.refs_0_.refs_4_.refs_1_), channel_id=1, source_target_pairs={{0,4},{6,2},{1,5},{7,3},{8,12},{14,10},{9,13},{15,11},{16,20},{22,... | collective-permute-start | bytes 2433032 | tf_op jit(solution)/shard_map/ppermute | solution.py:214
  29.3 11.6 %collective-permute-start.7 = (bf16[48,4224]{1,0:T(8,128)(2,1)S(1)}, bf16[48,4224]{1,0:T(8,128)(2,1)S(1)}, u32[]{:S(2)}, u32[]{:S(2)}) collective-permute-start(bf16[48,4224]{1,0:T(8,128)(2,1)S(1)} %slice.13), channel_id=1, source_target_pairs={{0,8},{8,0},{16,24},{24,16},{1,9},{9,1},{17,25},{25,17},{2,10},{10... | collective-permute-start | bytes 1216520 | tf_op jit(solution)/shard_map/ppermute | solution.py:204
  30.9 11.3 %collective-permute-start.6 = (bf16[48,4224]{1,0:T(8,128)(2,1)S(1)}, bf16[48,4224]{1,0:T(8,128)(2,1)S(1)}, u32[]{:S(2)}, u32[]{:S(2)}) collective-permute-start(bf16[48,4224]{1,0:T(8,128)(2,1)S(1)} %slice.12), channel_id=1, source_target_pairs={{0,16},{8,24},{16,0},{24,8},{1,17},{9,25},{17,1},{25,9},{2,18},{10... | collective-permute-start | bytes 1216520 | tf_op jit(solution)/shard_map/ppermute | solution.py:203
  44.2 0.6 copy-start.1
  46.7 0.7 %copy-start.2 = (f32[32,1,128]{2,1,0:T(1,128)S(1)}, f32[32,1,128]{2,1,0:T(1,128)}, u32[]{:S(2)}) copy-start(f32[32,1,128]{2,1,0:T(1,128)} %copy-done.1) | copy-start | bytes 49156
  46.7 3.0 %collective-permute-start.8 = (bf16[96,4224]{1,0:T(8,128)(2,1)}, bf16[96,4224]{1,0:T(8,128)(2,1)S(1)}, u32[]{:S(2)}, u32[]{:S(2)}) collective-permute-start(bf16[96,4224]{1,0:T(8,128)(2,1)} %shard_map.39.refs_0_), channel_id=1, source_target_pairs={{0,1},{1,0},{2,3},{3,2},{4,5},{5,4},{6,7},{7,6},{8,9},{9,8},{10,11... | collective-permute-start | bytes 2433032 | tf_op jit(solution)/shard_map/ppermute | solution.py:223

commit v5 on v4

v5 whole, which is shorter than its diff:
```python
import functools

import jax
import jax.numpy as jnp
from jax import lax
from jax.experimental import pallas as pl
from jax.experimental.pallas import tpu as pltpu
from jax.sharding import Mesh, PartitionSpec as P

AXES = ("group", "z", "core")
LANES = 128
CHUNK = 512
PER_CALL = 4
VMEM = pl.BlockSpec(memory_space=pltpu.VMEM)


def ring_pairs(length, shift):
    if 2 * shift < length:
        return [(k, (k + shift) % length) for k in range(length)]
    pairs = []
    for k in range(length // 2):
        low, high = k, k + shift
        pairs.append((low, high) if k % 2 == 0 else (high, low))
    return pairs


def flip(count, bits):
    return [(k, k ^ bits) for k in range(count)]


def unit_rows(values):
    values = values.astype(jnp.float32)
    total = jnp.sum(values * values, axis=1, keepdims=True) + values.shape[1] * 1e-06
    return (values * lax.rsqrt(total)).astype(jnp.bfloat16)


def lane_rows(first, second):
    count = first.shape[1]
    both = jnp.concatenate([first, second, jnp.zeros((6, count), jnp.float32)], axis=0)
    if count < LANES:
        both = jnp.concatenate([both, jnp.zeros((8, LANES - count), jnp.float32)], axis=1)
    return both


def pack_kernel(rows_ref, cluster_ref, order_ref, block_ref):
    rows, width = rows_ref.shape
    block_ref[:, :width] = unit_rows(rows_ref[...])
    meta = lane_rows(cluster_ref[...].astype(jnp.float32) + 1.0, order_ref[...].astype(jnp.float32))
    turned = meta.T[:rows]
    cluster, order = turned[:, 0:1], turned[:, 1:2]
    high = jnp.floor(order / 256.0)
    lane = lax.broadcasted_iota(jnp.int32, (rows, LANES), 1)
    tail = jnp.where(lane == 0, cluster, jnp.where(lane == 1, high, order - 256.0 * high))
    block_ref[:, width:] = jnp.where(lane < 3, tail, 0.0).astype(jnp.bfloat16)


def pack(rows, cluster_ids, order_index):
    count, width = rows.shape
    return pl.pallas_call(
        pack_kernel,
        in_specs=[VMEM] * 3,
        out_specs=VMEM,
        out_shape=jax.ShapeDtypeStruct((count, width + LANES), jnp.bfloat16),
        cost_estimate=pl.CostEstimate(
            flops=4 * count * width, bytes_accessed=4 * count * width, transcendentals=count
        ),
    )(rows, cluster_ids.reshape(1, count), order_index.reshape(1, count))


def maxima_kernel(homed, visitor_pieces, pieces, carried, *refs):
    take = list(refs)
    visitor_refs = [[take.pop(0) for _ in range(n)] for n in visitor_pieces]
    block_refs = [[take.pop(0) for _ in range(n)] for n in pieces]
    carry_refs = [take.pop(0) for _ in pieces] if carried else []
    row_refs = [take.pop(0) for _ in homed]
    col_refs = [take.pop(0) for _ in pieces]
    units, dots = take if len(homed) > 1 else (None, take[0])
    width = block_refs[0][0].shape[1] - LANES
    rows = sum(ref.shape[0] for ref in block_refs[0])
    lanes = LANES if units is not None else rows

    visitor_meta = []
    for v, parts in enumerate(visitor_refs):
        place, tail = v * LANES, []
        for ref in parts:
            if units is not None:
                units[place : place + ref.shape[0], :] = ref[:, :width]
            tail.append(ref[:, width:].astype(jnp.float32))
            place += ref.shape[0]
        spare = (v + 1) * LANES - place
        if spare:
            if units is not None:
                units[place : place + spare, :] = jnp.zeros((spare, width), jnp.bfloat16)
            tail.append(jnp.zeros((spare, LANES), jnp.float32))
        turned = jnp.concatenate(tail, axis=0).T
        visitor_meta.append((turned[0:1, :lanes], turned[1:2, :lanes] * 256.0 + turned[2:3, :lanes]))
    right = visitor_refs[0][0] if units is None else units
    flat = [ref for parts in block_refs for ref in parts]
    for k in range(0, width, CHUNK):
        left = jnp.concatenate([ref[:, k : k + CHUNK] for ref in flat], axis=0)
        part = lax.dot_general(
            left,
            right[:, k : k + CHUNK],
            (((1,), (1,)), ((), ())),
            preferred_element_type=jnp.float32,
        )
        dots[...] = part if k == 0 else dots[...] + part

    row_best = [jnp.full((1, lanes), -1.0, jnp.float32) for _ in homed]
    lane = lax.broadcasted_iota(jnp.int32, (rows, LANES), 1)
    col_all = jnp.full((rows, LANES), -1.0, jnp.float32)
    for j, parts in enumerate(block_refs):
        tail = jnp.concatenate([ref[:, width:] for ref in parts], axis=0).astype(jnp.float32)
        block_cluster, block_order = tail[:, 0:1], tail[:, 1:2] * 256.0 + tail[:, 2:3]
        col_best = jnp.full((rows, 1), -1.0, jnp.float32)
        for v in range(len(homed)):
            cosine = dots[j * rows : (j + 1) * rows, v * lanes : (v + 1) * lanes]
            cluster, order = visitor_meta[v]
            same = (block_cluster == cluster) & (cluster > 0)
            seen = jnp.where(same & (block_order < order), cosine, -1.0)
            row_best[v] = jnp.maximum(row_best[v], jnp.max(seen, axis=0, keepdims=True))
            if homed[v]:
                seen = jnp.where(same & (order < block_order), cosine, -1.0)
                col_best = jnp.maximum(col_best, jnp.max(seen, axis=1, keepdims=True))
        col_all = jnp.where(lane == j, col_best, col_all)
    for v in range(len(homed)):
        row_refs[v][:, :lanes] = row_best[v]
        if lanes < LANES:
            row_refs[v][:, lanes:] = jnp.full((1, LANES - lanes), -1.0, jnp.float32)
    if rows < LANES:
        fill = jnp.full((LANES - rows, LANES), -1.0, jnp.float32)
        col_all = jnp.concatenate([col_all, fill], axis=0)
    turned = col_all.T
    for j in range(len(pieces)):
        best = turned[j : j + 1, :]
        col_refs[j][...] = jnp.maximum(best, carry_refs[j][...]) if carried else best


def maxima(homed, visitors, blocks, carry=None):
    rows, width = sum(piece.shape[0] for piece in blocks[0]), visitors[0][0].shape[1] - LANES
    count, lanes = len(visitors), LANES if len(visitors) > 1 else rows
    row_best, col_best = None, []
    for first in range(0, len(blocks), PER_CALL):
        part = blocks[first : first + PER_CALL]
        operands = [piece for block in visitors + part for piece in block]
        operands += carry[first : first + PER_CALL] if carry else []
        scratch = [pltpu.VMEM((count * LANES, width), jnp.bfloat16)] if count > 1 else []
        best = pl.pallas_call(
            functools.partial(
                maxima_kernel,
                homed,
                [len(block) for block in visitors],
                [len(block) for block in part],
                carry is not None,
            ),
            in_specs=[VMEM] * len(operands),
            out_specs=[VMEM] * (count + len(part)),
            out_shape=[jax.ShapeDtypeStruct((1, LANES), jnp.float32)] * (count + len(part)),
            scratch_shapes=scratch + [pltpu.VMEM((len(part) * rows, count * lanes), jnp.float32)],
            compiler_params=pltpu.CompilerParams(vmem_limit_bytes=40 * 2**20),
            cost_estimate=pl.CostEstimate(
                flops=2 * len(part) * rows * count * LANES * width,
                bytes_accessed=2 * (len(part) + count) * rows * width,
                transcendentals=0,
            ),
        )(*operands)
        row, col_best = best[:count], col_best + list(best[count:])
        row_best = row if row_best is None else [jnp.maximum(a, b) for a, b in zip(row_best, row)]
    return row_best, col_best


def gather_plane(block, groups):
    half = block.shape[0] // 2
    blocks = {0: [block]}
    for s in range(1, groups):
        low, high = s & -s, 1 << (s.bit_length() - 1)
        if low == high:
            blocks[s] = [lax.ppermute(block, "group", flip(groups, s))]
            continue
        top, bottom = blocks[s ^ high], blocks[s ^ low]
        top = top[0][:half] if len(top) == 1 else top[0]
        bottom = bottom[0][half:] if len(bottom) == 1 else bottom[1]
        blocks[s] = [
            lax.ppermute(top, "group", flip(groups, high)),
            lax.ppermute(bottom, "group", flip(groups, low)),
        ]
    return blocks


def copy_kernel(value_ref, other_ref, out_ref):
    out_ref[...] = value_ref[...]


def copy_behind(value, other):
    return pl.pallas_call(
        copy_kernel,
        in_specs=[VMEM, VMEM],
        out_specs=VMEM,
        out_shape=jax.ShapeDtypeStruct(value.shape, value.dtype),
    )(value, other)


def swap(block):
    return lax.ppermute(block, "core", flip(2, 1))


def send_home(best, route):
    home = lax.ppermute(best, "z", [(b, a) for a, b in route])
    if len(route) == lax.axis_size("z"):
        return home
    here = lax.axis_index("z")
    sent = functools.reduce(jnp.logical_or, [here == a for a, _ in route])
    return jnp.where(sent, home, -1.0)


def local(embeddings, cluster_ids, order_index):
    rows = embeddings.shape[0]
    groups, length = lax.axis_size("group"), lax.axis_size("z")
    routes = [ring_pairs(length, shift) for shift in range(1, length // 2 + 1)]
    own = pack(embeddings, cluster_ids, order_index)
    arrived = [lax.ppermute(own, "z", route) for route in routes]
    blocks = list(gather_plane(own, groups).values())

    cut = rows * 2 // 3 // 16 * 16
    homed, visitors = [0, 0], [[own], [swap(own)]]
    for block in arrived[:-1]:
        homed += [1, 1]
        visitors += [[block], [swap(block[:cut]), swap(block[cut:])]]
    row, col = maxima(homed, visitors, blocks)
    bests = [row[0], swap(row[1])]
    for index, route in enumerate(routes[:-1]):
        merged = jnp.maximum(row[2 * index + 2], swap(row[2 * index + 3]))
        bests.append(send_home(merged, route))

    last = copy_behind(arrived[-1], bests[-1])
    row, col = maxima([1, 1], [[last], [swap(last)]], blocks, col)
    bests.append(col[0])
    bests += [lax.ppermute(col[s], "group", flip(groups, s)) for s in range(1, groups)]
    bests.append(send_home(jnp.maximum(row[0], swap(row[1])), routes[-1]))
    return functools.reduce(jnp.maximum, bests)[0, :rows]


def solution(mesh):
    groups, members = mesh.devices.shape
    fine = Mesh(mesh.devices.reshape(groups, members // 2, 2), AXES)
    placed = (P(AXES, None), P(AXES), P(AXES))
    return jax.shard_map(local, mesh=fine, in_specs=placed, out_specs=P(AXES), check_vma=False)
```

time: 64.1 us -> 81 us (1.26)
  waiting for transfers between devices: 28.9 us -> 47.8 us
  blocking collectives: 12.6 us -> 0 us
  starting transfers between devices: 12.6 us -> 21 us
  local copies, waits for them, and re-layouts: 1.38 us -> 2.94 us
  Pallas kernels: 7.78 us -> 8.9 us
    ppermute x3 -> x12, waiting for transfers between devices: 0.01 us -> 26.7 us  [the longest x2 19.7 us: send_home(): home = lax.ppermute(best, 'z', [(b, a) for a, b in route])]
    all_to_all x1 -> x0, blocking collectives: 12.6 us -> none  [local(): lax.all_to_all(answer, AXES, split_axis=0, concat_axis=0, tiled=True)]
    ppermute x1, waiting for transfers between devices: 8.39 us -> 1.56 us  [gather_plane(): lax.ppermute(bottom, 'group', flip(groups, low))]
    ppermute x2, waiting for transfers between devices: 19.2 us -> 12.7 us  [local(): arrived = [lax.ppermute(own, 'z', route) for route in routes]]
    ppermute x3 -> x12, starting transfers between devices: 0.01 us -> 6.18 us  [the longest x3 3.49 us: local(): lax.ppermute(col[s], 'group', flip(groups, s))]
    ppermute x1, waiting for transfers between devices: 1.31 us -> 6.79 us  [gather_plane(): lax.ppermute(top, 'group', flip(groups, high))]
    ppermute x2, starting transfers between devices: 6.49 us -> 8.4 us  [local(): arrived = [lax.ppermute(own, 'z', route) for route in routes]]
    pallas_call x4 -> x3, Pallas kernels: 5.38 us -> 6.5 us  [the longest x2 4.35 us: maxima(): pl.pallas_call(functools.partial(maxima_kernel, homed, [len(block) for bl...]
  transfers between devices with their start and end apart: 9 -> 18, of which waited for: 4 -> 10; matrix products, arithmetic and copies ran while one was open for 0% -> 0% of each run, Pallas kernels for 7% -> 3%
where the time goes in v5:
time: 81 us; the launch traced here: 80.7 us
  waiting for transfers between devices  47.8 us (59%)
  starting transfers between devices  21 us (26%)
  Pallas kernels  8.9 us (11%)
  local copies, waits for them, and re-layouts  2.94 us (4%)
    ppermute x2, waiting for transfers between devices, send_home(): home = lax.ppermute(best, 'z', [(b, a) for a, b in route])  19.7 us
    ppermute x2, waiting for transfers between devices, local(): arrived = [lax.ppermute(own, 'z', route) for route in routes]  12.7 us
    ppermute x2, starting transfers between devices, local(): arrived = [lax.ppermute(own, 'z', route) for route in routes]  8.4 us
    ppermute x1, waiting for transfers between devices, gather_plane(): lax.ppermute(top, 'group', flip(groups, high))  6.79 us
    ppermute x7, waiting for transfers between devices, swap(): return lax.ppermute(block, 'core', flip(2, 1))  5.31 us
    pallas_call x2, Pallas kernels, maxima(): pl.pallas_call(functools.partial(maxima_kernel, homed, [len(block) for bl...  4.35 us
    ppermute x3, starting transfers between devices, local(): lax.ppermute(col[s], 'group', flip(groups, s))  3.49 us
    ppermute x2, starting transfers between devices, gather_plane(): blocks[s] = [lax.ppermute(block, 'group', flip(groups, s))]  3.01 us
  transfers between devices with their start and end apart: 18, of which 10 were waited for; matrix products, arithmetic and copies ran while one was open for 0% of the time, Pallas kernels for 3%

profile of v5, /device:TPU:0, one launch (start us, length us, event | category | flops | bytes accessed | tf_op | source)
XLA Modules:
  0.0 80.7 jit_solution(4114743498939592829)
XLA Ops:
  0.0 2.4 %shard_map.37.refs_0_.refs_5_.refs_2_ = bf16[96,4224]{1,0:T(8,128)(2,1)} custom-call(bf16[96,4096]{1,0:T(8,128)(2,1)} %rows_ref.1, s32[1,96]{1,0:T(1,128)} %bitcast.4, s32[1,96]{1,0:T(1,128)} %bitcast.5), custom_call_target="tpu_custom_call" | custom-call | flops 1572864 | bytes 1572864 | tf_op jit(solution)/shard_map/pallas_call | solution.py:59
  2.4 3.0 %collective-permute-start.1 = (bf16[96,4224]{1,0:T(8,128)(2,1)}, bf16[96,4224]{1,0:T(8,128)(2,1)S(1)}, u32[]{:S(2)}, u32[]{:S(2)}) collective-permute-start(bf16[96,4224]{1,0:T(8,128)(2,1)} %shard_map.37.refs_0_.refs_5_.refs_2_), channel_id=1, source_target_pairs={{0,2},{2,4},{4,6},{6,0},{1,3},{3,5},{5,7},{7,1},{8,10},{10,12},{12... | collective-permute-start | bytes 2433032 | tf_op jit(solution)/shard_map/ppermute | solution.py:221
  5.4 1.5 %collective-permute-start.4 = (bf16[96,4224]{1,0:T(8,128)(2,1)}, bf16[96,4224]{1,0:T(8,128)(2,1)S(1)}, u32[]{:S(2)}, u32[]{:S(2)}) collective-permute-start(bf16[96,4224]{1,0:T(8,128)(2,1)} %shard_map.37.refs_0_.refs_5_.refs_2_), channel_id=1, source_target_pairs={{0,8},{8,0},{16,24},{24,16},{1,9},{9,1},{17,25},{25,17},{2,10},{10... | collective-permute-start | bytes 2433032 | tf_op jit(solution)/shard_map/ppermute | solution.py:178
  6.9 1.5 %collective-permute-start.5 = (bf16[96,4224]{1,0:T(8,128)(2,1)}, bf16[96,4224]{1,0:T(8,128)(2,1)S(1)}, u32[]{:S(2)}, u32[]{:S(2)}) collective-permute-start(bf16[96,4224]{1,0:T(8,128)(2,1)} %shard_map.37.refs_0_.refs_5_.refs_2_), channel_id=1, source_target_pairs={{0,16},{8,24},{16,0},{24,8},{1,17},{9,25},{17,1},{25,9},{2,18},{10... | collective-permute-start | bytes 2433032 | tf_op jit(solution)/shard_map/ppermute | solution.py:178
  8.4 5.4 %collective-permute-start.11 = (bf16[96,4224]{1,0:T(8,128)(2,1)}, bf16[96,4224]{1,0:T(8,128)(2,1)}, u32[]{:S(2)}, u32[]{:S(2)}) collective-permute-start(bf16[96,4224]{1,0:T(8,128)(2,1)} %shard_map.37.refs_0_.refs_5_.refs_2_), channel_id=1, source_target_pairs={{0,4},{6,2},{1,5},{7,3},{8,12},{14,10},{9,13},{15,11},{16,20},{22,... | collective-permute-start | bytes 2433032 | tf_op jit(solution)/shard_map/ppermute | solution.py:221
  13.8 12.7 %collective-permute-done.1.refs_2_ = bf16[96,4224]{1,0:T(8,128)(2,1)S(1)} collective-permute-done((bf16[96,4224]{1,0:T(8,128)(2,1)}, bf16[96,4224]{1,0:T(8,128)(2,1)S(1)}, u32[]{:S(2)}, u32[]{:S(2)}) %collective-permute-start.1) | collective-permute-done | bytes 811040 | tf_op jit(solution)/shard_map/ppermute | solution.py:221
  26.7 1.8 %collective-permute-start.6 = (bf16[48,4224]{1,0:T(8,128)(2,1)S(1)}, bf16[48,4224]{1,0:T(8,128)(2,1)S(1)}, u32[]{:S(2)}, u32[]{:S(2)}) collective-permute-start(bf16[48,4224]{1,0:T(8,128)(2,1)S(1)} %slice.22), channel_id=1, source_target_pairs={{0,16},{8,24},{16,0},{24,8},{1,17},{9,25},{17,1},{25,9},{2,18},{10... | collective-permute-start | bytes 1216520 | tf_op jit(solution)/shard_map/ppermute | solution.py:184
  28.6 1.6 %collective-permute-start.7 = (bf16[48,4224]{1,0:T(8,128)(2,1)S(1)}, bf16[48,4224]{1,0:T(8,128)(2,1)S(1)}, u32[]{:S(2)}, u32[]{:S(2)}) collective-permute-start(bf16[48,4224]{1,0:T(8,128)(2,1)S(1)} %slice.23), channel_id=1, source_target_pairs={{0,8},{8,0},{16,24},{24,16},{1,9},{9,1},{17,25},{25,17},{2,10},{10... | collective-permute-start | bytes 1216520 | tf_op jit(solution)/shard_map/ppermute | solution.py:185
  30.3 1.5 %collective-permute-done.3.refs_4_ = bf16[32,4224]{1,0:T(8,128)(2,1)S(1)} collective-permute-done((bf16[32,4224]{1,0:T(8,128)(2,1)S(1)}, bf16[32,4224]{1,0:T(8,128)(2,1)S(1)}, u32[]{:S(2)}, u32[]{:S(2)}) %collective-permute-start.3) | collective-permute-done | bytes 270368 | tf_op jit(solution)/shard_map/ppermute | solution.py:204
  31.8 6.8 %collective-permute-done.6.refs_8_.refs_5_ = bf16[48,4224]{1,0:T(8,128)(2,1)S(1)} collective-permute-done((bf16[48,4224]{1,0:T(8,128)(2,1)S(1)}, bf16[48,4224]{1,0:T(8,128)(2,1)S(1)}, u32[]{:S(2)}, u32[]{:S(2)}) %collective-permute-start.6) | collective-permute-done | bytes 405536 | tf_op jit(solution)/shard_map/ppermute | solution.py:184
  38.6 1.6 %collective-permute-done.7.refs_9_.refs_6_ = bf16[48,4224]{1,0:T(8,128)(2,1)S(1)} collective-permute-done((bf16[48,4224]{1,0:T(8,128)(2,1)S(1)}, bf16[48,4224]{1,0:T(8,128)(2,1)S(1)}, u32[]{:S(2)}, u32[]{:S(2)}) %collective-permute-start.7) | collective-permute-done | bytes 405536 | tf_op jit(solution)/shard_map/ppermute | solution.py:185
  40.2 2.0 %shard_map.38 = (f32[1,128]{1,0:T(1,128)S(1)}, f32[1,128]{1,0:T(1,128)S(1)}, f32[1,128]{1,0:T(1,128)S(1)}, f32[1,128]{1,0:T(1,128)S(1)}, f32[1,128]{1,0:T(1,128)...) custom-call(bf16[96,4224]{1,0:T(8,128)(2,1)S(1)} %copy-done, ...), custom_call_target="tpu_custom_call" | custom-call | flops 1610612736 | bytes 6291456 | tf_op jit(solution)/shard_map/pallas_call | solution.py:148
  42.3 1.1 %collective-permute-done.9 = f32[1,128]{1,0:T(1,128)S(1)} collective-permute-done((f32[1,128]{1,0:T(1,128)S(1)}, f32[1,128]{1,0:T(1,128)S(1)}, u32[]{:S(2)}, u32[]{:S(2)}) %collective-permute-start.9) | collective-permute-done | bytes 544 | tf_op jit(solution)/shard_map/ppermute | solution.py:204
  43.4 0.7 collective-permute-start.10
  44.0 2.9 %collective-permute-done.10.other_ref = f32[1,128]{1,0:T(1,128)S(1)} collective-permute-done((f32[1,128]{1,0:T(1,128)S(1)}, f32[1,128]{1,0:T(1,128)S(1)}, u32[]{:S(2)}, u32[]{:S(2)}) %collective-permute-start.10) | collective-permute-done | bytes 544 | tf_op jit(solution)/shard_map/ppermute | solution.py:208
  47.4 2.1 %shard_map.39.refs_0_ = bf16[96,4224]{1,0:T(8,128)(2,1)} custom-call(bf16[96,4224]{1,0:T(8,128)(2,1)} %collective-permute-done.11.value_ref, f32[1,128]{1,0:T(1,128)} %copy-done.2), custom_call_target="tpu_custom_call" | custom-call | tf_op jit(solution)/shard_map/pallas_call | solution.py:195
  49.6 2.7 %collective-permute-done.12.refs_1_ = bf16[96,4224]{1,0:T(8,128)(2,1)} collective-permute-done((bf16[96,4224]{1,0:T(8,128)(2,1)}, bf16[96,4224]{1,0:T(8,128)(2,1)}, u32[]{:S(2)}, u32[]{:S(2)}) %collective-permute-start.12) | collective-permute-done | bytes 811040 | tf_op jit(solution)/shard_map/ppermute | solution.py:204
  52.2 1.1 %copy-done.1 = bf16[96,4224]{1,0:T(8,128)(2,1)S(1)} copy-done((bf16[96,4224]{1,0:T(8,128)(2,1)S(1)}, bf16[96,4224]{1,0:T(8,128)(2,1)}, u32[]{:S(2)}) %copy-start.1) | copy-done | bytes 811032
  53.4 2.3 %shard_map.40 = (f32[1,128]{1,0:T(1,128)S(1)}, f32[1,128]{1,0:T(1,128)S(1)}, f32[1,128]{1,0:T(1,128)S(1)}, f32[1,128]{1,0:T(1,128)S(1)}, f32[1,128]{1,0:T(1,128)S(1)}, /*index=5*/f32[1,128]{1,0:T(1,128)S(1)}) custom-call(bf16[96,4224]{1,0:T(8,128)(2,1)S(1)} %copy-done.1, bf16[96,4224]{1,0:T(8,128)(2,1)} %collective-permute-done.12.refs_1_, ...), custom_call_target="tpu_custom_call" | custom-call | flops 805306368 | bytes 4718592 | tf_op jit(solution)/shard_map/pallas_call | solution.py:148
  56.2 1.5 %collective-permute-start.13 = (f32[1,128]{1,0:T(1,128)S(1)}, f32[1,128]{1,0:T(1,128)S(1)}, u32[]{:S(2)}, u32[]{:S(2)}) collective-permute-start(f32[1,128]{1,0:T(1,128)S(1)} %get-tuple-element.28), channel_id=1, source_target_pairs={{0,8},{8,0},{16,24},{24,16},{1,9},{9,1},{17,25},{25,17},{2,10},{10... | collective-permute-start | bytes 1544 | tf_op jit(solution)/shard_map/ppermute | solution.py:238
  58.2 1.5 %collective-permute-start.15 = (f32[1,128]{1,0:T(1,128)S(1)}, f32[1,128]{1,0:T(1,128)S(1)}, u32[]{:S(2)}, u32[]{:S(2)}) collective-permute-start(f32[1,128]{1,0:T(1,128)S(1)} %get-tuple-element.30), channel_id=1, source_target_pairs={{0,24},{8,16},{16,8},{24,0},{1,25},{9,17},{17,9},{25,1},{2,26},{10... | collective-permute-start | bytes 1544 | tf_op jit(solution)/shard_map/ppermute | solution.py:238
  59.7 1.3 %collective-permute-start.17 = (f32[1,128]{1,0:T(1,128)S(1)}, f32[1,128]{1,0:T(1,128)S(1)}, u32[]{:S(2)}, u32[]{:S(2)}) collective-permute-start(f32[1,128]{1,0:T(1,128)S(1)} %max.34), channel_id=1, source_target_pairs={{4,0},{2,6},{5,1},{3,7},{12,8},{10,14},{13,9},{11,15},{20,16},{18,... | collective-permute-start | bytes 1544 | tf_op jit(solution)/shard_map/ppermute | solution.py:208
  61.3 1.4 %collective-permute-done.15 = f32[1,128]{1,0:T(1,128)S(1)} collective-permute-done((f32[1,128]{1,0:T(1,128)S(1)}, f32[1,128]{1,0:T(1,128)S(1)}, u32[]{:S(2)}, u32[]{:S(2)}) %collective-permute-start.15) | collective-permute-done | bytes 544 | tf_op jit(solution)/shard_map/ppermute | solution.py:238
  62.7 16.9 %collective-permute-done.17 = f32[1,128]{1,0:T(1,128)S(1)} collective-permute-done((f32[1,128]{1,0:T(1,128)S(1)}, f32[1,128]{1,0:T(1,128)S(1)}, u32[]{:S(2)}, u32[]{:S(2)}) %collective-permute-start.17) | collective-permute-done | bytes 544 | tf_op jit(solution)/shard_map/ppermute | solution.py:208
  (32 shorter events, 3.3 us)
Async XLA Ops:
  2.4 24.2 %collective-permute-start.1 = (bf16[96,4224]{1,0:T(8,128)(2,1)}, bf16[96,4224]{1,0:T(8,128)(2,1)S(1)}, u32[]{:S(2)}, u32[]{:S(2)}) collective-permute-start(bf16[96,4224]{1,0:T(8,128)(2,1)} %shard_map.37.refs_0_.refs_5_.refs_2_), channel_id=1, source_target_pairs={{0,2},{2,4},{4,6},{6,0},{1,3},{3,5},{5,7},{7,1},{8,10},{10,12},{12... | collective-permute-start | bytes 2433032 | tf_op jit(solution)/shard_map/ppermute | solution.py:221
  5.4 21.3 %collective-permute-start.4 = (bf16[96,4224]{1,0:T(8,128)(2,1)}, bf16[96,4224]{1,0:T(8,128)(2,1)S(1)}, u32[]{:S(2)}, u32[]{:S(2)}) collective-permute-start(bf16[96,4224]{1,0:T(8,128)(2,1)} %shard_map.37.refs_0_.refs_5_.refs_2_), channel_id=1, source_target_pairs={{0,8},{8,0},{16,24},{24,16},{1,9},{9,1},{17,25},{25,17},{2,10},{10... | collective-permute-start | bytes 2433032 | tf_op jit(solution)/shard_map/ppermute | solution.py:178
  6.9 21.6 %collective-permute-start.5 = (bf16[96,4224]{1,0:T(8,128)(2,1)}, bf16[96,4224]{1,0:T(8,128)(2,1)S(1)}, u32[]{:S(2)}, u32[]{:S(2)}) collective-permute-start(bf16[96,4224]{1,0:T(8,128)(2,1)} %shard_map.37.refs_0_.refs_5_.refs_2_), channel_id=1, source_target_pairs={{0,16},{8,24},{16,0},{24,8},{1,17},{9,25},{17,1},{25,9},{2,18},{10... | collective-permute-start | bytes 2433032 | tf_op jit(solution)/shard_map/ppermute | solution.py:178
  8.4 21.7 %collective-permute-start = (bf16[96,4224]{1,0:T(8,128)(2,1)}, bf16[96,4224]{1,0:T(8,128)(2,1)S(1)}, u32[]{:S(2)}, u32[]{:S(2)}) collective-permute-start(bf16[96,4224]{1,0:T(8,128)(2,1)} %shard_map.37.refs_0_.refs_5_.refs_2_), channel_id=1, source_target_pairs={{0,1},{1,0},{2,3},{3,2},{4,5},{5,4},{6,7},{7,6},{8,9},{9,8},{10,11... | collective-permute-start | bytes 2433032 | tf_op jit(solution)/shard_map/ppermute | solution.py:204
  8.4 35.6 %collective-permute-start.11 = (bf16[96,4224]{1,0:T(8,128)(2,1)}, bf16[96,4224]{1,0:T(8,128)(2,1)}, u32[]{:S(2)}, u32[]{:S(2)}) collective-permute-start(bf16[96,4224]{1,0:T(8,128)(2,1)} %shard_map.37.refs_0_.refs_5_.refs_2_), channel_id=1, source_target_pairs={{0,4},{6,2},{1,5},{7,3},{8,12},{14,10},{9,13},{15,11},{16,20},{22,... | collective-permute-start | bytes 2433032 | tf_op jit(solution)/shard_map/ppermute | solution.py:221
  26.6 13.6 %collective-permute-start.2 = (bf16[64,4224]{1,0:T(8,128)(2,1)S(1)}, bf16[64,4224]{1,0:T(8,128)(2,1)S(1)}, u32[]{:S(2)}, u32[]{:S(2)}) collective-permute-start(bf16[64,4224]{1,0:T(8,128)(2,1)S(1)} %slice.20), channel_id=1, source_target_pairs={{0,1},{1,0},{2,3},{3,2},{4,5},{5,4},{6,7},{7,6},{8,9},{9,8},{10,11... | collective-permute-start | bytes 1622024 | tf_op jit(solution)/shard_map/ppermute | solution.py:204
  26.7 13.4 %copy-start = (bf16[96,4224]{1,0:T(8,128)(2,1)S(1)}, bf16[96,4224]{1,0:T(8,128)(2,1)}, u32[]{:S(2)}) copy-start(bf16[96,4224]{1,0:T(8,128)(2,1)} %shard_map.37.refs_0_.refs_5_.refs_2_) | copy-start | bytes 2433028
  26.7 11.9 %collective-permute-start.6 = (bf16[48,4224]{1,0:T(8,128)(2,1)S(1)}, bf16[48,4224]{1,0:T(8,128)(2,1)S(1)}, u32[]{:S(2)}, u32[]{:S(2)}) collective-permute-start(bf16[48,4224]{1,0:T(8,128)(2,1)S(1)} %slice.22), channel_id=1, source_target_pairs={{0,16},{8,24},{16,0},{24,8},{1,17},{9,25},{17,1},{25,9},{2,18},{10... | collective-permute-start | bytes 1216520 | tf_op jit(solution)/shard_map/ppermute | solution.py:184
  28.6 11.6 %collective-permute-start.7 = (bf16[48,4224]{1,0:T(8,128)(2,1)S(1)}, bf16[48,4224]{1,0:T(8,128)(2,1)S(1)}, u32[]{:S(2)}, u32[]{:S(2)}) collective-permute-start(bf16[48,4224]{1,0:T(8,128)(2,1)S(1)} %slice.23), channel_id=1, source_target_pairs={{0,8},{8,0},{16,24},{24,16},{1,9},{9,1},{17,25},{25,17},{2,10},{10... | collective-permute-start | bytes 1216520 | tf_op jit(solution)/shard_map/ppermute | solution.py:185
  30.2 1.6 %collective-permute-start.3 = (bf16[32,4224]{1,0:T(8,128)(2,1)S(1)}, bf16[32,4224]{1,0:T(8,128)(2,1)S(1)}, u32[]{:S(2)}, u32[]{:S(2)}) collective-permute-start(bf16[32,4224]{1,0:T(8,128)(2,1)S(1)} %slice.21), channel_id=1, source_target_pairs={{0,1},{1,0},{2,3},{3,2},{4,5},{5,4},{6,7},{7,6},{8,9},{9,8},{10,11... | collective-permute-start | bytes 811016 | tf_op jit(solution)/shard_map/ppermute | solution.py:204
  42.2 1.2 %collective-permute-start.9 = (f32[1,128]{1,0:T(1,128)S(1)}, f32[1,128]{1,0:T(1,128)S(1)}, u32[]{:S(2)}, u32[]{:S(2)}) collective-permute-start(f32[1,128]{1,0:T(1,128)S(1)} %get-tuple-element.22), channel_id=1, source_target_pairs={{0,1},{1,0},{2,3},{3,2},{4,5},{5,4},{6,7},{7,6},{8,9},{9,8},{10,11... | collective-permute-start | bytes 1544 | tf_op jit(solution)/shard_map/ppermute | solution.py:204
  43.4 3.5 %collective-permute-start.10 = (f32[1,128]{1,0:T(1,128)S(1)}, f32[1,128]{1,0:T(1,128)S(1)}, u32[]{:S(2)}, u32[]{:S(2)}) collective-permute-start(f32[1,128]{1,0:T(1,128)S(1)} %max.28), channel_id=1, source_target_pairs={{2,0},{4,2},{6,4},{0,6},{3,1},{5,3},{7,5},{1,7},{10,8},{12,10},{14... | collective-permute-start | bytes 1544 | tf_op jit(solution)/shard_map/ppermute | solution.py:208
  46.9 0.5 copy-start.2
  49.6 2.7 %collective-permute-start.12 = (bf16[96,4224]{1,0:T(8,128)(2,1)}, bf16[96,4224]{1,0:T(8,128)(2,1)}, u32[]{:S(2)}, u32[]{:S(2)}) collective-permute-start(bf16[96,4224]{1,0:T(8,128)(2,1)} %shard_map.39.refs_0_), channel_id=1, source_target_pairs={{0,1},{1,0},{2,3},{3,2},{4,5},{5,4},{6,7},{7,6},{8,9},{9,8},{10,11... | collective-permute-start | bytes 2433032 | tf_op jit(solution)/shard_map/ppermute | solution.py:204
  52.2 1.1 %copy-start.1 = (bf16[96,4224]{1,0:T(8,128)(2,1)S(1)}, bf16[96,4224]{1,0:T(8,128)(2,1)}, u32[]{:S(2)}) copy-start(bf16[96,4224]{1,0:T(8,128)(2,1)} %shard_map.39.refs_0_) | copy-start | bytes 2433028
  55.7 4.0 %collective-permute-start.16 = (f32[1,128]{1,0:T(1,128)S(1)}, f32[1,128]{1,0:T(1,128)S(1)}, u32[]{:S(2)}, u32[]{:S(2)}) collective-permute-start(f32[1,128]{1,0:T(1,128)S(1)} %get-tuple-element.32), channel_id=1, source_target_pairs={{0,1},{1,0},{2,3},{3,2},{4,5},{5,4},{6,7},{7,6},{8,9},{9,8},{10,11... | collective-permute-start | bytes 1544 | tf_op jit(solution)/shard_map/ppermute | solution.py:204
  55.9 5.2 %collective-permute-start.8 = (f32[1,128]{1,0:T(1,128)S(1)}, f32[1,128]{1,0:T(1,128)S(1)}, u32[]{:S(2)}, u32[]{:S(2)}) collective-permute-start(f32[1,128]{1,0:T(1,128)S(1)} %get-tuple-element.20), channel_id=1, source_target_pairs={{0,1},{1,0},{2,3},{3,2},{4,5},{5,4},{6,7},{7,6},{8,9},{9,8},{10,11... | collective-permute-start | bytes 1544 | tf_op jit(solution)/shard_map/ppermute | solution.py:204
  56.2 4.8 %collective-permute-start.13 = (f32[1,128]{1,0:T(1,128)S(1)}, f32[1,128]{1,0:T(1,128)S(1)}, u32[]{:S(2)}, u32[]{:S(2)}) collective-permute-start(f32[1,128]{1,0:T(1,128)S(1)} %get-tuple-element.28), channel_id=1, source_target_pairs={{0,8},{8,0},{16,24},{24,16},{1,9},{9,1},{17,25},{25,17},{2,10},{10... | collective-permute-start | bytes 1544 | tf_op jit(solution)/shard_map/ppermute | solution.py:238
  57.7 3.5 %collective-permute-start.14 = (f32[1,128]{1,0:T(1,128)S(1)}, f32[1,128]{1,0:T(1,128)S(1)}, u32[]{:S(2)}, u32[]{:S(2)}) collective-permute-start(f32[1,128]{1,0:T(1,128)S(1)} %get-tuple-element.29), channel_id=1, source_target_pairs={{0,16},{8,24},{16,0},{24,8},{1,17},{9,25},{17,1},{25,9},{2,18},{10... | collective-permute-start | bytes 1544 | tf_op jit(solution)/shard_map/ppermute | solution.py:238
  58.2 4.4 %collective-permute-start.15 = (f32[1,128]{1,0:T(1,128)S(1)}, f32[1,128]{1,0:T(1,128)S(1)}, u32[]{:S(2)}, u32[]{:S(2)}) collective-permute-start(f32[1,128]{1,0:T(1,128)S(1)} %get-tuple-element.30), channel_id=1, source_target_pairs={{0,24},{8,16},{16,8},{24,0},{1,25},{9,17},{17,9},{25,1},{2,26},{10... | collective-permute-start | bytes 1544 | tf_op jit(solution)/shard_map/ppermute | solution.py:238
  59.7 19.8 %collective-permute-start.17 = (f32[1,128]{1,0:T(1,128)S(1)}, f32[1,128]{1,0:T(1,128)S(1)}, u32[]{:S(2)}, u32[]{:S(2)}) collective-permute-start(f32[1,128]{1,0:T(1,128)S(1)} %max.34), channel_id=1, source_target_pairs={{4,0},{2,6},{5,1},{3,7},{12,8},{10,14},{13,9},{11,15},{20,16},{18,... | collective-permute-start | bytes 1544 | tf_op jit(solution)/shard_map/ppermute | solution.py:208
  79.6 0.7 copy-start.3

commit v6 on v5

--- a/solution.py
+++ b/solution.py
@@ -14,16 +14,6 @@
 VMEM = pl.BlockSpec(memory_space=pltpu.VMEM)
 
 
-def ring_pairs(length, shift):
-    if 2 * shift < length:
-        return [(k, (k + shift) % length) for k in range(length)]
-    pairs = []
-    for k in range(length // 2):
-        low, high = k, k + shift
-        pairs.append((low, high) if k % 2 == 0 else (high, low))
-    return pairs
-
-
 def flip(count, bits):
     return [(k, k ^ bits) for k in range(count)]
 
@@ -34,18 +24,19 @@
     return (values * lax.rsqrt(total)).astype(jnp.bfloat16)
 
 
-def lane_rows(first, second):
-    count = first.shape[1]
-    both = jnp.concatenate([first, second, jnp.zeros((6, count), jnp.float32)], axis=0)
-    if count < LANES:
-        both = jnp.concatenate([both, jnp.zeros((8, LANES - count), jnp.float32)], axis=1)
-    return both
-
-
 def pack_kernel(rows_ref, cluster_ref, order_ref, block_ref):
     rows, width = rows_ref.shape
     block_ref[:, :width] = unit_rows(rows_ref[...])
-    meta = lane_rows(cluster_ref[...].astype(jnp.float32) + 1.0, order_ref[...].astype(jnp.float32))
+    meta = jnp.concatenate(
+        [
+            cluster_ref[...].astype(jnp.float32) + 1.0,
+            order_ref[...].astype(jnp.float32),
+            jnp.zeros((6, rows), jnp.float32),
+        ],
+        axis=0,
+    )
+    if rows < LANES:
+        meta = jnp.concatenate([meta, jnp.zeros((8, LANES - rows), jnp.float32)], axis=1)
     turned = meta.T[:rows]
     cluster, order = turned[:, 0:1], turned[:, 1:2]
     high = jnp.floor(order / 256.0)
@@ -71,9 +62,9 @@
     take = list(refs)
     visitor_refs = [[take.pop(0) for _ in range(n)] for n in visitor_pieces]
     block_refs = [[take.pop(0) for _ in range(n)] for n in pieces]
-    carry_refs = [take.pop(0) for _ in pieces] if carried else []
+    carry_refs = [take.pop(0) for _ in range(2)] if carried else []
     row_refs = [take.pop(0) for _ in homed]
-    col_refs = [take.pop(0) for _ in pieces]
+    col_refs = [take.pop(0) for _ in range(2)]
     units, dots = take if len(homed) > 1 else (None, take[0])
     width = block_refs[0][0].shape[1] - LANES
     rows = sum(ref.shape[0] for ref in block_refs[0])
@@ -94,13 +85,13 @@
             tail.append(jnp.zeros((spare, LANES), jnp.float32))
         turned = jnp.concatenate(tail, axis=0).T
         visitor_meta.append((turned[0:1, :lanes], turned[1:2, :lanes] * 256.0 + turned[2:3, :lanes]))
-    right = visitor_refs[0][0] if units is None else units
+    right = visitor_refs[0] if units is None else [units]
     flat = [ref for parts in block_refs for ref in parts]
     for k in range(0, width, CHUNK):
         left = jnp.concatenate([ref[:, k : k + CHUNK] for ref in flat], axis=0)
         part = lax.dot_general(
             left,
-            right[:, k : k + CHUNK],
+            jnp.concatenate([ref[:, k : k + CHUNK] for ref in right], axis=0),
             (((1,), (1,)), ((), ())),
             preferred_element_type=jnp.float32,
         )
@@ -131,19 +122,19 @@
         fill = jnp.full((LANES - rows, LANES), -1.0, jnp.float32)
         col_all = jnp.concatenate([col_all, fill], axis=0)
     turned = col_all.T
-    for j in range(len(pieces)):
-        best = turned[j : j + 1, :]
-        col_refs[j][...] = jnp.maximum(best, carry_refs[j][...]) if carried else best
-
-
-def maxima(homed, visitors, blocks, carry=None):
-    rows, width = sum(piece.shape[0] for piece in blocks[0]), visitors[0][0].shape[1] - LANES
+    for c, col_ref in enumerate(col_refs):
+        best = turned[c * PER_CALL : (c + 1) * PER_CALL]
+        col_ref[...] = jnp.maximum(best, carry_refs[c][...]) if carried else best
+
+
+def maxima(homed, visitors, mine, others, carry=None):
+    rows, width = sum(piece.shape[0] for piece in mine[0]), visitors[0][0].shape[1] - LANES
     count, lanes = len(visitors), LANES if len(visitors) > 1 else rows
     row_best, col_best = None, []
-    for first in range(0, len(blocks), PER_CALL):
-        part = blocks[first : first + PER_CALL]
+    for first in range(0, len(mine), PER_CALL):
+        part = mine[first : first + PER_CALL] + others[first : first + PER_CALL]
         operands = [piece for block in visitors + part for piece in block]
-        operands += carry[first : first + PER_CALL] if carry else []
+        operands += carry[first // PER_CALL] if carry else []
         scratch = [pltpu.VMEM((count * LANES, width), jnp.bfloat16)] if count > 1 else []
         best = pl.pallas_call(
             functools.partial(
@@ -154,8 +145,9 @@
                 carry is not None,
             ),
             in_specs=[VMEM] * len(operands),
-            out_specs=[VMEM] * (count + len(part)),
-            out_shape=[jax.ShapeDtypeStruct((1, LANES), jnp.float32)] * (count + len(part)),
+            out_specs=[VMEM] * (count + 2),
+            out_shape=[jax.ShapeDtypeStruct((1, LANES), jnp.float32)] * count
+            + [jax.ShapeDtypeStruct((PER_CALL, LANES), jnp.float32)] * 2,
             scratch_shapes=scratch + [pltpu.VMEM((len(part) * rows, count * lanes), jnp.float32)],
             compiler_params=pltpu.CompilerParams(vmem_limit_bytes=40 * 2**20),
             cost_estimate=pl.CostEstimate(
@@ -164,27 +156,10 @@
                 transcendentals=0,
             ),
         )(*operands)
-        row, col_best = best[:count], col_best + list(best[count:])
+        row = best[:count]
         row_best = row if row_best is None else [jnp.maximum(a, b) for a, b in zip(row_best, row)]
+        col_best.append(list(best[count:]))
     return row_best, col_best
-
-
-def gather_plane(block, groups):
-    half = block.shape[0] // 2
-    blocks = {0: [block]}
-    for s in range(1, groups):
-        low, high = s & -s, 1 << (s.bit_length() - 1)
-        if low == high:
-            blocks[s] = [lax.ppermute(block, "group", flip(groups, s))]
-            continue
-        top, bottom = blocks[s ^ high], blocks[s ^ low]
-        top = top[0][:half] if len(top) == 1 else top[0]
-        bottom = bottom[0][half:] if len(bottom) == 1 else bottom[1]
-        blocks[s] = [
-            lax.ppermute(top, "group", flip(groups, high)),
-            lax.ppermute(bottom, "group", flip(groups, low)),
-        ]
-    return blocks
 
 
 def copy_kernel(value_ref, other_ref, out_ref):
@@ -194,10 +169,22 @@
 def copy_behind(value, other):
     return pl.pallas_call(
         copy_kernel,
-        in_specs=[VMEM, VMEM],
+        in_specs=[VMEM, pl.BlockSpec(memory_space=pl.ANY)],
         out_specs=VMEM,
         out_shape=jax.ShapeDtypeStruct(value.shape, value.dtype),
     )(value, other)
+
+
+def gather_plane(block, groups, other):
+    half = block.shape[0] // 2
+    blocks = {0: [block]}
+    halves = block[:half], block[half:]
+    for s in range(1, groups):
+        low, high = s & -s, 1 << (s.bit_length() - 1)
+        steps = (high, low)
+        ways = halves if low == high else (copy_behind(blocks[s ^ high][0], other), blocks[s ^ low][1])
+        blocks[s] = [lax.ppermute(p, "group", flip(groups, step)) for p, step in zip(ways, steps)]
+    return blocks
 
 
 def swap(block):
@@ -216,27 +203,29 @@
 def local(embeddings, cluster_ids, order_index):
     rows = embeddings.shape[0]
     groups, length = lax.axis_size("group"), lax.axis_size("z")
-    routes = [ring_pairs(length, shift) for shift in range(1, length // 2 + 1)]
     own = pack(embeddings, cluster_ids, order_index)
-    arrived = [lax.ppermute(own, "z", route) for route in routes]
-    blocks = list(gather_plane(own, groups).values())
-
-    cut = rows * 2 // 3 // 16 * 16
-    homed, visitors = [0, 0], [[own], [swap(own)]]
-    for block in arrived[:-1]:
-        homed += [1, 1]
-        visitors += [[block], [swap(block[:cut]), swap(block[cut:])]]
-    row, col = maxima(homed, visitors, blocks)
-    bests = [row[0], swap(row[1])]
-    for index, route in enumerate(routes[:-1]):
-        merged = jnp.maximum(row[2 * index + 2], swap(row[2 * index + 3]))
-        bests.append(send_home(merged, route))
-
-    last = copy_behind(arrived[-1], bests[-1])
-    row, col = maxima([1, 1], [[last], [swap(last)]], blocks, col)
-    bests.append(col[0])
-    bests += [lax.ppermute(col[s], "group", flip(groups, s)) for s in range(1, groups)]
-    bests.append(send_home(jnp.maximum(row[0], swap(row[1])), routes[-1]))
+    pieces, routes, arrived = [own], [], []
+    for shift in range(1, length // 2 + 1):
+        sources = range(length if 2 * shift < length else length // 2)
+        routes.append([(a, (a + shift) % length) for a in sources])
+        hops = [((a + shift - 1) % length, (a + shift) % length) for a in sources]
+        pieces = [lax.ppermute(piece, "z", hops) for piece in pieces]
+        arrived.append(pieces)
+    across = swap(own)
+    mine = list(gather_plane(own, groups, across).values())
+    others = [[across]] + [[swap(part) for part in parts] for parts in mine[1:]]
+
+    homed = [0] + [1] * (len(routes) - 1)
+    row, col = maxima(homed, [[own]] + arrived[:-1], mine, others)
+    bests = [row[0]] + [send_home(best, route) for best, route in zip(row[1:], routes)]
+    row, col = maxima([1], arrived[-1:], mine, others, col)
+    bests.append(send_home(row[0], routes[-1]))
+    merged = [jnp.maximum(best, swap(other)) for best, other in col]
+    for s in range(groups):
+        best = merged[s // PER_CALL]
+        if s:
+            best = lax.ppermute(best, "group", flip(groups, s))
+        bests.append(best[s % PER_CALL][None])
     return functools.reduce(jnp.maximum, bests)[0, :rows]
 
 

time: 81 us -> 68.8 us (0.85)
  waiting for transfers between devices: 47.8 us -> 25.4 us
  starting transfers between devices: 21 us -> 26.9 us
  Pallas kernels: 8.9 us -> 11.1 us
  local copies, waits for them, and re-layouts: 2.94 us -> 5.02 us
    ppermute x2, waiting for transfers between devices: 19.7 us -> 1.29 us  [send_home(): home = lax.ppermute(best, 'z', [(b, a) for a, b in route])]
    ppermute x2, starting transfers between devices: 1.95 us -> 9.69 us  [send_home(): home = lax.ppermute(best, 'z', [(b, a) for a, b in route])]
    ppermute x9 -> x11, starting transfers between devices: 18.3 us -> 15.5 us  [the longest x6 9.75 us: gather_plane(): lax.ppermute(p, 'group', flip(groups, step))]
    ppermute x7 -> x8, waiting for transfers between devices: 5.31 us -> 2.76 us  [swap(): return lax.ppermute(block, 'core', flip(2, 1))]
    pallas_call x2, Pallas kernels: 4.35 us -> 6.89 us  [maxima(): pl.pallas_call(functools.partial(maxima_kernel, homed, [len(block) for bl...]
    slice x4 -> x1, local copies, waits for them, and re-layouts: 0.11 us -> 1.92 us  [gather_plane(): halves = (block[:half], block[half:])]
    ppermute x9 -> x11, waiting for transfers between devices: 22.7 us -> 21.3 us  [the longest x6 21.3 us: gather_plane(): lax.ppermute(p, 'group', flip(groups, step))]
    ppermute x7 -> x8, starting transfers between devices: 0.74 us -> 1.71 us  [swap(): return lax.ppermute(block, 'core', flip(2, 1))]
  transfers between devices with their start and end apart: 18 -> 21, of which waited for: 10 -> 9; matrix products, arithmetic and copies ran while one was open for 0% -> 3% of each run, Pallas kernels for 3% -> 8%
where the time goes in v6:
time: 68.8 us; the launch traced here: 68.5 us
  starting transfers between devices  26.9 us (39%)
  waiting for transfers between devices  25.4 us (37%)
  Pallas kernels  11.1 us (16%)
  local copies, waits for them, and re-layouts  5.02 us (7%)
    ppermute x6, waiting for transfers between devices, gather_plane(): lax.ppermute(p, 'group', flip(groups, step))  21.3 us
    ppermute x6, starting transfers between devices, gather_plane(): lax.ppermute(p, 'group', flip(groups, step))  9.75 us
    ppermute x2, starting transfers between devices, send_home(): home = lax.ppermute(best, 'z', [(b, a) for a, b in route])  9.69 us
    pallas_call x2, Pallas kernels, maxima(): pl.pallas_call(functools.partial(maxima_kernel, homed, [len(block) for bl...  6.89 us
    ppermute x3, starting transfers between devices, local(): best = lax.ppermute(best, 'group', flip(groups, s))  3.49 us
    ppermute x8, waiting for transfers between devices, swap(): return lax.ppermute(block, 'core', flip(2, 1))  2.76 us
    unnamed x10, local copies, waits for them, and re-layouts  2.58 us
    pallas_call x1, Pallas kernels, pack(): pl.pallas_call(pack_kernel, in_specs=[VMEM] * 3, out_specs=VMEM, out_shap...  2.4 us
  transfers between devices with their start and end apart: 21, of which 9 were waited for; matrix products, arithmetic and copies ran while one was open for 3% of the time, Pallas kernels for 8%

profile of v6, /device:TPU:0, one launch (start us, length us, event | category | flops | bytes accessed | tf_op | source)
XLA Modules:
  0.0 68.5 jit_solution(18028502175363803651)
XLA Ops:
  0.0 2.4 %shard_map.37.refs_0_.refs_2_.refs_1_ = bf16[96,4224]{1,0:T(8,128)(2,1)} custom-call(bf16[96,4096]{1,0:T(8,128)(2,1)} %rows_ref.1, s32[1,96]{1,0:T(1,128)} %bitcast.4, s32[1,96]{1,0:T(1,128)} %bitcast.5), custom_call_target="tpu_custom_call" | custom-call | flops 1572864 | bytes 1572864 | tf_op jit(solution)/shard_map/pallas_call | solution.py:50
  2.9 1.9 %fusion.3 = (bf16[48,4224]{1,0:T(8,128)(2,1)S(1)}, bf16[48,4224]{1,0:T(8,128)(2,1)}) fusion(bf16[96,4224]{1,0:T(8,128)(2,1)} %shard_map.37.refs_0_.refs_2_.refs_1_), kind=kLoop, calls=%fused_computation.6 | loop fusion | bytes 1622016 | tf_op jit(solution)/shard_map/slice | solution.py:181
  4.8 2.6 %collective-permute-start.1 = (bf16[48,4224]{1,0:T(8,128)(2,1)}, bf16[48,4224]{1,0:T(8,128)(2,1)S(1)}, u32[]{:S(2)}, u32[]{:S(2)}) collective-permute-start(bf16[48,4224]{1,0:T(8,128)(2,1)} %get-tuple-element.20), channel_id=1, source_target_pairs={{0,8},{8,0},{16,24},{24,16},{1,9},{9,1},{17,25},{25,17},{2,10},{10... | collective-permute-start | bytes 1216520 | tf_op jit(solution)/shard_map/ppermute | solution.py:186
  7.3 1.6 %collective-permute-start = (bf16[96,4224]{1,0:T(8,128)(2,1)S(1)}, bf16[96,4224]{1,0:T(8,128)(2,1)}, u32[]{:S(2)}, u32[]{:S(2)}) collective-permute-start(bf16[96,4224]{1,0:T(8,128)(2,1)S(1)} %copy-done), channel_id=1, source_target_pairs={{0,2},{2,4},{4,6},{6,0},{1,3},{3,5},{5,7},{7,1},{8,10},{10,12},{12... | collective-permute-start | bytes 2433032 | tf_op jit(solution)/shard_map/ppermute | solution.py:212
  8.9 1.5 %collective-permute-start.4 = (bf16[48,4224]{1,0:T(8,128)(2,1)S(1)}, bf16[48,4224]{1,0:T(8,128)(2,1)S(1)}, u32[]{:S(2)}, u32[]{:S(2)}) collective-permute-start(bf16[48,4224]{1,0:T(8,128)(2,1)S(1)} %get-tuple-element.19), channel_id=1, source_target_pairs={{0,16},{8,24},{16,0},{24,8},{1,17},{9,25},{17,1},{25,9},{2,18},{10... | collective-permute-start | bytes 1216520 | tf_op jit(solution)/shard_map/ppermute | solution.py:186
  11.0 6.8 %collective-permute-done.1.value_ref.refs_3_.refs_2_ = bf16[48,4224]{1,0:T(8,128)(2,1)S(1)} collective-permute-done((bf16[48,4224]{1,0:T(8,128)(2,1)}, bf16[48,4224]{1,0:T(8,128)(2,1)S(1)}, u32[]{:S(2)}, u32[]{:S(2)}) %collective-permute-start.1) | collective-permute-done | bytes 405536 | tf_op jit(solution)/shard_map/ppermute | solution.py:186
  17.8 2.0 %collective-permute-start.3 = (bf16[48,4224]{1,0:T(8,128)(2,1)}, bf16[48,4224]{1,0:T(8,128)(2,1)S(1)}, u32[]{:S(2)}, u32[]{:S(2)}) collective-permute-start(bf16[48,4224]{1,0:T(8,128)(2,1)} %get-tuple-element.20), channel_id=1, source_target_pairs={{0,16},{8,24},{16,0},{24,8},{1,17},{9,25},{17,1},{25,9},{2,18},{10... | collective-permute-start | bytes 1216520 | tf_op jit(solution)/shard_map/ppermute | solution.py:186
  20.1 1.2 %collective-permute-start.7 = (bf16[48,4224]{1,0:T(8,128)(2,1)S(1)}, bf16[48,4224]{1,0:T(8,128)(2,1)}, u32[]{:S(2)}, u32[]{:S(2)}) collective-permute-start(bf16[48,4224]{1,0:T(8,128)(2,1)S(1)} %collective-permute-done.4.refs_6_.refs_5_), channel_id=1, source_target_pairs={{0,8},{8,0},{16,24},{24,16},{1,9},{9,1},{17,25},{25,17},{2,10},{10... | collective-permute-start | bytes 1216520 | tf_op jit(solution)/shard_map/ppermute | solution.py:186
  21.3 5.2 %collective-permute-done.2.refs_4_.refs_3_ = bf16[48,4224]{1,0:T(8,128)(2,1)S(1)} collective-permute-done((bf16[48,4224]{1,0:T(8,128)(2,1)S(1)}, bf16[48,4224]{1,0:T(8,128)(2,1)S(1)}, u32[]{:S(2)}, u32[]{:S(2)}) %collective-permute-start.2) | collective-permute-done | bytes 405536 | tf_op jit(solution)/shard_map/ppermute | solution.py:186
  27.4 1.8 %shard_map.38 = bf16[48,4224]{1,0:T(8,128)(2,1)} custom-call(bf16[48,4224]{1,0:T(8,128)(2,1)} %copy-done.3, bf16[96,4224]{1,0:T(8,128)(2,1)} %copy-done.1), custom_call_target="tpu_custom_call" | custom-call | tf_op jit(solution)/shard_map/pallas_call | solution.py:170
  29.2 2.0 %collective-permute-start.6 = (bf16[48,4224]{1,0:T(8,128)(2,1)}, bf16[48,4224]{1,0:T(8,128)(2,1)S(1)}, u32[]{:S(2)}, u32[]{:S(2)}) collective-permute-start(bf16[48,4224]{1,0:T(8,128)(2,1)} %shard_map.38), channel_id=1, source_target_pairs={{0,16},{8,24},{16,0},{24,8},{1,17},{9,25},{17,1},{25,9},{2,18},{10... | collective-permute-start | bytes 1216520 | tf_op jit(solution)/shard_map/ppermute | solution.py:186
  31.2 0.7 %collective-permute-start.15 = (bf16[96,4224]{1,0:T(8,128)(2,1)}, bf16[96,4224]{1,0:T(8,128)(2,1)S(1)}, u32[]{:S(2)}, u32[]{:S(2)}) collective-permute-start(bf16[96,4224]{1,0:T(8,128)(2,1)} %collective-permute-done.refs_1_), channel_id=1, source_target_pairs={{2,4},{4,6},{3,5},{5,7},{10,12},{12,14},{11,13},{13,15},{18,20},{2... | collective-permute-start | bytes 2433032 | tf_op jit(solution)/shard_map/ppermute | solution.py:212
  31.9 3.1 %collective-permute-done.7.refs_8_.refs_7_ = bf16[48,4224]{1,0:T(8,128)(2,1)} collective-permute-done((bf16[48,4224]{1,0:T(8,128)(2,1)S(1)}, bf16[48,4224]{1,0:T(8,128)(2,1)}, u32[]{:S(2)}, u32[]{:S(2)}) %collective-permute-start.7) | collective-permute-done | bytes 405536 | tf_op jit(solution)/shard_map/ppermute | solution.py:186
  35.6 5.9 %collective-permute-done.6.refs_7_.refs_6_ = bf16[48,4224]{1,0:T(8,128)(2,1)S(1)} collective-permute-done((bf16[48,4224]{1,0:T(8,128)(2,1)}, bf16[48,4224]{1,0:T(8,128)(2,1)S(1)}, u32[]{:S(2)}, u32[]{:S(2)}) %collective-permute-start.6) | collective-permute-done | bytes 405536 | tf_op jit(solution)/shard_map/ppermute | solution.py:186
  41.5 1.7 %collective-permute-done.12.refs_14_.refs_13_ = bf16[48,4224]{1,0:T(8,128)(2,1)S(1)} collective-permute-done((bf16[48,4224]{1,0:T(8,128)(2,1)S(1)}, bf16[48,4224]{1,0:T(8,128)(2,1)S(1)}, u32[]{:S(2)}, u32[]{:S(2)}) %collective-permute-start.12) | collective-permute-done | bytes 405536 | tf_op jit(solution)/shard_map/ppermute | solution.py:191
  43.2 1.1 %copy-done.2 = bf16[96,4224]{1,0:T(8,128)(2,1)S(1)} copy-done((bf16[96,4224]{1,0:T(8,128)(2,1)S(1)}, bf16[96,4224]{1,0:T(8,128)(2,1)}, u32[]{:S(2)}) %copy-start.2) | copy-done | bytes 811032
  44.3 1.0 %copy-done.4 = bf16[48,4224]{1,0:T(8,128)(2,1)S(1)} copy-done((bf16[48,4224]{1,0:T(8,128)(2,1)S(1)}, bf16[48,4224]{1,0:T(8,128)(2,1)}, u32[]{:S(2)}) %copy-start.4) | copy-done | bytes 405528
  45.3 3.5 %shard_map.39 = (f32[1,128]{1,0:T(1,128)S(1)}, f32[1,128]{1,0:T(1,128)S(1)}, f32[4,128]{1,0:T(4,128)S(1)}, f32[4,128]{1,0:T(4,128)S(1)}) custom-call(bf16[96,4224]{1,0:T(8,128)(2,1)S(1)} %copy-done, bf16[96,4224]{1,0:T(8,128)(2,1)} %collective-permute-done.refs_1_, bf16[96,4224]{1,0:T(8,128)(2,1)S(1)} %copy-done, bf16[48,4224]{1,0:T(8,128)(2,1)S(1)} %copy-done.4, ...), custom_call_target="tpu_custom_call" | custom-call | flops 1610612736 | bytes 7864320 | tf_op jit(solution)/shard_map/pallas_call | solution.py:139
  48.9 3.4 %shard_map.40 = (f32[1,128]{1,0:T(1,128)S(1)}, f32[4,128]{1,0:T(4,128)S(1)}, f32[4,128]{1,0:T(4,128)S(1)}) custom-call(bf16[96,4224]{1,0:T(8,128)(2,1)S(1)} %collective-permute-done.15.refs_0_, bf16[96,4224]{1,0:T(8,128)(2,1)S(1)} %copy-done, bf16[48,4224]{1,0:T(8,128)(2,1)S(1)} %copy-done.4, bf16[48,4224]{1,0:T(8,128)(2,1)S(1)} %collective-permute-done.2.refs_4_.refs_3_, ...), custom_call_target="tpu_custom_call" | custom-call | flops 805306368 | bytes 7077888 | tf_op jit(solution)/shard_map/pallas_call | solution.py:139
  52.4 1.0 %collective-permute-done.17 = f32[4,128]{1,0:T(4,128)S(1)} collective-permute-done((f32[4,128]{1,0:T(4,128)S(1)}, f32[4,128]{1,0:T(4,128)S(1)}, u32[]{:S(2)}, u32[]{:S(2)}) %collective-permute-start.17) | collective-permute-done | bytes 2080 | tf_op jit(solution)/shard_map/ppermute | solution.py:191
  53.4 2.7 %collective-permute-start.20 = (f32[4,128]{1,0:T(4,128)S(1)}, f32[4,128]{1,0:T(4,128)S(1)}, u32[]{:S(2)}, u32[]{:S(2)}) collective-permute-start(f32[4,128]{1,0:T(4,128)S(1)} %max.23), channel_id=1, source_target_pairs={{0,24},{8,16},{16,8},{24,0},{1,25},{9,17},{17,9},{25,1},{2,26},{10... | collective-permute-start | bytes 6152 | tf_op jit(solution)/shard_map/ppermute | solution.py:227
  56.9 1.3 %collective-permute-start.16 = (f32[1,128]{1,0:T(1,128)S(1)}, f32[1,128]{1,0:T(1,128)S(1)}, u32[]{:S(2)}, u32[]{:S(2)}) collective-permute-start(f32[1,128]{1,0:T(1,128)S(1)} %get-tuple-element.16), channel_id=1, source_target_pairs={{4,0},{6,2},{5,1},{7,3},{12,8},{14,10},{13,9},{15,11},{20,16},{22,... | collective-permute-start | bytes 1544 | tf_op jit(solution)/shard_map/ppermute | solution.py:195
  58.2 8.4 %collective-permute-start.14 = (f32[1,128]{1,0:T(1,128)S(1)}, f32[1,128]{1,0:T(1,128)S(1)}, u32[]{:S(2)}, u32[]{:S(2)}) collective-permute-start(f32[1,128]{1,0:T(1,128)S(1)} %get-tuple-element.13), channel_id=1, source_target_pairs={{2,0},{4,2},{6,4},{0,6},{3,1},{5,3},{7,5},{1,7},{10,8},{12,10},{14... | collective-permute-start | bytes 1544 | tf_op jit(solution)/shard_map/ppermute | solution.py:195
  66.9 1.0 %collective-permute-done.14 = f32[1,128]{1,0:T(1,128)S(1)} collective-permute-done((f32[1,128]{1,0:T(1,128)S(1)}, f32[1,128]{1,0:T(1,128)S(1)}, u32[]{:S(2)}, u32[]{:S(2)}) %collective-permute-start.14) | collective-permute-done | bytes 544 | tf_op jit(solution)/shard_map/ppermute | solution.py:195
  (36 shorter events, 4.7 us)
Async XLA Ops:
  2.4 4.9 %copy-start = (bf16[96,4224]{1,0:T(8,128)(2,1)S(1)}, bf16[96,4224]{1,0:T(8,128)(2,1)}, u32[]{:S(2)}) copy-start(bf16[96,4224]{1,0:T(8,128)(2,1)} %shard_map.37.refs_0_.refs_2_.refs_1_) | copy-start | bytes 2433028
  2.4 24.1 %collective-permute-start.5 = (bf16[96,4224]{1,0:T(8,128)(2,1)}, bf16[96,4224]{1,0:T(8,128)(2,1)S(1)}, u32[]{:S(2)}, u32[]{:S(2)}) collective-permute-start(bf16[96,4224]{1,0:T(8,128)(2,1)} %shard_map.37.refs_0_.refs_2_.refs_1_), channel_id=1, source_target_pairs={{0,1},{1,0},{2,3},{3,2},{4,5},{5,4},{6,7},{7,6},{8,9},{9,8},{10,11... | collective-permute-start | bytes 2433032 | tf_op jit(solution)/shard_map/ppermute | solution.py:191
  4.8 13.0 %collective-permute-start.1 = (bf16[48,4224]{1,0:T(8,128)(2,1)}, bf16[48,4224]{1,0:T(8,128)(2,1)S(1)}, u32[]{:S(2)}, u32[]{:S(2)}) collective-permute-start(bf16[48,4224]{1,0:T(8,128)(2,1)} %get-tuple-element.20), channel_id=1, source_target_pairs={{0,8},{8,0},{16,24},{24,16},{1,9},{9,1},{17,25},{25,17},{2,10},{10... | collective-permute-start | bytes 1216520 | tf_op jit(solution)/shard_map/ppermute | solution.py:186
  7.3 23.9 %collective-permute-start = (bf16[96,4224]{1,0:T(8,128)(2,1)S(1)}, bf16[96,4224]{1,0:T(8,128)(2,1)}, u32[]{:S(2)}, u32[]{:S(2)}) collective-permute-start(bf16[96,4224]{1,0:T(8,128)(2,1)S(1)} %copy-done), channel_id=1, source_target_pairs={{0,2},{2,4},{4,6},{6,0},{1,3},{3,5},{5,7},{7,1},{8,10},{10,12},{12... | collective-permute-start | bytes 2433032 | tf_op jit(solution)/shard_map/ppermute | solution.py:212
  8.9 11.2 %collective-permute-start.4 = (bf16[48,4224]{1,0:T(8,128)(2,1)S(1)}, bf16[48,4224]{1,0:T(8,128)(2,1)S(1)}, u32[]{:S(2)}, u32[]{:S(2)}) collective-permute-start(bf16[48,4224]{1,0:T(8,128)(2,1)S(1)} %get-tuple-element.19), channel_id=1, source_target_pairs={{0,16},{8,24},{16,0},{24,8},{1,17},{9,25},{17,1},{25,9},{2,18},{10... | collective-permute-start | bytes 1216520 | tf_op jit(solution)/shard_map/ppermute | solution.py:186
  10.4 16.0 %collective-permute-start.2 = (bf16[48,4224]{1,0:T(8,128)(2,1)S(1)}, bf16[48,4224]{1,0:T(8,128)(2,1)S(1)}, u32[]{:S(2)}, u32[]{:S(2)}) collective-permute-start(bf16[48,4224]{1,0:T(8,128)(2,1)S(1)} %get-tuple-element.19), channel_id=1, source_target_pairs={{0,8},{8,0},{16,24},{24,16},{1,9},{9,1},{17,25},{25,17},{2,10},{10... | collective-permute-start | bytes 1216520 | tf_op jit(solution)/shard_map/ppermute | solution.py:186
  17.8 9.2 %copy-start.3 = (bf16[48,4224]{1,0:T(8,128)(2,1)}, bf16[48,4224]{1,0:T(8,128)(2,1)S(1)}, u32[]{:S(2)}) copy-start(bf16[48,4224]{1,0:T(8,128)(2,1)S(1)} %collective-permute-done.1.value_ref.refs_3_.refs_2_) | copy-start | bytes 1216516
  17.8 11.4 %collective-permute-start.3 = (bf16[48,4224]{1,0:T(8,128)(2,1)}, bf16[48,4224]{1,0:T(8,128)(2,1)S(1)}, u32[]{:S(2)}, u32[]{:S(2)}) collective-permute-start(bf16[48,4224]{1,0:T(8,128)(2,1)} %get-tuple-element.20), channel_id=1, source_target_pairs={{0,16},{8,24},{16,0},{24,8},{1,17},{9,25},{17,1},{25,9},{2,18},{10... | collective-permute-start | bytes 1216520 | tf_op jit(solution)/shard_map/ppermute | solution.py:186
  20.1 14.9 %collective-permute-start.7 = (bf16[48,4224]{1,0:T(8,128)(2,1)S(1)}, bf16[48,4224]{1,0:T(8,128)(2,1)}, u32[]{:S(2)}, u32[]{:S(2)}) collective-permute-start(bf16[48,4224]{1,0:T(8,128)(2,1)S(1)} %collective-permute-done.4.refs_6_.refs_5_), channel_id=1, source_target_pairs={{0,8},{8,0},{16,24},{24,16},{1,9},{9,1},{17,25},{25,17},{2,10},{10... | collective-permute-start | bytes 1216520 | tf_op jit(solution)/shard_map/ppermute | solution.py:186
  26.5 8.5 %collective-permute-start.8 = (bf16[48,4224]{1,0:T(8,128)(2,1)S(1)}, bf16[48,4224]{1,0:T(8,128)(2,1)}, u32[]{:S(2)}, u32[]{:S(2)}) collective-permute-start(bf16[48,4224]{1,0:T(8,128)(2,1)S(1)} %collective-permute-done.1.value_ref.refs_3_.refs_2_), channel_id=1, source_target_pairs={{0,1},{1,0},{2,3},{3,2},{4,5},{5,4},{6,7},{7,6},{8,9},{9,8},{10,11... | collective-permute-start | bytes 1216520 | tf_op jit(solution)/shard_map/ppermute | solution.py:191
  26.5 9.0 %collective-permute-start.9 = (bf16[48,4224]{1,0:T(8,128)(2,1)S(1)}, bf16[48,4224]{1,0:T(8,128)(2,1)}, u32[]{:S(2)}, u32[]{:S(2)}) collective-permute-start(bf16[48,4224]{1,0:T(8,128)(2,1)S(1)} %collective-permute-done.2.refs_4_.refs_3_), channel_id=1, source_target_pairs={{0,1},{1,0},{2,3},{3,2},{4,5},{5,4},{6,7},{7,6},{8,9},{9,8},{10,11... | collective-permute-start | bytes 1216520 | tf_op jit(solution)/shard_map/ppermute | solution.py:191
  29.2 12.2 %collective-permute-start.6 = (bf16[48,4224]{1,0:T(8,128)(2,1)}, bf16[48,4224]{1,0:T(8,128)(2,1)S(1)}, u32[]{:S(2)}, u32[]{:S(2)}) collective-permute-start(bf16[48,4224]{1,0:T(8,128)(2,1)} %shard_map.38), channel_id=1, source_target_pairs={{0,16},{8,24},{16,0},{24,8},{1,17},{9,25},{17,1},{25,9},{2,18},{10... | collective-permute-start | bytes 1216520 | tf_op jit(solution)/shard_map/ppermute | solution.py:186
  31.2 17.7 %collective-permute-start.15 = (bf16[96,4224]{1,0:T(8,128)(2,1)}, bf16[96,4224]{1,0:T(8,128)(2,1)S(1)}, u32[]{:S(2)}, u32[]{:S(2)}) collective-permute-start(bf16[96,4224]{1,0:T(8,128)(2,1)} %collective-permute-done.refs_1_), channel_id=1, source_target_pairs={{2,4},{4,6},{3,5},{5,7},{10,12},{12,14},{11,13},{13,15},{18,20},{2... | collective-permute-start | bytes 2433032 | tf_op jit(solution)/shard_map/ppermute | solution.py:212
  35.0 6.5 %collective-permute-start.11 = (bf16[48,4224]{1,0:T(8,128)(2,1)S(1)}, bf16[48,4224]{1,0:T(8,128)(2,1)S(1)}, u32[]{:S(2)}, u32[]{:S(2)}) collective-permute-start(bf16[48,4224]{1,0:T(8,128)(2,1)S(1)} %collective-permute-done.4.refs_6_.refs_5_), channel_id=1, source_target_pairs={{0,1},{1,0},{2,3},{3,2},{4,5},{5,4},{6,7},{7,6},{8,9},{9,8},{10,11... | collective-permute-start | bytes 1216520 | tf_op jit(solution)/shard_map/ppermute | solution.py:191
  35.0 6.4 %collective-permute-start.10 = (bf16[48,4224]{1,0:T(8,128)(2,1)S(1)}, bf16[48,4224]{1,0:T(8,128)(2,1)S(1)}, u32[]{:S(2)}, u32[]{:S(2)}) collective-permute-start(bf16[48,4224]{1,0:T(8,128)(2,1)S(1)} %collective-permute-done.3.refs_5_.refs_4_), channel_id=1, source_target_pairs={{0,1},{1,0},{2,3},{3,2},{4,5},{5,4},{6,7},{7,6},{8,9},{9,8},{10,11... | collective-permute-start | bytes 1216520 | tf_op jit(solution)/shard_map/ppermute | solution.py:191
  35.5 5.9 %collective-permute-start.13 = (bf16[48,4224]{1,0:T(8,128)(2,1)}, bf16[48,4224]{1,0:T(8,128)(2,1)S(1)}, u32[]{:S(2)}, u32[]{:S(2)}) collective-permute-start(bf16[48,4224]{1,0:T(8,128)(2,1)} %collective-permute-done.7.refs_8_.refs_7_), channel_id=1, source_target_pairs={{0,1},{1,0},{2,3},{3,2},{4,5},{5,4},{6,7},{7,6},{8,9},{9,8},{10,11... | collective-permute-start | bytes 1216520 | tf_op jit(solution)/shard_map/ppermute | solution.py:191
  41.5 1.7 %collective-permute-start.12 = (bf16[48,4224]{1,0:T(8,128)(2,1)S(1)}, bf16[48,4224]{1,0:T(8,128)(2,1)S(1)}, u32[]{:S(2)}, u32[]{:S(2)}) collective-permute-start(bf16[48,4224]{1,0:T(8,128)(2,1)S(1)} %collective-permute-done.6.refs_7_.refs_6_), channel_id=1, source_target_pairs={{0,1},{1,0},{2,3},{3,2},{4,5},{5,4},{6,7},{7,6},{8,9},{9,8},{10,11... | collective-permute-start | bytes 1216520 | tf_op jit(solution)/shard_map/ppermute | solution.py:191
  43.2 1.1 %copy-start.2 = (bf16[96,4224]{1,0:T(8,128)(2,1)S(1)}, bf16[96,4224]{1,0:T(8,128)(2,1)}, u32[]{:S(2)}) copy-start(bf16[96,4224]{1,0:T(8,128)(2,1)} %copy-done.1) | copy-start | bytes 2433028
  52.2 1.2 %collective-permute-start.17 = (f32[4,128]{1,0:T(4,128)S(1)}, f32[4,128]{1,0:T(4,128)S(1)}, u32[]{:S(2)}, u32[]{:S(2)}) collective-permute-start(f32[4,128]{1,0:T(4,128)S(1)} %get-tuple-element.18), channel_id=1, source_target_pairs={{0,1},{1,0},{2,3},{3,2},{4,5},{5,4},{6,7},{7,6},{8,9},{9,8},{10,11... | collective-permute-start | bytes 6152 | tf_op jit(solution)/shard_map/ppermute | solution.py:191
  53.4 14.5 %collective-permute-start.20 = (f32[4,128]{1,0:T(4,128)S(1)}, f32[4,128]{1,0:T(4,128)S(1)}, u32[]{:S(2)}, u32[]{:S(2)}) collective-permute-start(f32[4,128]{1,0:T(4,128)S(1)} %max.23), channel_id=1, source_target_pairs={{0,24},{8,16},{16,8},{24,0},{1,25},{9,17},{17,9},{25,1},{2,26},{10... | collective-permute-start | bytes 6152 | tf_op jit(solution)/shard_map/ppermute | solution.py:227
  56.1 11.8 %collective-permute-start.19 = (f32[4,128]{1,0:T(4,128)S(1)}, f32[4,128]{1,0:T(4,128)S(1)}, u32[]{:S(2)}, u32[]{:S(2)}) collective-permute-start(f32[4,128]{1,0:T(4,128)S(1)} %max.23), channel_id=1, source_target_pairs={{0,16},{8,24},{16,0},{24,8},{1,17},{9,25},{17,1},{25,9},{2,18},{10... | collective-permute-start | bytes 6152 | tf_op jit(solution)/shard_map/ppermute | solution.py:227
  56.6 11.3 %collective-permute-start.18 = (f32[4,128]{1,0:T(4,128)S(1)}, f32[4,128]{1,0:T(4,128)S(1)}, u32[]{:S(2)}, u32[]{:S(2)}) collective-permute-start(f32[4,128]{1,0:T(4,128)S(1)} %max.23), channel_id=1, source_target_pairs={{0,8},{8,0},{16,24},{24,16},{1,9},{9,1},{17,25},{25,17},{2,10},{10... | collective-permute-start | bytes 6152 | tf_op jit(solution)/shard_map/ppermute | solution.py:227
  56.9 10.0 %collective-permute-start.16 = (f32[1,128]{1,0:T(1,128)S(1)}, f32[1,128]{1,0:T(1,128)S(1)}, u32[]{:S(2)}, u32[]{:S(2)}) collective-permute-start(f32[1,128]{1,0:T(1,128)S(1)} %get-tuple-element.16), channel_id=1, source_target_pairs={{4,0},{6,2},{5,1},{7,3},{12,8},{14,10},{13,9},{15,11},{20,16},{22,... | collective-permute-start | bytes 1544 | tf_op jit(solution)/shard_map/ppermute | solution.py:195
  58.2 9.7 %collective-permute-start.14 = (f32[1,128]{1,0:T(1,128)S(1)}, f32[1,128]{1,0:T(1,128)S(1)}, u32[]{:S(2)}, u32[]{:S(2)}) collective-permute-start(f32[1,128]{1,0:T(1,128)S(1)} %get-tuple-element.13), channel_id=1, source_target_pairs={{2,0},{4,2},{6,4},{0,6},{3,1},{5,3},{7,5},{1,7},{10,8},{12,10},{14... | collective-permute-start | bytes 1544 | tf_op jit(solution)/shard_map/ppermute | solution.py:195
  (2 other events, 1.9 us)

commit v7 on v5

--- a/solution.py
+++ b/solution.py
@@ -12,16 +12,6 @@
 CHUNK = 512
 PER_CALL = 4
 VMEM = pl.BlockSpec(memory_space=pltpu.VMEM)
-
-
-def ring_pairs(length, shift):
-    if 2 * shift < length:
-        return [(k, (k + shift) % length) for k in range(length)]
-    pairs = []
-    for k in range(length // 2):
-        low, high = k, k + shift
-        pairs.append((low, high) if k % 2 == 0 else (high, low))
-    return pairs
 
 
 def flip(count, bits):
@@ -187,16 +177,15 @@
     return blocks
 
 
-def copy_kernel(value_ref, other_ref, out_ref):
-    out_ref[...] = value_ref[...]
-
-
-def copy_behind(value, other):
+def after(value, other):
+    anywhere = pl.BlockSpec(memory_space=pl.ANY)
     return pl.pallas_call(
-        copy_kernel,
-        in_specs=[VMEM, VMEM],
-        out_specs=VMEM,
+        lambda *refs: None,
+        in_specs=[anywhere] * 2,
+        out_specs=anywhere,
         out_shape=jax.ShapeDtypeStruct(value.shape, value.dtype),
+        input_output_aliases={0: 0},
+        cost_estimate=pl.CostEstimate(flops=0, bytes_accessed=0, transcendentals=0),
     )(value, other)
 
 
@@ -205,39 +194,59 @@
 
 
 def send_home(best, route):
-    home = lax.ppermute(best, "z", [(b, a) for a, b in route])
-    if len(route) == lax.axis_size("z"):
-        return home
+    return lax.ppermute(best, "z", [(b, a) for a, b in route])
+
+
+def finish_kernel(route, *refs):
+    out_ref, last_ref = refs[-1], refs[-2]
     here = lax.axis_index("z")
     sent = functools.reduce(jnp.logical_or, [here == a for a, _ in route])
-    return jnp.where(sent, home, -1.0)
+    best = jnp.where(sent, last_ref[...], -1.0)
+    for ref in refs[:-2]:
+        best = jnp.maximum(best, ref[...])
+    out_ref[...] = best[0, : out_ref.shape[0]]
+
+
+def finish(bests, route, rows):
+    return pl.pallas_call(
+        functools.partial(finish_kernel, route),
+        in_specs=[VMEM] * len(bests),
+        out_specs=VMEM,
+        out_shape=jax.ShapeDtypeStruct((rows,), jnp.float32),
+    )(*bests)
 
 
 def local(embeddings, cluster_ids, order_index):
     rows = embeddings.shape[0]
     groups, length = lax.axis_size("group"), lax.axis_size("z")
-    routes = [ring_pairs(length, shift) for shift in range(1, length // 2 + 1)]
     own = pack(embeddings, cluster_ids, order_index)
-    arrived = [lax.ppermute(own, "z", route) for route in routes]
+    block, routes, arrived = own, [], []
+    for shift in range(1, length // 2 + 1):
+        sources = range(length if 2 * shift < length else length // 2)
+        routes.append([(a, (a + shift) % length) for a in sources])
+        hops = [((a + shift - 1) % length, (a + shift) % length) for a in sources]
+        block = lax.ppermute(block, "z", hops)
+        arrived.append(block)
     blocks = list(gather_plane(own, groups).values())
 
-    cut = rows * 2 // 3 // 16 * 16
     homed, visitors = [0, 0], [[own], [swap(own)]]
     for block in arrived[:-1]:
         homed += [1, 1]
-        visitors += [[block], [swap(block[:cut]), swap(block[cut:])]]
+        visitors += [[block], [swap(block)]]
     row, col = maxima(homed, visitors, blocks)
     bests = [row[0], swap(row[1])]
     for index, route in enumerate(routes[:-1]):
         merged = jnp.maximum(row[2 * index + 2], swap(row[2 * index + 3]))
         bests.append(send_home(merged, route))
 
-    last = copy_behind(arrived[-1], bests[-1])
-    row, col = maxima([1, 1], [[last], [swap(last)]], blocks, col)
+    last = after(arrived[-1], bests[-1])
+    other = swap(last)
+    row, col = maxima([1], [[last]], blocks, col)
+    other_row, col = maxima([1], [[other]], blocks, col)
     bests.append(col[0])
     bests += [lax.ppermute(col[s], "group", flip(groups, s)) for s in range(1, groups)]
-    bests.append(send_home(jnp.maximum(row[0], swap(row[1])), routes[-1]))
-    return functools.reduce(jnp.maximum, bests)[0, :rows]
+    bests.append(send_home(jnp.maximum(row[0], swap(other_row[0])), routes[-1]))
+    return finish(bests, routes[-1], rows)
 
 
 def solution(mesh):

time: 81 us -> 65.3 us (0.81)
  waiting for transfers between devices: 47.8 us -> 36 us
  starting transfers between devices: 21 us -> 17.4 us
    ppermute x4, waiting for transfers between devices: 32.5 us -> 23 us  [the longest x2 17.4 us: local(): block = lax.ppermute(block, 'z', hops)]
    ppermute x7 -> x6, waiting for transfers between devices: 5.31 us -> 1.32 us  [swap(): return lax.ppermute(block, 'core', flip(2, 1))]
    ppermute x4, starting transfers between devices: 10.4 us -> 7.28 us  [the longest x2 4.6 us: local(): block = lax.ppermute(block, 'z', hops)]
    ppermute x1, waiting for transfers between devices: 6.79 us -> 8.67 us  [gather_plane(): lax.ppermute(top, 'group', flip(groups, high))]
    pallas_call x2 -> x3, Pallas kernels: 4.35 us -> 5.57 us  [maxima(): pl.pallas_call(functools.partial(maxima_kernel, homed, [len(block) for bl...]
    pallas_call x1 -> x2, Pallas kernels: 2.15 us -> 1.25 us  [the longest x1 1.25 us: finish(): pl.pallas_call(functools.partial(finish_kernel, route), in_specs=[VMEM] *...]
    unnamed x8 -> x18, local copies, waits for them, and re-layouts: 2.31 us -> 2.27 us
  transfers between devices with their start and end apart: 18 -> 17, of which waited for: 10 -> 9; matrix products, arithmetic and copies ran while one was open for 0% -> 0% of each run, Pallas kernels for 3% -> 7%
where the time goes in v7:
time: 65.3 us; the launch traced here: 65.1 us
  waiting for transfers between devices  36 us (55%)
  starting transfers between devices  17.4 us (27%)
  Pallas kernels  9.23 us (14%)
  local copies, waits for them, and re-layouts  2.33 us (4%)
    ppermute x2, waiting for transfers between devices, local(): block = lax.ppermute(block, 'z', hops)  17.4 us
    ppermute x1, waiting for transfers between devices, gather_plane(): lax.ppermute(top, 'group', flip(groups, high))  8.67 us
    ppermute x2, waiting for transfers between devices, send_home(): return lax.ppermute(best, 'z', [(b, a) for a, b in route])  5.68 us
    pallas_call x3, Pallas kernels, maxima(): pl.pallas_call(functools.partial(maxima_kernel, homed, [len(block) for bl...  5.57 us
    ppermute x2, starting transfers between devices, local(): block = lax.ppermute(block, 'z', hops)  4.6 us
    ppermute x3, starting transfers between devices, local(): lax.ppermute(col[s], 'group', flip(groups, s))  3.49 us
    ppermute x2, starting transfers between devices, gather_plane(): blocks[s] = [lax.ppermute(block, 'group', flip(groups, s))]  3.01 us
    ppermute x2, starting transfers between devices, send_home(): return lax.ppermute(best, 'z', [(b, a) for a, b in route])  2.68 us
  transfers between devices with their start and end apart: 17, of which 9 were waited for; matrix products, arithmetic and copies ran while one was open for 0% of the time, Pallas kernels for 7%

profile of v7, /device:TPU:0, one launch (start us, length us, event | category | flops | bytes accessed | tf_op | source)
XLA Modules:
  0.0 65.1 jit_solution(634479909066151560)
XLA Ops:
  0.0 2.4 %shard_map.37.refs_0_.refs_4_.refs_1_ = bf16[96,4224]{1,0:T(8,128)(2,1)} custom-call(bf16[96,4096]{1,0:T(8,128)(2,1)} %rows_ref.1, s32[1,96]{1,0:T(1,128)} %bitcast.2, s32[1,96]{1,0:T(1,128)} %bitcast.3), custom_call_target="tpu_custom_call" | custom-call | flops 1572864 | bytes 1572864 | tf_op jit(solution)/shard_map/pallas_call | solution.py:49
  2.4 3.0 %collective-permute-start.1 = (bf16[96,4224]{1,0:T(8,128)(2,1)}, bf16[96,4224]{1,0:T(8,128)(2,1)S(1)}, u32[]{:S(2)}, u32[]{:S(2)}) collective-permute-start(bf16[96,4224]{1,0:T(8,128)(2,1)} %shard_map.37.refs_0_.refs_4_.refs_1_), channel_id=1, source_target_pairs={{0,2},{2,4},{4,6},{6,0},{1,3},{3,5},{5,7},{7,1},{8,10},{10,12},{12... | collective-permute-start | bytes 2433032 | tf_op jit(solution)/shard_map/ppermute | solution.py:228
  5.4 1.5 %collective-permute-start.3 = (bf16[96,4224]{1,0:T(8,128)(2,1)}, bf16[96,4224]{1,0:T(8,128)(2,1)S(1)}, u32[]{:S(2)}, u32[]{:S(2)}) collective-permute-start(bf16[96,4224]{1,0:T(8,128)(2,1)} %shard_map.37.refs_0_.refs_4_.refs_1_), channel_id=1, source_target_pairs={{0,8},{8,0},{16,24},{24,16},{1,9},{9,1},{17,25},{25,17},{2,10},{10... | collective-permute-start | bytes 2433032 | tf_op jit(solution)/shard_map/ppermute | solution.py:168
  6.9 1.5 %collective-permute-start.4 = (bf16[96,4224]{1,0:T(8,128)(2,1)}, bf16[96,4224]{1,0:T(8,128)(2,1)S(1)}, u32[]{:S(2)}, u32[]{:S(2)}) collective-permute-start(bf16[96,4224]{1,0:T(8,128)(2,1)} %shard_map.37.refs_0_.refs_4_.refs_1_), channel_id=1, source_target_pairs={{0,16},{8,24},{16,0},{24,8},{1,17},{9,25},{17,1},{25,9},{2,18},{10... | collective-permute-start | bytes 2433032 | tf_op jit(solution)/shard_map/ppermute | solution.py:168
  8.4 17.4 %collective-permute-done.1.refs_2_ = bf16[96,4224]{1,0:T(8,128)(2,1)S(1)} collective-permute-done((bf16[96,4224]{1,0:T(8,128)(2,1)}, bf16[96,4224]{1,0:T(8,128)(2,1)S(1)}, u32[]{:S(2)}, u32[]{:S(2)}) %collective-permute-start.1) | collective-permute-done | bytes 811040 | tf_op jit(solution)/shard_map/ppermute | solution.py:228
  25.8 1.6 %collective-permute-start.10 = (bf16[96,4224]{1,0:T(8,128)(2,1)S(1)}, bf16[96,4224]{1,0:T(8,128)(2,1)}, u32[]{:S(2)}, u32[]{:S(2)}) collective-permute-start(bf16[96,4224]{1,0:T(8,128)(2,1)S(1)} %collective-permute-done.1.refs_2_), channel_id=1, source_target_pairs={{2,4},{4,6},{3,5},{5,7},{10,12},{12,14},{11,13},{13,15},{18,20},{2... | collective-permute-start | bytes 2433032 | tf_op jit(solution)/shard_map/ppermute | solution.py:228
  27.4 1.6 %collective-permute-start.5 = (bf16[48,4224]{1,0:T(8,128)(2,1)S(1)}, bf16[48,4224]{1,0:T(8,128)(2,1)S(1)}, u32[]{:S(2)}, u32[]{:S(2)}) collective-permute-start(bf16[48,4224]{1,0:T(8,128)(2,1)S(1)} %slice.8), channel_id=1, source_target_pairs={{0,16},{8,24},{16,0},{24,8},{1,17},{9,25},{17,1},{25,9},{2,18},{10... | collective-permute-start | bytes 1216520 | tf_op jit(solution)/shard_map/ppermute | solution.py:174
  29.0 1.6 %collective-permute-start.6 = (bf16[48,4224]{1,0:T(8,128)(2,1)S(1)}, bf16[48,4224]{1,0:T(8,128)(2,1)S(1)}, u32[]{:S(2)}, u32[]{:S(2)}) collective-permute-start(bf16[48,4224]{1,0:T(8,128)(2,1)S(1)} %slice.9), channel_id=1, source_target_pairs={{0,8},{8,0},{16,24},{24,16},{1,9},{9,1},{17,25},{25,17},{2,10},{10... | collective-permute-start | bytes 1216520 | tf_op jit(solution)/shard_map/ppermute | solution.py:175
  30.6 8.7 %collective-permute-done.5.refs_7_.refs_4_ = bf16[48,4224]{1,0:T(8,128)(2,1)S(1)} collective-permute-done((bf16[48,4224]{1,0:T(8,128)(2,1)S(1)}, bf16[48,4224]{1,0:T(8,128)(2,1)S(1)}, u32[]{:S(2)}, u32[]{:S(2)}) %collective-permute-start.5) | collective-permute-done | bytes 405536 | tf_op jit(solution)/shard_map/ppermute | solution.py:174
  39.3 1.3 %collective-permute-done.6.refs_8_.refs_5_ = bf16[48,4224]{1,0:T(8,128)(2,1)S(1)} collective-permute-done((bf16[48,4224]{1,0:T(8,128)(2,1)S(1)}, bf16[48,4224]{1,0:T(8,128)(2,1)S(1)}, u32[]{:S(2)}, u32[]{:S(2)}) %collective-permute-start.6) | collective-permute-done | bytes 405536 | tf_op jit(solution)/shard_map/ppermute | solution.py:175
  40.6 2.0 %shard_map.38 = (f32[1,128]{1,0:T(1,128)S(1)}, f32[1,128]{1,0:T(1,128)S(1)}, f32[1,128]{1,0:T(1,128)S(1)}, f32[1,128]{1,0:T(1,128)S(1)}, f32[1,128]{1,0:T(1,128)...) custom-call(bf16[96,4224]{1,0:T(8,128)(2,1)S(1)} %copy-done, ...), custom_call_target="tpu_custom_call" | custom-call | flops 1610612736 | bytes 6291456 | tf_op jit(solution)/shard_map/pallas_call | solution.py:138
  42.7 0.6 copy-done.1
  43.3 1.1 %collective-permute-done.8 = f32[1,128]{1,0:T(1,128)S(1)} collective-permute-done((f32[1,128]{1,0:T(1,128)S(1)}, f32[1,128]{1,0:T(1,128)S(1)}, u32[]{:S(2)}, u32[]{:S(2)}) %collective-permute-start.8) | collective-permute-done | bytes 544 | tf_op jit(solution)/shard_map/ppermute | solution.py:193
  44.4 1.4 %collective-permute-start.9 = (f32[1,128]{1,0:T(1,128)S(1)}, f32[1,128]{1,0:T(1,128)S(1)}, u32[]{:S(2)}, u32[]{:S(2)}) collective-permute-start(f32[1,128]{1,0:T(1,128)S(1)} %max.6), channel_id=1, source_target_pairs={{2,0},{4,2},{6,4},{0,6},{3,1},{5,3},{7,5},{1,7},{10,8},{12,10},{14... | collective-permute-start | bytes 1544 | tf_op jit(solution)/shard_map/ppermute | solution.py:197
  45.8 2.3 %collective-permute-done.9.refs_1_.refs_2_ = f32[1,128]{1,0:T(1,128)S(1)} collective-permute-done((f32[1,128]{1,0:T(1,128)S(1)}, f32[1,128]{1,0:T(1,128)S(1)}, u32[]{:S(2)}, u32[]{:S(2)}) %collective-permute-start.9) | collective-permute-done | bytes 544 | tf_op jit(solution)/shard_map/ppermute | solution.py:197
  48.6 2.3 %shard_map.40 = (f32[1,128]{1,0:T(1,128)S(1)}, f32[1,128]{1,0:T(1,128)S(1)}, f32[1,128]{1,0:T(1,128)S(1)}, f32[1,128]{1,0:T(1,128)S(1)}, f32[1,128]{1,0:T(1,128)S(1)}) custom-call(bf16[96,4224]{1,0:T(8,128)(2,1)} %shard_map.39.refs_0_, bf16[96,4224]{1,0:T(8,128)(2,1)S(1)} %copy-done, bf16[96,4224]{1,0:T(8,128)(2,1)S(1)} %collective-permute-done.3.refs_5_.refs_2_, ...), custom_call_target="tpu_custom_call" | custom-call | flops 402653184 | bytes 3932160 | tf_op jit(solution)/shard_map/pallas_call | solution.py:138
  51.2 1.2 %shard_map.41 = (f32[1,128]{1,0:T(1,128)S(1)}, f32[1,128]{1,0:T(1,128)S(1)}, f32[1,128]{1,0:T(1,128)S(1)}, f32[1,128]{1,0:T(1,128)S(1)}, f32[1,128]{1,0:T(1,128)S(1)}) custom-call(bf16[96,4224]{1,0:T(8,128)(2,1)S(1)} %collective-permute-done.11.refs_0_, bf16[96,4224]{1,0:T(8,128)(2,1)S(1)} %copy-done, ...), custom_call_target="tpu_custom_call" | custom-call | flops 402653184 | bytes 3932160 | tf_op jit(solution)/shard_map/pallas_call | solution.py:138
  53.4 1.5 %collective-permute-start.12 = (f32[1,128]{1,0:T(1,128)S(1)}, f32[1,128]{1,0:T(1,128)S(1)}, u32[]{:S(2)}, u32[]{:S(2)}) collective-permute-start(f32[1,128]{1,0:T(1,128)S(1)} %get-tuple-element.36), channel_id=1, source_target_pairs={{0,8},{8,0},{16,24},{24,16},{1,9},{9,1},{17,25},{25,17},{2,10},{10... | collective-permute-start | bytes 1544 | tf_op jit(solution)/shard_map/ppermute | solution.py:247
  55.4 1.5 %collective-permute-start.14 = (f32[1,128]{1,0:T(1,128)S(1)}, f32[1,128]{1,0:T(1,128)S(1)}, u32[]{:S(2)}, u32[]{:S(2)}) collective-permute-start(f32[1,128]{1,0:T(1,128)S(1)} %get-tuple-element.38), channel_id=1, source_target_pairs={{0,24},{8,16},{16,8},{24,0},{1,25},{9,17},{17,9},{25,1},{2,26},{10... | collective-permute-start | bytes 1544 | tf_op jit(solution)/shard_map/ppermute | solution.py:247
  56.9 1.3 %collective-permute-start.16 = (f32[1,128]{1,0:T(1,128)S(1)}, f32[1,128]{1,0:T(1,128)S(1)}, u32[]{:S(2)}, u32[]{:S(2)}) collective-permute-start(f32[1,128]{1,0:T(1,128)S(1)} %max.7), channel_id=1, source_target_pairs={{4,0},{6,2},{5,1},{7,3},{12,8},{14,10},{13,9},{15,11},{20,16},{22,... | collective-permute-start | bytes 1544 | tf_op jit(solution)/shard_map/ppermute | solution.py:197
  58.5 1.4 %collective-permute-done.14.refs_6_ = f32[1,128]{1,0:T(1,128)S(1)} collective-permute-done((f32[1,128]{1,0:T(1,128)S(1)}, f32[1,128]{1,0:T(1,128)S(1)}, u32[]{:S(2)}, u32[]{:S(2)}) %collective-permute-start.14) | collective-permute-done | bytes 544 | tf_op jit(solution)/shard_map/ppermute | solution.py:247
  59.9 3.4 %collective-permute-done.16.refs_7_ = f32[1,128]{1,0:T(1,128)S(1)} collective-permute-done((f32[1,128]{1,0:T(1,128)S(1)}, f32[1,128]{1,0:T(1,128)S(1)}, u32[]{:S(2)}, u32[]{:S(2)}) %collective-permute-start.16) | collective-permute-done | bytes 544 | tf_op jit(solution)/shard_map/ppermute | solution.py:197
  63.3 0.6 copy-done.8
  63.8 1.3 %shard_map.42 = f32[96]{0:T(128)} custom-call(f32[1,128]{1,0:T(1,128)} %copy-done.1, f32[1,128]{1,0:T(1,128)} %copy-done.4, f32[1,128]{1,0:T(1,128)} %copy-done.3, f32[1,128]{1,0:T(1,128)} %copy-done.2, f32[1,128]{1,0:T(1,128)} %copy-done.5, f32[1,128]{1,0:T(1,128)} %copy-done.6, f32[1,128]{1,0:T(1,128)} %copy-done.7, f32[1,128]{1,0:T(1,128)} %copy-done.8), custom_call_target="tpu_custom_call" | custom-call | tf_op jit(solution)/shard_map/pallas_call | solution.py:211
  (38 shorter events, 2.6 us)
Async XLA Ops:
  2.4 38.2 %copy-start = (bf16[96,4224]{1,0:T(8,128)(2,1)S(1)}, bf16[96,4224]{1,0:T(8,128)(2,1)}, u32[]{:S(2)}) copy-start(bf16[96,4224]{1,0:T(8,128)(2,1)} %shard_map.37.refs_0_.refs_4_.refs_1_) | copy-start | bytes 2433028
  2.4 23.4 %collective-permute-start.1 = (bf16[96,4224]{1,0:T(8,128)(2,1)}, bf16[96,4224]{1,0:T(8,128)(2,1)S(1)}, u32[]{:S(2)}, u32[]{:S(2)}) collective-permute-start(bf16[96,4224]{1,0:T(8,128)(2,1)} %shard_map.37.refs_0_.refs_4_.refs_1_), channel_id=1, source_target_pairs={{0,2},{2,4},{4,6},{6,0},{1,3},{3,5},{5,7},{7,1},{8,10},{10,12},{12... | collective-permute-start | bytes 2433032 | tf_op jit(solution)/shard_map/ppermute | solution.py:228
  5.4 22.0 %collective-permute-start.3 = (bf16[96,4224]{1,0:T(8,128)(2,1)}, bf16[96,4224]{1,0:T(8,128)(2,1)S(1)}, u32[]{:S(2)}, u32[]{:S(2)}) collective-permute-start(bf16[96,4224]{1,0:T(8,128)(2,1)} %shard_map.37.refs_0_.refs_4_.refs_1_), channel_id=1, source_target_pairs={{0,8},{8,0},{16,24},{24,16},{1,9},{9,1},{17,25},{25,17},{2,10},{10... | collective-permute-start | bytes 2433032 | tf_op jit(solution)/shard_map/ppermute | solution.py:168
  6.9 22.1 %collective-permute-start.4 = (bf16[96,4224]{1,0:T(8,128)(2,1)}, bf16[96,4224]{1,0:T(8,128)(2,1)S(1)}, u32[]{:S(2)}, u32[]{:S(2)}) collective-permute-start(bf16[96,4224]{1,0:T(8,128)(2,1)} %shard_map.37.refs_0_.refs_4_.refs_1_), channel_id=1, source_target_pairs={{0,16},{8,24},{16,0},{24,8},{1,17},{9,25},{17,1},{25,9},{2,18},{10... | collective-permute-start | bytes 2433032 | tf_op jit(solution)/shard_map/ppermute | solution.py:168
  8.4 22.2 %collective-permute-start = (bf16[96,4224]{1,0:T(8,128)(2,1)}, bf16[96,4224]{1,0:T(8,128)(2,1)S(1)}, u32[]{:S(2)}, u32[]{:S(2)}) collective-permute-start(bf16[96,4224]{1,0:T(8,128)(2,1)} %shard_map.37.refs_0_.refs_4_.refs_1_), channel_id=1, source_target_pairs={{0,1},{1,0},{2,3},{3,2},{4,5},{5,4},{6,7},{7,6},{8,9},{9,8},{10,11... | collective-permute-start | bytes 2433032 | tf_op jit(solution)/shard_map/ppermute | solution.py:193
  25.8 14.8 %collective-permute-start.2 = (bf16[96,4224]{1,0:T(8,128)(2,1)S(1)}, bf16[96,4224]{1,0:T(8,128)(2,1)S(1)}, u32[]{:S(2)}, u32[]{:S(2)}) collective-permute-start(bf16[96,4224]{1,0:T(8,128)(2,1)S(1)} %collective-permute-done.1.refs_2_), channel_id=1, source_target_pairs={{0,1},{1,0},{2,3},{3,2},{4,5},{5,4},{6,7},{7,6},{8,9},{9,8},{10,11... | collective-permute-start | bytes 2433032 | tf_op jit(solution)/shard_map/ppermute | solution.py:193
  25.8 20.0 %collective-permute-start.10 = (bf16[96,4224]{1,0:T(8,128)(2,1)S(1)}, bf16[96,4224]{1,0:T(8,128)(2,1)}, u32[]{:S(2)}, u32[]{:S(2)}) collective-permute-start(bf16[96,4224]{1,0:T(8,128)(2,1)S(1)} %collective-permute-done.1.refs_2_), channel_id=1, source_target_pairs={{2,4},{4,6},{3,5},{5,7},{10,12},{12,14},{11,13},{13,15},{18,20},{2... | collective-permute-start | bytes 2433032 | tf_op jit(solution)/shard_map/ppermute | solution.py:228
  27.4 11.9 %collective-permute-start.5 = (bf16[48,4224]{1,0:T(8,128)(2,1)S(1)}, bf16[48,4224]{1,0:T(8,128)(2,1)S(1)}, u32[]{:S(2)}, u32[]{:S(2)}) collective-permute-start(bf16[48,4224]{1,0:T(8,128)(2,1)S(1)} %slice.8), channel_id=1, source_target_pairs={{0,16},{8,24},{16,0},{24,8},{1,17},{9,25},{17,1},{25,9},{2,18},{10... | collective-permute-start | bytes 1216520 | tf_op jit(solution)/shard_map/ppermute | solution.py:174
  29.0 11.6 %collective-permute-start.6 = (bf16[48,4224]{1,0:T(8,128)(2,1)S(1)}, bf16[48,4224]{1,0:T(8,128)(2,1)S(1)}, u32[]{:S(2)}, u32[]{:S(2)}) collective-permute-start(bf16[48,4224]{1,0:T(8,128)(2,1)S(1)} %slice.9), channel_id=1, source_target_pairs={{0,8},{8,0},{16,24},{24,16},{1,9},{9,1},{17,25},{25,17},{2,10},{10... | collective-permute-start | bytes 1216520 | tf_op jit(solution)/shard_map/ppermute | solution.py:175
  42.7 0.6 copy-start.1
  43.3 1.1 %collective-permute-start.8 = (f32[1,128]{1,0:T(1,128)S(1)}, f32[1,128]{1,0:T(1,128)S(1)}, u32[]{:S(2)}, u32[]{:S(2)}) collective-permute-start(f32[1,128]{1,0:T(1,128)S(1)} %get-tuple-element.26), channel_id=1, source_target_pairs={{0,1},{1,0},{2,3},{3,2},{4,5},{5,4},{6,7},{7,6},{8,9},{9,8},{10,11... | collective-permute-start | bytes 1544 | tf_op jit(solution)/shard_map/ppermute | solution.py:193
  44.4 3.7 %collective-permute-start.9 = (f32[1,128]{1,0:T(1,128)S(1)}, f32[1,128]{1,0:T(1,128)S(1)}, u32[]{:S(2)}, u32[]{:S(2)}) collective-permute-start(f32[1,128]{1,0:T(1,128)S(1)} %max.6), channel_id=1, source_target_pairs={{2,0},{4,2},{6,4},{0,6},{3,1},{5,3},{7,5},{1,7},{10,8},{12,10},{14... | collective-permute-start | bytes 1544 | tf_op jit(solution)/shard_map/ppermute | solution.py:197
  48.6 2.5 %collective-permute-start.11 = (bf16[96,4224]{1,0:T(8,128)(2,1)}, bf16[96,4224]{1,0:T(8,128)(2,1)S(1)}, u32[]{:S(2)}, u32[]{:S(2)}) collective-permute-start(bf16[96,4224]{1,0:T(8,128)(2,1)} %shard_map.39.refs_0_), channel_id=1, source_target_pairs={{0,1},{1,0},{2,3},{3,2},{4,5},{5,4},{6,7},{7,6},{8,9},{9,8},{10,11... | collective-permute-start | bytes 2433032 | tf_op jit(solution)/shard_map/ppermute | solution.py:193
  52.9 4.0 %collective-permute-start.15 = (f32[1,128]{1,0:T(1,128)S(1)}, f32[1,128]{1,0:T(1,128)S(1)}, u32[]{:S(2)}, u32[]{:S(2)}) collective-permute-start(f32[1,128]{1,0:T(1,128)S(1)} %get-tuple-element.40), channel_id=1, source_target_pairs={{0,1},{1,0},{2,3},{3,2},{4,5},{5,4},{6,7},{7,6},{8,9},{9,8},{10,11... | collective-permute-start | bytes 1544 | tf_op jit(solution)/shard_map/ppermute | solution.py:193
  53.2 5.0 %collective-permute-start.7 = (f32[1,128]{1,0:T(1,128)S(1)}, f32[1,128]{1,0:T(1,128)S(1)}, u32[]{:S(2)}, u32[]{:S(2)}) collective-permute-start(f32[1,128]{1,0:T(1,128)S(1)} %get-tuple-element.24), channel_id=1, source_target_pairs={{0,1},{1,0},{2,3},{3,2},{4,5},{5,4},{6,7},{7,6},{8,9},{9,8},{10,11... | collective-permute-start | bytes 1544 | tf_op jit(solution)/shard_map/ppermute | solution.py:193
  53.4 4.8 %collective-permute-start.12 = (f32[1,128]{1,0:T(1,128)S(1)}, f32[1,128]{1,0:T(1,128)S(1)}, u32[]{:S(2)}, u32[]{:S(2)}) collective-permute-start(f32[1,128]{1,0:T(1,128)S(1)} %get-tuple-element.36), channel_id=1, source_target_pairs={{0,8},{8,0},{16,24},{24,16},{1,9},{9,1},{17,25},{25,17},{2,10},{10... | collective-permute-start | bytes 1544 | tf_op jit(solution)/shard_map/ppermute | solution.py:247
  54.9 3.5 %collective-permute-start.13 = (f32[1,128]{1,0:T(1,128)S(1)}, f32[1,128]{1,0:T(1,128)S(1)}, u32[]{:S(2)}, u32[]{:S(2)}) collective-permute-start(f32[1,128]{1,0:T(1,128)S(1)} %get-tuple-element.37), channel_id=1, source_target_pairs={{0,16},{8,24},{16,0},{24,8},{1,17},{9,25},{17,1},{25,9},{2,18},{10... | collective-permute-start | bytes 1544 | tf_op jit(solution)/shard_map/ppermute | solution.py:247
  55.4 4.4 %collective-permute-start.14 = (f32[1,128]{1,0:T(1,128)S(1)}, f32[1,128]{1,0:T(1,128)S(1)}, u32[]{:S(2)}, u32[]{:S(2)}) collective-permute-start(f32[1,128]{1,0:T(1,128)S(1)} %get-tuple-element.38), channel_id=1, source_target_pairs={{0,24},{8,16},{16,8},{24,0},{1,25},{9,17},{17,9},{25,1},{2,26},{10... | collective-permute-start | bytes 1544 | tf_op jit(solution)/shard_map/ppermute | solution.py:247
  56.9 6.3 %collective-permute-start.16 = (f32[1,128]{1,0:T(1,128)S(1)}, f32[1,128]{1,0:T(1,128)S(1)}, u32[]{:S(2)}, u32[]{:S(2)}) collective-permute-start(f32[1,128]{1,0:T(1,128)S(1)} %max.7), channel_id=1, source_target_pairs={{4,0},{6,2},{5,1},{7,3},{12,8},{14,10},{13,9},{15,11},{20,16},{22,... | collective-permute-start | bytes 1544 | tf_op jit(solution)/shard_map/ppermute | solution.py:197
  58.2 5.0 %copy-start.4 = (f32[1,128]{1,0:T(1,128)}, f32[1,128]{1,0:T(1,128)S(1)}, u32[]{:S(2)}) copy-start(f32[1,128]{1,0:T(1,128)S(1)} %collective-permute-done.7.refs_1_) | copy-start | bytes 1540
  58.2 5.0 %copy-start.5 = (f32[1,128]{1,0:T(1,128)}, f32[1,128]{1,0:T(1,128)S(1)}, u32[]{:S(2)}) copy-start(f32[1,128]{1,0:T(1,128)S(1)} %collective-permute-done.12.refs_4_) | copy-start | bytes 1540
  58.5 4.8 %copy-start.6 = (f32[1,128]{1,0:T(1,128)}, f32[1,128]{1,0:T(1,128)S(1)}, u32[]{:S(2)}) copy-start(f32[1,128]{1,0:T(1,128)S(1)} %collective-permute-done.13.refs_5_) | copy-start | bytes 1540
  59.9 3.4 %copy-start.7 = (f32[1,128]{1,0:T(1,128)}, f32[1,128]{1,0:T(1,128)S(1)}, u32[]{:S(2)}) copy-start(f32[1,128]{1,0:T(1,128)S(1)} %collective-permute-done.14.refs_6_) | copy-start | bytes 1540
  63.2 0.6 copy-start.8
  (2 other events, 1.1 us)

commit v8 on v4

v8 whole, which is shorter than its diff:
```python
import functools

import jax
import jax.numpy as jnp
from jax import lax
from jax.experimental import pallas as pl
from jax.experimental.pallas import tpu as pltpu
from jax.sharding import Mesh, PartitionSpec as P

AXES = ("group", "z", "core")
LANES = 128
CHUNK = 512
PER_CALL = 6
VMEM = pl.BlockSpec(memory_space=pltpu.VMEM)


def flip(count, bits):
    return [(k, k ^ bits) for k in range(count)]


def unit_rows(values):
    values = values.astype(jnp.float32)
    total = jnp.sum(values * values, axis=1, keepdims=True) + values.shape[1] * 1e-06
    return (values * lax.rsqrt(total)).astype(jnp.bfloat16)


def ring_pairs(length, shift):
    if 2 * shift < length:
        return [(k, (k + shift) % length) for k in range(length)]
    pairs = [(k, k + shift) for k in range(length // 2)]
    return [pair[:: 1 - 2 * (pair[0] % 2)] for pair in pairs]


def pack_kernel(rows_ref, cluster_ref, order_ref, block_ref):
    rows, width = rows_ref.shape
    block_ref[:, :width] = unit_rows(rows_ref[...])
    meta = jnp.concatenate(
        [
            cluster_ref[...].astype(jnp.float32) + 1.0,
            order_ref[...].astype(jnp.float32),
            jnp.zeros((6, rows), jnp.float32),
        ],
        axis=0,
    )
    if rows < LANES:
        meta = jnp.concatenate([meta, jnp.zeros((8, LANES - rows), jnp.float32)], axis=1)
    turned = meta.T[:rows]
    cluster, order = turned[:, 0:1], turned[:, 1:2]
    high = jnp.floor(order / 256.0)
    lane = lax.broadcasted_iota(jnp.int32, (rows, LANES), 1)
    tail = jnp.where(lane == 0, cluster, jnp.where(lane == 1, high, order - 256.0 * high))
    block_ref[:, width:] = jnp.where(lane < 3, tail, 0.0).astype(jnp.bfloat16)


def pack(rows, cluster_ids, order_index):
    count, width = rows.shape
    return pl.pallas_call(
        pack_kernel,
        in_specs=[VMEM] * 3,
        out_specs=VMEM,
        out_shape=jax.ShapeDtypeStruct((count, width + LANES), jnp.bfloat16),
        cost_estimate=pl.CostEstimate(
            flops=4 * count * width, bytes_accessed=4 * count * width, transcendentals=count
        ),
    )(rows, cluster_ids.reshape(1, count), order_index.reshape(1, count))


def maxima_kernel(visitors, pieces, carried, *refs):
    take = list(refs)
    visitor_refs = [take.pop(0) for _ in range(visitors)]
    block_refs = [[take.pop(0) for _ in range(n)] for n in pieces]
    carry_ref = take.pop(0) if carried else None
    row_ref, col_ref, units, dots = take
    width = units.shape[1]
    rows = visitor_refs[0].shape[0]

    meta = []
    for v, ref in enumerate(visitor_refs):
        place, tail = v * LANES, ref[:, width:].astype(jnp.float32)
        units[place : place + rows, :] = ref[:, :width]
        if rows < LANES:
            units[place + rows : place + LANES, :] = jnp.zeros((LANES - rows, width), jnp.bfloat16)
            tail = jnp.concatenate([tail, jnp.zeros((LANES - rows, LANES), jnp.float32)], axis=0)
        turned = tail.T
        meta.append((turned[0:1], turned[1:2] * 256.0 + turned[2:3]))
    flat = [ref for parts in block_refs for ref in parts]
    for k in range(0, width, CHUNK):
        left = jnp.concatenate([ref[:, k : k + CHUNK] for ref in flat], axis=0)
        part = lax.dot_general(
            left,
            units[:, k : k + CHUNK],
            (((1,), (1,)), ((), ())),
            preferred_element_type=jnp.float32,
        )
        dots[...] = part if k == 0 else dots[...] + part

    row_best = [jnp.full((1, LANES), -1.0, jnp.float32) for _ in meta]
    lane = lax.broadcasted_iota(jnp.int32, (rows, LANES), 1)
    col_all = jnp.full((rows, LANES), -1.0, jnp.float32)
    for j, parts in enumerate(block_refs):
        tail = jnp.concatenate([ref[:, width:] for ref in parts], axis=0).astype(jnp.float32)
        block_cluster, block_order = tail[:, 0:1], tail[:, 1:2] * 256.0 + tail[:, 2:3]
        col_best = jnp.full((rows, 1), -1.0, jnp.float32)
        for v, (cluster, order) in enumerate(meta):
            cosine = dots[j * rows : (j + 1) * rows, v * LANES : (v + 1) * LANES]
            same = (block_cluster == cluster) & (cluster > 0)
            seen = jnp.where(same & (block_order < order), cosine, -1.0)
            row_best[v] = jnp.maximum(row_best[v], jnp.max(seen, axis=0, keepdims=True))
            if v > 0:
                seen = jnp.where(same & (order < block_order), cosine, -1.0)
                col_best = jnp.maximum(col_best, jnp.max(seen, axis=1, keepdims=True))
        col_all = jnp.where(lane == j, col_best, col_all)
    for v, best in enumerate(row_best):
        row_ref[v : v + 1, :] = jnp.maximum(best, carry_ref[v : v + 1, :]) if carried else best
    if rows < LANES:
        fill = jnp.full((LANES - rows, LANES), -1.0, jnp.float32)
        col_all = jnp.concatenate([col_all, fill], axis=0)
    col_ref[...] = col_all.T[: len(pieces)]


def maxima(visitors, blocks, carry=None):
    rows, width = visitors[0].shape[0], visitors[0].shape[1] - LANES
    count, col_best = len(visitors), []
    for first in range(0, len(blocks), PER_CALL):
        part = blocks[first : first + PER_CALL]
        operands = list(visitors) + [piece for block in part for piece in block]
        operands += [] if carry is None else [carry]
        carry, col = pl.pallas_call(
            functools.partial(
                maxima_kernel, count, [len(block) for block in part], carry is not None
            ),
            in_specs=[VMEM] * len(operands),
            out_specs=[VMEM] * 2,
            out_shape=[
                jax.ShapeDtypeStruct((count, LANES), jnp.float32),
                jax.ShapeDtypeStruct((len(part), LANES), jnp.float32),
            ],
            scratch_shapes=[
                pltpu.VMEM((count * LANES, width), jnp.bfloat16),
                pltpu.VMEM((len(part) * rows, count * LANES), jnp.float32),
            ],
            compiler_params=pltpu.CompilerParams(vmem_limit_bytes=40 * 2**20),
            cost_estimate=pl.CostEstimate(
                flops=2 * len(part) * rows * count * LANES * width,
                bytes_accessed=2 * (len(part) + count) * rows * width,
                transcendentals=0,
            ),
        )(*operands)
        col_best.append(col)
    return carry, jnp.concatenate(col_best)


def join_kernel(*refs):
    top_ref, bottom_ref, out_ref = refs[-3:]
    half = top_ref.shape[0]
    out_ref[:half] = top_ref[...]
    out_ref[half:] = bottom_ref[...]


def join(top, bottom, others):
    anywhere = pl.BlockSpec(memory_space=pl.ANY)
    rows, width = 2 * top.shape[0], top.shape[1]
    return pl.pallas_call(
        join_kernel,
        in_specs=[anywhere] * len(others) + [VMEM] * 2,
        out_specs=VMEM,
        out_shape=jax.ShapeDtypeStruct((rows, width), top.dtype),
        cost_estimate=pl.CostEstimate(flops=0, bytes_accessed=4 * rows * width, transcendentals=0),
    )(*others, top, bottom)


def cut_kernel(value_ref, other_ref, out_ref):
    out_ref[...] = value_ref[: out_ref.shape[0]]


def top_half(value, other):
    return pl.pallas_call(
        cut_kernel,
        in_specs=[VMEM, pl.BlockSpec(memory_space=pl.ANY)],
        out_specs=VMEM,
        out_shape=jax.ShapeDtypeStruct((value.shape[0] // 2, value.shape[1]), value.dtype),
    )(value, other)


def gather_plane(block, groups, other):
    half = block.shape[0] // 2
    blocks = {0: [block]}
    for s in range(1, groups):
        low, high = s & -s, 1 << (s.bit_length() - 1)
        if low == high:
            blocks[s] = [lax.ppermute(block, "group", flip(groups, s))]
            continue
        top, bottom = blocks[s ^ high], blocks[s ^ low]
        top = top_half(top[0], other) if len(top) == 1 else top[0]
        bottom = bottom[0][half:] if len(bottom) == 1 else bottom[1]
        blocks[s] = [
            lax.ppermute(top, "group", flip(groups, high)),
            lax.ppermute(bottom, "group", flip(groups, low)),
        ]
    return blocks


def swap(block):
    return lax.ppermute(block, "core", flip(2, 1))


def local(embeddings, cluster_ids, order_index):
    rows = embeddings.shape[0]
    groups, length = lax.axis_size("group"), lax.axis_size("z")
    routes = [ring_pairs(length, shift) for shift in range(1, length // 2 + 1)]
    own = pack(embeddings, cluster_ids, order_index)
    visitors = [own] + [lax.ppermute(own, "z", route) for route in routes]
    across = swap(own)
    plane = gather_plane(own, groups, across)

    last = plane.pop(groups - 1)
    blocks = [[own], [across]]
    for s in range(1, groups - 1):
        blocks += [plane[s], [swap(part) for part in plane[s]]]
    last = join(*last, visitors[1:])
    row, col = maxima(visitors, blocks)
    row, last_col = maxima(visitors, [[last], [swap(last)]], row)
    col = jnp.concatenate([col, last_col]).reshape(groups, 2, LANES)
    col = jnp.maximum(col[:, 0], swap(col[:, 1]))

    best = row[0]
    for index, route in enumerate(routes):
        home = lax.ppermute(row[index + 1], "z", [(b, a) for a, b in route])
        if len(route) < length:
            here = lax.axis_index("z")
            sent = functools.reduce(jnp.logical_or, [here == a for a, _ in route])
            home = jnp.where(sent, home, -1.0)
        best = jnp.maximum(best, home)
    for s in range(groups):
        home = lax.ppermute(col, "group", flip(groups, s)) if s else col
        best = jnp.maximum(best, home[s])
    return best[:rows]


def solution(mesh):
    groups, members = mesh.devices.shape
    fine = Mesh(mesh.devices.reshape(groups, members // 2, 2), AXES)
    placed = (P(AXES, None), P(AXES), P(AXES))
    return jax.shard_map(local, mesh=fine, in_specs=placed, out_specs=P(AXES), check_vma=False)
```

time: 64.1 us -> 70.8 us (1.10)
  blocking collectives: 12.6 us -> 0 us
  starting transfers between devices: 12.6 us -> 22 us
  local copies, waits for them, and re-layouts: 1.38 us -> 7.15 us
  Pallas kernels: 7.78 us -> 12.4 us
    all_to_all x1 -> x0, blocking collectives: 12.6 us -> none  [local(): lax.all_to_all(answer, AXES, split_axis=0, concat_axis=0, tiled=True)]
    ppermute x2, waiting for transfers between devices: 0.01 us -> 10.6 us  [gather_plane(): blocks[s] = [lax.ppermute(block, 'group', flip(groups, s))]]
    ppermute x1, waiting for transfers between devices: 8.39 us -> 0.01 us  [gather_plane(): lax.ppermute(bottom, 'group', flip(groups, low))]
    ppermute x5 -> x12, starting transfers between devices: 6.49 us -> 14.2 us  [the longest x2 6.11 us: local(): visitors = [own] + [lax.ppermute(own, 'z', route) for route in routes]]
    unnamed x6 -> x24, local copies, waits for them, and re-layouts: 1.32 us -> 6.11 us
    pallas_call x4, Pallas kernels: 5.38 us -> 9.97 us  [the longest x2 5.91 us: maxima(): pl.pallas_call(functools.partial(maxima_kernel, count, [len(block) for bl...]
    ppermute x5 -> x12, waiting for transfers between devices: 19.2 us -> 17.5 us  [the longest x2 11.7 us: local(): visitors = [own] + [lax.ppermute(own, 'z', route) for route in routes]]
    ppermute x2, starting transfers between devices: 3.01 us -> 4.46 us  [gather_plane(): blocks[s] = [lax.ppermute(block, 'group', flip(groups, s))]]
  transfers between devices with their start and end apart: 9 -> 16, of which waited for: 4 -> 5; matrix products, arithmetic and copies ran while one was open for 0% -> 1% of each run, Pallas kernels for 7% -> 12%
where the time goes in v8:
time: 70.8 us; the launch traced here: 70.4 us
  waiting for transfers between devices  28.2 us (40%)
  starting transfers between devices  22 us (31%)
  Pallas kernels  12.4 us (18%)
  local copies, waits for them, and re-layouts  7.15 us (10%)
    ppermute x2, waiting for transfers between devices, local(): visitors = [own] + [lax.ppermute(own, 'z', route) for route in routes]  11.7 us
    ppermute x2, waiting for transfers between devices, gather_plane(): blocks[s] = [lax.ppermute(block, 'group', flip(groups, s))]  10.6 us
    unnamed x24, local copies, waits for them, and re-layouts  6.11 us
    ppermute x2, starting transfers between devices, local(): visitors = [own] + [lax.ppermute(own, 'z', route) for route in routes]  6.11 us
    pallas_call x2, Pallas kernels, maxima(): pl.pallas_call(functools.partial(maxima_kernel, count, [len(block) for bl...  5.91 us
    ppermute x2, waiting for transfers between devices, local(): home = lax.ppermute(row[index + 1], 'z', [(b, a) for a, b in route])  5.02 us
    ppermute x2, starting transfers between devices, gather_plane(): blocks[s] = [lax.ppermute(block, 'group', flip(groups, s))]  4.46 us
    ppermute x2, starting transfers between devices, local(): home = lax.ppermute(row[index + 1], 'z', [(b, a) for a, b in route])  3.55 us
  transfers between devices with their start and end apart: 16, of which 5 were waited for; matrix products, arithmetic and copies ran while one was open for 1% of the time, Pallas kernels for 12%

profile of v8, /device:TPU:0, one launch (start us, length us, event | category | flops | bytes accessed | tf_op | source)
XLA Modules:
  0.0 70.4 jit_solution(5911669970271632777)
XLA Ops:
  0.0 2.4 %shard_map.37.refs_0_.refs_3_ = bf16[96,4224]{1,0:T(8,128)(2,1)} custom-call(bf16[96,4096]{1,0:T(8,128)(2,1)} %rows_ref.1, s32[1,96]{1,0:T(1,128)} %bitcast.33, s32[1,96]{1,0:T(1,128)} %bitcast.34), custom_call_target="tpu_custom_call" | custom-call | flops 1572864 | bytes 1572864 | tf_op jit(solution)/shard_map/pallas_call | solution.py:57
  2.4 2.9 %collective-permute-start.2 = (bf16[96,4224]{1,0:T(8,128)(2,1)}, bf16[96,4224]{1,0:T(8,128)(2,1)S(1)}, u32[]{:S(2)}, u32[]{:S(2)}) collective-permute-start(bf16[96,4224]{1,0:T(8,128)(2,1)} %shard_map.37.refs_0_.refs_3_), channel_id=1, source_target_pairs={{0,8},{8,0},{16,24},{24,16},{1,9},{9,1},{17,25},{25,17},{2,10},{10... | collective-permute-start | bytes 2433032 | tf_op jit(solution)/shard_map/ppermute | solution.py:191
  5.3 1.5 %collective-permute-start.5 = (bf16[96,4224]{1,0:T(8,128)(2,1)}, bf16[96,4224]{1,0:T(8,128)(2,1)}, u32[]{:S(2)}, u32[]{:S(2)}) collective-permute-start(bf16[96,4224]{1,0:T(8,128)(2,1)} %shard_map.37.refs_0_.refs_3_), channel_id=1, source_target_pairs={{0,16},{8,24},{16,0},{24,8},{1,17},{9,25},{17,1},{25,9},{2,18},{10... | collective-permute-start | bytes 2433032 | tf_op jit(solution)/shard_map/ppermute | solution.py:191
  6.8 1.6 %collective-permute-start = (bf16[96,4224]{1,0:T(8,128)(2,1)}, bf16[96,4224]{1,0:T(8,128)(2,1)S(1)}, u32[]{:S(2)}, u32[]{:S(2)}) collective-permute-start(bf16[96,4224]{1,0:T(8,128)(2,1)} %shard_map.37.refs_0_.refs_3_), channel_id=1, source_target_pairs={{0,2},{2,4},{4,6},{6,0},{1,3},{3,5},{5,7},{7,1},{8,10},{10,12},{12... | collective-permute-start | bytes 2433032 | tf_op jit(solution)/shard_map/ppermute | solution.py:212
  8.4 4.5 %collective-permute-start.1 = (bf16[96,4224]{1,0:T(8,128)(2,1)}, bf16[96,4224]{1,0:T(8,128)(2,1)S(1)}, u32[]{:S(2)}, u32[]{:S(2)}) collective-permute-start(bf16[96,4224]{1,0:T(8,128)(2,1)} %shard_map.37.refs_0_.refs_3_), channel_id=1, source_target_pairs={{0,4},{6,2},{1,5},{7,3},{8,12},{14,10},{9,13},{15,11},{16,20},{22,... | collective-permute-start | bytes 2433032 | tf_op jit(solution)/shard_map/ppermute | solution.py:212
  13.0 10.6 %collective-permute-done.2.value_ref.refs_5_ = bf16[96,4224]{1,0:T(8,128)(2,1)S(1)} collective-permute-done((bf16[96,4224]{1,0:T(8,128)(2,1)}, bf16[96,4224]{1,0:T(8,128)(2,1)S(1)}, u32[]{:S(2)}, u32[]{:S(2)}) %collective-permute-start.2) | collective-permute-done | bytes 811040 | tf_op jit(solution)/shard_map/ppermute | solution.py:191
  23.6 0.9 %copy-done.8 = bf16[96,4224]{1,0:T(8,128)(2,1)} copy-done((bf16[96,4224]{1,0:T(8,128)(2,1)}, bf16[96,4224]{1,0:T(8,128)(2,1)S(1)}, u32[]{:S(2)}) %copy-start.8) | copy-done | bytes 811032
  24.5 0.9 %copy-done.10 = bf16[96,4224]{1,0:T(8,128)(2,1)} copy-done((bf16[96,4224]{1,0:T(8,128)(2,1)}, bf16[96,4224]{1,0:T(8,128)(2,1)S(1)}, u32[]{:S(2)}) %copy-start.10) | copy-done | bytes 811032
  25.4 1.9 %shard_map.38 = bf16[48,4224]{1,0:T(8,128)(2,1)} custom-call(bf16[96,4224]{1,0:T(8,128)(2,1)} %copy-done.8, bf16[96,4224]{1,0:T(8,128)(2,1)} %copy-done.10), custom_call_target="tpu_custom_call" | custom-call | tf_op jit(solution)/shard_map/pallas_call | solution.py:177
  27.3 1.8 %collective-permute-start.4 = (bf16[48,4224]{1,0:T(8,128)(2,1)}, bf16[48,4224]{1,0:T(8,128)(2,1)}, u32[]{:S(2)}, u32[]{:S(2)}) collective-permute-start(bf16[48,4224]{1,0:T(8,128)(2,1)} %shard_map.38), channel_id=1, source_target_pairs={{0,16},{8,24},{16,0},{24,8},{1,17},{9,25},{17,1},{25,9},{2,18},{10... | collective-permute-start | bytes 1216520 | tf_op jit(solution)/shard_map/ppermute | solution.py:197
  29.1 1.0 %slice.44 = bf16[48,4224]{1,0:T(8,128)(2,1)S(1)} slice(bf16[96,4224]{1,0:T(8,128)(2,1)} %collective-permute-done.5.refs_7_), slice={[48:96], [0:4224]} | slice | bytes 811008 | tf_op jit(solution)/shard_map/slice | solution.py:195
  30.2 1.6 %collective-permute-start.6 = (bf16[48,4224]{1,0:T(8,128)(2,1)S(1)}, bf16[48,4224]{1,0:T(8,128)(2,1)}, u32[]{:S(2)}, u32[]{:S(2)}) collective-permute-start(bf16[48,4224]{1,0:T(8,128)(2,1)S(1)} %slice.44), channel_id=1, source_target_pairs={{0,8},{8,0},{16,24},{24,16},{1,9},{9,1},{17,25},{25,17},{2,10},{10... | collective-permute-start | bytes 1216520 | tf_op jit(solution)/shard_map/ppermute | solution.py:198
  32.2 11.7 %collective-permute-done.1.refs_1_.refs_2_ = bf16[96,4224]{1,0:T(8,128)(2,1)S(1)} collective-permute-done((bf16[96,4224]{1,0:T(8,128)(2,1)}, bf16[96,4224]{1,0:T(8,128)(2,1)S(1)}, u32[]{:S(2)}, u32[]{:S(2)}) %collective-permute-start.1) | collective-permute-done | bytes 811040 | tf_op jit(solution)/shard_map/ppermute | solution.py:212
  44.8 2.1 %shard_map.39.refs_3_ = bf16[96,4224]{1,0:T(8,128)(2,1)} custom-call(bf16[96,4224]{1,0:T(8,128)(2,1)} %copy-done.1, bf16[96,4224]{1,0:T(8,128)(2,1)} %copy-done.4, bf16[48,4224]{1,0:T(8,128)(2,1)} %collective-permute-done.4.refs_2_, bf16[48,4224]{1,0:T(8,128)(2,1)} %collective-permute-done.6.refs_3_), custom_call_target="tpu_custom_call" | custom-call | bytes 1622016 | tf_op jit(solution)/shard_map/pallas_call | solution.py:163
  46.9 1.1 %copy-done.2 = bf16[96,4224]{1,0:T(8,128)(2,1)S(1)} copy-done((bf16[96,4224]{1,0:T(8,128)(2,1)S(1)}, bf16[96,4224]{1,0:T(8,128)(2,1)}, u32[]{:S(2)}) %copy-start.2) | copy-done | bytes 811032
  48.1 1.1 %copy-done.5 = bf16[96,4224]{1,0:T(8,128)(2,1)S(1)} copy-done((bf16[96,4224]{1,0:T(8,128)(2,1)S(1)}, bf16[96,4224]{1,0:T(8,128)(2,1)}, u32[]{:S(2)}) %copy-start.5) | copy-done | bytes 811032
  49.2 1.1 %copy-done.11 = bf16[96,4224]{1,0:T(8,128)(2,1)S(1)} copy-done((bf16[96,4224]{1,0:T(8,128)(2,1)S(1)}, bf16[96,4224]{1,0:T(8,128)(2,1)}, u32[]{:S(2)}) %copy-start.11) | copy-done | bytes 811032
  50.3 4.6 %shard_map.40 = (f32[3,128]{1,0:T(4,128)S(1)}, f32[6,128]{1,0:T(8,128)S(1)}) custom-call(bf16[96,4224]{1,0:T(8,128)(2,1)S(1)} %copy-done, bf16[96,4224]{1,0:T(8,128)(2,1)S(1)} %copy-done.2, bf16[96,4224]{1,0:T(8,128)(2,1)S(1)} %copy-done.5, bf16[96,4224]{1,0:T(8,128)(2,1)S(1)} %copy-done, bf16[96,4224]{1,0:T(8,128)(2,1)S(1)} %copy-done.11, ...), custom_call_target="tpu_custom_call" | custom-call | flops 1811939328 | bytes 7077888 | tf_op jit(solution)/shard_map/pallas_call | solution.py:128
  55.0 1.3 %shard_map.41 = (f32[3,128]{1,0:T(4,128)S(1)}, f32[2,128]{1,0:T(2,128)S(1)}) custom-call(bf16[96,4224]{1,0:T(8,128)(2,1)S(1)} %copy-done, bf16[96,4224]{1,0:T(8,128)(2,1)S(1)} %copy-done.3, bf16[96,4224]{1,0:T(8,128)(2,1)S(1)} %copy-done.6, bf16[96,4224]{1,0:T(8,128)(2,1)S(1)} %copy-done.7, bf16[96,4224]{1,0:T(8,128)(2,1)S(1)} %collective-permute-done.7.refs_4_, ...), custom_call_target="tpu_custom_call" | custom-call | flops 603979776 | bytes 3932160 | tf_op jit(solution)/shard_map/pallas_call | solution.py:128
  58.8 2.5 %collective-permute-start.15 = (f32[4,128]{1,0:T(4,128)S(1)}, f32[4,128]{1,0:T(4,128)S(1)}, u32[]{:S(2)}, u32[]{:S(2)}) collective-permute-start(f32[4,128]{1,0:T(4,128)S(1)} %max.23), channel_id=1, source_target_pairs={{0,24},{8,16},{16,8},{24,0},{1,25},{9,17},{17,9},{25,1},{2,26},{10... | collective-permute-start | bytes 6152 | tf_op jit(solution)/shard_map/ppermute | solution.py:235
  61.2 2.3 %collective-permute-start.10 = (f32[128]{0:T(128)S(1)}, f32[128]{0:T(128)S(1)}, u32[]{:S(2)}, u32[]{:S(2)}) collective-permute-start(f32[128]{0:T(128)S(1)} %get-tuple-element.15), channel_id=1, source_target_pairs={{2,0},{4,2},{6,4},{0,6},{3,1},{5,3},{7,5},{1,7},{10,8},{12,10},{14... | collective-permute-start | bytes 1544 | tf_op jit(solution)/shard_map/ppermute | solution.py:228
  63.5 1.3 %collective-permute-start.11 = (f32[128]{0:T(128)S(1)}, f32[128]{0:T(128)S(1)}, u32[]{:S(2)}, u32[]{:S(2)}) collective-permute-start(f32[128]{0:T(128)S(1)} %get-tuple-element.16), channel_id=1, source_target_pairs={{4,0},{2,6},{5,1},{3,7},{12,8},{10,14},{13,9},{11,15},{20,16},{18,... | collective-permute-start | bytes 1544 | tf_op jit(solution)/shard_map/ppermute | solution.py:228
  64.8 1.2 %collective-permute-done.10 = f32[128]{0:T(128)S(1)} collective-permute-done((f32[128]{0:T(128)S(1)}, f32[128]{0:T(128)S(1)}, u32[]{:S(2)}, u32[]{:S(2)}) %collective-permute-start.10) | collective-permute-done | bytes 544 | tf_op jit(solution)/shard_map/ppermute | solution.py:228
  66.0 3.9 %collective-permute-done.11 = f32[128]{0:T(128)S(1)} collective-permute-done((f32[128]{0:T(128)S(1)}, f32[128]{0:T(128)S(1)}, u32[]{:S(2)}, u32[]{:S(2)}) %collective-permute-start.11) | collective-permute-done | bytes 544 | tf_op jit(solution)/shard_map/ppermute | solution.py:228
  (43 shorter events, 4.4 us)
Async XLA Ops:
  2.4 21.2 %collective-permute-start.2 = (bf16[96,4224]{1,0:T(8,128)(2,1)}, bf16[96,4224]{1,0:T(8,128)(2,1)S(1)}, u32[]{:S(2)}, u32[]{:S(2)}) collective-permute-start(bf16[96,4224]{1,0:T(8,128)(2,1)} %shard_map.37.refs_0_.refs_3_), channel_id=1, source_target_pairs={{0,8},{8,0},{16,24},{24,16},{1,9},{9,1},{17,25},{25,17},{2,10},{10... | collective-permute-start | bytes 2433032 | tf_op jit(solution)/shard_map/ppermute | solution.py:191
  5.3 18.3 %collective-permute-start.3 = (bf16[96,4224]{1,0:T(8,128)(2,1)}, bf16[96,4224]{1,0:T(8,128)(2,1)S(1)}, u32[]{:S(2)}, u32[]{:S(2)}) collective-permute-start(bf16[96,4224]{1,0:T(8,128)(2,1)} %shard_map.37.refs_0_.refs_3_), channel_id=1, source_target_pairs={{0,1},{1,0},{2,3},{3,2},{4,5},{5,4},{6,7},{7,6},{8,9},{9,8},{10,11... | collective-permute-start | bytes 2433032 | tf_op jit(solution)/shard_map/ppermute | solution.py:204
  5.3 23.8 %collective-permute-start.5 = (bf16[96,4224]{1,0:T(8,128)(2,1)}, bf16[96,4224]{1,0:T(8,128)(2,1)}, u32[]{:S(2)}, u32[]{:S(2)}) collective-permute-start(bf16[96,4224]{1,0:T(8,128)(2,1)} %shard_map.37.refs_0_.refs_3_), channel_id=1, source_target_pairs={{0,16},{8,24},{16,0},{24,8},{1,17},{9,25},{17,1},{25,9},{2,18},{10... | collective-permute-start | bytes 2433032 | tf_op jit(solution)/shard_map/ppermute | solution.py:191
  6.8 24.9 %collective-permute-start = (bf16[96,4224]{1,0:T(8,128)(2,1)}, bf16[96,4224]{1,0:T(8,128)(2,1)S(1)}, u32[]{:S(2)}, u32[]{:S(2)}) collective-permute-start(bf16[96,4224]{1,0:T(8,128)(2,1)} %shard_map.37.refs_0_.refs_3_), channel_id=1, source_target_pairs={{0,2},{2,4},{4,6},{6,0},{1,3},{3,5},{5,7},{7,1},{8,10},{10,12},{12... | collective-permute-start | bytes 2433032 | tf_op jit(solution)/shard_map/ppermute | solution.py:212
  8.4 35.5 %collective-permute-start.1 = (bf16[96,4224]{1,0:T(8,128)(2,1)}, bf16[96,4224]{1,0:T(8,128)(2,1)S(1)}, u32[]{:S(2)}, u32[]{:S(2)}) collective-permute-start(bf16[96,4224]{1,0:T(8,128)(2,1)} %shard_map.37.refs_0_.refs_3_), channel_id=1, source_target_pairs={{0,4},{6,2},{1,5},{7,3},{8,12},{14,10},{9,13},{15,11},{16,20},{22,... | collective-permute-start | bytes 2433032 | tf_op jit(solution)/shard_map/ppermute | solution.py:212
  27.3 4.4 %copy-start.9 = (bf16[96,4224]{1,0:T(8,128)(2,1)S(1)}, bf16[96,4224]{1,0:T(8,128)(2,1)}, u32[]{:S(2)}) copy-start(bf16[96,4224]{1,0:T(8,128)(2,1)} %copy-done.8) | copy-start | bytes 2433028
  27.3 16.6 %collective-permute-start.4 = (bf16[48,4224]{1,0:T(8,128)(2,1)}, bf16[48,4224]{1,0:T(8,128)(2,1)}, u32[]{:S(2)}, u32[]{:S(2)}) collective-permute-start(bf16[48,4224]{1,0:T(8,128)(2,1)} %shard_map.38), channel_id=1, source_target_pairs={{0,16},{8,24},{16,0},{24,8},{1,17},{9,25},{17,1},{25,9},{2,18},{10... | collective-permute-start | bytes 1216520 | tf_op jit(solution)/shard_map/ppermute | solution.py:197
  30.1 16.8 %copy-start = (bf16[96,4224]{1,0:T(8,128)(2,1)S(1)}, bf16[96,4224]{1,0:T(8,128)(2,1)}, u32[]{:S(2)}) copy-start(bf16[96,4224]{1,0:T(8,128)(2,1)} %shard_map.37.refs_0_.refs_3_) | copy-start | bytes 2433028
  30.2 13.7 %collective-permute-start.6 = (bf16[48,4224]{1,0:T(8,128)(2,1)S(1)}, bf16[48,4224]{1,0:T(8,128)(2,1)}, u32[]{:S(2)}, u32[]{:S(2)}) collective-permute-start(bf16[48,4224]{1,0:T(8,128)(2,1)S(1)} %slice.44), channel_id=1, source_target_pairs={{0,8},{8,0},{16,24},{24,16},{1,9},{9,1},{17,25},{25,17},{2,10},{10... | collective-permute-start | bytes 1216520 | tf_op jit(solution)/shard_map/ppermute | solution.py:198
  31.7 15.2 %collective-permute-start.8 = (bf16[96,4224]{1,0:T(8,128)(2,1)S(1)}, bf16[96,4224]{1,0:T(8,128)(2,1)}, u32[]{:S(2)}, u32[]{:S(2)}) collective-permute-start(bf16[96,4224]{1,0:T(8,128)(2,1)S(1)} %copy-done.9), channel_id=1, source_target_pairs={{0,1},{1,0},{2,3},{3,2},{4,5},{5,4},{6,7},{7,6},{8,9},{9,8},{10,11... | collective-permute-start | bytes 2433032 | tf_op jit(solution)/shard_map/ppermute | solution.py:204
  31.7 12.2 %copy-start.1 = (bf16[96,4224]{1,0:T(8,128)(2,1)}, bf16[96,4224]{1,0:T(8,128)(2,1)S(1)}, u32[]{:S(2)}) copy-start(bf16[96,4224]{1,0:T(8,128)(2,1)S(1)} %collective-permute-done.refs_0_.refs_1_) | copy-start | bytes 2433028
  31.7 15.2 %collective-permute-start.9 = (bf16[96,4224]{1,0:T(8,128)(2,1)}, bf16[96,4224]{1,0:T(8,128)(2,1)}, u32[]{:S(2)}, u32[]{:S(2)}) collective-permute-start(bf16[96,4224]{1,0:T(8,128)(2,1)} %collective-permute-done.5.refs_7_), channel_id=1, source_target_pairs={{0,1},{1,0},{2,3},{3,2},{4,5},{5,4},{6,7},{7,6},{8,9},{9,8},{10,11... | collective-permute-start | bytes 2433032 | tf_op jit(solution)/shard_map/ppermute | solution.py:204
  46.9 8.0 %collective-permute-start.7 = (bf16[96,4224]{1,0:T(8,128)(2,1)}, bf16[96,4224]{1,0:T(8,128)(2,1)S(1)}, u32[]{:S(2)}, u32[]{:S(2)}) collective-permute-start(bf16[96,4224]{1,0:T(8,128)(2,1)} %shard_map.39.refs_3_), channel_id=1, source_target_pairs={{0,1},{1,0},{2,3},{3,2},{4,5},{5,4},{6,7},{7,6},{8,9},{9,8},{10,11... | collective-permute-start | bytes 2433032 | tf_op jit(solution)/shard_map/ppermute | solution.py:204
  46.9 1.1 %copy-start.2 = (bf16[96,4224]{1,0:T(8,128)(2,1)S(1)}, bf16[96,4224]{1,0:T(8,128)(2,1)}, u32[]{:S(2)}) copy-start(bf16[96,4224]{1,0:T(8,128)(2,1)} %copy-done.1) | copy-start | bytes 2433028
  49.2 1.1 %copy-start.11 = (bf16[96,4224]{1,0:T(8,128)(2,1)S(1)}, bf16[96,4224]{1,0:T(8,128)(2,1)}, u32[]{:S(2)}) copy-start(bf16[96,4224]{1,0:T(8,128)(2,1)} %copy-done.10) | copy-start | bytes 2433028
  50.3 4.6 %copy-start.3 = (bf16[96,4224]{1,0:T(8,128)(2,1)S(1)}, bf16[96,4224]{1,0:T(8,128)(2,1)}, u32[]{:S(2)}) copy-start(bf16[96,4224]{1,0:T(8,128)(2,1)} %copy-done.1) | copy-start | bytes 2433028
  50.3 4.6 %copy-start.6 = (bf16[96,4224]{1,0:T(8,128)(2,1)S(1)}, bf16[96,4224]{1,0:T(8,128)(2,1)}, u32[]{:S(2)}) copy-start(bf16[96,4224]{1,0:T(8,128)(2,1)} %copy-done.4) | copy-start | bytes 2433028
  50.3 4.6 %copy-start.7 = (bf16[96,4224]{1,0:T(8,128)(2,1)S(1)}, bf16[96,4224]{1,0:T(8,128)(2,1)}, u32[]{:S(2)}) copy-start(bf16[96,4224]{1,0:T(8,128)(2,1)} %shard_map.39.refs_3_) | copy-start | bytes 2433028
  56.3 1.4 %collective-permute-start.12 = (f32[4,128]{1,0:T(4,128)S(1)}, f32[4,128]{1,0:T(4,128)S(1)}, u32[]{:S(2)}, u32[]{:S(2)}) collective-permute-start(f32[4,128]{1,0:T(4,128)S(1)} %bitcast.32), channel_id=1, source_target_pairs={{0,1},{1,0},{2,3},{3,2},{4,5},{5,4},{6,7},{7,6},{8,9},{9,8},{10,11... | collective-permute-start | bytes 6152 | tf_op jit(solution)/shard_map/ppermute | solution.py:204
  57.7 12.1 %collective-permute-start.13 = (f32[4,128]{1,0:T(4,128)S(1)}, f32[4,128]{1,0:T(4,128)S(1)}, u32[]{:S(2)}, u32[]{:S(2)}) collective-permute-start(f32[4,128]{1,0:T(4,128)S(1)} %max.23), channel_id=1, source_target_pairs={{0,8},{8,0},{16,24},{24,16},{1,9},{9,1},{17,25},{25,17},{2,10},{10... | collective-permute-start | bytes 6152 | tf_op jit(solution)/shard_map/ppermute | solution.py:235
  58.3 11.6 %collective-permute-start.14 = (f32[4,128]{1,0:T(4,128)S(1)}, f32[4,128]{1,0:T(4,128)S(1)}, u32[]{:S(2)}, u32[]{:S(2)}) collective-permute-start(f32[4,128]{1,0:T(4,128)S(1)} %max.23), channel_id=1, source_target_pairs={{0,16},{8,24},{16,0},{24,8},{1,17},{9,25},{17,1},{25,9},{2,18},{10... | collective-permute-start | bytes 6152 | tf_op jit(solution)/shard_map/ppermute | solution.py:235
  58.8 11.1 %collective-permute-start.15 = (f32[4,128]{1,0:T(4,128)S(1)}, f32[4,128]{1,0:T(4,128)S(1)}, u32[]{:S(2)}, u32[]{:S(2)}) collective-permute-start(f32[4,128]{1,0:T(4,128)S(1)} %max.23), channel_id=1, source_target_pairs={{0,24},{8,16},{16,8},{24,0},{1,25},{9,17},{17,9},{25,1},{2,26},{10... | collective-permute-start | bytes 6152 | tf_op jit(solution)/shard_map/ppermute | solution.py:235
  61.2 4.7 %collective-permute-start.10 = (f32[128]{0:T(128)S(1)}, f32[128]{0:T(128)S(1)}, u32[]{:S(2)}, u32[]{:S(2)}) collective-permute-start(f32[128]{0:T(128)S(1)} %get-tuple-element.15), channel_id=1, source_target_pairs={{2,0},{4,2},{6,4},{0,6},{3,1},{5,3},{7,5},{1,7},{10,8},{12,10},{14... | collective-permute-start | bytes 1544 | tf_op jit(solution)/shard_map/ppermute | solution.py:228
  63.5 6.3 %collective-permute-start.11 = (f32[128]{0:T(128)S(1)}, f32[128]{0:T(128)S(1)}, u32[]{:S(2)}, u32[]{:S(2)}) collective-permute-start(f32[128]{0:T(128)S(1)} %get-tuple-element.16), channel_id=1, source_target_pairs={{4,0},{2,6},{5,1},{3,7},{12,8},{10,14},{13,9},{11,15},{20,16},{18,... | collective-permute-start | bytes 1544 | tf_op jit(solution)/shard_map/ppermute | solution.py:228
  (4 other events, 3.8 us)

commit v9 on v1

v9 whole, which is shorter than its diff:
```python
import functools

import jax
import jax.numpy as jnp
from jax import lax
from jax.experimental import pallas as pl
from jax.experimental.pallas import tpu as pltpu
from jax.sharding import Mesh, PartitionSpec as P

AXES = ("group", "z", "core")
LANES = 128
CHUNK = 512
CALL = 8
VMEM = pl.BlockSpec(memory_space=pltpu.VMEM)


def flip(count, bits):
    return [(k, k ^ bits) for k in range(count)]


def unit_rows(values):
    values = values.astype(jnp.float32)
    total = jnp.sum(values * values, axis=1, keepdims=True) + values.shape[1] * 1e-06
    return (values * lax.rsqrt(total)).astype(jnp.bfloat16)


def ring_pairs(length, shift):
    if 2 * shift < length:
        return [(k, (k + shift) % length) for k in range(length)]
    pairs = [(k, k + shift) for k in range(length // 2)]
    return [pair[:: 1 - 2 * (pair[0] % 2)] for pair in pairs]


def gather_plane(block, groups):
    half = block.shape[0] // 2
    blocks = {0: [block]}
    for s in range(1, groups):
        low, high = s & -s, 1 << (s.bit_length() - 1)
        if low == high:
            blocks[s] = [lax.ppermute(block, "group", flip(groups, s))]
            continue
        top, bottom = blocks[s ^ high], blocks[s ^ low]
        top = top[0][:half] if len(top) == 1 else top[0]
        bottom = bottom[0][half:] if len(bottom) == 1 else bottom[1]
        blocks[s] = [
            lax.ppermute(top, "group", flip(groups, high)),
            lax.ppermute(bottom, "group", flip(groups, low)),
        ]
    return blocks


def swap(block):
    return lax.ppermute(block, "core", flip(2, 1))


def pack_kernel(*refs):
    both_ref, own_ref = refs[6:]
    rows, width = refs[0].shape
    core = lax.axis_index("core")
    for index, (rows_ref, cluster_ref, order_ref) in enumerate((refs[:3], refs[3:6])):
        unit = unit_rows(rows_ref[...])
        meta = jnp.concatenate(
            [
                cluster_ref[...].astype(jnp.float32) + 1.0,
                order_ref[...].astype(jnp.float32),
                jnp.zeros((6, rows), jnp.float32),
            ],
            axis=0,
        )
        if rows < LANES:
            meta = jnp.concatenate([meta, jnp.zeros((8, LANES - rows), jnp.float32)], axis=1)
        turned = meta.T[:rows]
        cluster, order = turned[:, 0:1], turned[:, 1:2]
        high = jnp.floor(order / 256.0)
        lane = lax.broadcasted_iota(jnp.int32, (rows, LANES), 1)
        tail = jnp.where(lane == 0, cluster, jnp.where(lane == 1, high, order - 256.0 * high))
        tail = jnp.where(lane < 3, tail, 0.0).astype(jnp.bfloat16)
        place = pl.ds(pl.multiple_of((core ^ index) * rows, 16), rows)
        both_ref[place, :width] = unit
        both_ref[place, width:] = tail
        if index == 0:
            own_ref[:, :width] = unit
            own_ref[:, width:] = tail


def pack(rows, cluster_ids, order_index):
    count, width = rows.shape
    operands = [rows, cluster_ids, order_index]
    operands += [swap(operand) for operand in operands]
    operands = [operand.reshape(-1, operand.shape[-1]) for operand in operands]
    return pl.pallas_call(
        pack_kernel,
        in_specs=[VMEM] * 6,
        out_specs=[VMEM] * 2,
        out_shape=[
            jax.ShapeDtypeStruct((2 * count, width + LANES), jnp.bfloat16),
            jax.ShapeDtypeStruct((count, width + LANES), jnp.bfloat16),
        ],
        compiler_params=pltpu.CompilerParams(vmem_limit_bytes=40 * 2**20),
        cost_estimate=pl.CostEstimate(
            flops=8 * count * width, bytes_accessed=10 * count * width, transcendentals=count
        ),
    )(*operands)


def own_kernel(*refs):
    both_ref, block_refs, (row_ref, *scratch) = refs[0], refs[1:-3], refs[-3:]
    (first, second), _ = best_pairs([both_ref], block_refs, False, *scratch)
    row_ref[...] = jnp.where(lax.axis_index("core") == 0, first, second)


def visit_kernel(visitors, arrays, first, *refs):
    block_refs = refs[visitors : visitors + arrays]
    row_ref, mine_ref, other_ref, *scratch = refs[visitors + arrays + 1 :]
    rows, cols = best_pairs(refs[:visitors], block_refs, True, *scratch)
    for v, best in enumerate(rows):
        row_ref[v : v + 1, :] = best
    for j, best in enumerate(cols):
        if first and j < 2:
            best = jnp.where(lax.axis_index("core") == 0, best, cols[1 - j])
        (mine_ref, other_ref)[j % 2][j // 2 : j // 2 + 1, :] = best


def best_pairs(visitor_refs, block_refs, homed, units, dots):
    width = units.shape[1]
    rows = visitor_refs[0].shape[0] // 2

    meta = []
    for v in range(2 * len(visitor_refs)):
        place, source = v * LANES, pl.ds(v % 2 * rows, rows)
        units[place : place + rows, :] = visitor_refs[v // 2][source, :width]
        tail = visitor_refs[v // 2][source, width:].astype(jnp.float32)
        if rows < LANES:
            units[place + rows : place + LANES, :] = jnp.zeros((LANES - rows, width), jnp.bfloat16)
            tail = jnp.concatenate([tail, jnp.zeros((LANES - rows, LANES), jnp.float32)], axis=0)
        turned = tail.T
        meta.append((turned[0:1], turned[1:2] * 256.0 + turned[2:3]))
    for k in range(0, width, CHUNK):
        left = jnp.concatenate([ref[:, k : k + CHUNK] for ref in block_refs], axis=0)
        part = lax.dot_general(
            left,
            units[:, k : k + CHUNK],
            (((1,), (1,)), ((), ())),
            preferred_element_type=jnp.float32,
        )
        dots[...] = part if k == 0 else dots[...] + part

    tails = jnp.concatenate([ref[:, width:] for ref in block_refs], axis=0).astype(jnp.float32)
    row_best = [jnp.full((1, LANES), -1.0, jnp.float32) for _ in meta]
    lane = lax.broadcasted_iota(jnp.int32, (rows, LANES), 1)
    col_all = jnp.full((rows, LANES), -1.0, jnp.float32)
    for j in range(dots.shape[0] // rows):
        tail = tails[j * rows : (j + 1) * rows]
        block_cluster, block_order = tail[:, 0:1], tail[:, 1:2] * 256.0 + tail[:, 2:3]
        col_best = jnp.full((rows, 1), -1.0, jnp.float32)
        for v, (cluster, order) in enumerate(meta):
            cosine = dots[j * rows : (j + 1) * rows, v * LANES : (v + 1) * LANES]
            same = (block_cluster == cluster) & (cluster > 0)
            seen = jnp.where(same & (block_order < order), cosine, -1.0)
            row_best[v] = jnp.maximum(row_best[v], jnp.max(seen, axis=0, keepdims=True))
            if homed:
                seen = jnp.where(same & (order < block_order), cosine, -1.0)
                col_best = jnp.maximum(col_best, jnp.max(seen, axis=1, keepdims=True))
        col_all = jnp.where(lane == j, col_best, col_all)
    if not homed:
        return row_best, None
    if rows < LANES:
        fill = jnp.full((LANES - rows, LANES), -1.0, jnp.float32)
        col_all = jnp.concatenate([col_all, fill], axis=0)
    turned = col_all.T
    return row_best, [turned[j : j + 1] for j in range(dots.shape[0] // rows)]


def call(kernel, operands, count, out_rows, total):
    width = operands[0].shape[1] - LANES
    return pl.pallas_call(
        kernel,
        in_specs=[VMEM] * len(operands),
        out_specs=[VMEM] * len(out_rows),
        out_shape=[jax.ShapeDtypeStruct((n, LANES), jnp.float32) for n in out_rows],
        scratch_shapes=[
            pltpu.VMEM((count * LANES, width), jnp.bfloat16),
            pltpu.VMEM((total, count * LANES), jnp.float32),
        ],
        compiler_params=pltpu.CompilerParams(vmem_limit_bytes=40 * 2**20),
        cost_estimate=pl.CostEstimate(
            flops=2 * total * count * LANES * width,
            bytes_accessed=2 * (total + count * LANES) * width,
            transcendentals=0,
        ),
    )(*operands)


def local(embeddings, cluster_ids, order_index):
    rows = embeddings.shape[0]
    groups, length = lax.axis_size("group"), lax.axis_size("z")
    z, core = lax.axis_index("z"), lax.axis_index("core")
    both, own = pack(embeddings, cluster_ids, order_index)

    routes = [ring_pairs(length, shift) for shift in range(1, length // 2 + 1)]
    trips = []
    for first in range(0, len(routes), 2):
        ways = enumerate(routes[first : first + 2])
        trips.append([(2 * a + way, 2 * b + way) for way, route in ways for a, b in route])
    visitors = [lax.ppermute(both, ("z", "core"), trip) for trip in trips]

    plane = gather_plane(own, groups)
    parts = [both]
    for s in range(1, groups):
        parts += [*plane[s], *(swap(part) for part in plane[s])]
    chunks, size = [[]], 0
    for part in parts:
        if size == CALL * rows:
            chunks, size = chunks + [[]], 0
        chunks[-1].append(part)
        size += part.shape[0]

    bests, answers = [], []
    for chunk in chunks:
        total = sum(part.shape[0] for part in chunk)
        bests += call(own_kernel, [both, *chunk], 2, [1], total)
    for index, chunk in enumerate(chunks):
        total = sum(part.shape[0] for part in chunk)
        kernel = functools.partial(visit_kernel, len(visitors), len(chunk), index == 0)
        count, half = 2 * len(visitors), total // rows // 2
        operands = [*visitors, *chunk, bests[index]]
        answers.append(call(kernel, operands, count, [count, half, half], total))
    home = functools.reduce(jnp.maximum, [answer[0] for answer in answers])
    for index, trip in enumerate(trips):
        part = home[2 * index : 2 * index + 2] if len(trips) > 1 else home
        back = lax.ppermute(part, ("z", "core"), [(b, a) for a, b in trip])
        for here, best in ((2 * z + core, back), (2 * z + (core ^ 1), swap(back))):
            sent = functools.reduce(jnp.logical_or, [here == a for a, _ in trip])
            bests.append(jnp.where(sent, jnp.where(core == 0, best[0:1], best[1:2]), -1.0))
    for index, (_, mine, other) in enumerate(answers):
        merged = jnp.maximum(mine, swap(other))
        for row in range(CALL // 2):
            s = index * CALL // 2 + row
            got = lax.ppermute(merged, "group", flip(groups, s)) if s else merged
            bests.append(got[row : row + 1])
    return functools.reduce(jnp.maximum, bests)[0, :rows]


def solution(mesh):
    groups, members = mesh.devices.shape
    fine = Mesh(mesh.devices.reshape(groups, members // 2, 2), AXES)
    placed = (P(AXES, None), P(AXES), P(AXES))
    return jax.shard_map(local, mesh=fine, in_specs=placed, out_specs=P(AXES), check_vma=False)
```

time: 85.7 us -> 61.3 us (0.72)
  between operations: 13.5 us -> 0.1 us
  matrix products: 10.4 us -> 0 us
  blocking collectives: 9.1 us -> 0 us
  waiting for transfers between devices: 27.5 us -> 34.9 us
  other arithmetic: 6.02 us -> 0.02 us
  Pallas kernels: 0 us -> 4.55 us
  local copies, waits for them, and re-layouts: 1.02 us -> 3.01 us
    ppermute x6 -> x18, waiting for transfers between devices: 23.7 us -> 34.9 us  [the longest x2 13.4 us: gather_plane(): blocks[s] = [lax.ppermute(block, 'group', flip(groups, s))]]
    dot_general x2 -> x0, matrix products: 10.4 us -> none  [maxima(): lax.dot_general(rows, cols, (((1,), (1,)), ((), ())), preferred_element_t...]
    all_gather x1 -> x0, blocking collectives: 9.1 us -> none  [local(): plane_meta = lax.all_gather(meta, ('group', 'core'), axis=0)]
    pallas_call x0 -> x3, Pallas kernels: none -> 4.55 us  [the longest x2 3.89 us: call(): pl.pallas_call(kernel, in_specs=[VMEM] * len(operands), out_specs=[VMEM]...]
    ppermute x6 -> x18, starting transfers between devices: 14.5 us -> 18.5 us  [the longest x2 4.44 us: gather_plane(): blocks[s] = [lax.ppermute(block, 'group', flip(groups, s))]]
    all_to_all x1 -> x0, starting transfers between devices: 3.26 us -> none  [local(): lax.all_to_all(col_best.reshape(-1, row_count), ('group', 'core'), split_...]
    all_gather x1 -> x0, waiting for transfers between devices: 3.11 us -> none  [local(): plane = lax.all_gather(embeddings, ('group', 'core'), axis=0, tiled=True)]
    unnamed x2 -> x6, local copies, waits for them, and re-layouts: 0.01 us -> 2.44 us
  transfers between devices with their start and end apart: 8 -> 18, of which waited for: 3 -> 8; matrix products, arithmetic and copies ran while one was open for 11% -> 0% of each run, Pallas kernels for 0% -> 3%
where the time goes in v9:
time: 61.3 us; the launch traced here: 61.1 us
  waiting for transfers between devices  34.9 us (57%)
  starting transfers between devices  18.5 us (30%)
  Pallas kernels  4.55 us (7%)
  local copies, waits for them, and re-layouts  3.01 us (5%)
    ppermute x2, waiting for transfers between devices, gather_plane(): blocks[s] = [lax.ppermute(block, 'group', flip(groups, s))]  13.4 us
    ppermute x1, waiting for transfers between devices, gather_plane(): lax.ppermute(top, 'group', flip(groups, high))  7.04 us
    ppermute x1, waiting for transfers between devices, local(): visitors = [lax.ppermute(both, ('z', 'core'), trip) for trip in trips]  6.53 us
    ppermute x2, starting transfers between devices, gather_plane(): blocks[s] = [lax.ppermute(block, 'group', flip(groups, s))]  4.44 us
    ppermute x9, waiting for transfers between devices, swap(): return lax.ppermute(block, 'core', flip(2, 1))  4.3 us
    pallas_call x2, Pallas kernels, call(): pl.pallas_call(kernel, in_specs=[VMEM] * len(operands), out_specs=[VMEM]...  3.89 us
    ppermute x3, starting transfers between devices, local(): got = lax.ppermute(merged, 'group', flip(groups, s)) if s else merged  3.55 us
    ppermute x1, starting transfers between devices, local(): visitors = [lax.ppermute(both, ('z', 'core'), trip) for trip in trips]  3.47 us
  transfers between devices with their start and end apart: 18, of which 8 were waited for; matrix products, arithmetic and copies ran while one was open for 0% of the time, Pallas kernels for 3%

profile of v9, /device:TPU:0, one launch (start us, length us, event | category | flops | bytes accessed | tf_op | source)
XLA Modules:
  0.0 61.1 jit_solution(16132623176158939457)
XLA Ops:
  1.0 1.6 %collective-permute-done.1 = s32[96]{0:T(128)S(1)} collective-permute-done((s32[96]{0:T(128)}, s32[96]{0:T(128)S(1)}, u32[]{:S(2)}, u32[]{:S(2)}) %collective-permute-start.1) | collective-permute-done | bytes 416 | tf_op jit(solution)/shard_map/ppermute | solution.py:53
  2.6 1.1 %copy-done = bf16[96,4096]{1,0:T(8,128)(2,1)S(1)} copy-done((bf16[96,4096]{1,0:T(8,128)(2,1)S(1)}, bf16[96,4096]{1,0:T(8,128)(2,1)}, u32[]{:S(2)}) %copy-start) | copy-done | bytes 786456
  3.7 0.7 %copy-done.1 = s32[96]{0:T(128)S(1)} copy-done((s32[96]{0:T(128)S(1)}, s32[96]{0:T(128)}, u32[]{:S(2)}) %copy-start.1) | copy-done | bytes 408
  4.4 0.7 %copy-done.2 = s32[96]{0:T(128)S(1)} copy-done((s32[96]{0:T(128)S(1)}, s32[96]{0:T(128)}, u32[]{:S(2)}) %copy-start.2) | copy-done | bytes 408
  5.0 0.7 %shard_map.37 = (bf16[192,4224]{1,0:T(8,128)(2,1)S(1)}, bf16[96,4224]{1,0:T(8,128)(2,1)S(1)}) custom-call(bf16[96,4096]{1,0:T(8,128)(2,1)S(1)} %copy-done, s32[1,96]{1,0:T(1,128)S(1)} %bitcast.6, s32[1,96]{1,0:T(1,128)S(1)} %bitcast.7, bf16[96,4096]{1,0:T(8,128)(2,1)S(1)} %collective-permute-done.refs_3_, s32[1,96]{1,0:T(1,128)S(1)} %bitcast.8, ...), custom_call_target="tpu_custom_call" | custom-call | flops 3145728 | bytes 3932160 | tf_op jit(solution)/shard_map/pallas_call | solution.py:91
  5.7 2.9 %collective-permute-start.3 = (bf16[96,4224]{1,0:T(8,128)(2,1)S(1)}, bf16[96,4224]{1,0:T(8,128)(2,1)S(1)}, u32[]{:S(2)}, u32[]{:S(2)}) collective-permute-start(bf16[96,4224]{1,0:T(8,128)(2,1)S(1)} %get-tuple-element.11), channel_id=1, source_target_pairs={{0,8},{8,0},{16,24},{24,16},{1,9},{9,1},{17,25},{25,17},{2,10},{10... | collective-permute-start | bytes 2433032 | tf_op jit(solution)/shard_map/ppermute | solution.py:40
  8.6 1.5 %collective-permute-start.5 = (bf16[96,4224]{1,0:T(8,128)(2,1)S(1)}, bf16[96,4224]{1,0:T(8,128)(2,1)S(1)}, u32[]{:S(2)}, u32[]{:S(2)}) collective-permute-start(bf16[96,4224]{1,0:T(8,128)(2,1)S(1)} %get-tuple-element.11), channel_id=1, source_target_pairs={{0,16},{8,24},{16,0},{24,8},{1,17},{9,25},{17,1},{25,9},{2,18},{10... | collective-permute-start | bytes 2433032 | tf_op jit(solution)/shard_map/ppermute | solution.py:40
  10.1 3.5 %collective-permute-start.11 = (bf16[192,4224]{1,0:T(8,128)(2,1)S(1)}, bf16[192,4224]{1,0:T(8,128)(2,1)S(1)}, u32[]{:S(2)}, u32[]{:S(2)}) collective-permute-start(bf16[192,4224]{1,0:T(8,128)(2,1)S(1)} %get-tuple-element.10.refs_0_.refs_1_), channel_id=1, source_target_pairs={{0,2},{2,4},{4,6},{6,0},{1,5},{7,3},{8,10},{10,12},{12,14},{14,8},... | collective-permute-start | bytes 4866056 | tf_op jit(solution)/shard_map/ppermute | solution.py:205
  13.6 13.4 %collective-permute-done.3.refs_2_ = bf16[96,4224]{1,0:T(8,128)(2,1)S(1)} collective-permute-done((bf16[96,4224]{1,0:T(8,128)(2,1)S(1)}, bf16[96,4224]{1,0:T(8,128)(2,1)S(1)}, u32[]{:S(2)}, u32[]{:S(2)}) %collective-permute-start.3) | collective-permute-done | bytes 811040 | tf_op jit(solution)/shard_map/ppermute | solution.py:40
  27.0 1.8 %collective-permute-start.7 = (bf16[48,4224]{1,0:T(8,128)(2,1)S(1)}, bf16[48,4224]{1,0:T(8,128)(2,1)S(1)}, u32[]{:S(2)}, u32[]{:S(2)}) collective-permute-start(bf16[48,4224]{1,0:T(8,128)(2,1)S(1)} %slice.44), channel_id=1, source_target_pairs={{0,16},{8,24},{16,0},{24,8},{1,17},{9,25},{17,1},{25,9},{2,18},{10... | collective-permute-start | bytes 1216520 | tf_op jit(solution)/shard_map/ppermute | solution.py:46
  29.4 1.6 %collective-permute-start.8 = (bf16[48,4224]{1,0:T(8,128)(2,1)S(1)}, bf16[48,4224]{1,0:T(8,128)(2,1)S(1)}, u32[]{:S(2)}, u32[]{:S(2)}) collective-permute-start(bf16[48,4224]{1,0:T(8,128)(2,1)S(1)} %slice.45), channel_id=1, source_target_pairs={{0,8},{8,0},{16,24},{24,16},{1,9},{9,1},{17,25},{25,17},{2,10},{10... | collective-permute-start | bytes 1216520 | tf_op jit(solution)/shard_map/ppermute | solution.py:47
  31.0 7.0 %collective-permute-done.7.refs_6_ = bf16[48,4224]{1,0:T(8,128)(2,1)S(1)} collective-permute-done((bf16[48,4224]{1,0:T(8,128)(2,1)S(1)}, bf16[48,4224]{1,0:T(8,128)(2,1)S(1)}, u32[]{:S(2)}, u32[]{:S(2)}) %collective-permute-start.7) | collective-permute-done | bytes 405536 | tf_op jit(solution)/shard_map/ppermute | solution.py:46
  38.0 2.8 %collective-permute-done.8.refs_7_ = bf16[48,4224]{1,0:T(8,128)(2,1)S(1)} collective-permute-done((bf16[48,4224]{1,0:T(8,128)(2,1)S(1)}, bf16[48,4224]{1,0:T(8,128)(2,1)S(1)}, u32[]{:S(2)}, u32[]{:S(2)}) %collective-permute-start.8) | collective-permute-done | bytes 405536 | tf_op jit(solution)/shard_map/ppermute | solution.py:47
  40.8 1.7 %collective-permute-done.10.refs_9_ = bf16[48,4224]{1,0:T(8,128)(2,1)S(1)} collective-permute-done((bf16[48,4224]{1,0:T(8,128)(2,1)S(1)}, bf16[48,4224]{1,0:T(8,128)(2,1)S(1)}, u32[]{:S(2)}, u32[]{:S(2)}) %collective-permute-start.10) | collective-permute-done | bytes 405536 | tf_op jit(solution)/shard_map/ppermute | solution.py:53
  42.5 1.8 %shard_map.38.refs_10_ = f32[1,128]{1,0:T(1,128)S(1)} custom-call(bf16[192,4224]{1,0:T(8,128)(2,1)S(1)} %get-tuple-element.10.refs_0_.refs_1_, bf16[192,4224]{1,0:T(8,128)(2,1)S(1)} %get-tuple-element.10.refs_0_.refs_1_, bf16[96,4224]{1,0:T(8,128)(2,1)S(1)} %collective-permute-done.3.refs_2_, bf16[96,4224]{1,0:T(8,128)(2,1)S(1)} %collective-permute-done.4.refs_3_, ...), custom_call_target="tpu_custom_call" | custom-call | flops 1610612736 | bytes 8388608 | tf_op jit(solution)/shard_map/pallas_call | solution.py:176
  44.3 6.5 %collective-permute-done.11.refs_0_ = bf16[192,4224]{1,0:T(8,128)(2,1)S(1)} collective-permute-done((bf16[192,4224]{1,0:T(8,128)(2,1)S(1)}, bf16[192,4224]{1,0:T(8,128)(2,1)S(1)}, u32[]{:S(2)}, u32[]{:S(2)}) %collective-permute-start.11) | collective-permute-done | bytes 1622048 | tf_op jit(solution)/shard_map/ppermute | solution.py:205
  50.9 2.1 %shard_map.39 = (f32[2,128]{1,0:T(2,128)S(1)}, f32[4,128]{1,0:T(4,128)S(1)}, f32[4,128]{1,0:T(4,128)S(1)}) custom-call(bf16[192,4224]{1,0:T(8,128)(2,1)S(1)} %collective-permute-done.11.refs_0_, bf16[192,4224]{1,0:T(8,128)(2,1)S(1)} %get-tuple-element.10.refs_0_.refs_1_, bf16[96,4224]{1,0:T(8,128)(2,1)S(1)} %collective-permute-done.3.refs_2_, ...), custom_call_target="tpu_custom_call" | custom-call | flops 1610612736 | bytes 8388608 | tf_op jit(solution)/shard_map/pallas_call | solution.py:176
  53.0 1.9 %collective-permute-start.12 = (f32[2,128]{1,0:T(2,128)S(1)}, f32[2,128]{1,0:T(2,128)S(1)}, u32[]{:S(2)}, u32[]{:S(2)}) collective-permute-start(f32[2,128]{1,0:T(2,128)S(1)} %get-tuple-element.12), channel_id=1, source_target_pairs={{2,0},{4,2},{6,4},{0,6},{5,1},{3,7},{10,8},{12,10},{14,12},{8,14},... | collective-permute-start | bytes 3080 | tf_op jit(solution)/shard_map/ppermute | solution.py:231
  54.9 0.5 collective-permute-start.17
  55.5 1.5 %collective-permute-start.16 = (f32[4,128]{1,0:T(4,128)S(1)}, f32[4,128]{1,0:T(4,128)S(1)}, u32[]{:S(2)}, u32[]{:S(2)}) collective-permute-start(f32[4,128]{1,0:T(4,128)S(1)} %max.23), channel_id=1, source_target_pairs={{0,16},{8,24},{16,0},{24,8},{1,17},{9,25},{17,1},{25,9},{2,18},{10... | collective-permute-start | bytes 6152 | tf_op jit(solution)/shard_map/ppermute | solution.py:239
  57.0 1.5 %collective-permute-start.15 = (f32[4,128]{1,0:T(4,128)S(1)}, f32[4,128]{1,0:T(4,128)S(1)}, u32[]{:S(2)}, u32[]{:S(2)}) collective-permute-start(f32[4,128]{1,0:T(4,128)S(1)} %max.23), channel_id=1, source_target_pairs={{0,8},{8,0},{16,24},{24,16},{1,9},{9,1},{17,25},{25,17},{2,10},{10... | collective-permute-start | bytes 6152 | tf_op jit(solution)/shard_map/ppermute | solution.py:239
  58.7 1.0 %collective-permute-done.13 = f32[2,128]{1,0:T(2,128)S(1)} collective-permute-done((f32[2,128]{1,0:T(2,128)S(1)}, f32[2,128]{1,0:T(2,128)S(1)}, u32[]{:S(2)}, u32[]{:S(2)}) %collective-permute-start.13) | collective-permute-done | bytes 1056 | tf_op jit(solution)/shard_map/ppermute | solution.py:53
  59.6 0.9 %collective-permute-done.15 = f32[4,128]{1,0:T(4,128)S(1)} collective-permute-done((f32[4,128]{1,0:T(4,128)S(1)}, f32[4,128]{1,0:T(4,128)S(1)}, u32[]{:S(2)}, u32[]{:S(2)}) %collective-permute-start.15) | collective-permute-done | bytes 2080 | tf_op jit(solution)/shard_map/ppermute | solution.py:239
  60.6 0.5 slice_bitcast_fusion
  (26 shorter events, 1.8 us)
Async XLA Ops:
  0.0 2.6 %collective-permute-start = (bf16[96,4096]{1,0:T(8,128)(2,1)}, bf16[96,4096]{1,0:T(8,128)(2,1)S(1)}, u32[]{:S(2)}, u32[]{:S(2)}) collective-permute-start(bf16[96,4096]{1,0:T(8,128)(2,1)} %refs_0_.1), channel_id=1, source_target_pairs={{0,1},{1,0},{2,3},{3,2},{4,5},{5,4},{6,7},{7,6},{8,9},{9,8},{10,11... | collective-permute-start | bytes 2359304 | tf_op jit(solution)/shard_map/ppermute | solution.py:53
  0.5 2.1 %collective-permute-start.1 = (s32[96]{0:T(128)}, s32[96]{0:T(128)S(1)}, u32[]{:S(2)}, u32[]{:S(2)}) collective-permute-start(s32[96]{0:T(128)} %param.4), channel_id=1, source_target_pairs={{0,1},{1,0},{2,3},{3,2},{4,5},{5,4},{6,7},{7,6},{8,9},{9,8},{10,11... | collective-permute-start | bytes 1160 | tf_op jit(solution)/shard_map/ppermute | solution.py:53
  0.5 2.1 %collective-permute-start.2 = (s32[96]{0:T(128)}, s32[96]{0:T(128)S(1)}, u32[]{:S(2)}, u32[]{:S(2)}) collective-permute-start(s32[96]{0:T(128)} %param.5), channel_id=1, source_target_pairs={{0,1},{1,0},{2,3},{3,2},{4,5},{5,4},{6,7},{7,6},{8,9},{9,8},{10,11... | collective-permute-start | bytes 1160 | tf_op jit(solution)/shard_map/ppermute | solution.py:53
  2.6 1.1 %copy-start = (bf16[96,4096]{1,0:T(8,128)(2,1)S(1)}, bf16[96,4096]{1,0:T(8,128)(2,1)}, u32[]{:S(2)}) copy-start(bf16[96,4096]{1,0:T(8,128)(2,1)} %refs_0_.1) | copy-start | bytes 2359300
  3.7 0.7 %copy-start.1 = (s32[96]{0:T(128)S(1)}, s32[96]{0:T(128)}, u32[]{:S(2)}) copy-start(s32[96]{0:T(128)} %param.4) | copy-start | bytes 1156
  4.4 0.7 %copy-start.2 = (s32[96]{0:T(128)S(1)}, s32[96]{0:T(128)}, u32[]{:S(2)}) copy-start(s32[96]{0:T(128)} %param.5) | copy-start | bytes 1156
  5.7 21.3 %collective-permute-start.3 = (bf16[96,4224]{1,0:T(8,128)(2,1)S(1)}, bf16[96,4224]{1,0:T(8,128)(2,1)S(1)}, u32[]{:S(2)}, u32[]{:S(2)}) collective-permute-start(bf16[96,4224]{1,0:T(8,128)(2,1)S(1)} %get-tuple-element.11), channel_id=1, source_target_pairs={{0,8},{8,0},{16,24},{24,16},{1,9},{9,1},{17,25},{25,17},{2,10},{10... | collective-permute-start | bytes 2433032 | tf_op jit(solution)/shard_map/ppermute | solution.py:40
  8.6 20.2 %collective-permute-start.5 = (bf16[96,4224]{1,0:T(8,128)(2,1)S(1)}, bf16[96,4224]{1,0:T(8,128)(2,1)S(1)}, u32[]{:S(2)}, u32[]{:S(2)}) collective-permute-start(bf16[96,4224]{1,0:T(8,128)(2,1)S(1)} %get-tuple-element.11), channel_id=1, source_target_pairs={{0,16},{8,24},{16,0},{24,8},{1,17},{9,25},{17,1},{25,9},{2,18},{10... | collective-permute-start | bytes 2433032 | tf_op jit(solution)/shard_map/ppermute | solution.py:40
  10.1 40.7 %collective-permute-start.11 = (bf16[192,4224]{1,0:T(8,128)(2,1)S(1)}, bf16[192,4224]{1,0:T(8,128)(2,1)S(1)}, u32[]{:S(2)}, u32[]{:S(2)}) collective-permute-start(bf16[192,4224]{1,0:T(8,128)(2,1)S(1)} %get-tuple-element.10.refs_0_.refs_1_), channel_id=1, source_target_pairs={{0,2},{2,4},{4,6},{6,0},{1,5},{7,3},{8,10},{10,12},{12,14},{14,8},... | collective-permute-start | bytes 4866056 | tf_op jit(solution)/shard_map/ppermute | solution.py:205
  27.0 11.0 %collective-permute-start.7 = (bf16[48,4224]{1,0:T(8,128)(2,1)S(1)}, bf16[48,4224]{1,0:T(8,128)(2,1)S(1)}, u32[]{:S(2)}, u32[]{:S(2)}) collective-permute-start(bf16[48,4224]{1,0:T(8,128)(2,1)S(1)} %slice.44), channel_id=1, source_target_pairs={{0,16},{8,24},{16,0},{24,8},{1,17},{9,25},{17,1},{25,9},{2,18},{10... | collective-permute-start | bytes 1216520 | tf_op jit(solution)/shard_map/ppermute | solution.py:46
  28.9 11.9 %collective-permute-start.4 = (bf16[96,4224]{1,0:T(8,128)(2,1)S(1)}, bf16[96,4224]{1,0:T(8,128)(2,1)S(1)}, u32[]{:S(2)}, u32[]{:S(2)}) collective-permute-start(bf16[96,4224]{1,0:T(8,128)(2,1)S(1)} %collective-permute-done.3.refs_2_), channel_id=1, source_target_pairs={{0,1},{1,0},{2,3},{3,2},{4,5},{5,4},{6,7},{7,6},{8,9},{9,8},{10,11... | collective-permute-start | bytes 2433032 | tf_op jit(solution)/shard_map/ppermute | solution.py:53
  28.9 11.9 %collective-permute-start.6 = (bf16[96,4224]{1,0:T(8,128)(2,1)S(1)}, bf16[96,4224]{1,0:T(8,128)(2,1)S(1)}, u32[]{:S(2)}, u32[]{:S(2)}) collective-permute-start(bf16[96,4224]{1,0:T(8,128)(2,1)S(1)} %collective-permute-done.5.refs_4_), channel_id=1, source_target_pairs={{0,1},{1,0},{2,3},{3,2},{4,5},{5,4},{6,7},{7,6},{8,9},{9,8},{10,11... | collective-permute-start | bytes 2433032 | tf_op jit(solution)/shard_map/ppermute | solution.py:53
  29.4 11.4 %collective-permute-start.8 = (bf16[48,4224]{1,0:T(8,128)(2,1)S(1)}, bf16[48,4224]{1,0:T(8,128)(2,1)S(1)}, u32[]{:S(2)}, u32[]{:S(2)}) collective-permute-start(bf16[48,4224]{1,0:T(8,128)(2,1)S(1)} %slice.45), channel_id=1, source_target_pairs={{0,8},{8,0},{16,24},{24,16},{1,9},{9,1},{17,25},{25,17},{2,10},{10... | collective-permute-start | bytes 1216520 | tf_op jit(solution)/shard_map/ppermute | solution.py:47
  38.0 2.8 %collective-permute-start.9 = (bf16[48,4224]{1,0:T(8,128)(2,1)S(1)}, bf16[48,4224]{1,0:T(8,128)(2,1)S(1)}, u32[]{:S(2)}, u32[]{:S(2)}) collective-permute-start(bf16[48,4224]{1,0:T(8,128)(2,1)S(1)} %collective-permute-done.7.refs_6_), channel_id=1, source_target_pairs={{0,1},{1,0},{2,3},{3,2},{4,5},{5,4},{6,7},{7,6},{8,9},{9,8},{10,11... | collective-permute-start | bytes 1216520 | tf_op jit(solution)/shard_map/ppermute | solution.py:53
  40.8 1.7 %collective-permute-start.10 = (bf16[48,4224]{1,0:T(8,128)(2,1)S(1)}, bf16[48,4224]{1,0:T(8,128)(2,1)S(1)}, u32[]{:S(2)}, u32[]{:S(2)}) collective-permute-start(bf16[48,4224]{1,0:T(8,128)(2,1)S(1)} %collective-permute-done.8.refs_7_), channel_id=1, source_target_pairs={{0,1},{1,0},{2,3},{3,2},{4,5},{5,4},{6,7},{7,6},{8,9},{9,8},{10,11... | collective-permute-start | bytes 1216520 | tf_op jit(solution)/shard_map/ppermute | solution.py:53
  52.9 2.0 %collective-permute-start.14 = (f32[4,128]{1,0:T(4,128)S(1)}, f32[4,128]{1,0:T(4,128)S(1)}, u32[]{:S(2)}, u32[]{:S(2)}) collective-permute-start(f32[4,128]{1,0:T(4,128)S(1)} %get-tuple-element.14), channel_id=1, source_target_pairs={{0,1},{1,0},{2,3},{3,2},{4,5},{5,4},{6,7},{7,6},{8,9},{9,8},{10,11... | collective-permute-start | bytes 6152 | tf_op jit(solution)/shard_map/ppermute | solution.py:53
  53.0 5.5 %collective-permute-start.12 = (f32[2,128]{1,0:T(2,128)S(1)}, f32[2,128]{1,0:T(2,128)S(1)}, u32[]{:S(2)}, u32[]{:S(2)}) collective-permute-start(f32[2,128]{1,0:T(2,128)S(1)} %get-tuple-element.12), channel_id=1, source_target_pairs={{2,0},{4,2},{6,4},{0,6},{5,1},{3,7},{10,8},{12,10},{14,12},{8,14},... | collective-permute-start | bytes 3080 | tf_op jit(solution)/shard_map/ppermute | solution.py:231
  54.9 4.7 %collective-permute-start.17 = (f32[4,128]{1,0:T(4,128)S(1)}, f32[4,128]{1,0:T(4,128)S(1)}, u32[]{:S(2)}, u32[]{:S(2)}) collective-permute-start(f32[4,128]{1,0:T(4,128)S(1)} %max.23), channel_id=1, source_target_pairs={{0,24},{8,16},{16,8},{24,0},{1,25},{9,17},{17,9},{25,1},{2,26},{10... | collective-permute-start | bytes 6152 | tf_op jit(solution)/shard_map/ppermute | solution.py:239
  55.5 4.2 %collective-permute-start.16 = (f32[4,128]{1,0:T(4,128)S(1)}, f32[4,128]{1,0:T(4,128)S(1)}, u32[]{:S(2)}, u32[]{:S(2)}) collective-permute-start(f32[4,128]{1,0:T(4,128)S(1)} %max.23), channel_id=1, source_target_pairs={{0,16},{8,24},{16,0},{24,8},{1,17},{9,25},{17,1},{25,9},{2,18},{10... | collective-permute-start | bytes 6152 | tf_op jit(solution)/shard_map/ppermute | solution.py:239
  57.0 3.6 %collective-permute-start.15 = (f32[4,128]{1,0:T(4,128)S(1)}, f32[4,128]{1,0:T(4,128)S(1)}, u32[]{:S(2)}, u32[]{:S(2)}) collective-permute-start(f32[4,128]{1,0:T(4,128)S(1)} %max.23), channel_id=1, source_target_pairs={{0,8},{8,0},{16,24},{24,16},{1,9},{9,1},{17,25},{25,17},{2,10},{10... | collective-permute-start | bytes 6152 | tf_op jit(solution)/shard_map/ppermute | solution.py:239
  58.5 1.1 %collective-permute-start.13 = (f32[2,128]{1,0:T(2,128)S(1)}, f32[2,128]{1,0:T(2,128)S(1)}, u32[]{:S(2)}, u32[]{:S(2)}) collective-permute-start(f32[2,128]{1,0:T(2,128)S(1)} %collective-permute-done.12), channel_id=1, source_target_pairs={{0,1},{1,0},{2,3},{3,2},{4,5},{5,4},{6,7},{7,6},{8,9},{9,8},{10,11... | collective-permute-start | bytes 3080 | tf_op jit(solution)/shard_map/ppermute | solution.py:53

commit v10 on v9

--- a/solution.py
+++ b/solution.py
@@ -11,6 +11,7 @@
 LANES = 128
 CHUNK = 512
 CALL = 8
+PARTS = 3
 VMEM = pl.BlockSpec(memory_space=pltpu.VMEM)
 
 
@@ -53,88 +54,110 @@
     return lax.ppermute(block, "core", flip(2, 1))
 
 
-def pack_kernel(*refs):
-    both_ref, own_ref = refs[6:]
-    rows, width = refs[0].shape
-    core = lax.axis_index("core")
-    for index, (rows_ref, cluster_ref, order_ref) in enumerate((refs[:3], refs[3:6])):
-        unit = unit_rows(rows_ref[...])
-        meta = jnp.concatenate(
-            [
-                cluster_ref[...].astype(jnp.float32) + 1.0,
-                order_ref[...].astype(jnp.float32),
-                jnp.zeros((6, rows), jnp.float32),
-            ],
-            axis=0,
+def pack_kernel(rows_ref, cluster_ref, order_ref, block_ref, raw, ids, arrived):
+    rows, width = raw.shape
+    step = rows // PARTS
+    parts = [pl.ds(index * step, step) for index in range(PARTS)]
+    copies = [
+        pltpu.make_async_copy(cluster_ref, ids.at[0], arrived.at[PARTS]),
+        pltpu.make_async_copy(order_ref, ids.at[1], arrived.at[PARTS + 1]),
+    ]
+    for index, part in enumerate(parts):
+        copies.append(
+            pltpu.make_async_copy(rows_ref.at[part], raw.at[part], arrived.at[index])
         )
-        if rows < LANES:
-            meta = jnp.concatenate([meta, jnp.zeros((8, LANES - rows), jnp.float32)], axis=1)
-        turned = meta.T[:rows]
-        cluster, order = turned[:, 0:1], turned[:, 1:2]
-        high = jnp.floor(order / 256.0)
-        lane = lax.broadcasted_iota(jnp.int32, (rows, LANES), 1)
-        tail = jnp.where(lane == 0, cluster, jnp.where(lane == 1, high, order - 256.0 * high))
-        tail = jnp.where(lane < 3, tail, 0.0).astype(jnp.bfloat16)
-        place = pl.ds(pl.multiple_of((core ^ index) * rows, 16), rows)
-        both_ref[place, :width] = unit
-        both_ref[place, width:] = tail
-        if index == 0:
-            own_ref[:, :width] = unit
-            own_ref[:, width:] = tail
+    for copy in copies:
+        copy.start()
+    for copy in copies[:2]:
+        copy.wait()
+    meta = jnp.concatenate(
+        [
+            ids[0].astype(jnp.float32) + 1.0,
+            ids[1].astype(jnp.float32),
+            jnp.zeros((6, rows), jnp.float32),
+        ],
+        axis=0,
+    )
+    if rows < LANES:
+        meta = jnp.concatenate([meta, jnp.zeros((8, LANES - rows), jnp.float32)], axis=1)
+    turned = meta.T[:rows]
+    cluster, order = turned[:, 0:1], turned[:, 1:2]
+    high = jnp.floor(order / 256.0)
+    lane = lax.broadcasted_iota(jnp.int32, (rows, LANES), 1)
+    tail = jnp.where(lane == 0, cluster, jnp.where(lane == 1, high, order - 256.0 * high))
+    block_ref[:, width:] = jnp.where(lane < 3, tail, 0.0).astype(jnp.bfloat16)
+    for part, copy in zip(parts, copies[2:]):
+        copy.wait()
+        block_ref[part, :width] = unit_rows(raw[part])
 
 
 def pack(rows, cluster_ids, order_index):
     count, width = rows.shape
-    operands = [rows, cluster_ids, order_index]
-    operands += [swap(operand) for operand in operands]
-    operands = [operand.reshape(-1, operand.shape[-1]) for operand in operands]
     return pl.pallas_call(
         pack_kernel,
-        in_specs=[VMEM] * 6,
-        out_specs=[VMEM] * 2,
-        out_shape=[
-            jax.ShapeDtypeStruct((2 * count, width + LANES), jnp.bfloat16),
-            jax.ShapeDtypeStruct((count, width + LANES), jnp.bfloat16),
+        in_specs=[pl.BlockSpec(memory_space=pl.ANY)] * 3,
+        out_specs=VMEM,
+        out_shape=jax.ShapeDtypeStruct((count, width + LANES), jnp.bfloat16),
+        scratch_shapes=[
+            pltpu.VMEM((count, width), jnp.bfloat16),
+            pltpu.VMEM((2, 1, count), jnp.int32),
+            pltpu.SemaphoreType.DMA((PARTS + 2,)),
         ],
-        compiler_params=pltpu.CompilerParams(vmem_limit_bytes=40 * 2**20),
         cost_estimate=pl.CostEstimate(
-            flops=8 * count * width, bytes_accessed=10 * count * width, transcendentals=count
+            flops=4 * count * width, bytes_accessed=4 * count * width, transcendentals=count
         ),
-    )(*operands)
+    )(rows, cluster_ids.reshape(1, count), order_index.reshape(1, count))
+
+
+def pair_kernel(own_ref, other_ref, both_ref):
+    rows = own_ref.shape[0]
+    core = lax.axis_index("core")
+    both_ref[pl.ds(pl.multiple_of(core * rows, 16), rows), :] = own_ref[...]
+    both_ref[pl.ds(pl.multiple_of((core ^ 1) * rows, 16), rows), :] = other_ref[...]
+
+
+def pair(own, other):
+    rows, width = own.shape
+    return pl.pallas_call(
+        pair_kernel,
+        in_specs=[VMEM] * 2,
+        out_specs=VMEM,
+        out_shape=jax.ShapeDtypeStruct((2 * rows, width), own.dtype),
+        cost_estimate=pl.CostEstimate(flops=0, bytes_accessed=8 * rows * width, transcendentals=0),
+    )(own, other)
 
 
 def own_kernel(*refs):
-    both_ref, block_refs, (row_ref, *scratch) = refs[0], refs[1:-3], refs[-3:]
-    (first, second), _ = best_pairs([both_ref], block_refs, False, *scratch)
-    row_ref[...] = jnp.where(lax.axis_index("core") == 0, first, second)
-
-
-def visit_kernel(visitors, arrays, first, *refs):
+    row_ref, *scratch = refs[-3:]
+    best, _ = best_of(refs[:1], refs[1:-3], refs[0].shape[0], False, *scratch)
+    row_ref[...] = best[0]
+
+
+def visit_kernel(visitors, arrays, *refs):
     block_refs = refs[visitors : visitors + arrays]
     row_ref, mine_ref, other_ref, *scratch = refs[visitors + arrays + 1 :]
-    rows, cols = best_pairs(refs[:visitors], block_refs, True, *scratch)
-    for v, best in enumerate(rows):
+    bests, cols = best_of(refs[:visitors], block_refs, refs[0].shape[0] // 2, True, *scratch)
+    for v, best in enumerate(bests):
         row_ref[v : v + 1, :] = best
     for j, best in enumerate(cols):
-        if first and j < 2:
-            best = jnp.where(lax.axis_index("core") == 0, best, cols[1 - j])
         (mine_ref, other_ref)[j % 2][j // 2 : j // 2 + 1, :] = best
 
 
-def best_pairs(visitor_refs, block_refs, homed, units, dots):
+def best_of(visitor_refs, block_refs, rows, homed, units, dots):
     width = units.shape[1]
-    rows = visitor_refs[0].shape[0] // 2
 
     meta = []
-    for v in range(2 * len(visitor_refs)):
-        place, source = v * LANES, pl.ds(v % 2 * rows, rows)
-        units[place : place + rows, :] = visitor_refs[v // 2][source, :width]
-        tail = visitor_refs[v // 2][source, width:].astype(jnp.float32)
-        if rows < LANES:
-            units[place + rows : place + LANES, :] = jnp.zeros((LANES - rows, width), jnp.bfloat16)
-            tail = jnp.concatenate([tail, jnp.zeros((LANES - rows, LANES), jnp.float32)], axis=0)
-        turned = tail.T
-        meta.append((turned[0:1], turned[1:2] * 256.0 + turned[2:3]))
+    for ref in visitor_refs:
+        for source in range(0, ref.shape[0], rows):
+            place, source = len(meta) * LANES, pl.ds(source, rows)
+            units[place : place + rows, :] = ref[source, :width]
+            tail = ref[source, width:].astype(jnp.float32)
+            if rows < LANES:
+                spare = LANES - rows
+                units[place + rows : place + LANES, :] = jnp.zeros((spare, width), jnp.bfloat16)
+                tail = jnp.concatenate([tail, jnp.zeros((spare, LANES), jnp.float32)], axis=0)
+            turned = tail.T
+            meta.append((turned[0:1], turned[1:2] * 256.0 + turned[2:3]))
     for k in range(0, width, CHUNK):
         left = jnp.concatenate([ref[:, k : k + CHUNK] for ref in block_refs], axis=0)
         part = lax.dot_general(
@@ -195,7 +218,9 @@
     rows = embeddings.shape[0]
     groups, length = lax.axis_size("group"), lax.axis_size("z")
     z, core = lax.axis_index("z"), lax.axis_index("core")
-    both, own = pack(embeddings, cluster_ids, order_index)
+    own = pack(embeddings, cluster_ids, order_index)
+    other = swap(own)
+    both = pair(own, other)
 
     routes = [ring_pairs(length, shift) for shift in range(1, length // 2 + 1)]
     trips = []
@@ -205,7 +230,7 @@
     visitors = [lax.ppermute(both, ("z", "core"), trip) for trip in trips]
 
     plane = gather_plane(own, groups)
-    parts = [both]
+    parts = [own, other]
     for s in range(1, groups):
         parts += [*plane[s], *(swap(part) for part in plane[s])]
     chunks, size = [[]], 0
@@ -218,10 +243,10 @@
     bests, answers = [], []
     for chunk in chunks:
         total = sum(part.shape[0] for part in chunk)
-        bests += call(own_kernel, [both, *chunk], 2, [1], total)
+        bests += call(own_kernel, [own, *chunk], 1, [1], total)
     for index, chunk in enumerate(chunks):
         total = sum(part.shape[0] for part in chunk)
-        kernel = functools.partial(visit_kernel, len(visitors), len(chunk), index == 0)
+        kernel = functools.partial(visit_kernel, len(visitors), len(chunk))
         count, half = 2 * len(visitors), total // rows // 2
         operands = [*visitors, *chunk, bests[index]]
         answers.append(call(kernel, operands, count, [count, half, half], total))

time: 61.3 us -> 63.1 us (1.029)
  Pallas kernels: 4.55 us -> 8.96 us
  local copies, waits for them, and re-layouts: 3.01 us -> 1.48 us
  starting transfers between devices: 18.5 us -> 17.8 us
    pallas_call x1 -> x2, Pallas kernels: 0.66 us -> 5.09 us  [the longest x1 2.68 us: pair(): pl.pallas_call(pair_kernel, in_specs=[VMEM] * 2, out_specs=VMEM, out_shap...]
    ppermute x1, waiting for transfers between devices: 6.53 us -> 10.3 us  [local(): visitors = [lax.ppermute(both, ('z', 'core'), trip) for trip in trips]]
    ppermute x2, waiting for transfers between devices: 13.4 us -> 10.2 us  [gather_plane(): blocks[s] = [lax.ppermute(block, 'group', flip(groups, s))]]
    ppermute x9 -> x7, waiting for transfers between devices: 4.3 us -> 2.69 us  [swap(): return lax.ppermute(block, 'core', flip(2, 1))]
    unnamed x6, local copies, waits for them, and re-layouts: 2.44 us -> 0.91 us
    ppermute x3, waiting for transfers between devices: 0.95 us -> 1.59 us  [local(): got = lax.ppermute(merged, 'group', flip(groups, s)) if s else merged]
    ppermute x9 -> x7, starting transfers between devices: 1.71 us -> 1.26 us  [swap(): return lax.ppermute(block, 'core', flip(2, 1))]
  transfers between devices with their start and end apart: 18 -> 16, of which waited for: 8 -> 8; matrix products, arithmetic and copies ran while one was open for 0% -> 0% of each run, Pallas kernels for 3% -> 7%
where the time goes in v10:
time: 63.1 us; the launch traced here: 62.9 us
  waiting for transfers between devices  34.5 us (55%)
  starting transfers between devices  17.8 us (28%)
  Pallas kernels  8.96 us (14%)
  local copies, waits for them, and re-layouts  1.48 us (2%)
    ppermute x1, waiting for transfers between devices, local(): visitors = [lax.ppermute(both, ('z', 'core'), trip) for trip in trips]  10.3 us
    ppermute x2, waiting for transfers between devices, gather_plane(): blocks[s] = [lax.ppermute(block, 'group', flip(groups, s))]  10.2 us
    ppermute x1, waiting for transfers between devices, gather_plane(): lax.ppermute(top, 'group', flip(groups, high))  7.25 us
    ppermute x2, starting transfers between devices, gather_plane(): blocks[s] = [lax.ppermute(block, 'group', flip(groups, s))]  4.08 us
    pallas_call x2, Pallas kernels, call(): pl.pallas_call(kernel, in_specs=[VMEM] * len(operands), out_specs=[VMEM]...  3.87 us
    ppermute x1, starting transfers between devices, local(): visitors = [lax.ppermute(both, ('z', 'core'), trip) for trip in trips]  3.6 us
    ppermute x3, starting transfers between devices, local(): got = lax.ppermute(merged, 'group', flip(groups, s)) if s else merged  3.55 us
    ppermute x7, waiting for transfers between devices, swap(): return lax.ppermute(block, 'core', flip(2, 1))  2.69 us
  transfers between devices with their start and end apart: 16, of which 8 were waited for; matrix products, arithmetic and copies ran while one was open for 0% of the time, Pallas kernels for 7%

profile of v10, /device:TPU:0, one launch (start us, length us, event | category | flops | bytes accessed | tf_op | source)
XLA Modules:
  0.0 62.9 jit_solution(17609468516109068231)
XLA Ops:
  0.0 2.4 %shard_map.37.refs_0_.refs_1_.own_ref = bf16[96,4224]{1,0:T(8,128)(2,1)} custom-call(bf16[96,4096]{1,0:T(8,128)(2,1)} %rows_ref.1, s32[1,96]{1,0:T(1,128)} %bitcast.4, s32[1,96]{1,0:T(1,128)} %bitcast.5), custom_call_target="tpu_custom_call" | custom-call | flops 1572864 | bytes 1572864 | tf_op jit(solution)/shard_map/pallas_call | solution.py:96
  2.4 0.5 collective-permute-start
  2.9 2.6 %collective-permute-start.1 = (bf16[96,4224]{1,0:T(8,128)(2,1)}, bf16[96,4224]{1,0:T(8,128)(2,1)S(1)}, u32[]{:S(2)}, u32[]{:S(2)}) collective-permute-start(bf16[96,4224]{1,0:T(8,128)(2,1)} %shard_map.37.refs_0_.refs_1_.own_ref), channel_id=1, source_target_pairs={{0,8},{8,0},{16,24},{24,16},{1,9},{9,1},{17,25},{25,17},{2,10},{10... | collective-permute-start | bytes 2433032 | tf_op jit(solution)/shard_map/ppermute | solution.py:41
  5.5 1.5 %collective-permute-start.3 = (bf16[96,4224]{1,0:T(8,128)(2,1)}, bf16[96,4224]{1,0:T(8,128)(2,1)S(1)}, u32[]{:S(2)}, u32[]{:S(2)}) collective-permute-start(bf16[96,4224]{1,0:T(8,128)(2,1)} %shard_map.37.refs_0_.refs_1_.own_ref), channel_id=1, source_target_pairs={{0,16},{8,24},{16,0},{24,8},{1,17},{9,25},{17,1},{25,9},{2,18},{10... | collective-permute-start | bytes 2433032 | tf_op jit(solution)/shard_map/ppermute | solution.py:41
  7.0 0.9 %copy-done.1 = bf16[96,4224]{1,0:T(8,128)(2,1)} copy-done((bf16[96,4224]{1,0:T(8,128)(2,1)}, bf16[96,4224]{1,0:T(8,128)(2,1)S(1)}, u32[]{:S(2)}) %copy-start.1) | copy-done | bytes 811032
  7.9 2.7 %shard_map.39 = bf16[192,4224]{1,0:T(8,128)(2,1)} custom-call(bf16[96,4224]{1,0:T(8,128)(2,1)} %shard_map.37.refs_0_.refs_1_.own_ref, bf16[96,4224]{1,0:T(8,128)(2,1)} %copy-done.1), custom_call_target="tpu_custom_call" | custom-call | bytes 3244032 | tf_op jit(solution)/shard_map/pallas_call | solution.py:121
  10.6 3.6 %collective-permute-start.9 = (bf16[192,4224]{1,0:T(8,128)(2,1)}, bf16[192,4224]{1,0:T(8,128)(2,1)S(1)}, u32[]{:S(2)}, u32[]{:S(2)}) collective-permute-start(bf16[192,4224]{1,0:T(8,128)(2,1)} %shard_map.39), channel_id=1, source_target_pairs={{0,2},{2,4},{4,6},{6,0},{1,5},{7,3},{8,10},{10,12},{12,14},{14,8},... | collective-permute-start | bytes 4866056 | tf_op jit(solution)/shard_map/ppermute | solution.py:230
  14.2 10.2 %collective-permute-done.1.refs_3_ = bf16[96,4224]{1,0:T(8,128)(2,1)S(1)} collective-permute-done((bf16[96,4224]{1,0:T(8,128)(2,1)}, bf16[96,4224]{1,0:T(8,128)(2,1)S(1)}, u32[]{:S(2)}, u32[]{:S(2)}) %collective-permute-start.1) | collective-permute-done | bytes 811040 | tf_op jit(solution)/shard_map/ppermute | solution.py:41
  24.4 1.9 %collective-permute-start.5 = (bf16[48,4224]{1,0:T(8,128)(2,1)S(1)}, bf16[48,4224]{1,0:T(8,128)(2,1)S(1)}, u32[]{:S(2)}, u32[]{:S(2)}) collective-permute-start(bf16[48,4224]{1,0:T(8,128)(2,1)S(1)} %slice.44), channel_id=1, source_target_pairs={{0,16},{8,24},{16,0},{24,8},{1,17},{9,25},{17,1},{25,9},{2,18},{10... | collective-permute-start | bytes 1216520 | tf_op jit(solution)/shard_map/ppermute | solution.py:47
  26.3 0.5 collective-permute-start.4
  26.8 1.6 %collective-permute-start.6 = (bf16[48,4224]{1,0:T(8,128)(2,1)S(1)}, bf16[48,4224]{1,0:T(8,128)(2,1)S(1)}, u32[]{:S(2)}, u32[]{:S(2)}) collective-permute-start(bf16[48,4224]{1,0:T(8,128)(2,1)S(1)} %slice.45), channel_id=1, source_target_pairs={{0,8},{8,0},{16,24},{24,16},{1,9},{9,1},{17,25},{25,17},{2,10},{10... | collective-permute-start | bytes 1216520 | tf_op jit(solution)/shard_map/ppermute | solution.py:48
  28.4 7.2 %collective-permute-done.5.refs_7_ = bf16[48,4224]{1,0:T(8,128)(2,1)S(1)} collective-permute-done((bf16[48,4224]{1,0:T(8,128)(2,1)S(1)}, bf16[48,4224]{1,0:T(8,128)(2,1)S(1)}, u32[]{:S(2)}, u32[]{:S(2)}) %collective-permute-start.5) | collective-permute-done | bytes 405536 | tf_op jit(solution)/shard_map/ppermute | solution.py:47
  35.6 2.5 %collective-permute-done.6.refs_8_ = bf16[48,4224]{1,0:T(8,128)(2,1)S(1)} collective-permute-done((bf16[48,4224]{1,0:T(8,128)(2,1)S(1)}, bf16[48,4224]{1,0:T(8,128)(2,1)S(1)}, u32[]{:S(2)}, u32[]{:S(2)}) %collective-permute-start.6) | collective-permute-done | bytes 405536 | tf_op jit(solution)/shard_map/ppermute | solution.py:48
  38.2 1.7 %collective-permute-done.8.refs_10_ = bf16[48,4224]{1,0:T(8,128)(2,1)S(1)} collective-permute-done((bf16[48,4224]{1,0:T(8,128)(2,1)S(1)}, bf16[48,4224]{1,0:T(8,128)(2,1)S(1)}, u32[]{:S(2)}, u32[]{:S(2)}) %collective-permute-start.8) | collective-permute-done | bytes 405536 | tf_op jit(solution)/shard_map/ppermute | solution.py:54
  39.9 1.8 %shard_map.38.refs_11_ = f32[1,128]{1,0:T(1,128)S(1)} custom-call(bf16[96,4224]{1,0:T(8,128)(2,1)S(1)} %copy-done, bf16[96,4224]{1,0:T(8,128)(2,1)S(1)} %copy-done, bf16[96,4224]{1,0:T(8,128)(2,1)S(1)} %copy-done.2, bf16[96,4224]{1,0:T(8,128)(2,1)S(1)} %collective-permute-done.1.refs_3_, bf16[96,4224]{1,0:T(8,128)(2,1)S(1)} %collective-permute-done.2.refs_4_, ...), custom_call_target="tpu_custom_call" | custom-call | flops 805306368 | bytes 7340032 | tf_op jit(solution)/shard_map/pallas_call | solution.py:199
  41.7 10.3 %collective-permute-done.9.refs_0_ = bf16[192,4224]{1,0:T(8,128)(2,1)S(1)} collective-permute-done((bf16[192,4224]{1,0:T(8,128)(2,1)}, bf16[192,4224]{1,0:T(8,128)(2,1)S(1)}, u32[]{:S(2)}, u32[]{:S(2)}) %collective-permute-start.9) | collective-permute-done | bytes 1622048 | tf_op jit(solution)/shard_map/ppermute | solution.py:230
  52.0 2.1 %shard_map.40 = (f32[2,128]{1,0:T(2,128)S(1)}, f32[4,128]{1,0:T(4,128)S(1)}, f32[4,128]{1,0:T(4,128)S(1)}) custom-call(bf16[192,4224]{1,0:T(8,128)(2,1)S(1)} %collective-permute-done.9.refs_0_, bf16[96,4224]{1,0:T(8,128)(2,1)S(1)} %copy-done, bf16[96,4224]{1,0:T(8,128)(2,1)S(1)} %copy-done.2, bf16[96,4224]{1,0:T(8,128)(2,1)S(1)} %collective-permute-done.1.refs_3_, ...), custom_call_target="tpu_custom_call" | custom-call | flops 1610612736 | bytes 8388608 | tf_op jit(solution)/shard_map/pallas_call | solution.py:199
  54.1 1.9 %collective-permute-start.10 = (f32[2,128]{1,0:T(2,128)S(1)}, f32[2,128]{1,0:T(2,128)S(1)}, u32[]{:S(2)}, u32[]{:S(2)}) collective-permute-start(f32[2,128]{1,0:T(2,128)S(1)} %get-tuple-element.8), channel_id=1, source_target_pairs={{2,0},{4,2},{6,4},{0,6},{5,1},{3,7},{10,8},{12,10},{14,12},{8,14},... | collective-permute-start | bytes 3080 | tf_op jit(solution)/shard_map/ppermute | solution.py:256
  56.1 2.2 %collective-permute-start.15 = (f32[4,128]{1,0:T(4,128)S(1)}, f32[4,128]{1,0:T(4,128)S(1)}, u32[]{:S(2)}, u32[]{:S(2)}) collective-permute-start(f32[4,128]{1,0:T(4,128)S(1)} %max.23), channel_id=1, source_target_pairs={{0,24},{8,16},{16,8},{24,0},{1,25},{9,17},{17,9},{25,1},{2,26},{10... | collective-permute-start | bytes 6152 | tf_op jit(solution)/shard_map/ppermute | solution.py:264
  58.3 0.5 collective-permute-start.14
  58.8 0.8 %collective-permute-start.13 = (f32[4,128]{1,0:T(4,128)S(1)}, f32[4,128]{1,0:T(4,128)S(1)}, u32[]{:S(2)}, u32[]{:S(2)}) collective-permute-start(f32[4,128]{1,0:T(4,128)S(1)} %max.23), channel_id=1, source_target_pairs={{0,8},{8,0},{16,24},{24,16},{1,9},{9,1},{17,25},{25,17},{2,10},{10... | collective-permute-start | bytes 6152 | tf_op jit(solution)/shard_map/ppermute | solution.py:264
  59.8 1.0 %collective-permute-done.11 = f32[2,128]{1,0:T(2,128)S(1)} collective-permute-done((f32[2,128]{1,0:T(2,128)S(1)}, f32[2,128]{1,0:T(2,128)S(1)}, u32[]{:S(2)}, u32[]{:S(2)}) %collective-permute-start.11) | collective-permute-done | bytes 1056 | tf_op jit(solution)/shard_map/ppermute | solution.py:54
  60.8 1.1 %collective-permute-done.14 = f32[4,128]{1,0:T(4,128)S(1)} collective-permute-done((f32[4,128]{1,0:T(4,128)S(1)}, f32[4,128]{1,0:T(4,128)S(1)}, u32[]{:S(2)}, u32[]{:S(2)}) %collective-permute-start.14) | collective-permute-done | bytes 2080 | tf_op jit(solution)/shard_map/ppermute | solution.py:264
  62.4 0.5 slice_bitcast_fusion
  (23 shorter events, 0.8 us)
Async XLA Ops:
  2.4 37.5 %copy-start = (bf16[96,4224]{1,0:T(8,128)(2,1)S(1)}, bf16[96,4224]{1,0:T(8,128)(2,1)}, u32[]{:S(2)}) copy-start(bf16[96,4224]{1,0:T(8,128)(2,1)} %shard_map.37.refs_0_.refs_1_.own_ref) | copy-start | bytes 2433028
  2.4 4.6 %collective-permute-start = (bf16[96,4224]{1,0:T(8,128)(2,1)}, bf16[96,4224]{1,0:T(8,128)(2,1)S(1)}, u32[]{:S(2)}, u32[]{:S(2)}) collective-permute-start(bf16[96,4224]{1,0:T(8,128)(2,1)} %shard_map.37.refs_0_.refs_1_.own_ref), channel_id=1, source_target_pairs={{0,1},{1,0},{2,3},{3,2},{4,5},{5,4},{6,7},{7,6},{8,9},{9,8},{10,11... | collective-permute-start | bytes 2433032 | tf_op jit(solution)/shard_map/ppermute | solution.py:54
  2.9 21.4 %collective-permute-start.1 = (bf16[96,4224]{1,0:T(8,128)(2,1)}, bf16[96,4224]{1,0:T(8,128)(2,1)S(1)}, u32[]{:S(2)}, u32[]{:S(2)}) collective-permute-start(bf16[96,4224]{1,0:T(8,128)(2,1)} %shard_map.37.refs_0_.refs_1_.own_ref), channel_id=1, source_target_pairs={{0,8},{8,0},{16,24},{24,16},{1,9},{9,1},{17,25},{25,17},{2,10},{10... | collective-permute-start | bytes 2433032 | tf_op jit(solution)/shard_map/ppermute | solution.py:41
  5.5 20.8 %collective-permute-start.3 = (bf16[96,4224]{1,0:T(8,128)(2,1)}, bf16[96,4224]{1,0:T(8,128)(2,1)S(1)}, u32[]{:S(2)}, u32[]{:S(2)}) collective-permute-start(bf16[96,4224]{1,0:T(8,128)(2,1)} %shard_map.37.refs_0_.refs_1_.own_ref), channel_id=1, source_target_pairs={{0,16},{8,24},{16,0},{24,8},{1,17},{9,25},{17,1},{25,9},{2,18},{10... | collective-permute-start | bytes 2433032 | tf_op jit(solution)/shard_map/ppermute | solution.py:41
  7.0 0.9 %copy-start.1 = (bf16[96,4224]{1,0:T(8,128)(2,1)}, bf16[96,4224]{1,0:T(8,128)(2,1)S(1)}, u32[]{:S(2)}) copy-start(bf16[96,4224]{1,0:T(8,128)(2,1)S(1)} %collective-permute-done.refs_2_.other_ref) | copy-start | bytes 2433028
  10.6 29.3 %copy-start.2 = (bf16[96,4224]{1,0:T(8,128)(2,1)S(1)}, bf16[96,4224]{1,0:T(8,128)(2,1)}, u32[]{:S(2)}) copy-start(bf16[96,4224]{1,0:T(8,128)(2,1)} %copy-done.1) | copy-start | bytes 2433028
  10.6 41.4 %collective-permute-start.9 = (bf16[192,4224]{1,0:T(8,128)(2,1)}, bf16[192,4224]{1,0:T(8,128)(2,1)S(1)}, u32[]{:S(2)}, u32[]{:S(2)}) collective-permute-start(bf16[192,4224]{1,0:T(8,128)(2,1)} %shard_map.39), channel_id=1, source_target_pairs={{0,2},{2,4},{4,6},{6,0},{1,5},{7,3},{8,10},{10,12},{12,14},{14,8},... | collective-permute-start | bytes 4866056 | tf_op jit(solution)/shard_map/ppermute | solution.py:230
  24.4 11.2 %collective-permute-start.5 = (bf16[48,4224]{1,0:T(8,128)(2,1)S(1)}, bf16[48,4224]{1,0:T(8,128)(2,1)S(1)}, u32[]{:S(2)}, u32[]{:S(2)}) collective-permute-start(bf16[48,4224]{1,0:T(8,128)(2,1)S(1)} %slice.44), channel_id=1, source_target_pairs={{0,16},{8,24},{16,0},{24,8},{1,17},{9,25},{17,1},{25,9},{2,18},{10... | collective-permute-start | bytes 1216520 | tf_op jit(solution)/shard_map/ppermute | solution.py:47
  26.3 11.9 %collective-permute-start.2 = (bf16[96,4224]{1,0:T(8,128)(2,1)S(1)}, bf16[96,4224]{1,0:T(8,128)(2,1)S(1)}, u32[]{:S(2)}, u32[]{:S(2)}) collective-permute-start(bf16[96,4224]{1,0:T(8,128)(2,1)S(1)} %collective-permute-done.1.refs_3_), channel_id=1, source_target_pairs={{0,1},{1,0},{2,3},{3,2},{4,5},{5,4},{6,7},{7,6},{8,9},{9,8},{10,11... | collective-permute-start | bytes 2433032 | tf_op jit(solution)/shard_map/ppermute | solution.py:54
  26.3 11.9 %collective-permute-start.4 = (bf16[96,4224]{1,0:T(8,128)(2,1)S(1)}, bf16[96,4224]{1,0:T(8,128)(2,1)S(1)}, u32[]{:S(2)}, u32[]{:S(2)}) collective-permute-start(bf16[96,4224]{1,0:T(8,128)(2,1)S(1)} %collective-permute-done.3.refs_5_), channel_id=1, source_target_pairs={{0,1},{1,0},{2,3},{3,2},{4,5},{5,4},{6,7},{7,6},{8,9},{9,8},{10,11... | collective-permute-start | bytes 2433032 | tf_op jit(solution)/shard_map/ppermute | solution.py:54
  26.8 11.4 %collective-permute-start.6 = (bf16[48,4224]{1,0:T(8,128)(2,1)S(1)}, bf16[48,4224]{1,0:T(8,128)(2,1)S(1)}, u32[]{:S(2)}, u32[]{:S(2)}) collective-permute-start(bf16[48,4224]{1,0:T(8,128)(2,1)S(1)} %slice.45), channel_id=1, source_target_pairs={{0,8},{8,0},{16,24},{24,16},{1,9},{9,1},{17,25},{25,17},{2,10},{10... | collective-permute-start | bytes 1216520 | tf_op jit(solution)/shard_map/ppermute | solution.py:48
  35.6 2.6 %collective-permute-start.7 = (bf16[48,4224]{1,0:T(8,128)(2,1)S(1)}, bf16[48,4224]{1,0:T(8,128)(2,1)S(1)}, u32[]{:S(2)}, u32[]{:S(2)}) collective-permute-start(bf16[48,4224]{1,0:T(8,128)(2,1)S(1)} %collective-permute-done.5.refs_7_), channel_id=1, source_target_pairs={{0,1},{1,0},{2,3},{3,2},{4,5},{5,4},{6,7},{7,6},{8,9},{9,8},{10,11... | collective-permute-start | bytes 1216520 | tf_op jit(solution)/shard_map/ppermute | solution.py:54
  38.2 1.7 %collective-permute-start.8 = (bf16[48,4224]{1,0:T(8,128)(2,1)S(1)}, bf16[48,4224]{1,0:T(8,128)(2,1)S(1)}, u32[]{:S(2)}, u32[]{:S(2)}) collective-permute-start(bf16[48,4224]{1,0:T(8,128)(2,1)S(1)} %collective-permute-done.6.refs_8_), channel_id=1, source_target_pairs={{0,1},{1,0},{2,3},{3,2},{4,5},{5,4},{6,7},{7,6},{8,9},{9,8},{10,11... | collective-permute-start | bytes 1216520 | tf_op jit(solution)/shard_map/ppermute | solution.py:54
  54.1 2.0 %collective-permute-start.12 = (f32[4,128]{1,0:T(4,128)S(1)}, f32[4,128]{1,0:T(4,128)S(1)}, u32[]{:S(2)}, u32[]{:S(2)}) collective-permute-start(f32[4,128]{1,0:T(4,128)S(1)} %get-tuple-element.10), channel_id=1, source_target_pairs={{0,1},{1,0},{2,3},{3,2},{4,5},{5,4},{6,7},{7,6},{8,9},{9,8},{10,11... | collective-permute-start | bytes 6152 | tf_op jit(solution)/shard_map/ppermute | solution.py:54
  54.1 5.5 %collective-permute-start.10 = (f32[2,128]{1,0:T(2,128)S(1)}, f32[2,128]{1,0:T(2,128)S(1)}, u32[]{:S(2)}, u32[]{:S(2)}) collective-permute-start(f32[2,128]{1,0:T(2,128)S(1)} %get-tuple-element.8), channel_id=1, source_target_pairs={{2,0},{4,2},{6,4},{0,6},{5,1},{3,7},{10,8},{12,10},{14,12},{8,14},... | collective-permute-start | bytes 3080 | tf_op jit(solution)/shard_map/ppermute | solution.py:256
  56.1 4.7 %collective-permute-start.15 = (f32[4,128]{1,0:T(4,128)S(1)}, f32[4,128]{1,0:T(4,128)S(1)}, u32[]{:S(2)}, u32[]{:S(2)}) collective-permute-start(f32[4,128]{1,0:T(4,128)S(1)} %max.23), channel_id=1, source_target_pairs={{0,24},{8,16},{16,8},{24,0},{1,25},{9,17},{17,9},{25,1},{2,26},{10... | collective-permute-start | bytes 6152 | tf_op jit(solution)/shard_map/ppermute | solution.py:264
  58.3 3.6 %collective-permute-start.14 = (f32[4,128]{1,0:T(4,128)S(1)}, f32[4,128]{1,0:T(4,128)S(1)}, u32[]{:S(2)}, u32[]{:S(2)}) collective-permute-start(f32[4,128]{1,0:T(4,128)S(1)} %max.23), channel_id=1, source_target_pairs={{0,16},{8,24},{16,0},{24,8},{1,17},{9,25},{17,1},{25,9},{2,18},{10... | collective-permute-start | bytes 6152 | tf_op jit(solution)/shard_map/ppermute | solution.py:264
  58.8 3.6 %collective-permute-start.13 = (f32[4,128]{1,0:T(4,128)S(1)}, f32[4,128]{1,0:T(4,128)S(1)}, u32[]{:S(2)}, u32[]{:S(2)}) collective-permute-start(f32[4,128]{1,0:T(4,128)S(1)} %max.23), channel_id=1, source_target_pairs={{0,8},{8,0},{16,24},{24,16},{1,9},{9,1},{17,25},{25,17},{2,10},{10... | collective-permute-start | bytes 6152 | tf_op jit(solution)/shard_map/ppermute | solution.py:264
  59.6 1.1 %collective-permute-start.11 = (f32[2,128]{1,0:T(2,128)S(1)}, f32[2,128]{1,0:T(2,128)S(1)}, u32[]{:S(2)}, u32[]{:S(2)}) collective-permute-start(f32[2,128]{1,0:T(2,128)S(1)} %collective-permute-done.10), channel_id=1, source_target_pairs={{0,1},{1,0},{2,3},{3,2},{4,5},{5,4},{6,7},{7,6},{8,9},{9,8},{10,11... | collective-permute-start | bytes 3080 | tf_op jit(solution)/shard_map/ppermute | solution.py:54

commit v11 on v10

--- a/solution.py
+++ b/solution.py
@@ -103,6 +103,7 @@
             pltpu.VMEM((2, 1, count), jnp.int32),
             pltpu.SemaphoreType.DMA((PARTS + 2,)),
         ],
+        compiler_params=pltpu.CompilerParams(vmem_limit_bytes=8 * 2**20),
         cost_estimate=pl.CostEstimate(
             flops=4 * count * width, bytes_accessed=4 * count * width, transcendentals=count
         ),
@@ -123,6 +124,7 @@
         in_specs=[VMEM] * 2,
         out_specs=VMEM,
         out_shape=jax.ShapeDtypeStruct((2 * rows, width), own.dtype),
+        compiler_params=pltpu.CompilerParams(vmem_limit_bytes=8 * 2**20),
         cost_estimate=pl.CostEstimate(flops=0, bytes_accessed=8 * rows * width, transcendentals=0),
     )(own, other)
 
@@ -205,7 +207,7 @@
             pltpu.VMEM((count * LANES, width), jnp.bfloat16),
             pltpu.VMEM((total, count * LANES), jnp.float32),
         ],
-        compiler_params=pltpu.CompilerParams(vmem_limit_bytes=40 * 2**20),
+        compiler_params=pltpu.CompilerParams(vmem_limit_bytes=24 * 2**20),
         cost_estimate=pl.CostEstimate(
             flops=2 * total * count * LANES * width,
             bytes_accessed=2 * (total + count * LANES) * width,

time: 63.1 us -> 59.9 us (0.949)
  Pallas kernels: 8.96 us -> 4.76 us
  local copies, waits for them, and re-layouts: 1.48 us -> 3.01 us
    ppermute x1, waiting for transfers between devices: 10.3 us -> 6.7 us  [local(): visitors = [lax.ppermute(both, ('z', 'core'), trip) for trip in trips]]
    ppermute x2, waiting for transfers between devices: 10.2 us -> 13.5 us  [gather_plane(): blocks[s] = [lax.ppermute(block, 'group', flip(groups, s))]]
    pallas_call x1, Pallas kernels: 2.68 us -> 0.12 us  [pair(): pl.pallas_call(pair_kernel, in_specs=[VMEM] * 2, out_specs=VMEM, out_shap...]
    pallas_call x1, Pallas kernels: 2.41 us -> 0.77 us  [pack(): pl.pallas_call(pack_kernel, in_specs=[pl.BlockSpec(memory_space=pl.ANY)]...]
    unnamed x6, local copies, waits for them, and re-layouts: 0.91 us -> 2.44 us
  transfers between devices with their start and end apart: 16 -> 16, of which waited for: 8 -> 8; matrix products, arithmetic and copies ran while one was open for 0% -> 0% of each run, Pallas kernels for 7% -> 3%
where the time goes in v11:
time: 59.9 us; the launch traced here: 59.7 us
  waiting for transfers between devices  34.1 us (57%)
  starting transfers between devices  17.7 us (30%)
  Pallas kernels  4.76 us (8%)
  local copies, waits for them, and re-layouts  3.01 us (5%)
    ppermute x2, waiting for transfers between devices, gather_plane(): blocks[s] = [lax.ppermute(block, 'group', flip(groups, s))]  13.5 us
    ppermute x1, waiting for transfers between devices, gather_plane(): lax.ppermute(top, 'group', flip(groups, high))  7.25 us
    ppermute x1, waiting for transfers between devices, local(): visitors = [lax.ppermute(both, ('z', 'core'), trip) for trip in trips]  6.7 us
    ppermute x2, starting transfers between devices, gather_plane(): blocks[s] = [lax.ppermute(block, 'group', flip(groups, s))]  4.08 us
    pallas_call x2, Pallas kernels, call(): pl.pallas_call(kernel, in_specs=[VMEM] * len(operands), out_specs=[VMEM]...  3.87 us
    ppermute x3, starting transfers between devices, local(): got = lax.ppermute(merged, 'group', flip(groups, s)) if s else merged  3.55 us
    ppermute x1, starting transfers between devices, local(): visitors = [lax.ppermute(both, ('z', 'core'), trip) for trip in trips]  3.48 us
    ppermute x7, waiting for transfers between devices, swap(): return lax.ppermute(block, 'core', flip(2, 1))  2.69 us
  transfers between devices with their start and end apart: 16, of which 8 were waited for; matrix products, arithmetic and copies ran while one was open for 0% of the time, Pallas kernels for 3%

profile of v11, /device:TPU:0, one launch (start us, length us, event | category | flops | bytes accessed | tf_op | source)
XLA Modules:
  0.0 59.7 jit_solution(8574941889539748930)
XLA Ops:
  0.0 1.1 %copy-done = bf16[96,4096]{1,0:T(8,128)(2,1)S(1)} copy-done((bf16[96,4096]{1,0:T(8,128)(2,1)S(1)}, bf16[96,4096]{1,0:T(8,128)(2,1)}, u32[]{:S(2)}) %copy-start) | copy-done | bytes 786456
  1.1 0.7 %copy-done.1 = s32[96]{0:T(128)S(1)} copy-done((s32[96]{0:T(128)S(1)}, s32[96]{0:T(128)}, u32[]{:S(2)}) %copy-start.1) | copy-done | bytes 408
  1.8 0.7 %copy-done.2 = s32[96]{0:T(128)S(1)} copy-done((s32[96]{0:T(128)S(1)}, s32[96]{0:T(128)}, u32[]{:S(2)}) %copy-start.2) | copy-done | bytes 408
  2.4 0.8 %shard_map.37.refs_0_.refs_1_.own_ref = bf16[96,4224]{1,0:T(8,128)(2,1)S(1)} custom-call(bf16[96,4096]{1,0:T(8,128)(2,1)S(1)} %copy-done, s32[1,96]{1,0:T(1,128)S(1)} %bitcast.4, s32[1,96]{1,0:T(1,128)S(1)} %bitcast.5), custom_call_target="tpu_custom_call" | custom-call | flops 1572864 | bytes 1572864 | tf_op jit(solution)/shard_map/pallas_call | solution.py:96
  3.2 0.5 collective-permute-start
  3.7 2.6 %collective-permute-start.1 = (bf16[96,4224]{1,0:T(8,128)(2,1)S(1)}, bf16[96,4224]{1,0:T(8,128)(2,1)S(1)}, u32[]{:S(2)}, u32[]{:S(2)}) collective-permute-start(bf16[96,4224]{1,0:T(8,128)(2,1)S(1)} %shard_map.37.refs_0_.refs_1_.own_ref), channel_id=1, source_target_pairs={{0,8},{8,0},{16,24},{24,16},{1,9},{9,1},{17,25},{25,17},{2,10},{10... | collective-permute-start | bytes 2433032 | tf_op jit(solution)/shard_map/ppermute | solution.py:41
  6.3 1.5 %collective-permute-start.3 = (bf16[96,4224]{1,0:T(8,128)(2,1)S(1)}, bf16[96,4224]{1,0:T(8,128)(2,1)S(1)}, u32[]{:S(2)}, u32[]{:S(2)}) collective-permute-start(bf16[96,4224]{1,0:T(8,128)(2,1)S(1)} %shard_map.37.refs_0_.refs_1_.own_ref), channel_id=1, source_target_pairs={{0,16},{8,24},{16,0},{24,8},{1,17},{9,25},{17,1},{25,9},{2,18},{10... | collective-permute-start | bytes 2433032 | tf_op jit(solution)/shard_map/ppermute | solution.py:41
  8.0 3.5 %collective-permute-start.9 = (bf16[192,4224]{1,0:T(8,128)(2,1)S(1)}, bf16[192,4224]{1,0:T(8,128)(2,1)S(1)}, u32[]{:S(2)}, u32[]{:S(2)}) collective-permute-start(bf16[192,4224]{1,0:T(8,128)(2,1)S(1)} %shard_map.39), channel_id=1, source_target_pairs={{0,2},{2,4},{4,6},{6,0},{1,5},{7,3},{8,10},{10,12},{12,14},{14,8},... | collective-permute-start | bytes 4866056 | tf_op jit(solution)/shard_map/ppermute | solution.py:232
  11.4 13.5 %collective-permute-done.1.refs_3_ = bf16[96,4224]{1,0:T(8,128)(2,1)S(1)} collective-permute-done((bf16[96,4224]{1,0:T(8,128)(2,1)S(1)}, bf16[96,4224]{1,0:T(8,128)(2,1)S(1)}, u32[]{:S(2)}, u32[]{:S(2)}) %collective-permute-start.1) | collective-permute-done | bytes 811040 | tf_op jit(solution)/shard_map/ppermute | solution.py:41
  25.0 1.9 %collective-permute-start.5 = (bf16[48,4224]{1,0:T(8,128)(2,1)S(1)}, bf16[48,4224]{1,0:T(8,128)(2,1)S(1)}, u32[]{:S(2)}, u32[]{:S(2)}) collective-permute-start(bf16[48,4224]{1,0:T(8,128)(2,1)S(1)} %slice.44), channel_id=1, source_target_pairs={{0,16},{8,24},{16,0},{24,8},{1,17},{9,25},{17,1},{25,9},{2,18},{10... | collective-permute-start | bytes 1216520 | tf_op jit(solution)/shard_map/ppermute | solution.py:47
  26.9 0.5 collective-permute-start.4
  27.4 1.6 %collective-permute-start.6 = (bf16[48,4224]{1,0:T(8,128)(2,1)S(1)}, bf16[48,4224]{1,0:T(8,128)(2,1)S(1)}, u32[]{:S(2)}, u32[]{:S(2)}) collective-permute-start(bf16[48,4224]{1,0:T(8,128)(2,1)S(1)} %slice.45), channel_id=1, source_target_pairs={{0,8},{8,0},{16,24},{24,16},{1,9},{9,1},{17,25},{25,17},{2,10},{10... | collective-permute-start | bytes 1216520 | tf_op jit(solution)/shard_map/ppermute | solution.py:48
  29.0 7.2 %collective-permute-done.5.refs_7_ = bf16[48,4224]{1,0:T(8,128)(2,1)S(1)} collective-permute-done((bf16[48,4224]{1,0:T(8,128)(2,1)S(1)}, bf16[48,4224]{1,0:T(8,128)(2,1)S(1)}, u32[]{:S(2)}, u32[]{:S(2)}) %collective-permute-start.5) | collective-permute-done | bytes 405536 | tf_op jit(solution)/shard_map/ppermute | solution.py:47
  36.2 2.5 %collective-permute-done.6.refs_8_ = bf16[48,4224]{1,0:T(8,128)(2,1)S(1)} collective-permute-done((bf16[48,4224]{1,0:T(8,128)(2,1)S(1)}, bf16[48,4224]{1,0:T(8,128)(2,1)S(1)}, u32[]{:S(2)}, u32[]{:S(2)}) %collective-permute-start.6) | collective-permute-done | bytes 405536 | tf_op jit(solution)/shard_map/ppermute | solution.py:48
  38.8 1.7 %collective-permute-done.8.refs_10_ = bf16[48,4224]{1,0:T(8,128)(2,1)S(1)} collective-permute-done((bf16[48,4224]{1,0:T(8,128)(2,1)S(1)}, bf16[48,4224]{1,0:T(8,128)(2,1)S(1)}, u32[]{:S(2)}, u32[]{:S(2)}) %collective-permute-start.8) | collective-permute-done | bytes 405536 | tf_op jit(solution)/shard_map/ppermute | solution.py:54
  40.5 1.8 %shard_map.38.refs_11_ = f32[1,128]{1,0:T(1,128)S(1)} custom-call(bf16[96,4224]{1,0:T(8,128)(2,1)S(1)} %shard_map.37.refs_0_.refs_1_.own_ref, bf16[96,4224]{1,0:T(8,128)(2,1)S(1)} %shard_map.37.refs_0_.refs_1_.own_ref, bf16[96,4224]{1,0:T(8,128)(2,1)S(1)} %collective-permute-done.refs_2_.other_ref, bf16[96,4224]{1,0:T(8,128)(2,1)S(1)} %collective-permute-done.1.refs_3_, ...), custom_call_target="tpu_custom_call" | custom-call | flops 805306368 | bytes 7340032 | tf_op jit(solution)/shard_map/pallas_call | solution.py:201
  42.3 6.7 %collective-permute-done.9.refs_0_ = bf16[192,4224]{1,0:T(8,128)(2,1)S(1)} collective-permute-done((bf16[192,4224]{1,0:T(8,128)(2,1)S(1)}, bf16[192,4224]{1,0:T(8,128)(2,1)S(1)}, u32[]{:S(2)}, u32[]{:S(2)}) %collective-permute-start.9) | collective-permute-done | bytes 1622048 | tf_op jit(solution)/shard_map/ppermute | solution.py:232
  49.0 2.1 %shard_map.40 = (f32[2,128]{1,0:T(2,128)S(1)}, f32[4,128]{1,0:T(4,128)S(1)}, f32[4,128]{1,0:T(4,128)S(1)}) custom-call(bf16[192,4224]{1,0:T(8,128)(2,1)S(1)} %collective-permute-done.9.refs_0_, bf16[96,4224]{1,0:T(8,128)(2,1)S(1)} %shard_map.37.refs_0_.refs_1_.own_ref, bf16[96,4224]{1,0:T(8,128)(2,1)S(1)} %collective-permute-done.refs_2_.other_ref, ...), custom_call_target="tpu_custom_call" | custom-call | flops 1610612736 | bytes 8388608 | tf_op jit(solution)/shard_map/pallas_call | solution.py:201
  51.1 1.9 %collective-permute-start.10 = (f32[2,128]{1,0:T(2,128)S(1)}, f32[2,128]{1,0:T(2,128)S(1)}, u32[]{:S(2)}, u32[]{:S(2)}) collective-permute-start(f32[2,128]{1,0:T(2,128)S(1)} %get-tuple-element.8), channel_id=1, source_target_pairs={{2,0},{4,2},{6,4},{0,6},{5,1},{3,7},{10,8},{12,10},{14,12},{8,14},... | collective-permute-start | bytes 3080 | tf_op jit(solution)/shard_map/ppermute | solution.py:258
  53.1 2.0 %collective-permute-start.15 = (f32[4,128]{1,0:T(4,128)S(1)}, f32[4,128]{1,0:T(4,128)S(1)}, u32[]{:S(2)}, u32[]{:S(2)}) collective-permute-start(f32[4,128]{1,0:T(4,128)S(1)} %max.23), channel_id=1, source_target_pairs={{0,24},{8,16},{16,8},{24,0},{1,25},{9,17},{17,9},{25,1},{2,26},{10... | collective-permute-start | bytes 6152 | tf_op jit(solution)/shard_map/ppermute | solution.py:266
  55.6 1.1 %collective-permute-start.13 = (f32[4,128]{1,0:T(4,128)S(1)}, f32[4,128]{1,0:T(4,128)S(1)}, u32[]{:S(2)}, u32[]{:S(2)}) collective-permute-start(f32[4,128]{1,0:T(4,128)S(1)} %max.23), channel_id=1, source_target_pairs={{0,8},{8,0},{16,24},{24,16},{1,9},{9,1},{17,25},{25,17},{2,10},{10... | collective-permute-start | bytes 6152 | tf_op jit(solution)/shard_map/ppermute | solution.py:266
  56.8 1.0 %collective-permute-done.11 = f32[2,128]{1,0:T(2,128)S(1)} collective-permute-done((f32[2,128]{1,0:T(2,128)S(1)}, f32[2,128]{1,0:T(2,128)S(1)}, u32[]{:S(2)}, u32[]{:S(2)}) %collective-permute-start.11) | collective-permute-done | bytes 1056 | tf_op jit(solution)/shard_map/ppermute | solution.py:54
  57.8 0.9 %collective-permute-done.14 = f32[4,128]{1,0:T(4,128)S(1)} collective-permute-done((f32[4,128]{1,0:T(4,128)S(1)}, f32[4,128]{1,0:T(4,128)S(1)}, u32[]{:S(2)}, u32[]{:S(2)}) %collective-permute-start.14) | collective-permute-done | bytes 2080 | tf_op jit(solution)/shard_map/ppermute | solution.py:266
  59.2 0.5 slice_bitcast_fusion
  (23 shorter events, 1.5 us)
Async XLA Ops:
  0.0 1.1 %copy-start = (bf16[96,4096]{1,0:T(8,128)(2,1)S(1)}, bf16[96,4096]{1,0:T(8,128)(2,1)}, u32[]{:S(2)}) copy-start(bf16[96,4096]{1,0:T(8,128)(2,1)} %rows_ref.1) | copy-start | bytes 2359300
  1.1 0.7 %copy-start.1 = (s32[96]{0:T(128)S(1)}, s32[96]{0:T(128)}, u32[]{:S(2)}) copy-start(s32[96]{0:T(128)} %param.4) | copy-start | bytes 1156
  1.8 0.7 %copy-start.2 = (s32[96]{0:T(128)S(1)}, s32[96]{0:T(128)}, u32[]{:S(2)}) copy-start(s32[96]{0:T(128)} %param.5) | copy-start | bytes 1156
  3.2 4.6 %collective-permute-start = (bf16[96,4224]{1,0:T(8,128)(2,1)S(1)}, bf16[96,4224]{1,0:T(8,128)(2,1)S(1)}, u32[]{:S(2)}, u32[]{:S(2)}) collective-permute-start(bf16[96,4224]{1,0:T(8,128)(2,1)S(1)} %shard_map.37.refs_0_.refs_1_.own_ref), channel_id=1, source_target_pairs={{0,1},{1,0},{2,3},{3,2},{4,5},{5,4},{6,7},{7,6},{8,9},{9,8},{10,11... | collective-permute-start | bytes 2433032 | tf_op jit(solution)/shard_map/ppermute | solution.py:54
  3.7 21.2 %collective-permute-start.1 = (bf16[96,4224]{1,0:T(8,128)(2,1)S(1)}, bf16[96,4224]{1,0:T(8,128)(2,1)S(1)}, u32[]{:S(2)}, u32[]{:S(2)}) collective-permute-start(bf16[96,4224]{1,0:T(8,128)(2,1)S(1)} %shard_map.37.refs_0_.refs_1_.own_ref), channel_id=1, source_target_pairs={{0,8},{8,0},{16,24},{24,16},{1,9},{9,1},{17,25},{25,17},{2,10},{10... | collective-permute-start | bytes 2433032 | tf_op jit(solution)/shard_map/ppermute | solution.py:41
  6.3 20.6 %collective-permute-start.3 = (bf16[96,4224]{1,0:T(8,128)(2,1)S(1)}, bf16[96,4224]{1,0:T(8,128)(2,1)S(1)}, u32[]{:S(2)}, u32[]{:S(2)}) collective-permute-start(bf16[96,4224]{1,0:T(8,128)(2,1)S(1)} %shard_map.37.refs_0_.refs_1_.own_ref), channel_id=1, source_target_pairs={{0,16},{8,24},{16,0},{24,8},{1,17},{9,25},{17,1},{25,9},{2,18},{10... | collective-permute-start | bytes 2433032 | tf_op jit(solution)/shard_map/ppermute | solution.py:41
  8.0 41.0 %collective-permute-start.9 = (bf16[192,4224]{1,0:T(8,128)(2,1)S(1)}, bf16[192,4224]{1,0:T(8,128)(2,1)S(1)}, u32[]{:S(2)}, u32[]{:S(2)}) collective-permute-start(bf16[192,4224]{1,0:T(8,128)(2,1)S(1)} %shard_map.39), channel_id=1, source_target_pairs={{0,2},{2,4},{4,6},{6,0},{1,5},{7,3},{8,10},{10,12},{12,14},{14,8},... | collective-permute-start | bytes 4866056 | tf_op jit(solution)/shard_map/ppermute | solution.py:232
  25.0 11.2 %collective-permute-start.5 = (bf16[48,4224]{1,0:T(8,128)(2,1)S(1)}, bf16[48,4224]{1,0:T(8,128)(2,1)S(1)}, u32[]{:S(2)}, u32[]{:S(2)}) collective-permute-start(bf16[48,4224]{1,0:T(8,128)(2,1)S(1)} %slice.44), channel_id=1, source_target_pairs={{0,16},{8,24},{16,0},{24,8},{1,17},{9,25},{17,1},{25,9},{2,18},{10... | collective-permute-start | bytes 1216520 | tf_op jit(solution)/shard_map/ppermute | solution.py:47
  26.9 11.9 %collective-permute-start.2 = (bf16[96,4224]{1,0:T(8,128)(2,1)S(1)}, bf16[96,4224]{1,0:T(8,128)(2,1)S(1)}, u32[]{:S(2)}, u32[]{:S(2)}) collective-permute-start(bf16[96,4224]{1,0:T(8,128)(2,1)S(1)} %collective-permute-done.1.refs_3_), channel_id=1, source_target_pairs={{0,1},{1,0},{2,3},{3,2},{4,5},{5,4},{6,7},{7,6},{8,9},{9,8},{10,11... | collective-permute-start | bytes 2433032 | tf_op jit(solution)/shard_map/ppermute | solution.py:54
  26.9 11.9 %collective-permute-start.4 = (bf16[96,4224]{1,0:T(8,128)(2,1)S(1)}, bf16[96,4224]{1,0:T(8,128)(2,1)S(1)}, u32[]{:S(2)}, u32[]{:S(2)}) collective-permute-start(bf16[96,4224]{1,0:T(8,128)(2,1)S(1)} %collective-permute-done.3.refs_5_), channel_id=1, source_target_pairs={{0,1},{1,0},{2,3},{3,2},{4,5},{5,4},{6,7},{7,6},{8,9},{9,8},{10,11... | collective-permute-start | bytes 2433032 | tf_op jit(solution)/shard_map/ppermute | solution.py:54
  27.4 11.4 %collective-permute-start.6 = (bf16[48,4224]{1,0:T(8,128)(2,1)S(1)}, bf16[48,4224]{1,0:T(8,128)(2,1)S(1)}, u32[]{:S(2)}, u32[]{:S(2)}) collective-permute-start(bf16[48,4224]{1,0:T(8,128)(2,1)S(1)} %slice.45), channel_id=1, source_target_pairs={{0,8},{8,0},{16,24},{24,16},{1,9},{9,1},{17,25},{25,17},{2,10},{10... | collective-permute-start | bytes 1216520 | tf_op jit(solution)/shard_map/ppermute | solution.py:48
  36.2 2.6 %collective-permute-start.7 = (bf16[48,4224]{1,0:T(8,128)(2,1)S(1)}, bf16[48,4224]{1,0:T(8,128)(2,1)S(1)}, u32[]{:S(2)}, u32[]{:S(2)}) collective-permute-start(bf16[48,4224]{1,0:T(8,128)(2,1)S(1)} %collective-permute-done.5.refs_7_), channel_id=1, source_target_pairs={{0,1},{1,0},{2,3},{3,2},{4,5},{5,4},{6,7},{7,6},{8,9},{9,8},{10,11... | collective-permute-start | bytes 1216520 | tf_op jit(solution)/shard_map/ppermute | solution.py:54
  38.8 1.7 %collective-permute-start.8 = (bf16[48,4224]{1,0:T(8,128)(2,1)S(1)}, bf16[48,4224]{1,0:T(8,128)(2,1)S(1)}, u32[]{:S(2)}, u32[]{:S(2)}) collective-permute-start(bf16[48,4224]{1,0:T(8,128)(2,1)S(1)} %collective-permute-done.6.refs_8_), channel_id=1, source_target_pairs={{0,1},{1,0},{2,3},{3,2},{4,5},{5,4},{6,7},{7,6},{8,9},{9,8},{10,11... | collective-permute-start | bytes 1216520 | tf_op jit(solution)/shard_map/ppermute | solution.py:54
  51.1 2.0 %collective-permute-start.12 = (f32[4,128]{1,0:T(4,128)S(1)}, f32[4,128]{1,0:T(4,128)S(1)}, u32[]{:S(2)}, u32[]{:S(2)}) collective-permute-start(f32[4,128]{1,0:T(4,128)S(1)} %get-tuple-element.10), channel_id=1, source_target_pairs={{0,1},{1,0},{2,3},{3,2},{4,5},{5,4},{6,7},{7,6},{8,9},{9,8},{10,11... | collective-permute-start | bytes 6152 | tf_op jit(solution)/shard_map/ppermute | solution.py:54
  51.1 5.5 %collective-permute-start.10 = (f32[2,128]{1,0:T(2,128)S(1)}, f32[2,128]{1,0:T(2,128)S(1)}, u32[]{:S(2)}, u32[]{:S(2)}) collective-permute-start(f32[2,128]{1,0:T(2,128)S(1)} %get-tuple-element.8), channel_id=1, source_target_pairs={{2,0},{4,2},{6,4},{0,6},{5,1},{3,7},{10,8},{12,10},{14,12},{8,14},... | collective-permute-start | bytes 3080 | tf_op jit(solution)/shard_map/ppermute | solution.py:258
  53.1 4.7 %collective-permute-start.15 = (f32[4,128]{1,0:T(4,128)S(1)}, f32[4,128]{1,0:T(4,128)S(1)}, u32[]{:S(2)}, u32[]{:S(2)}) collective-permute-start(f32[4,128]{1,0:T(4,128)S(1)} %max.23), channel_id=1, source_target_pairs={{0,24},{8,16},{16,8},{24,0},{1,25},{9,17},{17,9},{25,1},{2,26},{10... | collective-permute-start | bytes 6152 | tf_op jit(solution)/shard_map/ppermute | solution.py:266
  55.1 3.6 %collective-permute-start.14 = (f32[4,128]{1,0:T(4,128)S(1)}, f32[4,128]{1,0:T(4,128)S(1)}, u32[]{:S(2)}, u32[]{:S(2)}) collective-permute-start(f32[4,128]{1,0:T(4,128)S(1)} %max.23), channel_id=1, source_target_pairs={{0,16},{8,24},{16,0},{24,8},{1,17},{9,25},{17,1},{25,9},{2,18},{10... | collective-permute-start | bytes 6152 | tf_op jit(solution)/shard_map/ppermute | solution.py:266
  55.6 3.6 %collective-permute-start.13 = (f32[4,128]{1,0:T(4,128)S(1)}, f32[4,128]{1,0:T(4,128)S(1)}, u32[]{:S(2)}, u32[]{:S(2)}) collective-permute-start(f32[4,128]{1,0:T(4,128)S(1)} %max.23), channel_id=1, source_target_pairs={{0,8},{8,0},{16,24},{24,16},{1,9},{9,1},{17,25},{25,17},{2,10},{10... | collective-permute-start | bytes 6152 | tf_op jit(solution)/shard_map/ppermute | solution.py:266
  56.6 1.1 %collective-permute-start.11 = (f32[2,128]{1,0:T(2,128)S(1)}, f32[2,128]{1,0:T(2,128)S(1)}, u32[]{:S(2)}, u32[]{:S(2)}) collective-permute-start(f32[2,128]{1,0:T(2,128)S(1)} %collective-permute-done.10), channel_id=1, source_target_pairs={{0,1},{1,0},{2,3},{3,2},{4,5},{5,4},{6,7},{7,6},{8,9},{9,8},{10,11... | collective-permute-start | bytes 3080 | tf_op jit(solution)/shard_map/ppermute | solution.py:54

commit v12 on v11

v12 whole, which is shorter than its diff:
```python
import functools

import jax
import jax.numpy as jnp
from jax import lax
from jax.experimental import pallas as pl
from jax.experimental.pallas import tpu as pltpu
from jax.sharding import Mesh, PartitionSpec as P

AXES = ("group", "z", "core")
LANES = 128
CHUNK = 1024
CALL = 8
VMEM = pl.BlockSpec(memory_space=pltpu.VMEM)


def flip(count, bits):
    return [(k, k ^ bits) for k in range(count)]


def unit_rows(values):
    values = values.astype(jnp.float32)
    total = jnp.sum(values * values, axis=1, keepdims=True) + values.shape[1] * 1e-06
    return (values * lax.rsqrt(total)).astype(jnp.bfloat16)


def ring_pairs(length, shift):
    if 2 * shift < length:
        return [(k, (k + shift) % length) for k in range(length)]
    pairs = [(k, k + shift) for k in range(length // 2)]
    return [pair[:: 1 - 2 * (pair[0] % 2)] for pair in pairs]


def gather_plane(block, groups):
    half = block.shape[0] // 2
    blocks = {0: [block]}
    for s in range(1, groups):
        low, high = s & -s, 1 << (s.bit_length() - 1)
        if low == high:
            blocks[s] = [lax.ppermute(block, "group", flip(groups, s))]
            continue
        top, bottom = blocks[s ^ high], blocks[s ^ low]
        top = top[0][:half] if len(top) == 1 else top[0]
        bottom = bottom[0][half:] if len(bottom) == 1 else bottom[1]
        blocks[s] = [
            lax.ppermute(top, "group", flip(groups, high)),
            lax.ppermute(bottom, "group", flip(groups, low)),
        ]
    return blocks


def swap(block):
    return lax.ppermute(block, "core", flip(2, 1))


def pack_kernel(rows_ref, meta_ref, block_ref):
    rows, width = rows_ref.shape
    block_ref[:, :width] = unit_rows(rows_ref[...])
    turned = meta_ref[...].T[:rows]
    cluster, order = turned[:, 0:1], turned[:, 1:2]
    high = jnp.floor(order / 256.0)
    lane = lax.broadcasted_iota(jnp.int32, (rows, LANES), 1)
    tail = jnp.where(lane == 0, cluster, jnp.where(lane == 1, high, order - 256.0 * high))
    block_ref[:, width:] = jnp.where(lane < 3, tail, 0.0).astype(jnp.bfloat16)


def pack(rows, cluster_ids, order_index):
    count, width = rows.shape
    meta = jnp.stack([cluster_ids + 1, order_index]).astype(jnp.float32)
    meta = jnp.pad(meta, ((0, 6), (0, LANES - count)))
    return pl.pallas_call(
        pack_kernel,
        in_specs=[VMEM] * 2,
        out_specs=VMEM,
        out_shape=jax.ShapeDtypeStruct((count, width + LANES), jnp.bfloat16),
        compiler_params=pltpu.CompilerParams(vmem_limit_bytes=8 * 2**20),
        cost_estimate=pl.CostEstimate(
            flops=4 * count * width, bytes_accessed=4 * count * width, transcendentals=count
        ),
    )(rows, meta)


def pair_kernel(own_ref, other_ref, both_ref):
    rows = own_ref.shape[0]
    core = lax.axis_index("core")
    both_ref[pl.ds(pl.multiple_of(core * rows, 16), rows), :] = own_ref[...]
    both_ref[pl.ds(pl.multiple_of((core ^ 1) * rows, 16), rows), :] = other_ref[...]


def pair(own, other):
    rows, width = own.shape
    return pl.pallas_call(
        pair_kernel,
        in_specs=[VMEM] * 2,
        out_specs=VMEM,
        out_shape=jax.ShapeDtypeStruct((2 * rows, width), own.dtype),
        compiler_params=pltpu.CompilerParams(vmem_limit_bytes=8 * 2**20),
        cost_estimate=pl.CostEstimate(flops=0, bytes_accessed=8 * rows * width, transcendentals=0),
    )(own, other)


def own_kernel(*refs):
    row_ref, dots_ref = refs[-2:]
    row_ref[...], _ = best_of(refs[:1], refs[1:-2], refs[0].shape[0], False, [dots_ref])


def visit_kernel(visitors, arrays, *refs):
    block_refs = refs[visitors : visitors + arrays]
    out_refs = refs[visitors + arrays + 1 :]
    rows = refs[0].shape[0] // 2
    bests, col = best_of(refs[:visitors], block_refs, rows, True, out_refs[visitors + 2 :])
    for ref, best in zip(out_refs[:visitors], bests):
        ref[...] = best
    lower_ref, upper_ref = out_refs[visitors : visitors + 2]
    half = lower_ref.shape[0]
    lower_ref[...] = col[:half]
    upper_ref[...] = col[half : 2 * half]


def best_of(visitor_refs, block_refs, rows, homed, dots_refs):
    width = visitor_refs[0].shape[1] - LANES
    meta = []
    for ref in visitor_refs:
        count = ref.shape[0]
        tail = ref[:, width:].astype(jnp.float32)
        if count % LANES:
            tail = jnp.concatenate([tail, jnp.zeros((-count % LANES, LANES), jnp.float32)], axis=0)
        turned = tail.T
        meta.append((turned[0:1, :count], turned[1:2, :count] * 256.0 + turned[2:3, :count]))
    for k in range(0, width, CHUNK):
        left = jnp.concatenate([ref[:, k : k + CHUNK] for ref in block_refs], axis=0)
        for ref, dots in zip(visitor_refs, dots_refs):
            part = lax.dot_general(
                left,
                ref[:, k : k + CHUNK],
                (((1,), (1,)), ((), ())),
                preferred_element_type=jnp.float32,
            )
            dots[...] = part if k == 0 else dots[...] + part

    tails = jnp.concatenate([ref[:, width:] for ref in block_refs], axis=0).astype(jnp.float32)
    row_best = [jnp.full(cluster.shape, -1.0, jnp.float32) for cluster, _ in meta]
    lane = lax.broadcasted_iota(jnp.int32, (rows, LANES), 1)
    col_all = jnp.full((rows, LANES), -1.0, jnp.float32)
    for j in range(tails.shape[0] // rows):
        tail = tails[j * rows : (j + 1) * rows]
        block_cluster, block_order = tail[:, 0:1], tail[:, 1:2] * 256.0 + tail[:, 2:3]
        col_best = jnp.full((rows, 1), -1.0, jnp.float32)
        for v, (cluster, order) in enumerate(meta):
            cosine = dots_refs[v][j * rows : (j + 1) * rows, :]
            same = (block_cluster == cluster) & (cluster > 0)
            seen = jnp.where(same & (block_order < order), cosine, -1.0)
            row_best[v] = jnp.maximum(row_best[v], jnp.max(seen, axis=0, keepdims=True))
            if homed:
                seen = jnp.where(same & (order < block_order), cosine, -1.0)
                col_best = jnp.maximum(col_best, jnp.max(seen, axis=1, keepdims=True))
        col_all = jnp.where(lane == j, col_best, col_all)
    if not homed:
        return row_best[0], None
    if rows < LANES:
        fill = jnp.full((LANES - rows, LANES), -1.0, jnp.float32)
        col_all = jnp.concatenate([col_all, fill], axis=0)
    return row_best, col_all.T


def call(kernel, operands, counts, shapes, total):
    width = operands[0].shape[1] - LANES
    return pl.pallas_call(
        kernel,
        in_specs=[VMEM] * len(operands),
        out_specs=[VMEM] * len(shapes),
        out_shape=[jax.ShapeDtypeStruct(shape, jnp.float32) for shape in shapes],
        scratch_shapes=[pltpu.VMEM((total, count), jnp.float32) for count in counts],
        compiler_params=pltpu.CompilerParams(vmem_limit_bytes=24 * 2**20),
        cost_estimate=pl.CostEstimate(
            flops=2 * total * sum(counts) * width,
            bytes_accessed=2 * (total + sum(counts)) * width,
            transcendentals=0,
        ),
    )(*operands)


def local(embeddings, cluster_ids, order_index):
    rows = embeddings.shape[0]
    groups, length = lax.axis_size("group"), lax.axis_size("z")
    z, core = lax.axis_index("z"), lax.axis_index("core")
    own = pack(embeddings, cluster_ids, order_index)
    other = swap(own)
    both = pair(own, other)

    routes = [ring_pairs(length, shift) for shift in range(1, length // 2 + 1)]
    trips = []
    for first in range(0, len(routes), 2):
        ways = enumerate(routes[first : first + 2])
        trips.append([(2 * a + way, 2 * b + way) for way, route in ways for a, b in route])
    visitors = [lax.ppermute(both, ("z", "core"), trip) for trip in trips]

    plane = gather_plane(own, groups)
    parts = [own, other]
    for s in range(1, groups):
        parts += [*plane[s], *(swap(part) for part in plane[s])]
    chunks, size = [[]], 0
    for part in parts:
        if size == CALL * rows:
            chunks, size = chunks + [[]], 0
        chunks[-1].append(part)
        size += part.shape[0]

    bests, homes, cols = [], [], []
    for chunk in chunks:
        total = sum(part.shape[0] for part in chunk)
        bests += call(own_kernel, [own, *chunk], [rows], [(1, rows)], total)
    for index, chunk in enumerate(chunks):
        total = sum(part.shape[0] for part in chunk)
        kernel = functools.partial(visit_kernel, len(visitors), len(chunk))
        counts = [2 * rows] * len(visitors)
        shapes = [(1, count) for count in counts] + [(CALL // 2, LANES)] * 2
        answer = call(kernel, [*visitors, *chunk, bests[index]], counts, shapes, total)
        homes.append(answer[: len(visitors)])
        cols += answer[len(visitors) :]

    while len(cols) > 1:
        half = len(cols) // 2
        got = [lax.ppermute(col, "group", flip(groups, CALL // 4 * half)) for col in cols[half:]]
        cols = [jnp.maximum(a, b) for a, b in zip(cols, got)]
    (col,) = cols
    while col.shape[0] > 2:
        half = col.shape[0] // 4
        got = lax.ppermute(col, "group", flip(groups, half))
        col = jnp.maximum(col[: 2 * half], got[2 * half :])
    mine, others = [col[0:1, :rows]], [col[1:2, :rows]]
    for trip, parts in zip(trips, zip(*homes)):
        back = functools.reduce(jnp.maximum, parts)
        back = lax.ppermute(back, ("z", "core"), [(b, a) for a, b in trip])
        sent = functools.reduce(jnp.logical_or, [2 * z + core == a for a, _ in trip])
        back = jnp.where(sent, back, -1.0)
        first, second = back[:, :rows], back[:, rows:]
        mine.append(jnp.where(core == 0, first, second))
        others.append(jnp.where(core == 0, second, first))
    bests += mine + [swap(functools.reduce(jnp.maximum, others))]
    return functools.reduce(jnp.maximum, bests)[0]


def solution(mesh):
    groups, members = mesh.devices.shape
    fine = Mesh(mesh.devices.reshape(groups, members // 2, 2), AXES)
    placed = (P(AXES, None), P(AXES), P(AXES))
    return jax.shard_map(local, mesh=fine, in_specs=placed, out_specs=P(AXES), check_vma=False)
```

time: 59.9 us -> 60 us (level)
  other arithmetic: 0.02 us -> 1.99 us
  waiting for transfers between devices: 34.1 us -> 36 us
  local copies, waits for them, and re-layouts: 3.01 us -> 1.19 us
  starting transfers between devices: 17.7 us -> 15.9 us
    ppermute x4 -> x3, waiting for transfers between devices: 1.38 us -> 3.27 us  [the longest x1 1.89 us: local(): back = lax.ppermute(back, ('z', 'core'), [(b, a) for a, b in trip])]
    ppermute x4 -> x3, starting transfers between devices: 5.47 us -> 3.91 us  [the longest x1 1.91 us: local(): back = lax.ppermute(back, ('z', 'core'), [(b, a) for a, b in trip])]
    unnamed x6 -> x2, local copies, waits for them, and re-layouts: 2.44 us -> 1.13 us
    convert_element_type x0 -> x1, other arithmetic: none -> 0.66 us  [pack(): meta = jnp.stack([cluster_ids + 1, order_index]).astype(jnp.float32)]
    another operation x0 -> x1, other arithmetic: none -> 0.66 us  [pack(): meta = jnp.stack([cluster_ids + 1, order_index]).astype(jnp.float32)]
    ppermute x7 -> x6, starting transfers between devices: 1.26 us -> 1.04 us  [swap(): return lax.ppermute(block, 'core', flip(2, 1))]
    ppermute x7 -> x6, waiting for transfers between devices: 2.69 us -> 2.84 us  [swap(): return lax.ppermute(block, 'core', flip(2, 1))]
  transfers between devices with their start and end apart: 16 -> 14, of which waited for: 8 -> 9; matrix products, arithmetic and copies ran while one was open for 0% -> 0% of each run, Pallas kernels for 3% -> 3%
where the time goes in v12:
time: 60 us; the launch traced here: 59.8 us
  waiting for transfers between devices  36 us (60%)
  starting transfers between devices  15.9 us (26%)
  Pallas kernels  4.62 us (8%)
  other arithmetic  1.99 us (3%)
  local copies, waits for them, and re-layouts  1.19 us (2%)
    ppermute x2, waiting for transfers between devices, gather_plane(): blocks[s] = [lax.ppermute(block, 'group', flip(groups, s))]  13.5 us
    ppermute x1, waiting for transfers between devices, gather_plane(): lax.ppermute(top, 'group', flip(groups, high))  7.25 us
    ppermute x1, waiting for transfers between devices, local(): visitors = [lax.ppermute(both, ('z', 'core'), trip) for trip in trips]  6.54 us
    pallas_call x2, Pallas kernels, call(): pl.pallas_call(kernel, in_specs=[VMEM] * len(operands), out_specs=[VMEM]...  4.21 us
    ppermute x2, starting transfers between devices, gather_plane(): blocks[s] = [lax.ppermute(block, 'group', flip(groups, s))]  4.08 us
    ppermute x1, starting transfers between devices, local(): visitors = [lax.ppermute(both, ('z', 'core'), trip) for trip in trips]  3.48 us
    ppermute x6, waiting for transfers between devices, swap(): return lax.ppermute(block, 'core', flip(2, 1))  2.84 us
    ppermute x1, waiting for transfers between devices, gather_plane(): lax.ppermute(bottom, 'group', flip(groups, low))  2.55 us
  transfers between devices with their start and end apart: 14, of which 9 were waited for; matrix products, arithmetic and copies ran while one was open for 0% of the time, Pallas kernels for 3%

profile of v12, /device:TPU:0, one launch (start us, length us, event | category | flops | bytes accessed | tf_op | source)
XLA Modules:
  0.0 59.8 jit_solution(15633774268941226107)
XLA Ops:
  0.0 0.7 %add_bitcast_fusion = s32[1,96]{1,0:T(1,128)S(1)} fusion(s32[96]{0:T(128)} %param.4), kind=kLoop, calls=%fused_computation.8 | loop fusion | flops 96 | bytes 768 | tf_op jit(solution)/shard_map/stack | solution.py:69
  0.7 0.7 %add_convert_fusion = f32[2,96]{1,0:T(2,128)S(1)} fusion(s32[1,96]{1,0:T(1,128)} %bitcast.5, s32[1,96]{1,0:T(1,128)S(1)} %add_bitcast_fusion), kind=kLoop, calls=%fused_computation.1 | loop fusion | flops 384 | bytes 1536 | tf_op jit(solution)/shard_map/convert_element_type | solution.py:69
  1.3 1.1 %copy-done = bf16[96,4096]{1,0:T(8,128)(2,1)S(1)} copy-done((bf16[96,4096]{1,0:T(8,128)(2,1)S(1)}, bf16[96,4096]{1,0:T(8,128)(2,1)}, u32[]{:S(2)}) %copy-start) | copy-done | bytes 786456
  2.8 0.5 collective-permute-start
  3.3 2.6 %collective-permute-start.1 = (bf16[96,4224]{1,0:T(8,128)(2,1)S(1)}, bf16[96,4224]{1,0:T(8,128)(2,1)S(1)}, u32[]{:S(2)}, u32[]{:S(2)}) collective-permute-start(bf16[96,4224]{1,0:T(8,128)(2,1)S(1)} %shard_map.37.refs_0_.refs_1_.own_ref), channel_id=1, source_target_pairs={{0,8},{8,0},{16,24},{24,16},{1,9},{9,1},{17,25},{25,17},{2,10},{10... | collective-permute-start | bytes 2433032 | tf_op jit(solution)/shard_map/ppermute | solution.py:40
  5.8 1.5 %collective-permute-start.3 = (bf16[96,4224]{1,0:T(8,128)(2,1)S(1)}, bf16[96,4224]{1,0:T(8,128)(2,1)S(1)}, u32[]{:S(2)}, u32[]{:S(2)}) collective-permute-start(bf16[96,4224]{1,0:T(8,128)(2,1)S(1)} %shard_map.37.refs_0_.refs_1_.own_ref), channel_id=1, source_target_pairs={{0,16},{8,24},{16,0},{24,8},{1,17},{9,25},{17,1},{25,9},{2,18},{10... | collective-permute-start | bytes 2433032 | tf_op jit(solution)/shard_map/ppermute | solution.py:40
  7.5 3.5 %collective-permute-start.9 = (bf16[192,4224]{1,0:T(8,128)(2,1)S(1)}, bf16[192,4224]{1,0:T(8,128)(2,1)S(1)}, u32[]{:S(2)}, u32[]{:S(2)}) collective-permute-start(bf16[192,4224]{1,0:T(8,128)(2,1)S(1)} %shard_map.39), channel_id=1, source_target_pairs={{0,2},{2,4},{4,6},{6,0},{1,5},{7,3},{8,10},{10,12},{12,14},{14,8},... | collective-permute-start | bytes 4866056 | tf_op jit(solution)/shard_map/ppermute | solution.py:196
  11.0 13.5 %collective-permute-done.1.refs_3_ = bf16[96,4224]{1,0:T(8,128)(2,1)S(1)} collective-permute-done((bf16[96,4224]{1,0:T(8,128)(2,1)S(1)}, bf16[96,4224]{1,0:T(8,128)(2,1)S(1)}, u32[]{:S(2)}, u32[]{:S(2)}) %collective-permute-start.1) | collective-permute-done | bytes 811040 | tf_op jit(solution)/shard_map/ppermute | solution.py:40
  24.5 1.9 %collective-permute-start.5 = (bf16[48,4224]{1,0:T(8,128)(2,1)S(1)}, bf16[48,4224]{1,0:T(8,128)(2,1)S(1)}, u32[]{:S(2)}, u32[]{:S(2)}) collective-permute-start(bf16[48,4224]{1,0:T(8,128)(2,1)S(1)} %slice.32), channel_id=1, source_target_pairs={{0,16},{8,24},{16,0},{24,8},{1,17},{9,25},{17,1},{25,9},{2,18},{10... | collective-permute-start | bytes 1216520 | tf_op jit(solution)/shard_map/ppermute | solution.py:46
  26.9 1.6 %collective-permute-start.6 = (bf16[48,4224]{1,0:T(8,128)(2,1)S(1)}, bf16[48,4224]{1,0:T(8,128)(2,1)S(1)}, u32[]{:S(2)}, u32[]{:S(2)}) collective-permute-start(bf16[48,4224]{1,0:T(8,128)(2,1)S(1)} %slice.33), channel_id=1, source_target_pairs={{0,8},{8,0},{16,24},{24,16},{1,9},{9,1},{17,25},{25,17},{2,10},{10... | collective-permute-start | bytes 1216520 | tf_op jit(solution)/shard_map/ppermute | solution.py:47
  28.5 7.2 %collective-permute-done.5.refs_7_ = bf16[48,4224]{1,0:T(8,128)(2,1)S(1)} collective-permute-done((bf16[48,4224]{1,0:T(8,128)(2,1)S(1)}, bf16[48,4224]{1,0:T(8,128)(2,1)S(1)}, u32[]{:S(2)}, u32[]{:S(2)}) %collective-permute-start.5) | collective-permute-done | bytes 405536 | tf_op jit(solution)/shard_map/ppermute | solution.py:46
  35.7 2.5 %collective-permute-done.6.refs_8_ = bf16[48,4224]{1,0:T(8,128)(2,1)S(1)} collective-permute-done((bf16[48,4224]{1,0:T(8,128)(2,1)S(1)}, bf16[48,4224]{1,0:T(8,128)(2,1)S(1)}, u32[]{:S(2)}, u32[]{:S(2)}) %collective-permute-start.6) | collective-permute-done | bytes 405536 | tf_op jit(solution)/shard_map/ppermute | solution.py:47
  38.3 1.7 %collective-permute-done.8.refs_10_ = bf16[48,4224]{1,0:T(8,128)(2,1)S(1)} collective-permute-done((bf16[48,4224]{1,0:T(8,128)(2,1)S(1)}, bf16[48,4224]{1,0:T(8,128)(2,1)S(1)}, u32[]{:S(2)}, u32[]{:S(2)}) %collective-permute-start.8) | collective-permute-done | bytes 405536 | tf_op jit(solution)/shard_map/ppermute | solution.py:53
  40.0 2.0 %shard_map.38.refs_11_ = f32[1,96]{1,0:T(1,128)S(1)} custom-call(bf16[96,4224]{1,0:T(8,128)(2,1)S(1)} %shard_map.37.refs_0_.refs_1_.own_ref, bf16[96,4224]{1,0:T(8,128)(2,1)S(1)} %shard_map.37.refs_0_.refs_1_.own_ref, bf16[96,4224]{1,0:T(8,128)(2,1)S(1)} %collective-permute-done.refs_2_.other_ref, bf16[96,4224]{1,0:T(8,128)(2,1)S(1)} %collective-permute-done.1.refs_3_, ...), custom_call_target="tpu_custom_call" | custom-call | flops 603979776 | bytes 7077888 | tf_op jit(solution)/shard_map/pallas_call | solution.py:168
  42.0 6.5 %collective-permute-done.9.refs_0_ = bf16[192,4224]{1,0:T(8,128)(2,1)S(1)} collective-permute-done((bf16[192,4224]{1,0:T(8,128)(2,1)S(1)}, bf16[192,4224]{1,0:T(8,128)(2,1)S(1)}, u32[]{:S(2)}, u32[]{:S(2)}) %collective-permute-start.9) | collective-permute-done | bytes 1622048 | tf_op jit(solution)/shard_map/ppermute | solution.py:196
  48.5 2.2 %shard_map.40 = (f32[1,192]{1,0:T(1,128)S(1)}, f32[4,128]{1,0:T(4,128)S(1)}, f32[4,128]{1,0:T(4,128)S(1)}) custom-call(bf16[192,4224]{1,0:T(8,128)(2,1)S(1)} %collective-permute-done.9.refs_0_, bf16[96,4224]{1,0:T(8,128)(2,1)S(1)} %shard_map.37.refs_0_.refs_1_.own_ref, bf16[96,4224]{1,0:T(8,128)(2,1)S(1)} %collective-permute-done.refs_2_.other_ref, ...), custom_call_target="tpu_custom_call" | custom-call | flops 1207959552 | bytes 7864320 | tf_op jit(solution)/shard_map/pallas_call | solution.py:168
  50.8 1.0 %collective-permute-start.10 = (f32[4,128]{1,0:T(4,128)S(1)}, f32[4,128]{1,0:T(4,128)S(1)}, u32[]{:S(2)}, u32[]{:S(2)}) collective-permute-start(f32[4,128]{1,0:T(4,128)S(1)} %get-tuple-element.9), channel_id=1, source_target_pairs={{0,16},{8,24},{16,0},{24,8},{1,17},{9,25},{17,1},{25,9},{2,18},{10... | collective-permute-start | bytes 6152 | tf_op jit(solution)/shard_map/ppermute | solution.py:224
  51.8 1.9 %collective-permute-start.12 = (f32[1,192]{1,0:T(1,128)S(1)}, f32[1,192]{1,0:T(1,128)S(1)}, u32[]{:S(2)}, u32[]{:S(2)}) collective-permute-start(f32[1,192]{1,0:T(1,128)S(1)} %get-tuple-element.10), channel_id=1, source_target_pairs={{2,0},{4,2},{6,4},{0,6},{5,1},{3,7},{10,8},{12,10},{14,12},{8,14},... | collective-permute-start | bytes 2312 | tf_op jit(solution)/shard_map/ppermute | solution.py:234
  53.7 0.7 %collective-permute-done.10 = f32[4,128]{1,0:T(4,128)S(1)} collective-permute-done((f32[4,128]{1,0:T(4,128)S(1)}, f32[4,128]{1,0:T(4,128)S(1)}, u32[]{:S(2)}, u32[]{:S(2)}) %collective-permute-start.10) | collective-permute-done | bytes 2080 | tf_op jit(solution)/shard_map/ppermute | solution.py:224
  54.4 1.0 %collective-permute-start.11 = (f32[4,128]{1,0:T(4,128)S(1)}, f32[4,128]{1,0:T(4,128)S(1)}, u32[]{:S(2)}, u32[]{:S(2)}) collective-permute-start(f32[4,128]{1,0:T(4,128)S(1)} %max.18), channel_id=1, source_target_pairs={{0,8},{8,0},{16,24},{24,16},{1,9},{9,1},{17,25},{25,17},{2,10},{10... | collective-permute-start | bytes 6152 | tf_op jit(solution)/shard_map/ppermute | solution.py:229
  55.4 1.9 %collective-permute-done.12 = f32[1,192]{1,0:T(1,128)S(1)} collective-permute-done((f32[1,192]{1,0:T(1,128)S(1)}, f32[1,192]{1,0:T(1,128)S(1)}, u32[]{:S(2)}, u32[]{:S(2)}) %collective-permute-start.12) | collective-permute-done | bytes 800 | tf_op jit(solution)/shard_map/ppermute | solution.py:234
  57.3 0.7 %collective-permute-done.11 = f32[4,128]{1,0:T(4,128)S(1)} collective-permute-done((f32[4,128]{1,0:T(4,128)S(1)}, f32[4,128]{1,0:T(4,128)S(1)}, u32[]{:S(2)}, u32[]{:S(2)}) %collective-permute-start.11) | collective-permute-done | bytes 2080 | tf_op jit(solution)/shard_map/ppermute | solution.py:229
  58.1 1.1 %collective-permute-done.13 = f32[1,96]{1,0:T(1,128)S(1)} collective-permute-done((f32[1,96]{1,0:T(1,128)S(1)}, f32[1,96]{1,0:T(1,128)S(1)}, u32[]{:S(2)}, u32[]{:S(2)}) %collective-permute-start.13) | collective-permute-done | bytes 416 | tf_op jit(solution)/shard_map/ppermute | solution.py:53
  59.2 0.6 fusion.3
  (20 shorter events, 1.1 us)
Async XLA Ops:
  1.3 1.1 %copy-start = (bf16[96,4096]{1,0:T(8,128)(2,1)S(1)}, bf16[96,4096]{1,0:T(8,128)(2,1)}, u32[]{:S(2)}) copy-start(bf16[96,4096]{1,0:T(8,128)(2,1)} %rows_ref.1) | copy-start | bytes 2359300
  2.8 4.6 %collective-permute-start = (bf16[96,4224]{1,0:T(8,128)(2,1)S(1)}, bf16[96,4224]{1,0:T(8,128)(2,1)S(1)}, u32[]{:S(2)}, u32[]{:S(2)}) collective-permute-start(bf16[96,4224]{1,0:T(8,128)(2,1)S(1)} %shard_map.37.refs_0_.refs_1_.own_ref), channel_id=1, source_target_pairs={{0,1},{1,0},{2,3},{3,2},{4,5},{5,4},{6,7},{7,6},{8,9},{9,8},{10,11... | collective-permute-start | bytes 2433032 | tf_op jit(solution)/shard_map/ppermute | solution.py:53
  3.3 21.2 %collective-permute-start.1 = (bf16[96,4224]{1,0:T(8,128)(2,1)S(1)}, bf16[96,4224]{1,0:T(8,128)(2,1)S(1)}, u32[]{:S(2)}, u32[]{:S(2)}) collective-permute-start(bf16[96,4224]{1,0:T(8,128)(2,1)S(1)} %shard_map.37.refs_0_.refs_1_.own_ref), channel_id=1, source_target_pairs={{0,8},{8,0},{16,24},{24,16},{1,9},{9,1},{17,25},{25,17},{2,10},{10... | collective-permute-start | bytes 2433032 | tf_op jit(solution)/shard_map/ppermute | solution.py:40
  5.8 20.6 %collective-permute-start.3 = (bf16[96,4224]{1,0:T(8,128)(2,1)S(1)}, bf16[96,4224]{1,0:T(8,128)(2,1)S(1)}, u32[]{:S(2)}, u32[]{:S(2)}) collective-permute-start(bf16[96,4224]{1,0:T(8,128)(2,1)S(1)} %shard_map.37.refs_0_.refs_1_.own_ref), channel_id=1, source_target_pairs={{0,16},{8,24},{16,0},{24,8},{1,17},{9,25},{17,1},{25,9},{2,18},{10... | collective-permute-start | bytes 2433032 | tf_op jit(solution)/shard_map/ppermute | solution.py:40
  7.5 41.0 %collective-permute-start.9 = (bf16[192,4224]{1,0:T(8,128)(2,1)S(1)}, bf16[192,4224]{1,0:T(8,128)(2,1)S(1)}, u32[]{:S(2)}, u32[]{:S(2)}) collective-permute-start(bf16[192,4224]{1,0:T(8,128)(2,1)S(1)} %shard_map.39), channel_id=1, source_target_pairs={{0,2},{2,4},{4,6},{6,0},{1,5},{7,3},{8,10},{10,12},{12,14},{14,8},... | collective-permute-start | bytes 4866056 | tf_op jit(solution)/shard_map/ppermute | solution.py:196
  24.5 11.2 %collective-permute-start.5 = (bf16[48,4224]{1,0:T(8,128)(2,1)S(1)}, bf16[48,4224]{1,0:T(8,128)(2,1)S(1)}, u32[]{:S(2)}, u32[]{:S(2)}) collective-permute-start(bf16[48,4224]{1,0:T(8,128)(2,1)S(1)} %slice.32), channel_id=1, source_target_pairs={{0,16},{8,24},{16,0},{24,8},{1,17},{9,25},{17,1},{25,9},{2,18},{10... | collective-permute-start | bytes 1216520 | tf_op jit(solution)/shard_map/ppermute | solution.py:46
  26.4 11.9 %collective-permute-start.2 = (bf16[96,4224]{1,0:T(8,128)(2,1)S(1)}, bf16[96,4224]{1,0:T(8,128)(2,1)S(1)}, u32[]{:S(2)}, u32[]{:S(2)}) collective-permute-start(bf16[96,4224]{1,0:T(8,128)(2,1)S(1)} %collective-permute-done.1.refs_3_), channel_id=1, source_target_pairs={{0,1},{1,0},{2,3},{3,2},{4,5},{5,4},{6,7},{7,6},{8,9},{9,8},{10,11... | collective-permute-start | bytes 2433032 | tf_op jit(solution)/shard_map/ppermute | solution.py:53
  26.4 11.9 %collective-permute-start.4 = (bf16[96,4224]{1,0:T(8,128)(2,1)S(1)}, bf16[96,4224]{1,0:T(8,128)(2,1)S(1)}, u32[]{:S(2)}, u32[]{:S(2)}) collective-permute-start(bf16[96,4224]{1,0:T(8,128)(2,1)S(1)} %collective-permute-done.3.refs_5_), channel_id=1, source_target_pairs={{0,1},{1,0},{2,3},{3,2},{4,5},{5,4},{6,7},{7,6},{8,9},{9,8},{10,11... | collective-permute-start | bytes 2433032 | tf_op jit(solution)/shard_map/ppermute | solution.py:53
  26.9 11.4 %collective-permute-start.6 = (bf16[48,4224]{1,0:T(8,128)(2,1)S(1)}, bf16[48,4224]{1,0:T(8,128)(2,1)S(1)}, u32[]{:S(2)}, u32[]{:S(2)}) collective-permute-start(bf16[48,4224]{1,0:T(8,128)(2,1)S(1)} %slice.33), channel_id=1, source_target_pairs={{0,8},{8,0},{16,24},{24,16},{1,9},{9,1},{17,25},{25,17},{2,10},{10... | collective-permute-start | bytes 1216520 | tf_op jit(solution)/shard_map/ppermute | solution.py:47
  35.7 2.6 %collective-permute-start.7 = (bf16[48,4224]{1,0:T(8,128)(2,1)S(1)}, bf16[48,4224]{1,0:T(8,128)(2,1)S(1)}, u32[]{:S(2)}, u32[]{:S(2)}) collective-permute-start(bf16[48,4224]{1,0:T(8,128)(2,1)S(1)} %collective-permute-done.5.refs_7_), channel_id=1, source_target_pairs={{0,1},{1,0},{2,3},{3,2},{4,5},{5,4},{6,7},{7,6},{8,9},{9,8},{10,11... | collective-permute-start | bytes 1216520 | tf_op jit(solution)/shard_map/ppermute | solution.py:53
  38.3 1.7 %collective-permute-start.8 = (bf16[48,4224]{1,0:T(8,128)(2,1)S(1)}, bf16[48,4224]{1,0:T(8,128)(2,1)S(1)}, u32[]{:S(2)}, u32[]{:S(2)}) collective-permute-start(bf16[48,4224]{1,0:T(8,128)(2,1)S(1)} %collective-permute-done.6.refs_8_), channel_id=1, source_target_pairs={{0,1},{1,0},{2,3},{3,2},{4,5},{5,4},{6,7},{7,6},{8,9},{9,8},{10,11... | collective-permute-start | bytes 1216520 | tf_op jit(solution)/shard_map/ppermute | solution.py:53
  50.8 3.6 %collective-permute-start.10 = (f32[4,128]{1,0:T(4,128)S(1)}, f32[4,128]{1,0:T(4,128)S(1)}, u32[]{:S(2)}, u32[]{:S(2)}) collective-permute-start(f32[4,128]{1,0:T(4,128)S(1)} %get-tuple-element.9), channel_id=1, source_target_pairs={{0,16},{8,24},{16,0},{24,8},{1,17},{9,25},{17,1},{25,9},{2,18},{10... | collective-permute-start | bytes 6152 | tf_op jit(solution)/shard_map/ppermute | solution.py:224
  51.8 5.5 %collective-permute-start.12 = (f32[1,192]{1,0:T(1,128)S(1)}, f32[1,192]{1,0:T(1,128)S(1)}, u32[]{:S(2)}, u32[]{:S(2)}) collective-permute-start(f32[1,192]{1,0:T(1,128)S(1)} %get-tuple-element.10), channel_id=1, source_target_pairs={{2,0},{4,2},{6,4},{0,6},{5,1},{3,7},{10,8},{12,10},{14,12},{8,14},... | collective-permute-start | bytes 2312 | tf_op jit(solution)/shard_map/ppermute | solution.py:234
  54.4 3.6 %collective-permute-start.11 = (f32[4,128]{1,0:T(4,128)S(1)}, f32[4,128]{1,0:T(4,128)S(1)}, u32[]{:S(2)}, u32[]{:S(2)}) collective-permute-start(f32[4,128]{1,0:T(4,128)S(1)} %max.18), channel_id=1, source_target_pairs={{0,8},{8,0},{16,24},{24,16},{1,9},{9,1},{17,25},{25,17},{2,10},{10... | collective-permute-start | bytes 6152 | tf_op jit(solution)/shard_map/ppermute | solution.py:229
  58.1 1.1 %collective-permute-start.13 = (f32[1,96]{1,0:T(1,128)S(1)}, f32[1,96]{1,0:T(1,128)S(1)}, u32[]{:S(2)}, u32[]{:S(2)}) collective-permute-start(f32[1,96]{1,0:T(1,128)S(1)} %fusion.2), channel_id=1, source_target_pairs={{0,1},{1,0},{2,3},{3,2},{4,5},{5,4},{6,7},{7,6},{8,9},{9,8},{10,11... | collective-permute-start | bytes 1160 | tf_op jit(solution)/shard_map/ppermute | solution.py:53

commit v13 on v11

--- a/solution.py
+++ b/solution.py
@@ -11,7 +11,6 @@
 LANES = 128
 CHUNK = 512
 CALL = 8
-PARTS = 3
 VMEM = pl.BlockSpec(memory_space=pltpu.VMEM)
 
 
@@ -54,60 +53,33 @@
     return lax.ppermute(block, "core", flip(2, 1))
 
 
-def pack_kernel(rows_ref, cluster_ref, order_ref, block_ref, raw, ids, arrived):
-    rows, width = raw.shape
-    step = rows // PARTS
-    parts = [pl.ds(index * step, step) for index in range(PARTS)]
-    copies = [
-        pltpu.make_async_copy(cluster_ref, ids.at[0], arrived.at[PARTS]),
-        pltpu.make_async_copy(order_ref, ids.at[1], arrived.at[PARTS + 1]),
-    ]
-    for index, part in enumerate(parts):
-        copies.append(
-            pltpu.make_async_copy(rows_ref.at[part], raw.at[part], arrived.at[index])
-        )
-    for copy in copies:
-        copy.start()
-    for copy in copies[:2]:
-        copy.wait()
-    meta = jnp.concatenate(
-        [
-            ids[0].astype(jnp.float32) + 1.0,
-            ids[1].astype(jnp.float32),
-            jnp.zeros((6, rows), jnp.float32),
-        ],
-        axis=0,
-    )
+def pack_kernel(rows_ref, ids_ref, block_ref):
+    rows, width = rows_ref.shape
+    block_ref[:, :width] = unit_rows(rows_ref[...])
+    ids = ids_ref[...].astype(jnp.float32)
+    meta = jnp.concatenate([ids, jnp.zeros((6, rows), jnp.float32)], axis=0)
     if rows < LANES:
         meta = jnp.concatenate([meta, jnp.zeros((8, LANES - rows), jnp.float32)], axis=1)
     turned = meta.T[:rows]
-    cluster, order = turned[:, 0:1], turned[:, 1:2]
+    cluster, order = turned[:, 0:1] + 1.0, turned[:, 1:2]
     high = jnp.floor(order / 256.0)
     lane = lax.broadcasted_iota(jnp.int32, (rows, LANES), 1)
     tail = jnp.where(lane == 0, cluster, jnp.where(lane == 1, high, order - 256.0 * high))
     block_ref[:, width:] = jnp.where(lane < 3, tail, 0.0).astype(jnp.bfloat16)
-    for part, copy in zip(parts, copies[2:]):
-        copy.wait()
-        block_ref[part, :width] = unit_rows(raw[part])
 
 
 def pack(rows, cluster_ids, order_index):
     count, width = rows.shape
     return pl.pallas_call(
         pack_kernel,
-        in_specs=[pl.BlockSpec(memory_space=pl.ANY)] * 3,
+        in_specs=[VMEM] * 2,
         out_specs=VMEM,
         out_shape=jax.ShapeDtypeStruct((count, width + LANES), jnp.bfloat16),
-        scratch_shapes=[
-            pltpu.VMEM((count, width), jnp.bfloat16),
-            pltpu.VMEM((2, 1, count), jnp.int32),
-            pltpu.SemaphoreType.DMA((PARTS + 2,)),
-        ],
         compiler_params=pltpu.CompilerParams(vmem_limit_bytes=8 * 2**20),
         cost_estimate=pl.CostEstimate(
             flops=4 * count * width, bytes_accessed=4 * count * width, transcendentals=count
         ),
-    )(rows, cluster_ids.reshape(1, count), order_index.reshape(1, count))
+    )(rows, jnp.stack([cluster_ids, order_index]))
 
 
 def pair_kernel(own_ref, other_ref, both_ref):

time: 59.9 us -> 58.8 us (0.982)
  local copies, waits for them, and re-layouts: 3.01 us -> 1.7 us
  other arithmetic: 0.02 us -> 0.7 us
    unnamed x6 -> x2, local copies, waits for them, and re-layouts: 2.44 us -> 1.13 us
    another operation x0 -> x1, other arithmetic: none -> 0.68 us  [pack(): jnp.stack([cluster_ids, order_index])]
where the time goes in v13:
time: 58.8 us; the launch traced here: 58.6 us
  waiting for transfers between devices  34.1 us (58%)
  starting transfers between devices  17.7 us (30%)
  Pallas kernels  4.28 us (7%)
  local copies, waits for them, and re-layouts  1.7 us (3%)
  other arithmetic  0.7 us (1%)
    ppermute x2, waiting for transfers between devices, gather_plane(): blocks[s] = [lax.ppermute(block, 'group', flip(groups, s))]  13.5 us
    ppermute x1, waiting for transfers between devices, gather_plane(): lax.ppermute(top, 'group', flip(groups, high))  7.25 us
    ppermute x1, waiting for transfers between devices, local(): visitors = [lax.ppermute(both, ('z', 'core'), trip) for trip in trips]  6.7 us
    ppermute x2, starting transfers between devices, gather_plane(): blocks[s] = [lax.ppermute(block, 'group', flip(groups, s))]  4.08 us
    pallas_call x2, Pallas kernels, call(): pl.pallas_call(kernel, in_specs=[VMEM] * len(operands), out_specs=[VMEM]...  3.87 us
    ppermute x3, starting transfers between devices, local(): got = lax.ppermute(merged, 'group', flip(groups, s)) if s else merged  3.55 us
    ppermute x1, starting transfers between devices, local(): visitors = [lax.ppermute(both, ('z', 'core'), trip) for trip in trips]  3.48 us
    ppermute x7, waiting for transfers between devices, swap(): return lax.ppermute(block, 'core', flip(2, 1))  2.69 us
  transfers between devices with their start and end apart: 16, of which 8 were waited for; matrix products, arithmetic and copies ran while one was open for 0% of the time, Pallas kernels for 3%

profile of v13, /device:TPU:0, one launch (start us, length us, event | category | flops | bytes accessed | tf_op | source)
XLA Modules:
  0.0 58.6 jit_solution(5807403854552619269)
XLA Ops:
  0.0 0.7 %pad_add_fusion.ids_ref = s32[2,96]{1,0:T(2,128)S(1)} fusion(s32[1,96]{1,0:T(1,128)} %bitcast.4, s32[1,96]{1,0:T(1,128)} %bitcast.5), kind=kLoop, calls=%fused_computation | loop fusion | flops 192 | bytes 1536 | tf_op jit(solution)/shard_map/stack | solution.py:82
  0.7 1.1 %copy-done = bf16[96,4096]{1,0:T(8,128)(2,1)S(1)} copy-done((bf16[96,4096]{1,0:T(8,128)(2,1)S(1)}, bf16[96,4096]{1,0:T(8,128)(2,1)}, u32[]{:S(2)}) %copy-start) | copy-done | bytes 786456
  2.1 0.5 collective-permute-start
  2.6 2.6 %collective-permute-start.1 = (bf16[96,4224]{1,0:T(8,128)(2,1)S(1)}, bf16[96,4224]{1,0:T(8,128)(2,1)S(1)}, u32[]{:S(2)}, u32[]{:S(2)}) collective-permute-start(bf16[96,4224]{1,0:T(8,128)(2,1)S(1)} %shard_map.37.refs_0_.refs_1_.own_ref), channel_id=1, source_target_pairs={{0,8},{8,0},{16,24},{24,16},{1,9},{9,1},{17,25},{25,17},{2,10},{10... | collective-permute-start | bytes 2433032 | tf_op jit(solution)/shard_map/ppermute | solution.py:40
  5.2 1.5 %collective-permute-start.3 = (bf16[96,4224]{1,0:T(8,128)(2,1)S(1)}, bf16[96,4224]{1,0:T(8,128)(2,1)S(1)}, u32[]{:S(2)}, u32[]{:S(2)}) collective-permute-start(bf16[96,4224]{1,0:T(8,128)(2,1)S(1)} %shard_map.37.refs_0_.refs_1_.own_ref), channel_id=1, source_target_pairs={{0,16},{8,24},{16,0},{24,8},{1,17},{9,25},{17,1},{25,9},{2,18},{10... | collective-permute-start | bytes 2433032 | tf_op jit(solution)/shard_map/ppermute | solution.py:40
  6.8 3.5 %collective-permute-start.9 = (bf16[192,4224]{1,0:T(8,128)(2,1)S(1)}, bf16[192,4224]{1,0:T(8,128)(2,1)S(1)}, u32[]{:S(2)}, u32[]{:S(2)}) collective-permute-start(bf16[192,4224]{1,0:T(8,128)(2,1)S(1)} %shard_map.39), channel_id=1, source_target_pairs={{0,2},{2,4},{4,6},{6,0},{1,5},{7,3},{8,10},{10,12},{12,14},{14,8},... | collective-permute-start | bytes 4866056 | tf_op jit(solution)/shard_map/ppermute | solution.py:204
  10.3 13.5 %collective-permute-done.1.refs_3_ = bf16[96,4224]{1,0:T(8,128)(2,1)S(1)} collective-permute-done((bf16[96,4224]{1,0:T(8,128)(2,1)S(1)}, bf16[96,4224]{1,0:T(8,128)(2,1)S(1)}, u32[]{:S(2)}, u32[]{:S(2)}) %collective-permute-start.1) | collective-permute-done | bytes 811040 | tf_op jit(solution)/shard_map/ppermute | solution.py:40
  23.9 1.9 %collective-permute-start.5 = (bf16[48,4224]{1,0:T(8,128)(2,1)S(1)}, bf16[48,4224]{1,0:T(8,128)(2,1)S(1)}, u32[]{:S(2)}, u32[]{:S(2)}) collective-permute-start(bf16[48,4224]{1,0:T(8,128)(2,1)S(1)} %slice.44), channel_id=1, source_target_pairs={{0,16},{8,24},{16,0},{24,8},{1,17},{9,25},{17,1},{25,9},{2,18},{10... | collective-permute-start | bytes 1216520 | tf_op jit(solution)/shard_map/ppermute | solution.py:46
  25.8 0.5 collective-permute-start.4
  26.3 1.6 %collective-permute-start.6 = (bf16[48,4224]{1,0:T(8,128)(2,1)S(1)}, bf16[48,4224]{1,0:T(8,128)(2,1)S(1)}, u32[]{:S(2)}, u32[]{:S(2)}) collective-permute-start(bf16[48,4224]{1,0:T(8,128)(2,1)S(1)} %slice.45), channel_id=1, source_target_pairs={{0,8},{8,0},{16,24},{24,16},{1,9},{9,1},{17,25},{25,17},{2,10},{10... | collective-permute-start | bytes 1216520 | tf_op jit(solution)/shard_map/ppermute | solution.py:47
  27.8 7.2 %collective-permute-done.5.refs_7_ = bf16[48,4224]{1,0:T(8,128)(2,1)S(1)} collective-permute-done((bf16[48,4224]{1,0:T(8,128)(2,1)S(1)}, bf16[48,4224]{1,0:T(8,128)(2,1)S(1)}, u32[]{:S(2)}, u32[]{:S(2)}) %collective-permute-start.5) | collective-permute-done | bytes 405536 | tf_op jit(solution)/shard_map/ppermute | solution.py:46
  35.1 2.5 %collective-permute-done.6.refs_8_ = bf16[48,4224]{1,0:T(8,128)(2,1)S(1)} collective-permute-done((bf16[48,4224]{1,0:T(8,128)(2,1)S(1)}, bf16[48,4224]{1,0:T(8,128)(2,1)S(1)}, u32[]{:S(2)}, u32[]{:S(2)}) %collective-permute-start.6) | collective-permute-done | bytes 405536 | tf_op jit(solution)/shard_map/ppermute | solution.py:47
  37.7 1.7 %collective-permute-done.8.refs_10_ = bf16[48,4224]{1,0:T(8,128)(2,1)S(1)} collective-permute-done((bf16[48,4224]{1,0:T(8,128)(2,1)S(1)}, bf16[48,4224]{1,0:T(8,128)(2,1)S(1)}, u32[]{:S(2)}, u32[]{:S(2)}) %collective-permute-start.8) | collective-permute-done | bytes 405536 | tf_op jit(solution)/shard_map/ppermute | solution.py:53
  39.4 1.8 %shard_map.38.refs_11_ = f32[1,128]{1,0:T(1,128)S(1)} custom-call(bf16[96,4224]{1,0:T(8,128)(2,1)S(1)} %shard_map.37.refs_0_.refs_1_.own_ref, bf16[96,4224]{1,0:T(8,128)(2,1)S(1)} %shard_map.37.refs_0_.refs_1_.own_ref, bf16[96,4224]{1,0:T(8,128)(2,1)S(1)} %collective-permute-done.refs_2_.other_ref, bf16[96,4224]{1,0:T(8,128)(2,1)S(1)} %collective-permute-done.1.refs_3_, ...), custom_call_target="tpu_custom_call" | custom-call | flops 805306368 | bytes 7340032 | tf_op jit(solution)/shard_map/pallas_call | solution.py:173
  41.2 6.7 %collective-permute-done.9.refs_0_ = bf16[192,4224]{1,0:T(8,128)(2,1)S(1)} collective-permute-done((bf16[192,4224]{1,0:T(8,128)(2,1)S(1)}, bf16[192,4224]{1,0:T(8,128)(2,1)S(1)}, u32[]{:S(2)}, u32[]{:S(2)}) %collective-permute-start.9) | collective-permute-done | bytes 1622048 | tf_op jit(solution)/shard_map/ppermute | solution.py:204
  47.9 2.1 %shard_map.40 = (f32[2,128]{1,0:T(2,128)S(1)}, f32[4,128]{1,0:T(4,128)S(1)}, f32[4,128]{1,0:T(4,128)S(1)}) custom-call(bf16[192,4224]{1,0:T(8,128)(2,1)S(1)} %collective-permute-done.9.refs_0_, bf16[96,4224]{1,0:T(8,128)(2,1)S(1)} %shard_map.37.refs_0_.refs_1_.own_ref, bf16[96,4224]{1,0:T(8,128)(2,1)S(1)} %collective-permute-done.refs_2_.other_ref, ...), custom_call_target="tpu_custom_call" | custom-call | flops 1610612736 | bytes 8388608 | tf_op jit(solution)/shard_map/pallas_call | solution.py:173
  50.0 1.9 %collective-permute-start.10 = (f32[2,128]{1,0:T(2,128)S(1)}, f32[2,128]{1,0:T(2,128)S(1)}, u32[]{:S(2)}, u32[]{:S(2)}) collective-permute-start(f32[2,128]{1,0:T(2,128)S(1)} %get-tuple-element.8), channel_id=1, source_target_pairs={{2,0},{4,2},{6,4},{0,6},{5,1},{3,7},{10,8},{12,10},{14,12},{8,14},... | collective-permute-start | bytes 3080 | tf_op jit(solution)/shard_map/ppermute | solution.py:230
  52.0 2.0 %collective-permute-start.15 = (f32[4,128]{1,0:T(4,128)S(1)}, f32[4,128]{1,0:T(4,128)S(1)}, u32[]{:S(2)}, u32[]{:S(2)}) collective-permute-start(f32[4,128]{1,0:T(4,128)S(1)} %max.23), channel_id=1, source_target_pairs={{0,24},{8,16},{16,8},{24,0},{1,25},{9,17},{17,9},{25,1},{2,26},{10... | collective-permute-start | bytes 6152 | tf_op jit(solution)/shard_map/ppermute | solution.py:238
  54.0 0.5 collective-permute-start.14
  54.5 1.1 %collective-permute-start.13 = (f32[4,128]{1,0:T(4,128)S(1)}, f32[4,128]{1,0:T(4,128)S(1)}, u32[]{:S(2)}, u32[]{:S(2)}) collective-permute-start(f32[4,128]{1,0:T(4,128)S(1)} %max.23), channel_id=1, source_target_pairs={{0,8},{8,0},{16,24},{24,16},{1,9},{9,1},{17,25},{25,17},{2,10},{10... | collective-permute-start | bytes 6152 | tf_op jit(solution)/shard_map/ppermute | solution.py:238
  55.7 1.0 %collective-permute-done.11 = f32[2,128]{1,0:T(2,128)S(1)} collective-permute-done((f32[2,128]{1,0:T(2,128)S(1)}, f32[2,128]{1,0:T(2,128)S(1)}, u32[]{:S(2)}, u32[]{:S(2)}) %collective-permute-start.11) | collective-permute-done | bytes 1056 | tf_op jit(solution)/shard_map/ppermute | solution.py:53
  56.7 0.9 %collective-permute-done.14 = f32[4,128]{1,0:T(4,128)S(1)} collective-permute-done((f32[4,128]{1,0:T(4,128)S(1)}, f32[4,128]{1,0:T(4,128)S(1)}, u32[]{:S(2)}, u32[]{:S(2)}) %collective-permute-start.14) | collective-permute-done | bytes 2080 | tf_op jit(solution)/shard_map/ppermute | solution.py:238
  57.5 0.5 collective-permute-done.13
  58.1 0.5 slice_bitcast_fusion
  (20 shorter events, 0.7 us)
Async XLA Ops:
  0.7 1.1 %copy-start = (bf16[96,4096]{1,0:T(8,128)(2,1)S(1)}, bf16[96,4096]{1,0:T(8,128)(2,1)}, u32[]{:S(2)}) copy-start(bf16[96,4096]{1,0:T(8,128)(2,1)} %rows_ref.1) | copy-start | bytes 2359300
  2.1 4.6 %collective-permute-start = (bf16[96,4224]{1,0:T(8,128)(2,1)S(1)}, bf16[96,4224]{1,0:T(8,128)(2,1)S(1)}, u32[]{:S(2)}, u32[]{:S(2)}) collective-permute-start(bf16[96,4224]{1,0:T(8,128)(2,1)S(1)} %shard_map.37.refs_0_.refs_1_.own_ref), channel_id=1, source_target_pairs={{0,1},{1,0},{2,3},{3,2},{4,5},{5,4},{6,7},{7,6},{8,9},{9,8},{10,11... | collective-permute-start | bytes 2433032 | tf_op jit(solution)/shard_map/ppermute | solution.py:53
  2.6 21.2 %collective-permute-start.1 = (bf16[96,4224]{1,0:T(8,128)(2,1)S(1)}, bf16[96,4224]{1,0:T(8,128)(2,1)S(1)}, u32[]{:S(2)}, u32[]{:S(2)}) collective-permute-start(bf16[96,4224]{1,0:T(8,128)(2,1)S(1)} %shard_map.37.refs_0_.refs_1_.own_ref), channel_id=1, source_target_pairs={{0,8},{8,0},{16,24},{24,16},{1,9},{9,1},{17,25},{25,17},{2,10},{10... | collective-permute-start | bytes 2433032 | tf_op jit(solution)/shard_map/ppermute | solution.py:40
  5.2 20.6 %collective-permute-start.3 = (bf16[96,4224]{1,0:T(8,128)(2,1)S(1)}, bf16[96,4224]{1,0:T(8,128)(2,1)S(1)}, u32[]{:S(2)}, u32[]{:S(2)}) collective-permute-start(bf16[96,4224]{1,0:T(8,128)(2,1)S(1)} %shard_map.37.refs_0_.refs_1_.own_ref), channel_id=1, source_target_pairs={{0,16},{8,24},{16,0},{24,8},{1,17},{9,25},{17,1},{25,9},{2,18},{10... | collective-permute-start | bytes 2433032 | tf_op jit(solution)/shard_map/ppermute | solution.py:40
  6.8 41.0 %collective-permute-start.9 = (bf16[192,4224]{1,0:T(8,128)(2,1)S(1)}, bf16[192,4224]{1,0:T(8,128)(2,1)S(1)}, u32[]{:S(2)}, u32[]{:S(2)}) collective-permute-start(bf16[192,4224]{1,0:T(8,128)(2,1)S(1)} %shard_map.39), channel_id=1, source_target_pairs={{0,2},{2,4},{4,6},{6,0},{1,5},{7,3},{8,10},{10,12},{12,14},{14,8},... | collective-permute-start | bytes 4866056 | tf_op jit(solution)/shard_map/ppermute | solution.py:204
  23.9 11.2 %collective-permute-start.5 = (bf16[48,4224]{1,0:T(8,128)(2,1)S(1)}, bf16[48,4224]{1,0:T(8,128)(2,1)S(1)}, u32[]{:S(2)}, u32[]{:S(2)}) collective-permute-start(bf16[48,4224]{1,0:T(8,128)(2,1)S(1)} %slice.44), channel_id=1, source_target_pairs={{0,16},{8,24},{16,0},{24,8},{1,17},{9,25},{17,1},{25,9},{2,18},{10... | collective-permute-start | bytes 1216520 | tf_op jit(solution)/shard_map/ppermute | solution.py:46
  25.7 11.9 %collective-permute-start.2 = (bf16[96,4224]{1,0:T(8,128)(2,1)S(1)}, bf16[96,4224]{1,0:T(8,128)(2,1)S(1)}, u32[]{:S(2)}, u32[]{:S(2)}) collective-permute-start(bf16[96,4224]{1,0:T(8,128)(2,1)S(1)} %collective-permute-done.1.refs_3_), channel_id=1, source_target_pairs={{0,1},{1,0},{2,3},{3,2},{4,5},{5,4},{6,7},{7,6},{8,9},{9,8},{10,11... | collective-permute-start | bytes 2433032 | tf_op jit(solution)/shard_map/ppermute | solution.py:53
  25.8 11.9 %collective-permute-start.4 = (bf16[96,4224]{1,0:T(8,128)(2,1)S(1)}, bf16[96,4224]{1,0:T(8,128)(2,1)S(1)}, u32[]{:S(2)}, u32[]{:S(2)}) collective-permute-start(bf16[96,4224]{1,0:T(8,128)(2,1)S(1)} %collective-permute-done.3.refs_5_), channel_id=1, source_target_pairs={{0,1},{1,0},{2,3},{3,2},{4,5},{5,4},{6,7},{7,6},{8,9},{9,8},{10,11... | collective-permute-start | bytes 2433032 | tf_op jit(solution)/shard_map/ppermute | solution.py:53
  26.3 11.4 %collective-permute-start.6 = (bf16[48,4224]{1,0:T(8,128)(2,1)S(1)}, bf16[48,4224]{1,0:T(8,128)(2,1)S(1)}, u32[]{:S(2)}, u32[]{:S(2)}) collective-permute-start(bf16[48,4224]{1,0:T(8,128)(2,1)S(1)} %slice.45), channel_id=1, source_target_pairs={{0,8},{8,0},{16,24},{24,16},{1,9},{9,1},{17,25},{25,17},{2,10},{10... | collective-permute-start | bytes 1216520 | tf_op jit(solution)/shard_map/ppermute | solution.py:47
  35.1 2.6 %collective-permute-start.7 = (bf16[48,4224]{1,0:T(8,128)(2,1)S(1)}, bf16[48,4224]{1,0:T(8,128)(2,1)S(1)}, u32[]{:S(2)}, u32[]{:S(2)}) collective-permute-start(bf16[48,4224]{1,0:T(8,128)(2,1)S(1)} %collective-permute-done.5.refs_7_), channel_id=1, source_target_pairs={{0,1},{1,0},{2,3},{3,2},{4,5},{5,4},{6,7},{7,6},{8,9},{9,8},{10,11... | collective-permute-start | bytes 1216520 | tf_op jit(solution)/shard_map/ppermute | solution.py:53
  37.6 1.7 %collective-permute-start.8 = (bf16[48,4224]{1,0:T(8,128)(2,1)S(1)}, bf16[48,4224]{1,0:T(8,128)(2,1)S(1)}, u32[]{:S(2)}, u32[]{:S(2)}) collective-permute-start(bf16[48,4224]{1,0:T(8,128)(2,1)S(1)} %collective-permute-done.6.refs_8_), channel_id=1, source_target_pairs={{0,1},{1,0},{2,3},{3,2},{4,5},{5,4},{6,7},{7,6},{8,9},{9,8},{10,11... | collective-permute-start | bytes 1216520 | tf_op jit(solution)/shard_map/ppermute | solution.py:53
  50.0 2.0 %collective-permute-start.12 = (f32[4,128]{1,0:T(4,128)S(1)}, f32[4,128]{1,0:T(4,128)S(1)}, u32[]{:S(2)}, u32[]{:S(2)}) collective-permute-start(f32[4,128]{1,0:T(4,128)S(1)} %get-tuple-element.10), channel_id=1, source_target_pairs={{0,1},{1,0},{2,3},{3,2},{4,5},{5,4},{6,7},{7,6},{8,9},{9,8},{10,11... | collective-permute-start | bytes 6152 | tf_op jit(solution)/shard_map/ppermute | solution.py:53
  50.0 5.5 %collective-permute-start.10 = (f32[2,128]{1,0:T(2,128)S(1)}, f32[2,128]{1,0:T(2,128)S(1)}, u32[]{:S(2)}, u32[]{:S(2)}) collective-permute-start(f32[2,128]{1,0:T(2,128)S(1)} %get-tuple-element.8), channel_id=1, source_target_pairs={{2,0},{4,2},{6,4},{0,6},{5,1},{3,7},{10,8},{12,10},{14,12},{8,14},... | collective-permute-start | bytes 3080 | tf_op jit(solution)/shard_map/ppermute | solution.py:230
  52.0 4.7 %collective-permute-start.15 = (f32[4,128]{1,0:T(4,128)S(1)}, f32[4,128]{1,0:T(4,128)S(1)}, u32[]{:S(2)}, u32[]{:S(2)}) collective-permute-start(f32[4,128]{1,0:T(4,128)S(1)} %max.23), channel_id=1, source_target_pairs={{0,24},{8,16},{16,8},{24,0},{1,25},{9,17},{17,9},{25,1},{2,26},{10... | collective-permute-start | bytes 6152 | tf_op jit(solution)/shard_map/ppermute | solution.py:238
  54.0 3.6 %collective-permute-start.14 = (f32[4,128]{1,0:T(4,128)S(1)}, f32[4,128]{1,0:T(4,128)S(1)}, u32[]{:S(2)}, u32[]{:S(2)}) collective-permute-start(f32[4,128]{1,0:T(4,128)S(1)} %max.23), channel_id=1, source_target_pairs={{0,16},{8,24},{16,0},{24,8},{1,17},{9,25},{17,1},{25,9},{2,18},{10... | collective-permute-start | bytes 6152 | tf_op jit(solution)/shard_map/ppermute | solution.py:238
  54.5 3.6 %collective-permute-start.13 = (f32[4,128]{1,0:T(4,128)S(1)}, f32[4,128]{1,0:T(4,128)S(1)}, u32[]{:S(2)}, u32[]{:S(2)}) collective-permute-start(f32[4,128]{1,0:T(4,128)S(1)} %max.23), channel_id=1, source_target_pairs={{0,8},{8,0},{16,24},{24,16},{1,9},{9,1},{17,25},{25,17},{2,10},{10... | collective-permute-start | bytes 6152 | tf_op jit(solution)/shard_map/ppermute | solution.py:238
  55.5 1.1 %collective-permute-start.11 = (f32[2,128]{1,0:T(2,128)S(1)}, f32[2,128]{1,0:T(2,128)S(1)}, u32[]{:S(2)}, u32[]{:S(2)}) collective-permute-start(f32[2,128]{1,0:T(2,128)S(1)} %collective-permute-done.10), channel_id=1, source_target_pairs={{0,1},{1,0},{2,3},{3,2},{4,5},{5,4},{6,7},{7,6},{8,9},{9,8},{10,11... | collective-permute-start | bytes 3080 | tf_op jit(solution)/shard_map/ppermute | solution.py:53

commit v14 on v13

--- a/solution.py
+++ b/solution.py
@@ -114,7 +114,8 @@
     for v, best in enumerate(bests):
         row_ref[v : v + 1, :] = best
     for j, best in enumerate(cols):
-        (mine_ref, other_ref)[j % 2][j // 2 : j // 2 + 1, :] = best
+        place = (lax.axis_index("group") ^ (j // 2)) & (CALL // 2 - 1)
+        (mine_ref, other_ref)[j % 2][place] = best
 
 
 def best_of(visitor_refs, block_refs, rows, homed, units, dots):
@@ -174,7 +175,7 @@
         kernel,
         in_specs=[VMEM] * len(operands),
         out_specs=[VMEM] * len(out_rows),
-        out_shape=[jax.ShapeDtypeStruct((n, LANES), jnp.float32) for n in out_rows],
+        out_shape=[jax.ShapeDtypeStruct((*n, LANES), jnp.float32) for n in out_rows],
         scratch_shapes=[
             pltpu.VMEM((count * LANES, width), jnp.bfloat16),
             pltpu.VMEM((total, count * LANES), jnp.float32),
@@ -217,13 +218,13 @@
     bests, answers = [], []
     for chunk in chunks:
         total = sum(part.shape[0] for part in chunk)
-        bests += call(own_kernel, [own, *chunk], 1, [1], total)
+        bests += call(own_kernel, [own, *chunk], 1, [(1,)], total)
     for index, chunk in enumerate(chunks):
         total = sum(part.shape[0] for part in chunk)
         kernel = functools.partial(visit_kernel, len(visitors), len(chunk))
-        count, half = 2 * len(visitors), total // rows // 2
+        count, pairs = 2 * len(visitors), (CALL // 2, 1)
         operands = [*visitors, *chunk, bests[index]]
-        answers.append(call(kernel, operands, count, [count, half, half], total))
+        answers.append(call(kernel, operands, count, [(count,), pairs, pairs], total))
     home = functools.reduce(jnp.maximum, [answer[0] for answer in answers])
     for index, trip in enumerate(trips):
         part = home[2 * index : 2 * index + 2] if len(trips) > 1 else home
@@ -231,12 +232,12 @@
         for here, best in ((2 * z + core, back), (2 * z + (core ^ 1), swap(back))):
             sent = functools.reduce(jnp.logical_or, [here == a for a, _ in trip])
             bests.append(jnp.where(sent, jnp.where(core == 0, best[0:1], best[1:2]), -1.0))
-    for index, (_, mine, other) in enumerate(answers):
-        merged = jnp.maximum(mine, swap(other))
-        for row in range(CALL // 2):
-            s = index * CALL // 2 + row
-            got = lax.ppermute(merged, "group", flip(groups, s)) if s else merged
-            bests.append(got[row : row + 1])
+    merged = [jnp.maximum(mine, swap(other)) for _, mine, other in answers]
+    if len(merged) > 1:
+        turn = (lax.axis_index("group") // (CALL // 2)) ^ jnp.arange(len(merged))
+        merged = [jnp.stack(merged)[turn].reshape(groups, 1, LANES)]
+    parts = lax.all_to_all(merged[0], "group", split_axis=0, concat_axis=0, tiled=True)
+    bests += [parts[s] for s in range(groups)]
     return functools.reduce(jnp.maximum, bests)[0, :rows]
 
 

time: 58.8 us -> 61.2 us (1.041)
  waiting for transfers between devices: 34.1 us -> 36.3 us
    ppermute x3 -> x0, starting transfers between devices: 3.55 us -> none  [local(): got = lax.ppermute(merged, 'group', flip(groups, s)) if s else merged]
    all_to_all x0 -> x1, waiting for transfers between devices: none -> 3.41 us  [local(): lax.all_to_all(merged[0], 'group', split_axis=0, concat_axis=0, tiled=True)]
    all_to_all x0 -> x1, starting transfers between devices: none -> 3.19 us  [local(): lax.all_to_all(merged[0], 'group', split_axis=0, concat_axis=0, tiled=True)]
    ppermute x3 -> x0, waiting for transfers between devices: 1.38 us -> none  [local(): got = lax.ppermute(merged, 'group', flip(groups, s)) if s else merged]
  transfers between devices with their start and end apart: 16 -> 14, of which waited for: 8 -> 7; matrix products, arithmetic and copies ran while one was open for 0% -> 1% of each run, Pallas kernels for 3% -> 3%
where the time goes in v14:
time: 61.2 us; the launch traced here: 60.9 us
  waiting for transfers between devices  36.3 us (59%)
  starting transfers between devices  17.2 us (28%)
  Pallas kernels  4.28 us (7%)
  local copies, waits for them, and re-layouts  1.7 us (3%)
  other arithmetic  1.27 us (2%)
    ppermute x2, waiting for transfers between devices, gather_plane(): blocks[s] = [lax.ppermute(block, 'group', flip(groups, s))]  13.5 us
    ppermute x1, waiting for transfers between devices, gather_plane(): lax.ppermute(top, 'group', flip(groups, high))  7.25 us
    ppermute x1, waiting for transfers between devices, local(): visitors = [lax.ppermute(both, ('z', 'core'), trip) for trip in trips]  6.7 us
    ppermute x2, starting transfers between devices, gather_plane(): blocks[s] = [lax.ppermute(block, 'group', flip(groups, s))]  4.08 us
    pallas_call x2, Pallas kernels, call(): pl.pallas_call(kernel, in_specs=[VMEM] * len(operands), out_specs=[VMEM]...  3.86 us
    ppermute x1, starting transfers between devices, local(): visitors = [lax.ppermute(both, ('z', 'core'), trip) for trip in trips]  3.48 us
    all_to_all x1, waiting for transfers between devices, local(): lax.all_to_all(merged[0], 'group', split_axis=0, concat_axis=0, tiled=True)  3.41 us
    all_to_all x1, starting transfers between devices, local(): lax.all_to_all(merged[0], 'group', split_axis=0, concat_axis=0, tiled=True)  3.19 us
  transfers between devices with their start and end apart: 14, of which 7 were waited for; matrix products, arithmetic and copies ran while one was open for 1% of the time, Pallas kernels for 3%

profile of v14, /device:TPU:0, one launch (start us, length us, event | category | flops | bytes accessed | tf_op | source)
XLA Modules:
  0.0 60.9 jit_solution(9018907864963021344)
XLA Ops:
  0.0 0.7 %pad_add_fusion.ids_ref = s32[2,96]{1,0:T(2,128)S(1)} fusion(s32[1,96]{1,0:T(1,128)} %bitcast.26, s32[1,96]{1,0:T(1,128)} %bitcast.27), kind=kLoop, calls=%fused_computation | loop fusion | flops 192 | bytes 1536 | tf_op jit(solution)/shard_map/stack | solution.py:82
  0.7 1.1 %copy-done = bf16[96,4096]{1,0:T(8,128)(2,1)S(1)} copy-done((bf16[96,4096]{1,0:T(8,128)(2,1)S(1)}, bf16[96,4096]{1,0:T(8,128)(2,1)}, u32[]{:S(2)}) %copy-start) | copy-done | bytes 786456
  1.8 0.3 shard_map.37.refs_0_.refs_1_.own_ref
  2.1 0.5 collective-permute-start
  2.6 2.6 %collective-permute-start.1 = (bf16[96,4224]{1,0:T(8,128)(2,1)S(1)}, bf16[96,4224]{1,0:T(8,128)(2,1)S(1)}, u32[]{:S(2)}, u32[]{:S(2)}) collective-permute-start(bf16[96,4224]{1,0:T(8,128)(2,1)S(1)} %shard_map.37.refs_0_.refs_1_.own_ref), channel_id=1, source_target_pairs={{0,8},{8,0},{16,24},{24,16},{1,9},{9,1},{17,25},{25,17},{2,10},{10... | collective-permute-start | bytes 2433032 | tf_op jit(solution)/shard_map/ppermute | solution.py:40
  5.2 1.5 %collective-permute-start.3 = (bf16[96,4224]{1,0:T(8,128)(2,1)S(1)}, bf16[96,4224]{1,0:T(8,128)(2,1)S(1)}, u32[]{:S(2)}, u32[]{:S(2)}) collective-permute-start(bf16[96,4224]{1,0:T(8,128)(2,1)S(1)} %shard_map.37.refs_0_.refs_1_.own_ref), channel_id=1, source_target_pairs={{0,16},{8,24},{16,0},{24,8},{1,17},{9,25},{17,1},{25,9},{2,18},{10... | collective-permute-start | bytes 2433032 | tf_op jit(solution)/shard_map/ppermute | solution.py:40
  6.7 0.1 shard_map.39
  6.8 3.5 %collective-permute-start.9 = (bf16[192,4224]{1,0:T(8,128)(2,1)S(1)}, bf16[192,4224]{1,0:T(8,128)(2,1)S(1)}, u32[]{:S(2)}, u32[]{:S(2)}) collective-permute-start(bf16[192,4224]{1,0:T(8,128)(2,1)S(1)} %shard_map.39), channel_id=1, source_target_pairs={{0,2},{2,4},{4,6},{6,0},{1,5},{7,3},{8,10},{10,12},{12,14},{14,8},... | collective-permute-start | bytes 4866056 | tf_op jit(solution)/shard_map/ppermute | solution.py:205
  10.3 13.5 %collective-permute-done.1.refs_3_ = bf16[96,4224]{1,0:T(8,128)(2,1)S(1)} collective-permute-done((bf16[96,4224]{1,0:T(8,128)(2,1)S(1)}, bf16[96,4224]{1,0:T(8,128)(2,1)S(1)}, u32[]{:S(2)}, u32[]{:S(2)}) %collective-permute-start.1) | collective-permute-done | bytes 811040 | tf_op jit(solution)/shard_map/ppermute | solution.py:40
  23.9 1.9 %collective-permute-start.5 = (bf16[48,4224]{1,0:T(8,128)(2,1)S(1)}, bf16[48,4224]{1,0:T(8,128)(2,1)S(1)}, u32[]{:S(2)}, u32[]{:S(2)}) collective-permute-start(bf16[48,4224]{1,0:T(8,128)(2,1)S(1)} %slice.44), channel_id=1, source_target_pairs={{0,16},{8,24},{16,0},{24,8},{1,17},{9,25},{17,1},{25,9},{2,18},{10... | collective-permute-start | bytes 1216520 | tf_op jit(solution)/shard_map/ppermute | solution.py:46
  25.8 0.5 collective-permute-start.4
  26.3 1.6 %collective-permute-start.6 = (bf16[48,4224]{1,0:T(8,128)(2,1)S(1)}, bf16[48,4224]{1,0:T(8,128)(2,1)S(1)}, u32[]{:S(2)}, u32[]{:S(2)}) collective-permute-start(bf16[48,4224]{1,0:T(8,128)(2,1)S(1)} %slice.45), channel_id=1, source_target_pairs={{0,8},{8,0},{16,24},{24,16},{1,9},{9,1},{17,25},{25,17},{2,10},{10... | collective-permute-start | bytes 1216520 | tf_op jit(solution)/shard_map/ppermute | solution.py:47
  27.8 7.2 %collective-permute-done.5.refs_7_ = bf16[48,4224]{1,0:T(8,128)(2,1)S(1)} collective-permute-done((bf16[48,4224]{1,0:T(8,128)(2,1)S(1)}, bf16[48,4224]{1,0:T(8,128)(2,1)S(1)}, u32[]{:S(2)}, u32[]{:S(2)}) %collective-permute-start.5) | collective-permute-done | bytes 405536 | tf_op jit(solution)/shard_map/ppermute | solution.py:46
  35.1 2.5 %collective-permute-done.6.refs_8_ = bf16[48,4224]{1,0:T(8,128)(2,1)S(1)} collective-permute-done((bf16[48,4224]{1,0:T(8,128)(2,1)S(1)}, bf16[48,4224]{1,0:T(8,128)(2,1)S(1)}, u32[]{:S(2)}, u32[]{:S(2)}) %collective-permute-start.6) | collective-permute-done | bytes 405536 | tf_op jit(solution)/shard_map/ppermute | solution.py:47
  37.7 1.7 %collective-permute-done.8.refs_10_ = bf16[48,4224]{1,0:T(8,128)(2,1)S(1)} collective-permute-done((bf16[48,4224]{1,0:T(8,128)(2,1)S(1)}, bf16[48,4224]{1,0:T(8,128)(2,1)S(1)}, u32[]{:S(2)}, u32[]{:S(2)}) %collective-permute-start.8) | collective-permute-done | bytes 405536 | tf_op jit(solution)/shard_map/ppermute | solution.py:53
  39.4 1.8 %shard_map.38.refs_11_ = f32[1,128]{1,0:T(1,128)S(1)} custom-call(bf16[96,4224]{1,0:T(8,128)(2,1)S(1)} %shard_map.37.refs_0_.refs_1_.own_ref, bf16[96,4224]{1,0:T(8,128)(2,1)S(1)} %shard_map.37.refs_0_.refs_1_.own_ref, bf16[96,4224]{1,0:T(8,128)(2,1)S(1)} %collective-permute-done.refs_2_.other_ref, bf16[96,4224]{1,0:T(8,128)(2,1)S(1)} %collective-permute-done.1.refs_3_, ...), custom_call_target="tpu_custom_call" | custom-call | flops 805306368 | bytes 7340032 | tf_op jit(solution)/shard_map/pallas_call | solution.py:174
  41.2 6.7 %collective-permute-done.9.refs_0_ = bf16[192,4224]{1,0:T(8,128)(2,1)S(1)} collective-permute-done((bf16[192,4224]{1,0:T(8,128)(2,1)S(1)}, bf16[192,4224]{1,0:T(8,128)(2,1)S(1)}, u32[]{:S(2)}, u32[]{:S(2)}) %collective-permute-start.9) | collective-permute-done | bytes 1622048 | tf_op jit(solution)/shard_map/ppermute | solution.py:205
  47.9 2.1 %shard_map.40 = (f32[2,128]{1,0:T(2,128)S(1)}, f32[4,1,128]{2,1,0:T(1,128)S(1)}, f32[4,1,128]{2,1,0:T(1,128)S(1)}) custom-call(bf16[192,4224]{1,0:T(8,128)(2,1)S(1)} %collective-permute-done.9.refs_0_, bf16[96,4224]{1,0:T(8,128)(2,1)S(1)} %shard_map.37.refs_0_.refs_1_.own_ref, bf16[96,4224]{1,0:T(8,128)(2,1)S(1)} %collective-permute-done.refs_2_.other_ref, ...), custom_call_target="tpu_custom_call" | custom-call | flops 1610612736 | bytes 8388608 | tf_op jit(solution)/shard_map/pallas_call | solution.py:174
  50.0 1.9 %collective-permute-start.10 = (f32[2,128]{1,0:T(2,128)S(1)}, f32[2,128]{1,0:T(2,128)S(1)}, u32[]{:S(2)}, u32[]{:S(2)}) collective-permute-start(f32[2,128]{1,0:T(2,128)S(1)} %get-tuple-element.8), channel_id=1, source_target_pairs={{2,0},{4,2},{6,4},{0,6},{5,1},{3,7},{10,8},{12,10},{14,12},{8,14},... | collective-permute-start | bytes 3080 | tf_op jit(solution)/shard_map/ppermute | solution.py:231
  52.0 0.6 max.23
  52.5 3.2 %all-to-all-start = ((f32[4,1,128]{2,1,0:T(1,128)}), f32[4,1,128]{2,1,0:T(1,128)S(1)}, u32[]{:S(2)}, u32[]{:S(2)}) async-start(f32[4,1,128]{2,1,0:T(1,128)} %max.23), calls=%async_computation | async-start | bytes 4096 | tf_op jit(solution)/shard_map/all_to_all | solution.py:239
  55.9 1.1 %collective-permute-done.11 = f32[2,128]{1,0:T(2,128)S(1)} collective-permute-done((f32[2,128]{1,0:T(2,128)S(1)}, f32[2,128]{1,0:T(2,128)S(1)}, u32[]{:S(2)}, u32[]{:S(2)}) %collective-permute-start.11) | collective-permute-done | bytes 1056 | tf_op jit(solution)/shard_map/ppermute | solution.py:53
  57.0 3.4 %all-to-all-done = f32[4,1,128]{2,1,0:T(1,128)S(1)} async-done(((f32[4,1,128]{2,1,0:T(1,128)}), f32[4,1,128]{2,1,0:T(1,128)S(1)}, u32[]{:S(2)}, u32[]{:S(2)}) %all-to-all-start) | async-done | bytes 2080 | tf_op jit(solution)/shard_map/all_to_all | solution.py:239
  60.4 0.5 slice_bitcast_fusion.4
  (16 shorter events, 0.2 us)
Async XLA Ops:
  0.7 1.1 %copy-start = (bf16[96,4096]{1,0:T(8,128)(2,1)S(1)}, bf16[96,4096]{1,0:T(8,128)(2,1)}, u32[]{:S(2)}) copy-start(bf16[96,4096]{1,0:T(8,128)(2,1)} %rows_ref.1) | copy-start | bytes 2359300
  2.1 4.6 %collective-permute-start = (bf16[96,4224]{1,0:T(8,128)(2,1)S(1)}, bf16[96,4224]{1,0:T(8,128)(2,1)S(1)}, u32[]{:S(2)}, u32[]{:S(2)}) collective-permute-start(bf16[96,4224]{1,0:T(8,128)(2,1)S(1)} %shard_map.37.refs_0_.refs_1_.own_ref), channel_id=1, source_target_pairs={{0,1},{1,0},{2,3},{3,2},{4,5},{5,4},{6,7},{7,6},{8,9},{9,8},{10,11... | collective-permute-start | bytes 2433032 | tf_op jit(solution)/shard_map/ppermute | solution.py:53
  2.6 21.2 %collective-permute-start.1 = (bf16[96,4224]{1,0:T(8,128)(2,1)S(1)}, bf16[96,4224]{1,0:T(8,128)(2,1)S(1)}, u32[]{:S(2)}, u32[]{:S(2)}) collective-permute-start(bf16[96,4224]{1,0:T(8,128)(2,1)S(1)} %shard_map.37.refs_0_.refs_1_.own_ref), channel_id=1, source_target_pairs={{0,8},{8,0},{16,24},{24,16},{1,9},{9,1},{17,25},{25,17},{2,10},{10... | collective-permute-start | bytes 2433032 | tf_op jit(solution)/shard_map/ppermute | solution.py:40
  5.2 20.6 %collective-permute-start.3 = (bf16[96,4224]{1,0:T(8,128)(2,1)S(1)}, bf16[96,4224]{1,0:T(8,128)(2,1)S(1)}, u32[]{:S(2)}, u32[]{:S(2)}) collective-permute-start(bf16[96,4224]{1,0:T(8,128)(2,1)S(1)} %shard_map.37.refs_0_.refs_1_.own_ref), channel_id=1, source_target_pairs={{0,16},{8,24},{16,0},{24,8},{1,17},{9,25},{17,1},{25,9},{2,18},{10... | collective-permute-start | bytes 2433032 | tf_op jit(solution)/shard_map/ppermute | solution.py:40
  6.8 41.0 %collective-permute-start.9 = (bf16[192,4224]{1,0:T(8,128)(2,1)S(1)}, bf16[192,4224]{1,0:T(8,128)(2,1)S(1)}, u32[]{:S(2)}, u32[]{:S(2)}) collective-permute-start(bf16[192,4224]{1,0:T(8,128)(2,1)S(1)} %shard_map.39), channel_id=1, source_target_pairs={{0,2},{2,4},{4,6},{6,0},{1,5},{7,3},{8,10},{10,12},{12,14},{14,8},... | collective-permute-start | bytes 4866056 | tf_op jit(solution)/shard_map/ppermute | solution.py:205
  23.9 11.2 %collective-permute-start.5 = (bf16[48,4224]{1,0:T(8,128)(2,1)S(1)}, bf16[48,4224]{1,0:T(8,128)(2,1)S(1)}, u32[]{:S(2)}, u32[]{:S(2)}) collective-permute-start(bf16[48,4224]{1,0:T(8,128)(2,1)S(1)} %slice.44), channel_id=1, source_target_pairs={{0,16},{8,24},{16,0},{24,8},{1,17},{9,25},{17,1},{25,9},{2,18},{10... | collective-permute-start | bytes 1216520 | tf_op jit(solution)/shard_map/ppermute | solution.py:46
  25.7 11.9 %collective-permute-start.2 = (bf16[96,4224]{1,0:T(8,128)(2,1)S(1)}, bf16[96,4224]{1,0:T(8,128)(2,1)S(1)}, u32[]{:S(2)}, u32[]{:S(2)}) collective-permute-start(bf16[96,4224]{1,0:T(8,128)(2,1)S(1)} %collective-permute-done.1.refs_3_), channel_id=1, source_target_pairs={{0,1},{1,0},{2,3},{3,2},{4,5},{5,4},{6,7},{7,6},{8,9},{9,8},{10,11... | collective-permute-start | bytes 2433032 | tf_op jit(solution)/shard_map/ppermute | solution.py:53
  25.8 11.9 %collective-permute-start.4 = (bf16[96,4224]{1,0:T(8,128)(2,1)S(1)}, bf16[96,4224]{1,0:T(8,128)(2,1)S(1)}, u32[]{:S(2)}, u32[]{:S(2)}) collective-permute-start(bf16[96,4224]{1,0:T(8,128)(2,1)S(1)} %collective-permute-done.3.refs_5_), channel_id=1, source_target_pairs={{0,1},{1,0},{2,3},{3,2},{4,5},{5,4},{6,7},{7,6},{8,9},{9,8},{10,11... | collective-permute-start | bytes 2433032 | tf_op jit(solution)/shard_map/ppermute | solution.py:53
  26.3 11.4 %collective-permute-start.6 = (bf16[48,4224]{1,0:T(8,128)(2,1)S(1)}, bf16[48,4224]{1,0:T(8,128)(2,1)S(1)}, u32[]{:S(2)}, u32[]{:S(2)}) collective-permute-start(bf16[48,4224]{1,0:T(8,128)(2,1)S(1)} %slice.45), channel_id=1, source_target_pairs={{0,8},{8,0},{16,24},{24,16},{1,9},{9,1},{17,25},{25,17},{2,10},{10... | collective-permute-start | bytes 1216520 | tf_op jit(solution)/shard_map/ppermute | solution.py:47
  35.1 2.6 %collective-permute-start.7 = (bf16[48,4224]{1,0:T(8,128)(2,1)S(1)}, bf16[48,4224]{1,0:T(8,128)(2,1)S(1)}, u32[]{:S(2)}, u32[]{:S(2)}) collective-permute-start(bf16[48,4224]{1,0:T(8,128)(2,1)S(1)} %collective-permute-done.5.refs_7_), channel_id=1, source_target_pairs={{0,1},{1,0},{2,3},{3,2},{4,5},{5,4},{6,7},{7,6},{8,9},{9,8},{10,11... | collective-permute-start | bytes 1216520 | tf_op jit(solution)/shard_map/ppermute | solution.py:53
  37.6 1.7 %collective-permute-start.8 = (bf16[48,4224]{1,0:T(8,128)(2,1)S(1)}, bf16[48,4224]{1,0:T(8,128)(2,1)S(1)}, u32[]{:S(2)}, u32[]{:S(2)}) collective-permute-start(bf16[48,4224]{1,0:T(8,128)(2,1)S(1)} %collective-permute-done.6.refs_8_), channel_id=1, source_target_pairs={{0,1},{1,0},{2,3},{3,2},{4,5},{5,4},{6,7},{7,6},{8,9},{9,8},{10,11... | collective-permute-start | bytes 1216520 | tf_op jit(solution)/shard_map/ppermute | solution.py:53
  50.0 2.0 %collective-permute-start.12 = (f32[4,1,128]{2,1,0:T(1,128)S(1)}, f32[4,1,128]{2,1,0:T(1,128)S(1)}, u32[]{:S(2)}, u32[]{:S(2)}) collective-permute-start(f32[4,1,128]{2,1,0:T(1,128)S(1)} %get-tuple-element.10), channel_id=1, source_target_pairs={{0,1},{1,0},{2,3},{3,2},{4,5},{5,4},{6,7},{7,6},{8,9},{9,8},{10,11... | collective-permute-start | bytes 6152 | tf_op jit(solution)/shard_map/ppermute | solution.py:53
  50.0 5.7 %collective-permute-start.10 = (f32[2,128]{1,0:T(2,128)S(1)}, f32[2,128]{1,0:T(2,128)S(1)}, u32[]{:S(2)}, u32[]{:S(2)}) collective-permute-start(f32[2,128]{1,0:T(2,128)S(1)} %get-tuple-element.8), channel_id=1, source_target_pairs={{2,0},{4,2},{6,4},{0,6},{5,1},{3,7},{10,8},{12,10},{14,12},{8,14},... | collective-permute-start | bytes 3080 | tf_op jit(solution)/shard_map/ppermute | solution.py:231
  52.5 7.8 %all-to-all-start = ((f32[4,1,128]{2,1,0:T(1,128)}), f32[4,1,128]{2,1,0:T(1,128)S(1)}, u32[]{:S(2)}, u32[]{:S(2)}) async-start(f32[4,1,128]{2,1,0:T(1,128)} %max.23), calls=%async_computation | async-start | bytes 4096 | tf_op jit(solution)/shard_map/all_to_all | solution.py:239
  55.8 1.2 %collective-permute-start.11 = (f32[2,128]{1,0:T(2,128)S(1)}, f32[2,128]{1,0:T(2,128)S(1)}, u32[]{:S(2)}, u32[]{:S(2)}) collective-permute-start(f32[2,128]{1,0:T(2,128)S(1)} %collective-permute-done.10), channel_id=1, source_target_pairs={{0,1},{1,0},{2,3},{3,2},{4,5},{5,4},{6,7},{7,6},{8,9},{9,8},{10,11... | collective-permute-start | bytes 3080 | tf_op jit(solution)/shard_map/ppermute | solution.py:53

commit v15 on v13

--- a/solution.py
+++ b/solution.py
@@ -10,7 +10,6 @@
 AXES = ("group", "z", "core")
 LANES = 128
 CHUNK = 512
-CALL = 8
 VMEM = pl.BlockSpec(memory_space=pltpu.VMEM)
 
 
@@ -29,24 +28,6 @@
         return [(k, (k + shift) % length) for k in range(length)]
     pairs = [(k, k + shift) for k in range(length // 2)]
     return [pair[:: 1 - 2 * (pair[0] % 2)] for pair in pairs]
-
-
-def gather_plane(block, groups):
-    half = block.shape[0] // 2
-    blocks = {0: [block]}
-    for s in range(1, groups):
-        low, high = s & -s, 1 << (s.bit_length() - 1)
-        if low == high:
-            blocks[s] = [lax.ppermute(block, "group", flip(groups, s))]
-            continue
-        top, bottom = blocks[s ^ high], blocks[s ^ low]
-        top = top[0][:half] if len(top) == 1 else top[0]
-        bottom = bottom[0][half:] if len(bottom) == 1 else bottom[1]
-        blocks[s] = [
-            lax.ppermute(top, "group", flip(groups, high)),
-            lax.ppermute(bottom, "group", flip(groups, low)),
-        ]
-    return blocks
 
 
 def swap(block):
@@ -84,9 +65,8 @@
 
 def pair_kernel(own_ref, other_ref, both_ref):
     rows = own_ref.shape[0]
-    core = lax.axis_index("core")
-    both_ref[pl.ds(pl.multiple_of(core * rows, 16), rows), :] = own_ref[...]
-    both_ref[pl.ds(pl.multiple_of((core ^ 1) * rows, 16), rows), :] = other_ref[...]
+    both_ref[:rows, :] = own_ref[...]
+    both_ref[rows:, :] = other_ref[...]
 
 
 def pair(own, other):
@@ -107,14 +87,16 @@
     row_ref[...] = best[0]
 
 
-def visit_kernel(visitors, arrays, *refs):
+def visit_kernel(visitors, arrays, mine, others, *refs):
     block_refs = refs[visitors : visitors + arrays]
     row_ref, mine_ref, other_ref, *scratch = refs[visitors + arrays + 1 :]
-    bests, cols = best_of(refs[:visitors], block_refs, refs[0].shape[0] // 2, True, *scratch)
+    rows = refs[0].shape[0] // 2
+    bests, cols = best_of(refs[:visitors], block_refs, rows, True, *scratch)
     for v, best in enumerate(bests):
         row_ref[v : v + 1, :] = best
-    for j, best in enumerate(cols):
-        (mine_ref, other_ref)[j % 2][j // 2 : j // 2 + 1, :] = best
+    for ref, picked in ((mine_ref, mine), (other_ref, others)):
+        for row, j in enumerate(picked):
+            ref[row : row + 1, :] = cols[j]
 
 
 def best_of(visitor_refs, block_refs, rows, homed, units, dots):
@@ -188,55 +170,63 @@
     )(*operands)
 
 
+def group_trip(groups, first, second):
+    return [(2 * k + c, 2 * (k ^ s) + c) for k in range(groups) for c, s in enumerate((first, second))]
+
+
 def local(embeddings, cluster_ids, order_index):
     rows = embeddings.shape[0]
     groups, length = lax.axis_size("group"), lax.axis_size("z")
     z, core = lax.axis_index("z"), lax.axis_index("core")
+    plane_axes, line_axes = ("group", "core"), ("z", "core")
     own = pack(embeddings, cluster_ids, order_index)
-    other = swap(own)
-    both = pair(own, other)
+    both = pair(own, swap(own))
 
     routes = [ring_pairs(length, shift) for shift in range(1, length // 2 + 1)]
     trips = []
     for first in range(0, len(routes), 2):
         ways = enumerate(routes[first : first + 2])
         trips.append([(2 * a + way, 2 * b + way) for way, route in ways for a, b in route])
-    visitors = [lax.ppermute(both, ("z", "core"), trip) for trip in trips]
-
-    plane = gather_plane(own, groups)
-    parts = [own, other]
-    for s in range(1, groups):
-        parts += [*plane[s], *(swap(part) for part in plane[s])]
-    chunks, size = [[]], 0
-    for part in parts:
-        if size == CALL * rows:
-            chunks, size = chunks + [[]], 0
-        chunks[-1].append(part)
-        size += part.shape[0]
-
+    visitors = [lax.ppermute(both, line_axes, trip) for trip in trips]
+
+    partners = [(s, s + 1) for s in range(1, groups - 1, 2)]
+    arrived = [lax.ppermute(both, plane_axes, group_trip(groups, *way)) for way in partners]
+    last = groups - 1
+    relay = group_trip(groups, last ^ partners[-1][0], last ^ partners[-1][1])
+    half = rows // 2
+    corner = [arrived[-1][first : first + half] for first in (0, half)]
+    corner = [lax.ppermute(part, plane_axes, relay) for part in corner]
+    sides = [(block, swap(block)) for block in arrived]
+    chunks = [[both, *sides[-1], *corner, *(swap(part) for part in corner)]]
+    chunks += [[*sides[k], *sides[k + 1]] for k in range(0, len(sides) - 1, 2)]
+
+    orders = [((2, 5, 6, 0), (4, 3, 7, 1))] + [((0, 3, 4, 7), (2, 1, 6, 5))] * (len(chunks) - 1)
     bests, answers = [], []
     for chunk in chunks:
-        total = sum(part.shape[0] for part in chunk)
-        bests += call(own_kernel, [own, *chunk], 1, [1], total)
-    for index, chunk in enumerate(chunks):
-        total = sum(part.shape[0] for part in chunk)
-        kernel = functools.partial(visit_kernel, len(visitors), len(chunk))
-        count, half = 2 * len(visitors), total // rows // 2
+        bests += call(own_kernel, [own, *chunk], 1, [1], 8 * rows)
+    for index, (chunk, order) in enumerate(zip(chunks, orders)):
+        kernel = functools.partial(visit_kernel, len(visitors), len(chunk), *order)
+        count = 2 * len(visitors)
         operands = [*visitors, *chunk, bests[index]]
-        answers.append(call(kernel, operands, count, [count, half, half], total))
+        answers.append(call(kernel, operands, count, [count, 4, 4], 8 * rows))
     home = functools.reduce(jnp.maximum, [answer[0] for answer in answers])
+    merged = [jnp.maximum(mine, swap(others)) for _, mine, others in answers]
+
     for index, trip in enumerate(trips):
         part = home[2 * index : 2 * index + 2] if len(trips) > 1 else home
-        back = lax.ppermute(part, ("z", "core"), [(b, a) for a, b in trip])
-        for here, best in ((2 * z + core, back), (2 * z + (core ^ 1), swap(back))):
+        back = lax.ppermute(part, line_axes, [(b, a) for a, b in trip])
+        for here, best in ((2 * z + core, back[0:1]), (2 * z + (core ^ 1), swap(back)[1:2])):
             sent = functools.reduce(jnp.logical_or, [here == a for a, _ in trip])
-            bests.append(jnp.where(sent, jnp.where(core == 0, best[0:1], best[1:2]), -1.0))
-    for index, (_, mine, other) in enumerate(answers):
-        merged = jnp.maximum(mine, swap(other))
-        for row in range(CALL // 2):
-            s = index * CALL // 2 + row
-            got = lax.ppermute(merged, "group", flip(groups, s)) if s else merged
+            bests.append(jnp.where(sent, best, -1.0))
+    ways = [(0, 0, partners[-1])]
+    ways += [(1 + k // 2, 2 * (k % 2), way) for k, way in enumerate(partners[:-1])]
+    for chunk, row, (first, second) in ways:
+        for order in ((first, second), (second, first)):
+            got = lax.ppermute(merged[chunk], plane_axes, group_trip(groups, *order))
             bests.append(got[row : row + 1])
+            row += 1
+    bests.append(lax.ppermute(merged[0], "group", flip(groups, last))[2:3])
+    bests.append(merged[0][3:4])
     return functools.reduce(jnp.maximum, bests)[0, :rows]
 
 

time: 58.8 us -> 60 us (1.020)
  waiting for transfers between devices: 34.1 us -> 38.2 us
  starting transfers between devices: 17.7 us -> 14.8 us
    ppermute x9 -> x8, starting transfers between devices: 16.4 us -> 14.1 us  [the longest x1 3.47 us: local(): visitors = [lax.ppermute(both, line_axes, trip) for trip in trips]]
    ppermute x9 -> x8, waiting for transfers between devices: 31.4 us -> 33.6 us  [the longest x1 15.4 us: local(): lax.ppermute(both, plane_axes, group_trip(groups, *way))]
    ppermute x7 -> x6, waiting for transfers between devices: 2.69 us -> 4.65 us  [swap(): return lax.ppermute(block, 'core', flip(2, 1))]
    ppermute x7 -> x6, starting transfers between devices: 1.26 us -> 0.75 us  [swap(): return lax.ppermute(block, 'core', flip(2, 1))]
  transfers between devices with their start and end apart: 16 -> 14, of which waited for: 8 -> 8; matrix products, arithmetic and copies ran while one was open for 0% -> 0% of each run, Pallas kernels for 3% -> 3%
where the time goes in v15:
time: 60 us; the launch traced here: 59.8 us
  waiting for transfers between devices  38.2 us (64%)
  starting transfers between devices  14.8 us (25%)
  Pallas kernels  4.27 us (7%)
  local copies, waits for them, and re-layouts  1.7 us (3%)
  other arithmetic  0.69 us (1%)
    ppermute x1, waiting for transfers between devices, local(): lax.ppermute(both, plane_axes, group_trip(groups, *way))  15.4 us
    ppermute x2, waiting for transfers between devices, local(): corner = [lax.ppermute(part, plane_axes, relay) for part in corner]  10.1 us
    ppermute x1, waiting for transfers between devices, local(): visitors = [lax.ppermute(both, line_axes, trip) for trip in trips]  6.14 us
    ppermute x6, waiting for transfers between devices, swap(): return lax.ppermute(block, 'core', flip(2, 1))  4.65 us
    pallas_call x2, Pallas kernels, call(): pl.pallas_call(kernel, in_specs=[VMEM] * len(operands), out_specs=[VMEM]...  3.86 us
    ppermute x1, starting transfers between devices, local(): visitors = [lax.ppermute(both, line_axes, trip) for trip in trips]  3.47 us
    ppermute x1, starting transfers between devices, local(): lax.ppermute(both, plane_axes, group_trip(groups, *way))  2.92 us
    ppermute x2, starting transfers between devices, local(): corner = [lax.ppermute(part, plane_axes, relay) for part in corner]  2.19 us
  transfers between devices with their start and end apart: 14, of which 8 were waited for; matrix products, arithmetic and copies ran while one was open for 0% of the time, Pallas kernels for 3%

profile of v15, /device:TPU:0, one launch (start us, length us, event | category | flops | bytes accessed | tf_op | source)
XLA Modules:
  0.0 59.8 jit_solution(12795990799187582037)
XLA Ops:
  0.0 0.7 %pad_add_fusion.ids_ref = s32[2,96]{1,0:T(2,128)S(1)} fusion(s32[1,96]{1,0:T(1,128)} %bitcast.4, s32[1,96]{1,0:T(1,128)} %bitcast.5), kind=kLoop, calls=%fused_computation | loop fusion | flops 192 | bytes 1536 | tf_op jit(solution)/shard_map/stack | solution.py:63
  0.7 1.1 %copy-done = bf16[96,4096]{1,0:T(8,128)(2,1)S(1)} copy-done((bf16[96,4096]{1,0:T(8,128)(2,1)S(1)}, bf16[96,4096]{1,0:T(8,128)(2,1)}, u32[]{:S(2)}) %copy-start) | copy-done | bytes 786456
  1.8 0.3 shard_map.37.own_ref.refs_0_
  2.1 0.5 collective-permute-start
  2.6 1.9 %collective-permute-done.other_ref = bf16[96,4224]{1,0:T(8,128)(2,1)S(1)} collective-permute-done((bf16[96,4224]{1,0:T(8,128)(2,1)S(1)}, bf16[96,4224]{1,0:T(8,128)(2,1)S(1)}, u32[]{:S(2)}, u32[]{:S(2)}) %collective-permute-start) | collective-permute-done | bytes 811040 | tf_op jit(solution)/shard_map/ppermute | solution.py:34
  4.6 0.1 shard_map.38.refs_1_
  4.7 2.9 %collective-permute-start.1 = (bf16[192,4224]{1,0:T(8,128)(2,1)S(1)}, bf16[192,4224]{1,0:T(8,128)(2,1)S(1)}, u32[]{:S(2)}, u32[]{:S(2)}) collective-permute-start(bf16[192,4224]{1,0:T(8,128)(2,1)S(1)} %shard_map.38.refs_1_), channel_id=1, source_target_pairs={{0,8},{1,17},{8,0},{9,25},{16,24},{17,1},{24,16},{25,9},{2,10},{3,... | collective-permute-start | bytes 4866056 | tf_op jit(solution)/shard_map/ppermute | solution.py:193
  7.6 3.5 %collective-permute-start.7 = (bf16[192,4224]{1,0:T(8,128)(2,1)S(1)}, bf16[192,4224]{1,0:T(8,128)(2,1)S(1)}, u32[]{:S(2)}, u32[]{:S(2)}) collective-permute-start(bf16[192,4224]{1,0:T(8,128)(2,1)S(1)} %shard_map.38.refs_1_), channel_id=1, source_target_pairs={{0,2},{2,4},{4,6},{6,0},{1,5},{7,3},{8,10},{10,12},{12,14},{14,8},... | collective-permute-start | bytes 4866056 | tf_op jit(solution)/shard_map/ppermute | solution.py:190
  11.1 15.4 %collective-permute-done.1.refs_2_ = bf16[192,4224]{1,0:T(8,128)(2,1)S(1)} collective-permute-done((bf16[192,4224]{1,0:T(8,128)(2,1)S(1)}, bf16[192,4224]{1,0:T(8,128)(2,1)S(1)}, u32[]{:S(2)}, u32[]{:S(2)}) %collective-permute-start.1) | collective-permute-done | bytes 1622048 | tf_op jit(solution)/shard_map/ppermute | solution.py:193
  26.6 2.1 %collective-permute-start.3 = (bf16[48,4224]{1,0:T(8,128)(2,1)S(1)}, bf16[48,4224]{1,0:T(8,128)(2,1)S(1)}, u32[]{:S(2)}, u32[]{:S(2)}) collective-permute-start(bf16[48,4224]{1,0:T(8,128)(2,1)S(1)} %get-tuple-element.12), channel_id=1, source_target_pairs={{0,16},{1,9},{8,24},{9,1},{16,0},{17,25},{24,8},{25,17},{2,18},{3,... | collective-permute-start | bytes 1216520 | tf_op jit(solution)/shard_map/ppermute | solution.py:198
  28.8 5.8 %collective-permute-done.3.refs_4_ = bf16[48,4224]{1,0:T(8,128)(2,1)S(1)} collective-permute-done((bf16[48,4224]{1,0:T(8,128)(2,1)S(1)}, bf16[48,4224]{1,0:T(8,128)(2,1)S(1)}, u32[]{:S(2)}, u32[]{:S(2)}) %collective-permute-start.3) | collective-permute-done | bytes 405536 | tf_op jit(solution)/shard_map/ppermute | solution.py:198
  34.6 4.3 %collective-permute-done.4.refs_5_ = bf16[48,4224]{1,0:T(8,128)(2,1)S(1)} collective-permute-done((bf16[48,4224]{1,0:T(8,128)(2,1)S(1)}, bf16[48,4224]{1,0:T(8,128)(2,1)S(1)}, u32[]{:S(2)}, u32[]{:S(2)}) %collective-permute-start.4) | collective-permute-done | bytes 405536 | tf_op jit(solution)/shard_map/ppermute | solution.py:198
  39.0 1.7 %collective-permute-done.6.refs_7_ = bf16[48,4224]{1,0:T(8,128)(2,1)S(1)} collective-permute-done((bf16[48,4224]{1,0:T(8,128)(2,1)S(1)}, bf16[48,4224]{1,0:T(8,128)(2,1)S(1)}, u32[]{:S(2)}, u32[]{:S(2)}) %collective-permute-start.6) | collective-permute-done | bytes 405536 | tf_op jit(solution)/shard_map/ppermute | solution.py:34
  40.7 1.8 %shard_map.39.refs_8_ = f32[1,128]{1,0:T(1,128)S(1)} custom-call(bf16[96,4224]{1,0:T(8,128)(2,1)S(1)} %shard_map.37.own_ref.refs_0_, bf16[192,4224]{1,0:T(8,128)(2,1)S(1)} %shard_map.38.refs_1_, bf16[192,4224]{1,0:T(8,128)(2,1)S(1)} %collective-permute-done.1.refs_2_, bf16[192,4224]{1,0:T(8,128)(2,1)S(1)} %collective-permute-done.2.refs_3_, ...), custom_call_target="tpu_custom_call" | custom-call | flops 805306368 | bytes 7340032 | tf_op jit(solution)/shard_map/pallas_call | solution.py:155
  42.5 6.1 %collective-permute-done.7.refs_0_ = bf16[192,4224]{1,0:T(8,128)(2,1)S(1)} collective-permute-done((bf16[192,4224]{1,0:T(8,128)(2,1)S(1)}, bf16[192,4224]{1,0:T(8,128)(2,1)S(1)}, u32[]{:S(2)}, u32[]{:S(2)}) %collective-permute-start.7) | collective-permute-done | bytes 1622048 | tf_op jit(solution)/shard_map/ppermute | solution.py:190
  48.7 2.0 %shard_map.40 = (f32[2,128]{1,0:T(2,128)S(1)}, f32[4,128]{1,0:T(4,128)S(1)}, f32[4,128]{1,0:T(4,128)S(1)}) custom-call(bf16[192,4224]{1,0:T(8,128)(2,1)S(1)} %collective-permute-done.7.refs_0_, bf16[192,4224]{1,0:T(8,128)(2,1)S(1)} %shard_map.38.refs_1_, bf16[192,4224]{1,0:T(8,128)(2,1)S(1)} %collective-permute-done.1.refs_2_, ...), custom_call_target="tpu_custom_call" | custom-call | flops 1610612736 | bytes 8388608 | tf_op jit(solution)/shard_map/pallas_call | solution.py:155
  50.8 1.9 %collective-permute-start.8 = (f32[2,128]{1,0:T(2,128)S(1)}, f32[2,128]{1,0:T(2,128)S(1)}, u32[]{:S(2)}, u32[]{:S(2)}) collective-permute-start(f32[2,128]{1,0:T(2,128)S(1)} %get-tuple-element.8), channel_id=1, source_target_pairs={{2,0},{4,2},{6,4},{0,6},{5,1},{3,7},{10,8},{12,10},{14,12},{8,14},... | collective-permute-start | bytes 3080 | tf_op jit(solution)/shard_map/ppermute | solution.py:217
  52.7 1.2 %collective-permute-start.11 = (f32[4,128]{1,0:T(4,128)S(1)}, f32[4,128]{1,0:T(4,128)S(1)}, u32[]{:S(2)}, u32[]{:S(2)}) collective-permute-start(f32[4,128]{1,0:T(4,128)S(1)} %max.23), channel_id=1, source_target_pairs={{0,8},{1,17},{8,0},{9,25},{16,24},{17,1},{24,16},{25,9},{2,10},{3,... | collective-permute-start | bytes 6152 | tf_op jit(solution)/shard_map/ppermute | solution.py:225
  53.9 0.9 %collective-permute-start.12 = (f32[4,128]{1,0:T(4,128)S(1)}, f32[4,128]{1,0:T(4,128)S(1)}, u32[]{:S(2)}, u32[]{:S(2)}) collective-permute-start(f32[4,128]{1,0:T(4,128)S(1)} %max.23), channel_id=1, source_target_pairs={{0,16},{1,9},{8,24},{9,1},{16,0},{17,25},{24,8},{25,17},{2,18},{3,... | collective-permute-start | bytes 6152 | tf_op jit(solution)/shard_map/ppermute | solution.py:225
  54.8 1.5 %collective-permute-start.13 = (f32[4,128]{1,0:T(4,128)S(1)}, f32[4,128]{1,0:T(4,128)S(1)}, u32[]{:S(2)}, u32[]{:S(2)}) collective-permute-start(f32[4,128]{1,0:T(4,128)S(1)} %max.23), channel_id=1, source_target_pairs={{0,24},{8,16},{16,8},{24,0},{1,25},{9,17},{17,9},{25,1},{2,26},{10... | collective-permute-start | bytes 6152 | tf_op jit(solution)/shard_map/ppermute | solution.py:228
  56.3 0.2 collective-permute-start.9
  56.5 1.0 %collective-permute-done.9 = f32[2,128]{1,0:T(2,128)S(1)} collective-permute-done((f32[2,128]{1,0:T(2,128)S(1)}, f32[2,128]{1,0:T(2,128)S(1)}, u32[]{:S(2)}, u32[]{:S(2)}) %collective-permute-start.9) | collective-permute-done | bytes 1056 | tf_op jit(solution)/shard_map/ppermute | solution.py:34
  57.5 1.8 %collective-permute-done.13 = f32[4,128]{1,0:T(4,128)S(1)} collective-permute-done((f32[4,128]{1,0:T(4,128)S(1)}, f32[4,128]{1,0:T(4,128)S(1)}, u32[]{:S(2)}, u32[]{:S(2)}) %collective-permute-start.13) | collective-permute-done | bytes 2080 | tf_op jit(solution)/shard_map/ppermute | solution.py:228
  59.3 0.5 slice_bitcast_fusion
  (15 shorter events, 0.3 us)
Async XLA Ops:
  0.7 1.1 %copy-start = (bf16[96,4096]{1,0:T(8,128)(2,1)S(1)}, bf16[96,4096]{1,0:T(8,128)(2,1)}, u32[]{:S(2)}) copy-start(bf16[96,4096]{1,0:T(8,128)(2,1)} %rows_ref.1) | copy-start | bytes 2359300
  2.1 2.5 %collective-permute-start = (bf16[96,4224]{1,0:T(8,128)(2,1)S(1)}, bf16[96,4224]{1,0:T(8,128)(2,1)S(1)}, u32[]{:S(2)}, u32[]{:S(2)}) collective-permute-start(bf16[96,4224]{1,0:T(8,128)(2,1)S(1)} %shard_map.37.own_ref.refs_0_), channel_id=1, source_target_pairs={{0,1},{1,0},{2,3},{3,2},{4,5},{5,4},{6,7},{7,6},{8,9},{9,8},{10,11... | collective-permute-start | bytes 2433032 | tf_op jit(solution)/shard_map/ppermute | solution.py:34
  4.7 21.8 %collective-permute-start.1 = (bf16[192,4224]{1,0:T(8,128)(2,1)S(1)}, bf16[192,4224]{1,0:T(8,128)(2,1)S(1)}, u32[]{:S(2)}, u32[]{:S(2)}) collective-permute-start(bf16[192,4224]{1,0:T(8,128)(2,1)S(1)} %shard_map.38.refs_1_), channel_id=1, source_target_pairs={{0,8},{1,17},{8,0},{9,25},{16,24},{17,1},{24,16},{25,9},{2,10},{3,... | collective-permute-start | bytes 4866056 | tf_op jit(solution)/shard_map/ppermute | solution.py:193
  7.6 41.0 %collective-permute-start.7 = (bf16[192,4224]{1,0:T(8,128)(2,1)S(1)}, bf16[192,4224]{1,0:T(8,128)(2,1)S(1)}, u32[]{:S(2)}, u32[]{:S(2)}) collective-permute-start(bf16[192,4224]{1,0:T(8,128)(2,1)S(1)} %shard_map.38.refs_1_), channel_id=1, source_target_pairs={{0,2},{2,4},{4,6},{6,0},{1,5},{7,3},{8,10},{10,12},{12,14},{14,8},... | collective-permute-start | bytes 4866056 | tf_op jit(solution)/shard_map/ppermute | solution.py:190
  26.5 14.2 %collective-permute-start.2 = (bf16[192,4224]{1,0:T(8,128)(2,1)S(1)}, bf16[192,4224]{1,0:T(8,128)(2,1)S(1)}, u32[]{:S(2)}, u32[]{:S(2)}) collective-permute-start(bf16[192,4224]{1,0:T(8,128)(2,1)S(1)} %collective-permute-done.1.refs_2_), channel_id=1, source_target_pairs={{0,1},{1,0},{2,3},{3,2},{4,5},{5,4},{6,7},{7,6},{8,9},{9,8},{10,11... | collective-permute-start | bytes 4866056 | tf_op jit(solution)/shard_map/ppermute | solution.py:34
  26.6 8.0 %collective-permute-start.3 = (bf16[48,4224]{1,0:T(8,128)(2,1)S(1)}, bf16[48,4224]{1,0:T(8,128)(2,1)S(1)}, u32[]{:S(2)}, u32[]{:S(2)}) collective-permute-start(bf16[48,4224]{1,0:T(8,128)(2,1)S(1)} %get-tuple-element.12), channel_id=1, source_target_pairs={{0,16},{1,9},{8,24},{9,1},{16,0},{17,25},{24,8},{25,17},{2,18},{3,... | collective-permute-start | bytes 1216520 | tf_op jit(solution)/shard_map/ppermute | solution.py:198
  28.7 10.2 %collective-permute-start.4 = (bf16[48,4224]{1,0:T(8,128)(2,1)S(1)}, bf16[48,4224]{1,0:T(8,128)(2,1)S(1)}, u32[]{:S(2)}, u32[]{:S(2)}) collective-permute-start(bf16[48,4224]{1,0:T(8,128)(2,1)S(1)} %get-tuple-element.11), channel_id=1, source_target_pairs={{0,16},{1,9},{8,24},{9,1},{16,0},{17,25},{24,8},{25,17},{2,18},{3,... | collective-permute-start | bytes 1216520 | tf_op jit(solution)/shard_map/ppermute | solution.py:198
  34.6 4.4 %collective-permute-start.5 = (bf16[48,4224]{1,0:T(8,128)(2,1)S(1)}, bf16[48,4224]{1,0:T(8,128)(2,1)S(1)}, u32[]{:S(2)}, u32[]{:S(2)}) collective-permute-start(bf16[48,4224]{1,0:T(8,128)(2,1)S(1)} %collective-permute-done.3.refs_4_), channel_id=1, source_target_pairs={{0,1},{1,0},{2,3},{3,2},{4,5},{5,4},{6,7},{7,6},{8,9},{9,8},{10,11... | collective-permute-start | bytes 1216520 | tf_op jit(solution)/shard_map/ppermute | solution.py:34
  39.0 1.7 %collective-permute-start.6 = (bf16[48,4224]{1,0:T(8,128)(2,1)S(1)}, bf16[48,4224]{1,0:T(8,128)(2,1)S(1)}, u32[]{:S(2)}, u32[]{:S(2)}) collective-permute-start(bf16[48,4224]{1,0:T(8,128)(2,1)S(1)} %collective-permute-done.4.refs_5_), channel_id=1, source_target_pairs={{0,1},{1,0},{2,3},{3,2},{4,5},{5,4},{6,7},{7,6},{8,9},{9,8},{10,11... | collective-permute-start | bytes 1216520 | tf_op jit(solution)/shard_map/ppermute | solution.py:34
  50.7 2.0 %collective-permute-start.10 = (f32[4,128]{1,0:T(4,128)S(1)}, f32[4,128]{1,0:T(4,128)S(1)}, u32[]{:S(2)}, u32[]{:S(2)}) collective-permute-start(f32[4,128]{1,0:T(4,128)S(1)} %get-tuple-element.10), channel_id=1, source_target_pairs={{0,1},{1,0},{2,3},{3,2},{4,5},{5,4},{6,7},{7,6},{8,9},{9,8},{10,11... | collective-permute-start | bytes 6152 | tf_op jit(solution)/shard_map/ppermute | solution.py:34
  50.8 5.5 %collective-permute-start.8 = (f32[2,128]{1,0:T(2,128)S(1)}, f32[2,128]{1,0:T(2,128)S(1)}, u32[]{:S(2)}, u32[]{:S(2)}) collective-permute-start(f32[2,128]{1,0:T(2,128)S(1)} %get-tuple-element.8), channel_id=1, source_target_pairs={{2,0},{4,2},{6,4},{0,6},{5,1},{3,7},{10,8},{12,10},{14,12},{8,14},... | collective-permute-start | bytes 3080 | tf_op jit(solution)/shard_map/ppermute | solution.py:217
  52.7 4.7 %collective-permute-start.11 = (f32[4,128]{1,0:T(4,128)S(1)}, f32[4,128]{1,0:T(4,128)S(1)}, u32[]{:S(2)}, u32[]{:S(2)}) collective-permute-start(f32[4,128]{1,0:T(4,128)S(1)} %max.23), channel_id=1, source_target_pairs={{0,8},{1,17},{8,0},{9,25},{16,24},{17,1},{24,16},{25,9},{2,10},{3,... | collective-permute-start | bytes 6152 | tf_op jit(solution)/shard_map/ppermute | solution.py:225
  53.9 3.6 %collective-permute-start.12 = (f32[4,128]{1,0:T(4,128)S(1)}, f32[4,128]{1,0:T(4,128)S(1)}, u32[]{:S(2)}, u32[]{:S(2)}) collective-permute-start(f32[4,128]{1,0:T(4,128)S(1)} %max.23), channel_id=1, source_target_pairs={{0,16},{1,9},{8,24},{9,1},{16,0},{17,25},{24,8},{25,17},{2,18},{3,... | collective-permute-start | bytes 6152 | tf_op jit(solution)/shard_map/ppermute | solution.py:225
  54.8 4.5 %collective-permute-start.13 = (f32[4,128]{1,0:T(4,128)S(1)}, f32[4,128]{1,0:T(4,128)S(1)}, u32[]{:S(2)}, u32[]{:S(2)}) collective-permute-start(f32[4,128]{1,0:T(4,128)S(1)} %max.23), channel_id=1, source_target_pairs={{0,24},{8,16},{16,8},{24,0},{1,25},{9,17},{17,9},{25,1},{2,26},{10... | collective-permute-start | bytes 6152 | tf_op jit(solution)/shard_map/ppermute | solution.py:228
  56.3 1.1 %collective-permute-start.9 = (f32[2,128]{1,0:T(2,128)S(1)}, f32[2,128]{1,0:T(2,128)S(1)}, u32[]{:S(2)}, u32[]{:S(2)}) collective-permute-start(f32[2,128]{1,0:T(2,128)S(1)} %collective-permute-done.8), channel_id=1, source_target_pairs={{0,1},{1,0},{2,3},{3,2},{4,5},{5,4},{6,7},{7,6},{8,9},{9,8},{10,11... | collective-permute-start | bytes 3080 | tf_op jit(solution)/shard_map/ppermute | solution.py:34

commit v16 on v15

--- a/solution.py
+++ b/solution.py
@@ -34,51 +34,43 @@
     return lax.ppermute(block, "core", flip(2, 1))
 
 
-def pack_kernel(rows_ref, ids_ref, block_ref):
-    rows, width = rows_ref.shape
-    block_ref[:, :width] = unit_rows(rows_ref[...])
-    ids = ids_ref[...].astype(jnp.float32)
-    meta = jnp.concatenate([ids, jnp.zeros((6, rows), jnp.float32)], axis=0)
-    if rows < LANES:
-        meta = jnp.concatenate([meta, jnp.zeros((8, LANES - rows), jnp.float32)], axis=1)
-    turned = meta.T[:rows]
+def pack_into(block_ref, start, rows, ids):
+    count, width = rows.shape
+    place = pl.ds(start, count)
+    block_ref[place, :width] = unit_rows(rows)
+    meta = jnp.concatenate([ids.astype(jnp.float32), jnp.zeros((6, count), jnp.float32)], axis=0)
+    if count < LANES:
+        meta = jnp.concatenate([meta, jnp.zeros((8, LANES - count), jnp.float32)], axis=1)
+    turned = meta.T[:count]
     cluster, order = turned[:, 0:1] + 1.0, turned[:, 1:2]
     high = jnp.floor(order / 256.0)
-    lane = lax.broadcasted_iota(jnp.int32, (rows, LANES), 1)
+    lane = lax.broadcasted_iota(jnp.int32, (count, LANES), 1)
     tail = jnp.where(lane == 0, cluster, jnp.where(lane == 1, high, order - 256.0 * high))
-    block_ref[:, width:] = jnp.where(lane < 3, tail, 0.0).astype(jnp.bfloat16)
-
-
-def pack(rows, cluster_ids, order_index):
-    count, width = rows.shape
+    block_ref[place, width:] = jnp.where(lane < 3, tail, 0.0).astype(jnp.bfloat16)
+
+
+def pack_kernel(rows_ref, ids_ref, block_ref):
+    pack_into(block_ref, 0, rows_ref[...], ids_ref[...])
+
+
+def pair_kernel(own_ref, rows_ref, ids_ref, both_ref):
+    count = own_ref.shape[0]
+    both_ref[:count, :] = own_ref[...]
+    pack_into(both_ref, count, rows_ref[...], ids_ref[...])
+
+
+def pack(kernel, operands, count):
+    rows, width = operands[-2].shape
     return pl.pallas_call(
-        pack_kernel,
-        in_specs=[VMEM] * 2,
+        kernel,
+        in_specs=[VMEM] * len(operands),
         out_specs=VMEM,
-        out_shape=jax.ShapeDtypeStruct((count, width + LANES), jnp.bfloat16),
+        out_shape=jax.ShapeDtypeStruct((count * rows, width + LANES), jnp.bfloat16),
         compiler_params=pltpu.CompilerParams(vmem_limit_bytes=8 * 2**20),
         cost_estimate=pl.CostEstimate(
-            flops=4 * count * width, bytes_accessed=4 * count * width, transcendentals=count
+            flops=4 * rows * width, bytes_accessed=4 * rows * width, transcendentals=rows
         ),
-    )(rows, jnp.stack([cluster_ids, order_index]))
-
-
-def pair_kernel(own_ref, other_ref, both_ref):
-    rows = own_ref.shape[0]
-    both_ref[:rows, :] = own_ref[...]
-    both_ref[rows:, :] = other_ref[...]
-
-
-def pair(own, other):
-    rows, width = own.shape
-    return pl.pallas_call(
-        pair_kernel,
-        in_specs=[VMEM] * 2,
-        out_specs=VMEM,
-        out_shape=jax.ShapeDtypeStruct((2 * rows, width), own.dtype),
-        compiler_params=pltpu.CompilerParams(vmem_limit_bytes=8 * 2**20),
-        cost_estimate=pl.CostEstimate(flops=0, bytes_accessed=8 * rows * width, transcendentals=0),
-    )(own, other)
+    )(*operands)
 
 
 def own_kernel(*refs):
@@ -179,8 +171,9 @@
     groups, length = lax.axis_size("group"), lax.axis_size("z")
     z, core = lax.axis_index("z"), lax.axis_index("core")
     plane_axes, line_axes = ("group", "core"), ("z", "core")
-    own = pack(embeddings, cluster_ids, order_index)
-    both = pair(own, swap(own))
+    ids = jnp.stack([cluster_ids, order_index])
+    own = pack(pack_kernel, [embeddings, ids], 1)
+    both = pack(pair_kernel, [own, swap(embeddings), swap(ids)], 2)
 
     routes = [ring_pairs(length, shift) for shift in range(1, length // 2 + 1)]
     trips = []
@@ -218,6 +211,7 @@
         for here, best in ((2 * z + core, back[0:1]), (2 * z + (core ^ 1), swap(back)[1:2])):
             sent = functools.reduce(jnp.logical_or, [here == a for a, _ in trip])
             bests.append(jnp.where(sent, best, -1.0))
+    bests.append(lax.ppermute(merged[0], "group", flip(groups, last))[2:3])
     ways = [(0, 0, partners[-1])]
     ways += [(1 + k // 2, 2 * (k % 2), way) for k, way in enumerate(partners[:-1])]
     for chunk, row, (first, second) in ways:
@@ -225,7 +219,6 @@
             got = lax.ppermute(merged[chunk], plane_axes, group_trip(groups, *order))
             bests.append(got[row : row + 1])
             row += 1
-    bests.append(lax.ppermute(merged[0], "group", flip(groups, last))[2:3])
     bests.append(merged[0][3:4])
     return functools.reduce(jnp.maximum, bests)[0, :rows]
 

time: 60 us -> 57.3 us (0.955)
  waiting for transfers between devices: 38.2 us -> 35.2 us
    ppermute x6 -> x7, waiting for transfers between devices: 4.65 us -> 2.7 us  [swap(): return lax.ppermute(block, 'core', flip(2, 1))]
    ppermute x1, waiting for transfers between devices: 1.8 us -> 0.01 us  [local(): bests.append(lax.ppermute(merged[0], 'group', flip(groups, last))[2:3])]
    ppermute x2, waiting for transfers between devices: 0.05 us -> 0.92 us  [local(): got = lax.ppermute(merged[chunk], plane_axes, group_trip(groups, *order))]
  transfers between devices with their start and end apart: 14 -> 15, of which waited for: 8 -> 8; matrix products, arithmetic and copies ran while one was open for 0% -> 1% of each run, Pallas kernels for 3% -> 4%
where the time goes in v16:
time: 57.3 us; the launch traced here: 57.1 us
  waiting for transfers between devices  35.2 us (61%)
  starting transfers between devices  14.9 us (26%)
  Pallas kernels  4.5 us (8%)
  local copies, waits for them, and re-layouts  1.7 us (3%)
  other arithmetic  0.69 us (1%)
    ppermute x1, waiting for transfers between devices, local(): lax.ppermute(both, plane_axes, group_trip(groups, *way))  15.4 us
    ppermute x2, waiting for transfers between devices, local(): corner = [lax.ppermute(part, plane_axes, relay) for part in corner]  10.2 us
    ppermute x1, waiting for transfers between devices, local(): visitors = [lax.ppermute(both, line_axes, trip) for trip in trips]  6.02 us
    pallas_call x2, Pallas kernels, call(): pl.pallas_call(kernel, in_specs=[VMEM] * len(operands), out_specs=[VMEM]...  3.85 us
    ppermute x1, starting transfers between devices, local(): visitors = [lax.ppermute(both, line_axes, trip) for trip in trips]  3.47 us
    ppermute x1, starting transfers between devices, local(): lax.ppermute(both, plane_axes, group_trip(groups, *way))  3 us
    ppermute x7, waiting for transfers between devices, swap(): return lax.ppermute(block, 'core', flip(2, 1))  2.7 us
    ppermute x2, starting transfers between devices, local(): corner = [lax.ppermute(part, plane_axes, relay) for part in corner]  2.19 us
  transfers between devices with their start and end apart: 15, of which 8 were waited for; matrix products, arithmetic and copies ran while one was open for 1% of the time, Pallas kernels for 4%

profile of v16, /device:TPU:0, one launch (start us, length us, event | category | flops | bytes accessed | tf_op | source)
XLA Modules:
  0.0 57.1 jit_solution(4193461955262534521)
XLA Ops:
  0.0 0.5 collective-permute-start
  0.5 0.7 %pad_add_fusion.ids_ref = s32[2,96]{1,0:T(2,128)S(1)} fusion(s32[1,96]{1,0:T(1,128)} %bitcast.4, s32[1,96]{1,0:T(1,128)} %bitcast.5), kind=kLoop, calls=%fused_computation | loop fusion | flops 192 | bytes 1536 | tf_op jit(solution)/shard_map/stack | solution.py:174
  1.2 1.1 %copy-done = bf16[96,4096]{1,0:T(8,128)(2,1)S(1)} copy-done((bf16[96,4096]{1,0:T(8,128)(2,1)S(1)}, bf16[96,4096]{1,0:T(8,128)(2,1)}, u32[]{:S(2)}) %copy-start) | copy-done | bytes 786456
  2.3 0.3 shard_map.37.own_ref.refs_0_
  2.6 0.3 shard_map.38.refs_1_
  3.0 3.0 %collective-permute-start.2 = (bf16[192,4224]{1,0:T(8,128)(2,1)S(1)}, bf16[192,4224]{1,0:T(8,128)(2,1)S(1)}, u32[]{:S(2)}, u32[]{:S(2)}) collective-permute-start(bf16[192,4224]{1,0:T(8,128)(2,1)S(1)} %shard_map.38.refs_1_), channel_id=1, source_target_pairs={{0,8},{1,17},{8,0},{9,25},{16,24},{17,1},{24,16},{25,9},{2,10},{3,... | collective-permute-start | bytes 4866056 | tf_op jit(solution)/shard_map/ppermute | solution.py:186
  6.0 3.5 %collective-permute-start.8 = (bf16[192,4224]{1,0:T(8,128)(2,1)S(1)}, bf16[192,4224]{1,0:T(8,128)(2,1)S(1)}, u32[]{:S(2)}, u32[]{:S(2)}) collective-permute-start(bf16[192,4224]{1,0:T(8,128)(2,1)S(1)} %shard_map.38.refs_1_), channel_id=1, source_target_pairs={{0,2},{2,4},{4,6},{6,0},{1,5},{7,3},{8,10},{10,12},{12,14},{14,8},... | collective-permute-start | bytes 4866056 | tf_op jit(solution)/shard_map/ppermute | solution.py:183
  9.5 15.4 %collective-permute-done.2.refs_2_ = bf16[192,4224]{1,0:T(8,128)(2,1)S(1)} collective-permute-done((bf16[192,4224]{1,0:T(8,128)(2,1)S(1)}, bf16[192,4224]{1,0:T(8,128)(2,1)S(1)}, u32[]{:S(2)}, u32[]{:S(2)}) %collective-permute-start.2) | collective-permute-done | bytes 1622048 | tf_op jit(solution)/shard_map/ppermute | solution.py:186
  25.0 2.1 %collective-permute-start.4 = (bf16[48,4224]{1,0:T(8,128)(2,1)S(1)}, bf16[48,4224]{1,0:T(8,128)(2,1)S(1)}, u32[]{:S(2)}, u32[]{:S(2)}) collective-permute-start(bf16[48,4224]{1,0:T(8,128)(2,1)S(1)} %get-tuple-element.12), channel_id=1, source_target_pairs={{0,16},{1,9},{8,24},{9,1},{16,0},{17,25},{24,8},{25,17},{2,18},{3,... | collective-permute-start | bytes 1216520 | tf_op jit(solution)/shard_map/ppermute | solution.py:191
  27.2 5.8 %collective-permute-done.4.refs_4_ = bf16[48,4224]{1,0:T(8,128)(2,1)S(1)} collective-permute-done((bf16[48,4224]{1,0:T(8,128)(2,1)S(1)}, bf16[48,4224]{1,0:T(8,128)(2,1)S(1)}, u32[]{:S(2)}, u32[]{:S(2)}) %collective-permute-start.4) | collective-permute-done | bytes 405536 | tf_op jit(solution)/shard_map/ppermute | solution.py:191
  33.0 4.3 %collective-permute-done.5.refs_5_ = bf16[48,4224]{1,0:T(8,128)(2,1)S(1)} collective-permute-done((bf16[48,4224]{1,0:T(8,128)(2,1)S(1)}, bf16[48,4224]{1,0:T(8,128)(2,1)S(1)}, u32[]{:S(2)}, u32[]{:S(2)}) %collective-permute-start.5) | collective-permute-done | bytes 405536 | tf_op jit(solution)/shard_map/ppermute | solution.py:191
  37.3 1.7 %collective-permute-done.7.refs_7_ = bf16[48,4224]{1,0:T(8,128)(2,1)S(1)} collective-permute-done((bf16[48,4224]{1,0:T(8,128)(2,1)S(1)}, bf16[48,4224]{1,0:T(8,128)(2,1)S(1)}, u32[]{:S(2)}, u32[]{:S(2)}) %collective-permute-start.7) | collective-permute-done | bytes 405536 | tf_op jit(solution)/shard_map/ppermute | solution.py:34
  39.1 1.8 %shard_map.39.refs_8_ = f32[1,128]{1,0:T(1,128)S(1)} custom-call(bf16[96,4224]{1,0:T(8,128)(2,1)S(1)} %shard_map.37.own_ref.refs_0_, bf16[192,4224]{1,0:T(8,128)(2,1)S(1)} %shard_map.38.refs_1_, bf16[192,4224]{1,0:T(8,128)(2,1)S(1)} %collective-permute-done.2.refs_2_, bf16[192,4224]{1,0:T(8,128)(2,1)S(1)} %collective-permute-done.3.refs_3_, ...), custom_call_target="tpu_custom_call" | custom-call | flops 805306368 | bytes 7340032 | tf_op jit(solution)/shard_map/pallas_call | solution.py:147
  40.9 6.0 %collective-permute-done.8.refs_0_ = bf16[192,4224]{1,0:T(8,128)(2,1)S(1)} collective-permute-done((bf16[192,4224]{1,0:T(8,128)(2,1)S(1)}, bf16[192,4224]{1,0:T(8,128)(2,1)S(1)}, u32[]{:S(2)}, u32[]{:S(2)}) %collective-permute-start.8) | collective-permute-done | bytes 1622048 | tf_op jit(solution)/shard_map/ppermute | solution.py:183
  46.9 2.0 %shard_map.40 = (f32[2,128]{1,0:T(2,128)S(1)}, f32[4,128]{1,0:T(4,128)S(1)}, f32[4,128]{1,0:T(4,128)S(1)}) custom-call(bf16[192,4224]{1,0:T(8,128)(2,1)S(1)} %collective-permute-done.8.refs_0_, bf16[192,4224]{1,0:T(8,128)(2,1)S(1)} %shard_map.38.refs_1_, bf16[192,4224]{1,0:T(8,128)(2,1)S(1)} %collective-permute-done.2.refs_2_, ...), custom_call_target="tpu_custom_call" | custom-call | flops 1610612736 | bytes 8388608 | tf_op jit(solution)/shard_map/pallas_call | solution.py:147
  49.0 1.9 %collective-permute-start.9 = (f32[2,128]{1,0:T(2,128)S(1)}, f32[2,128]{1,0:T(2,128)S(1)}, u32[]{:S(2)}, u32[]{:S(2)}) collective-permute-start(f32[2,128]{1,0:T(2,128)S(1)} %get-tuple-element.8), channel_id=1, source_target_pairs={{2,0},{4,2},{6,4},{0,6},{5,1},{3,7},{10,8},{12,10},{14,12},{8,14},... | collective-permute-start | bytes 3080 | tf_op jit(solution)/shard_map/ppermute | solution.py:210
  51.0 1.5 %collective-permute-start.12 = (f32[4,128]{1,0:T(4,128)S(1)}, f32[4,128]{1,0:T(4,128)S(1)}, u32[]{:S(2)}, u32[]{:S(2)}) collective-permute-start(f32[4,128]{1,0:T(4,128)S(1)} %max.23), channel_id=1, source_target_pairs={{0,24},{8,16},{16,8},{24,0},{1,25},{9,17},{17,9},{25,1},{2,26},{10... | collective-permute-start | bytes 6152 | tf_op jit(solution)/shard_map/ppermute | solution.py:214
  52.5 0.5 collective-permute-start.13
  53.0 1.5 %collective-permute-start.14 = (f32[4,128]{1,0:T(4,128)S(1)}, f32[4,128]{1,0:T(4,128)S(1)}, u32[]{:S(2)}, u32[]{:S(2)}) collective-permute-start(f32[4,128]{1,0:T(4,128)S(1)} %max.23), channel_id=1, source_target_pairs={{0,16},{1,9},{8,24},{9,1},{16,0},{17,25},{24,8},{25,17},{2,18},{3,... | collective-permute-start | bytes 6152 | tf_op jit(solution)/shard_map/ppermute | solution.py:219
  54.5 0.2 collective-permute-start.10
  54.7 1.0 %collective-permute-done.10 = f32[2,128]{1,0:T(2,128)S(1)} collective-permute-done((f32[2,128]{1,0:T(2,128)S(1)}, f32[2,128]{1,0:T(2,128)S(1)}, u32[]{:S(2)}, u32[]{:S(2)}) %collective-permute-start.10) | collective-permute-done | bytes 1056 | tf_op jit(solution)/shard_map/ppermute | solution.py:34
  55.7 0.4 collective-permute-done.13
  56.1 0.5 collective-permute-done.14
  56.6 0.5 slice_bitcast_fusion
  (17 shorter events, 0.3 us)
Async XLA Ops:
  0.0 2.6 %collective-permute-start = (bf16[96,4096]{1,0:T(8,128)(2,1)}, bf16[96,4096]{1,0:T(8,128)(2,1)S(1)}, u32[]{:S(2)}, u32[]{:S(2)}) collective-permute-start(bf16[96,4096]{1,0:T(8,128)(2,1)} %rows_ref.1), channel_id=1, source_target_pairs={{0,1},{1,0},{2,3},{3,2},{4,5},{5,4},{6,7},{7,6},{8,9},{9,8},{10,11... | collective-permute-start | bytes 2359304 | tf_op jit(solution)/shard_map/ppermute | solution.py:34
  1.1 1.5 %collective-permute-start.1 = (s32[2,96]{1,0:T(2,128)S(1)}, s32[2,96]{1,0:T(2,128)S(1)}, u32[]{:S(2)}, u32[]{:S(2)}) collective-permute-start(s32[2,96]{1,0:T(2,128)S(1)} %pad_add_fusion.ids_ref), channel_id=1, source_target_pairs={{0,1},{1,0},{2,3},{3,2},{4,5},{5,4},{6,7},{7,6},{8,9},{9,8},{10,11... | collective-permute-start | bytes 2312 | tf_op jit(solution)/shard_map/ppermute | solution.py:34
  1.2 1.1 %copy-start = (bf16[96,4096]{1,0:T(8,128)(2,1)S(1)}, bf16[96,4096]{1,0:T(8,128)(2,1)}, u32[]{:S(2)}) copy-start(bf16[96,4096]{1,0:T(8,128)(2,1)} %rows_ref.1) | copy-start | bytes 2359300
  3.0 21.9 %collective-permute-start.2 = (bf16[192,4224]{1,0:T(8,128)(2,1)S(1)}, bf16[192,4224]{1,0:T(8,128)(2,1)S(1)}, u32[]{:S(2)}, u32[]{:S(2)}) collective-permute-start(bf16[192,4224]{1,0:T(8,128)(2,1)S(1)} %shard_map.38.refs_1_), channel_id=1, source_target_pairs={{0,8},{1,17},{8,0},{9,25},{16,24},{17,1},{24,16},{25,9},{2,10},{3,... | collective-permute-start | bytes 4866056 | tf_op jit(solution)/shard_map/ppermute | solution.py:186
  6.0 40.9 %collective-permute-start.8 = (bf16[192,4224]{1,0:T(8,128)(2,1)S(1)}, bf16[192,4224]{1,0:T(8,128)(2,1)S(1)}, u32[]{:S(2)}, u32[]{:S(2)}) collective-permute-start(bf16[192,4224]{1,0:T(8,128)(2,1)S(1)} %shard_map.38.refs_1_), channel_id=1, source_target_pairs={{0,2},{2,4},{4,6},{6,0},{1,5},{7,3},{8,10},{10,12},{12,14},{14,8},... | collective-permute-start | bytes 4866056 | tf_op jit(solution)/shard_map/ppermute | solution.py:183
  24.9 14.2 %collective-permute-start.3 = (bf16[192,4224]{1,0:T(8,128)(2,1)S(1)}, bf16[192,4224]{1,0:T(8,128)(2,1)S(1)}, u32[]{:S(2)}, u32[]{:S(2)}) collective-permute-start(bf16[192,4224]{1,0:T(8,128)(2,1)S(1)} %collective-permute-done.2.refs_2_), channel_id=1, source_target_pairs={{0,1},{1,0},{2,3},{3,2},{4,5},{5,4},{6,7},{7,6},{8,9},{9,8},{10,11... | collective-permute-start | bytes 4866056 | tf_op jit(solution)/shard_map/ppermute | solution.py:34
  25.0 8.0 %collective-permute-start.4 = (bf16[48,4224]{1,0:T(8,128)(2,1)S(1)}, bf16[48,4224]{1,0:T(8,128)(2,1)S(1)}, u32[]{:S(2)}, u32[]{:S(2)}) collective-permute-start(bf16[48,4224]{1,0:T(8,128)(2,1)S(1)} %get-tuple-element.12), channel_id=1, source_target_pairs={{0,16},{1,9},{8,24},{9,1},{16,0},{17,25},{24,8},{25,17},{2,18},{3,... | collective-permute-start | bytes 1216520 | tf_op jit(solution)/shard_map/ppermute | solution.py:191
  27.1 10.2 %collective-permute-start.5 = (bf16[48,4224]{1,0:T(8,128)(2,1)S(1)}, bf16[48,4224]{1,0:T(8,128)(2,1)S(1)}, u32[]{:S(2)}, u32[]{:S(2)}) collective-permute-start(bf16[48,4224]{1,0:T(8,128)(2,1)S(1)} %get-tuple-element.11), channel_id=1, source_target_pairs={{0,16},{1,9},{8,24},{9,1},{16,0},{17,25},{24,8},{25,17},{2,18},{3,... | collective-permute-start | bytes 1216520 | tf_op jit(solution)/shard_map/ppermute | solution.py:191
  33.0 4.4 %collective-permute-start.6 = (bf16[48,4224]{1,0:T(8,128)(2,1)S(1)}, bf16[48,4224]{1,0:T(8,128)(2,1)S(1)}, u32[]{:S(2)}, u32[]{:S(2)}) collective-permute-start(bf16[48,4224]{1,0:T(8,128)(2,1)S(1)} %collective-permute-done.4.refs_4_), channel_id=1, source_target_pairs={{0,1},{1,0},{2,3},{3,2},{4,5},{5,4},{6,7},{7,6},{8,9},{9,8},{10,11... | collective-permute-start | bytes 1216520 | tf_op jit(solution)/shard_map/ppermute | solution.py:34
  37.3 1.7 %collective-permute-start.7 = (bf16[48,4224]{1,0:T(8,128)(2,1)S(1)}, bf16[48,4224]{1,0:T(8,128)(2,1)S(1)}, u32[]{:S(2)}, u32[]{:S(2)}) collective-permute-start(bf16[48,4224]{1,0:T(8,128)(2,1)S(1)} %collective-permute-done.5.refs_5_), channel_id=1, source_target_pairs={{0,1},{1,0},{2,3},{3,2},{4,5},{5,4},{6,7},{7,6},{8,9},{9,8},{10,11... | collective-permute-start | bytes 1216520 | tf_op jit(solution)/shard_map/ppermute | solution.py:34
  49.0 2.0 %collective-permute-start.11 = (f32[4,128]{1,0:T(4,128)S(1)}, f32[4,128]{1,0:T(4,128)S(1)}, u32[]{:S(2)}, u32[]{:S(2)}) collective-permute-start(f32[4,128]{1,0:T(4,128)S(1)} %get-tuple-element.10), channel_id=1, source_target_pairs={{0,1},{1,0},{2,3},{3,2},{4,5},{5,4},{6,7},{7,6},{8,9},{9,8},{10,11... | collective-permute-start | bytes 6152 | tf_op jit(solution)/shard_map/ppermute | solution.py:34
  49.0 5.5 %collective-permute-start.9 = (f32[2,128]{1,0:T(2,128)S(1)}, f32[2,128]{1,0:T(2,128)S(1)}, u32[]{:S(2)}, u32[]{:S(2)}) collective-permute-start(f32[2,128]{1,0:T(2,128)S(1)} %get-tuple-element.8), channel_id=1, source_target_pairs={{2,0},{4,2},{6,4},{0,6},{5,1},{3,7},{10,8},{12,10},{14,12},{8,14},... | collective-permute-start | bytes 3080 | tf_op jit(solution)/shard_map/ppermute | solution.py:210
  51.0 4.7 %collective-permute-start.12 = (f32[4,128]{1,0:T(4,128)S(1)}, f32[4,128]{1,0:T(4,128)S(1)}, u32[]{:S(2)}, u32[]{:S(2)}) collective-permute-start(f32[4,128]{1,0:T(4,128)S(1)} %max.23), channel_id=1, source_target_pairs={{0,24},{8,16},{16,8},{24,0},{1,25},{9,17},{17,9},{25,1},{2,26},{10... | collective-permute-start | bytes 6152 | tf_op jit(solution)/shard_map/ppermute | solution.py:214
  52.5 3.6 %collective-permute-start.13 = (f32[4,128]{1,0:T(4,128)S(1)}, f32[4,128]{1,0:T(4,128)S(1)}, u32[]{:S(2)}, u32[]{:S(2)}) collective-permute-start(f32[4,128]{1,0:T(4,128)S(1)} %max.23), channel_id=1, source_target_pairs={{0,8},{1,17},{8,0},{9,25},{16,24},{17,1},{24,16},{25,9},{2,10},{3,... | collective-permute-start | bytes 6152 | tf_op jit(solution)/shard_map/ppermute | solution.py:219
  53.0 3.6 %collective-permute-start.14 = (f32[4,128]{1,0:T(4,128)S(1)}, f32[4,128]{1,0:T(4,128)S(1)}, u32[]{:S(2)}, u32[]{:S(2)}) collective-permute-start(f32[4,128]{1,0:T(4,128)S(1)} %max.23), channel_id=1, source_target_pairs={{0,16},{1,9},{8,24},{9,1},{16,0},{17,25},{24,8},{25,17},{2,18},{3,... | collective-permute-start | bytes 6152 | tf_op jit(solution)/shard_map/ppermute | solution.py:219
  54.5 1.1 %collective-permute-start.10 = (f32[2,128]{1,0:T(2,128)S(1)}, f32[2,128]{1,0:T(2,128)S(1)}, u32[]{:S(2)}, u32[]{:S(2)}) collective-permute-start(f32[2,128]{1,0:T(2,128)S(1)} %collective-permute-done.9), channel_id=1, source_target_pairs={{0,1},{1,0},{2,3},{3,2},{4,5},{5,4},{6,7},{7,6},{8,9},{9,8},{10,11... | collective-permute-start | bytes 3080 | tf_op jit(solution)/shard_map/ppermute | solution.py:34

commit v17 on v16

--- a/solution.py
+++ b/solution.py
@@ -23,11 +23,18 @@
     return (values * lax.rsqrt(total)).astype(jnp.bfloat16)
 
 
-def ring_pairs(length, shift):
-    if 2 * shift < length:
-        return [(k, (k + shift) % length) for k in range(length)]
-    pairs = [(k, k + shift) for k in range(length // 2)]
-    return [pair[:: 1 - 2 * (pair[0] % 2)] for pair in pairs]
+def line_trips(length):
+    if length == 4:
+        ways = [[(0, 1), (2, 3), (3, 0)], [(0, 2), (2, 1), (1, 3)]]
+    else:
+        ways = [[(k, (k + shift) % length) for k in range(length)] for shift in range(1, (length + 1) // 2)]
+        if length % 2 == 0:
+            pairs = [(k, k + length // 2) for k in range(length // 2)]
+            ways.append([pair[:: 1 - 2 * (pair[0] % 2)] for pair in pairs])
+    return [
+        [(2 * a + core, 2 * b + core) for core, way in enumerate(ways[first : first + 2]) for a, b in way]
+        for first in range(0, len(ways), 2)
+    ]
 
 
 def swap(block):
@@ -175,11 +182,7 @@
     own = pack(pack_kernel, [embeddings, ids], 1)
     both = pack(pair_kernel, [own, swap(embeddings), swap(ids)], 2)
 
-    routes = [ring_pairs(length, shift) for shift in range(1, length // 2 + 1)]
-    trips = []
-    for first in range(0, len(routes), 2):
-        ways = enumerate(routes[first : first + 2])
-        trips.append([(2 * a + way, 2 * b + way) for way, route in ways for a, b in route])
+    trips = line_trips(length)
     visitors = [lax.ppermute(both, line_axes, trip) for trip in trips]
 
     partners = [(s, s + 1) for s in range(1, groups - 1, 2)]

time: 57.3 us -> 61.1 us (1.066)
  starting transfers between devices: 14.9 us -> 19.3 us
    ppermute x1, starting transfers between devices: 1.92 us -> 6.5 us  [local(): back = lax.ppermute(part, line_axes, [(b, a) for a, b in trip])]
    ppermute x1, waiting for transfers between devices: 6.02 us -> 4.21 us  [local(): visitors = [lax.ppermute(both, line_axes, trip) for trip in trips]]
    ppermute x2, waiting for transfers between devices: 0.92 us -> 1.95 us  [local(): got = lax.ppermute(merged[chunk], plane_axes, group_trip(groups, *order))]
  transfers between devices with their start and end apart: 15 -> 15, of which waited for: 8 -> 8; matrix products, arithmetic and copies ran while one was open for 1% -> 1% of each run, Pallas kernels for 4% -> 3%
where the time goes in v17:
time: 61.1 us; the launch traced here: 60.9 us
  waiting for transfers between devices  34.6 us (57%)
  starting transfers between devices  19.3 us (32%)
  Pallas kernels  4.5 us (7%)
  local copies, waits for them, and re-layouts  1.7 us (3%)
  other arithmetic  0.69 us (1%)
    ppermute x1, waiting for transfers between devices, local(): lax.ppermute(both, plane_axes, group_trip(groups, *way))  15.4 us
    ppermute x2, waiting for transfers between devices, local(): corner = [lax.ppermute(part, plane_axes, relay) for part in corner]  10.2 us
    ppermute x1, starting transfers between devices, local(): back = lax.ppermute(part, line_axes, [(b, a) for a, b in trip])  6.5 us
    ppermute x1, waiting for transfers between devices, local(): visitors = [lax.ppermute(both, line_axes, trip) for trip in trips]  4.21 us
    pallas_call x2, Pallas kernels, call(): pl.pallas_call(kernel, in_specs=[VMEM] * len(operands), out_specs=[VMEM]...  3.85 us
    ppermute x1, starting transfers between devices, local(): visitors = [lax.ppermute(both, line_axes, trip) for trip in trips]  3.47 us
    ppermute x1, starting transfers between devices, local(): lax.ppermute(both, plane_axes, group_trip(groups, *way))  3 us
    ppermute x7, waiting for transfers between devices, swap(): return lax.ppermute(block, 'core', flip(2, 1))  2.88 us
  transfers between devices with their start and end apart: 15, of which 8 were waited for; matrix products, arithmetic and copies ran while one was open for 1% of the time, Pallas kernels for 3%

profile of v17, /device:TPU:0, one launch (start us, length us, event | category | flops | bytes accessed | tf_op | source)
XLA Modules:
  0.0 60.9 jit_solution(8281167309734920581)
XLA Ops:
  0.0 0.5 collective-permute-start
  0.5 0.7 %pad_add_fusion.ids_ref = s32[2,96]{1,0:T(2,128)S(1)} fusion(s32[1,96]{1,0:T(1,128)} %bitcast.4, s32[1,96]{1,0:T(1,128)} %bitcast.5), kind=kLoop, calls=%fused_computation | loop fusion | flops 192 | bytes 1536 | tf_op jit(solution)/shard_map/stack | solution.py:181
  1.2 1.1 %copy-done = bf16[96,4096]{1,0:T(8,128)(2,1)S(1)} copy-done((bf16[96,4096]{1,0:T(8,128)(2,1)S(1)}, bf16[96,4096]{1,0:T(8,128)(2,1)}, u32[]{:S(2)}) %copy-start) | copy-done | bytes 786456
  2.3 0.3 shard_map.37.own_ref.refs_0_
  2.6 0.3 shard_map.38.refs_1_
  3.0 3.0 %collective-permute-start.2 = (bf16[192,4224]{1,0:T(8,128)(2,1)S(1)}, bf16[192,4224]{1,0:T(8,128)(2,1)S(1)}, u32[]{:S(2)}, u32[]{:S(2)}) collective-permute-start(bf16[192,4224]{1,0:T(8,128)(2,1)S(1)} %shard_map.38.refs_1_), channel_id=1, source_target_pairs={{0,8},{1,17},{8,0},{9,25},{16,24},{17,1},{24,16},{25,9},{2,10},{3,... | collective-permute-start | bytes 4866056 | tf_op jit(solution)/shard_map/ppermute | solution.py:189
  6.0 3.5 %collective-permute-start.8 = (bf16[192,4224]{1,0:T(8,128)(2,1)S(1)}, bf16[192,4224]{1,0:T(8,128)(2,1)S(1)}, u32[]{:S(2)}, u32[]{:S(2)}) collective-permute-start(bf16[192,4224]{1,0:T(8,128)(2,1)S(1)} %shard_map.38.refs_1_), channel_id=1, source_target_pairs={{0,2},{4,6},{6,0},{1,5},{5,3},{3,7},{8,10},{12,14},{14,8},{9,13},{... | collective-permute-start | bytes 4866056 | tf_op jit(solution)/shard_map/ppermute | solution.py:186
  9.5 15.4 %collective-permute-done.2.refs_2_ = bf16[192,4224]{1,0:T(8,128)(2,1)S(1)} collective-permute-done((bf16[192,4224]{1,0:T(8,128)(2,1)S(1)}, bf16[192,4224]{1,0:T(8,128)(2,1)S(1)}, u32[]{:S(2)}, u32[]{:S(2)}) %collective-permute-start.2) | collective-permute-done | bytes 1622048 | tf_op jit(solution)/shard_map/ppermute | solution.py:189
  25.0 2.1 %collective-permute-start.4 = (bf16[48,4224]{1,0:T(8,128)(2,1)S(1)}, bf16[48,4224]{1,0:T(8,128)(2,1)S(1)}, u32[]{:S(2)}, u32[]{:S(2)}) collective-permute-start(bf16[48,4224]{1,0:T(8,128)(2,1)S(1)} %get-tuple-element.12), channel_id=1, source_target_pairs={{0,16},{1,9},{8,24},{9,1},{16,0},{17,25},{24,8},{25,17},{2,18},{3,... | collective-permute-start | bytes 1216520 | tf_op jit(solution)/shard_map/ppermute | solution.py:194
  27.1 0.1 collective-permute-start.5
  27.2 5.8 %collective-permute-done.4.refs_4_ = bf16[48,4224]{1,0:T(8,128)(2,1)S(1)} collective-permute-done((bf16[48,4224]{1,0:T(8,128)(2,1)S(1)}, bf16[48,4224]{1,0:T(8,128)(2,1)S(1)}, u32[]{:S(2)}, u32[]{:S(2)}) %collective-permute-start.4) | collective-permute-done | bytes 405536 | tf_op jit(solution)/shard_map/ppermute | solution.py:194
  33.0 4.3 %collective-permute-done.5.refs_5_ = bf16[48,4224]{1,0:T(8,128)(2,1)S(1)} collective-permute-done((bf16[48,4224]{1,0:T(8,128)(2,1)S(1)}, bf16[48,4224]{1,0:T(8,128)(2,1)S(1)}, u32[]{:S(2)}, u32[]{:S(2)}) %collective-permute-start.5) | collective-permute-done | bytes 405536 | tf_op jit(solution)/shard_map/ppermute | solution.py:194
  37.3 1.7 %collective-permute-done.7.refs_7_ = bf16[48,4224]{1,0:T(8,128)(2,1)S(1)} collective-permute-done((bf16[48,4224]{1,0:T(8,128)(2,1)S(1)}, bf16[48,4224]{1,0:T(8,128)(2,1)S(1)}, u32[]{:S(2)}, u32[]{:S(2)}) %collective-permute-start.7) | collective-permute-done | bytes 405536 | tf_op jit(solution)/shard_map/ppermute | solution.py:41
  39.1 1.8 %shard_map.39.refs_8_ = f32[1,128]{1,0:T(1,128)S(1)} custom-call(bf16[96,4224]{1,0:T(8,128)(2,1)S(1)} %shard_map.37.own_ref.refs_0_, bf16[192,4224]{1,0:T(8,128)(2,1)S(1)} %shard_map.38.refs_1_, bf16[192,4224]{1,0:T(8,128)(2,1)S(1)} %collective-permute-done.2.refs_2_, bf16[192,4224]{1,0:T(8,128)(2,1)S(1)} %collective-permute-done.3.refs_3_, ...), custom_call_target="tpu_custom_call" | custom-call | flops 805306368 | bytes 7340032 | tf_op jit(solution)/shard_map/pallas_call | solution.py:154
  40.9 4.2 %collective-permute-done.8.refs_0_ = bf16[192,4224]{1,0:T(8,128)(2,1)S(1)} collective-permute-done((bf16[192,4224]{1,0:T(8,128)(2,1)S(1)}, bf16[192,4224]{1,0:T(8,128)(2,1)S(1)}, u32[]{:S(2)}, u32[]{:S(2)}) %collective-permute-start.8) | collective-permute-done | bytes 1622048 | tf_op jit(solution)/shard_map/ppermute | solution.py:186
  45.1 2.0 %shard_map.40 = (f32[2,128]{1,0:T(2,128)S(1)}, f32[4,128]{1,0:T(4,128)S(1)}, f32[4,128]{1,0:T(4,128)S(1)}) custom-call(bf16[192,4224]{1,0:T(8,128)(2,1)S(1)} %collective-permute-done.8.refs_0_, bf16[192,4224]{1,0:T(8,128)(2,1)S(1)} %shard_map.38.refs_1_, bf16[192,4224]{1,0:T(8,128)(2,1)S(1)} %collective-permute-done.2.refs_2_, ...), custom_call_target="tpu_custom_call" | custom-call | flops 1610612736 | bytes 8388608 | tf_op jit(solution)/shard_map/pallas_call | solution.py:154
  47.2 6.5 %collective-permute-start.9 = (f32[2,128]{1,0:T(2,128)S(1)}, f32[2,128]{1,0:T(2,128)S(1)}, u32[]{:S(2)}, u32[]{:S(2)}) collective-permute-start(f32[2,128]{1,0:T(2,128)S(1)} %get-tuple-element.8), channel_id=1, source_target_pairs={{2,0},{6,4},{0,6},{5,1},{3,5},{7,3},{10,8},{14,12},{8,14},{13,9},{... | collective-permute-start | bytes 3080 | tf_op jit(solution)/shard_map/ppermute | solution.py:213
  53.7 1.6 %collective-permute-start.12 = (f32[4,128]{1,0:T(4,128)S(1)}, f32[4,128]{1,0:T(4,128)S(1)}, u32[]{:S(2)}, u32[]{:S(2)}) collective-permute-start(f32[4,128]{1,0:T(4,128)S(1)} %max.23), channel_id=1, source_target_pairs={{0,24},{8,16},{16,8},{24,0},{1,25},{9,17},{17,9},{25,1},{2,26},{10... | collective-permute-start | bytes 6152 | tf_op jit(solution)/shard_map/ppermute | solution.py:217
  55.3 1.5 %collective-permute-start.13 = (f32[4,128]{1,0:T(4,128)S(1)}, f32[4,128]{1,0:T(4,128)S(1)}, u32[]{:S(2)}, u32[]{:S(2)}) collective-permute-start(f32[4,128]{1,0:T(4,128)S(1)} %max.23), channel_id=1, source_target_pairs={{0,8},{1,17},{8,0},{9,25},{16,24},{17,1},{24,16},{25,9},{2,10},{3,... | collective-permute-start | bytes 6152 | tf_op jit(solution)/shard_map/ppermute | solution.py:222
  56.8 0.5 collective-permute-start.14
  57.3 1.1 %collective-permute-done.10 = f32[2,128]{1,0:T(2,128)S(1)} collective-permute-done((f32[2,128]{1,0:T(2,128)S(1)}, f32[2,128]{1,0:T(2,128)S(1)}, u32[]{:S(2)}, u32[]{:S(2)}) %collective-permute-start.10) | collective-permute-done | bytes 1056 | tf_op jit(solution)/shard_map/ppermute | solution.py:41
  58.4 0.4 collective-permute-done.13
  58.9 1.5 %collective-permute-done.14 = f32[4,128]{1,0:T(4,128)S(1)} collective-permute-done((f32[4,128]{1,0:T(4,128)S(1)}, f32[4,128]{1,0:T(4,128)S(1)}, u32[]{:S(2)}, u32[]{:S(2)}) %collective-permute-start.14) | collective-permute-done | bytes 2080 | tf_op jit(solution)/shard_map/ppermute | solution.py:222
  60.4 0.5 slice_bitcast_fusion
  (17 shorter events, 0.2 us)
Async XLA Ops:
  0.0 2.6 %collective-permute-start = (bf16[96,4096]{1,0:T(8,128)(2,1)}, bf16[96,4096]{1,0:T(8,128)(2,1)S(1)}, u32[]{:S(2)}, u32[]{:S(2)}) collective-permute-start(bf16[96,4096]{1,0:T(8,128)(2,1)} %rows_ref.1), channel_id=1, source_target_pairs={{0,1},{1,0},{2,3},{3,2},{4,5},{5,4},{6,7},{7,6},{8,9},{9,8},{10,11... | collective-permute-start | bytes 2359304 | tf_op jit(solution)/shard_map/ppermute | solution.py:41
  1.1 1.5 %collective-permute-start.1 = (s32[2,96]{1,0:T(2,128)S(1)}, s32[2,96]{1,0:T(2,128)S(1)}, u32[]{:S(2)}, u32[]{:S(2)}) collective-permute-start(s32[2,96]{1,0:T(2,128)S(1)} %pad_add_fusion.ids_ref), channel_id=1, source_target_pairs={{0,1},{1,0},{2,3},{3,2},{4,5},{5,4},{6,7},{7,6},{8,9},{9,8},{10,11... | collective-permute-start | bytes 2312 | tf_op jit(solution)/shard_map/ppermute | solution.py:41
  1.2 1.1 %copy-start = (bf16[96,4096]{1,0:T(8,128)(2,1)S(1)}, bf16[96,4096]{1,0:T(8,128)(2,1)}, u32[]{:S(2)}) copy-start(bf16[96,4096]{1,0:T(8,128)(2,1)} %rows_ref.1) | copy-start | bytes 2359300
  3.0 21.9 %collective-permute-start.2 = (bf16[192,4224]{1,0:T(8,128)(2,1)S(1)}, bf16[192,4224]{1,0:T(8,128)(2,1)S(1)}, u32[]{:S(2)}, u32[]{:S(2)}) collective-permute-start(bf16[192,4224]{1,0:T(8,128)(2,1)S(1)} %shard_map.38.refs_1_), channel_id=1, source_target_pairs={{0,8},{1,17},{8,0},{9,25},{16,24},{17,1},{24,16},{25,9},{2,10},{3,... | collective-permute-start | bytes 4866056 | tf_op jit(solution)/shard_map/ppermute | solution.py:189
  6.0 39.1 %collective-permute-start.8 = (bf16[192,4224]{1,0:T(8,128)(2,1)S(1)}, bf16[192,4224]{1,0:T(8,128)(2,1)S(1)}, u32[]{:S(2)}, u32[]{:S(2)}) collective-permute-start(bf16[192,4224]{1,0:T(8,128)(2,1)S(1)} %shard_map.38.refs_1_), channel_id=1, source_target_pairs={{0,2},{4,6},{6,0},{1,5},{5,3},{3,7},{8,10},{12,14},{14,8},{9,13},{... | collective-permute-start | bytes 4866056 | tf_op jit(solution)/shard_map/ppermute | solution.py:186
  24.9 14.2 %collective-permute-start.3 = (bf16[192,4224]{1,0:T(8,128)(2,1)S(1)}, bf16[192,4224]{1,0:T(8,128)(2,1)S(1)}, u32[]{:S(2)}, u32[]{:S(2)}) collective-permute-start(bf16[192,4224]{1,0:T(8,128)(2,1)S(1)} %collective-permute-done.2.refs_2_), channel_id=1, source_target_pairs={{0,1},{1,0},{2,3},{3,2},{4,5},{5,4},{6,7},{7,6},{8,9},{9,8},{10,11... | collective-permute-start | bytes 4866056 | tf_op jit(solution)/shard_map/ppermute | solution.py:41
  25.0 8.0 %collective-permute-start.4 = (bf16[48,4224]{1,0:T(8,128)(2,1)S(1)}, bf16[48,4224]{1,0:T(8,128)(2,1)S(1)}, u32[]{:S(2)}, u32[]{:S(2)}) collective-permute-start(bf16[48,4224]{1,0:T(8,128)(2,1)S(1)} %get-tuple-element.12), channel_id=1, source_target_pairs={{0,16},{1,9},{8,24},{9,1},{16,0},{17,25},{24,8},{25,17},{2,18},{3,... | collective-permute-start | bytes 1216520 | tf_op jit(solution)/shard_map/ppermute | solution.py:194
  27.1 10.2 %collective-permute-start.5 = (bf16[48,4224]{1,0:T(8,128)(2,1)S(1)}, bf16[48,4224]{1,0:T(8,128)(2,1)S(1)}, u32[]{:S(2)}, u32[]{:S(2)}) collective-permute-start(bf16[48,4224]{1,0:T(8,128)(2,1)S(1)} %get-tuple-element.11), channel_id=1, source_target_pairs={{0,16},{1,9},{8,24},{9,1},{16,0},{17,25},{24,8},{25,17},{2,18},{3,... | collective-permute-start | bytes 1216520 | tf_op jit(solution)/shard_map/ppermute | solution.py:194
  33.0 4.4 %collective-permute-start.6 = (bf16[48,4224]{1,0:T(8,128)(2,1)S(1)}, bf16[48,4224]{1,0:T(8,128)(2,1)S(1)}, u32[]{:S(2)}, u32[]{:S(2)}) collective-permute-start(bf16[48,4224]{1,0:T(8,128)(2,1)S(1)} %collective-permute-done.4.refs_4_), channel_id=1, source_target_pairs={{0,1},{1,0},{2,3},{3,2},{4,5},{5,4},{6,7},{7,6},{8,9},{9,8},{10,11... | collective-permute-start | bytes 1216520 | tf_op jit(solution)/shard_map/ppermute | solution.py:41
  37.3 1.7 %collective-permute-start.7 = (bf16[48,4224]{1,0:T(8,128)(2,1)S(1)}, bf16[48,4224]{1,0:T(8,128)(2,1)S(1)}, u32[]{:S(2)}, u32[]{:S(2)}) collective-permute-start(bf16[48,4224]{1,0:T(8,128)(2,1)S(1)} %collective-permute-done.5.refs_5_), channel_id=1, source_target_pairs={{0,1},{1,0},{2,3},{3,2},{4,5},{5,4},{6,7},{7,6},{8,9},{9,8},{10,11... | collective-permute-start | bytes 1216520 | tf_op jit(solution)/shard_map/ppermute | solution.py:41
  47.2 6.6 %collective-permute-start.11 = (f32[4,128]{1,0:T(4,128)S(1)}, f32[4,128]{1,0:T(4,128)S(1)}, u32[]{:S(2)}, u32[]{:S(2)}) collective-permute-start(f32[4,128]{1,0:T(4,128)S(1)} %get-tuple-element.10), channel_id=1, source_target_pairs={{0,1},{1,0},{2,3},{3,2},{4,5},{5,4},{6,7},{7,6},{8,9},{9,8},{10,11... | collective-permute-start | bytes 6152 | tf_op jit(solution)/shard_map/ppermute | solution.py:41
  47.2 10.1 %collective-permute-start.9 = (f32[2,128]{1,0:T(2,128)S(1)}, f32[2,128]{1,0:T(2,128)S(1)}, u32[]{:S(2)}, u32[]{:S(2)}) collective-permute-start(f32[2,128]{1,0:T(2,128)S(1)} %get-tuple-element.8), channel_id=1, source_target_pairs={{2,0},{6,4},{0,6},{5,1},{3,5},{7,3},{10,8},{14,12},{8,14},{13,9},{... | collective-permute-start | bytes 3080 | tf_op jit(solution)/shard_map/ppermute | solution.py:213
  53.7 4.7 %collective-permute-start.12 = (f32[4,128]{1,0:T(4,128)S(1)}, f32[4,128]{1,0:T(4,128)S(1)}, u32[]{:S(2)}, u32[]{:S(2)}) collective-permute-start(f32[4,128]{1,0:T(4,128)S(1)} %max.23), channel_id=1, source_target_pairs={{0,24},{8,16},{16,8},{24,0},{1,25},{9,17},{17,9},{25,1},{2,26},{10... | collective-permute-start | bytes 6152 | tf_op jit(solution)/shard_map/ppermute | solution.py:217
  55.3 3.6 %collective-permute-start.13 = (f32[4,128]{1,0:T(4,128)S(1)}, f32[4,128]{1,0:T(4,128)S(1)}, u32[]{:S(2)}, u32[]{:S(2)}) collective-permute-start(f32[4,128]{1,0:T(4,128)S(1)} %max.23), channel_id=1, source_target_pairs={{0,8},{1,17},{8,0},{9,25},{16,24},{17,1},{24,16},{25,9},{2,10},{3,... | collective-permute-start | bytes 6152 | tf_op jit(solution)/shard_map/ppermute | solution.py:222
  56.8 3.6 %collective-permute-start.14 = (f32[4,128]{1,0:T(4,128)S(1)}, f32[4,128]{1,0:T(4,128)S(1)}, u32[]{:S(2)}, u32[]{:S(2)}) collective-permute-start(f32[4,128]{1,0:T(4,128)S(1)} %max.23), channel_id=1, source_target_pairs={{0,16},{1,9},{8,24},{9,1},{16,0},{17,25},{24,8},{25,17},{2,18},{3,... | collective-permute-start | bytes 6152 | tf_op jit(solution)/shard_map/ppermute | solution.py:222
  57.3 1.1 %collective-permute-start.10 = (f32[2,128]{1,0:T(2,128)S(1)}, f32[2,128]{1,0:T(2,128)S(1)}, u32[]{:S(2)}, u32[]{:S(2)}) collective-permute-start(f32[2,128]{1,0:T(2,128)S(1)} %collective-permute-done.9), channel_id=1, source_target_pairs={{0,1},{1,0},{2,3},{3,2},{4,5},{5,4},{6,7},{7,6},{8,9},{9,8},{10,11... | collective-permute-start | bytes 3080 | tf_op jit(solution)/shard_map/ppermute | solution.py:41

commit v18 on v17

--- a/solution.py
+++ b/solution.py
@@ -25,7 +25,7 @@
 
 def line_trips(length):
     if length == 4:
-        ways = [[(0, 1), (2, 3), (3, 0)], [(0, 2), (2, 1), (1, 3)]]
+        ways = [[(0, 1), (1, 3), (3, 2), (2, 0)], [(3, 0), (1, 2)]]
     else:
         ways = [[(k, (k + shift) % length) for k in range(length)] for shift in range(1, (length + 1) // 2)]
         if length % 2 == 0:

time: 61.1 us -> 57.9 us (0.948)
  starting transfers between devices: 19.3 us -> 15.7 us
    ppermute x1, starting transfers between devices: 6.5 us -> 2.47 us  [local(): back = lax.ppermute(part, line_axes, [(b, a) for a, b in trip])]
    ppermute x1, waiting for transfers between devices: 4.21 us -> 5.9 us  [local(): visitors = [lax.ppermute(both, line_axes, trip) for trip in trips]]
    ppermute x2, waiting for transfers between devices: 1.95 us -> 0.55 us  [local(): got = lax.ppermute(merged[chunk], plane_axes, group_trip(groups, *order))]
  transfers between devices with their start and end apart: 15 -> 15, of which waited for: 8 -> 8; matrix products, arithmetic and copies ran while one was open for 1% -> 1% of each run, Pallas kernels for 3% -> 4%
where the time goes in v18:
time: 57.9 us; the launch traced here: 57.4 us
  waiting for transfers between devices  34.6 us (60%)
  starting transfers between devices  15.7 us (27%)
  Pallas kernels  4.5 us (8%)
  local copies, waits for them, and re-layouts  1.7 us (3%)
  other arithmetic  0.69 us (1%)
    ppermute x1, waiting for transfers between devices, local(): lax.ppermute(both, plane_axes, group_trip(groups, *way))  15.4 us
    ppermute x2, waiting for transfers between devices, local(): corner = [lax.ppermute(part, plane_axes, relay) for part in corner]  10.2 us
    ppermute x1, waiting for transfers between devices, local(): visitors = [lax.ppermute(both, line_axes, trip) for trip in trips]  5.9 us
    pallas_call x2, Pallas kernels, call(): pl.pallas_call(kernel, in_specs=[VMEM] * len(operands), out_specs=[VMEM]...  3.86 us
    ppermute x1, starting transfers between devices, local(): visitors = [lax.ppermute(both, line_axes, trip) for trip in trips]  3.47 us
    ppermute x1, starting transfers between devices, local(): lax.ppermute(both, plane_axes, group_trip(groups, *way))  3 us
    ppermute x7, waiting for transfers between devices, swap(): return lax.ppermute(block, 'core', flip(2, 1))  2.57 us
    ppermute x1, starting transfers between devices, local(): back = lax.ppermute(part, line_axes, [(b, a) for a, b in trip])  2.47 us
  transfers between devices with their start and end apart: 15, of which 8 were waited for; matrix products, arithmetic and copies ran while one was open for 1% of the time, Pallas kernels for 4%

profile of v18, /device:TPU:0, one launch (start us, length us, event | category | flops | bytes accessed | tf_op | source)
XLA Modules:
  0.0 57.4 jit_solution(1500594820111499459)
XLA Ops:
  0.0 0.5 collective-permute-start
  0.5 0.7 %pad_add_fusion.ids_ref = s32[2,96]{1,0:T(2,128)S(1)} fusion(s32[1,96]{1,0:T(1,128)} %bitcast.4, s32[1,96]{1,0:T(1,128)} %bitcast.5), kind=kLoop, calls=%fused_computation | loop fusion | flops 192 | bytes 1536 | tf_op jit(solution)/shard_map/stack | solution.py:181
  1.2 1.1 %copy-done = bf16[96,4096]{1,0:T(8,128)(2,1)S(1)} copy-done((bf16[96,4096]{1,0:T(8,128)(2,1)S(1)}, bf16[96,4096]{1,0:T(8,128)(2,1)}, u32[]{:S(2)}) %copy-start) | copy-done | bytes 786456
  2.3 0.3 shard_map.37.own_ref.refs_0_
  2.6 0.3 shard_map.38.refs_1_
  3.0 3.0 %collective-permute-start.2 = (bf16[192,4224]{1,0:T(8,128)(2,1)S(1)}, bf16[192,4224]{1,0:T(8,128)(2,1)S(1)}, u32[]{:S(2)}, u32[]{:S(2)}) collective-permute-start(bf16[192,4224]{1,0:T(8,128)(2,1)S(1)} %shard_map.38.refs_1_), channel_id=1, source_target_pairs={{0,8},{1,17},{8,0},{9,25},{16,24},{17,1},{24,16},{25,9},{2,10},{3,... | collective-permute-start | bytes 4866056 | tf_op jit(solution)/shard_map/ppermute | solution.py:189
  6.0 3.5 %collective-permute-start.8 = (bf16[192,4224]{1,0:T(8,128)(2,1)S(1)}, bf16[192,4224]{1,0:T(8,128)(2,1)S(1)}, u32[]{:S(2)}, u32[]{:S(2)}) collective-permute-start(bf16[192,4224]{1,0:T(8,128)(2,1)S(1)} %shard_map.38.refs_1_), channel_id=1, source_target_pairs={{0,2},{2,6},{6,4},{4,0},{7,1},{3,5},{8,10},{10,14},{14,12},{12,8},... | collective-permute-start | bytes 4866056 | tf_op jit(solution)/shard_map/ppermute | solution.py:186
  9.5 15.4 %collective-permute-done.2.refs_2_ = bf16[192,4224]{1,0:T(8,128)(2,1)S(1)} collective-permute-done((bf16[192,4224]{1,0:T(8,128)(2,1)S(1)}, bf16[192,4224]{1,0:T(8,128)(2,1)S(1)}, u32[]{:S(2)}, u32[]{:S(2)}) %collective-permute-start.2) | collective-permute-done | bytes 1622048 | tf_op jit(solution)/shard_map/ppermute | solution.py:189
  25.0 2.1 %collective-permute-start.4 = (bf16[48,4224]{1,0:T(8,128)(2,1)S(1)}, bf16[48,4224]{1,0:T(8,128)(2,1)S(1)}, u32[]{:S(2)}, u32[]{:S(2)}) collective-permute-start(bf16[48,4224]{1,0:T(8,128)(2,1)S(1)} %get-tuple-element.12), channel_id=1, source_target_pairs={{0,16},{1,9},{8,24},{9,1},{16,0},{17,25},{24,8},{25,17},{2,18},{3,... | collective-permute-start | bytes 1216520 | tf_op jit(solution)/shard_map/ppermute | solution.py:194
  27.2 5.8 %collective-permute-done.4.refs_4_ = bf16[48,4224]{1,0:T(8,128)(2,1)S(1)} collective-permute-done((bf16[48,4224]{1,0:T(8,128)(2,1)S(1)}, bf16[48,4224]{1,0:T(8,128)(2,1)S(1)}, u32[]{:S(2)}, u32[]{:S(2)}) %collective-permute-start.4) | collective-permute-done | bytes 405536 | tf_op jit(solution)/shard_map/ppermute | solution.py:194
  33.0 4.3 %collective-permute-done.5.refs_5_ = bf16[48,4224]{1,0:T(8,128)(2,1)S(1)} collective-permute-done((bf16[48,4224]{1,0:T(8,128)(2,1)S(1)}, bf16[48,4224]{1,0:T(8,128)(2,1)S(1)}, u32[]{:S(2)}, u32[]{:S(2)}) %collective-permute-start.5) | collective-permute-done | bytes 405536 | tf_op jit(solution)/shard_map/ppermute | solution.py:194
  37.3 1.7 %collective-permute-done.7.refs_7_ = bf16[48,4224]{1,0:T(8,128)(2,1)S(1)} collective-permute-done((bf16[48,4224]{1,0:T(8,128)(2,1)S(1)}, bf16[48,4224]{1,0:T(8,128)(2,1)S(1)}, u32[]{:S(2)}, u32[]{:S(2)}) %collective-permute-start.7) | collective-permute-done | bytes 405536 | tf_op jit(solution)/shard_map/ppermute | solution.py:41
  39.1 1.8 %shard_map.39.refs_8_ = f32[1,128]{1,0:T(1,128)S(1)} custom-call(bf16[96,4224]{1,0:T(8,128)(2,1)S(1)} %shard_map.37.own_ref.refs_0_, bf16[192,4224]{1,0:T(8,128)(2,1)S(1)} %shard_map.38.refs_1_, bf16[192,4224]{1,0:T(8,128)(2,1)S(1)} %collective-permute-done.2.refs_2_, bf16[192,4224]{1,0:T(8,128)(2,1)S(1)} %collective-permute-done.3.refs_3_, ...), custom_call_target="tpu_custom_call" | custom-call | flops 805306368 | bytes 7340032 | tf_op jit(solution)/shard_map/pallas_call | solution.py:154
  40.9 5.9 %collective-permute-done.8.refs_0_ = bf16[192,4224]{1,0:T(8,128)(2,1)S(1)} collective-permute-done((bf16[192,4224]{1,0:T(8,128)(2,1)S(1)}, bf16[192,4224]{1,0:T(8,128)(2,1)S(1)}, u32[]{:S(2)}, u32[]{:S(2)}) %collective-permute-start.8) | collective-permute-done | bytes 1622048 | tf_op jit(solution)/shard_map/ppermute | solution.py:186
  46.8 2.1 %shard_map.40 = (f32[2,128]{1,0:T(2,128)S(1)}, f32[4,128]{1,0:T(4,128)S(1)}, f32[4,128]{1,0:T(4,128)S(1)}) custom-call(bf16[192,4224]{1,0:T(8,128)(2,1)S(1)} %collective-permute-done.8.refs_0_, bf16[192,4224]{1,0:T(8,128)(2,1)S(1)} %shard_map.38.refs_1_, bf16[192,4224]{1,0:T(8,128)(2,1)S(1)} %collective-permute-done.2.refs_2_, ...), custom_call_target="tpu_custom_call" | custom-call | flops 1610612736 | bytes 8388608 | tf_op jit(solution)/shard_map/pallas_call | solution.py:154
  48.9 2.5 %collective-permute-start.9 = (f32[2,128]{1,0:T(2,128)S(1)}, f32[2,128]{1,0:T(2,128)S(1)}, u32[]{:S(2)}, u32[]{:S(2)}) collective-permute-start(f32[2,128]{1,0:T(2,128)S(1)} %get-tuple-element.8), channel_id=1, source_target_pairs={{2,0},{6,2},{4,6},{0,4},{1,7},{5,3},{10,8},{14,10},{12,14},{8,12},... | collective-permute-start | bytes 3080 | tf_op jit(solution)/shard_map/ppermute | solution.py:213
  51.4 1.5 %collective-permute-start.12 = (f32[4,128]{1,0:T(4,128)S(1)}, f32[4,128]{1,0:T(4,128)S(1)}, u32[]{:S(2)}, u32[]{:S(2)}) collective-permute-start(f32[4,128]{1,0:T(4,128)S(1)} %max.23), channel_id=1, source_target_pairs={{0,24},{8,16},{16,8},{24,0},{1,25},{9,17},{17,9},{25,1},{2,26},{10... | collective-permute-start | bytes 6152 | tf_op jit(solution)/shard_map/ppermute | solution.py:217
  52.9 0.3 collective-permute-start.13
  53.2 1.7 %collective-permute-start.14 = (f32[4,128]{1,0:T(4,128)S(1)}, f32[4,128]{1,0:T(4,128)S(1)}, u32[]{:S(2)}, u32[]{:S(2)}) collective-permute-start(f32[4,128]{1,0:T(4,128)S(1)} %max.23), channel_id=1, source_target_pairs={{0,16},{1,9},{8,24},{9,1},{16,0},{17,25},{24,8},{25,17},{2,18},{3,... | collective-permute-start | bytes 6152 | tf_op jit(solution)/shard_map/ppermute | solution.py:222
  55.0 0.5 collective-permute-start.10
  55.5 0.8 %collective-permute-done.10 = f32[2,128]{1,0:T(2,128)S(1)} collective-permute-done((f32[2,128]{1,0:T(2,128)S(1)}, f32[2,128]{1,0:T(2,128)S(1)}, u32[]{:S(2)}, u32[]{:S(2)}) %collective-permute-start.10) | collective-permute-done | bytes 1056 | tf_op jit(solution)/shard_map/ppermute | solution.py:41
  56.3 0.2 collective-permute-done.13
  56.5 0.3 collective-permute-done.14
  56.8 0.5 slice_bitcast_fusion
  (17 shorter events, 0.3 us)
Async XLA Ops:
  0.0 2.6 %collective-permute-start = (bf16[96,4096]{1,0:T(8,128)(2,1)}, bf16[96,4096]{1,0:T(8,128)(2,1)S(1)}, u32[]{:S(2)}, u32[]{:S(2)}) collective-permute-start(bf16[96,4096]{1,0:T(8,128)(2,1)} %rows_ref.1), channel_id=1, source_target_pairs={{0,1},{1,0},{2,3},{3,2},{4,5},{5,4},{6,7},{7,6},{8,9},{9,8},{10,11... | collective-permute-start | bytes 2359304 | tf_op jit(solution)/shard_map/ppermute | solution.py:41
  1.1 1.5 %collective-permute-start.1 = (s32[2,96]{1,0:T(2,128)S(1)}, s32[2,96]{1,0:T(2,128)S(1)}, u32[]{:S(2)}, u32[]{:S(2)}) collective-permute-start(s32[2,96]{1,0:T(2,128)S(1)} %pad_add_fusion.ids_ref), channel_id=1, source_target_pairs={{0,1},{1,0},{2,3},{3,2},{4,5},{5,4},{6,7},{7,6},{8,9},{9,8},{10,11... | collective-permute-start | bytes 2312 | tf_op jit(solution)/shard_map/ppermute | solution.py:41
  1.2 1.1 %copy-start = (bf16[96,4096]{1,0:T(8,128)(2,1)S(1)}, bf16[96,4096]{1,0:T(8,128)(2,1)}, u32[]{:S(2)}) copy-start(bf16[96,4096]{1,0:T(8,128)(2,1)} %rows_ref.1) | copy-start | bytes 2359300
  3.0 21.9 %collective-permute-start.2 = (bf16[192,4224]{1,0:T(8,128)(2,1)S(1)}, bf16[192,4224]{1,0:T(8,128)(2,1)S(1)}, u32[]{:S(2)}, u32[]{:S(2)}) collective-permute-start(bf16[192,4224]{1,0:T(8,128)(2,1)S(1)} %shard_map.38.refs_1_), channel_id=1, source_target_pairs={{0,8},{1,17},{8,0},{9,25},{16,24},{17,1},{24,16},{25,9},{2,10},{3,... | collective-permute-start | bytes 4866056 | tf_op jit(solution)/shard_map/ppermute | solution.py:189
  6.0 40.8 %collective-permute-start.8 = (bf16[192,4224]{1,0:T(8,128)(2,1)S(1)}, bf16[192,4224]{1,0:T(8,128)(2,1)S(1)}, u32[]{:S(2)}, u32[]{:S(2)}) collective-permute-start(bf16[192,4224]{1,0:T(8,128)(2,1)S(1)} %shard_map.38.refs_1_), channel_id=1, source_target_pairs={{0,2},{2,6},{6,4},{4,0},{7,1},{3,5},{8,10},{10,14},{14,12},{12,8},... | collective-permute-start | bytes 4866056 | tf_op jit(solution)/shard_map/ppermute | solution.py:186
  24.9 14.2 %collective-permute-start.3 = (bf16[192,4224]{1,0:T(8,128)(2,1)S(1)}, bf16[192,4224]{1,0:T(8,128)(2,1)S(1)}, u32[]{:S(2)}, u32[]{:S(2)}) collective-permute-start(bf16[192,4224]{1,0:T(8,128)(2,1)S(1)} %collective-permute-done.2.refs_2_), channel_id=1, source_target_pairs={{0,1},{1,0},{2,3},{3,2},{4,5},{5,4},{6,7},{7,6},{8,9},{9,8},{10,11... | collective-permute-start | bytes 4866056 | tf_op jit(solution)/shard_map/ppermute | solution.py:41
  25.0 8.0 %collective-permute-start.4 = (bf16[48,4224]{1,0:T(8,128)(2,1)S(1)}, bf16[48,4224]{1,0:T(8,128)(2,1)S(1)}, u32[]{:S(2)}, u32[]{:S(2)}) collective-permute-start(bf16[48,4224]{1,0:T(8,128)(2,1)S(1)} %get-tuple-element.12), channel_id=1, source_target_pairs={{0,16},{1,9},{8,24},{9,1},{16,0},{17,25},{24,8},{25,17},{2,18},{3,... | collective-permute-start | bytes 1216520 | tf_op jit(solution)/shard_map/ppermute | solution.py:194
  27.1 10.2 %collective-permute-start.5 = (bf16[48,4224]{1,0:T(8,128)(2,1)S(1)}, bf16[48,4224]{1,0:T(8,128)(2,1)S(1)}, u32[]{:S(2)}, u32[]{:S(2)}) collective-permute-start(bf16[48,4224]{1,0:T(8,128)(2,1)S(1)} %get-tuple-element.11), channel_id=1, source_target_pairs={{0,16},{1,9},{8,24},{9,1},{16,0},{17,25},{24,8},{25,17},{2,18},{3,... | collective-permute-start | bytes 1216520 | tf_op jit(solution)/shard_map/ppermute | solution.py:194
  33.0 4.4 %collective-permute-start.6 = (bf16[48,4224]{1,0:T(8,128)(2,1)S(1)}, bf16[48,4224]{1,0:T(8,128)(2,1)S(1)}, u32[]{:S(2)}, u32[]{:S(2)}) collective-permute-start(bf16[48,4224]{1,0:T(8,128)(2,1)S(1)} %collective-permute-done.4.refs_4_), channel_id=1, source_target_pairs={{0,1},{1,0},{2,3},{3,2},{4,5},{5,4},{6,7},{7,6},{8,9},{9,8},{10,11... | collective-permute-start | bytes 1216520 | tf_op jit(solution)/shard_map/ppermute | solution.py:41
  37.3 1.7 %collective-permute-start.7 = (bf16[48,4224]{1,0:T(8,128)(2,1)S(1)}, bf16[48,4224]{1,0:T(8,128)(2,1)S(1)}, u32[]{:S(2)}, u32[]{:S(2)}) collective-permute-start(bf16[48,4224]{1,0:T(8,128)(2,1)S(1)} %collective-permute-done.5.refs_5_), channel_id=1, source_target_pairs={{0,1},{1,0},{2,3},{3,2},{4,5},{5,4},{6,7},{7,6},{8,9},{9,8},{10,11... | collective-permute-start | bytes 1216520 | tf_op jit(solution)/shard_map/ppermute | solution.py:41
  48.9 2.5 %collective-permute-start.11 = (f32[4,128]{1,0:T(4,128)S(1)}, f32[4,128]{1,0:T(4,128)S(1)}, u32[]{:S(2)}, u32[]{:S(2)}) collective-permute-start(f32[4,128]{1,0:T(4,128)S(1)} %get-tuple-element.10), channel_id=1, source_target_pairs={{0,1},{1,0},{2,3},{3,2},{4,5},{5,4},{6,7},{7,6},{8,9},{9,8},{10,11... | collective-permute-start | bytes 6152 | tf_op jit(solution)/shard_map/ppermute | solution.py:41
  48.9 6.1 %collective-permute-start.9 = (f32[2,128]{1,0:T(2,128)S(1)}, f32[2,128]{1,0:T(2,128)S(1)}, u32[]{:S(2)}, u32[]{:S(2)}) collective-permute-start(f32[2,128]{1,0:T(2,128)S(1)} %get-tuple-element.8), channel_id=1, source_target_pairs={{2,0},{6,2},{4,6},{0,4},{1,7},{5,3},{10,8},{14,10},{12,14},{8,12},... | collective-permute-start | bytes 3080 | tf_op jit(solution)/shard_map/ppermute | solution.py:213
  51.4 4.9 %collective-permute-start.12 = (f32[4,128]{1,0:T(4,128)S(1)}, f32[4,128]{1,0:T(4,128)S(1)}, u32[]{:S(2)}, u32[]{:S(2)}) collective-permute-start(f32[4,128]{1,0:T(4,128)S(1)} %max.23), channel_id=1, source_target_pairs={{0,24},{8,16},{16,8},{24,0},{1,25},{9,17},{17,9},{25,1},{2,26},{10... | collective-permute-start | bytes 6152 | tf_op jit(solution)/shard_map/ppermute | solution.py:217
  52.9 3.6 %collective-permute-start.13 = (f32[4,128]{1,0:T(4,128)S(1)}, f32[4,128]{1,0:T(4,128)S(1)}, u32[]{:S(2)}, u32[]{:S(2)}) collective-permute-start(f32[4,128]{1,0:T(4,128)S(1)} %max.23), channel_id=1, source_target_pairs={{0,8},{1,17},{8,0},{9,25},{16,24},{17,1},{24,16},{25,9},{2,10},{3,... | collective-permute-start | bytes 6152 | tf_op jit(solution)/shard_map/ppermute | solution.py:222
  53.2 3.6 %collective-permute-start.14 = (f32[4,128]{1,0:T(4,128)S(1)}, f32[4,128]{1,0:T(4,128)S(1)}, u32[]{:S(2)}, u32[]{:S(2)}) collective-permute-start(f32[4,128]{1,0:T(4,128)S(1)} %max.23), channel_id=1, source_target_pairs={{0,16},{1,9},{8,24},{9,1},{16,0},{17,25},{24,8},{25,17},{2,18},{3,... | collective-permute-start | bytes 6152 | tf_op jit(solution)/shard_map/ppermute | solution.py:222
  55.0 1.3 %collective-permute-start.10 = (f32[2,128]{1,0:T(2,128)S(1)}, f32[2,128]{1,0:T(2,128)S(1)}, u32[]{:S(2)}, u32[]{:S(2)}) collective-permute-start(f32[2,128]{1,0:T(2,128)S(1)} %collective-permute-done.9), channel_id=1, source_target_pairs={{0,1},{1,0},{2,3},{3,2},{4,5},{5,4},{6,7},{7,6},{8,9},{9,8},{10,11... | collective-permute-start | bytes 3080 | tf_op jit(solution)/shard_map/ppermute | solution.py:41

commit v19 on v16

--- a/solution.py
+++ b/solution.py
@@ -10,6 +10,7 @@
 AXES = ("group", "z", "core")
 LANES = 128
 CHUNK = 512
+TAIL = 16
 VMEM = pl.BlockSpec(memory_space=pltpu.VMEM)
 
 
@@ -53,19 +54,31 @@
     pack_into(block_ref, 0, rows_ref[...], ids_ref[...])
 
 
-def pair_kernel(own_ref, rows_ref, ids_ref, both_ref):
-    count = own_ref.shape[0]
+def pair_kernel(own_ref, own_ids_ref, rows_ref, ids_ref, both_ref, line_ref):
+    count, width = rows_ref.shape
     both_ref[:count, :] = own_ref[...]
     pack_into(both_ref, count, rows_ref[...], ids_ref[...])
-
-
-def pack(kernel, operands, count):
+    for k in range(width // LANES):
+        columns = both_ref[:, k * LANES : (k + 1) * LANES]
+        line_ref[2 * count * k : 2 * count * (k + 1), :] = columns
+    lines = []
+    for ref in (own_ids_ref, ids_ref):
+        ids = ref[...].astype(jnp.float32)
+        high = jnp.floor(ids[1:2] / 256.0)
+        lines += [ids[0:1] + 1.0, high, ids[1:2] - 256.0 * high]
+    tail = jnp.concatenate(lines + [jnp.zeros((TAIL - 6, count), jnp.float32)], axis=0)
+    if count < LANES:
+        tail = jnp.concatenate([tail, jnp.zeros((TAIL, LANES - count), jnp.float32)], axis=1)
+    line_ref[2 * count * (width // LANES) :, :] = tail.astype(jnp.bfloat16)
+
+
+def pack(kernel, operands, shapes):
     rows, width = operands[-2].shape
     return pl.pallas_call(
         kernel,
         in_specs=[VMEM] * len(operands),
-        out_specs=VMEM,
-        out_shape=jax.ShapeDtypeStruct((count * rows, width + LANES), jnp.bfloat16),
+        out_specs=[VMEM] * len(shapes),
+        out_shape=[jax.ShapeDtypeStruct(shape, jnp.bfloat16) for shape in shapes],
         compiler_params=pltpu.CompilerParams(vmem_limit_bytes=8 * 2**20),
         cost_estimate=pl.CostEstimate(
             flops=4 * rows * width, bytes_accessed=4 * rows * width, transcendentals=rows
@@ -73,17 +86,48 @@
     )(*operands)
 
 
+def padded(rows):
+    spare = -rows.shape[0] % LANES
+    if not spare:
+        return rows
+    return jnp.concatenate([rows, jnp.zeros((spare, rows.shape[1]), rows.dtype)], axis=0)
+
+
 def own_kernel(*refs):
-    row_ref, *scratch = refs[-3:]
-    best, _ = best_of(refs[:1], refs[1:-3], refs[0].shape[0], False, *scratch)
-    row_ref[...] = best[0]
+    own_ref, row_ref, dots = refs[0], *refs[-2:]
+    rows, width = own_ref.shape[0], own_ref.shape[1] - LANES
+    turned = padded(own_ref[:, width:].astype(jnp.float32)).T
+    meta = [(turned[0:1], turned[1:2] * 256.0 + turned[2:3])]
+
+    def visitors_at(k):
+        return padded(own_ref[:, k : k + CHUNK])
+
+    bests, _ = best_of(visitors_at, meta, refs[1:-2], rows, False, dots)
+    row_ref[...] = bests[0]
 
 
 def visit_kernel(visitors, arrays, mine, others, *refs):
-    block_refs = refs[visitors : visitors + arrays]
-    row_ref, mine_ref, other_ref, *scratch = refs[visitors + arrays + 1 :]
-    rows = refs[0].shape[0] // 2
-    bests, cols = best_of(refs[:visitors], block_refs, rows, True, *scratch)
+    line_refs, block_refs = refs[:visitors], refs[visitors : visitors + arrays]
+    row_ref, mine_ref, other_ref, dots = refs[visitors + arrays + 1 :]
+    width = block_refs[0].shape[1] - LANES
+    rows = (line_refs[0].shape[0] - TAIL) // (2 * width // LANES)
+    meta = []
+    for ref in line_refs:
+        tail = ref[2 * rows * (width // LANES) :, :].astype(jnp.float32)
+        for row in (0, 3):
+            order = tail[row + 1 : row + 2] * 256.0 + tail[row + 2 : row + 3]
+            meta.append((tail[row : row + 1], order))
+
+    def visitors_at(k):
+        parts = []
+        for ref in line_refs:
+            for core in range(2):
+                starts = [rows * (2 * block + core) for block in range(k // LANES, (k + CHUNK) // LANES)]
+                columns = [ref[start : start + rows, :] for start in starts]
+                parts.append(padded(jnp.concatenate(columns, axis=1)))
+        return jnp.concatenate(parts, axis=0)
+
+    bests, cols = best_of(visitors_at, meta, block_refs, rows, True, dots)
     for v, best in enumerate(bests):
         row_ref[v : v + 1, :] = best
     for ref, picked in ((mine_ref, mine), (other_ref, others)):
@@ -91,26 +135,13 @@
             ref[row : row + 1, :] = cols[j]
 
 
-def best_of(visitor_refs, block_refs, rows, homed, units, dots):
-    width = units.shape[1]
-
-    meta = []
-    for ref in visitor_refs:
-        for source in range(0, ref.shape[0], rows):
-            place, source = len(meta) * LANES, pl.ds(source, rows)
-            units[place : place + rows, :] = ref[source, :width]
-            tail = ref[source, width:].astype(jnp.float32)
-            if rows < LANES:
-                spare = LANES - rows
-                units[place + rows : place + LANES, :] = jnp.zeros((spare, width), jnp.bfloat16)
-                tail = jnp.concatenate([tail, jnp.zeros((spare, LANES), jnp.float32)], axis=0)
-            turned = tail.T
-            meta.append((turned[0:1], turned[1:2] * 256.0 + turned[2:3]))
+def best_of(visitors_at, meta, block_refs, rows, homed, dots):
+    width = block_refs[0].shape[1] - LANES
     for k in range(0, width, CHUNK):
         left = jnp.concatenate([ref[:, k : k + CHUNK] for ref in block_refs], axis=0)
         part = lax.dot_general(
             left,
-            units[:, k : k + CHUNK],
+            visitors_at(k),
             (((1,), (1,)), ((), ())),
             preferred_element_type=jnp.float32,
         )
@@ -142,17 +173,13 @@
     return row_best, [turned[j : j + 1] for j in range(dots.shape[0] // rows)]
 
 
-def call(kernel, operands, count, out_rows, total):
-    width = operands[0].shape[1] - LANES
+def call(kernel, operands, count, out_rows, total, width):
     return pl.pallas_call(
         kernel,
         in_specs=[VMEM] * len(operands),
         out_specs=[VMEM] * len(out_rows),
         out_shape=[jax.ShapeDtypeStruct((n, LANES), jnp.float32) for n in out_rows],
-        scratch_shapes=[
-            pltpu.VMEM((count * LANES, width), jnp.bfloat16),
-            pltpu.VMEM((total, count * LANES), jnp.float32),
-        ],
+        scratch_shapes=[pltpu.VMEM((total, count * LANES), jnp.float32)],
         compiler_params=pltpu.CompilerParams(vmem_limit_bytes=24 * 2**20),
         cost_estimate=pl.CostEstimate(
             flops=2 * total * count * LANES * width,
@@ -167,20 +194,21 @@
 
 
 def local(embeddings, cluster_ids, order_index):
-    rows = embeddings.shape[0]
+    rows, width = embeddings.shape
     groups, length = lax.axis_size("group"), lax.axis_size("z")
     z, core = lax.axis_index("z"), lax.axis_index("core")
     plane_axes, line_axes = ("group", "core"), ("z", "core")
     ids = jnp.stack([cluster_ids, order_index])
-    own = pack(pack_kernel, [embeddings, ids], 1)
-    both = pack(pair_kernel, [own, swap(embeddings), swap(ids)], 2)
+    (own,) = pack(pack_kernel, [embeddings, ids], [(rows, width + LANES)])
+    shapes = [(2 * rows, width + LANES), (2 * rows * width // LANES + TAIL, LANES)]
+    both, line = pack(pair_kernel, [own, ids, swap(embeddings), swap(ids)], shapes)
 
     routes = [ring_pairs(length, shift) for shift in range(1, length // 2 + 1)]
     trips = []
     for first in range(0, len(routes), 2):
         ways = enumerate(routes[first : first + 2])
         trips.append([(2 * a + way, 2 * b + way) for way, route in ways for a, b in route])
-    visitors = [lax.ppermute(both, line_axes, trip) for trip in trips]
+    visitors = [lax.ppermute(line, line_axes, trip) for trip in trips]
 
     partners = [(s, s + 1) for s in range(1, groups - 1, 2)]
     arrived = [lax.ppermute(both, plane_axes, group_trip(groups, *way)) for way in partners]
@@ -196,12 +224,12 @@
     orders = [((2, 5, 6, 0), (4, 3, 7, 1))] + [((0, 3, 4, 7), (2, 1, 6, 5))] * (len(chunks) - 1)
     bests, answers = [], []
     for chunk in chunks:
-        bests += call(own_kernel, [own, *chunk], 1, [1], 8 * rows)
+        bests += call(own_kernel, [own, *chunk], 1, [1], 8 * rows, width)
     for index, (chunk, order) in enumerate(zip(chunks, orders)):
         kernel = functools.partial(visit_kernel, len(visitors), len(chunk), *order)
         count = 2 * len(visitors)
         operands = [*visitors, *chunk, bests[index]]
-        answers.append(call(kernel, operands, count, [count, 4, 4], 8 * rows))
+        answers.append(call(kernel, operands, count, [count, 4, 4], 8 * rows, width))
     home = functools.reduce(jnp.maximum, [answer[0] for answer in answers])
     merged = [jnp.maximum(mine, swap(others)) for _, mine, others in answers]
 
@@ -211,7 +239,6 @@
         for here, best in ((2 * z + core, back[0:1]), (2 * z + (core ^ 1), swap(back)[1:2])):
             sent = functools.reduce(jnp.logical_or, [here == a for a, _ in trip])
             bests.append(jnp.where(sent, best, -1.0))
-    bests.append(lax.ppermute(merged[0], "group", flip(groups, last))[2:3])
     ways = [(0, 0, partners[-1])]
     ways += [(1 + k // 2, 2 * (k % 2), way) for k, way in enumerate(partners[:-1])]
     for chunk, row, (first, second) in ways:
@@ -219,6 +246,7 @@
             got = lax.ppermute(merged[chunk], plane_axes, group_trip(groups, *order))
             bests.append(got[row : row + 1])
             row += 1
+    bests.append(lax.ppermute(merged[0], "group", flip(groups, last))[2:3])
     bests.append(merged[0][3:4])
     return functools.reduce(jnp.maximum, bests)[0, :rows]
 

time: 57.3 us -> 57.5 us (level)
    ppermute x1, waiting for transfers between devices: 6.02 us -> 5.06 us  [local(): visitors = [lax.ppermute(line, line_axes, trip) for trip in trips]]
    ppermute x2, waiting for transfers between devices: 0.92 us -> 1.76 us  [local(): got = lax.ppermute(merged[chunk], plane_axes, group_trip(groups, *order))]
where the time goes in v19:
time: 57.5 us; the launch traced here: 57.3 us
  waiting for transfers between devices  35.1 us (61%)
  starting transfers between devices  14.9 us (26%)
  Pallas kernels  4.83 us (8%)
  local copies, waits for them, and re-layouts  1.7 us (3%)
  other arithmetic  0.69 us (1%)
    ppermute x1, waiting for transfers between devices, local(): lax.ppermute(both, plane_axes, group_trip(groups, *way))  15.4 us
    ppermute x2, waiting for transfers between devices, local(): corner = [lax.ppermute(part, plane_axes, relay) for part in corner]  10.2 us
    ppermute x1, waiting for transfers between devices, local(): visitors = [lax.ppermute(line, line_axes, trip) for trip in trips]  5.06 us
    pallas_call x2, Pallas kernels, call(): pl.pallas_call(kernel, in_specs=[VMEM] * len(operands), out_specs=[VMEM]...  3.86 us
    ppermute x1, starting transfers between devices, local(): visitors = [lax.ppermute(line, line_axes, trip) for trip in trips]  3.47 us
    ppermute x1, starting transfers between devices, local(): lax.ppermute(both, plane_axes, group_trip(groups, *way))  3 us
    ppermute x7, waiting for transfers between devices, swap(): return lax.ppermute(block, 'core', flip(2, 1))  2.7 us
    ppermute x2, starting transfers between devices, local(): corner = [lax.ppermute(part, plane_axes, relay) for part in corner]  2.19 us
  transfers between devices with their start and end apart: 15, of which 8 were waited for; matrix products, arithmetic and copies ran while one was open for 1% of the time, Pallas kernels for 4%

profile of v19, /device:TPU:0, one launch (start us, length us, event | category | flops | bytes accessed | tf_op | source)
XLA Modules:
  0.0 57.3 jit_solution(4603992893183806188)
XLA Ops:
  0.0 0.5 collective-permute-start
  0.5 0.7 %pad_add_fusion.ids_ref.own_ids_ref = s32[2,96]{1,0:T(2,128)S(1)} fusion(s32[1,96]{1,0:T(1,128)} %bitcast.4, s32[1,96]{1,0:T(1,128)} %bitcast.5), kind=kLoop, calls=%fused_computation | loop fusion | flops 192 | bytes 1536 | tf_op jit(solution)/shard_map/stack | solution.py:201
  1.2 1.1 %copy-done = bf16[96,4096]{1,0:T(8,128)(2,1)S(1)} copy-done((bf16[96,4096]{1,0:T(8,128)(2,1)S(1)}, bf16[96,4096]{1,0:T(8,128)(2,1)}, u32[]{:S(2)}) %copy-start) | copy-done | bytes 786456
  2.3 0.3 shard_map.37.own_ref.refs_0_
  2.6 0.7 %shard_map.38 = (bf16[192,4224]{1,0:T(8,128)(2,1)S(1)}, bf16[6160,128]{1,0:T(8,128)(2,1)S(1)}) custom-call(bf16[96,4224]{1,0:T(8,128)(2,1)S(1)} %shard_map.37.own_ref.refs_0_, s32[2,96]{1,0:T(2,128)S(1)} %pad_add_fusion.ids_ref.own_ids_ref, bf16[96,4096]{1,0:T(8,128)(2,1)S(1)} %collective-permute-done.rows_ref, s32[2,96]{1,0:T(2,128)S(1)} %collective-permute-done.1.ids_ref), custom_call_target="tpu_custom_call" | custom-call | flops 1572864 | bytes 1572864 | tf_op jit(solution)/shard_map/pallas_call | solution.py:77
  3.3 3.0 %collective-permute-start.2 = (bf16[192,4224]{1,0:T(8,128)(2,1)S(1)}, bf16[192,4224]{1,0:T(8,128)(2,1)S(1)}, u32[]{:S(2)}, u32[]{:S(2)}) collective-permute-start(bf16[192,4224]{1,0:T(8,128)(2,1)S(1)} %get-tuple-element.10.refs_1_), channel_id=1, source_target_pairs={{0,8},{1,17},{8,0},{9,25},{16,24},{17,1},{24,16},{25,9},{2,10},{3,... | collective-permute-start | bytes 4866056 | tf_op jit(solution)/shard_map/ppermute | solution.py:214
  6.3 3.5 %collective-permute-start.8 = (bf16[6160,128]{1,0:T(8,128)(2,1)S(1)}, bf16[6160,128]{1,0:T(8,128)(2,1)S(1)}, u32[]{:S(2)}, u32[]{:S(2)}) collective-permute-start(bf16[6160,128]{1,0:T(8,128)(2,1)S(1)} %get-tuple-element.11), channel_id=1, source_target_pairs={{0,2},{2,4},{4,6},{6,0},{1,5},{7,3},{8,10},{10,12},{12,14},{14,8},... | collective-permute-start | bytes 4730888 | tf_op jit(solution)/shard_map/ppermute | solution.py:211
  9.8 15.4 %collective-permute-done.2.refs_2_ = bf16[192,4224]{1,0:T(8,128)(2,1)S(1)} collective-permute-done((bf16[192,4224]{1,0:T(8,128)(2,1)S(1)}, bf16[192,4224]{1,0:T(8,128)(2,1)S(1)}, u32[]{:S(2)}, u32[]{:S(2)}) %collective-permute-start.2) | collective-permute-done | bytes 1622048 | tf_op jit(solution)/shard_map/ppermute | solution.py:214
  25.3 2.1 %collective-permute-start.4 = (bf16[48,4224]{1,0:T(8,128)(2,1)S(1)}, bf16[48,4224]{1,0:T(8,128)(2,1)S(1)}, u32[]{:S(2)}, u32[]{:S(2)}) collective-permute-start(bf16[48,4224]{1,0:T(8,128)(2,1)S(1)} %get-tuple-element.16), channel_id=1, source_target_pairs={{0,16},{1,9},{8,24},{9,1},{16,0},{17,25},{24,8},{25,17},{2,18},{3,... | collective-permute-start | bytes 1216520 | tf_op jit(solution)/shard_map/ppermute | solution.py:219
  27.5 5.8 %collective-permute-done.4.refs_4_ = bf16[48,4224]{1,0:T(8,128)(2,1)S(1)} collective-permute-done((bf16[48,4224]{1,0:T(8,128)(2,1)S(1)}, bf16[48,4224]{1,0:T(8,128)(2,1)S(1)}, u32[]{:S(2)}, u32[]{:S(2)}) %collective-permute-start.4) | collective-permute-done | bytes 405536 | tf_op jit(solution)/shard_map/ppermute | solution.py:219
  33.3 4.3 %collective-permute-done.5.refs_5_ = bf16[48,4224]{1,0:T(8,128)(2,1)S(1)} collective-permute-done((bf16[48,4224]{1,0:T(8,128)(2,1)S(1)}, bf16[48,4224]{1,0:T(8,128)(2,1)S(1)}, u32[]{:S(2)}, u32[]{:S(2)}) %collective-permute-start.5) | collective-permute-done | bytes 405536 | tf_op jit(solution)/shard_map/ppermute | solution.py:219
  37.7 1.7 %collective-permute-done.7.refs_7_ = bf16[48,4224]{1,0:T(8,128)(2,1)S(1)} collective-permute-done((bf16[48,4224]{1,0:T(8,128)(2,1)S(1)}, bf16[48,4224]{1,0:T(8,128)(2,1)S(1)}, u32[]{:S(2)}, u32[]{:S(2)}) %collective-permute-start.7) | collective-permute-done | bytes 405536 | tf_op jit(solution)/shard_map/ppermute | solution.py:35
  39.4 1.8 %shard_map.39.refs_8_ = f32[1,128]{1,0:T(1,128)S(1)} custom-call(bf16[96,4224]{1,0:T(8,128)(2,1)S(1)} %shard_map.37.own_ref.refs_0_, bf16[192,4224]{1,0:T(8,128)(2,1)S(1)} %get-tuple-element.10.refs_1_, bf16[192,4224]{1,0:T(8,128)(2,1)S(1)} %collective-permute-done.2.refs_2_, bf16[192,4224]{1,0:T(8,128)(2,1)S(1)} %collective-permute-done.3.refs_3_, ...), custom_call_target="tpu_custom_call" | custom-call | flops 805306368 | bytes 7340032 | tf_op jit(solution)/shard_map/pallas_call | solution.py:177
  41.2 5.1 %collective-permute-done.8.refs_0_ = bf16[6160,128]{1,0:T(8,128)(2,1)S(1)} collective-permute-done((bf16[6160,128]{1,0:T(8,128)(2,1)S(1)}, bf16[6160,128]{1,0:T(8,128)(2,1)S(1)}, u32[]{:S(2)}, u32[]{:S(2)}) %collective-permute-start.8) | collective-permute-done | bytes 1576992 | tf_op jit(solution)/shard_map/ppermute | solution.py:211
  46.3 2.1 %shard_map.40 = (f32[2,128]{1,0:T(2,128)S(1)}, f32[4,128]{1,0:T(4,128)S(1)}, f32[4,128]{1,0:T(4,128)S(1)}) custom-call(bf16[6160,128]{1,0:T(8,128)(2,1)S(1)} %collective-permute-done.8.refs_0_, bf16[192,4224]{1,0:T(8,128)(2,1)S(1)} %get-tuple-element.10.refs_1_, bf16[192,4224]{1,0:T(8,128)(2,1)S(1)} %collective-permute-done.2.refs_2_, ...), custom_call_target="tpu_custom_call" | custom-call | flops 1610612736 | bytes 8388608 | tf_op jit(solution)/shard_map/pallas_call | solution.py:177
  48.4 1.9 %collective-permute-start.9 = (f32[2,128]{1,0:T(2,128)S(1)}, f32[2,128]{1,0:T(2,128)S(1)}, u32[]{:S(2)}, u32[]{:S(2)}) collective-permute-start(f32[2,128]{1,0:T(2,128)S(1)} %get-tuple-element.12), channel_id=1, source_target_pairs={{2,0},{4,2},{6,4},{0,6},{5,1},{3,7},{10,8},{12,10},{14,12},{8,14},... | collective-permute-start | bytes 3080 | tf_op jit(solution)/shard_map/ppermute | solution.py:238
  50.3 1.7 %collective-permute-start.14 = (f32[4,128]{1,0:T(4,128)S(1)}, f32[4,128]{1,0:T(4,128)S(1)}, u32[]{:S(2)}, u32[]{:S(2)}) collective-permute-start(f32[4,128]{1,0:T(4,128)S(1)} %max.23), channel_id=1, source_target_pairs={{0,24},{8,16},{16,8},{24,0},{1,25},{9,17},{17,9},{25,1},{2,26},{10... | collective-permute-start | bytes 6152 | tf_op jit(solution)/shard_map/ppermute | solution.py:249
  52.0 1.2 %collective-permute-start.13 = (f32[4,128]{1,0:T(4,128)S(1)}, f32[4,128]{1,0:T(4,128)S(1)}, u32[]{:S(2)}, u32[]{:S(2)}) collective-permute-start(f32[4,128]{1,0:T(4,128)S(1)} %max.23), channel_id=1, source_target_pairs={{0,16},{1,9},{8,24},{9,1},{16,0},{17,25},{24,8},{25,17},{2,18},{3,... | collective-permute-start | bytes 6152 | tf_op jit(solution)/shard_map/ppermute | solution.py:246
  53.2 0.7 %collective-permute-start.12 = (f32[4,128]{1,0:T(4,128)S(1)}, f32[4,128]{1,0:T(4,128)S(1)}, u32[]{:S(2)}, u32[]{:S(2)}) collective-permute-start(f32[4,128]{1,0:T(4,128)S(1)} %max.23), channel_id=1, source_target_pairs={{0,8},{1,17},{8,0},{9,25},{16,24},{17,1},{24,16},{25,9},{2,10},{3,... | collective-permute-start | bytes 6152 | tf_op jit(solution)/shard_map/ppermute | solution.py:246
  53.9 0.2 collective-permute-start.10
  54.1 1.0 %collective-permute-done.10 = f32[2,128]{1,0:T(2,128)S(1)} collective-permute-done((f32[2,128]{1,0:T(2,128)S(1)}, f32[2,128]{1,0:T(2,128)S(1)}, u32[]{:S(2)}, u32[]{:S(2)}) %collective-permute-start.10) | collective-permute-done | bytes 1056 | tf_op jit(solution)/shard_map/ppermute | solution.py:35
  55.0 0.5 collective-permute-done.13
  55.6 1.2 %collective-permute-done.12 = f32[4,128]{1,0:T(4,128)S(1)} collective-permute-done((f32[4,128]{1,0:T(4,128)S(1)}, f32[4,128]{1,0:T(4,128)S(1)}, u32[]{:S(2)}, u32[]{:S(2)}) %collective-permute-start.12) | collective-permute-done | bytes 2080 | tf_op jit(solution)/shard_map/ppermute | solution.py:246
  56.8 0.5 slice_bitcast_fusion
  (17 shorter events, 0.3 us)
Async XLA Ops:
  0.0 2.6 %collective-permute-start = (bf16[96,4096]{1,0:T(8,128)(2,1)}, bf16[96,4096]{1,0:T(8,128)(2,1)S(1)}, u32[]{:S(2)}, u32[]{:S(2)}) collective-permute-start(bf16[96,4096]{1,0:T(8,128)(2,1)} %rows_ref.1), channel_id=1, source_target_pairs={{0,1},{1,0},{2,3},{3,2},{4,5},{5,4},{6,7},{7,6},{8,9},{9,8},{10,11... | collective-permute-start | bytes 2359304 | tf_op jit(solution)/shard_map/ppermute | solution.py:35
  1.1 1.5 %collective-permute-start.1 = (s32[2,96]{1,0:T(2,128)S(1)}, s32[2,96]{1,0:T(2,128)S(1)}, u32[]{:S(2)}, u32[]{:S(2)}) collective-permute-start(s32[2,96]{1,0:T(2,128)S(1)} %pad_add_fusion.ids_ref.own_ids_ref), channel_id=1, source_target_pairs={{0,1},{1,0},{2,3},{3,2},{4,5},{5,4},{6,7},{7,6},{8,9},{9,8},{10,11... | collective-permute-start | bytes 2312 | tf_op jit(solution)/shard_map/ppermute | solution.py:35
  1.2 1.1 %copy-start = (bf16[96,4096]{1,0:T(8,128)(2,1)S(1)}, bf16[96,4096]{1,0:T(8,128)(2,1)}, u32[]{:S(2)}) copy-start(bf16[96,4096]{1,0:T(8,128)(2,1)} %rows_ref.1) | copy-start | bytes 2359300
  3.3 21.9 %collective-permute-start.2 = (bf16[192,4224]{1,0:T(8,128)(2,1)S(1)}, bf16[192,4224]{1,0:T(8,128)(2,1)S(1)}, u32[]{:S(2)}, u32[]{:S(2)}) collective-permute-start(bf16[192,4224]{1,0:T(8,128)(2,1)S(1)} %get-tuple-element.10.refs_1_), channel_id=1, source_target_pairs={{0,8},{1,17},{8,0},{9,25},{16,24},{17,1},{24,16},{25,9},{2,10},{3,... | collective-permute-start | bytes 4866056 | tf_op jit(solution)/shard_map/ppermute | solution.py:214
  6.3 39.9 %collective-permute-start.8 = (bf16[6160,128]{1,0:T(8,128)(2,1)S(1)}, bf16[6160,128]{1,0:T(8,128)(2,1)S(1)}, u32[]{:S(2)}, u32[]{:S(2)}) collective-permute-start(bf16[6160,128]{1,0:T(8,128)(2,1)S(1)} %get-tuple-element.11), channel_id=1, source_target_pairs={{0,2},{2,4},{4,6},{6,0},{1,5},{7,3},{8,10},{10,12},{12,14},{14,8},... | collective-permute-start | bytes 4730888 | tf_op jit(solution)/shard_map/ppermute | solution.py:211
  25.3 14.2 %collective-permute-start.3 = (bf16[192,4224]{1,0:T(8,128)(2,1)S(1)}, bf16[192,4224]{1,0:T(8,128)(2,1)S(1)}, u32[]{:S(2)}, u32[]{:S(2)}) collective-permute-start(bf16[192,4224]{1,0:T(8,128)(2,1)S(1)} %collective-permute-done.2.refs_2_), channel_id=1, source_target_pairs={{0,1},{1,0},{2,3},{3,2},{4,5},{5,4},{6,7},{7,6},{8,9},{9,8},{10,11... | collective-permute-start | bytes 4866056 | tf_op jit(solution)/shard_map/ppermute | solution.py:35
  25.3 8.0 %collective-permute-start.4 = (bf16[48,4224]{1,0:T(8,128)(2,1)S(1)}, bf16[48,4224]{1,0:T(8,128)(2,1)S(1)}, u32[]{:S(2)}, u32[]{:S(2)}) collective-permute-start(bf16[48,4224]{1,0:T(8,128)(2,1)S(1)} %get-tuple-element.16), channel_id=1, source_target_pairs={{0,16},{1,9},{8,24},{9,1},{16,0},{17,25},{24,8},{25,17},{2,18},{3,... | collective-permute-start | bytes 1216520 | tf_op jit(solution)/shard_map/ppermute | solution.py:219
  27.4 10.2 %collective-permute-start.5 = (bf16[48,4224]{1,0:T(8,128)(2,1)S(1)}, bf16[48,4224]{1,0:T(8,128)(2,1)S(1)}, u32[]{:S(2)}, u32[]{:S(2)}) collective-permute-start(bf16[48,4224]{1,0:T(8,128)(2,1)S(1)} %get-tuple-element.15), channel_id=1, source_target_pairs={{0,16},{1,9},{8,24},{9,1},{16,0},{17,25},{24,8},{25,17},{2,18},{3,... | collective-permute-start | bytes 1216520 | tf_op jit(solution)/shard_map/ppermute | solution.py:219
  33.3 4.4 %collective-permute-start.6 = (bf16[48,4224]{1,0:T(8,128)(2,1)S(1)}, bf16[48,4224]{1,0:T(8,128)(2,1)S(1)}, u32[]{:S(2)}, u32[]{:S(2)}) collective-permute-start(bf16[48,4224]{1,0:T(8,128)(2,1)S(1)} %collective-permute-done.4.refs_4_), channel_id=1, source_target_pairs={{0,1},{1,0},{2,3},{3,2},{4,5},{5,4},{6,7},{7,6},{8,9},{9,8},{10,11... | collective-permute-start | bytes 1216520 | tf_op jit(solution)/shard_map/ppermute | solution.py:35
  37.7 1.7 %collective-permute-start.7 = (bf16[48,4224]{1,0:T(8,128)(2,1)S(1)}, bf16[48,4224]{1,0:T(8,128)(2,1)S(1)}, u32[]{:S(2)}, u32[]{:S(2)}) collective-permute-start(bf16[48,4224]{1,0:T(8,128)(2,1)S(1)} %collective-permute-done.5.refs_5_), channel_id=1, source_target_pairs={{0,1},{1,0},{2,3},{3,2},{4,5},{5,4},{6,7},{7,6},{8,9},{9,8},{10,11... | collective-permute-start | bytes 1216520 | tf_op jit(solution)/shard_map/ppermute | solution.py:35
  48.3 2.0 %collective-permute-start.11 = (f32[4,128]{1,0:T(4,128)S(1)}, f32[4,128]{1,0:T(4,128)S(1)}, u32[]{:S(2)}, u32[]{:S(2)}) collective-permute-start(f32[4,128]{1,0:T(4,128)S(1)} %get-tuple-element.14), channel_id=1, source_target_pairs={{0,1},{1,0},{2,3},{3,2},{4,5},{5,4},{6,7},{7,6},{8,9},{9,8},{10,11... | collective-permute-start | bytes 6152 | tf_op jit(solution)/shard_map/ppermute | solution.py:35
  48.4 5.5 %collective-permute-start.9 = (f32[2,128]{1,0:T(2,128)S(1)}, f32[2,128]{1,0:T(2,128)S(1)}, u32[]{:S(2)}, u32[]{:S(2)}) collective-permute-start(f32[2,128]{1,0:T(2,128)S(1)} %get-tuple-element.12), channel_id=1, source_target_pairs={{2,0},{4,2},{6,4},{0,6},{5,1},{3,7},{10,8},{12,10},{14,12},{8,14},... | collective-permute-start | bytes 3080 | tf_op jit(solution)/shard_map/ppermute | solution.py:238
  50.3 4.7 %collective-permute-start.14 = (f32[4,128]{1,0:T(4,128)S(1)}, f32[4,128]{1,0:T(4,128)S(1)}, u32[]{:S(2)}, u32[]{:S(2)}) collective-permute-start(f32[4,128]{1,0:T(4,128)S(1)} %max.23), channel_id=1, source_target_pairs={{0,24},{8,16},{16,8},{24,0},{1,25},{9,17},{17,9},{25,1},{2,26},{10... | collective-permute-start | bytes 6152 | tf_op jit(solution)/shard_map/ppermute | solution.py:249
  52.0 3.6 %collective-permute-start.13 = (f32[4,128]{1,0:T(4,128)S(1)}, f32[4,128]{1,0:T(4,128)S(1)}, u32[]{:S(2)}, u32[]{:S(2)}) collective-permute-start(f32[4,128]{1,0:T(4,128)S(1)} %max.23), channel_id=1, source_target_pairs={{0,16},{1,9},{8,24},{9,1},{16,0},{17,25},{24,8},{25,17},{2,18},{3,... | collective-permute-start | bytes 6152 | tf_op jit(solution)/shard_map/ppermute | solution.py:246
  53.2 3.6 %collective-permute-start.12 = (f32[4,128]{1,0:T(4,128)S(1)}, f32[4,128]{1,0:T(4,128)S(1)}, u32[]{:S(2)}, u32[]{:S(2)}) collective-permute-start(f32[4,128]{1,0:T(4,128)S(1)} %max.23), channel_id=1, source_target_pairs={{0,8},{1,17},{8,0},{9,25},{16,24},{17,1},{24,16},{25,9},{2,10},{3,... | collective-permute-start | bytes 6152 | tf_op jit(solution)/shard_map/ppermute | solution.py:246
  53.9 1.1 %collective-permute-start.10 = (f32[2,128]{1,0:T(2,128)S(1)}, f32[2,128]{1,0:T(2,128)S(1)}, u32[]{:S(2)}, u32[]{:S(2)}) collective-permute-start(f32[2,128]{1,0:T(2,128)S(1)} %collective-permute-done.9), channel_id=1, source_target_pairs={{0,1},{1,0},{2,3},{3,2},{4,5},{5,4},{6,7},{7,6},{8,9},{9,8},{10,11... | collective-permute-start | bytes 3080 | tf_op jit(solution)/shard_map/ppermute | solution.py:35

commit v20 on v19

--- a/solution.py
+++ b/solution.py
@@ -206,7 +206,7 @@
     routes = [ring_pairs(length, shift) for shift in range(1, length // 2 + 1)]
     trips = []
     for first in range(0, len(routes), 2):
-        ways = enumerate(routes[first : first + 2])
+        ways = enumerate(routes[first : first + 2][::-1])
         trips.append([(2 * a + way, 2 * b + way) for way, route in ways for a, b in route])
     visitors = [lax.ppermute(line, line_axes, trip) for trip in trips]
 
@@ -242,10 +242,9 @@
     ways = [(0, 0, partners[-1])]
     ways += [(1 + k // 2, 2 * (k % 2), way) for k, way in enumerate(partners[:-1])]
     for chunk, row, (first, second) in ways:
-        for order in ((first, second), (second, first)):
+        for offset, order in ((1, (second, first)), (0, (first, second))):
             got = lax.ppermute(merged[chunk], plane_axes, group_trip(groups, *order))
-            bests.append(got[row : row + 1])
-            row += 1
+            bests.append(got[row + offset : row + offset + 1])
     bests.append(lax.ppermute(merged[0], "group", flip(groups, last))[2:3])
     bests.append(merged[0][3:4])
     return functools.reduce(jnp.maximum, bests)[0, :rows]

time: 57.5 us -> 55.2 us (0.960)
  waiting for transfers between devices: 35.1 us -> 30.7 us
  starting transfers between devices: 14.9 us -> 16.9 us
    ppermute x1, waiting for transfers between devices: 5.06 us -> 2.29 us  [local(): visitors = [lax.ppermute(line, line_axes, trip) for trip in trips]]
    ppermute x2, waiting for transfers between devices: 1.76 us -> 0.03 us  [local(): got = lax.ppermute(merged[chunk], plane_axes, group_trip(groups, *order))]
    ppermute x1, starting transfers between devices: 3.47 us -> 4.58 us  [local(): visitors = [lax.ppermute(line, line_axes, trip) for trip in trips]]
    ppermute x1, waiting for transfers between devices: 15.4 us -> 14.3 us  [local(): lax.ppermute(both, plane_axes, group_trip(groups, *way))]
    ppermute x7, starting transfers between devices: 0.75 us -> 1.81 us  [swap(): return lax.ppermute(block, 'core', flip(2, 1))]
    ppermute x1, waiting for transfers between devices: 0.01 us -> 1.03 us  [local(): back = lax.ppermute(part, line_axes, [(b, a) for a, b in trip])]
    ppermute x2, starting transfers between devices: 1.89 us -> 2.58 us  [local(): got = lax.ppermute(merged[chunk], plane_axes, group_trip(groups, *order))]
    ppermute x1, starting transfers between devices: 1.92 us -> 1.28 us  [local(): back = lax.ppermute(part, line_axes, [(b, a) for a, b in trip])]
  transfers between devices with their start and end apart: 15 -> 15, of which waited for: 8 -> 7; matrix products, arithmetic and copies ran while one was open for 1% -> 1% of each run, Pallas kernels for 4% -> 4%
where the time goes in v20:
time: 55.2 us; the launch traced here: 54.9 us
  waiting for transfers between devices  30.7 us (56%)
  starting transfers between devices  16.9 us (31%)
  Pallas kernels  4.83 us (9%)
  local copies, waits for them, and re-layouts  1.7 us (3%)
  other arithmetic  0.69 us (1%)
    ppermute x1, waiting for transfers between devices, local(): lax.ppermute(both, plane_axes, group_trip(groups, *way))  14.3 us
    ppermute x2, waiting for transfers between devices, local(): corner = [lax.ppermute(part, plane_axes, relay) for part in corner]  10.2 us
    ppermute x1, starting transfers between devices, local(): visitors = [lax.ppermute(line, line_axes, trip) for trip in trips]  4.58 us
    pallas_call x2, Pallas kernels, call(): pl.pallas_call(kernel, in_specs=[VMEM] * len(operands), out_specs=[VMEM]...  3.86 us
    ppermute x1, starting transfers between devices, local(): lax.ppermute(both, plane_axes, group_trip(groups, *way))  3 us
    ppermute x7, waiting for transfers between devices, swap(): return lax.ppermute(block, 'core', flip(2, 1))  2.88 us
    ppermute x2, starting transfers between devices, local(): got = lax.ppermute(merged[chunk], plane_axes, group_trip(groups, *order))  2.58 us
    ppermute x1, waiting for transfers between devices, local(): visitors = [lax.ppermute(line, line_axes, trip) for trip in trips]  2.29 us
  transfers between devices with their start and end apart: 15, of which 7 were waited for; matrix products, arithmetic and copies ran while one was open for 1% of the time, Pallas kernels for 4%

profile of v20, /device:TPU:0, one launch (start us, length us, event | category | flops | bytes accessed | tf_op | source)
XLA Modules:
  0.0 54.9 jit_solution(906736332618394179)
XLA Ops:
  0.0 0.5 collective-permute-start
  0.5 0.7 %pad_add_fusion.ids_ref.own_ids_ref = s32[2,96]{1,0:T(2,128)S(1)} fusion(s32[1,96]{1,0:T(1,128)} %bitcast.4, s32[1,96]{1,0:T(1,128)} %bitcast.5), kind=kLoop, calls=%fused_computation | loop fusion | flops 192 | bytes 1536 | tf_op jit(solution)/shard_map/stack | solution.py:201
  1.2 1.1 %copy-done = bf16[96,4096]{1,0:T(8,128)(2,1)S(1)} copy-done((bf16[96,4096]{1,0:T(8,128)(2,1)S(1)}, bf16[96,4096]{1,0:T(8,128)(2,1)}, u32[]{:S(2)}) %copy-start) | copy-done | bytes 786456
  2.3 0.3 shard_map.37.own_ref.refs_0_
  2.6 0.7 %shard_map.38 = (bf16[192,4224]{1,0:T(8,128)(2,1)S(1)}, bf16[6160,128]{1,0:T(8,128)(2,1)S(1)}) custom-call(bf16[96,4224]{1,0:T(8,128)(2,1)S(1)} %shard_map.37.own_ref.refs_0_, s32[2,96]{1,0:T(2,128)S(1)} %pad_add_fusion.ids_ref.own_ids_ref, bf16[96,4096]{1,0:T(8,128)(2,1)S(1)} %collective-permute-done.rows_ref, s32[2,96]{1,0:T(2,128)S(1)} %collective-permute-done.1.ids_ref), custom_call_target="tpu_custom_call" | custom-call | flops 1572864 | bytes 1572864 | tf_op jit(solution)/shard_map/pallas_call | solution.py:77
  3.3 3.0 %collective-permute-start.2 = (bf16[192,4224]{1,0:T(8,128)(2,1)S(1)}, bf16[192,4224]{1,0:T(8,128)(2,1)S(1)}, u32[]{:S(2)}, u32[]{:S(2)}) collective-permute-start(bf16[192,4224]{1,0:T(8,128)(2,1)S(1)} %get-tuple-element.10.refs_1_), channel_id=1, source_target_pairs={{0,8},{1,17},{8,0},{9,25},{16,24},{17,1},{24,16},{25,9},{2,10},{3,... | collective-permute-start | bytes 4866056 | tf_op jit(solution)/shard_map/ppermute | solution.py:214
  6.3 4.6 %collective-permute-start.8 = (bf16[6160,128]{1,0:T(8,128)(2,1)S(1)}, bf16[6160,128]{1,0:T(8,128)(2,1)S(1)}, u32[]{:S(2)}, u32[]{:S(2)}) collective-permute-start(bf16[6160,128]{1,0:T(8,128)(2,1)S(1)} %get-tuple-element.11), channel_id=1, source_target_pairs={{0,4},{6,2},{1,3},{3,5},{5,7},{7,1},{8,12},{14,10},{9,11},{11,13},... | collective-permute-start | bytes 4730888 | tf_op jit(solution)/shard_map/ppermute | solution.py:211
  10.9 14.3 %collective-permute-done.2.refs_2_ = bf16[192,4224]{1,0:T(8,128)(2,1)S(1)} collective-permute-done((bf16[192,4224]{1,0:T(8,128)(2,1)S(1)}, bf16[192,4224]{1,0:T(8,128)(2,1)S(1)}, u32[]{:S(2)}, u32[]{:S(2)}) %collective-permute-start.2) | collective-permute-done | bytes 1622048 | tf_op jit(solution)/shard_map/ppermute | solution.py:214
  25.3 2.1 %collective-permute-start.4 = (bf16[48,4224]{1,0:T(8,128)(2,1)S(1)}, bf16[48,4224]{1,0:T(8,128)(2,1)S(1)}, u32[]{:S(2)}, u32[]{:S(2)}) collective-permute-start(bf16[48,4224]{1,0:T(8,128)(2,1)S(1)} %get-tuple-element.16), channel_id=1, source_target_pairs={{0,16},{1,9},{8,24},{9,1},{16,0},{17,25},{24,8},{25,17},{2,18},{3,... | collective-permute-start | bytes 1216520 | tf_op jit(solution)/shard_map/ppermute | solution.py:219
  27.4 0.1 collective-permute-start.5
  27.5 5.8 %collective-permute-done.4.refs_4_ = bf16[48,4224]{1,0:T(8,128)(2,1)S(1)} collective-permute-done((bf16[48,4224]{1,0:T(8,128)(2,1)S(1)}, bf16[48,4224]{1,0:T(8,128)(2,1)S(1)}, u32[]{:S(2)}, u32[]{:S(2)}) %collective-permute-start.4) | collective-permute-done | bytes 405536 | tf_op jit(solution)/shard_map/ppermute | solution.py:219
  33.3 4.3 %collective-permute-done.5.refs_5_ = bf16[48,4224]{1,0:T(8,128)(2,1)S(1)} collective-permute-done((bf16[48,4224]{1,0:T(8,128)(2,1)S(1)}, bf16[48,4224]{1,0:T(8,128)(2,1)S(1)}, u32[]{:S(2)}, u32[]{:S(2)}) %collective-permute-start.5) | collective-permute-done | bytes 405536 | tf_op jit(solution)/shard_map/ppermute | solution.py:219
  37.7 1.7 %collective-permute-done.7.refs_7_ = bf16[48,4224]{1,0:T(8,128)(2,1)S(1)} collective-permute-done((bf16[48,4224]{1,0:T(8,128)(2,1)S(1)}, bf16[48,4224]{1,0:T(8,128)(2,1)S(1)}, u32[]{:S(2)}, u32[]{:S(2)}) %collective-permute-start.7) | collective-permute-done | bytes 405536 | tf_op jit(solution)/shard_map/ppermute | solution.py:35
  39.4 1.8 %shard_map.39.refs_8_ = f32[1,128]{1,0:T(1,128)S(1)} custom-call(bf16[96,4224]{1,0:T(8,128)(2,1)S(1)} %shard_map.37.own_ref.refs_0_, bf16[192,4224]{1,0:T(8,128)(2,1)S(1)} %get-tuple-element.10.refs_1_, bf16[192,4224]{1,0:T(8,128)(2,1)S(1)} %collective-permute-done.2.refs_2_, bf16[192,4224]{1,0:T(8,128)(2,1)S(1)} %collective-permute-done.3.refs_3_, ...), custom_call_target="tpu_custom_call" | custom-call | flops 805306368 | bytes 7340032 | tf_op jit(solution)/shard_map/pallas_call | solution.py:177
  41.2 2.3 %collective-permute-done.8.refs_0_ = bf16[6160,128]{1,0:T(8,128)(2,1)S(1)} collective-permute-done((bf16[6160,128]{1,0:T(8,128)(2,1)S(1)}, bf16[6160,128]{1,0:T(8,128)(2,1)S(1)}, u32[]{:S(2)}, u32[]{:S(2)}) %collective-permute-start.8) | collective-permute-done | bytes 1576992 | tf_op jit(solution)/shard_map/ppermute | solution.py:211
  43.5 2.1 %shard_map.40 = (f32[2,128]{1,0:T(2,128)S(1)}, f32[4,128]{1,0:T(4,128)S(1)}, f32[4,128]{1,0:T(4,128)S(1)}) custom-call(bf16[6160,128]{1,0:T(8,128)(2,1)S(1)} %collective-permute-done.8.refs_0_, bf16[192,4224]{1,0:T(8,128)(2,1)S(1)} %get-tuple-element.10.refs_1_, bf16[192,4224]{1,0:T(8,128)(2,1)S(1)} %collective-permute-done.2.refs_2_, ...), custom_call_target="tpu_custom_call" | custom-call | flops 1610612736 | bytes 8388608 | tf_op jit(solution)/shard_map/pallas_call | solution.py:177
  45.6 1.3 %collective-permute-start.11 = (f32[4,128]{1,0:T(4,128)S(1)}, f32[4,128]{1,0:T(4,128)S(1)}, u32[]{:S(2)}, u32[]{:S(2)}) collective-permute-start(f32[4,128]{1,0:T(4,128)S(1)} %get-tuple-element.14), channel_id=1, source_target_pairs={{0,1},{1,0},{2,3},{3,2},{4,5},{5,4},{6,7},{7,6},{8,9},{9,8},{10,11... | collective-permute-start | bytes 6152 | tf_op jit(solution)/shard_map/ppermute | solution.py:35
  46.9 1.3 %collective-permute-start.9 = (f32[2,128]{1,0:T(2,128)S(1)}, f32[2,128]{1,0:T(2,128)S(1)}, u32[]{:S(2)}, u32[]{:S(2)}) collective-permute-start(f32[2,128]{1,0:T(2,128)S(1)} %get-tuple-element.12), channel_id=1, source_target_pairs={{4,0},{2,6},{3,1},{5,3},{7,5},{1,7},{12,8},{10,14},{11,9},{13,11},... | collective-permute-start | bytes 3080 | tf_op jit(solution)/shard_map/ppermute | solution.py:238
  48.2 1.4 %collective-permute-start.14 = (f32[4,128]{1,0:T(4,128)S(1)}, f32[4,128]{1,0:T(4,128)S(1)}, u32[]{:S(2)}, u32[]{:S(2)}) collective-permute-start(f32[4,128]{1,0:T(4,128)S(1)} %max.23), channel_id=1, source_target_pairs={{0,24},{8,16},{16,8},{24,0},{1,25},{9,17},{17,9},{25,1},{2,26},{10... | collective-permute-start | bytes 6152 | tf_op jit(solution)/shard_map/ppermute | solution.py:248
  49.6 1.2 %collective-permute-start.13 = (f32[4,128]{1,0:T(4,128)S(1)}, f32[4,128]{1,0:T(4,128)S(1)}, u32[]{:S(2)}, u32[]{:S(2)}) collective-permute-start(f32[4,128]{1,0:T(4,128)S(1)} %max.23), channel_id=1, source_target_pairs={{0,8},{1,17},{8,0},{9,25},{16,24},{17,1},{24,16},{25,9},{2,10},{3,... | collective-permute-start | bytes 6152 | tf_op jit(solution)/shard_map/ppermute | solution.py:246
  50.8 1.4 %collective-permute-start.12 = (f32[4,128]{1,0:T(4,128)S(1)}, f32[4,128]{1,0:T(4,128)S(1)}, u32[]{:S(2)}, u32[]{:S(2)}) collective-permute-start(f32[4,128]{1,0:T(4,128)S(1)} %max.23), channel_id=1, source_target_pairs={{0,16},{1,9},{8,24},{9,1},{16,0},{17,25},{24,8},{25,17},{2,18},{3,... | collective-permute-start | bytes 6152 | tf_op jit(solution)/shard_map/ppermute | solution.py:246
  52.2 1.0 %collective-permute-done.9 = f32[2,128]{1,0:T(2,128)S(1)} collective-permute-done((f32[2,128]{1,0:T(2,128)S(1)}, f32[2,128]{1,0:T(2,128)S(1)}, u32[]{:S(2)}, u32[]{:S(2)}) %collective-permute-start.9) | collective-permute-done | bytes 1056 | tf_op jit(solution)/shard_map/ppermute | solution.py:238
  53.2 1.1 %collective-permute-done.10 = f32[2,128]{1,0:T(2,128)S(1)} collective-permute-done((f32[2,128]{1,0:T(2,128)S(1)}, f32[2,128]{1,0:T(2,128)S(1)}, u32[]{:S(2)}, u32[]{:S(2)}) %collective-permute-start.10) | collective-permute-done | bytes 1056 | tf_op jit(solution)/shard_map/ppermute | solution.py:35
  54.4 0.5 slice_bitcast_fusion
  (17 shorter events, 0.2 us)
Async XLA Ops:
  0.0 2.6 %collective-permute-start = (bf16[96,4096]{1,0:T(8,128)(2,1)}, bf16[96,4096]{1,0:T(8,128)(2,1)S(1)}, u32[]{:S(2)}, u32[]{:S(2)}) collective-permute-start(bf16[96,4096]{1,0:T(8,128)(2,1)} %rows_ref.1), channel_id=1, source_target_pairs={{0,1},{1,0},{2,3},{3,2},{4,5},{5,4},{6,7},{7,6},{8,9},{9,8},{10,11... | collective-permute-start | bytes 2359304 | tf_op jit(solution)/shard_map/ppermute | solution.py:35
  1.1 1.5 %collective-permute-start.1 = (s32[2,96]{1,0:T(2,128)S(1)}, s32[2,96]{1,0:T(2,128)S(1)}, u32[]{:S(2)}, u32[]{:S(2)}) collective-permute-start(s32[2,96]{1,0:T(2,128)S(1)} %pad_add_fusion.ids_ref.own_ids_ref), channel_id=1, source_target_pairs={{0,1},{1,0},{2,3},{3,2},{4,5},{5,4},{6,7},{7,6},{8,9},{9,8},{10,11... | collective-permute-start | bytes 2312 | tf_op jit(solution)/shard_map/ppermute | solution.py:35
  1.2 1.1 %copy-start = (bf16[96,4096]{1,0:T(8,128)(2,1)S(1)}, bf16[96,4096]{1,0:T(8,128)(2,1)}, u32[]{:S(2)}) copy-start(bf16[96,4096]{1,0:T(8,128)(2,1)} %rows_ref.1) | copy-start | bytes 2359300
  3.3 21.9 %collective-permute-start.2 = (bf16[192,4224]{1,0:T(8,128)(2,1)S(1)}, bf16[192,4224]{1,0:T(8,128)(2,1)S(1)}, u32[]{:S(2)}, u32[]{:S(2)}) collective-permute-start(bf16[192,4224]{1,0:T(8,128)(2,1)S(1)} %get-tuple-element.10.refs_1_), channel_id=1, source_target_pairs={{0,8},{1,17},{8,0},{9,25},{16,24},{17,1},{24,16},{25,9},{2,10},{3,... | collective-permute-start | bytes 4866056 | tf_op jit(solution)/shard_map/ppermute | solution.py:214
  6.3 37.2 %collective-permute-start.8 = (bf16[6160,128]{1,0:T(8,128)(2,1)S(1)}, bf16[6160,128]{1,0:T(8,128)(2,1)S(1)}, u32[]{:S(2)}, u32[]{:S(2)}) collective-permute-start(bf16[6160,128]{1,0:T(8,128)(2,1)S(1)} %get-tuple-element.11), channel_id=1, source_target_pairs={{0,4},{6,2},{1,3},{3,5},{5,7},{7,1},{8,12},{14,10},{9,11},{11,13},... | collective-permute-start | bytes 4730888 | tf_op jit(solution)/shard_map/ppermute | solution.py:211
  25.3 14.2 %collective-permute-start.3 = (bf16[192,4224]{1,0:T(8,128)(2,1)S(1)}, bf16[192,4224]{1,0:T(8,128)(2,1)S(1)}, u32[]{:S(2)}, u32[]{:S(2)}) collective-permute-start(bf16[192,4224]{1,0:T(8,128)(2,1)S(1)} %collective-permute-done.2.refs_2_), channel_id=1, source_target_pairs={{0,1},{1,0},{2,3},{3,2},{4,5},{5,4},{6,7},{7,6},{8,9},{9,8},{10,11... | collective-permute-start | bytes 4866056 | tf_op jit(solution)/shard_map/ppermute | solution.py:35
  25.3 8.0 %collective-permute-start.4 = (bf16[48,4224]{1,0:T(8,128)(2,1)S(1)}, bf16[48,4224]{1,0:T(8,128)(2,1)S(1)}, u32[]{:S(2)}, u32[]{:S(2)}) collective-permute-start(bf16[48,4224]{1,0:T(8,128)(2,1)S(1)} %get-tuple-element.16), channel_id=1, source_target_pairs={{0,16},{1,9},{8,24},{9,1},{16,0},{17,25},{24,8},{25,17},{2,18},{3,... | collective-permute-start | bytes 1216520 | tf_op jit(solution)/shard_map/ppermute | solution.py:219
  27.4 10.2 %collective-permute-start.5 = (bf16[48,4224]{1,0:T(8,128)(2,1)S(1)}, bf16[48,4224]{1,0:T(8,128)(2,1)S(1)}, u32[]{:S(2)}, u32[]{:S(2)}) collective-permute-start(bf16[48,4224]{1,0:T(8,128)(2,1)S(1)} %get-tuple-element.15), channel_id=1, source_target_pairs={{0,16},{1,9},{8,24},{9,1},{16,0},{17,25},{24,8},{25,17},{2,18},{3,... | collective-permute-start | bytes 1216520 | tf_op jit(solution)/shard_map/ppermute | solution.py:219
  33.3 4.4 %collective-permute-start.6 = (bf16[48,4224]{1,0:T(8,128)(2,1)S(1)}, bf16[48,4224]{1,0:T(8,128)(2,1)S(1)}, u32[]{:S(2)}, u32[]{:S(2)}) collective-permute-start(bf16[48,4224]{1,0:T(8,128)(2,1)S(1)} %collective-permute-done.4.refs_4_), channel_id=1, source_target_pairs={{0,1},{1,0},{2,3},{3,2},{4,5},{5,4},{6,7},{7,6},{8,9},{9,8},{10,11... | collective-permute-start | bytes 1216520 | tf_op jit(solution)/shard_map/ppermute | solution.py:35
  37.7 1.7 %collective-permute-start.7 = (bf16[48,4224]{1,0:T(8,128)(2,1)S(1)}, bf16[48,4224]{1,0:T(8,128)(2,1)S(1)}, u32[]{:S(2)}, u32[]{:S(2)}) collective-permute-start(bf16[48,4224]{1,0:T(8,128)(2,1)S(1)} %collective-permute-done.5.refs_5_), channel_id=1, source_target_pairs={{0,1},{1,0},{2,3},{3,2},{4,5},{5,4},{6,7},{7,6},{8,9},{9,8},{10,11... | collective-permute-start | bytes 1216520 | tf_op jit(solution)/shard_map/ppermute | solution.py:35
  45.6 2.6 %collective-permute-start.11 = (f32[4,128]{1,0:T(4,128)S(1)}, f32[4,128]{1,0:T(4,128)S(1)}, u32[]{:S(2)}, u32[]{:S(2)}) collective-permute-start(f32[4,128]{1,0:T(4,128)S(1)} %get-tuple-element.14), channel_id=1, source_target_pairs={{0,1},{1,0},{2,3},{3,2},{4,5},{5,4},{6,7},{7,6},{8,9},{9,8},{10,11... | collective-permute-start | bytes 6152 | tf_op jit(solution)/shard_map/ppermute | solution.py:35
  46.9 6.3 %collective-permute-start.9 = (f32[2,128]{1,0:T(2,128)S(1)}, f32[2,128]{1,0:T(2,128)S(1)}, u32[]{:S(2)}, u32[]{:S(2)}) collective-permute-start(f32[2,128]{1,0:T(2,128)S(1)} %get-tuple-element.12), channel_id=1, source_target_pairs={{4,0},{2,6},{3,1},{5,3},{7,5},{1,7},{12,8},{10,14},{11,9},{13,11},... | collective-permute-start | bytes 3080 | tf_op jit(solution)/shard_map/ppermute | solution.py:238
  48.2 6.2 %collective-permute-start.14 = (f32[4,128]{1,0:T(4,128)S(1)}, f32[4,128]{1,0:T(4,128)S(1)}, u32[]{:S(2)}, u32[]{:S(2)}) collective-permute-start(f32[4,128]{1,0:T(4,128)S(1)} %max.23), channel_id=1, source_target_pairs={{0,24},{8,16},{16,8},{24,0},{1,25},{9,17},{17,9},{25,1},{2,26},{10... | collective-permute-start | bytes 6152 | tf_op jit(solution)/shard_map/ppermute | solution.py:248
  49.6 4.8 %collective-permute-start.13 = (f32[4,128]{1,0:T(4,128)S(1)}, f32[4,128]{1,0:T(4,128)S(1)}, u32[]{:S(2)}, u32[]{:S(2)}) collective-permute-start(f32[4,128]{1,0:T(4,128)S(1)} %max.23), channel_id=1, source_target_pairs={{0,8},{1,17},{8,0},{9,25},{16,24},{17,1},{24,16},{25,9},{2,10},{3,... | collective-permute-start | bytes 6152 | tf_op jit(solution)/shard_map/ppermute | solution.py:246
  50.8 3.6 %collective-permute-start.12 = (f32[4,128]{1,0:T(4,128)S(1)}, f32[4,128]{1,0:T(4,128)S(1)}, u32[]{:S(2)}, u32[]{:S(2)}) collective-permute-start(f32[4,128]{1,0:T(4,128)S(1)} %max.23), channel_id=1, source_target_pairs={{0,16},{1,9},{8,24},{9,1},{16,0},{17,25},{24,8},{25,17},{2,18},{3,... | collective-permute-start | bytes 6152 | tf_op jit(solution)/shard_map/ppermute | solution.py:246
  53.2 1.1 %collective-permute-start.10 = (f32[2,128]{1,0:T(2,128)S(1)}, f32[2,128]{1,0:T(2,128)S(1)}, u32[]{:S(2)}, u32[]{:S(2)}) collective-permute-start(f32[2,128]{1,0:T(2,128)S(1)} %collective-permute-done.9), channel_id=1, source_target_pairs={{0,1},{1,0},{2,3},{3,2},{4,5},{5,4},{6,7},{7,6},{8,9},{9,8},{10,11... | collective-permute-start | bytes 3080 | tf_op jit(solution)/shard_map/ppermute | solution.py:35

commit v21 on v20

--- a/solution.py
+++ b/solution.py
@@ -9,7 +9,7 @@
 
 AXES = ("group", "z", "core")
 LANES = 128
-CHUNK = 512
+CHUNK = 1024
 TAIL = 16
 VMEM = pl.BlockSpec(memory_space=pltpu.VMEM)
 
@@ -59,8 +59,9 @@
     both_ref[:count, :] = own_ref[...]
     pack_into(both_ref, count, rows_ref[...], ids_ref[...])
     for k in range(width // LANES):
-        columns = both_ref[:, k * LANES : (k + 1) * LANES]
-        line_ref[2 * count * k : 2 * count * (k + 1), :] = columns
+        columns, start = pl.ds(k * LANES, LANES), 2 * count * k
+        line_ref[start : start + count, :] = own_ref[:, columns]
+        line_ref[start + count : start + 2 * count, :] = both_ref[count:, columns]
     lines = []
     for ref in (own_ids_ref, ids_ref):
         ids = ref[...].astype(jnp.float32)

time: 55.2 us -> 55.2 us (level)
  no operation moved by 1% of the time
where the time goes in v21:
time: 55.2 us; the launch traced here: 54.9 us
  waiting for transfers between devices  30.7 us (56%)
  starting transfers between devices  16.9 us (31%)
  Pallas kernels  4.83 us (9%)
  local copies, waits for them, and re-layouts  1.7 us (3%)
  other arithmetic  0.69 us (1%)
    ppermute x1, waiting for transfers between devices, local(): lax.ppermute(both, plane_axes, group_trip(groups, *way))  14.3 us
    ppermute x2, waiting for transfers between devices, local(): corner = [lax.ppermute(part, plane_axes, relay) for part in corner]  10.2 us
    ppermute x1, starting transfers between devices, local(): visitors = [lax.ppermute(line, line_axes, trip) for trip in trips]  4.58 us
    pallas_call x2, Pallas kernels, call(): pl.pallas_call(kernel, in_specs=[VMEM] * len(operands), out_specs=[VMEM]...  3.86 us
    ppermute x1, starting transfers between devices, local(): lax.ppermute(both, plane_axes, group_trip(groups, *way))  3 us
    ppermute x7, waiting for transfers between devices, swap(): return lax.ppermute(block, 'core', flip(2, 1))  2.88 us
    ppermute x2, starting transfers between devices, local(): got = lax.ppermute(merged[chunk], plane_axes, group_trip(groups, *order))  2.58 us
    ppermute x1, waiting for transfers between devices, local(): visitors = [lax.ppermute(line, line_axes, trip) for trip in trips]  2.29 us
  transfers between devices with their start and end apart: 15, of which 7 were waited for; matrix products, arithmetic and copies ran while one was open for 1% of the time, Pallas kernels for 4%

profile of v21, /device:TPU:0, one launch (start us, length us, event | category | flops | bytes accessed | tf_op | source)
XLA Modules:
  0.0 54.9 jit_solution(629546323980639444)
XLA Ops:
  0.0 0.5 collective-permute-start
  0.5 0.7 %pad_add_fusion.ids_ref.own_ids_ref = s32[2,96]{1,0:T(2,128)S(1)} fusion(s32[1,96]{1,0:T(1,128)} %bitcast.4, s32[1,96]{1,0:T(1,128)} %bitcast.5), kind=kLoop, calls=%fused_computation | loop fusion | flops 192 | bytes 1536 | tf_op jit(solution)/shard_map/stack | solution.py:202
  1.2 1.1 %copy-done = bf16[96,4096]{1,0:T(8,128)(2,1)S(1)} copy-done((bf16[96,4096]{1,0:T(8,128)(2,1)S(1)}, bf16[96,4096]{1,0:T(8,128)(2,1)}, u32[]{:S(2)}) %copy-start) | copy-done | bytes 786456
  2.3 0.3 shard_map.37.own_ref.refs_0_
  2.6 0.7 %shard_map.38 = (bf16[192,4224]{1,0:T(8,128)(2,1)S(1)}, bf16[6160,128]{1,0:T(8,128)(2,1)S(1)}) custom-call(bf16[96,4224]{1,0:T(8,128)(2,1)S(1)} %shard_map.37.own_ref.refs_0_, s32[2,96]{1,0:T(2,128)S(1)} %pad_add_fusion.ids_ref.own_ids_ref, bf16[96,4096]{1,0:T(8,128)(2,1)S(1)} %collective-permute-done.rows_ref, s32[2,96]{1,0:T(2,128)S(1)} %collective-permute-done.1.ids_ref), custom_call_target="tpu_custom_call" | custom-call | flops 1572864 | bytes 1572864 | tf_op jit(solution)/shard_map/pallas_call | solution.py:78
  3.3 3.0 %collective-permute-start.2 = (bf16[192,4224]{1,0:T(8,128)(2,1)S(1)}, bf16[192,4224]{1,0:T(8,128)(2,1)S(1)}, u32[]{:S(2)}, u32[]{:S(2)}) collective-permute-start(bf16[192,4224]{1,0:T(8,128)(2,1)S(1)} %get-tuple-element.10.refs_1_), channel_id=1, source_target_pairs={{0,8},{1,17},{8,0},{9,25},{16,24},{17,1},{24,16},{25,9},{2,10},{3,... | collective-permute-start | bytes 4866056 | tf_op jit(solution)/shard_map/ppermute | solution.py:215
  6.3 4.6 %collective-permute-start.8 = (bf16[6160,128]{1,0:T(8,128)(2,1)S(1)}, bf16[6160,128]{1,0:T(8,128)(2,1)S(1)}, u32[]{:S(2)}, u32[]{:S(2)}) collective-permute-start(bf16[6160,128]{1,0:T(8,128)(2,1)S(1)} %get-tuple-element.11), channel_id=1, source_target_pairs={{0,4},{6,2},{1,3},{3,5},{5,7},{7,1},{8,12},{14,10},{9,11},{11,13},... | collective-permute-start | bytes 4730888 | tf_op jit(solution)/shard_map/ppermute | solution.py:212
  10.9 14.3 %collective-permute-done.2.refs_2_ = bf16[192,4224]{1,0:T(8,128)(2,1)S(1)} collective-permute-done((bf16[192,4224]{1,0:T(8,128)(2,1)S(1)}, bf16[192,4224]{1,0:T(8,128)(2,1)S(1)}, u32[]{:S(2)}, u32[]{:S(2)}) %collective-permute-start.2) | collective-permute-done | bytes 1622048 | tf_op jit(solution)/shard_map/ppermute | solution.py:215
  25.3 2.1 %collective-permute-start.4 = (bf16[48,4224]{1,0:T(8,128)(2,1)S(1)}, bf16[48,4224]{1,0:T(8,128)(2,1)S(1)}, u32[]{:S(2)}, u32[]{:S(2)}) collective-permute-start(bf16[48,4224]{1,0:T(8,128)(2,1)S(1)} %get-tuple-element.16), channel_id=1, source_target_pairs={{0,16},{1,9},{8,24},{9,1},{16,0},{17,25},{24,8},{25,17},{2,18},{3,... | collective-permute-start | bytes 1216520 | tf_op jit(solution)/shard_map/ppermute | solution.py:220
  27.4 0.1 collective-permute-start.5
  27.5 5.8 %collective-permute-done.4.refs_4_ = bf16[48,4224]{1,0:T(8,128)(2,1)S(1)} collective-permute-done((bf16[48,4224]{1,0:T(8,128)(2,1)S(1)}, bf16[48,4224]{1,0:T(8,128)(2,1)S(1)}, u32[]{:S(2)}, u32[]{:S(2)}) %collective-permute-start.4) | collective-permute-done | bytes 405536 | tf_op jit(solution)/shard_map/ppermute | solution.py:220
  33.3 4.3 %collective-permute-done.5.refs_5_ = bf16[48,4224]{1,0:T(8,128)(2,1)S(1)} collective-permute-done((bf16[48,4224]{1,0:T(8,128)(2,1)S(1)}, bf16[48,4224]{1,0:T(8,128)(2,1)S(1)}, u32[]{:S(2)}, u32[]{:S(2)}) %collective-permute-start.5) | collective-permute-done | bytes 405536 | tf_op jit(solution)/shard_map/ppermute | solution.py:220
  37.7 1.7 %collective-permute-done.7.refs_7_ = bf16[48,4224]{1,0:T(8,128)(2,1)S(1)} collective-permute-done((bf16[48,4224]{1,0:T(8,128)(2,1)S(1)}, bf16[48,4224]{1,0:T(8,128)(2,1)S(1)}, u32[]{:S(2)}, u32[]{:S(2)}) %collective-permute-start.7) | collective-permute-done | bytes 405536 | tf_op jit(solution)/shard_map/ppermute | solution.py:35
  39.4 1.8 %shard_map.39.refs_8_ = f32[1,128]{1,0:T(1,128)S(1)} custom-call(bf16[96,4224]{1,0:T(8,128)(2,1)S(1)} %shard_map.37.own_ref.refs_0_, bf16[192,4224]{1,0:T(8,128)(2,1)S(1)} %get-tuple-element.10.refs_1_, bf16[192,4224]{1,0:T(8,128)(2,1)S(1)} %collective-permute-done.2.refs_2_, bf16[192,4224]{1,0:T(8,128)(2,1)S(1)} %collective-permute-done.3.refs_3_, ...), custom_call_target="tpu_custom_call" | custom-call | flops 805306368 | bytes 7340032 | tf_op jit(solution)/shard_map/pallas_call | solution.py:178
  41.2 2.3 %collective-permute-done.8.refs_0_ = bf16[6160,128]{1,0:T(8,128)(2,1)S(1)} collective-permute-done((bf16[6160,128]{1,0:T(8,128)(2,1)S(1)}, bf16[6160,128]{1,0:T(8,128)(2,1)S(1)}, u32[]{:S(2)}, u32[]{:S(2)}) %collective-permute-start.8) | collective-permute-done | bytes 1576992 | tf_op jit(solution)/shard_map/ppermute | solution.py:212
  43.5 2.1 %shard_map.40 = (f32[2,128]{1,0:T(2,128)S(1)}, f32[4,128]{1,0:T(4,128)S(1)}, f32[4,128]{1,0:T(4,128)S(1)}) custom-call(bf16[6160,128]{1,0:T(8,128)(2,1)S(1)} %collective-permute-done.8.refs_0_, bf16[192,4224]{1,0:T(8,128)(2,1)S(1)} %get-tuple-element.10.refs_1_, bf16[192,4224]{1,0:T(8,128)(2,1)S(1)} %collective-permute-done.2.refs_2_, ...), custom_call_target="tpu_custom_call" | custom-call | flops 1610612736 | bytes 8388608 | tf_op jit(solution)/shard_map/pallas_call | solution.py:178
  45.6 1.3 %collective-permute-start.11 = (f32[4,128]{1,0:T(4,128)S(1)}, f32[4,128]{1,0:T(4,128)S(1)}, u32[]{:S(2)}, u32[]{:S(2)}) collective-permute-start(f32[4,128]{1,0:T(4,128)S(1)} %get-tuple-element.14), channel_id=1, source_target_pairs={{0,1},{1,0},{2,3},{3,2},{4,5},{5,4},{6,7},{7,6},{8,9},{9,8},{10,11... | collective-permute-start | bytes 6152 | tf_op jit(solution)/shard_map/ppermute | solution.py:35
  46.9 1.3 %collective-permute-start.9 = (f32[2,128]{1,0:T(2,128)S(1)}, f32[2,128]{1,0:T(2,128)S(1)}, u32[]{:S(2)}, u32[]{:S(2)}) collective-permute-start(f32[2,128]{1,0:T(2,128)S(1)} %get-tuple-element.12), channel_id=1, source_target_pairs={{4,0},{2,6},{3,1},{5,3},{7,5},{1,7},{12,8},{10,14},{11,9},{13,11},... | collective-permute-start | bytes 3080 | tf_op jit(solution)/shard_map/ppermute | solution.py:239
  48.2 1.4 %collective-permute-start.14 = (f32[4,128]{1,0:T(4,128)S(1)}, f32[4,128]{1,0:T(4,128)S(1)}, u32[]{:S(2)}, u32[]{:S(2)}) collective-permute-start(f32[4,128]{1,0:T(4,128)S(1)} %max.23), channel_id=1, source_target_pairs={{0,24},{8,16},{16,8},{24,0},{1,25},{9,17},{17,9},{25,1},{2,26},{10... | collective-permute-start | bytes 6152 | tf_op jit(solution)/shard_map/ppermute | solution.py:249
  49.6 1.2 %collective-permute-start.13 = (f32[4,128]{1,0:T(4,128)S(1)}, f32[4,128]{1,0:T(4,128)S(1)}, u32[]{:S(2)}, u32[]{:S(2)}) collective-permute-start(f32[4,128]{1,0:T(4,128)S(1)} %max.23), channel_id=1, source_target_pairs={{0,8},{1,17},{8,0},{9,25},{16,24},{17,1},{24,16},{25,9},{2,10},{3,... | collective-permute-start | bytes 6152 | tf_op jit(solution)/shard_map/ppermute | solution.py:247
  50.8 1.4 %collective-permute-start.12 = (f32[4,128]{1,0:T(4,128)S(1)}, f32[4,128]{1,0:T(4,128)S(1)}, u32[]{:S(2)}, u32[]{:S(2)}) collective-permute-start(f32[4,128]{1,0:T(4,128)S(1)} %max.23), channel_id=1, source_target_pairs={{0,16},{1,9},{8,24},{9,1},{16,0},{17,25},{24,8},{25,17},{2,18},{3,... | collective-permute-start | bytes 6152 | tf_op jit(solution)/shard_map/ppermute | solution.py:247
  52.2 1.0 %collective-permute-done.9 = f32[2,128]{1,0:T(2,128)S(1)} collective-permute-done((f32[2,128]{1,0:T(2,128)S(1)}, f32[2,128]{1,0:T(2,128)S(1)}, u32[]{:S(2)}, u32[]{:S(2)}) %collective-permute-start.9) | collective-permute-done | bytes 1056 | tf_op jit(solution)/shard_map/ppermute | solution.py:239
  53.2 1.1 %collective-permute-done.10 = f32[2,128]{1,0:T(2,128)S(1)} collective-permute-done((f32[2,128]{1,0:T(2,128)S(1)}, f32[2,128]{1,0:T(2,128)S(1)}, u32[]{:S(2)}, u32[]{:S(2)}) %collective-permute-start.10) | collective-permute-done | bytes 1056 | tf_op jit(solution)/shard_map/ppermute | solution.py:35
  54.4 0.5 slice_bitcast_fusion
  (17 shorter events, 0.2 us)
Async XLA Ops:
  0.0 2.6 %collective-permute-start = (bf16[96,4096]{1,0:T(8,128)(2,1)}, bf16[96,4096]{1,0:T(8,128)(2,1)S(1)}, u32[]{:S(2)}, u32[]{:S(2)}) collective-permute-start(bf16[96,4096]{1,0:T(8,128)(2,1)} %rows_ref.1), channel_id=1, source_target_pairs={{0,1},{1,0},{2,3},{3,2},{4,5},{5,4},{6,7},{7,6},{8,9},{9,8},{10,11... | collective-permute-start | bytes 2359304 | tf_op jit(solution)/shard_map/ppermute | solution.py:35
  1.1 1.5 %collective-permute-start.1 = (s32[2,96]{1,0:T(2,128)S(1)}, s32[2,96]{1,0:T(2,128)S(1)}, u32[]{:S(2)}, u32[]{:S(2)}) collective-permute-start(s32[2,96]{1,0:T(2,128)S(1)} %pad_add_fusion.ids_ref.own_ids_ref), channel_id=1, source_target_pairs={{0,1},{1,0},{2,3},{3,2},{4,5},{5,4},{6,7},{7,6},{8,9},{9,8},{10,11... | collective-permute-start | bytes 2312 | tf_op jit(solution)/shard_map/ppermute | solution.py:35
  1.2 1.1 %copy-start = (bf16[96,4096]{1,0:T(8,128)(2,1)S(1)}, bf16[96,4096]{1,0:T(8,128)(2,1)}, u32[]{:S(2)}) copy-start(bf16[96,4096]{1,0:T(8,128)(2,1)} %rows_ref.1) | copy-start | bytes 2359300
  3.3 21.9 %collective-permute-start.2 = (bf16[192,4224]{1,0:T(8,128)(2,1)S(1)}, bf16[192,4224]{1,0:T(8,128)(2,1)S(1)}, u32[]{:S(2)}, u32[]{:S(2)}) collective-permute-start(bf16[192,4224]{1,0:T(8,128)(2,1)S(1)} %get-tuple-element.10.refs_1_), channel_id=1, source_target_pairs={{0,8},{1,17},{8,0},{9,25},{16,24},{17,1},{24,16},{25,9},{2,10},{3,... | collective-permute-start | bytes 4866056 | tf_op jit(solution)/shard_map/ppermute | solution.py:215
  6.3 37.2 %collective-permute-start.8 = (bf16[6160,128]{1,0:T(8,128)(2,1)S(1)}, bf16[6160,128]{1,0:T(8,128)(2,1)S(1)}, u32[]{:S(2)}, u32[]{:S(2)}) collective-permute-start(bf16[6160,128]{1,0:T(8,128)(2,1)S(1)} %get-tuple-element.11), channel_id=1, source_target_pairs={{0,4},{6,2},{1,3},{3,5},{5,7},{7,1},{8,12},{14,10},{9,11},{11,13},... | collective-permute-start | bytes 4730888 | tf_op jit(solution)/shard_map/ppermute | solution.py:212
  25.3 14.2 %collective-permute-start.3 = (bf16[192,4224]{1,0:T(8,128)(2,1)S(1)}, bf16[192,4224]{1,0:T(8,128)(2,1)S(1)}, u32[]{:S(2)}, u32[]{:S(2)}) collective-permute-start(bf16[192,4224]{1,0:T(8,128)(2,1)S(1)} %collective-permute-done.2.refs_2_), channel_id=1, source_target_pairs={{0,1},{1,0},{2,3},{3,2},{4,5},{5,4},{6,7},{7,6},{8,9},{9,8},{10,11... | collective-permute-start | bytes 4866056 | tf_op jit(solution)/shard_map/ppermute | solution.py:35
  25.3 8.0 %collective-permute-start.4 = (bf16[48,4224]{1,0:T(8,128)(2,1)S(1)}, bf16[48,4224]{1,0:T(8,128)(2,1)S(1)}, u32[]{:S(2)}, u32[]{:S(2)}) collective-permute-start(bf16[48,4224]{1,0:T(8,128)(2,1)S(1)} %get-tuple-element.16), channel_id=1, source_target_pairs={{0,16},{1,9},{8,24},{9,1},{16,0},{17,25},{24,8},{25,17},{2,18},{3,... | collective-permute-start | bytes 1216520 | tf_op jit(solution)/shard_map/ppermute | solution.py:220
  27.4 10.2 %collective-permute-start.5 = (bf16[48,4224]{1,0:T(8,128)(2,1)S(1)}, bf16[48,4224]{1,0:T(8,128)(2,1)S(1)}, u32[]{:S(2)}, u32[]{:S(2)}) collective-permute-start(bf16[48,4224]{1,0:T(8,128)(2,1)S(1)} %get-tuple-element.15), channel_id=1, source_target_pairs={{0,16},{1,9},{8,24},{9,1},{16,0},{17,25},{24,8},{25,17},{2,18},{3,... | collective-permute-start | bytes 1216520 | tf_op jit(solution)/shard_map/ppermute | solution.py:220
  33.3 4.4 %collective-permute-start.6 = (bf16[48,4224]{1,0:T(8,128)(2,1)S(1)}, bf16[48,4224]{1,0:T(8,128)(2,1)S(1)}, u32[]{:S(2)}, u32[]{:S(2)}) collective-permute-start(bf16[48,4224]{1,0:T(8,128)(2,1)S(1)} %collective-permute-done.4.refs_4_), channel_id=1, source_target_pairs={{0,1},{1,0},{2,3},{3,2},{4,5},{5,4},{6,7},{7,6},{8,9},{9,8},{10,11... | collective-permute-start | bytes 1216520 | tf_op jit(solution)/shard_map/ppermute | solution.py:35
  37.7 1.7 %collective-permute-start.7 = (bf16[48,4224]{1,0:T(8,128)(2,1)S(1)}, bf16[48,4224]{1,0:T(8,128)(2,1)S(1)}, u32[]{:S(2)}, u32[]{:S(2)}) collective-permute-start(bf16[48,4224]{1,0:T(8,128)(2,1)S(1)} %collective-permute-done.5.refs_5_), channel_id=1, source_target_pairs={{0,1},{1,0},{2,3},{3,2},{4,5},{5,4},{6,7},{7,6},{8,9},{9,8},{10,11... | collective-permute-start | bytes 1216520 | tf_op jit(solution)/shard_map/ppermute | solution.py:35
  45.6 2.6 %collective-permute-start.11 = (f32[4,128]{1,0:T(4,128)S(1)}, f32[4,128]{1,0:T(4,128)S(1)}, u32[]{:S(2)}, u32[]{:S(2)}) collective-permute-start(f32[4,128]{1,0:T(4,128)S(1)} %get-tuple-element.14), channel_id=1, source_target_pairs={{0,1},{1,0},{2,3},{3,2},{4,5},{5,4},{6,7},{7,6},{8,9},{9,8},{10,11... | collective-permute-start | bytes 6152 | tf_op jit(solution)/shard_map/ppermute | solution.py:35
  46.9 6.3 %collective-permute-start.9 = (f32[2,128]{1,0:T(2,128)S(1)}, f32[2,128]{1,0:T(2,128)S(1)}, u32[]{:S(2)}, u32[]{:S(2)}) collective-permute-start(f32[2,128]{1,0:T(2,128)S(1)} %get-tuple-element.12), channel_id=1, source_target_pairs={{4,0},{2,6},{3,1},{5,3},{7,5},{1,7},{12,8},{10,14},{11,9},{13,11},... | collective-permute-start | bytes 3080 | tf_op jit(solution)/shard_map/ppermute | solution.py:239
  48.2 6.2 %collective-permute-start.14 = (f32[4,128]{1,0:T(4,128)S(1)}, f32[4,128]{1,0:T(4,128)S(1)}, u32[]{:S(2)}, u32[]{:S(2)}) collective-permute-start(f32[4,128]{1,0:T(4,128)S(1)} %max.23), channel_id=1, source_target_pairs={{0,24},{8,16},{16,8},{24,0},{1,25},{9,17},{17,9},{25,1},{2,26},{10... | collective-permute-start | bytes 6152 | tf_op jit(solution)/shard_map/ppermute | solution.py:249
  49.6 4.8 %collective-permute-start.13 = (f32[4,128]{1,0:T(4,128)S(1)}, f32[4,128]{1,0:T(4,128)S(1)}, u32[]{:S(2)}, u32[]{:S(2)}) collective-permute-start(f32[4,128]{1,0:T(4,128)S(1)} %max.23), channel_id=1, source_target_pairs={{0,8},{1,17},{8,0},{9,25},{16,24},{17,1},{24,16},{25,9},{2,10},{3,... | collective-permute-start | bytes 6152 | tf_op jit(solution)/shard_map/ppermute | solution.py:247
  50.8 3.6 %collective-permute-start.12 = (f32[4,128]{1,0:T(4,128)S(1)}, f32[4,128]{1,0:T(4,128)S(1)}, u32[]{:S(2)}, u32[]{:S(2)}) collective-permute-start(f32[4,128]{1,0:T(4,128)S(1)} %max.23), channel_id=1, source_target_pairs={{0,16},{1,9},{8,24},{9,1},{16,0},{17,25},{24,8},{25,17},{2,18},{3,... | collective-permute-start | bytes 6152 | tf_op jit(solution)/shard_map/ppermute | solution.py:247
  53.2 1.1 %collective-permute-start.10 = (f32[2,128]{1,0:T(2,128)S(1)}, f32[2,128]{1,0:T(2,128)S(1)}, u32[]{:S(2)}, u32[]{:S(2)}) collective-permute-start(f32[2,128]{1,0:T(2,128)S(1)} %collective-permute-done.9), channel_id=1, source_target_pairs={{0,1},{1,0},{2,3},{3,2},{4,5},{5,4},{6,7},{7,6},{8,9},{9,8},{10,11... | collective-permute-start | bytes 3080 | tf_op jit(solution)/shard_map/ppermute | solution.py:35

commit v22 on v20

--- a/solution.py
+++ b/solution.py
@@ -24,15 +24,22 @@
     return (values * lax.rsqrt(total)).astype(jnp.bfloat16)
 
 
-def ring_pairs(length, shift):
-    if 2 * shift < length:
-        return [(k, (k + shift) % length) for k in range(length)]
-    pairs = [(k, k + shift) for k in range(length // 2)]
-    return [pair[:: 1 - 2 * (pair[0] % 2)] for pair in pairs]
-
-
 def swap(block):
     return lax.ppermute(block, "core", flip(2, 1))
+
+
+def line_trips(length):
+    if length == 4:
+        ways = [[(0, 1), (1, 2), (2, 3)], [(2, 0), (3, 1), (0, 3)]]
+    else:
+        ways = [[(k, (k + shift) % length) for k in range(length)] for shift in range(1, (length + 1) // 2)]
+        if length % 2 == 0:
+            pairs = [(k, k + length // 2) for k in range(length // 2)]
+            ways.append([pair[:: 1 - 2 * (pair[0] % 2)] for pair in pairs])
+    return [
+        [(2 * a + core, 2 * b + core) for core, way in enumerate(ways[first : first + 2]) for a, b in way]
+        for first in range(0, len(ways), 2)
+    ]
 
 
 def pack_into(block_ref, start, rows, ids):
@@ -203,11 +210,7 @@
     shapes = [(2 * rows, width + LANES), (2 * rows * width // LANES + TAIL, LANES)]
     both, line = pack(pair_kernel, [own, ids, swap(embeddings), swap(ids)], shapes)
 
-    routes = [ring_pairs(length, shift) for shift in range(1, length // 2 + 1)]
-    trips = []
-    for first in range(0, len(routes), 2):
-        ways = enumerate(routes[first : first + 2][::-1])
-        trips.append([(2 * a + way, 2 * b + way) for way, route in ways for a, b in route])
+    trips = line_trips(length)
     visitors = [lax.ppermute(line, line_axes, trip) for trip in trips]
 
     partners = [(s, s + 1) for s in range(1, groups - 1, 2)]

time: 55.2 us -> 56.7 us (1.027)
  starting transfers between devices: 16.9 us -> 17.9 us
  waiting for transfers between devices: 30.7 us -> 31.3 us
    ppermute x7, starting transfers between devices: 1.81 us -> 4.27 us  [swap(): return lax.ppermute(block, 'core', flip(2, 1))]
    ppermute x1, starting transfers between devices: 4.58 us -> 3.57 us  [local(): visitors = [lax.ppermute(line, line_axes, trip) for trip in trips]]
    ppermute x1, waiting for transfers between devices: 14.3 us -> 15.3 us  [local(): lax.ppermute(both, plane_axes, group_trip(groups, *way))]
where the time goes in v22:
time: 56.7 us; the launch traced here: 56.5 us
  waiting for transfers between devices  31.3 us (55%)
  starting transfers between devices  17.9 us (32%)
  Pallas kernels  4.83 us (9%)
  local copies, waits for them, and re-layouts  1.7 us (3%)
  other arithmetic  0.7 us (1%)
    ppermute x1, waiting for transfers between devices, local(): lax.ppermute(both, plane_axes, group_trip(groups, *way))  15.3 us
    ppermute x2, waiting for transfers between devices, local(): corner = [lax.ppermute(part, plane_axes, relay) for part in corner]  10.2 us
    ppermute x7, starting transfers between devices, swap(): return lax.ppermute(block, 'core', flip(2, 1))  4.27 us
    pallas_call x2, Pallas kernels, call(): pl.pallas_call(kernel, in_specs=[VMEM] * len(operands), out_specs=[VMEM]...  3.86 us
    ppermute x1, starting transfers between devices, local(): visitors = [lax.ppermute(line, line_axes, trip) for trip in trips]  3.57 us
    ppermute x1, starting transfers between devices, local(): lax.ppermute(both, plane_axes, group_trip(groups, *way))  3 us
    ppermute x1, waiting for transfers between devices, local(): visitors = [lax.ppermute(line, line_axes, trip) for trip in trips]  2.66 us
    ppermute x7, waiting for transfers between devices, swap(): return lax.ppermute(block, 'core', flip(2, 1))  2.57 us
  transfers between devices with their start and end apart: 15, of which 7 were waited for; matrix products, arithmetic and copies ran while one was open for 1% of the time, Pallas kernels for 4%

profile of v22, /device:TPU:0, one launch (start us, length us, event | category | flops | bytes accessed | tf_op | source)
XLA Modules:
  0.0 56.5 jit_solution(5256608175070440996)
XLA Ops:
  0.0 0.5 collective-permute-start
  0.5 0.7 %pad_add_fusion.ids_ref.own_ids_ref = s32[2,96]{1,0:T(2,128)S(1)} fusion(s32[1,96]{1,0:T(1,128)} %bitcast.4, s32[1,96]{1,0:T(1,128)} %bitcast.5), kind=kLoop, calls=%fused_computation | loop fusion | flops 192 | bytes 1536 | tf_op jit(solution)/shard_map/stack | solution.py:208
  1.2 1.1 %copy-done = bf16[96,4096]{1,0:T(8,128)(2,1)S(1)} copy-done((bf16[96,4096]{1,0:T(8,128)(2,1)S(1)}, bf16[96,4096]{1,0:T(8,128)(2,1)}, u32[]{:S(2)}) %copy-start) | copy-done | bytes 786456
  2.3 0.3 shard_map.37.own_ref.refs_0_
  2.6 0.7 %shard_map.38 = (bf16[192,4224]{1,0:T(8,128)(2,1)S(1)}, bf16[6160,128]{1,0:T(8,128)(2,1)S(1)}) custom-call(bf16[96,4224]{1,0:T(8,128)(2,1)S(1)} %shard_map.37.own_ref.refs_0_, s32[2,96]{1,0:T(2,128)S(1)} %pad_add_fusion.ids_ref.own_ids_ref, bf16[96,4096]{1,0:T(8,128)(2,1)S(1)} %collective-permute-done.rows_ref, s32[2,96]{1,0:T(2,128)S(1)} %collective-permute-done.1.ids_ref), custom_call_target="tpu_custom_call" | custom-call | flops 1572864 | bytes 1572864 | tf_op jit(solution)/shard_map/pallas_call | solution.py:84
  3.3 3.0 %collective-permute-start.2 = (bf16[192,4224]{1,0:T(8,128)(2,1)S(1)}, bf16[192,4224]{1,0:T(8,128)(2,1)S(1)}, u32[]{:S(2)}, u32[]{:S(2)}) collective-permute-start(bf16[192,4224]{1,0:T(8,128)(2,1)S(1)} %get-tuple-element.10.refs_1_), channel_id=1, source_target_pairs={{0,8},{1,17},{8,0},{9,25},{16,24},{17,1},{24,16},{25,9},{2,10},{3,... | collective-permute-start | bytes 4866056 | tf_op jit(solution)/shard_map/ppermute | solution.py:217
  6.3 3.6 %collective-permute-start.8 = (bf16[6160,128]{1,0:T(8,128)(2,1)S(1)}, bf16[6160,128]{1,0:T(8,128)(2,1)S(1)}, u32[]{:S(2)}, u32[]{:S(2)}) collective-permute-start(bf16[6160,128]{1,0:T(8,128)(2,1)S(1)} %get-tuple-element.11), channel_id=1, source_target_pairs={{0,2},{2,4},{4,6},{5,1},{7,3},{1,7},{8,10},{10,12},{12,14},{13,9},... | collective-permute-start | bytes 4730888 | tf_op jit(solution)/shard_map/ppermute | solution.py:214
  9.9 15.3 %collective-permute-done.2.refs_2_ = bf16[192,4224]{1,0:T(8,128)(2,1)S(1)} collective-permute-done((bf16[192,4224]{1,0:T(8,128)(2,1)S(1)}, bf16[192,4224]{1,0:T(8,128)(2,1)S(1)}, u32[]{:S(2)}, u32[]{:S(2)}) %collective-permute-start.2) | collective-permute-done | bytes 1622048 | tf_op jit(solution)/shard_map/ppermute | solution.py:217
  25.3 2.1 %collective-permute-start.4 = (bf16[48,4224]{1,0:T(8,128)(2,1)S(1)}, bf16[48,4224]{1,0:T(8,128)(2,1)S(1)}, u32[]{:S(2)}, u32[]{:S(2)}) collective-permute-start(bf16[48,4224]{1,0:T(8,128)(2,1)S(1)} %get-tuple-element.16), channel_id=1, source_target_pairs={{0,16},{1,9},{8,24},{9,1},{16,0},{17,25},{24,8},{25,17},{2,18},{3,... | collective-permute-start | bytes 1216520 | tf_op jit(solution)/shard_map/ppermute | solution.py:222
  27.5 5.8 %collective-permute-done.4.refs_4_ = bf16[48,4224]{1,0:T(8,128)(2,1)S(1)} collective-permute-done((bf16[48,4224]{1,0:T(8,128)(2,1)S(1)}, bf16[48,4224]{1,0:T(8,128)(2,1)S(1)}, u32[]{:S(2)}, u32[]{:S(2)}) %collective-permute-start.4) | collective-permute-done | bytes 405536 | tf_op jit(solution)/shard_map/ppermute | solution.py:222
  33.3 4.3 %collective-permute-done.5.refs_5_ = bf16[48,4224]{1,0:T(8,128)(2,1)S(1)} collective-permute-done((bf16[48,4224]{1,0:T(8,128)(2,1)S(1)}, bf16[48,4224]{1,0:T(8,128)(2,1)S(1)}, u32[]{:S(2)}, u32[]{:S(2)}) %collective-permute-start.5) | collective-permute-done | bytes 405536 | tf_op jit(solution)/shard_map/ppermute | solution.py:222
  37.7 1.7 %collective-permute-done.7.refs_7_ = bf16[48,4224]{1,0:T(8,128)(2,1)S(1)} collective-permute-done((bf16[48,4224]{1,0:T(8,128)(2,1)S(1)}, bf16[48,4224]{1,0:T(8,128)(2,1)S(1)}, u32[]{:S(2)}, u32[]{:S(2)}) %collective-permute-start.7) | collective-permute-done | bytes 405536 | tf_op jit(solution)/shard_map/ppermute | solution.py:28
  39.4 1.8 %shard_map.39.refs_8_ = f32[1,128]{1,0:T(1,128)S(1)} custom-call(bf16[96,4224]{1,0:T(8,128)(2,1)S(1)} %shard_map.37.own_ref.refs_0_, bf16[192,4224]{1,0:T(8,128)(2,1)S(1)} %get-tuple-element.10.refs_1_, bf16[192,4224]{1,0:T(8,128)(2,1)S(1)} %collective-permute-done.2.refs_2_, bf16[192,4224]{1,0:T(8,128)(2,1)S(1)} %collective-permute-done.3.refs_3_, ...), custom_call_target="tpu_custom_call" | custom-call | flops 805306368 | bytes 7340032 | tf_op jit(solution)/shard_map/pallas_call | solution.py:184
  41.2 2.7 %collective-permute-done.8.refs_0_ = bf16[6160,128]{1,0:T(8,128)(2,1)S(1)} collective-permute-done((bf16[6160,128]{1,0:T(8,128)(2,1)S(1)}, bf16[6160,128]{1,0:T(8,128)(2,1)S(1)}, u32[]{:S(2)}, u32[]{:S(2)}) %collective-permute-start.8) | collective-permute-done | bytes 1576992 | tf_op jit(solution)/shard_map/ppermute | solution.py:214
  43.9 2.1 %shard_map.40 = (f32[2,128]{1,0:T(2,128)S(1)}, f32[4,128]{1,0:T(4,128)S(1)}, f32[4,128]{1,0:T(4,128)S(1)}) custom-call(bf16[6160,128]{1,0:T(8,128)(2,1)S(1)} %collective-permute-done.8.refs_0_, bf16[192,4224]{1,0:T(8,128)(2,1)S(1)} %get-tuple-element.10.refs_1_, bf16[192,4224]{1,0:T(8,128)(2,1)S(1)} %collective-permute-done.2.refs_2_, ...), custom_call_target="tpu_custom_call" | custom-call | flops 1610612736 | bytes 8388608 | tf_op jit(solution)/shard_map/pallas_call | solution.py:184
  45.9 1.2 %collective-permute-start.11 = (f32[4,128]{1,0:T(4,128)S(1)}, f32[4,128]{1,0:T(4,128)S(1)}, u32[]{:S(2)}, u32[]{:S(2)}) collective-permute-start(f32[4,128]{1,0:T(4,128)S(1)} %get-tuple-element.14), channel_id=1, source_target_pairs={{0,1},{1,0},{2,3},{3,2},{4,5},{5,4},{6,7},{7,6},{8,9},{9,8},{10,11... | collective-permute-start | bytes 6152 | tf_op jit(solution)/shard_map/ppermute | solution.py:28
  47.2 1.3 %collective-permute-start.9 = (f32[2,128]{1,0:T(2,128)S(1)}, f32[2,128]{1,0:T(2,128)S(1)}, u32[]{:S(2)}, u32[]{:S(2)}) collective-permute-start(f32[2,128]{1,0:T(2,128)S(1)} %get-tuple-element.12), channel_id=1, source_target_pairs={{2,0},{4,2},{6,4},{1,5},{3,7},{7,1},{10,8},{12,10},{14,12},{9,13},... | collective-permute-start | bytes 3080 | tf_op jit(solution)/shard_map/ppermute | solution.py:241
  48.5 1.5 %collective-permute-start.14 = (f32[4,128]{1,0:T(4,128)S(1)}, f32[4,128]{1,0:T(4,128)S(1)}, u32[]{:S(2)}, u32[]{:S(2)}) collective-permute-start(f32[4,128]{1,0:T(4,128)S(1)} %max.23), channel_id=1, source_target_pairs={{0,24},{8,16},{16,8},{24,0},{1,25},{9,17},{17,9},{25,1},{2,26},{10... | collective-permute-start | bytes 6152 | tf_op jit(solution)/shard_map/ppermute | solution.py:251
  50.0 1.0 %collective-permute-start.13 = (f32[4,128]{1,0:T(4,128)S(1)}, f32[4,128]{1,0:T(4,128)S(1)}, u32[]{:S(2)}, u32[]{:S(2)}) collective-permute-start(f32[4,128]{1,0:T(4,128)S(1)} %max.23), channel_id=1, source_target_pairs={{0,8},{1,17},{8,0},{9,25},{16,24},{17,1},{24,16},{25,9},{2,10},{3,... | collective-permute-start | bytes 6152 | tf_op jit(solution)/shard_map/ppermute | solution.py:249
  51.0 1.1 %collective-permute-start.12 = (f32[4,128]{1,0:T(4,128)S(1)}, f32[4,128]{1,0:T(4,128)S(1)}, u32[]{:S(2)}, u32[]{:S(2)}) collective-permute-start(f32[4,128]{1,0:T(4,128)S(1)} %max.23), channel_id=1, source_target_pairs={{0,16},{1,9},{8,24},{9,1},{16,0},{17,25},{24,8},{25,17},{2,18},{3,... | collective-permute-start | bytes 6152 | tf_op jit(solution)/shard_map/ppermute | solution.py:249
  52.0 0.6 %collective-permute-done.9 = f32[2,128]{1,0:T(2,128)S(1)} collective-permute-done((f32[2,128]{1,0:T(2,128)S(1)}, f32[2,128]{1,0:T(2,128)S(1)}, u32[]{:S(2)}, u32[]{:S(2)}) %collective-permute-start.9) | collective-permute-done | bytes 1056 | tf_op jit(solution)/shard_map/ppermute | solution.py:241
  52.6 2.5 %collective-permute-start.10 = (f32[2,128]{1,0:T(2,128)S(1)}, f32[2,128]{1,0:T(2,128)S(1)}, u32[]{:S(2)}, u32[]{:S(2)}) collective-permute-start(f32[2,128]{1,0:T(2,128)S(1)} %collective-permute-done.9), channel_id=1, source_target_pairs={{0,1},{1,0},{2,3},{3,2},{4,5},{5,4},{6,7},{7,6},{8,9},{9,8},{10,11... | collective-permute-start | bytes 3080 | tf_op jit(solution)/shard_map/ppermute | solution.py:28
  55.1 0.8 %collective-permute-done.10 = f32[2,128]{1,0:T(2,128)S(1)} collective-permute-done((f32[2,128]{1,0:T(2,128)S(1)}, f32[2,128]{1,0:T(2,128)S(1)}, u32[]{:S(2)}, u32[]{:S(2)}) %collective-permute-start.10) | collective-permute-done | bytes 1056 | tf_op jit(solution)/shard_map/ppermute | solution.py:28
  56.0 0.5 slice_bitcast_fusion
  (17 shorter events, 0.2 us)
Async XLA Ops:
  0.0 2.6 %collective-permute-start = (bf16[96,4096]{1,0:T(8,128)(2,1)}, bf16[96,4096]{1,0:T(8,128)(2,1)S(1)}, u32[]{:S(2)}, u32[]{:S(2)}) collective-permute-start(bf16[96,4096]{1,0:T(8,128)(2,1)} %rows_ref.1), channel_id=1, source_target_pairs={{0,1},{1,0},{2,3},{3,2},{4,5},{5,4},{6,7},{7,6},{8,9},{9,8},{10,11... | collective-permute-start | bytes 2359304 | tf_op jit(solution)/shard_map/ppermute | solution.py:28
  1.1 1.5 %collective-permute-start.1 = (s32[2,96]{1,0:T(2,128)S(1)}, s32[2,96]{1,0:T(2,128)S(1)}, u32[]{:S(2)}, u32[]{:S(2)}) collective-permute-start(s32[2,96]{1,0:T(2,128)S(1)} %pad_add_fusion.ids_ref.own_ids_ref), channel_id=1, source_target_pairs={{0,1},{1,0},{2,3},{3,2},{4,5},{5,4},{6,7},{7,6},{8,9},{9,8},{10,11... | collective-permute-start | bytes 2312 | tf_op jit(solution)/shard_map/ppermute | solution.py:28
  1.2 1.1 %copy-start = (bf16[96,4096]{1,0:T(8,128)(2,1)S(1)}, bf16[96,4096]{1,0:T(8,128)(2,1)}, u32[]{:S(2)}) copy-start(bf16[96,4096]{1,0:T(8,128)(2,1)} %rows_ref.1) | copy-start | bytes 2359300
  3.3 21.9 %collective-permute-start.2 = (bf16[192,4224]{1,0:T(8,128)(2,1)S(1)}, bf16[192,4224]{1,0:T(8,128)(2,1)S(1)}, u32[]{:S(2)}, u32[]{:S(2)}) collective-permute-start(bf16[192,4224]{1,0:T(8,128)(2,1)S(1)} %get-tuple-element.10.refs_1_), channel_id=1, source_target_pairs={{0,8},{1,17},{8,0},{9,25},{16,24},{17,1},{24,16},{25,9},{2,10},{3,... | collective-permute-start | bytes 4866056 | tf_op jit(solution)/shard_map/ppermute | solution.py:217
  6.3 37.5 %collective-permute-start.8 = (bf16[6160,128]{1,0:T(8,128)(2,1)S(1)}, bf16[6160,128]{1,0:T(8,128)(2,1)S(1)}, u32[]{:S(2)}, u32[]{:S(2)}) collective-permute-start(bf16[6160,128]{1,0:T(8,128)(2,1)S(1)} %get-tuple-element.11), channel_id=1, source_target_pairs={{0,2},{2,4},{4,6},{5,1},{7,3},{1,7},{8,10},{10,12},{12,14},{13,9},... | collective-permute-start | bytes 4730888 | tf_op jit(solution)/shard_map/ppermute | solution.py:214
  25.3 14.2 %collective-permute-start.3 = (bf16[192,4224]{1,0:T(8,128)(2,1)S(1)}, bf16[192,4224]{1,0:T(8,128)(2,1)S(1)}, u32[]{:S(2)}, u32[]{:S(2)}) collective-permute-start(bf16[192,4224]{1,0:T(8,128)(2,1)S(1)} %collective-permute-done.2.refs_2_), channel_id=1, source_target_pairs={{0,1},{1,0},{2,3},{3,2},{4,5},{5,4},{6,7},{7,6},{8,9},{9,8},{10,11... | collective-permute-start | bytes 4866056 | tf_op jit(solution)/shard_map/ppermute | solution.py:28
  25.3 8.0 %collective-permute-start.4 = (bf16[48,4224]{1,0:T(8,128)(2,1)S(1)}, bf16[48,4224]{1,0:T(8,128)(2,1)S(1)}, u32[]{:S(2)}, u32[]{:S(2)}) collective-permute-start(bf16[48,4224]{1,0:T(8,128)(2,1)S(1)} %get-tuple-element.16), channel_id=1, source_target_pairs={{0,16},{1,9},{8,24},{9,1},{16,0},{17,25},{24,8},{25,17},{2,18},{3,... | collective-permute-start | bytes 1216520 | tf_op jit(solution)/shard_map/ppermute | solution.py:222
  27.4 10.2 %collective-permute-start.5 = (bf16[48,4224]{1,0:T(8,128)(2,1)S(1)}, bf16[48,4224]{1,0:T(8,128)(2,1)S(1)}, u32[]{:S(2)}, u32[]{:S(2)}) collective-permute-start(bf16[48,4224]{1,0:T(8,128)(2,1)S(1)} %get-tuple-element.15), channel_id=1, source_target_pairs={{0,16},{1,9},{8,24},{9,1},{16,0},{17,25},{24,8},{25,17},{2,18},{3,... | collective-permute-start | bytes 1216520 | tf_op jit(solution)/shard_map/ppermute | solution.py:222
  33.3 4.4 %collective-permute-start.6 = (bf16[48,4224]{1,0:T(8,128)(2,1)S(1)}, bf16[48,4224]{1,0:T(8,128)(2,1)S(1)}, u32[]{:S(2)}, u32[]{:S(2)}) collective-permute-start(bf16[48,4224]{1,0:T(8,128)(2,1)S(1)} %collective-permute-done.4.refs_4_), channel_id=1, source_target_pairs={{0,1},{1,0},{2,3},{3,2},{4,5},{5,4},{6,7},{7,6},{8,9},{9,8},{10,11... | collective-permute-start | bytes 1216520 | tf_op jit(solution)/shard_map/ppermute | solution.py:28
  37.7 1.7 %collective-permute-start.7 = (bf16[48,4224]{1,0:T(8,128)(2,1)S(1)}, bf16[48,4224]{1,0:T(8,128)(2,1)S(1)}, u32[]{:S(2)}, u32[]{:S(2)}) collective-permute-start(bf16[48,4224]{1,0:T(8,128)(2,1)S(1)} %collective-permute-done.5.refs_5_), channel_id=1, source_target_pairs={{0,1},{1,0},{2,3},{3,2},{4,5},{5,4},{6,7},{7,6},{8,9},{9,8},{10,11... | collective-permute-start | bytes 1216520 | tf_op jit(solution)/shard_map/ppermute | solution.py:28
  45.9 2.5 %collective-permute-start.11 = (f32[4,128]{1,0:T(4,128)S(1)}, f32[4,128]{1,0:T(4,128)S(1)}, u32[]{:S(2)}, u32[]{:S(2)}) collective-permute-start(f32[4,128]{1,0:T(4,128)S(1)} %get-tuple-element.14), channel_id=1, source_target_pairs={{0,1},{1,0},{2,3},{3,2},{4,5},{5,4},{6,7},{7,6},{8,9},{9,8},{10,11... | collective-permute-start | bytes 6152 | tf_op jit(solution)/shard_map/ppermute | solution.py:28
  47.2 5.5 %collective-permute-start.9 = (f32[2,128]{1,0:T(2,128)S(1)}, f32[2,128]{1,0:T(2,128)S(1)}, u32[]{:S(2)}, u32[]{:S(2)}) collective-permute-start(f32[2,128]{1,0:T(2,128)S(1)} %get-tuple-element.12), channel_id=1, source_target_pairs={{2,0},{4,2},{6,4},{1,5},{3,7},{7,1},{10,8},{12,10},{14,12},{9,13},... | collective-permute-start | bytes 3080 | tf_op jit(solution)/shard_map/ppermute | solution.py:241
  48.5 7.5 %collective-permute-start.14 = (f32[4,128]{1,0:T(4,128)S(1)}, f32[4,128]{1,0:T(4,128)S(1)}, u32[]{:S(2)}, u32[]{:S(2)}) collective-permute-start(f32[4,128]{1,0:T(4,128)S(1)} %max.23), channel_id=1, source_target_pairs={{0,24},{8,16},{16,8},{24,0},{1,25},{9,17},{17,9},{25,1},{2,26},{10... | collective-permute-start | bytes 6152 | tf_op jit(solution)/shard_map/ppermute | solution.py:251
  50.0 6.0 %collective-permute-start.13 = (f32[4,128]{1,0:T(4,128)S(1)}, f32[4,128]{1,0:T(4,128)S(1)}, u32[]{:S(2)}, u32[]{:S(2)}) collective-permute-start(f32[4,128]{1,0:T(4,128)S(1)} %max.23), channel_id=1, source_target_pairs={{0,8},{1,17},{8,0},{9,25},{16,24},{17,1},{24,16},{25,9},{2,10},{3,... | collective-permute-start | bytes 6152 | tf_op jit(solution)/shard_map/ppermute | solution.py:249
  51.0 5.0 %collective-permute-start.12 = (f32[4,128]{1,0:T(4,128)S(1)}, f32[4,128]{1,0:T(4,128)S(1)}, u32[]{:S(2)}, u32[]{:S(2)}) collective-permute-start(f32[4,128]{1,0:T(4,128)S(1)} %max.23), channel_id=1, source_target_pairs={{0,16},{1,9},{8,24},{9,1},{16,0},{17,25},{24,8},{25,17},{2,18},{3,... | collective-permute-start | bytes 6152 | tf_op jit(solution)/shard_map/ppermute | solution.py:249
  52.6 3.3 %collective-permute-start.10 = (f32[2,128]{1,0:T(2,128)S(1)}, f32[2,128]{1,0:T(2,128)S(1)}, u32[]{:S(2)}, u32[]{:S(2)}) collective-permute-start(f32[2,128]{1,0:T(2,128)S(1)} %collective-permute-done.9), channel_id=1, source_target_pairs={{0,1},{1,0},{2,3},{3,2},{4,5},{5,4},{6,7},{7,6},{8,9},{9,8},{10,11... | collective-permute-start | bytes 3080 | tf_op jit(solution)/shard_map/ppermute | solution.py:28

commit v23 on v20

--- a/solution.py
+++ b/solution.py
@@ -26,7 +26,7 @@
 
 def ring_pairs(length, shift):
     if 2 * shift < length:
-        return [(k, (k + shift) % length) for k in range(length)]
+        return [((k + shift) % length, k) for k in range(length)]
     pairs = [(k, k + shift) for k in range(length // 2)]
     return [pair[:: 1 - 2 * (pair[0] % 2)] for pair in pairs]
 

time: 55.2 us -> 57.3 us (1.038)
  the two profiles are of different devices: /device:TPU:0 before, /device:TPU:12 now
where the time goes in v23:
time: 57.3 us; the launch traced here: 57.1 us
  waiting for transfers between devices  36.3 us (63%)
  starting transfers between devices  13.4 us (23%)
  Pallas kernels  4.83 us (8%)
  local copies, waits for them, and re-layouts  1.7 us (3%)
  other arithmetic  0.7 us (1%)
    ppermute x1, waiting for transfers between devices, local(): lax.ppermute(both, plane_axes, group_trip(groups, *way))  18.2 us
    ppermute x2, waiting for transfers between devices, local(): corner = [lax.ppermute(part, plane_axes, relay) for part in corner]  10.2 us
    pallas_call x2, Pallas kernels, call(): pl.pallas_call(kernel, in_specs=[VMEM] * len(operands), out_specs=[VMEM]...  3.85 us
    ppermute x1, starting transfers between devices, local(): back = lax.ppermute(part, line_axes, [(b, a) for a, b in trip])  3.83 us
    ppermute x1, starting transfers between devices, local(): bests.append(lax.ppermute(merged[0], 'group', flip(groups, last))[2:3])  3 us
    ppermute x7, waiting for transfers between devices, swap(): return lax.ppermute(block, 'core', flip(2, 1))  2.85 us
    ppermute x1, waiting for transfers between devices, local(): visitors = [lax.ppermute(line, line_axes, trip) for trip in trips]  2.65 us
    ppermute x2, waiting for transfers between devices, local(): got = lax.ppermute(merged[chunk], plane_axes, group_trip(groups, *order))  2.43 us
  transfers between devices with their start and end apart: 15, of which 8 were waited for; matrix products, arithmetic and copies ran while one was open for 1% of the time, Pallas kernels for 4%

profile of v23, /device:TPU:12, one launch (start us, length us, event | category | flops | bytes accessed | tf_op | source)
XLA Modules:
  0.0 57.1 jit_solution(15607352516171670664)
XLA Ops:
  0.0 0.7 %pad_add_fusion.ids_ref.own_ids_ref = s32[2,96]{1,0:T(2,128)S(1)} fusion(s32[1,96]{1,0:T(1,128)} %bitcast.4, s32[1,96]{1,0:T(1,128)} %bitcast.5), kind=kLoop, calls=%fused_computation | loop fusion | flops 192 | bytes 1536 | tf_op jit(solution)/shard_map/stack | solution.py:201
  0.7 0.5 collective-permute-start.1
  1.2 1.1 %copy-done = bf16[96,4096]{1,0:T(8,128)(2,1)S(1)} copy-done((bf16[96,4096]{1,0:T(8,128)(2,1)S(1)}, bf16[96,4096]{1,0:T(8,128)(2,1)}, u32[]{:S(2)}) %copy-start) | copy-done | bytes 786456
  2.3 0.3 shard_map.37.own_ref.refs_0_
  2.6 0.7 %shard_map.38 = (bf16[192,4224]{1,0:T(8,128)(2,1)S(1)}, bf16[6160,128]{1,0:T(8,128)(2,1)S(1)}) custom-call(bf16[96,4224]{1,0:T(8,128)(2,1)S(1)} %shard_map.37.own_ref.refs_0_, s32[2,96]{1,0:T(2,128)S(1)} %pad_add_fusion.ids_ref.own_ids_ref, bf16[96,4096]{1,0:T(8,128)(2,1)S(1)} %collective-permute-done.rows_ref, s32[2,96]{1,0:T(2,128)S(1)} %collective-permute-done.1.ids_ref), custom_call_target="tpu_custom_call" | custom-call | flops 1572864 | bytes 1572864 | tf_op jit(solution)/shard_map/pallas_call | solution.py:77
  3.3 1.6 %collective-permute-start.2 = (bf16[192,4224]{1,0:T(8,128)(2,1)S(1)}, bf16[192,4224]{1,0:T(8,128)(2,1)S(1)}, u32[]{:S(2)}, u32[]{:S(2)}) collective-permute-start(bf16[192,4224]{1,0:T(8,128)(2,1)S(1)} %get-tuple-element.10.refs_1_), channel_id=1, source_target_pairs={{0,8},{1,17},{8,0},{9,25},{16,24},{17,1},{24,16},{25,9},{2,10},{3,... | collective-permute-start | bytes 4866056 | tf_op jit(solution)/shard_map/ppermute | solution.py:214
  4.9 1.3 %collective-permute-start.8 = (bf16[6160,128]{1,0:T(8,128)(2,1)S(1)}, bf16[6160,128]{1,0:T(8,128)(2,1)S(1)}, u32[]{:S(2)}, u32[]{:S(2)}) collective-permute-start(bf16[6160,128]{1,0:T(8,128)(2,1)S(1)} %get-tuple-element.11), channel_id=1, source_target_pairs={{0,4},{6,2},{3,1},{5,3},{7,5},{1,7},{8,12},{14,10},{11,9},{13,11},... | collective-permute-start | bytes 4730888 | tf_op jit(solution)/shard_map/ppermute | solution.py:211
  6.2 18.2 %collective-permute-done.2.refs_2_ = bf16[192,4224]{1,0:T(8,128)(2,1)S(1)} collective-permute-done((bf16[192,4224]{1,0:T(8,128)(2,1)S(1)}, bf16[192,4224]{1,0:T(8,128)(2,1)S(1)}, u32[]{:S(2)}, u32[]{:S(2)}) %collective-permute-start.2) | collective-permute-done | bytes 1622048 | tf_op jit(solution)/shard_map/ppermute | solution.py:214
  24.3 0.1 fusion.3
  24.4 0.6 %collective-permute-start.4 = (bf16[48,4224]{1,0:T(8,128)(2,1)S(1)}, bf16[48,4224]{1,0:T(8,128)(2,1)S(1)}, u32[]{:S(2)}, u32[]{:S(2)}) collective-permute-start(bf16[48,4224]{1,0:T(8,128)(2,1)S(1)} %get-tuple-element.16), channel_id=1, source_target_pairs={{0,16},{1,9},{8,24},{9,1},{16,0},{17,25},{24,8},{25,17},{2,18},{3,... | collective-permute-start | bytes 1216520 | tf_op jit(solution)/shard_map/ppermute | solution.py:219
  25.0 1.5 %collective-permute-start.5 = (bf16[48,4224]{1,0:T(8,128)(2,1)S(1)}, bf16[48,4224]{1,0:T(8,128)(2,1)S(1)}, u32[]{:S(2)}, u32[]{:S(2)}) collective-permute-start(bf16[48,4224]{1,0:T(8,128)(2,1)S(1)} %get-tuple-element.15), channel_id=1, source_target_pairs={{0,16},{1,9},{8,24},{9,1},{16,0},{17,25},{24,8},{25,17},{2,18},{3,... | collective-permute-start | bytes 1216520 | tf_op jit(solution)/shard_map/ppermute | solution.py:219
  26.5 5.9 %collective-permute-done.4.refs_4_ = bf16[48,4224]{1,0:T(8,128)(2,1)S(1)} collective-permute-done((bf16[48,4224]{1,0:T(8,128)(2,1)S(1)}, bf16[48,4224]{1,0:T(8,128)(2,1)S(1)}, u32[]{:S(2)}, u32[]{:S(2)}) %collective-permute-start.4) | collective-permute-done | bytes 405536 | tf_op jit(solution)/shard_map/ppermute | solution.py:219
  32.4 4.3 %collective-permute-done.5.refs_5_ = bf16[48,4224]{1,0:T(8,128)(2,1)S(1)} collective-permute-done((bf16[48,4224]{1,0:T(8,128)(2,1)S(1)}, bf16[48,4224]{1,0:T(8,128)(2,1)S(1)}, u32[]{:S(2)}, u32[]{:S(2)}) %collective-permute-start.5) | collective-permute-done | bytes 405536 | tf_op jit(solution)/shard_map/ppermute | solution.py:219
  36.7 1.7 %collective-permute-done.7.refs_7_ = bf16[48,4224]{1,0:T(8,128)(2,1)S(1)} collective-permute-done((bf16[48,4224]{1,0:T(8,128)(2,1)S(1)}, bf16[48,4224]{1,0:T(8,128)(2,1)S(1)}, u32[]{:S(2)}, u32[]{:S(2)}) %collective-permute-start.7) | collective-permute-done | bytes 405536 | tf_op jit(solution)/shard_map/ppermute | solution.py:35
  38.5 1.8 %shard_map.39.refs_8_ = f32[1,128]{1,0:T(1,128)S(1)} custom-call(bf16[96,4224]{1,0:T(8,128)(2,1)S(1)} %shard_map.37.own_ref.refs_0_, bf16[192,4224]{1,0:T(8,128)(2,1)S(1)} %get-tuple-element.10.refs_1_, bf16[192,4224]{1,0:T(8,128)(2,1)S(1)} %collective-permute-done.2.refs_2_, bf16[192,4224]{1,0:T(8,128)(2,1)S(1)} %collective-permute-done.3.refs_3_, ...), custom_call_target="tpu_custom_call" | custom-call | flops 805306368 | bytes 7340032 | tf_op jit(solution)/shard_map/pallas_call | solution.py:177
  40.3 2.6 %collective-permute-done.8.refs_0_ = bf16[6160,128]{1,0:T(8,128)(2,1)S(1)} collective-permute-done((bf16[6160,128]{1,0:T(8,128)(2,1)S(1)}, bf16[6160,128]{1,0:T(8,128)(2,1)S(1)}, u32[]{:S(2)}, u32[]{:S(2)}) %collective-permute-start.8) | collective-permute-done | bytes 1576992 | tf_op jit(solution)/shard_map/ppermute | solution.py:211
  42.9 2.1 %shard_map.40 = (f32[2,128]{1,0:T(2,128)S(1)}, f32[4,128]{1,0:T(4,128)S(1)}, f32[4,128]{1,0:T(4,128)S(1)}) custom-call(bf16[6160,128]{1,0:T(8,128)(2,1)S(1)} %collective-permute-done.8.refs_0_, bf16[192,4224]{1,0:T(8,128)(2,1)S(1)} %get-tuple-element.10.refs_1_, bf16[192,4224]{1,0:T(8,128)(2,1)S(1)} %collective-permute-done.2.refs_2_, ...), custom_call_target="tpu_custom_call" | custom-call | flops 1610612736 | bytes 8388608 | tf_op jit(solution)/shard_map/pallas_call | solution.py:177
  45.0 3.8 %collective-permute-start.9 = (f32[2,128]{1,0:T(2,128)S(1)}, f32[2,128]{1,0:T(2,128)S(1)}, u32[]{:S(2)}, u32[]{:S(2)}) collective-permute-start(f32[2,128]{1,0:T(2,128)S(1)} %get-tuple-element.12), channel_id=1, source_target_pairs={{4,0},{2,6},{1,3},{3,5},{5,7},{7,1},{12,8},{10,14},{9,11},{11,13},... | collective-permute-start | bytes 3080 | tf_op jit(solution)/shard_map/ppermute | solution.py:238
  48.9 3.0 %collective-permute-start.14 = (f32[4,128]{1,0:T(4,128)S(1)}, f32[4,128]{1,0:T(4,128)S(1)}, u32[]{:S(2)}, u32[]{:S(2)}) collective-permute-start(f32[4,128]{1,0:T(4,128)S(1)} %max.23), channel_id=1, source_target_pairs={{0,24},{8,16},{16,8},{24,0},{1,25},{9,17},{17,9},{25,1},{2,26},{10... | collective-permute-start | bytes 6152 | tf_op jit(solution)/shard_map/ppermute | solution.py:248
  51.9 1.1 %collective-permute-start.13 = (f32[4,128]{1,0:T(4,128)S(1)}, f32[4,128]{1,0:T(4,128)S(1)}, u32[]{:S(2)}, u32[]{:S(2)}) collective-permute-start(f32[4,128]{1,0:T(4,128)S(1)} %max.23), channel_id=1, source_target_pairs={{0,8},{1,17},{8,0},{9,25},{16,24},{17,1},{24,16},{25,9},{2,10},{3,... | collective-permute-start | bytes 6152 | tf_op jit(solution)/shard_map/ppermute | solution.py:246
  53.0 1.1 %collective-permute-done.10 = f32[2,128]{1,0:T(2,128)S(1)} collective-permute-done((f32[2,128]{1,0:T(2,128)S(1)}, f32[2,128]{1,0:T(2,128)S(1)}, u32[]{:S(2)}, u32[]{:S(2)}) %collective-permute-start.10) | collective-permute-done | bytes 1056 | tf_op jit(solution)/shard_map/ppermute | solution.py:35
  54.1 1.3 %collective-permute-done.13 = f32[4,128]{1,0:T(4,128)S(1)} collective-permute-done((f32[4,128]{1,0:T(4,128)S(1)}, f32[4,128]{1,0:T(4,128)S(1)}, u32[]{:S(2)}, u32[]{:S(2)}) %collective-permute-start.13) | collective-permute-done | bytes 2080 | tf_op jit(solution)/shard_map/ppermute | solution.py:246
  55.5 1.1 %collective-permute-done.12 = f32[4,128]{1,0:T(4,128)S(1)} collective-permute-done((f32[4,128]{1,0:T(4,128)S(1)}, f32[4,128]{1,0:T(4,128)S(1)}, u32[]{:S(2)}, u32[]{:S(2)}) %collective-permute-start.12) | collective-permute-done | bytes 2080 | tf_op jit(solution)/shard_map/ppermute | solution.py:246
  56.6 0.5 slice_bitcast_fusion
  (17 shorter events, 0.1 us)
Async XLA Ops:
  0.0 2.6 %collective-permute-start = (bf16[96,4096]{1,0:T(8,128)(2,1)}, bf16[96,4096]{1,0:T(8,128)(2,1)S(1)}, u32[]{:S(2)}, u32[]{:S(2)}) collective-permute-start(bf16[96,4096]{1,0:T(8,128)(2,1)} %rows_ref.1), channel_id=1, source_target_pairs={{0,1},{1,0},{2,3},{3,2},{4,5},{5,4},{6,7},{7,6},{8,9},{9,8},{10,11... | collective-permute-start | bytes 2359304 | tf_op jit(solution)/shard_map/ppermute | solution.py:35
  0.7 1.9 %collective-permute-start.1 = (s32[2,96]{1,0:T(2,128)S(1)}, s32[2,96]{1,0:T(2,128)S(1)}, u32[]{:S(2)}, u32[]{:S(2)}) collective-permute-start(s32[2,96]{1,0:T(2,128)S(1)} %pad_add_fusion.ids_ref.own_ids_ref), channel_id=1, source_target_pairs={{0,1},{1,0},{2,3},{3,2},{4,5},{5,4},{6,7},{7,6},{8,9},{9,8},{10,11... | collective-permute-start | bytes 2312 | tf_op jit(solution)/shard_map/ppermute | solution.py:35
  1.2 1.1 %copy-start = (bf16[96,4096]{1,0:T(8,128)(2,1)S(1)}, bf16[96,4096]{1,0:T(8,128)(2,1)}, u32[]{:S(2)}) copy-start(bf16[96,4096]{1,0:T(8,128)(2,1)} %rows_ref.1) | copy-start | bytes 2359300
  3.3 21.0 %collective-permute-start.2 = (bf16[192,4224]{1,0:T(8,128)(2,1)S(1)}, bf16[192,4224]{1,0:T(8,128)(2,1)S(1)}, u32[]{:S(2)}, u32[]{:S(2)}) collective-permute-start(bf16[192,4224]{1,0:T(8,128)(2,1)S(1)} %get-tuple-element.10.refs_1_), channel_id=1, source_target_pairs={{0,8},{1,17},{8,0},{9,25},{16,24},{17,1},{24,16},{25,9},{2,10},{3,... | collective-permute-start | bytes 4866056 | tf_op jit(solution)/shard_map/ppermute | solution.py:214
  4.9 38.0 %collective-permute-start.8 = (bf16[6160,128]{1,0:T(8,128)(2,1)S(1)}, bf16[6160,128]{1,0:T(8,128)(2,1)S(1)}, u32[]{:S(2)}, u32[]{:S(2)}) collective-permute-start(bf16[6160,128]{1,0:T(8,128)(2,1)S(1)} %get-tuple-element.11), channel_id=1, source_target_pairs={{0,4},{6,2},{3,1},{5,3},{7,5},{1,7},{8,12},{14,10},{11,9},{13,11},... | collective-permute-start | bytes 4730888 | tf_op jit(solution)/shard_map/ppermute | solution.py:211
  24.3 14.1 %collective-permute-start.3 = (bf16[192,4224]{1,0:T(8,128)(2,1)S(1)}, bf16[192,4224]{1,0:T(8,128)(2,1)S(1)}, u32[]{:S(2)}, u32[]{:S(2)}) collective-permute-start(bf16[192,4224]{1,0:T(8,128)(2,1)S(1)} %collective-permute-done.2.refs_2_), channel_id=1, source_target_pairs={{0,1},{1,0},{2,3},{3,2},{4,5},{5,4},{6,7},{7,6},{8,9},{9,8},{10,11... | collective-permute-start | bytes 4866056 | tf_op jit(solution)/shard_map/ppermute | solution.py:35
  24.4 8.0 %collective-permute-start.4 = (bf16[48,4224]{1,0:T(8,128)(2,1)S(1)}, bf16[48,4224]{1,0:T(8,128)(2,1)S(1)}, u32[]{:S(2)}, u32[]{:S(2)}) collective-permute-start(bf16[48,4224]{1,0:T(8,128)(2,1)S(1)} %get-tuple-element.16), channel_id=1, source_target_pairs={{0,16},{1,9},{8,24},{9,1},{16,0},{17,25},{24,8},{25,17},{2,18},{3,... | collective-permute-start | bytes 1216520 | tf_op jit(solution)/shard_map/ppermute | solution.py:219
  25.0 11.7 %collective-permute-start.5 = (bf16[48,4224]{1,0:T(8,128)(2,1)S(1)}, bf16[48,4224]{1,0:T(8,128)(2,1)S(1)}, u32[]{:S(2)}, u32[]{:S(2)}) collective-permute-start(bf16[48,4224]{1,0:T(8,128)(2,1)S(1)} %get-tuple-element.15), channel_id=1, source_target_pairs={{0,16},{1,9},{8,24},{9,1},{16,0},{17,25},{24,8},{25,17},{2,18},{3,... | collective-permute-start | bytes 1216520 | tf_op jit(solution)/shard_map/ppermute | solution.py:219
  32.4 4.4 %collective-permute-start.6 = (bf16[48,4224]{1,0:T(8,128)(2,1)S(1)}, bf16[48,4224]{1,0:T(8,128)(2,1)S(1)}, u32[]{:S(2)}, u32[]{:S(2)}) collective-permute-start(bf16[48,4224]{1,0:T(8,128)(2,1)S(1)} %collective-permute-done.4.refs_4_), channel_id=1, source_target_pairs={{0,1},{1,0},{2,3},{3,2},{4,5},{5,4},{6,7},{7,6},{8,9},{9,8},{10,11... | collective-permute-start | bytes 1216520 | tf_op jit(solution)/shard_map/ppermute | solution.py:35
  36.7 1.7 %collective-permute-start.7 = (bf16[48,4224]{1,0:T(8,128)(2,1)S(1)}, bf16[48,4224]{1,0:T(8,128)(2,1)S(1)}, u32[]{:S(2)}, u32[]{:S(2)}) collective-permute-start(bf16[48,4224]{1,0:T(8,128)(2,1)S(1)} %collective-permute-done.5.refs_5_), channel_id=1, source_target_pairs={{0,1},{1,0},{2,3},{3,2},{4,5},{5,4},{6,7},{7,6},{8,9},{9,8},{10,11... | collective-permute-start | bytes 1216520 | tf_op jit(solution)/shard_map/ppermute | solution.py:35
  45.0 3.9 %collective-permute-start.11 = (f32[4,128]{1,0:T(4,128)S(1)}, f32[4,128]{1,0:T(4,128)S(1)}, u32[]{:S(2)}, u32[]{:S(2)}) collective-permute-start(f32[4,128]{1,0:T(4,128)S(1)} %get-tuple-element.14), channel_id=1, source_target_pairs={{0,1},{1,0},{2,3},{3,2},{4,5},{5,4},{6,7},{7,6},{8,9},{9,8},{10,11... | collective-permute-start | bytes 6152 | tf_op jit(solution)/shard_map/ppermute | solution.py:35
  45.0 8.0 %collective-permute-start.9 = (f32[2,128]{1,0:T(2,128)S(1)}, f32[2,128]{1,0:T(2,128)S(1)}, u32[]{:S(2)}, u32[]{:S(2)}) collective-permute-start(f32[2,128]{1,0:T(2,128)S(1)} %get-tuple-element.12), channel_id=1, source_target_pairs={{4,0},{2,6},{1,3},{3,5},{5,7},{7,1},{12,8},{10,14},{9,11},{11,13},... | collective-permute-start | bytes 3080 | tf_op jit(solution)/shard_map/ppermute | solution.py:238
  48.9 5.2 %collective-permute-start.14 = (f32[4,128]{1,0:T(4,128)S(1)}, f32[4,128]{1,0:T(4,128)S(1)}, u32[]{:S(2)}, u32[]{:S(2)}) collective-permute-start(f32[4,128]{1,0:T(4,128)S(1)} %max.23), channel_id=1, source_target_pairs={{0,24},{8,16},{16,8},{24,0},{1,25},{9,17},{17,9},{25,1},{2,26},{10... | collective-permute-start | bytes 6152 | tf_op jit(solution)/shard_map/ppermute | solution.py:248
  51.9 3.6 %collective-permute-start.13 = (f32[4,128]{1,0:T(4,128)S(1)}, f32[4,128]{1,0:T(4,128)S(1)}, u32[]{:S(2)}, u32[]{:S(2)}) collective-permute-start(f32[4,128]{1,0:T(4,128)S(1)} %max.23), channel_id=1, source_target_pairs={{0,8},{1,17},{8,0},{9,25},{16,24},{17,1},{24,16},{25,9},{2,10},{3,... | collective-permute-start | bytes 6152 | tf_op jit(solution)/shard_map/ppermute | solution.py:246
  53.0 3.6 %collective-permute-start.12 = (f32[4,128]{1,0:T(4,128)S(1)}, f32[4,128]{1,0:T(4,128)S(1)}, u32[]{:S(2)}, u32[]{:S(2)}) collective-permute-start(f32[4,128]{1,0:T(4,128)S(1)} %max.23), channel_id=1, source_target_pairs={{0,16},{1,9},{8,24},{9,1},{16,0},{17,25},{24,8},{25,17},{2,18},{3,... | collective-permute-start | bytes 6152 | tf_op jit(solution)/shard_map/ppermute | solution.py:246
  53.0 1.1 %collective-permute-start.10 = (f32[2,128]{1,0:T(2,128)S(1)}, f32[2,128]{1,0:T(2,128)S(1)}, u32[]{:S(2)}, u32[]{:S(2)}) collective-permute-start(f32[2,128]{1,0:T(2,128)S(1)} %collective-permute-done.9), channel_id=1, source_target_pairs={{0,1},{1,0},{2,3},{3,2},{4,5},{5,4},{6,7},{7,6},{8,9},{9,8},{10,11... | collective-permute-start | bytes 3080 | tf_op jit(solution)/shard_map/ppermute | solution.py:35

commit v24 on v20

--- a/solution.py
+++ b/solution.py
@@ -242,10 +242,12 @@
     ways = [(0, 0, partners[-1])]
     ways += [(1 + k // 2, 2 * (k % 2), way) for k, way in enumerate(partners[:-1])]
     for chunk, row, (first, second) in ways:
-        for offset, order in ((1, (second, first)), (0, (first, second))):
-            got = lax.ppermute(merged[chunk], plane_axes, group_trip(groups, *order))
-            bests.append(got[row + offset : row + offset + 1])
+        got = lax.ppermute(merged[chunk], plane_axes, group_trip(groups, second, first))
+        bests.append(got[row + 1 : row + 2])
     bests.append(lax.ppermute(merged[0], "group", flip(groups, last))[2:3])
+    for chunk, row, (first, second) in ways:
+        got = lax.ppermute(merged[chunk], plane_axes, group_trip(groups, first, second))
+        bests.append(got[row : row + 1])
     bests.append(merged[0][3:4])
     return functools.reduce(jnp.maximum, bests)[0, :rows]
 

time: 55.2 us -> 55.9 us (1.013)
  waiting for transfers between devices: 30.7 us -> 31.5 us
    ppermute x2, starting transfers between devices: 2.58 us -> 4.09 us  [the longest x1 2.55 us: local(): lax.ppermute(merged[chunk], plane_axes, group_trip(groups, first, second))]
    ppermute x1, starting transfers between devices: 1.43 us -> 0.01 us  [local(): bests.append(lax.ppermute(merged[0], 'group', flip(groups, last))[2:3])]
    ppermute x1, waiting for transfers between devices: 0.01 us -> 0.85 us  [local(): bests.append(lax.ppermute(merged[0], 'group', flip(groups, last))[2:3])]
  transfers between devices with their start and end apart: 15 -> 15, of which waited for: 7 -> 8; matrix products, arithmetic and copies ran while one was open for 1% -> 1% of each run, Pallas kernels for 4% -> 4%
where the time goes in v24:
time: 55.9 us; the launch traced here: 55.7 us
  waiting for transfers between devices  31.5 us (56%)
  starting transfers between devices  17 us (30%)
  Pallas kernels  4.83 us (9%)
  local copies, waits for them, and re-layouts  1.7 us (3%)
  other arithmetic  0.69 us (1%)
    ppermute x1, waiting for transfers between devices, local(): lax.ppermute(both, plane_axes, group_trip(groups, *way))  14.3 us
    ppermute x2, waiting for transfers between devices, local(): corner = [lax.ppermute(part, plane_axes, relay) for part in corner]  10.2 us
    ppermute x1, starting transfers between devices, local(): visitors = [lax.ppermute(line, line_axes, trip) for trip in trips]  4.58 us
    pallas_call x2, Pallas kernels, call(): pl.pallas_call(kernel, in_specs=[VMEM] * len(operands), out_specs=[VMEM]...  3.86 us
    ppermute x1, starting transfers between devices, local(): lax.ppermute(both, plane_axes, group_trip(groups, *way))  3 us
    ppermute x7, waiting for transfers between devices, swap(): return lax.ppermute(block, 'core', flip(2, 1))  2.88 us
    ppermute x1, starting transfers between devices, local(): lax.ppermute(merged[chunk], plane_axes, group_trip(groups, first, second))  2.55 us
    ppermute x1, waiting for transfers between devices, local(): visitors = [lax.ppermute(line, line_axes, trip) for trip in trips]  2.29 us
  transfers between devices with their start and end apart: 15, of which 8 were waited for; matrix products, arithmetic and copies ran while one was open for 1% of the time, Pallas kernels for 4%

profile of v24, /device:TPU:0, one launch (start us, length us, event | category | flops | bytes accessed | tf_op | source)
XLA Modules:
  0.0 55.7 jit_solution(15813797631042534054)
XLA Ops:
  0.0 0.5 collective-permute-start
  0.5 0.7 %pad_add_fusion.ids_ref.own_ids_ref = s32[2,96]{1,0:T(2,128)S(1)} fusion(s32[1,96]{1,0:T(1,128)} %bitcast.4, s32[1,96]{1,0:T(1,128)} %bitcast.5), kind=kLoop, calls=%fused_computation | loop fusion | flops 192 | bytes 1536 | tf_op jit(solution)/shard_map/stack | solution.py:201
  1.2 1.1 %copy-done = bf16[96,4096]{1,0:T(8,128)(2,1)S(1)} copy-done((bf16[96,4096]{1,0:T(8,128)(2,1)S(1)}, bf16[96,4096]{1,0:T(8,128)(2,1)}, u32[]{:S(2)}) %copy-start) | copy-done | bytes 786456
  2.3 0.3 shard_map.37.own_ref.refs_0_
  2.6 0.7 %shard_map.38 = (bf16[192,4224]{1,0:T(8,128)(2,1)S(1)}, bf16[6160,128]{1,0:T(8,128)(2,1)S(1)}) custom-call(bf16[96,4224]{1,0:T(8,128)(2,1)S(1)} %shard_map.37.own_ref.refs_0_, s32[2,96]{1,0:T(2,128)S(1)} %pad_add_fusion.ids_ref.own_ids_ref, bf16[96,4096]{1,0:T(8,128)(2,1)S(1)} %collective-permute-done.rows_ref, s32[2,96]{1,0:T(2,128)S(1)} %collective-permute-done.1.ids_ref), custom_call_target="tpu_custom_call" | custom-call | flops 1572864 | bytes 1572864 | tf_op jit(solution)/shard_map/pallas_call | solution.py:77
  3.3 3.0 %collective-permute-start.2 = (bf16[192,4224]{1,0:T(8,128)(2,1)S(1)}, bf16[192,4224]{1,0:T(8,128)(2,1)S(1)}, u32[]{:S(2)}, u32[]{:S(2)}) collective-permute-start(bf16[192,4224]{1,0:T(8,128)(2,1)S(1)} %get-tuple-element.10.refs_1_), channel_id=1, source_target_pairs={{0,8},{1,17},{8,0},{9,25},{16,24},{17,1},{24,16},{25,9},{2,10},{3,... | collective-permute-start | bytes 4866056 | tf_op jit(solution)/shard_map/ppermute | solution.py:214
  6.3 4.6 %collective-permute-start.8 = (bf16[6160,128]{1,0:T(8,128)(2,1)S(1)}, bf16[6160,128]{1,0:T(8,128)(2,1)S(1)}, u32[]{:S(2)}, u32[]{:S(2)}) collective-permute-start(bf16[6160,128]{1,0:T(8,128)(2,1)S(1)} %get-tuple-element.11), channel_id=1, source_target_pairs={{0,4},{6,2},{1,3},{3,5},{5,7},{7,1},{8,12},{14,10},{9,11},{11,13},... | collective-permute-start | bytes 4730888 | tf_op jit(solution)/shard_map/ppermute | solution.py:211
  10.9 14.3 %collective-permute-done.2.refs_2_ = bf16[192,4224]{1,0:T(8,128)(2,1)S(1)} collective-permute-done((bf16[192,4224]{1,0:T(8,128)(2,1)S(1)}, bf16[192,4224]{1,0:T(8,128)(2,1)S(1)}, u32[]{:S(2)}, u32[]{:S(2)}) %collective-permute-start.2) | collective-permute-done | bytes 1622048 | tf_op jit(solution)/shard_map/ppermute | solution.py:214
  25.3 2.1 %collective-permute-start.4 = (bf16[48,4224]{1,0:T(8,128)(2,1)S(1)}, bf16[48,4224]{1,0:T(8,128)(2,1)S(1)}, u32[]{:S(2)}, u32[]{:S(2)}) collective-permute-start(bf16[48,4224]{1,0:T(8,128)(2,1)S(1)} %get-tuple-element.16), channel_id=1, source_target_pairs={{0,16},{1,9},{8,24},{9,1},{16,0},{17,25},{24,8},{25,17},{2,18},{3,... | collective-permute-start | bytes 1216520 | tf_op jit(solution)/shard_map/ppermute | solution.py:219
  27.4 0.1 collective-permute-start.5
  27.5 5.8 %collective-permute-done.4.refs_4_ = bf16[48,4224]{1,0:T(8,128)(2,1)S(1)} collective-permute-done((bf16[48,4224]{1,0:T(8,128)(2,1)S(1)}, bf16[48,4224]{1,0:T(8,128)(2,1)S(1)}, u32[]{:S(2)}, u32[]{:S(2)}) %collective-permute-start.4) | collective-permute-done | bytes 405536 | tf_op jit(solution)/shard_map/ppermute | solution.py:219
  33.3 4.3 %collective-permute-done.5.refs_5_ = bf16[48,4224]{1,0:T(8,128)(2,1)S(1)} collective-permute-done((bf16[48,4224]{1,0:T(8,128)(2,1)S(1)}, bf16[48,4224]{1,0:T(8,128)(2,1)S(1)}, u32[]{:S(2)}, u32[]{:S(2)}) %collective-permute-start.5) | collective-permute-done | bytes 405536 | tf_op jit(solution)/shard_map/ppermute | solution.py:219
  37.7 1.7 %collective-permute-done.7.refs_7_ = bf16[48,4224]{1,0:T(8,128)(2,1)S(1)} collective-permute-done((bf16[48,4224]{1,0:T(8,128)(2,1)S(1)}, bf16[48,4224]{1,0:T(8,128)(2,1)S(1)}, u32[]{:S(2)}, u32[]{:S(2)}) %collective-permute-start.7) | collective-permute-done | bytes 405536 | tf_op jit(solution)/shard_map/ppermute | solution.py:35
  39.4 1.8 %shard_map.39.refs_8_ = f32[1,128]{1,0:T(1,128)S(1)} custom-call(bf16[96,4224]{1,0:T(8,128)(2,1)S(1)} %shard_map.37.own_ref.refs_0_, bf16[192,4224]{1,0:T(8,128)(2,1)S(1)} %get-tuple-element.10.refs_1_, bf16[192,4224]{1,0:T(8,128)(2,1)S(1)} %collective-permute-done.2.refs_2_, bf16[192,4224]{1,0:T(8,128)(2,1)S(1)} %collective-permute-done.3.refs_3_, ...), custom_call_target="tpu_custom_call" | custom-call | flops 805306368 | bytes 7340032 | tf_op jit(solution)/shard_map/pallas_call | solution.py:177
  41.2 2.3 %collective-permute-done.8.refs_0_ = bf16[6160,128]{1,0:T(8,128)(2,1)S(1)} collective-permute-done((bf16[6160,128]{1,0:T(8,128)(2,1)S(1)}, bf16[6160,128]{1,0:T(8,128)(2,1)S(1)}, u32[]{:S(2)}, u32[]{:S(2)}) %collective-permute-start.8) | collective-permute-done | bytes 1576992 | tf_op jit(solution)/shard_map/ppermute | solution.py:211
  43.5 2.1 %shard_map.40 = (f32[2,128]{1,0:T(2,128)S(1)}, f32[4,128]{1,0:T(4,128)S(1)}, f32[4,128]{1,0:T(4,128)S(1)}) custom-call(bf16[6160,128]{1,0:T(8,128)(2,1)S(1)} %collective-permute-done.8.refs_0_, bf16[192,4224]{1,0:T(8,128)(2,1)S(1)} %get-tuple-element.10.refs_1_, bf16[192,4224]{1,0:T(8,128)(2,1)S(1)} %collective-permute-done.2.refs_2_, ...), custom_call_target="tpu_custom_call" | custom-call | flops 1610612736 | bytes 8388608 | tf_op jit(solution)/shard_map/pallas_call | solution.py:177
  45.6 1.3 %collective-permute-start.11 = (f32[4,128]{1,0:T(4,128)S(1)}, f32[4,128]{1,0:T(4,128)S(1)}, u32[]{:S(2)}, u32[]{:S(2)}) collective-permute-start(f32[4,128]{1,0:T(4,128)S(1)} %get-tuple-element.14), channel_id=1, source_target_pairs={{0,1},{1,0},{2,3},{3,2},{4,5},{5,4},{6,7},{7,6},{8,9},{9,8},{10,11... | collective-permute-start | bytes 6152 | tf_op jit(solution)/shard_map/ppermute | solution.py:35
  46.9 1.3 %collective-permute-start.9 = (f32[2,128]{1,0:T(2,128)S(1)}, f32[2,128]{1,0:T(2,128)S(1)}, u32[]{:S(2)}, u32[]{:S(2)}) collective-permute-start(f32[2,128]{1,0:T(2,128)S(1)} %get-tuple-element.12), channel_id=1, source_target_pairs={{4,0},{2,6},{3,1},{5,3},{7,5},{1,7},{12,8},{10,14},{11,9},{13,11},... | collective-permute-start | bytes 3080 | tf_op jit(solution)/shard_map/ppermute | solution.py:238
  48.2 2.5 %collective-permute-start.14 = (f32[4,128]{1,0:T(4,128)S(1)}, f32[4,128]{1,0:T(4,128)S(1)}, u32[]{:S(2)}, u32[]{:S(2)}) collective-permute-start(f32[4,128]{1,0:T(4,128)S(1)} %max.23), channel_id=1, source_target_pairs={{0,8},{1,17},{8,0},{9,25},{16,24},{17,1},{24,16},{25,9},{2,10},{3,... | collective-permute-start | bytes 6152 | tf_op jit(solution)/shard_map/ppermute | solution.py:249
  50.7 1.5 %collective-permute-start.12 = (f32[4,128]{1,0:T(4,128)S(1)}, f32[4,128]{1,0:T(4,128)S(1)}, u32[]{:S(2)}, u32[]{:S(2)}) collective-permute-start(f32[4,128]{1,0:T(4,128)S(1)} %max.23), channel_id=1, source_target_pairs={{0,16},{1,9},{8,24},{9,1},{16,0},{17,25},{24,8},{25,17},{2,18},{3,... | collective-permute-start | bytes 6152 | tf_op jit(solution)/shard_map/ppermute | solution.py:245
  52.3 0.9 %collective-permute-done.9 = f32[2,128]{1,0:T(2,128)S(1)} collective-permute-done((f32[2,128]{1,0:T(2,128)S(1)}, f32[2,128]{1,0:T(2,128)S(1)}, u32[]{:S(2)}, u32[]{:S(2)}) %collective-permute-start.9) | collective-permute-done | bytes 1056 | tf_op jit(solution)/shard_map/ppermute | solution.py:238
  53.2 1.1 %collective-permute-done.10 = f32[2,128]{1,0:T(2,128)S(1)} collective-permute-done((f32[2,128]{1,0:T(2,128)S(1)}, f32[2,128]{1,0:T(2,128)S(1)}, u32[]{:S(2)}, u32[]{:S(2)}) %collective-permute-start.10) | collective-permute-done | bytes 1056 | tf_op jit(solution)/shard_map/ppermute | solution.py:35
  54.4 0.8 %collective-permute-done.13 = f32[4,128]{1,0:T(4,128)S(1)} collective-permute-done((f32[4,128]{1,0:T(4,128)S(1)}, f32[4,128]{1,0:T(4,128)S(1)}, u32[]{:S(2)}, u32[]{:S(2)}) %collective-permute-start.13) | collective-permute-done | bytes 2080 | tf_op jit(solution)/shard_map/ppermute | solution.py:247
  55.2 0.5 slice_bitcast_fusion
  (17 shorter events, 0.2 us)
Async XLA Ops:
  0.0 2.6 %collective-permute-start = (bf16[96,4096]{1,0:T(8,128)(2,1)}, bf16[96,4096]{1,0:T(8,128)(2,1)S(1)}, u32[]{:S(2)}, u32[]{:S(2)}) collective-permute-start(bf16[96,4096]{1,0:T(8,128)(2,1)} %rows_ref.1), channel_id=1, source_target_pairs={{0,1},{1,0},{2,3},{3,2},{4,5},{5,4},{6,7},{7,6},{8,9},{9,8},{10,11... | collective-permute-start | bytes 2359304 | tf_op jit(solution)/shard_map/ppermute | solution.py:35
  1.1 1.5 %collective-permute-start.1 = (s32[2,96]{1,0:T(2,128)S(1)}, s32[2,96]{1,0:T(2,128)S(1)}, u32[]{:S(2)}, u32[]{:S(2)}) collective-permute-start(s32[2,96]{1,0:T(2,128)S(1)} %pad_add_fusion.ids_ref.own_ids_ref), channel_id=1, source_target_pairs={{0,1},{1,0},{2,3},{3,2},{4,5},{5,4},{6,7},{7,6},{8,9},{9,8},{10,11... | collective-permute-start | bytes 2312 | tf_op jit(solution)/shard_map/ppermute | solution.py:35
  1.2 1.1 %copy-start = (bf16[96,4096]{1,0:T(8,128)(2,1)S(1)}, bf16[96,4096]{1,0:T(8,128)(2,1)}, u32[]{:S(2)}) copy-start(bf16[96,4096]{1,0:T(8,128)(2,1)} %rows_ref.1) | copy-start | bytes 2359300
  3.3 21.9 %collective-permute-start.2 = (bf16[192,4224]{1,0:T(8,128)(2,1)S(1)}, bf16[192,4224]{1,0:T(8,128)(2,1)S(1)}, u32[]{:S(2)}, u32[]{:S(2)}) collective-permute-start(bf16[192,4224]{1,0:T(8,128)(2,1)S(1)} %get-tuple-element.10.refs_1_), channel_id=1, source_target_pairs={{0,8},{1,17},{8,0},{9,25},{16,24},{17,1},{24,16},{25,9},{2,10},{3,... | collective-permute-start | bytes 4866056 | tf_op jit(solution)/shard_map/ppermute | solution.py:214
  6.3 37.2 %collective-permute-start.8 = (bf16[6160,128]{1,0:T(8,128)(2,1)S(1)}, bf16[6160,128]{1,0:T(8,128)(2,1)S(1)}, u32[]{:S(2)}, u32[]{:S(2)}) collective-permute-start(bf16[6160,128]{1,0:T(8,128)(2,1)S(1)} %get-tuple-element.11), channel_id=1, source_target_pairs={{0,4},{6,2},{1,3},{3,5},{5,7},{7,1},{8,12},{14,10},{9,11},{11,13},... | collective-permute-start | bytes 4730888 | tf_op jit(solution)/shard_map/ppermute | solution.py:211
  25.3 14.2 %collective-permute-start.3 = (bf16[192,4224]{1,0:T(8,128)(2,1)S(1)}, bf16[192,4224]{1,0:T(8,128)(2,1)S(1)}, u32[]{:S(2)}, u32[]{:S(2)}) collective-permute-start(bf16[192,4224]{1,0:T(8,128)(2,1)S(1)} %collective-permute-done.2.refs_2_), channel_id=1, source_target_pairs={{0,1},{1,0},{2,3},{3,2},{4,5},{5,4},{6,7},{7,6},{8,9},{9,8},{10,11... | collective-permute-start | bytes 4866056 | tf_op jit(solution)/shard_map/ppermute | solution.py:35
  25.3 8.0 %collective-permute-start.4 = (bf16[48,4224]{1,0:T(8,128)(2,1)S(1)}, bf16[48,4224]{1,0:T(8,128)(2,1)S(1)}, u32[]{:S(2)}, u32[]{:S(2)}) collective-permute-start(bf16[48,4224]{1,0:T(8,128)(2,1)S(1)} %get-tuple-element.16), channel_id=1, source_target_pairs={{0,16},{1,9},{8,24},{9,1},{16,0},{17,25},{24,8},{25,17},{2,18},{3,... | collective-permute-start | bytes 1216520 | tf_op jit(solution)/shard_map/ppermute | solution.py:219
  27.4 10.2 %collective-permute-start.5 = (bf16[48,4224]{1,0:T(8,128)(2,1)S(1)}, bf16[48,4224]{1,0:T(8,128)(2,1)S(1)}, u32[]{:S(2)}, u32[]{:S(2)}) collective-permute-start(bf16[48,4224]{1,0:T(8,128)(2,1)S(1)} %get-tuple-element.15), channel_id=1, source_target_pairs={{0,16},{1,9},{8,24},{9,1},{16,0},{17,25},{24,8},{25,17},{2,18},{3,... | collective-permute-start | bytes 1216520 | tf_op jit(solution)/shard_map/ppermute | solution.py:219
  33.3 4.4 %collective-permute-start.6 = (bf16[48,4224]{1,0:T(8,128)(2,1)S(1)}, bf16[48,4224]{1,0:T(8,128)(2,1)S(1)}, u32[]{:S(2)}, u32[]{:S(2)}) collective-permute-start(bf16[48,4224]{1,0:T(8,128)(2,1)S(1)} %collective-permute-done.4.refs_4_), channel_id=1, source_target_pairs={{0,1},{1,0},{2,3},{3,2},{4,5},{5,4},{6,7},{7,6},{8,9},{9,8},{10,11... | collective-permute-start | bytes 1216520 | tf_op jit(solution)/shard_map/ppermute | solution.py:35
  37.7 1.7 %collective-permute-start.7 = (bf16[48,4224]{1,0:T(8,128)(2,1)S(1)}, bf16[48,4224]{1,0:T(8,128)(2,1)S(1)}, u32[]{:S(2)}, u32[]{:S(2)}) collective-permute-start(bf16[48,4224]{1,0:T(8,128)(2,1)S(1)} %collective-permute-done.5.refs_5_), channel_id=1, source_target_pairs={{0,1},{1,0},{2,3},{3,2},{4,5},{5,4},{6,7},{7,6},{8,9},{9,8},{10,11... | collective-permute-start | bytes 1216520 | tf_op jit(solution)/shard_map/ppermute | solution.py:35
  45.6 2.6 %collective-permute-start.11 = (f32[4,128]{1,0:T(4,128)S(1)}, f32[4,128]{1,0:T(4,128)S(1)}, u32[]{:S(2)}, u32[]{:S(2)}) collective-permute-start(f32[4,128]{1,0:T(4,128)S(1)} %get-tuple-element.14), channel_id=1, source_target_pairs={{0,1},{1,0},{2,3},{3,2},{4,5},{5,4},{6,7},{7,6},{8,9},{9,8},{10,11... | collective-permute-start | bytes 6152 | tf_op jit(solution)/shard_map/ppermute | solution.py:35
  46.9 6.3 %collective-permute-start.9 = (f32[2,128]{1,0:T(2,128)S(1)}, f32[2,128]{1,0:T(2,128)S(1)}, u32[]{:S(2)}, u32[]{:S(2)}) collective-permute-start(f32[2,128]{1,0:T(2,128)S(1)} %get-tuple-element.12), channel_id=1, source_target_pairs={{4,0},{2,6},{3,1},{5,3},{7,5},{1,7},{12,8},{10,14},{11,9},{13,11},... | collective-permute-start | bytes 3080 | tf_op jit(solution)/shard_map/ppermute | solution.py:238
  48.2 6.2 %collective-permute-start.14 = (f32[4,128]{1,0:T(4,128)S(1)}, f32[4,128]{1,0:T(4,128)S(1)}, u32[]{:S(2)}, u32[]{:S(2)}) collective-permute-start(f32[4,128]{1,0:T(4,128)S(1)} %max.23), channel_id=1, source_target_pairs={{0,8},{1,17},{8,0},{9,25},{16,24},{17,1},{24,16},{25,9},{2,10},{3,... | collective-permute-start | bytes 6152 | tf_op jit(solution)/shard_map/ppermute | solution.py:249
  50.7 4.5 %collective-permute-start.13 = (f32[4,128]{1,0:T(4,128)S(1)}, f32[4,128]{1,0:T(4,128)S(1)}, u32[]{:S(2)}, u32[]{:S(2)}) collective-permute-start(f32[4,128]{1,0:T(4,128)S(1)} %max.23), channel_id=1, source_target_pairs={{0,24},{8,16},{16,8},{24,0},{1,25},{9,17},{17,9},{25,1},{2,26},{10... | collective-permute-start | bytes 6152 | tf_op jit(solution)/shard_map/ppermute | solution.py:247
  50.7 4.5 %collective-permute-start.12 = (f32[4,128]{1,0:T(4,128)S(1)}, f32[4,128]{1,0:T(4,128)S(1)}, u32[]{:S(2)}, u32[]{:S(2)}) collective-permute-start(f32[4,128]{1,0:T(4,128)S(1)} %max.23), channel_id=1, source_target_pairs={{0,16},{1,9},{8,24},{9,1},{16,0},{17,25},{24,8},{25,17},{2,18},{3,... | collective-permute-start | bytes 6152 | tf_op jit(solution)/shard_map/ppermute | solution.py:245
  53.2 1.1 %collective-permute-start.10 = (f32[2,128]{1,0:T(2,128)S(1)}, f32[2,128]{1,0:T(2,128)S(1)}, u32[]{:S(2)}, u32[]{:S(2)}) collective-permute-start(f32[2,128]{1,0:T(2,128)S(1)} %collective-permute-done.9), channel_id=1, source_target_pairs={{0,1},{1,0},{2,3},{3,2},{4,5},{5,4},{6,7},{7,6},{8,9},{9,8},{10,11... | collective-permute-start | bytes 3080 | tf_op jit(solution)/shard_map/ppermute | solution.py:35

commit v25 on v20

--- a/solution.py
+++ b/solution.py
@@ -230,6 +230,7 @@
         count = 2 * len(visitors)
         operands = [*visitors, *chunk, bests[index]]
         answers.append(call(kernel, operands, count, [count, 4, 4], 8 * rows, width))
+    bests = [best[0, :rows] for best in bests]
     home = functools.reduce(jnp.maximum, [answer[0] for answer in answers])
     merged = [jnp.maximum(mine, swap(others)) for _, mine, others in answers]
 
@@ -238,16 +239,16 @@
         back = lax.ppermute(part, line_axes, [(b, a) for a, b in trip])
         for here, best in ((2 * z + core, back[0:1]), (2 * z + (core ^ 1), swap(back)[1:2])):
             sent = functools.reduce(jnp.logical_or, [here == a for a, _ in trip])
-            bests.append(jnp.where(sent, best, -1.0))
+            bests.append(jnp.where(sent, best[0, :rows], -1.0))
     ways = [(0, 0, partners[-1])]
     ways += [(1 + k // 2, 2 * (k % 2), way) for k, way in enumerate(partners[:-1])]
     for chunk, row, (first, second) in ways:
         for offset, order in ((1, (second, first)), (0, (first, second))):
             got = lax.ppermute(merged[chunk], plane_axes, group_trip(groups, *order))
-            bests.append(got[row + offset : row + offset + 1])
-    bests.append(lax.ppermute(merged[0], "group", flip(groups, last))[2:3])
-    bests.append(merged[0][3:4])
-    return functools.reduce(jnp.maximum, bests)[0, :rows]
+            bests.append(got[row + offset, :rows])
+    bests.append(lax.ppermute(merged[0], "group", flip(groups, last))[2, :rows])
+    bests.append(merged[0][3, :rows])
+    return functools.reduce(jnp.maximum, bests)
 
 
 def solution(mesh):

time: 55.2 us -> 55.2 us (level)
  no operation moved by 1% of the time
where the time goes in v25:
time: 55.2 us; the launch traced here: 54.9 us
  waiting for transfers between devices  30.7 us (56%)
  starting transfers between devices  16.9 us (31%)
  Pallas kernels  4.83 us (9%)
  other arithmetic  1.2 us (2%)
  local copies, waits for them, and re-layouts  1.19 us (2%)
    ppermute x1, waiting for transfers between devices, local(): lax.ppermute(both, plane_axes, group_trip(groups, *way))  14.3 us
    ppermute x2, waiting for transfers between devices, local(): corner = [lax.ppermute(part, plane_axes, relay) for part in corner]  10.2 us
    ppermute x1, starting transfers between devices, local(): visitors = [lax.ppermute(line, line_axes, trip) for trip in trips]  4.58 us
    pallas_call x2, Pallas kernels, call(): pl.pallas_call(kernel, in_specs=[VMEM] * len(operands), out_specs=[VMEM]...  3.86 us
    ppermute x1, starting transfers between devices, local(): lax.ppermute(both, plane_axes, group_trip(groups, *way))  3 us
    ppermute x7, waiting for transfers between devices, swap(): return lax.ppermute(block, 'core', flip(2, 1))  2.88 us
    ppermute x2, starting transfers between devices, local(): got = lax.ppermute(merged[chunk], plane_axes, group_trip(groups, *order))  2.58 us
    ppermute x1, waiting for transfers between devices, local(): visitors = [lax.ppermute(line, line_axes, trip) for trip in trips]  2.29 us
  transfers between devices with their start and end apart: 15, of which 7 were waited for; matrix products, arithmetic and copies ran while one was open for 1% of the time, Pallas kernels for 4%

profile of v25, /device:TPU:0, one launch (start us, length us, event | category | flops | bytes accessed | tf_op | source)
XLA Modules:
  0.0 54.9 jit_solution(2865994633109270752)
XLA Ops:
  0.0 0.5 collective-permute-start
  0.5 0.7 %pad_add_fusion.ids_ref.own_ids_ref = s32[2,96]{1,0:T(2,128)S(1)} fusion(s32[1,96]{1,0:T(1,128)} %bitcast.4, s32[1,96]{1,0:T(1,128)} %bitcast.5), kind=kLoop, calls=%fused_computation | loop fusion | flops 192 | bytes 1536 | tf_op jit(solution)/shard_map/stack | solution.py:201
  1.2 1.1 %copy-done = bf16[96,4096]{1,0:T(8,128)(2,1)S(1)} copy-done((bf16[96,4096]{1,0:T(8,128)(2,1)S(1)}, bf16[96,4096]{1,0:T(8,128)(2,1)}, u32[]{:S(2)}) %copy-start) | copy-done | bytes 786456
  2.3 0.3 shard_map.37.own_ref.refs_0_
  2.6 0.7 %shard_map.38 = (bf16[192,4224]{1,0:T(8,128)(2,1)S(1)}, bf16[6160,128]{1,0:T(8,128)(2,1)S(1)}) custom-call(bf16[96,4224]{1,0:T(8,128)(2,1)S(1)} %shard_map.37.own_ref.refs_0_, s32[2,96]{1,0:T(2,128)S(1)} %pad_add_fusion.ids_ref.own_ids_ref, bf16[96,4096]{1,0:T(8,128)(2,1)S(1)} %collective-permute-done.rows_ref, s32[2,96]{1,0:T(2,128)S(1)} %collective-permute-done.1.ids_ref), custom_call_target="tpu_custom_call" | custom-call | flops 1572864 | bytes 1572864 | tf_op jit(solution)/shard_map/pallas_call | solution.py:77
  3.3 3.0 %collective-permute-start.2 = (bf16[192,4224]{1,0:T(8,128)(2,1)S(1)}, bf16[192,4224]{1,0:T(8,128)(2,1)S(1)}, u32[]{:S(2)}, u32[]{:S(2)}) collective-permute-start(bf16[192,4224]{1,0:T(8,128)(2,1)S(1)} %get-tuple-element.10.refs_1_), channel_id=1, source_target_pairs={{0,8},{1,17},{8,0},{9,25},{16,24},{17,1},{24,16},{25,9},{2,10},{3,... | collective-permute-start | bytes 4866056 | tf_op jit(solution)/shard_map/ppermute | solution.py:214
  6.3 4.6 %collective-permute-start.8 = (bf16[6160,128]{1,0:T(8,128)(2,1)S(1)}, bf16[6160,128]{1,0:T(8,128)(2,1)S(1)}, u32[]{:S(2)}, u32[]{:S(2)}) collective-permute-start(bf16[6160,128]{1,0:T(8,128)(2,1)S(1)} %get-tuple-element.11), channel_id=1, source_target_pairs={{0,4},{6,2},{1,3},{3,5},{5,7},{7,1},{8,12},{14,10},{9,11},{11,13},... | collective-permute-start | bytes 4730888 | tf_op jit(solution)/shard_map/ppermute | solution.py:211
  10.9 14.3 %collective-permute-done.2.refs_2_ = bf16[192,4224]{1,0:T(8,128)(2,1)S(1)} collective-permute-done((bf16[192,4224]{1,0:T(8,128)(2,1)S(1)}, bf16[192,4224]{1,0:T(8,128)(2,1)S(1)}, u32[]{:S(2)}, u32[]{:S(2)}) %collective-permute-start.2) | collective-permute-done | bytes 1622048 | tf_op jit(solution)/shard_map/ppermute | solution.py:214
  25.3 2.1 %collective-permute-start.4 = (bf16[48,4224]{1,0:T(8,128)(2,1)S(1)}, bf16[48,4224]{1,0:T(8,128)(2,1)S(1)}, u32[]{:S(2)}, u32[]{:S(2)}) collective-permute-start(bf16[48,4224]{1,0:T(8,128)(2,1)S(1)} %get-tuple-element.16), channel_id=1, source_target_pairs={{0,16},{1,9},{8,24},{9,1},{16,0},{17,25},{24,8},{25,17},{2,18},{3,... | collective-permute-start | bytes 1216520 | tf_op jit(solution)/shard_map/ppermute | solution.py:219
  27.4 0.1 collective-permute-start.5
  27.5 5.8 %collective-permute-done.4.refs_4_ = bf16[48,4224]{1,0:T(8,128)(2,1)S(1)} collective-permute-done((bf16[48,4224]{1,0:T(8,128)(2,1)S(1)}, bf16[48,4224]{1,0:T(8,128)(2,1)S(1)}, u32[]{:S(2)}, u32[]{:S(2)}) %collective-permute-start.4) | collective-permute-done | bytes 405536 | tf_op jit(solution)/shard_map/ppermute | solution.py:219
  33.3 4.3 %collective-permute-done.5.refs_5_ = bf16[48,4224]{1,0:T(8,128)(2,1)S(1)} collective-permute-done((bf16[48,4224]{1,0:T(8,128)(2,1)S(1)}, bf16[48,4224]{1,0:T(8,128)(2,1)S(1)}, u32[]{:S(2)}, u32[]{:S(2)}) %collective-permute-start.5) | collective-permute-done | bytes 405536 | tf_op jit(solution)/shard_map/ppermute | solution.py:219
  37.7 1.7 %collective-permute-done.7.refs_7_ = bf16[48,4224]{1,0:T(8,128)(2,1)S(1)} collective-permute-done((bf16[48,4224]{1,0:T(8,128)(2,1)S(1)}, bf16[48,4224]{1,0:T(8,128)(2,1)S(1)}, u32[]{:S(2)}, u32[]{:S(2)}) %collective-permute-start.7) | collective-permute-done | bytes 405536 | tf_op jit(solution)/shard_map/ppermute | solution.py:35
  39.4 1.8 %shard_map.39.refs_8_ = f32[1,128]{1,0:T(1,128)S(1)} custom-call(bf16[96,4224]{1,0:T(8,128)(2,1)S(1)} %shard_map.37.own_ref.refs_0_, bf16[192,4224]{1,0:T(8,128)(2,1)S(1)} %get-tuple-element.10.refs_1_, bf16[192,4224]{1,0:T(8,128)(2,1)S(1)} %collective-permute-done.2.refs_2_, bf16[192,4224]{1,0:T(8,128)(2,1)S(1)} %collective-permute-done.3.refs_3_, ...), custom_call_target="tpu_custom_call" | custom-call | flops 805306368 | bytes 7340032 | tf_op jit(solution)/shard_map/pallas_call | solution.py:177
  41.2 2.3 %collective-permute-done.8.refs_0_ = bf16[6160,128]{1,0:T(8,128)(2,1)S(1)} collective-permute-done((bf16[6160,128]{1,0:T(8,128)(2,1)S(1)}, bf16[6160,128]{1,0:T(8,128)(2,1)S(1)}, u32[]{:S(2)}, u32[]{:S(2)}) %collective-permute-start.8) | collective-permute-done | bytes 1576992 | tf_op jit(solution)/shard_map/ppermute | solution.py:211
  43.5 2.1 %shard_map.40 = (f32[2,128]{1,0:T(2,128)S(1)}, f32[4,128]{1,0:T(4,128)S(1)}, f32[4,128]{1,0:T(4,128)S(1)}) custom-call(bf16[6160,128]{1,0:T(8,128)(2,1)S(1)} %collective-permute-done.8.refs_0_, bf16[192,4224]{1,0:T(8,128)(2,1)S(1)} %get-tuple-element.10.refs_1_, bf16[192,4224]{1,0:T(8,128)(2,1)S(1)} %collective-permute-done.2.refs_2_, ...), custom_call_target="tpu_custom_call" | custom-call | flops 1610612736 | bytes 8388608 | tf_op jit(solution)/shard_map/pallas_call | solution.py:177
  45.6 1.3 %collective-permute-start.11 = (f32[4,128]{1,0:T(4,128)S(1)}, f32[4,128]{1,0:T(4,128)S(1)}, u32[]{:S(2)}, u32[]{:S(2)}) collective-permute-start(f32[4,128]{1,0:T(4,128)S(1)} %get-tuple-element.14), channel_id=1, source_target_pairs={{0,1},{1,0},{2,3},{3,2},{4,5},{5,4},{6,7},{7,6},{8,9},{9,8},{10,11... | collective-permute-start | bytes 6152 | tf_op jit(solution)/shard_map/ppermute | solution.py:35
  46.9 1.3 %collective-permute-start.9 = (f32[2,128]{1,0:T(2,128)S(1)}, f32[2,128]{1,0:T(2,128)S(1)}, u32[]{:S(2)}, u32[]{:S(2)}) collective-permute-start(f32[2,128]{1,0:T(2,128)S(1)} %get-tuple-element.12), channel_id=1, source_target_pairs={{4,0},{2,6},{3,1},{5,3},{7,5},{1,7},{12,8},{10,14},{11,9},{13,11},... | collective-permute-start | bytes 3080 | tf_op jit(solution)/shard_map/ppermute | solution.py:239
  48.2 1.4 %collective-permute-start.14 = (f32[4,128]{1,0:T(4,128)S(1)}, f32[4,128]{1,0:T(4,128)S(1)}, u32[]{:S(2)}, u32[]{:S(2)}) collective-permute-start(f32[4,128]{1,0:T(4,128)S(1)} %max.28), channel_id=1, source_target_pairs={{0,24},{8,16},{16,8},{24,0},{1,25},{9,17},{17,9},{25,1},{2,26},{10... | collective-permute-start | bytes 6152 | tf_op jit(solution)/shard_map/ppermute | solution.py:249
  49.6 1.2 %collective-permute-start.13 = (f32[4,128]{1,0:T(4,128)S(1)}, f32[4,128]{1,0:T(4,128)S(1)}, u32[]{:S(2)}, u32[]{:S(2)}) collective-permute-start(f32[4,128]{1,0:T(4,128)S(1)} %max.28), channel_id=1, source_target_pairs={{0,8},{1,17},{8,0},{9,25},{16,24},{17,1},{24,16},{25,9},{2,10},{3,... | collective-permute-start | bytes 6152 | tf_op jit(solution)/shard_map/ppermute | solution.py:247
  50.8 1.4 %collective-permute-start.12 = (f32[4,128]{1,0:T(4,128)S(1)}, f32[4,128]{1,0:T(4,128)S(1)}, u32[]{:S(2)}, u32[]{:S(2)}) collective-permute-start(f32[4,128]{1,0:T(4,128)S(1)} %max.28), channel_id=1, source_target_pairs={{0,16},{1,9},{8,24},{9,1},{16,0},{17,25},{24,8},{25,17},{2,18},{3,... | collective-permute-start | bytes 6152 | tf_op jit(solution)/shard_map/ppermute | solution.py:247
  52.2 1.0 %collective-permute-done.9 = f32[2,128]{1,0:T(2,128)S(1)} collective-permute-done((f32[2,128]{1,0:T(2,128)S(1)}, f32[2,128]{1,0:T(2,128)S(1)}, u32[]{:S(2)}, u32[]{:S(2)}) %collective-permute-start.9) | collective-permute-done | bytes 1056 | tf_op jit(solution)/shard_map/ppermute | solution.py:239
  53.2 1.1 %collective-permute-done.10 = f32[2,128]{1,0:T(2,128)S(1)} collective-permute-done((f32[2,128]{1,0:T(2,128)S(1)}, f32[2,128]{1,0:T(2,128)S(1)}, u32[]{:S(2)}, u32[]{:S(2)}) %collective-permute-start.10) | collective-permute-done | bytes 1056 | tf_op jit(solution)/shard_map/ppermute | solution.py:35
  54.4 0.5 maximum_bitcast_fusion
  (16 shorter events, 0.2 us)
Async XLA Ops:
  0.0 2.6 %collective-permute-start = (bf16[96,4096]{1,0:T(8,128)(2,1)}, bf16[96,4096]{1,0:T(8,128)(2,1)S(1)}, u32[]{:S(2)}, u32[]{:S(2)}) collective-permute-start(bf16[96,4096]{1,0:T(8,128)(2,1)} %rows_ref.1), channel_id=1, source_target_pairs={{0,1},{1,0},{2,3},{3,2},{4,5},{5,4},{6,7},{7,6},{8,9},{9,8},{10,11... | collective-permute-start | bytes 2359304 | tf_op jit(solution)/shard_map/ppermute | solution.py:35
  1.1 1.5 %collective-permute-start.1 = (s32[2,96]{1,0:T(2,128)S(1)}, s32[2,96]{1,0:T(2,128)S(1)}, u32[]{:S(2)}, u32[]{:S(2)}) collective-permute-start(s32[2,96]{1,0:T(2,128)S(1)} %pad_add_fusion.ids_ref.own_ids_ref), channel_id=1, source_target_pairs={{0,1},{1,0},{2,3},{3,2},{4,5},{5,4},{6,7},{7,6},{8,9},{9,8},{10,11... | collective-permute-start | bytes 2312 | tf_op jit(solution)/shard_map/ppermute | solution.py:35
  1.2 1.1 %copy-start = (bf16[96,4096]{1,0:T(8,128)(2,1)S(1)}, bf16[96,4096]{1,0:T(8,128)(2,1)}, u32[]{:S(2)}) copy-start(bf16[96,4096]{1,0:T(8,128)(2,1)} %rows_ref.1) | copy-start | bytes 2359300
  3.3 21.9 %collective-permute-start.2 = (bf16[192,4224]{1,0:T(8,128)(2,1)S(1)}, bf16[192,4224]{1,0:T(8,128)(2,1)S(1)}, u32[]{:S(2)}, u32[]{:S(2)}) collective-permute-start(bf16[192,4224]{1,0:T(8,128)(2,1)S(1)} %get-tuple-element.10.refs_1_), channel_id=1, source_target_pairs={{0,8},{1,17},{8,0},{9,25},{16,24},{17,1},{24,16},{25,9},{2,10},{3,... | collective-permute-start | bytes 4866056 | tf_op jit(solution)/shard_map/ppermute | solution.py:214
  6.3 37.2 %collective-permute-start.8 = (bf16[6160,128]{1,0:T(8,128)(2,1)S(1)}, bf16[6160,128]{1,0:T(8,128)(2,1)S(1)}, u32[]{:S(2)}, u32[]{:S(2)}) collective-permute-start(bf16[6160,128]{1,0:T(8,128)(2,1)S(1)} %get-tuple-element.11), channel_id=1, source_target_pairs={{0,4},{6,2},{1,3},{3,5},{5,7},{7,1},{8,12},{14,10},{9,11},{11,13},... | collective-permute-start | bytes 4730888 | tf_op jit(solution)/shard_map/ppermute | solution.py:211
  25.3 14.2 %collective-permute-start.3 = (bf16[192,4224]{1,0:T(8,128)(2,1)S(1)}, bf16[192,4224]{1,0:T(8,128)(2,1)S(1)}, u32[]{:S(2)}, u32[]{:S(2)}) collective-permute-start(bf16[192,4224]{1,0:T(8,128)(2,1)S(1)} %collective-permute-done.2.refs_2_), channel_id=1, source_target_pairs={{0,1},{1,0},{2,3},{3,2},{4,5},{5,4},{6,7},{7,6},{8,9},{9,8},{10,11... | collective-permute-start | bytes 4866056 | tf_op jit(solution)/shard_map/ppermute | solution.py:35
  25.3 8.0 %collective-permute-start.4 = (bf16[48,4224]{1,0:T(8,128)(2,1)S(1)}, bf16[48,4224]{1,0:T(8,128)(2,1)S(1)}, u32[]{:S(2)}, u32[]{:S(2)}) collective-permute-start(bf16[48,4224]{1,0:T(8,128)(2,1)S(1)} %get-tuple-element.16), channel_id=1, source_target_pairs={{0,16},{1,9},{8,24},{9,1},{16,0},{17,25},{24,8},{25,17},{2,18},{3,... | collective-permute-start | bytes 1216520 | tf_op jit(solution)/shard_map/ppermute | solution.py:219
  27.4 10.2 %collective-permute-start.5 = (bf16[48,4224]{1,0:T(8,128)(2,1)S(1)}, bf16[48,4224]{1,0:T(8,128)(2,1)S(1)}, u32[]{:S(2)}, u32[]{:S(2)}) collective-permute-start(bf16[48,4224]{1,0:T(8,128)(2,1)S(1)} %get-tuple-element.15), channel_id=1, source_target_pairs={{0,16},{1,9},{8,24},{9,1},{16,0},{17,25},{24,8},{25,17},{2,18},{3,... | collective-permute-start | bytes 1216520 | tf_op jit(solution)/shard_map/ppermute | solution.py:219
  33.3 4.4 %collective-permute-start.6 = (bf16[48,4224]{1,0:T(8,128)(2,1)S(1)}, bf16[48,4224]{1,0:T(8,128)(2,1)S(1)}, u32[]{:S(2)}, u32[]{:S(2)}) collective-permute-start(bf16[48,4224]{1,0:T(8,128)(2,1)S(1)} %collective-permute-done.4.refs_4_), channel_id=1, source_target_pairs={{0,1},{1,0},{2,3},{3,2},{4,5},{5,4},{6,7},{7,6},{8,9},{9,8},{10,11... | collective-permute-start | bytes 1216520 | tf_op jit(solution)/shard_map/ppermute | solution.py:35
  37.7 1.7 %collective-permute-start.7 = (bf16[48,4224]{1,0:T(8,128)(2,1)S(1)}, bf16[48,4224]{1,0:T(8,128)(2,1)S(1)}, u32[]{:S(2)}, u32[]{:S(2)}) collective-permute-start(bf16[48,4224]{1,0:T(8,128)(2,1)S(1)} %collective-permute-done.5.refs_5_), channel_id=1, source_target_pairs={{0,1},{1,0},{2,3},{3,2},{4,5},{5,4},{6,7},{7,6},{8,9},{9,8},{10,11... | collective-permute-start | bytes 1216520 | tf_op jit(solution)/shard_map/ppermute | solution.py:35
  45.6 2.6 %collective-permute-start.11 = (f32[4,128]{1,0:T(4,128)S(1)}, f32[4,128]{1,0:T(4,128)S(1)}, u32[]{:S(2)}, u32[]{:S(2)}) collective-permute-start(f32[4,128]{1,0:T(4,128)S(1)} %get-tuple-element.14), channel_id=1, source_target_pairs={{0,1},{1,0},{2,3},{3,2},{4,5},{5,4},{6,7},{7,6},{8,9},{9,8},{10,11... | collective-permute-start | bytes 6152 | tf_op jit(solution)/shard_map/ppermute | solution.py:35
  46.9 6.3 %collective-permute-start.9 = (f32[2,128]{1,0:T(2,128)S(1)}, f32[2,128]{1,0:T(2,128)S(1)}, u32[]{:S(2)}, u32[]{:S(2)}) collective-permute-start(f32[2,128]{1,0:T(2,128)S(1)} %get-tuple-element.12), channel_id=1, source_target_pairs={{4,0},{2,6},{3,1},{5,3},{7,5},{1,7},{12,8},{10,14},{11,9},{13,11},... | collective-permute-start | bytes 3080 | tf_op jit(solution)/shard_map/ppermute | solution.py:239
  48.2 6.2 %collective-permute-start.14 = (f32[4,128]{1,0:T(4,128)S(1)}, f32[4,128]{1,0:T(4,128)S(1)}, u32[]{:S(2)}, u32[]{:S(2)}) collective-permute-start(f32[4,128]{1,0:T(4,128)S(1)} %max.28), channel_id=1, source_target_pairs={{0,24},{8,16},{16,8},{24,0},{1,25},{9,17},{17,9},{25,1},{2,26},{10... | collective-permute-start | bytes 6152 | tf_op jit(solution)/shard_map/ppermute | solution.py:249
  49.6 4.8 %collective-permute-start.13 = (f32[4,128]{1,0:T(4,128)S(1)}, f32[4,128]{1,0:T(4,128)S(1)}, u32[]{:S(2)}, u32[]{:S(2)}) collective-permute-start(f32[4,128]{1,0:T(4,128)S(1)} %max.28), channel_id=1, source_target_pairs={{0,8},{1,17},{8,0},{9,25},{16,24},{17,1},{24,16},{25,9},{2,10},{3,... | collective-permute-start | bytes 6152 | tf_op jit(solution)/shard_map/ppermute | solution.py:247
  50.8 3.6 %collective-permute-start.12 = (f32[4,128]{1,0:T(4,128)S(1)}, f32[4,128]{1,0:T(4,128)S(1)}, u32[]{:S(2)}, u32[]{:S(2)}) collective-permute-start(f32[4,128]{1,0:T(4,128)S(1)} %max.28), channel_id=1, source_target_pairs={{0,16},{1,9},{8,24},{9,1},{16,0},{17,25},{24,8},{25,17},{2,18},{3,... | collective-permute-start | bytes 6152 | tf_op jit(solution)/shard_map/ppermute | solution.py:247
  53.2 1.1 %collective-permute-start.10 = (f32[2,128]{1,0:T(2,128)S(1)}, f32[2,128]{1,0:T(2,128)S(1)}, u32[]{:S(2)}, u32[]{:S(2)}) collective-permute-start(f32[2,128]{1,0:T(2,128)S(1)} %collective-permute-done.9), channel_id=1, source_target_pairs={{0,1},{1,0},{2,3},{3,2},{4,5},{5,4},{6,7},{7,6},{8,9},{9,8},{10,11... | collective-permute-start | bytes 3080 | tf_op jit(solution)/shard_map/ppermute | solution.py:35

commit v26 on v25

--- a/solution.py
+++ b/solution.py
@@ -210,7 +210,7 @@
         trips.append([(2 * a + way, 2 * b + way) for way, route in ways for a, b in route])
     visitors = [lax.ppermute(line, line_axes, trip) for trip in trips]
 
-    partners = [(s, s + 1) for s in range(1, groups - 1, 2)]
+    partners = [(s + 1, s) for s in range(1, groups - 1, 2)]
     arrived = [lax.ppermute(both, plane_axes, group_trip(groups, *way)) for way in partners]
     last = groups - 1
     relay = group_trip(groups, last ^ partners[-1][0], last ^ partners[-1][1])

time: 55.2 us -> 55.2 us (level)
  transfers between devices with their start and end apart: 15 -> 15, of which waited for: 7 -> 8; matrix products, arithmetic and copies ran while one was open for 1% -> 1% of each run, Pallas kernels for 4% -> 4%
where the time goes in v26:
time: 55.2 us; the launch traced here: 54.9 us
  waiting for transfers between devices  30.7 us (56%)
  starting transfers between devices  16.9 us (31%)
  Pallas kernels  4.83 us (9%)
  other arithmetic  1.2 us (2%)
  local copies, waits for them, and re-layouts  1.19 us (2%)
    ppermute x1, waiting for transfers between devices, local(): lax.ppermute(both, plane_axes, group_trip(groups, *way))  14.3 us
    ppermute x2, waiting for transfers between devices, local(): corner = [lax.ppermute(part, plane_axes, relay) for part in corner]  10.2 us
    ppermute x1, starting transfers between devices, local(): visitors = [lax.ppermute(line, line_axes, trip) for trip in trips]  4.58 us
    pallas_call x2, Pallas kernels, call(): pl.pallas_call(kernel, in_specs=[VMEM] * len(operands), out_specs=[VMEM]...  3.85 us
    ppermute x1, starting transfers between devices, local(): lax.ppermute(both, plane_axes, group_trip(groups, *way))  3.03 us
    ppermute x7, waiting for transfers between devices, swap(): return lax.ppermute(block, 'core', flip(2, 1))  2.88 us
    ppermute x2, starting transfers between devices, local(): got = lax.ppermute(merged[chunk], plane_axes, group_trip(groups, *order))  2.48 us
    ppermute x1, waiting for transfers between devices, local(): visitors = [lax.ppermute(line, line_axes, trip) for trip in trips]  2.26 us
  transfers between devices with their start and end apart: 15, of which 8 were waited for; matrix products, arithmetic and copies ran while one was open for 1% of the time, Pallas kernels for 4%

profile of v26, /device:TPU:0, one launch (start us, length us, event | category | flops | bytes accessed | tf_op | source)
XLA Modules:
  0.0 54.9 jit_solution(7282150609387437528)
XLA Ops:
  0.0 0.5 collective-permute-start
  0.5 0.7 %pad_add_fusion.ids_ref.own_ids_ref = s32[2,96]{1,0:T(2,128)S(1)} fusion(s32[1,96]{1,0:T(1,128)} %bitcast.4, s32[1,96]{1,0:T(1,128)} %bitcast.5), kind=kLoop, calls=%fused_computation | loop fusion | flops 192 | bytes 1536 | tf_op jit(solution)/shard_map/stack | solution.py:201
  1.2 1.1 %copy-done = bf16[96,4096]{1,0:T(8,128)(2,1)S(1)} copy-done((bf16[96,4096]{1,0:T(8,128)(2,1)S(1)}, bf16[96,4096]{1,0:T(8,128)(2,1)}, u32[]{:S(2)}) %copy-start) | copy-done | bytes 786456
  2.3 0.3 shard_map.37.own_ref.refs_0_
  2.6 0.7 %shard_map.38 = (bf16[192,4224]{1,0:T(8,128)(2,1)S(1)}, bf16[6160,128]{1,0:T(8,128)(2,1)S(1)}) custom-call(bf16[96,4224]{1,0:T(8,128)(2,1)S(1)} %shard_map.37.own_ref.refs_0_, s32[2,96]{1,0:T(2,128)S(1)} %pad_add_fusion.ids_ref.own_ids_ref, bf16[96,4096]{1,0:T(8,128)(2,1)S(1)} %collective-permute-done.rows_ref, s32[2,96]{1,0:T(2,128)S(1)} %collective-permute-done.1.ids_ref), custom_call_target="tpu_custom_call" | custom-call | flops 1572864 | bytes 1572864 | tf_op jit(solution)/shard_map/pallas_call | solution.py:77
  3.3 3.0 %collective-permute-start.2 = (bf16[192,4224]{1,0:T(8,128)(2,1)S(1)}, bf16[192,4224]{1,0:T(8,128)(2,1)S(1)}, u32[]{:S(2)}, u32[]{:S(2)}) collective-permute-start(bf16[192,4224]{1,0:T(8,128)(2,1)S(1)} %get-tuple-element.10.refs_1_), channel_id=1, source_target_pairs={{0,16},{1,9},{8,24},{9,1},{16,0},{17,25},{24,8},{25,17},{2,18},{3,... | collective-permute-start | bytes 4866056 | tf_op jit(solution)/shard_map/ppermute | solution.py:214
  6.4 4.6 %collective-permute-start.8 = (bf16[6160,128]{1,0:T(8,128)(2,1)S(1)}, bf16[6160,128]{1,0:T(8,128)(2,1)S(1)}, u32[]{:S(2)}, u32[]{:S(2)}) collective-permute-start(bf16[6160,128]{1,0:T(8,128)(2,1)S(1)} %get-tuple-element.11), channel_id=1, source_target_pairs={{0,4},{6,2},{1,3},{3,5},{5,7},{7,1},{8,12},{14,10},{9,11},{11,13},... | collective-permute-start | bytes 4730888 | tf_op jit(solution)/shard_map/ppermute | solution.py:211
  11.0 14.3 %collective-permute-done.2.refs_2_ = bf16[192,4224]{1,0:T(8,128)(2,1)S(1)} collective-permute-done((bf16[192,4224]{1,0:T(8,128)(2,1)S(1)}, bf16[192,4224]{1,0:T(8,128)(2,1)S(1)}, u32[]{:S(2)}, u32[]{:S(2)}) %collective-permute-start.2) | collective-permute-done | bytes 1622048 | tf_op jit(solution)/shard_map/ppermute | solution.py:214
  25.4 2.1 %collective-permute-start.4 = (bf16[48,4224]{1,0:T(8,128)(2,1)S(1)}, bf16[48,4224]{1,0:T(8,128)(2,1)S(1)}, u32[]{:S(2)}, u32[]{:S(2)}) collective-permute-start(bf16[48,4224]{1,0:T(8,128)(2,1)S(1)} %get-tuple-element.16), channel_id=1, source_target_pairs={{0,8},{1,17},{8,0},{9,25},{16,24},{17,1},{24,16},{25,9},{2,10},{3,... | collective-permute-start | bytes 1216520 | tf_op jit(solution)/shard_map/ppermute | solution.py:219
  27.5 5.8 %collective-permute-done.4.refs_4_ = bf16[48,4224]{1,0:T(8,128)(2,1)S(1)} collective-permute-done((bf16[48,4224]{1,0:T(8,128)(2,1)S(1)}, bf16[48,4224]{1,0:T(8,128)(2,1)S(1)}, u32[]{:S(2)}, u32[]{:S(2)}) %collective-permute-start.4) | collective-permute-done | bytes 405536 | tf_op jit(solution)/shard_map/ppermute | solution.py:219
  33.3 4.3 %collective-permute-done.5.refs_5_ = bf16[48,4224]{1,0:T(8,128)(2,1)S(1)} collective-permute-done((bf16[48,4224]{1,0:T(8,128)(2,1)S(1)}, bf16[48,4224]{1,0:T(8,128)(2,1)S(1)}, u32[]{:S(2)}, u32[]{:S(2)}) %collective-permute-start.5) | collective-permute-done | bytes 405536 | tf_op jit(solution)/shard_map/ppermute | solution.py:219
  37.7 1.7 %collective-permute-done.7.refs_7_ = bf16[48,4224]{1,0:T(8,128)(2,1)S(1)} collective-permute-done((bf16[48,4224]{1,0:T(8,128)(2,1)S(1)}, bf16[48,4224]{1,0:T(8,128)(2,1)S(1)}, u32[]{:S(2)}, u32[]{:S(2)}) %collective-permute-start.7) | collective-permute-done | bytes 405536 | tf_op jit(solution)/shard_map/ppermute | solution.py:35
  39.4 1.8 %shard_map.39.refs_8_ = f32[1,128]{1,0:T(1,128)S(1)} custom-call(bf16[96,4224]{1,0:T(8,128)(2,1)S(1)} %shard_map.37.own_ref.refs_0_, bf16[192,4224]{1,0:T(8,128)(2,1)S(1)} %get-tuple-element.10.refs_1_, bf16[192,4224]{1,0:T(8,128)(2,1)S(1)} %collective-permute-done.2.refs_2_, bf16[192,4224]{1,0:T(8,128)(2,1)S(1)} %collective-permute-done.3.refs_3_, ...), custom_call_target="tpu_custom_call" | custom-call | flops 805306368 | bytes 7340032 | tf_op jit(solution)/shard_map/pallas_call | solution.py:177
  41.2 2.3 %collective-permute-done.8.refs_0_ = bf16[6160,128]{1,0:T(8,128)(2,1)S(1)} collective-permute-done((bf16[6160,128]{1,0:T(8,128)(2,1)S(1)}, bf16[6160,128]{1,0:T(8,128)(2,1)S(1)}, u32[]{:S(2)}, u32[]{:S(2)}) %collective-permute-start.8) | collective-permute-done | bytes 1576992 | tf_op jit(solution)/shard_map/ppermute | solution.py:211
  43.5 2.1 %shard_map.40 = (f32[2,128]{1,0:T(2,128)S(1)}, f32[4,128]{1,0:T(4,128)S(1)}, f32[4,128]{1,0:T(4,128)S(1)}) custom-call(bf16[6160,128]{1,0:T(8,128)(2,1)S(1)} %collective-permute-done.8.refs_0_, bf16[192,4224]{1,0:T(8,128)(2,1)S(1)} %get-tuple-element.10.refs_1_, bf16[192,4224]{1,0:T(8,128)(2,1)S(1)} %collective-permute-done.2.refs_2_, ...), custom_call_target="tpu_custom_call" | custom-call | flops 1610612736 | bytes 8388608 | tf_op jit(solution)/shard_map/pallas_call | solution.py:177
  45.5 1.2 %collective-permute-start.11 = (f32[4,128]{1,0:T(4,128)S(1)}, f32[4,128]{1,0:T(4,128)S(1)}, u32[]{:S(2)}, u32[]{:S(2)}) collective-permute-start(f32[4,128]{1,0:T(4,128)S(1)} %get-tuple-element.14), channel_id=1, source_target_pairs={{0,1},{1,0},{2,3},{3,2},{4,5},{5,4},{6,7},{7,6},{8,9},{9,8},{10,11... | collective-permute-start | bytes 6152 | tf_op jit(solution)/shard_map/ppermute | solution.py:35
  46.8 1.3 %collective-permute-start.9 = (f32[2,128]{1,0:T(2,128)S(1)}, f32[2,128]{1,0:T(2,128)S(1)}, u32[]{:S(2)}, u32[]{:S(2)}) collective-permute-start(f32[2,128]{1,0:T(2,128)S(1)} %get-tuple-element.12), channel_id=1, source_target_pairs={{4,0},{2,6},{3,1},{5,3},{7,5},{1,7},{12,8},{10,14},{11,9},{13,11},... | collective-permute-start | bytes 3080 | tf_op jit(solution)/shard_map/ppermute | solution.py:239
  48.1 1.6 %collective-permute-start.14 = (f32[4,128]{1,0:T(4,128)S(1)}, f32[4,128]{1,0:T(4,128)S(1)}, u32[]{:S(2)}, u32[]{:S(2)}) collective-permute-start(f32[4,128]{1,0:T(4,128)S(1)} %max.28), channel_id=1, source_target_pairs={{0,24},{8,16},{16,8},{24,0},{1,25},{9,17},{17,9},{25,1},{2,26},{10... | collective-permute-start | bytes 6152 | tf_op jit(solution)/shard_map/ppermute | solution.py:249
  49.7 1.1 %collective-permute-start.13 = (f32[4,128]{1,0:T(4,128)S(1)}, f32[4,128]{1,0:T(4,128)S(1)}, u32[]{:S(2)}, u32[]{:S(2)}) collective-permute-start(f32[4,128]{1,0:T(4,128)S(1)} %max.28), channel_id=1, source_target_pairs={{0,16},{1,9},{8,24},{9,1},{16,0},{17,25},{24,8},{25,17},{2,18},{3,... | collective-permute-start | bytes 6152 | tf_op jit(solution)/shard_map/ppermute | solution.py:247
  50.8 1.4 %collective-permute-start.12 = (f32[4,128]{1,0:T(4,128)S(1)}, f32[4,128]{1,0:T(4,128)S(1)}, u32[]{:S(2)}, u32[]{:S(2)}) collective-permute-start(f32[4,128]{1,0:T(4,128)S(1)} %max.28), channel_id=1, source_target_pairs={{0,8},{1,17},{8,0},{9,25},{16,24},{17,1},{24,16},{25,9},{2,10},{3,... | collective-permute-start | bytes 6152 | tf_op jit(solution)/shard_map/ppermute | solution.py:247
  52.2 0.9 %collective-permute-done.9 = f32[2,128]{1,0:T(2,128)S(1)} collective-permute-done((f32[2,128]{1,0:T(2,128)S(1)}, f32[2,128]{1,0:T(2,128)S(1)}, u32[]{:S(2)}, u32[]{:S(2)}) %collective-permute-start.9) | collective-permute-done | bytes 1056 | tf_op jit(solution)/shard_map/ppermute | solution.py:239
  53.1 1.1 %collective-permute-done.10 = f32[2,128]{1,0:T(2,128)S(1)} collective-permute-done((f32[2,128]{1,0:T(2,128)S(1)}, f32[2,128]{1,0:T(2,128)S(1)}, u32[]{:S(2)}, u32[]{:S(2)}) %collective-permute-start.10) | collective-permute-done | bytes 1056 | tf_op jit(solution)/shard_map/ppermute | solution.py:35
  54.3 0.1 collective-permute-done.12
  54.4 0.5 maximum_bitcast_fusion
  (16 shorter events, 0.2 us)
Async XLA Ops:
  0.0 2.6 %collective-permute-start = (bf16[96,4096]{1,0:T(8,128)(2,1)}, bf16[96,4096]{1,0:T(8,128)(2,1)S(1)}, u32[]{:S(2)}, u32[]{:S(2)}) collective-permute-start(bf16[96,4096]{1,0:T(8,128)(2,1)} %rows_ref.1), channel_id=1, source_target_pairs={{0,1},{1,0},{2,3},{3,2},{4,5},{5,4},{6,7},{7,6},{8,9},{9,8},{10,11... | collective-permute-start | bytes 2359304 | tf_op jit(solution)/shard_map/ppermute | solution.py:35
  1.1 1.5 %collective-permute-start.1 = (s32[2,96]{1,0:T(2,128)S(1)}, s32[2,96]{1,0:T(2,128)S(1)}, u32[]{:S(2)}, u32[]{:S(2)}) collective-permute-start(s32[2,96]{1,0:T(2,128)S(1)} %pad_add_fusion.ids_ref.own_ids_ref), channel_id=1, source_target_pairs={{0,1},{1,0},{2,3},{3,2},{4,5},{5,4},{6,7},{7,6},{8,9},{9,8},{10,11... | collective-permute-start | bytes 2312 | tf_op jit(solution)/shard_map/ppermute | solution.py:35
  1.2 1.1 %copy-start = (bf16[96,4096]{1,0:T(8,128)(2,1)S(1)}, bf16[96,4096]{1,0:T(8,128)(2,1)}, u32[]{:S(2)}) copy-start(bf16[96,4096]{1,0:T(8,128)(2,1)} %rows_ref.1) | copy-start | bytes 2359300
  3.3 22.0 %collective-permute-start.2 = (bf16[192,4224]{1,0:T(8,128)(2,1)S(1)}, bf16[192,4224]{1,0:T(8,128)(2,1)S(1)}, u32[]{:S(2)}, u32[]{:S(2)}) collective-permute-start(bf16[192,4224]{1,0:T(8,128)(2,1)S(1)} %get-tuple-element.10.refs_1_), channel_id=1, source_target_pairs={{0,16},{1,9},{8,24},{9,1},{16,0},{17,25},{24,8},{25,17},{2,18},{3,... | collective-permute-start | bytes 4866056 | tf_op jit(solution)/shard_map/ppermute | solution.py:214
  6.4 37.1 %collective-permute-start.8 = (bf16[6160,128]{1,0:T(8,128)(2,1)S(1)}, bf16[6160,128]{1,0:T(8,128)(2,1)S(1)}, u32[]{:S(2)}, u32[]{:S(2)}) collective-permute-start(bf16[6160,128]{1,0:T(8,128)(2,1)S(1)} %get-tuple-element.11), channel_id=1, source_target_pairs={{0,4},{6,2},{1,3},{3,5},{5,7},{7,1},{8,12},{14,10},{9,11},{11,13},... | collective-permute-start | bytes 4730888 | tf_op jit(solution)/shard_map/ppermute | solution.py:211
  25.3 14.1 %collective-permute-start.3 = (bf16[192,4224]{1,0:T(8,128)(2,1)S(1)}, bf16[192,4224]{1,0:T(8,128)(2,1)S(1)}, u32[]{:S(2)}, u32[]{:S(2)}) collective-permute-start(bf16[192,4224]{1,0:T(8,128)(2,1)S(1)} %collective-permute-done.2.refs_2_), channel_id=1, source_target_pairs={{0,1},{1,0},{2,3},{3,2},{4,5},{5,4},{6,7},{7,6},{8,9},{9,8},{10,11... | collective-permute-start | bytes 4866056 | tf_op jit(solution)/shard_map/ppermute | solution.py:35
  25.4 8.0 %collective-permute-start.4 = (bf16[48,4224]{1,0:T(8,128)(2,1)S(1)}, bf16[48,4224]{1,0:T(8,128)(2,1)S(1)}, u32[]{:S(2)}, u32[]{:S(2)}) collective-permute-start(bf16[48,4224]{1,0:T(8,128)(2,1)S(1)} %get-tuple-element.16), channel_id=1, source_target_pairs={{0,8},{1,17},{8,0},{9,25},{16,24},{17,1},{24,16},{25,9},{2,10},{3,... | collective-permute-start | bytes 1216520 | tf_op jit(solution)/shard_map/ppermute | solution.py:219
  27.4 10.3 %collective-permute-start.5 = (bf16[48,4224]{1,0:T(8,128)(2,1)S(1)}, bf16[48,4224]{1,0:T(8,128)(2,1)S(1)}, u32[]{:S(2)}, u32[]{:S(2)}) collective-permute-start(bf16[48,4224]{1,0:T(8,128)(2,1)S(1)} %get-tuple-element.15), channel_id=1, source_target_pairs={{0,8},{1,17},{8,0},{9,25},{16,24},{17,1},{24,16},{25,9},{2,10},{3,... | collective-permute-start | bytes 1216520 | tf_op jit(solution)/shard_map/ppermute | solution.py:219
  33.3 4.4 %collective-permute-start.6 = (bf16[48,4224]{1,0:T(8,128)(2,1)S(1)}, bf16[48,4224]{1,0:T(8,128)(2,1)S(1)}, u32[]{:S(2)}, u32[]{:S(2)}) collective-permute-start(bf16[48,4224]{1,0:T(8,128)(2,1)S(1)} %collective-permute-done.4.refs_4_), channel_id=1, source_target_pairs={{0,1},{1,0},{2,3},{3,2},{4,5},{5,4},{6,7},{7,6},{8,9},{9,8},{10,11... | collective-permute-start | bytes 1216520 | tf_op jit(solution)/shard_map/ppermute | solution.py:35
  37.7 1.7 %collective-permute-start.7 = (bf16[48,4224]{1,0:T(8,128)(2,1)S(1)}, bf16[48,4224]{1,0:T(8,128)(2,1)S(1)}, u32[]{:S(2)}, u32[]{:S(2)}) collective-permute-start(bf16[48,4224]{1,0:T(8,128)(2,1)S(1)} %collective-permute-done.5.refs_5_), channel_id=1, source_target_pairs={{0,1},{1,0},{2,3},{3,2},{4,5},{5,4},{6,7},{7,6},{8,9},{9,8},{10,11... | collective-permute-start | bytes 1216520 | tf_op jit(solution)/shard_map/ppermute | solution.py:35
  45.5 2.5 %collective-permute-start.11 = (f32[4,128]{1,0:T(4,128)S(1)}, f32[4,128]{1,0:T(4,128)S(1)}, u32[]{:S(2)}, u32[]{:S(2)}) collective-permute-start(f32[4,128]{1,0:T(4,128)S(1)} %get-tuple-element.14), channel_id=1, source_target_pairs={{0,1},{1,0},{2,3},{3,2},{4,5},{5,4},{6,7},{7,6},{8,9},{9,8},{10,11... | collective-permute-start | bytes 6152 | tf_op jit(solution)/shard_map/ppermute | solution.py:35
  46.8 6.3 %collective-permute-start.9 = (f32[2,128]{1,0:T(2,128)S(1)}, f32[2,128]{1,0:T(2,128)S(1)}, u32[]{:S(2)}, u32[]{:S(2)}) collective-permute-start(f32[2,128]{1,0:T(2,128)S(1)} %get-tuple-element.12), channel_id=1, source_target_pairs={{4,0},{2,6},{3,1},{5,3},{7,5},{1,7},{12,8},{10,14},{11,9},{13,11},... | collective-permute-start | bytes 3080 | tf_op jit(solution)/shard_map/ppermute | solution.py:239
  48.1 6.2 %collective-permute-start.14 = (f32[4,128]{1,0:T(4,128)S(1)}, f32[4,128]{1,0:T(4,128)S(1)}, u32[]{:S(2)}, u32[]{:S(2)}) collective-permute-start(f32[4,128]{1,0:T(4,128)S(1)} %max.28), channel_id=1, source_target_pairs={{0,24},{8,16},{16,8},{24,0},{1,25},{9,17},{17,9},{25,1},{2,26},{10... | collective-permute-start | bytes 6152 | tf_op jit(solution)/shard_map/ppermute | solution.py:249
  49.7 4.6 %collective-permute-start.13 = (f32[4,128]{1,0:T(4,128)S(1)}, f32[4,128]{1,0:T(4,128)S(1)}, u32[]{:S(2)}, u32[]{:S(2)}) collective-permute-start(f32[4,128]{1,0:T(4,128)S(1)} %max.28), channel_id=1, source_target_pairs={{0,16},{1,9},{8,24},{9,1},{16,0},{17,25},{24,8},{25,17},{2,18},{3,... | collective-permute-start | bytes 6152 | tf_op jit(solution)/shard_map/ppermute | solution.py:247
  50.8 3.6 %collective-permute-start.12 = (f32[4,128]{1,0:T(4,128)S(1)}, f32[4,128]{1,0:T(4,128)S(1)}, u32[]{:S(2)}, u32[]{:S(2)}) collective-permute-start(f32[4,128]{1,0:T(4,128)S(1)} %max.28), channel_id=1, source_target_pairs={{0,8},{1,17},{8,0},{9,25},{16,24},{17,1},{24,16},{25,9},{2,10},{3,... | collective-permute-start | bytes 6152 | tf_op jit(solution)/shard_map/ppermute | solution.py:247
  53.1 1.1 %collective-permute-start.10 = (f32[2,128]{1,0:T(2,128)S(1)}, f32[2,128]{1,0:T(2,128)S(1)}, u32[]{:S(2)}, u32[]{:S(2)}) collective-permute-start(f32[2,128]{1,0:T(2,128)S(1)} %collective-permute-done.9), channel_id=1, source_target_pairs={{0,1},{1,0},{2,3},{3,2},{4,5},{5,4},{6,7},{7,6},{8,9},{9,8},{10,11... | collective-permute-start | bytes 3080 | tf_op jit(solution)/shard_map/ppermute | solution.py:35

commit v27 on v25

--- a/solution.py
+++ b/solution.py
@@ -148,22 +148,27 @@
         dots[...] = part if k == 0 else dots[...] + part
 
     tails = jnp.concatenate([ref[:, width:] for ref in block_refs], axis=0).astype(jnp.float32)
-    row_best = [jnp.full((1, LANES), -1.0, jnp.float32) for _ in meta]
+    lowest = jnp.full((rows, LANES), -1.0, jnp.float32)
+    row_best = [lowest for _ in meta]
     lane = lax.broadcasted_iota(jnp.int32, (rows, LANES), 1)
-    col_all = jnp.full((rows, LANES), -1.0, jnp.float32)
-    for j in range(dots.shape[0] // rows):
+    col_all = lowest
+    for j in range(tails.shape[0] // rows):
         tail = tails[j * rows : (j + 1) * rows]
         block_cluster, block_order = tail[:, 0:1], tail[:, 1:2] * 256.0 + tail[:, 2:3]
-        col_best = jnp.full((rows, 1), -1.0, jnp.float32)
+        col_best = lowest
         for v, (cluster, order) in enumerate(meta):
-            cosine = dots[j * rows : (j + 1) * rows, v * LANES : (v + 1) * LANES]
-            same = (block_cluster == cluster) & (cluster > 0)
-            seen = jnp.where(same & (block_order < order), cosine, -1.0)
-            row_best[v] = jnp.maximum(row_best[v], jnp.max(seen, axis=0, keepdims=True))
+            cosine = jnp.where(
+                block_cluster == cluster,
+                dots[j * rows : (j + 1) * rows, v * LANES : (v + 1) * LANES],
+                -1.0,
+            )
+            seen = jnp.where(block_order < order, cosine, -1.0)
+            row_best[v] = jnp.maximum(row_best[v], seen)
             if homed:
-                seen = jnp.where(same & (order < block_order), cosine, -1.0)
-                col_best = jnp.maximum(col_best, jnp.max(seen, axis=1, keepdims=True))
-        col_all = jnp.where(lane == j, col_best, col_all)
+                col_best = jnp.maximum(col_best, jnp.where(order < block_order, cosine, -1.0))
+        if homed:
+            col_all = jnp.where(lane == j, jnp.max(col_best, axis=1, keepdims=True), col_all)
+    row_best = [jnp.max(best, axis=0, keepdims=True) for best in row_best]
     if not homed:
         return row_best, None
     if rows < LANES:

time: 55.2 us -> 55.1 us (level)
  no operation moved by 1% of the time
where the time goes in v27:
time: 55.1 us; the launch traced here: 54.8 us
  waiting for transfers between devices  30.7 us (56%)
  starting transfers between devices  16.9 us (31%)
  Pallas kernels  4.78 us (9%)
  other arithmetic  1.2 us (2%)
  local copies, waits for them, and re-layouts  1.19 us (2%)
    ppermute x1, waiting for transfers between devices, local(): lax.ppermute(both, plane_axes, group_trip(groups, *way))  14.3 us
    ppermute x2, waiting for transfers between devices, local(): corner = [lax.ppermute(part, plane_axes, relay) for part in corner]  10.2 us
    ppermute x1, starting transfers between devices, local(): visitors = [lax.ppermute(line, line_axes, trip) for trip in trips]  4.58 us
    pallas_call x2, Pallas kernels, call(): pl.pallas_call(kernel, in_specs=[VMEM] * len(operands), out_specs=[VMEM]...  3.8 us
    ppermute x1, starting transfers between devices, local(): lax.ppermute(both, plane_axes, group_trip(groups, *way))  3 us
    ppermute x7, waiting for transfers between devices, swap(): return lax.ppermute(block, 'core', flip(2, 1))  2.88 us
    ppermute x2, starting transfers between devices, local(): got = lax.ppermute(merged[chunk], plane_axes, group_trip(groups, *order))  2.58 us
    ppermute x1, waiting for transfers between devices, local(): visitors = [lax.ppermute(line, line_axes, trip) for trip in trips]  2.29 us
  transfers between devices with their start and end apart: 15, of which 7 were waited for; matrix products, arithmetic and copies ran while one was open for 1% of the time, Pallas kernels for 4%

profile of v27, /device:TPU:0, one launch (start us, length us, event | category | flops | bytes accessed | tf_op | source)
XLA Modules:
  0.0 54.8 jit_solution(10182244760714790183)
XLA Ops:
  0.0 0.5 collective-permute-start
  0.5 0.7 %pad_add_fusion.ids_ref.own_ids_ref = s32[2,96]{1,0:T(2,128)S(1)} fusion(s32[1,96]{1,0:T(1,128)} %bitcast.4, s32[1,96]{1,0:T(1,128)} %bitcast.5), kind=kLoop, calls=%fused_computation | loop fusion | flops 192 | bytes 1536 | tf_op jit(solution)/shard_map/stack | solution.py:206
  1.2 1.1 %copy-done = bf16[96,4096]{1,0:T(8,128)(2,1)S(1)} copy-done((bf16[96,4096]{1,0:T(8,128)(2,1)S(1)}, bf16[96,4096]{1,0:T(8,128)(2,1)}, u32[]{:S(2)}) %copy-start) | copy-done | bytes 786456
  2.3 0.3 shard_map.37.own_ref.refs_0_
  2.6 0.7 %shard_map.38 = (bf16[192,4224]{1,0:T(8,128)(2,1)S(1)}, bf16[6160,128]{1,0:T(8,128)(2,1)S(1)}) custom-call(bf16[96,4224]{1,0:T(8,128)(2,1)S(1)} %shard_map.37.own_ref.refs_0_, s32[2,96]{1,0:T(2,128)S(1)} %pad_add_fusion.ids_ref.own_ids_ref, bf16[96,4096]{1,0:T(8,128)(2,1)S(1)} %collective-permute-done.rows_ref, s32[2,96]{1,0:T(2,128)S(1)} %collective-permute-done.1.ids_ref), custom_call_target="tpu_custom_call" | custom-call | flops 1572864 | bytes 1572864 | tf_op jit(solution)/shard_map/pallas_call | solution.py:77
  3.3 3.0 %collective-permute-start.2 = (bf16[192,4224]{1,0:T(8,128)(2,1)S(1)}, bf16[192,4224]{1,0:T(8,128)(2,1)S(1)}, u32[]{:S(2)}, u32[]{:S(2)}) collective-permute-start(bf16[192,4224]{1,0:T(8,128)(2,1)S(1)} %get-tuple-element.10.refs_1_), channel_id=1, source_target_pairs={{0,8},{1,17},{8,0},{9,25},{16,24},{17,1},{24,16},{25,9},{2,10},{3,... | collective-permute-start | bytes 4866056 | tf_op jit(solution)/shard_map/ppermute | solution.py:219
  6.3 4.6 %collective-permute-start.8 = (bf16[6160,128]{1,0:T(8,128)(2,1)S(1)}, bf16[6160,128]{1,0:T(8,128)(2,1)S(1)}, u32[]{:S(2)}, u32[]{:S(2)}) collective-permute-start(bf16[6160,128]{1,0:T(8,128)(2,1)S(1)} %get-tuple-element.11), channel_id=1, source_target_pairs={{0,4},{6,2},{1,3},{3,5},{5,7},{7,1},{8,12},{14,10},{9,11},{11,13},... | collective-permute-start | bytes 4730888 | tf_op jit(solution)/shard_map/ppermute | solution.py:216
  10.9 14.3 %collective-permute-done.2.refs_2_ = bf16[192,4224]{1,0:T(8,128)(2,1)S(1)} collective-permute-done((bf16[192,4224]{1,0:T(8,128)(2,1)S(1)}, bf16[192,4224]{1,0:T(8,128)(2,1)S(1)}, u32[]{:S(2)}, u32[]{:S(2)}) %collective-permute-start.2) | collective-permute-done | bytes 1622048 | tf_op jit(solution)/shard_map/ppermute | solution.py:219
  25.3 2.1 %collective-permute-start.4 = (bf16[48,4224]{1,0:T(8,128)(2,1)S(1)}, bf16[48,4224]{1,0:T(8,128)(2,1)S(1)}, u32[]{:S(2)}, u32[]{:S(2)}) collective-permute-start(bf16[48,4224]{1,0:T(8,128)(2,1)S(1)} %get-tuple-element.16), channel_id=1, source_target_pairs={{0,16},{1,9},{8,24},{9,1},{16,0},{17,25},{24,8},{25,17},{2,18},{3,... | collective-permute-start | bytes 1216520 | tf_op jit(solution)/shard_map/ppermute | solution.py:224
  27.4 0.1 collective-permute-start.5
  27.5 5.8 %collective-permute-done.4.refs_4_ = bf16[48,4224]{1,0:T(8,128)(2,1)S(1)} collective-permute-done((bf16[48,4224]{1,0:T(8,128)(2,1)S(1)}, bf16[48,4224]{1,0:T(8,128)(2,1)S(1)}, u32[]{:S(2)}, u32[]{:S(2)}) %collective-permute-start.4) | collective-permute-done | bytes 405536 | tf_op jit(solution)/shard_map/ppermute | solution.py:224
  33.3 4.3 %collective-permute-done.5.refs_5_ = bf16[48,4224]{1,0:T(8,128)(2,1)S(1)} collective-permute-done((bf16[48,4224]{1,0:T(8,128)(2,1)S(1)}, bf16[48,4224]{1,0:T(8,128)(2,1)S(1)}, u32[]{:S(2)}, u32[]{:S(2)}) %collective-permute-start.5) | collective-permute-done | bytes 405536 | tf_op jit(solution)/shard_map/ppermute | solution.py:224
  37.7 1.7 %collective-permute-done.7.refs_7_ = bf16[48,4224]{1,0:T(8,128)(2,1)S(1)} collective-permute-done((bf16[48,4224]{1,0:T(8,128)(2,1)S(1)}, bf16[48,4224]{1,0:T(8,128)(2,1)S(1)}, u32[]{:S(2)}, u32[]{:S(2)}) %collective-permute-start.7) | collective-permute-done | bytes 405536 | tf_op jit(solution)/shard_map/ppermute | solution.py:35
  39.4 1.8 %shard_map.39.refs_8_ = f32[1,128]{1,0:T(1,128)S(1)} custom-call(bf16[96,4224]{1,0:T(8,128)(2,1)S(1)} %shard_map.37.own_ref.refs_0_, bf16[192,4224]{1,0:T(8,128)(2,1)S(1)} %get-tuple-element.10.refs_1_, bf16[192,4224]{1,0:T(8,128)(2,1)S(1)} %collective-permute-done.2.refs_2_, bf16[192,4224]{1,0:T(8,128)(2,1)S(1)} %collective-permute-done.3.refs_3_, ...), custom_call_target="tpu_custom_call" | custom-call | flops 805306368 | bytes 7340032 | tf_op jit(solution)/shard_map/pallas_call | solution.py:182
  41.2 2.3 %collective-permute-done.8.refs_0_ = bf16[6160,128]{1,0:T(8,128)(2,1)S(1)} collective-permute-done((bf16[6160,128]{1,0:T(8,128)(2,1)S(1)}, bf16[6160,128]{1,0:T(8,128)(2,1)S(1)}, u32[]{:S(2)}, u32[]{:S(2)}) %collective-permute-start.8) | collective-permute-done | bytes 1576992 | tf_op jit(solution)/shard_map/ppermute | solution.py:216
  43.5 2.0 %shard_map.40 = (f32[2,128]{1,0:T(2,128)S(1)}, f32[4,128]{1,0:T(4,128)S(1)}, f32[4,128]{1,0:T(4,128)S(1)}) custom-call(bf16[6160,128]{1,0:T(8,128)(2,1)S(1)} %collective-permute-done.8.refs_0_, bf16[192,4224]{1,0:T(8,128)(2,1)S(1)} %get-tuple-element.10.refs_1_, bf16[192,4224]{1,0:T(8,128)(2,1)S(1)} %collective-permute-done.2.refs_2_, ...), custom_call_target="tpu_custom_call" | custom-call | flops 1610612736 | bytes 8388608 | tf_op jit(solution)/shard_map/pallas_call | solution.py:182
  45.5 1.3 %collective-permute-start.11 = (f32[4,128]{1,0:T(4,128)S(1)}, f32[4,128]{1,0:T(4,128)S(1)}, u32[]{:S(2)}, u32[]{:S(2)}) collective-permute-start(f32[4,128]{1,0:T(4,128)S(1)} %get-tuple-element.14), channel_id=1, source_target_pairs={{0,1},{1,0},{2,3},{3,2},{4,5},{5,4},{6,7},{7,6},{8,9},{9,8},{10,11... | collective-permute-start | bytes 6152 | tf_op jit(solution)/shard_map/ppermute | solution.py:35
  46.8 1.3 %collective-permute-start.9 = (f32[2,128]{1,0:T(2,128)S(1)}, f32[2,128]{1,0:T(2,128)S(1)}, u32[]{:S(2)}, u32[]{:S(2)}) collective-permute-start(f32[2,128]{1,0:T(2,128)S(1)} %get-tuple-element.12), channel_id=1, source_target_pairs={{4,0},{2,6},{3,1},{5,3},{7,5},{1,7},{12,8},{10,14},{11,9},{13,11},... | collective-permute-start | bytes 3080 | tf_op jit(solution)/shard_map/ppermute | solution.py:244
  48.1 1.4 %collective-permute-start.14 = (f32[4,128]{1,0:T(4,128)S(1)}, f32[4,128]{1,0:T(4,128)S(1)}, u32[]{:S(2)}, u32[]{:S(2)}) collective-permute-start(f32[4,128]{1,0:T(4,128)S(1)} %max.28), channel_id=1, source_target_pairs={{0,24},{8,16},{16,8},{24,0},{1,25},{9,17},{17,9},{25,1},{2,26},{10... | collective-permute-start | bytes 6152 | tf_op jit(solution)/shard_map/ppermute | solution.py:254
  49.5 1.2 %collective-permute-start.13 = (f32[4,128]{1,0:T(4,128)S(1)}, f32[4,128]{1,0:T(4,128)S(1)}, u32[]{:S(2)}, u32[]{:S(2)}) collective-permute-start(f32[4,128]{1,0:T(4,128)S(1)} %max.28), channel_id=1, source_target_pairs={{0,8},{1,17},{8,0},{9,25},{16,24},{17,1},{24,16},{25,9},{2,10},{3,... | collective-permute-start | bytes 6152 | tf_op jit(solution)/shard_map/ppermute | solution.py:252
  50.7 1.4 %collective-permute-start.12 = (f32[4,128]{1,0:T(4,128)S(1)}, f32[4,128]{1,0:T(4,128)S(1)}, u32[]{:S(2)}, u32[]{:S(2)}) collective-permute-start(f32[4,128]{1,0:T(4,128)S(1)} %max.28), channel_id=1, source_target_pairs={{0,16},{1,9},{8,24},{9,1},{16,0},{17,25},{24,8},{25,17},{2,18},{3,... | collective-permute-start | bytes 6152 | tf_op jit(solution)/shard_map/ppermute | solution.py:252
  52.1 1.0 %collective-permute-done.9 = f32[2,128]{1,0:T(2,128)S(1)} collective-permute-done((f32[2,128]{1,0:T(2,128)S(1)}, f32[2,128]{1,0:T(2,128)S(1)}, u32[]{:S(2)}, u32[]{:S(2)}) %collective-permute-start.9) | collective-permute-done | bytes 1056 | tf_op jit(solution)/shard_map/ppermute | solution.py:244
  53.2 1.1 %collective-permute-done.10 = f32[2,128]{1,0:T(2,128)S(1)} collective-permute-done((f32[2,128]{1,0:T(2,128)S(1)}, f32[2,128]{1,0:T(2,128)S(1)}, u32[]{:S(2)}, u32[]{:S(2)}) %collective-permute-start.10) | collective-permute-done | bytes 1056 | tf_op jit(solution)/shard_map/ppermute | solution.py:35
  54.3 0.5 maximum_bitcast_fusion
  (16 shorter events, 0.2 us)
Async XLA Ops:
  0.0 2.6 %collective-permute-start = (bf16[96,4096]{1,0:T(8,128)(2,1)}, bf16[96,4096]{1,0:T(8,128)(2,1)S(1)}, u32[]{:S(2)}, u32[]{:S(2)}) collective-permute-start(bf16[96,4096]{1,0:T(8,128)(2,1)} %rows_ref.1), channel_id=1, source_target_pairs={{0,1},{1,0},{2,3},{3,2},{4,5},{5,4},{6,7},{7,6},{8,9},{9,8},{10,11... | collective-permute-start | bytes 2359304 | tf_op jit(solution)/shard_map/ppermute | solution.py:35
  1.1 1.5 %collective-permute-start.1 = (s32[2,96]{1,0:T(2,128)S(1)}, s32[2,96]{1,0:T(2,128)S(1)}, u32[]{:S(2)}, u32[]{:S(2)}) collective-permute-start(s32[2,96]{1,0:T(2,128)S(1)} %pad_add_fusion.ids_ref.own_ids_ref), channel_id=1, source_target_pairs={{0,1},{1,0},{2,3},{3,2},{4,5},{5,4},{6,7},{7,6},{8,9},{9,8},{10,11... | collective-permute-start | bytes 2312 | tf_op jit(solution)/shard_map/ppermute | solution.py:35
  1.2 1.1 %copy-start = (bf16[96,4096]{1,0:T(8,128)(2,1)S(1)}, bf16[96,4096]{1,0:T(8,128)(2,1)}, u32[]{:S(2)}) copy-start(bf16[96,4096]{1,0:T(8,128)(2,1)} %rows_ref.1) | copy-start | bytes 2359300
  3.3 21.9 %collective-permute-start.2 = (bf16[192,4224]{1,0:T(8,128)(2,1)S(1)}, bf16[192,4224]{1,0:T(8,128)(2,1)S(1)}, u32[]{:S(2)}, u32[]{:S(2)}) collective-permute-start(bf16[192,4224]{1,0:T(8,128)(2,1)S(1)} %get-tuple-element.10.refs_1_), channel_id=1, source_target_pairs={{0,8},{1,17},{8,0},{9,25},{16,24},{17,1},{24,16},{25,9},{2,10},{3,... | collective-permute-start | bytes 4866056 | tf_op jit(solution)/shard_map/ppermute | solution.py:219
  6.3 37.2 %collective-permute-start.8 = (bf16[6160,128]{1,0:T(8,128)(2,1)S(1)}, bf16[6160,128]{1,0:T(8,128)(2,1)S(1)}, u32[]{:S(2)}, u32[]{:S(2)}) collective-permute-start(bf16[6160,128]{1,0:T(8,128)(2,1)S(1)} %get-tuple-element.11), channel_id=1, source_target_pairs={{0,4},{6,2},{1,3},{3,5},{5,7},{7,1},{8,12},{14,10},{9,11},{11,13},... | collective-permute-start | bytes 4730888 | tf_op jit(solution)/shard_map/ppermute | solution.py:216
  25.3 14.2 %collective-permute-start.3 = (bf16[192,4224]{1,0:T(8,128)(2,1)S(1)}, bf16[192,4224]{1,0:T(8,128)(2,1)S(1)}, u32[]{:S(2)}, u32[]{:S(2)}) collective-permute-start(bf16[192,4224]{1,0:T(8,128)(2,1)S(1)} %collective-permute-done.2.refs_2_), channel_id=1, source_target_pairs={{0,1},{1,0},{2,3},{3,2},{4,5},{5,4},{6,7},{7,6},{8,9},{9,8},{10,11... | collective-permute-start | bytes 4866056 | tf_op jit(solution)/shard_map/ppermute | solution.py:35
  25.3 8.0 %collective-permute-start.4 = (bf16[48,4224]{1,0:T(8,128)(2,1)S(1)}, bf16[48,4224]{1,0:T(8,128)(2,1)S(1)}, u32[]{:S(2)}, u32[]{:S(2)}) collective-permute-start(bf16[48,4224]{1,0:T(8,128)(2,1)S(1)} %get-tuple-element.16), channel_id=1, source_target_pairs={{0,16},{1,9},{8,24},{9,1},{16,0},{17,25},{24,8},{25,17},{2,18},{3,... | collective-permute-start | bytes 1216520 | tf_op jit(solution)/shard_map/ppermute | solution.py:224
  27.4 10.2 %collective-permute-start.5 = (bf16[48,4224]{1,0:T(8,128)(2,1)S(1)}, bf16[48,4224]{1,0:T(8,128)(2,1)S(1)}, u32[]{:S(2)}, u32[]{:S(2)}) collective-permute-start(bf16[48,4224]{1,0:T(8,128)(2,1)S(1)} %get-tuple-element.15), channel_id=1, source_target_pairs={{0,16},{1,9},{8,24},{9,1},{16,0},{17,25},{24,8},{25,17},{2,18},{3,... | collective-permute-start | bytes 1216520 | tf_op jit(solution)/shard_map/ppermute | solution.py:224
  33.3 4.4 %collective-permute-start.6 = (bf16[48,4224]{1,0:T(8,128)(2,1)S(1)}, bf16[48,4224]{1,0:T(8,128)(2,1)S(1)}, u32[]{:S(2)}, u32[]{:S(2)}) collective-permute-start(bf16[48,4224]{1,0:T(8,128)(2,1)S(1)} %collective-permute-done.4.refs_4_), channel_id=1, source_target_pairs={{0,1},{1,0},{2,3},{3,2},{4,5},{5,4},{6,7},{7,6},{8,9},{9,8},{10,11... | collective-permute-start | bytes 1216520 | tf_op jit(solution)/shard_map/ppermute | solution.py:35
  37.7 1.7 %collective-permute-start.7 = (bf16[48,4224]{1,0:T(8,128)(2,1)S(1)}, bf16[48,4224]{1,0:T(8,128)(2,1)S(1)}, u32[]{:S(2)}, u32[]{:S(2)}) collective-permute-start(bf16[48,4224]{1,0:T(8,128)(2,1)S(1)} %collective-permute-done.5.refs_5_), channel_id=1, source_target_pairs={{0,1},{1,0},{2,3},{3,2},{4,5},{5,4},{6,7},{7,6},{8,9},{9,8},{10,11... | collective-permute-start | bytes 1216520 | tf_op jit(solution)/shard_map/ppermute | solution.py:35
  45.5 2.6 %collective-permute-start.11 = (f32[4,128]{1,0:T(4,128)S(1)}, f32[4,128]{1,0:T(4,128)S(1)}, u32[]{:S(2)}, u32[]{:S(2)}) collective-permute-start(f32[4,128]{1,0:T(4,128)S(1)} %get-tuple-element.14), channel_id=1, source_target_pairs={{0,1},{1,0},{2,3},{3,2},{4,5},{5,4},{6,7},{7,6},{8,9},{9,8},{10,11... | collective-permute-start | bytes 6152 | tf_op jit(solution)/shard_map/ppermute | solution.py:35
  46.8 6.3 %collective-permute-start.9 = (f32[2,128]{1,0:T(2,128)S(1)}, f32[2,128]{1,0:T(2,128)S(1)}, u32[]{:S(2)}, u32[]{:S(2)}) collective-permute-start(f32[2,128]{1,0:T(2,128)S(1)} %get-tuple-element.12), channel_id=1, source_target_pairs={{4,0},{2,6},{3,1},{5,3},{7,5},{1,7},{12,8},{10,14},{11,9},{13,11},... | collective-permute-start | bytes 3080 | tf_op jit(solution)/shard_map/ppermute | solution.py:244
  48.1 6.2 %collective-permute-start.14 = (f32[4,128]{1,0:T(4,128)S(1)}, f32[4,128]{1,0:T(4,128)S(1)}, u32[]{:S(2)}, u32[]{:S(2)}) collective-permute-start(f32[4,128]{1,0:T(4,128)S(1)} %max.28), channel_id=1, source_target_pairs={{0,24},{8,16},{16,8},{24,0},{1,25},{9,17},{17,9},{25,1},{2,26},{10... | collective-permute-start | bytes 6152 | tf_op jit(solution)/shard_map/ppermute | solution.py:254
  49.5 4.8 %collective-permute-start.13 = (f32[4,128]{1,0:T(4,128)S(1)}, f32[4,128]{1,0:T(4,128)S(1)}, u32[]{:S(2)}, u32[]{:S(2)}) collective-permute-start(f32[4,128]{1,0:T(4,128)S(1)} %max.28), channel_id=1, source_target_pairs={{0,8},{1,17},{8,0},{9,25},{16,24},{17,1},{24,16},{25,9},{2,10},{3,... | collective-permute-start | bytes 6152 | tf_op jit(solution)/shard_map/ppermute | solution.py:252
  50.7 3.6 %collective-permute-start.12 = (f32[4,128]{1,0:T(4,128)S(1)}, f32[4,128]{1,0:T(4,128)S(1)}, u32[]{:S(2)}, u32[]{:S(2)}) collective-permute-start(f32[4,128]{1,0:T(4,128)S(1)} %max.28), channel_id=1, source_target_pairs={{0,16},{1,9},{8,24},{9,1},{16,0},{17,25},{24,8},{25,17},{2,18},{3,... | collective-permute-start | bytes 6152 | tf_op jit(solution)/shard_map/ppermute | solution.py:252
  53.2 1.1 %collective-permute-start.10 = (f32[2,128]{1,0:T(2,128)S(1)}, f32[2,128]{1,0:T(2,128)S(1)}, u32[]{:S(2)}, u32[]{:S(2)}) collective-permute-start(f32[2,128]{1,0:T(2,128)S(1)} %collective-permute-done.9), channel_id=1, source_target_pairs={{0,1},{1,0},{2,3},{3,2},{4,5},{5,4},{6,7},{7,6},{8,9},{9,8},{10,11... | collective-permute-start | bytes 3080 | tf_op jit(solution)/shard_map/ppermute | solution.py:35

commit v28 on v27

--- a/solution.py
+++ b/solution.py
@@ -248,7 +248,7 @@
     ways = [(0, 0, partners[-1])]
     ways += [(1 + k // 2, 2 * (k % 2), way) for k, way in enumerate(partners[:-1])]
     for chunk, row, (first, second) in ways:
-        for offset, order in ((1, (second, first)), (0, (first, second))):
+        for offset, order in ((0, (first, second)), (1, (second, first))):
             got = lax.ppermute(merged[chunk], plane_axes, group_trip(groups, *order))
             bests.append(got[row + offset, :rows])
     bests.append(lax.ppermute(merged[0], "group", flip(groups, last))[2, :rows])

time: 55.1 us -> 56.4 us (1.024)
  waiting for transfers between devices: 30.7 us -> 32.1 us
    ppermute x2, waiting for transfers between devices: 0.03 us -> 1.41 us  [local(): got = lax.ppermute(merged[chunk], plane_axes, group_trip(groups, *order))]
  transfers between devices with their start and end apart: 15 -> 15, of which waited for: 7 -> 8; matrix products, arithmetic and copies ran while one was open for 1% -> 1% of each run, Pallas kernels for 4% -> 4%
where the time goes in v28:
time: 56.4 us; the launch traced here: 56.2 us
  waiting for transfers between devices  32.1 us (57%)
  starting transfers between devices  16.9 us (30%)
  Pallas kernels  4.78 us (8%)
  other arithmetic  1.2 us (2%)
  local copies, waits for them, and re-layouts  1.19 us (2%)
    ppermute x1, waiting for transfers between devices, local(): lax.ppermute(both, plane_axes, group_trip(groups, *way))  14.3 us
    ppermute x2, waiting for transfers between devices, local(): corner = [lax.ppermute(part, plane_axes, relay) for part in corner]  10.2 us
    ppermute x1, starting transfers between devices, local(): visitors = [lax.ppermute(line, line_axes, trip) for trip in trips]  4.58 us
    pallas_call x2, Pallas kernels, call(): pl.pallas_call(kernel, in_specs=[VMEM] * len(operands), out_specs=[VMEM]...  3.8 us
    ppermute x1, starting transfers between devices, local(): lax.ppermute(both, plane_axes, group_trip(groups, *way))  3 us
    ppermute x7, waiting for transfers between devices, swap(): return lax.ppermute(block, 'core', flip(2, 1))  2.88 us
    ppermute x2, starting transfers between devices, local(): got = lax.ppermute(merged[chunk], plane_axes, group_trip(groups, *order))  2.58 us
    ppermute x1, waiting for transfers between devices, local(): visitors = [lax.ppermute(line, line_axes, trip) for trip in trips]  2.29 us
  transfers between devices with their start and end apart: 15, of which 8 were waited for; matrix products, arithmetic and copies ran while one was open for 1% of the time, Pallas kernels for 4%

profile of v28, /device:TPU:0, one launch (start us, length us, event | category | flops | bytes accessed | tf_op | source)
XLA Modules:
  0.0 56.2 jit_solution(11413683042853886683)
XLA Ops:
  0.0 0.5 collective-permute-start
  0.5 0.7 %pad_add_fusion.ids_ref.own_ids_ref = s32[2,96]{1,0:T(2,128)S(1)} fusion(s32[1,96]{1,0:T(1,128)} %bitcast.4, s32[1,96]{1,0:T(1,128)} %bitcast.5), kind=kLoop, calls=%fused_computation | loop fusion | flops 192 | bytes 1536 | tf_op jit(solution)/shard_map/stack | solution.py:206
  1.2 1.1 %copy-done = bf16[96,4096]{1,0:T(8,128)(2,1)S(1)} copy-done((bf16[96,4096]{1,0:T(8,128)(2,1)S(1)}, bf16[96,4096]{1,0:T(8,128)(2,1)}, u32[]{:S(2)}) %copy-start) | copy-done | bytes 786456
  2.3 0.3 shard_map.37.own_ref.refs_0_
  2.6 0.7 %shard_map.38 = (bf16[192,4224]{1,0:T(8,128)(2,1)S(1)}, bf16[6160,128]{1,0:T(8,128)(2,1)S(1)}) custom-call(bf16[96,4224]{1,0:T(8,128)(2,1)S(1)} %shard_map.37.own_ref.refs_0_, s32[2,96]{1,0:T(2,128)S(1)} %pad_add_fusion.ids_ref.own_ids_ref, bf16[96,4096]{1,0:T(8,128)(2,1)S(1)} %collective-permute-done.rows_ref, s32[2,96]{1,0:T(2,128)S(1)} %collective-permute-done.1.ids_ref), custom_call_target="tpu_custom_call" | custom-call | flops 1572864 | bytes 1572864 | tf_op jit(solution)/shard_map/pallas_call | solution.py:77
  3.3 3.0 %collective-permute-start.2 = (bf16[192,4224]{1,0:T(8,128)(2,1)S(1)}, bf16[192,4224]{1,0:T(8,128)(2,1)S(1)}, u32[]{:S(2)}, u32[]{:S(2)}) collective-permute-start(bf16[192,4224]{1,0:T(8,128)(2,1)S(1)} %get-tuple-element.10.refs_1_), channel_id=1, source_target_pairs={{0,8},{1,17},{8,0},{9,25},{16,24},{17,1},{24,16},{25,9},{2,10},{3,... | collective-permute-start | bytes 4866056 | tf_op jit(solution)/shard_map/ppermute | solution.py:219
  6.3 4.6 %collective-permute-start.8 = (bf16[6160,128]{1,0:T(8,128)(2,1)S(1)}, bf16[6160,128]{1,0:T(8,128)(2,1)S(1)}, u32[]{:S(2)}, u32[]{:S(2)}) collective-permute-start(bf16[6160,128]{1,0:T(8,128)(2,1)S(1)} %get-tuple-element.11), channel_id=1, source_target_pairs={{0,4},{6,2},{1,3},{3,5},{5,7},{7,1},{8,12},{14,10},{9,11},{11,13},... | collective-permute-start | bytes 4730888 | tf_op jit(solution)/shard_map/ppermute | solution.py:216
  10.9 14.3 %collective-permute-done.2.refs_2_ = bf16[192,4224]{1,0:T(8,128)(2,1)S(1)} collective-permute-done((bf16[192,4224]{1,0:T(8,128)(2,1)S(1)}, bf16[192,4224]{1,0:T(8,128)(2,1)S(1)}, u32[]{:S(2)}, u32[]{:S(2)}) %collective-permute-start.2) | collective-permute-done | bytes 1622048 | tf_op jit(solution)/shard_map/ppermute | solution.py:219
  25.3 2.1 %collective-permute-start.4 = (bf16[48,4224]{1,0:T(8,128)(2,1)S(1)}, bf16[48,4224]{1,0:T(8,128)(2,1)S(1)}, u32[]{:S(2)}, u32[]{:S(2)}) collective-permute-start(bf16[48,4224]{1,0:T(8,128)(2,1)S(1)} %get-tuple-element.16), channel_id=1, source_target_pairs={{0,16},{1,9},{8,24},{9,1},{16,0},{17,25},{24,8},{25,17},{2,18},{3,... | collective-permute-start | bytes 1216520 | tf_op jit(solution)/shard_map/ppermute | solution.py:224
  27.4 0.1 collective-permute-start.5
  27.5 5.8 %collective-permute-done.4.refs_4_ = bf16[48,4224]{1,0:T(8,128)(2,1)S(1)} collective-permute-done((bf16[48,4224]{1,0:T(8,128)(2,1)S(1)}, bf16[48,4224]{1,0:T(8,128)(2,1)S(1)}, u32[]{:S(2)}, u32[]{:S(2)}) %collective-permute-start.4) | collective-permute-done | bytes 405536 | tf_op jit(solution)/shard_map/ppermute | solution.py:224
  33.3 4.3 %collective-permute-done.5.refs_5_ = bf16[48,4224]{1,0:T(8,128)(2,1)S(1)} collective-permute-done((bf16[48,4224]{1,0:T(8,128)(2,1)S(1)}, bf16[48,4224]{1,0:T(8,128)(2,1)S(1)}, u32[]{:S(2)}, u32[]{:S(2)}) %collective-permute-start.5) | collective-permute-done | bytes 405536 | tf_op jit(solution)/shard_map/ppermute | solution.py:224
  37.7 1.7 %collective-permute-done.7.refs_7_ = bf16[48,4224]{1,0:T(8,128)(2,1)S(1)} collective-permute-done((bf16[48,4224]{1,0:T(8,128)(2,1)S(1)}, bf16[48,4224]{1,0:T(8,128)(2,1)S(1)}, u32[]{:S(2)}, u32[]{:S(2)}) %collective-permute-start.7) | collective-permute-done | bytes 405536 | tf_op jit(solution)/shard_map/ppermute | solution.py:35
  39.4 1.8 %shard_map.39.refs_8_ = f32[1,128]{1,0:T(1,128)S(1)} custom-call(bf16[96,4224]{1,0:T(8,128)(2,1)S(1)} %shard_map.37.own_ref.refs_0_, bf16[192,4224]{1,0:T(8,128)(2,1)S(1)} %get-tuple-element.10.refs_1_, bf16[192,4224]{1,0:T(8,128)(2,1)S(1)} %collective-permute-done.2.refs_2_, bf16[192,4224]{1,0:T(8,128)(2,1)S(1)} %collective-permute-done.3.refs_3_, ...), custom_call_target="tpu_custom_call" | custom-call | flops 805306368 | bytes 7340032 | tf_op jit(solution)/shard_map/pallas_call | solution.py:182
  41.2 2.3 %collective-permute-done.8.refs_0_ = bf16[6160,128]{1,0:T(8,128)(2,1)S(1)} collective-permute-done((bf16[6160,128]{1,0:T(8,128)(2,1)S(1)}, bf16[6160,128]{1,0:T(8,128)(2,1)S(1)}, u32[]{:S(2)}, u32[]{:S(2)}) %collective-permute-start.8) | collective-permute-done | bytes 1576992 | tf_op jit(solution)/shard_map/ppermute | solution.py:216
  43.5 2.0 %shard_map.40 = (f32[2,128]{1,0:T(2,128)S(1)}, f32[4,128]{1,0:T(4,128)S(1)}, f32[4,128]{1,0:T(4,128)S(1)}) custom-call(bf16[6160,128]{1,0:T(8,128)(2,1)S(1)} %collective-permute-done.8.refs_0_, bf16[192,4224]{1,0:T(8,128)(2,1)S(1)} %get-tuple-element.10.refs_1_, bf16[192,4224]{1,0:T(8,128)(2,1)S(1)} %collective-permute-done.2.refs_2_, ...), custom_call_target="tpu_custom_call" | custom-call | flops 1610612736 | bytes 8388608 | tf_op jit(solution)/shard_map/pallas_call | solution.py:182
  45.5 1.3 %collective-permute-start.11 = (f32[4,128]{1,0:T(4,128)S(1)}, f32[4,128]{1,0:T(4,128)S(1)}, u32[]{:S(2)}, u32[]{:S(2)}) collective-permute-start(f32[4,128]{1,0:T(4,128)S(1)} %get-tuple-element.14), channel_id=1, source_target_pairs={{0,1},{1,0},{2,3},{3,2},{4,5},{5,4},{6,7},{7,6},{8,9},{9,8},{10,11... | collective-permute-start | bytes 6152 | tf_op jit(solution)/shard_map/ppermute | solution.py:35
  46.8 1.3 %collective-permute-start.9 = (f32[2,128]{1,0:T(2,128)S(1)}, f32[2,128]{1,0:T(2,128)S(1)}, u32[]{:S(2)}, u32[]{:S(2)}) collective-permute-start(f32[2,128]{1,0:T(2,128)S(1)} %get-tuple-element.12), channel_id=1, source_target_pairs={{4,0},{2,6},{3,1},{5,3},{7,5},{1,7},{12,8},{10,14},{11,9},{13,11},... | collective-permute-start | bytes 3080 | tf_op jit(solution)/shard_map/ppermute | solution.py:244
  48.1 1.4 %collective-permute-start.14 = (f32[4,128]{1,0:T(4,128)S(1)}, f32[4,128]{1,0:T(4,128)S(1)}, u32[]{:S(2)}, u32[]{:S(2)}) collective-permute-start(f32[4,128]{1,0:T(4,128)S(1)} %max.28), channel_id=1, source_target_pairs={{0,24},{8,16},{16,8},{24,0},{1,25},{9,17},{17,9},{25,1},{2,26},{10... | collective-permute-start | bytes 6152 | tf_op jit(solution)/shard_map/ppermute | solution.py:254
  49.5 2.6 %collective-permute-start.13 = (f32[4,128]{1,0:T(4,128)S(1)}, f32[4,128]{1,0:T(4,128)S(1)}, u32[]{:S(2)}, u32[]{:S(2)}) collective-permute-start(f32[4,128]{1,0:T(4,128)S(1)} %max.28), channel_id=1, source_target_pairs={{0,16},{1,9},{8,24},{9,1},{16,0},{17,25},{24,8},{25,17},{2,18},{3,... | collective-permute-start | bytes 6152 | tf_op jit(solution)/shard_map/ppermute | solution.py:252
  52.1 1.0 %collective-permute-done.9 = f32[2,128]{1,0:T(2,128)S(1)} collective-permute-done((f32[2,128]{1,0:T(2,128)S(1)}, f32[2,128]{1,0:T(2,128)S(1)}, u32[]{:S(2)}, u32[]{:S(2)}) %collective-permute-start.9) | collective-permute-done | bytes 1056 | tf_op jit(solution)/shard_map/ppermute | solution.py:244
  53.2 1.1 %collective-permute-done.10 = f32[2,128]{1,0:T(2,128)S(1)} collective-permute-done((f32[2,128]{1,0:T(2,128)S(1)}, f32[2,128]{1,0:T(2,128)S(1)}, u32[]{:S(2)}, u32[]{:S(2)}) %collective-permute-start.10) | collective-permute-done | bytes 1056 | tf_op jit(solution)/shard_map/ppermute | solution.py:35
  54.3 1.4 %collective-permute-done.12 = f32[4,128]{1,0:T(4,128)S(1)} collective-permute-done((f32[4,128]{1,0:T(4,128)S(1)}, f32[4,128]{1,0:T(4,128)S(1)}, u32[]{:S(2)}, u32[]{:S(2)}) %collective-permute-start.12) | collective-permute-done | bytes 2080 | tf_op jit(solution)/shard_map/ppermute | solution.py:252
  55.7 0.5 maximum_bitcast_fusion
  (16 shorter events, 0.2 us)
Async XLA Ops:
  0.0 2.6 %collective-permute-start = (bf16[96,4096]{1,0:T(8,128)(2,1)}, bf16[96,4096]{1,0:T(8,128)(2,1)S(1)}, u32[]{:S(2)}, u32[]{:S(2)}) collective-permute-start(bf16[96,4096]{1,0:T(8,128)(2,1)} %rows_ref.1), channel_id=1, source_target_pairs={{0,1},{1,0},{2,3},{3,2},{4,5},{5,4},{6,7},{7,6},{8,9},{9,8},{10,11... | collective-permute-start | bytes 2359304 | tf_op jit(solution)/shard_map/ppermute | solution.py:35
  1.1 1.5 %collective-permute-start.1 = (s32[2,96]{1,0:T(2,128)S(1)}, s32[2,96]{1,0:T(2,128)S(1)}, u32[]{:S(2)}, u32[]{:S(2)}) collective-permute-start(s32[2,96]{1,0:T(2,128)S(1)} %pad_add_fusion.ids_ref.own_ids_ref), channel_id=1, source_target_pairs={{0,1},{1,0},{2,3},{3,2},{4,5},{5,4},{6,7},{7,6},{8,9},{9,8},{10,11... | collective-permute-start | bytes 2312 | tf_op jit(solution)/shard_map/ppermute | solution.py:35
  1.2 1.1 %copy-start = (bf16[96,4096]{1,0:T(8,128)(2,1)S(1)}, bf16[96,4096]{1,0:T(8,128)(2,1)}, u32[]{:S(2)}) copy-start(bf16[96,4096]{1,0:T(8,128)(2,1)} %rows_ref.1) | copy-start | bytes 2359300
  3.3 21.9 %collective-permute-start.2 = (bf16[192,4224]{1,0:T(8,128)(2,1)S(1)}, bf16[192,4224]{1,0:T(8,128)(2,1)S(1)}, u32[]{:S(2)}, u32[]{:S(2)}) collective-permute-start(bf16[192,4224]{1,0:T(8,128)(2,1)S(1)} %get-tuple-element.10.refs_1_), channel_id=1, source_target_pairs={{0,8},{1,17},{8,0},{9,25},{16,24},{17,1},{24,16},{25,9},{2,10},{3,... | collective-permute-start | bytes 4866056 | tf_op jit(solution)/shard_map/ppermute | solution.py:219
  6.3 37.2 %collective-permute-start.8 = (bf16[6160,128]{1,0:T(8,128)(2,1)S(1)}, bf16[6160,128]{1,0:T(8,128)(2,1)S(1)}, u32[]{:S(2)}, u32[]{:S(2)}) collective-permute-start(bf16[6160,128]{1,0:T(8,128)(2,1)S(1)} %get-tuple-element.11), channel_id=1, source_target_pairs={{0,4},{6,2},{1,3},{3,5},{5,7},{7,1},{8,12},{14,10},{9,11},{11,13},... | collective-permute-start | bytes 4730888 | tf_op jit(solution)/shard_map/ppermute | solution.py:216
  25.3 14.2 %collective-permute-start.3 = (bf16[192,4224]{1,0:T(8,128)(2,1)S(1)}, bf16[192,4224]{1,0:T(8,128)(2,1)S(1)}, u32[]{:S(2)}, u32[]{:S(2)}) collective-permute-start(bf16[192,4224]{1,0:T(8,128)(2,1)S(1)} %collective-permute-done.2.refs_2_), channel_id=1, source_target_pairs={{0,1},{1,0},{2,3},{3,2},{4,5},{5,4},{6,7},{7,6},{8,9},{9,8},{10,11... | collective-permute-start | bytes 4866056 | tf_op jit(solution)/shard_map/ppermute | solution.py:35
  25.3 8.0 %collective-permute-start.4 = (bf16[48,4224]{1,0:T(8,128)(2,1)S(1)}, bf16[48,4224]{1,0:T(8,128)(2,1)S(1)}, u32[]{:S(2)}, u32[]{:S(2)}) collective-permute-start(bf16[48,4224]{1,0:T(8,128)(2,1)S(1)} %get-tuple-element.16), channel_id=1, source_target_pairs={{0,16},{1,9},{8,24},{9,1},{16,0},{17,25},{24,8},{25,17},{2,18},{3,... | collective-permute-start | bytes 1216520 | tf_op jit(solution)/shard_map/ppermute | solution.py:224
  27.4 10.2 %collective-permute-start.5 = (bf16[48,4224]{1,0:T(8,128)(2,1)S(1)}, bf16[48,4224]{1,0:T(8,128)(2,1)S(1)}, u32[]{:S(2)}, u32[]{:S(2)}) collective-permute-start(bf16[48,4224]{1,0:T(8,128)(2,1)S(1)} %get-tuple-element.15), channel_id=1, source_target_pairs={{0,16},{1,9},{8,24},{9,1},{16,0},{17,25},{24,8},{25,17},{2,18},{3,... | collective-permute-start | bytes 1216520 | tf_op jit(solution)/shard_map/ppermute | solution.py:224
  33.3 4.4 %collective-permute-start.6 = (bf16[48,4224]{1,0:T(8,128)(2,1)S(1)}, bf16[48,4224]{1,0:T(8,128)(2,1)S(1)}, u32[]{:S(2)}, u32[]{:S(2)}) collective-permute-start(bf16[48,4224]{1,0:T(8,128)(2,1)S(1)} %collective-permute-done.4.refs_4_), channel_id=1, source_target_pairs={{0,1},{1,0},{2,3},{3,2},{4,5},{5,4},{6,7},{7,6},{8,9},{9,8},{10,11... | collective-permute-start | bytes 1216520 | tf_op jit(solution)/shard_map/ppermute | solution.py:35
  37.7 1.7 %collective-permute-start.7 = (bf16[48,4224]{1,0:T(8,128)(2,1)S(1)}, bf16[48,4224]{1,0:T(8,128)(2,1)S(1)}, u32[]{:S(2)}, u32[]{:S(2)}) collective-permute-start(bf16[48,4224]{1,0:T(8,128)(2,1)S(1)} %collective-permute-done.5.refs_5_), channel_id=1, source_target_pairs={{0,1},{1,0},{2,3},{3,2},{4,5},{5,4},{6,7},{7,6},{8,9},{9,8},{10,11... | collective-permute-start | bytes 1216520 | tf_op jit(solution)/shard_map/ppermute | solution.py:35
  45.5 2.6 %collective-permute-start.11 = (f32[4,128]{1,0:T(4,128)S(1)}, f32[4,128]{1,0:T(4,128)S(1)}, u32[]{:S(2)}, u32[]{:S(2)}) collective-permute-start(f32[4,128]{1,0:T(4,128)S(1)} %get-tuple-element.14), channel_id=1, source_target_pairs={{0,1},{1,0},{2,3},{3,2},{4,5},{5,4},{6,7},{7,6},{8,9},{9,8},{10,11... | collective-permute-start | bytes 6152 | tf_op jit(solution)/shard_map/ppermute | solution.py:35
  46.8 6.3 %collective-permute-start.9 = (f32[2,128]{1,0:T(2,128)S(1)}, f32[2,128]{1,0:T(2,128)S(1)}, u32[]{:S(2)}, u32[]{:S(2)}) collective-permute-start(f32[2,128]{1,0:T(2,128)S(1)} %get-tuple-element.12), channel_id=1, source_target_pairs={{4,0},{2,6},{3,1},{5,3},{7,5},{1,7},{12,8},{10,14},{11,9},{13,11},... | collective-permute-start | bytes 3080 | tf_op jit(solution)/shard_map/ppermute | solution.py:244
  48.1 6.2 %collective-permute-start.14 = (f32[4,128]{1,0:T(4,128)S(1)}, f32[4,128]{1,0:T(4,128)S(1)}, u32[]{:S(2)}, u32[]{:S(2)}) collective-permute-start(f32[4,128]{1,0:T(4,128)S(1)} %max.28), channel_id=1, source_target_pairs={{0,24},{8,16},{16,8},{24,0},{1,25},{9,17},{17,9},{25,1},{2,26},{10... | collective-permute-start | bytes 6152 | tf_op jit(solution)/shard_map/ppermute | solution.py:254
  49.5 4.8 %collective-permute-start.13 = (f32[4,128]{1,0:T(4,128)S(1)}, f32[4,128]{1,0:T(4,128)S(1)}, u32[]{:S(2)}, u32[]{:S(2)}) collective-permute-start(f32[4,128]{1,0:T(4,128)S(1)} %max.28), channel_id=1, source_target_pairs={{0,16},{1,9},{8,24},{9,1},{16,0},{17,25},{24,8},{25,17},{2,18},{3,... | collective-permute-start | bytes 6152 | tf_op jit(solution)/shard_map/ppermute | solution.py:252
  52.1 3.6 %collective-permute-start.12 = (f32[4,128]{1,0:T(4,128)S(1)}, f32[4,128]{1,0:T(4,128)S(1)}, u32[]{:S(2)}, u32[]{:S(2)}) collective-permute-start(f32[4,128]{1,0:T(4,128)S(1)} %max.28), channel_id=1, source_target_pairs={{0,8},{1,17},{8,0},{9,25},{16,24},{17,1},{24,16},{25,9},{2,10},{3,... | collective-permute-start | bytes 6152 | tf_op jit(solution)/shard_map/ppermute | solution.py:252
  53.2 1.1 %collective-permute-start.10 = (f32[2,128]{1,0:T(2,128)S(1)}, f32[2,128]{1,0:T(2,128)S(1)}, u32[]{:S(2)}, u32[]{:S(2)}) collective-permute-start(f32[2,128]{1,0:T(2,128)S(1)} %collective-permute-done.9), channel_id=1, source_target_pairs={{0,1},{1,0},{2,3},{3,2},{4,5},{5,4},{6,7},{7,6},{8,9},{9,8},{10,11... | collective-permute-start | bytes 3080 | tf_op jit(solution)/shard_map/ppermute | solution.py:35

commit v29 on v27

--- a/solution.py
+++ b/solution.py
@@ -9,7 +9,7 @@
 
 AXES = ("group", "z", "core")
 LANES = 128
-CHUNK = 512
+CHUNK = 256
 TAIL = 16
 VMEM = pl.BlockSpec(memory_space=pltpu.VMEM)
 

time: 55.1 us -> 55.1 us (level)
  no operation moved by 1% of the time
where the time goes in v29:
time: 55.1 us; the launch traced here: 54.8 us
  waiting for transfers between devices  30.7 us (56%)
  starting transfers between devices  16.9 us (31%)
  Pallas kernels  4.78 us (9%)
  other arithmetic  1.2 us (2%)
  local copies, waits for them, and re-layouts  1.19 us (2%)
    ppermute x1, waiting for transfers between devices, local(): lax.ppermute(both, plane_axes, group_trip(groups, *way))  14.3 us
    ppermute x2, waiting for transfers between devices, local(): corner = [lax.ppermute(part, plane_axes, relay) for part in corner]  10.2 us
    ppermute x1, starting transfers between devices, local(): visitors = [lax.ppermute(line, line_axes, trip) for trip in trips]  4.58 us
    pallas_call x2, Pallas kernels, call(): pl.pallas_call(kernel, in_specs=[VMEM] * len(operands), out_specs=[VMEM]...  3.8 us
    ppermute x1, starting transfers between devices, local(): lax.ppermute(both, plane_axes, group_trip(groups, *way))  3 us
    ppermute x7, waiting for transfers between devices, swap(): return lax.ppermute(block, 'core', flip(2, 1))  2.88 us
    ppermute x2, starting transfers between devices, local(): got = lax.ppermute(merged[chunk], plane_axes, group_trip(groups, *order))  2.58 us
    ppermute x1, waiting for transfers between devices, local(): visitors = [lax.ppermute(line, line_axes, trip) for trip in trips]  2.29 us
  transfers between devices with their start and end apart: 15, of which 7 were waited for; matrix products, arithmetic and copies ran while one was open for 1% of the time, Pallas kernels for 4%

profile of v29, /device:TPU:0, one launch (start us, length us, event | category | flops | bytes accessed | tf_op | source)
XLA Modules:
  0.0 54.8 jit_solution(10182244760714790183)
XLA Ops:
  0.0 0.5 collective-permute-start
  0.5 0.7 %pad_add_fusion.ids_ref.own_ids_ref = s32[2,96]{1,0:T(2,128)S(1)} fusion(s32[1,96]{1,0:T(1,128)} %bitcast.4, s32[1,96]{1,0:T(1,128)} %bitcast.5), kind=kLoop, calls=%fused_computation | loop fusion | flops 192 | bytes 1536 | tf_op jit(solution)/shard_map/stack | solution.py:206
  1.2 1.1 %copy-done = bf16[96,4096]{1,0:T(8,128)(2,1)S(1)} copy-done((bf16[96,4096]{1,0:T(8,128)(2,1)S(1)}, bf16[96,4096]{1,0:T(8,128)(2,1)}, u32[]{:S(2)}) %copy-start) | copy-done | bytes 786456
  2.3 0.3 shard_map.37.own_ref.refs_0_
  2.6 0.7 %shard_map.38 = (bf16[192,4224]{1,0:T(8,128)(2,1)S(1)}, bf16[6160,128]{1,0:T(8,128)(2,1)S(1)}) custom-call(bf16[96,4224]{1,0:T(8,128)(2,1)S(1)} %shard_map.37.own_ref.refs_0_, s32[2,96]{1,0:T(2,128)S(1)} %pad_add_fusion.ids_ref.own_ids_ref, bf16[96,4096]{1,0:T(8,128)(2,1)S(1)} %collective-permute-done.rows_ref, s32[2,96]{1,0:T(2,128)S(1)} %collective-permute-done.1.ids_ref), custom_call_target="tpu_custom_call" | custom-call | flops 1572864 | bytes 1572864 | tf_op jit(solution)/shard_map/pallas_call | solution.py:77
  3.3 3.0 %collective-permute-start.2 = (bf16[192,4224]{1,0:T(8,128)(2,1)S(1)}, bf16[192,4224]{1,0:T(8,128)(2,1)S(1)}, u32[]{:S(2)}, u32[]{:S(2)}) collective-permute-start(bf16[192,4224]{1,0:T(8,128)(2,1)S(1)} %get-tuple-element.10.refs_1_), channel_id=1, source_target_pairs={{0,8},{1,17},{8,0},{9,25},{16,24},{17,1},{24,16},{25,9},{2,10},{3,... | collective-permute-start | bytes 4866056 | tf_op jit(solution)/shard_map/ppermute | solution.py:219
  6.3 4.6 %collective-permute-start.8 = (bf16[6160,128]{1,0:T(8,128)(2,1)S(1)}, bf16[6160,128]{1,0:T(8,128)(2,1)S(1)}, u32[]{:S(2)}, u32[]{:S(2)}) collective-permute-start(bf16[6160,128]{1,0:T(8,128)(2,1)S(1)} %get-tuple-element.11), channel_id=1, source_target_pairs={{0,4},{6,2},{1,3},{3,5},{5,7},{7,1},{8,12},{14,10},{9,11},{11,13},... | collective-permute-start | bytes 4730888 | tf_op jit(solution)/shard_map/ppermute | solution.py:216
  10.9 14.3 %collective-permute-done.2.refs_2_ = bf16[192,4224]{1,0:T(8,128)(2,1)S(1)} collective-permute-done((bf16[192,4224]{1,0:T(8,128)(2,1)S(1)}, bf16[192,4224]{1,0:T(8,128)(2,1)S(1)}, u32[]{:S(2)}, u32[]{:S(2)}) %collective-permute-start.2) | collective-permute-done | bytes 1622048 | tf_op jit(solution)/shard_map/ppermute | solution.py:219
  25.3 2.1 %collective-permute-start.4 = (bf16[48,4224]{1,0:T(8,128)(2,1)S(1)}, bf16[48,4224]{1,0:T(8,128)(2,1)S(1)}, u32[]{:S(2)}, u32[]{:S(2)}) collective-permute-start(bf16[48,4224]{1,0:T(8,128)(2,1)S(1)} %get-tuple-element.16), channel_id=1, source_target_pairs={{0,16},{1,9},{8,24},{9,1},{16,0},{17,25},{24,8},{25,17},{2,18},{3,... | collective-permute-start | bytes 1216520 | tf_op jit(solution)/shard_map/ppermute | solution.py:224
  27.4 0.1 collective-permute-start.5
  27.5 5.8 %collective-permute-done.4.refs_4_ = bf16[48,4224]{1,0:T(8,128)(2,1)S(1)} collective-permute-done((bf16[48,4224]{1,0:T(8,128)(2,1)S(1)}, bf16[48,4224]{1,0:T(8,128)(2,1)S(1)}, u32[]{:S(2)}, u32[]{:S(2)}) %collective-permute-start.4) | collective-permute-done | bytes 405536 | tf_op jit(solution)/shard_map/ppermute | solution.py:224
  33.3 4.3 %collective-permute-done.5.refs_5_ = bf16[48,4224]{1,0:T(8,128)(2,1)S(1)} collective-permute-done((bf16[48,4224]{1,0:T(8,128)(2,1)S(1)}, bf16[48,4224]{1,0:T(8,128)(2,1)S(1)}, u32[]{:S(2)}, u32[]{:S(2)}) %collective-permute-start.5) | collective-permute-done | bytes 405536 | tf_op jit(solution)/shard_map/ppermute | solution.py:224
  37.7 1.7 %collective-permute-done.7.refs_7_ = bf16[48,4224]{1,0:T(8,128)(2,1)S(1)} collective-permute-done((bf16[48,4224]{1,0:T(8,128)(2,1)S(1)}, bf16[48,4224]{1,0:T(8,128)(2,1)S(1)}, u32[]{:S(2)}, u32[]{:S(2)}) %collective-permute-start.7) | collective-permute-done | bytes 405536 | tf_op jit(solution)/shard_map/ppermute | solution.py:35
  39.4 1.8 %shard_map.39.refs_8_ = f32[1,128]{1,0:T(1,128)S(1)} custom-call(bf16[96,4224]{1,0:T(8,128)(2,1)S(1)} %shard_map.37.own_ref.refs_0_, bf16[192,4224]{1,0:T(8,128)(2,1)S(1)} %get-tuple-element.10.refs_1_, bf16[192,4224]{1,0:T(8,128)(2,1)S(1)} %collective-permute-done.2.refs_2_, bf16[192,4224]{1,0:T(8,128)(2,1)S(1)} %collective-permute-done.3.refs_3_, ...), custom_call_target="tpu_custom_call" | custom-call | flops 805306368 | bytes 7340032 | tf_op jit(solution)/shard_map/pallas_call | solution.py:182
  41.2 2.3 %collective-permute-done.8.refs_0_ = bf16[6160,128]{1,0:T(8,128)(2,1)S(1)} collective-permute-done((bf16[6160,128]{1,0:T(8,128)(2,1)S(1)}, bf16[6160,128]{1,0:T(8,128)(2,1)S(1)}, u32[]{:S(2)}, u32[]{:S(2)}) %collective-permute-start.8) | collective-permute-done | bytes 1576992 | tf_op jit(solution)/shard_map/ppermute | solution.py:216
  43.5 2.0 %shard_map.40 = (f32[2,128]{1,0:T(2,128)S(1)}, f32[4,128]{1,0:T(4,128)S(1)}, f32[4,128]{1,0:T(4,128)S(1)}) custom-call(bf16[6160,128]{1,0:T(8,128)(2,1)S(1)} %collective-permute-done.8.refs_0_, bf16[192,4224]{1,0:T(8,128)(2,1)S(1)} %get-tuple-element.10.refs_1_, bf16[192,4224]{1,0:T(8,128)(2,1)S(1)} %collective-permute-done.2.refs_2_, ...), custom_call_target="tpu_custom_call" | custom-call | flops 1610612736 | bytes 8388608 | tf_op jit(solution)/shard_map/pallas_call | solution.py:182
  45.5 1.3 %collective-permute-start.11 = (f32[4,128]{1,0:T(4,128)S(1)}, f32[4,128]{1,0:T(4,128)S(1)}, u32[]{:S(2)}, u32[]{:S(2)}) collective-permute-start(f32[4,128]{1,0:T(4,128)S(1)} %get-tuple-element.14), channel_id=1, source_target_pairs={{0,1},{1,0},{2,3},{3,2},{4,5},{5,4},{6,7},{7,6},{8,9},{9,8},{10,11... | collective-permute-start | bytes 6152 | tf_op jit(solution)/shard_map/ppermute | solution.py:35
  46.8 1.3 %collective-permute-start.9 = (f32[2,128]{1,0:T(2,128)S(1)}, f32[2,128]{1,0:T(2,128)S(1)}, u32[]{:S(2)}, u32[]{:S(2)}) collective-permute-start(f32[2,128]{1,0:T(2,128)S(1)} %get-tuple-element.12), channel_id=1, source_target_pairs={{4,0},{2,6},{3,1},{5,3},{7,5},{1,7},{12,8},{10,14},{11,9},{13,11},... | collective-permute-start | bytes 3080 | tf_op jit(solution)/shard_map/ppermute | solution.py:244
  48.1 1.4 %collective-permute-start.14 = (f32[4,128]{1,0:T(4,128)S(1)}, f32[4,128]{1,0:T(4,128)S(1)}, u32[]{:S(2)}, u32[]{:S(2)}) collective-permute-start(f32[4,128]{1,0:T(4,128)S(1)} %max.28), channel_id=1, source_target_pairs={{0,24},{8,16},{16,8},{24,0},{1,25},{9,17},{17,9},{25,1},{2,26},{10... | collective-permute-start | bytes 6152 | tf_op jit(solution)/shard_map/ppermute | solution.py:254
  49.5 1.2 %collective-permute-start.13 = (f32[4,128]{1,0:T(4,128)S(1)}, f32[4,128]{1,0:T(4,128)S(1)}, u32[]{:S(2)}, u32[]{:S(2)}) collective-permute-start(f32[4,128]{1,0:T(4,128)S(1)} %max.28), channel_id=1, source_target_pairs={{0,8},{1,17},{8,0},{9,25},{16,24},{17,1},{24,16},{25,9},{2,10},{3,... | collective-permute-start | bytes 6152 | tf_op jit(solution)/shard_map/ppermute | solution.py:252
  50.7 1.4 %collective-permute-start.12 = (f32[4,128]{1,0:T(4,128)S(1)}, f32[4,128]{1,0:T(4,128)S(1)}, u32[]{:S(2)}, u32[]{:S(2)}) collective-permute-start(f32[4,128]{1,0:T(4,128)S(1)} %max.28), channel_id=1, source_target_pairs={{0,16},{1,9},{8,24},{9,1},{16,0},{17,25},{24,8},{25,17},{2,18},{3,... | collective-permute-start | bytes 6152 | tf_op jit(solution)/shard_map/ppermute | solution.py:252
  52.1 1.0 %collective-permute-done.9 = f32[2,128]{1,0:T(2,128)S(1)} collective-permute-done((f32[2,128]{1,0:T(2,128)S(1)}, f32[2,128]{1,0:T(2,128)S(1)}, u32[]{:S(2)}, u32[]{:S(2)}) %collective-permute-start.9) | collective-permute-done | bytes 1056 | tf_op jit(solution)/shard_map/ppermute | solution.py:244
  53.2 1.1 %collective-permute-done.10 = f32[2,128]{1,0:T(2,128)S(1)} collective-permute-done((f32[2,128]{1,0:T(2,128)S(1)}, f32[2,128]{1,0:T(2,128)S(1)}, u32[]{:S(2)}, u32[]{:S(2)}) %collective-permute-start.10) | collective-permute-done | bytes 1056 | tf_op jit(solution)/shard_map/ppermute | solution.py:35
  54.3 0.5 maximum_bitcast_fusion
  (16 shorter events, 0.2 us)
Async XLA Ops:
  0.0 2.6 %collective-permute-start = (bf16[96,4096]{1,0:T(8,128)(2,1)}, bf16[96,4096]{1,0:T(8,128)(2,1)S(1)}, u32[]{:S(2)}, u32[]{:S(2)}) collective-permute-start(bf16[96,4096]{1,0:T(8,128)(2,1)} %rows_ref.1), channel_id=1, source_target_pairs={{0,1},{1,0},{2,3},{3,2},{4,5},{5,4},{6,7},{7,6},{8,9},{9,8},{10,11... | collective-permute-start | bytes 2359304 | tf_op jit(solution)/shard_map/ppermute | solution.py:35
  1.1 1.5 %collective-permute-start.1 = (s32[2,96]{1,0:T(2,128)S(1)}, s32[2,96]{1,0:T(2,128)S(1)}, u32[]{:S(2)}, u32[]{:S(2)}) collective-permute-start(s32[2,96]{1,0:T(2,128)S(1)} %pad_add_fusion.ids_ref.own_ids_ref), channel_id=1, source_target_pairs={{0,1},{1,0},{2,3},{3,2},{4,5},{5,4},{6,7},{7,6},{8,9},{9,8},{10,11... | collective-permute-start | bytes 2312 | tf_op jit(solution)/shard_map/ppermute | solution.py:35
  1.2 1.1 %copy-start = (bf16[96,4096]{1,0:T(8,128)(2,1)S(1)}, bf16[96,4096]{1,0:T(8,128)(2,1)}, u32[]{:S(2)}) copy-start(bf16[96,4096]{1,0:T(8,128)(2,1)} %rows_ref.1) | copy-start | bytes 2359300
  3.3 21.9 %collective-permute-start.2 = (bf16[192,4224]{1,0:T(8,128)(2,1)S(1)}, bf16[192,4224]{1,0:T(8,128)(2,1)S(1)}, u32[]{:S(2)}, u32[]{:S(2)}) collective-permute-start(bf16[192,4224]{1,0:T(8,128)(2,1)S(1)} %get-tuple-element.10.refs_1_), channel_id=1, source_target_pairs={{0,8},{1,17},{8,0},{9,25},{16,24},{17,1},{24,16},{25,9},{2,10},{3,... | collective-permute-start | bytes 4866056 | tf_op jit(solution)/shard_map/ppermute | solution.py:219
  6.3 37.2 %collective-permute-start.8 = (bf16[6160,128]{1,0:T(8,128)(2,1)S(1)}, bf16[6160,128]{1,0:T(8,128)(2,1)S(1)}, u32[]{:S(2)}, u32[]{:S(2)}) collective-permute-start(bf16[6160,128]{1,0:T(8,128)(2,1)S(1)} %get-tuple-element.11), channel_id=1, source_target_pairs={{0,4},{6,2},{1,3},{3,5},{5,7},{7,1},{8,12},{14,10},{9,11},{11,13},... | collective-permute-start | bytes 4730888 | tf_op jit(solution)/shard_map/ppermute | solution.py:216
  25.3 14.2 %collective-permute-start.3 = (bf16[192,4224]{1,0:T(8,128)(2,1)S(1)}, bf16[192,4224]{1,0:T(8,128)(2,1)S(1)}, u32[]{:S(2)}, u32[]{:S(2)}) collective-permute-start(bf16[192,4224]{1,0:T(8,128)(2,1)S(1)} %collective-permute-done.2.refs_2_), channel_id=1, source_target_pairs={{0,1},{1,0},{2,3},{3,2},{4,5},{5,4},{6,7},{7,6},{8,9},{9,8},{10,11... | collective-permute-start | bytes 4866056 | tf_op jit(solution)/shard_map/ppermute | solution.py:35
  25.3 8.0 %collective-permute-start.4 = (bf16[48,4224]{1,0:T(8,128)(2,1)S(1)}, bf16[48,4224]{1,0:T(8,128)(2,1)S(1)}, u32[]{:S(2)}, u32[]{:S(2)}) collective-permute-start(bf16[48,4224]{1,0:T(8,128)(2,1)S(1)} %get-tuple-element.16), channel_id=1, source_target_pairs={{0,16},{1,9},{8,24},{9,1},{16,0},{17,25},{24,8},{25,17},{2,18},{3,... | collective-permute-start | bytes 1216520 | tf_op jit(solution)/shard_map/ppermute | solution.py:224
  27.4 10.2 %collective-permute-start.5 = (bf16[48,4224]{1,0:T(8,128)(2,1)S(1)}, bf16[48,4224]{1,0:T(8,128)(2,1)S(1)}, u32[]{:S(2)}, u32[]{:S(2)}) collective-permute-start(bf16[48,4224]{1,0:T(8,128)(2,1)S(1)} %get-tuple-element.15), channel_id=1, source_target_pairs={{0,16},{1,9},{8,24},{9,1},{16,0},{17,25},{24,8},{25,17},{2,18},{3,... | collective-permute-start | bytes 1216520 | tf_op jit(solution)/shard_map/ppermute | solution.py:224
  33.3 4.4 %collective-permute-start.6 = (bf16[48,4224]{1,0:T(8,128)(2,1)S(1)}, bf16[48,4224]{1,0:T(8,128)(2,1)S(1)}, u32[]{:S(2)}, u32[]{:S(2)}) collective-permute-start(bf16[48,4224]{1,0:T(8,128)(2,1)S(1)} %collective-permute-done.4.refs_4_), channel_id=1, source_target_pairs={{0,1},{1,0},{2,3},{3,2},{4,5},{5,4},{6,7},{7,6},{8,9},{9,8},{10,11... | collective-permute-start | bytes 1216520 | tf_op jit(solution)/shard_map/ppermute | solution.py:35
  37.7 1.7 %collective-permute-start.7 = (bf16[48,4224]{1,0:T(8,128)(2,1)S(1)}, bf16[48,4224]{1,0:T(8,128)(2,1)S(1)}, u32[]{:S(2)}, u32[]{:S(2)}) collective-permute-start(bf16[48,4224]{1,0:T(8,128)(2,1)S(1)} %collective-permute-done.5.refs_5_), channel_id=1, source_target_pairs={{0,1},{1,0},{2,3},{3,2},{4,5},{5,4},{6,7},{7,6},{8,9},{9,8},{10,11... | collective-permute-start | bytes 1216520 | tf_op jit(solution)/shard_map/ppermute | solution.py:35
  45.5 2.6 %collective-permute-start.11 = (f32[4,128]{1,0:T(4,128)S(1)}, f32[4,128]{1,0:T(4,128)S(1)}, u32[]{:S(2)}, u32[]{:S(2)}) collective-permute-start(f32[4,128]{1,0:T(4,128)S(1)} %get-tuple-element.14), channel_id=1, source_target_pairs={{0,1},{1,0},{2,3},{3,2},{4,5},{5,4},{6,7},{7,6},{8,9},{9,8},{10,11... | collective-permute-start | bytes 6152 | tf_op jit(solution)/shard_map/ppermute | solution.py:35
  46.8 6.3 %collective-permute-start.9 = (f32[2,128]{1,0:T(2,128)S(1)}, f32[2,128]{1,0:T(2,128)S(1)}, u32[]{:S(2)}, u32[]{:S(2)}) collective-permute-start(f32[2,128]{1,0:T(2,128)S(1)} %get-tuple-element.12), channel_id=1, source_target_pairs={{4,0},{2,6},{3,1},{5,3},{7,5},{1,7},{12,8},{10,14},{11,9},{13,11},... | collective-permute-start | bytes 3080 | tf_op jit(solution)/shard_map/ppermute | solution.py:244
  48.1 6.2 %collective-permute-start.14 = (f32[4,128]{1,0:T(4,128)S(1)}, f32[4,128]{1,0:T(4,128)S(1)}, u32[]{:S(2)}, u32[]{:S(2)}) collective-permute-start(f32[4,128]{1,0:T(4,128)S(1)} %max.28), channel_id=1, source_target_pairs={{0,24},{8,16},{16,8},{24,0},{1,25},{9,17},{17,9},{25,1},{2,26},{10... | collective-permute-start | bytes 6152 | tf_op jit(solution)/shard_map/ppermute | solution.py:254
  49.5 4.8 %collective-permute-start.13 = (f32[4,128]{1,0:T(4,128)S(1)}, f32[4,128]{1,0:T(4,128)S(1)}, u32[]{:S(2)}, u32[]{:S(2)}) collective-permute-start(f32[4,128]{1,0:T(4,128)S(1)} %max.28), channel_id=1, source_target_pairs={{0,8},{1,17},{8,0},{9,25},{16,24},{17,1},{24,16},{25,9},{2,10},{3,... | collective-permute-start | bytes 6152 | tf_op jit(solution)/shard_map/ppermute | solution.py:252
  50.7 3.6 %collective-permute-start.12 = (f32[4,128]{1,0:T(4,128)S(1)}, f32[4,128]{1,0:T(4,128)S(1)}, u32[]{:S(2)}, u32[]{:S(2)}) collective-permute-start(f32[4,128]{1,0:T(4,128)S(1)} %max.28), channel_id=1, source_target_pairs={{0,16},{1,9},{8,24},{9,1},{16,0},{17,25},{24,8},{25,17},{2,18},{3,... | collective-permute-start | bytes 6152 | tf_op jit(solution)/shard_map/ppermute | solution.py:252
  53.2 1.1 %collective-permute-start.10 = (f32[2,128]{1,0:T(2,128)S(1)}, f32[2,128]{1,0:T(2,128)S(1)}, u32[]{:S(2)}, u32[]{:S(2)}) collective-permute-start(f32[2,128]{1,0:T(2,128)S(1)} %collective-permute-done.9), channel_id=1, source_target_pairs={{0,1},{1,0},{2,3},{3,2},{4,5},{5,4},{6,7},{7,6},{8,9},{9,8},{10,11... | collective-permute-start | bytes 3080 | tf_op jit(solution)/shard_map/ppermute | solution.py:35
